TPU v7x, 32 devices: a whole 2x2x4 slice. The times are simulated.
32 devices in a mesh: vocab: 32 (over z, y, x, core).
Axes of the slice: x: 2, y: 2, z: 4, core: 2. Of those that a mesh axis runs over, the one named last changes fastest.
Arguments:
- hidden_states: bfloat16 [512, 5120], P('vocab'), may hold values from -8 to 8
- head_weight: bfloat16 [5120, 32768], P(None, 'vocab'), may hold values from -0.25 to 0.25
- teacher_logits: bfloat16 [4, 64, 128, 128], P(None, None, 'vocab'), may hold values from -15 to 260
- block_lists: int32 [4, 64], replicated, may hold values from 0 to 255, as said below
- row_reader: int32 [4, 128], replicated, may hold values from 0 to 127, each once within a row
- tail_mass: float32 [512], replicated, may hold values from 0.05 to 0.5
- token_weight: float32 [512], replicated, may hold values from 1 to 8
Outputs:
- token_loss: float32 [512], P('vocab')
- grad_head: bfloat16 [5120, 32768], P(None, 'vocab')
- grad_hidden: bfloat16 [512, 5120], P('vocab')
Inputs may be any that keep to these rules, and one draw needn't show every extreme that they name: `block_lists`: for each token block the 64 listed vocabulary blocks are distinct; at most 4 of them lie in any slab of 8 consecutive blocks starting at a multiple of 8, and in every token block some slab holds exactly 4. `row_reader`: each row is a permutation.
All inputs are finite; a program needn't handle non-finite values.
Results may differ from a plain program's by a relative error of at most 0.0048.
Values may be sent and summed in bfloat16 or wider, within the bound.
No kernel may reach another device: no remote copies, remote signals or barrier semaphores. Data moves between devices by JAX's collectives and lax.ppermute only.
A program may use at most 128 MiB of HBM per device.

v0:
```python
import jax
import jax.numpy as jnp
from jax import lax
from jax.sharding import PartitionSpec as P


def row_parts(scores, teacher_slab, listed_mask, student_exp, teacher_exp):
    return (
        jnp.sum(student_exp, axis=(2, 3)),
        jnp.sum(teacher_exp, axis=(2, 3)),
        jnp.sum(teacher_exp * scores, axis=(2, 3)),
        jnp.sum(teacher_exp * teacher_slab, axis=(2, 3)),
        jnp.sum(scores, axis=(2, 3)),
        jnp.sum(jnp.where(listed_mask, scores, 0.0), axis=(2, 3)),
    )


def on_device(
    hidden_states, head_weight, teacher_logits, block_lists, row_reader, tail_mass, token_weight
):
    blocks, listed_count, stored_rows, block_side = teacher_logits.shape
    slab_width = head_weight.shape[1]
    slab_blocks = slab_width // block_side
    devices = lax.axis_size("vocab")
    rank_self = lax.axis_index("vocab")
    tokens = blocks * block_side
    shard_rows = hidden_states.shape[0]
    gathered = lax.all_gather(hidden_states, "vocab", axis=0, tiled=True)
    logits = jnp.dot(gathered, head_weight, preferred_element_type=jnp.float32)
    owner_dev = block_lists // slab_blocks
    owned_here = owner_dev == rank_self
    within = block_lists - rank_self * slab_blocks
    token_iota = lax.broadcasted_iota(jnp.int32, (1, block_side, block_side), 1)
    token_map = (row_reader[:, None, :] == token_iota).astype(jnp.bfloat16)
    place_iota = lax.broadcasted_iota(jnp.int32, (1, slab_blocks, 1), 1)
    block_iota = lax.broadcasted_iota(jnp.int32, (1, devices * slab_blocks, 1), 1)
    picker = (block_lists[:, None, :] == block_iota).astype(jnp.bfloat16)
    outgoing = jnp.einsum(
        "tnk,tkrc->tnrc", picker, teacher_logits, preferred_element_type=jnp.float32
    ).astype(jnp.bfloat16)
    incoming = lax.all_to_all(outgoing, "vocab", split_axis=1, concat_axis=2, tiled=True)
    teacher_slab = jnp.einsum(
        "tpj,tbjc->tpbc", token_map, incoming, preferred_element_type=jnp.float32
    )
    listed = jnp.sum(
        ((within[:, None, :] == place_iota) & owned_here[:, None, :]).astype(jnp.int32), axis=2
    )
    scores = logits.reshape(blocks, block_side, slab_blocks, block_side)
    listed_mask = (listed > 0)[:, None, :, None]
    local_smax = jnp.max(scores, axis=(2, 3))
    local_tmax = jnp.max(jnp.where(listed_mask, teacher_slab, -1e30), axis=(2, 3))
    student_max, teacher_max = lax.pmax((local_smax, local_tmax), "vocab")
    student_exp = jnp.exp(scores - student_max[:, :, None, None])
    teacher_exp = jnp.exp(
        jnp.where(listed_mask, teacher_slab - teacher_max[:, :, None, None], -jnp.inf)
    )
    parts = row_parts(scores, teacher_slab, listed_mask, student_exp, teacher_exp)
    student_sum, teacher_sum, cross_sum, self_sum, logit_total, listed_total = lax.psum(
        (parts[0], parts[1], parts[2], parts[3], parts[4], parts[5]), "vocab"
    )
    tail_share = tail_mass.reshape(blocks, block_side)
    unlisted = float(devices * slab_width - block_side * listed_count)
    kept_mass = 1.0 - tail_share
    log_norm = student_max + jnp.log(student_sum)
    row_loss = (
        kept_mass * (jnp.log(kept_mass) - teacher_max - jnp.log(teacher_sum))
        + kept_mass * self_sum / teacher_sum
        + tail_share * jnp.log(tail_share / unlisted)
        - kept_mass * cross_sum / teacher_sum
        - tail_share / unlisted * (logit_total - listed_total)
        + log_norm
    )
    token_loss = lax.dynamic_slice_in_dim(
        row_loss.reshape(tokens), rank_self * shard_rows, shard_rows, 0
    )
    student_prob = student_exp / student_sum[:, :, None, None]
    teacher_prob = jnp.where(
        listed_mask,
        (kept_mass / teacher_sum)[:, :, None, None] * teacher_exp,
        (tail_share / unlisted)[:, :, None, None],
    )
    weight = token_weight.reshape(blocks, block_side)[:, :, None, None]
    grad_logits = (
        (weight * (student_prob - teacher_prob)).astype(jnp.bfloat16).reshape(tokens, slab_width)
    )
    grad_head = lax.dot_general(
        gathered, grad_logits, (((0,), (0,)), ((), ())), preferred_element_type=jnp.float32
    ).astype(jnp.bfloat16)
    grad_hidden = lax.psum_scatter(
        lax.dot_general(
            grad_logits, head_weight, (((1,), (1,)), ((), ())), preferred_element_type=jnp.float32
        ),
        "vocab",
        scatter_dimension=0,
        tiled=True,
    ).astype(jnp.bfloat16)
    return (token_loss, grad_head, grad_hidden)


def solution(mesh):
    in_specs = (
        P("vocab", None),
        P(None, "vocab"),
        P(None, None, "vocab", None),
        P(),
        P(),
        P(),
        P(),
    )
    out_specs = (P("vocab"), P(None, "vocab"), P("vocab", None))
    return jax.shard_map(
        on_device, mesh=mesh, in_specs=in_specs, out_specs=out_specs, check_vma=False
    )
```

profile of v0, /device:TPU:0, one launch (start us, length us, event | category | flops | bytes accessed | tf_op | source)
XLA Modules:
  0.0 357.8 jit_solution(12752503593705309650)
XLA Ops:
  7.2 0.0 copy-start
  7.2 0.0 all-gather.2.cloned.1.call-start
  7.2 0.7 all-gather.2.cloned.1.call-update
  7.9 0.2 copy-done
  8.1 1.3 convolution_convert_fusion
  9.4 0.0 copy-start.3
  9.4 1.8 copy.40
  11.2 7.3 %all-to-all-start = ((bf16[4,256,4,128]{3,2,0,1:T(4,128)(2,1)}), bf16[4,256,4,128]{3,2,0,1:T(4,128)(2,1)S(1)}, u32[]{:S(2)}, u32[]{:S(2)}) async-start(bf16[4,256,4,128]{3,2,0,1:T(4,128)(2,1)} %copy.40), calls=%async_computation | async-start | bytes 2097152 | tf_op jit(solution)/shard_map/all_to_all | solution.py:41
  18.5 0.0 reduce-scatter.2.cloned.1.call-start
  18.6 0.0 copy-done.3
  18.6 0.1 convert_reduce_fusion
  18.8 33.2 %all-to-all-done = bf16[4,256,4,128]{3,2,0,1:T(4,128)(2,1)S(1)} async-done(((bf16[4,256,4,128]{3,2,0,1:T(4,128)(2,1)}), bf16[4,256,4,128]{3,2,0,1:T(4,128)(2,1)S(1)}, u32[]{:S(2)}, u32[]{:S(2)}) %all-to-all-start) | async-done | bytes 1048608 | tf_op jit(solution)/shard_map/all_to_all | solution.py:41
  52.0 0.3 copy.66
  52.2 0.0 copy-start.6
  52.3 0.2 copy.42
  52.5 0.8 copy.43
  53.3 0.0 copy-done.6
  53.3 0.5 select_reduce_fusion.1
  53.7 29.2 %all-gather.2.cloned.1.call-done = bf16[512,5120]{1,0:T(8,128)(2,1)} async-done(((bf16[16,5120]{1,0:T(8,128)(2,1)}), bf16[512,5120]{1,0:T(8,128)(2,1)}) %all-gather.2.cloned.1.call-update) | async-done | bytes 5242896 | tf_op jit(solution)/shard_map/all_gather | solution.py:28
  82.9 10.0 %fusion.26 = (f32[512]{0:T(512)S(1)}, f32[512,1024]{1,0:T(8,128)S(1)}) fusion(bf16[512,5120]{1,0:T(8,128)(2,1)} %all-gather.2.cloned.1.call-done, bf16[5120,1024]{1,0:T(8,128)(2,1)} %param.8), kind=kOutput, calls=%fused_computation.49 | convolution fusion | flops 5369232896 | bytes 17827840 | tf_op jit(solution)/shard_map/dot_general | solution.py:29
  92.9 0.0 copy-start.2
  92.9 2.0 copy.51
  94.9 0.0 copy-done.2
  94.9 2.9 copy.44
  97.8 39.6 %all-reduce.1 = (f32[4,128]{1,0:T(4,128)S(1)}, f32[4,128]{1,0:T(4,128)S(1)}) all-reduce(f32[4,128]{1,0:T(4,128)S(1)} %bitcast.94, f32[4,128]{1,0:T(4,128)S(1)} %get-tuple-element.37), channel_id=1, replica_groups=mesh['vocab'=32] {'vocab'}, use_global_device_ids=true, to_apply=%region_14.15 | all-reduce | flops 1024 | bytes 8192 | tf_op jit(solution)/shard_map/pmax | solution.py:52
  137.4 0.0 copy-start.1
  137.4 0.2 broadcast_in_dim.50.clone
  137.6 2.5 select_reduce_fusion
  140.1 0.0 copy-done.1
  140.1 0.0 copy-start.5
  140.1 0.0 copy-start.4
  140.1 0.8 multiply_reduce_fusion.1
  140.9 39.9 %all-reduce = (f32[4,128]{1,0:T(4,128)S(1)}, f32[4,128]{1,0:T(4,128)S(1)}, f32[4,128]{1,0:T(4,128)S(1)}, f32[4,128]{1,0:T(4,128)S(1)}, f32[4,128]{1,0:T(4,128)S(1)}, /*index=5*/f32[4,128]{1,0:T(4,128)S(1)}) all-reduce(f32[4,128]{1,0:T(4,128)S(1)} %bitcast.91, f32[4,128]{1,0:T(4,128)S(1)} %bitcast.92, ...), channel_id=1, replica_groups=mesh['vocab'=32] {'vocab'}, use_global_device_ids=true, to_apply=%region_16.17 | all-reduce | flops 3072 | bytes 24576 | tf_op jit(solution)/shard_map/psum | solution.py:58
  180.8 0.0 copy-done.5
  180.8 0.0 copy-done.4
  180.8 2.6 multiply_convert_fusion
  183.4 0.7 copy.47
  184.2 12.2 %fusion.1 = f32[512,5120]{1,0:T(8,128)} fusion(bf16[5120,1024]{1,0:T(8,128)(2,1)} %param.8, bf16[64,8,8,128]{3,2,1,0:T(8,128)(2,1)S(1)} %bitcast.87), kind=kOutput, calls=%fused_computation.10 | convolution fusion | flops 5368709120 | bytes 22020096 | tf_op jit(solution)/shard_map/dot_general | solution.py:90
  196.4 0.0 reduce-scatter.2.cloned.1.call-update
  196.4 10.7 %convert_bitcast_fusion = bf16[5120,1024]{0,1:T(8,128)(2,1)} fusion(bf16[512,5120]{1,0:T(8,128)(2,1)} %all-gather.2.cloned.1.call-done, bf16[64,8,8,128]{3,2,1,0:T(8,128)(2,1)S(1)} %bitcast.88), kind=kOutput, calls=%fused_computation | convolution fusion | flops 5373952000 | bytes 16777216 | tf_op jit(solution)/shard_map/dot_general | solution.py:86
  207.1 14.4 %copy.48 = bf16[5120,1024]{1,0:T(8,128)(2,1)} copy(bf16[5120,1024]{0,1:T(8,128)(2,1)} %convert_bitcast_fusion) | data formatting | bytes 20971520
  221.5 0.6 dynamic_slice.3
  222.1 127.3 %reduce-scatter.2.cloned.1.call-done = f32[16,5120]{1,0:T(8,128)} async-done(((f32[512,5120]{1,0:T(8,128)}), f32[16,5120]{1,0:T(8,128)}) %reduce-scatter.2.cloned.1.call-update) | async-done | bytes 327696 | tf_op jit(solution)/shard_map/reduce_scatter | solution.py:89
  349.3 1.7 convert_element_type.25
  (4 shorter events, 0.0 us)
Async XLA Ops:
  7.2 1.0 copy-start
  7.2 75.7 %all-gather.2.cloned.1.call-start = ((), (), s32[]{:S(2)}) async-start(), calls=%async_computation.2 | async-start | bytes 5406720 | tf_op jit(solution)/shard_map/all_gather | solution.py:28
  9.4 9.2 %copy-start.3 = (s32[4,64]{1,0:T(4,128)S(1)}, s32[4,64]{1,0:T(4,128)}, u32[]{:S(2)}) copy-start(s32[4,64]{1,0:T(4,128)} %param.10) | copy-start | bytes 3076
  11.2 40.8 %all-to-all-start = ((bf16[4,256,4,128]{3,2,0,1:T(4,128)(2,1)}), bf16[4,256,4,128]{3,2,0,1:T(4,128)(2,1)S(1)}, u32[]{:S(2)}, u32[]{:S(2)}) async-start(bf16[4,256,4,128]{3,2,0,1:T(4,128)(2,1)} %copy.40), calls=%async_computation | async-start | bytes 2097152 | tf_op jit(solution)/shard_map/all_to_all | solution.py:41
  18.5 330.8 %reduce-scatter.2.cloned.1.call-start = ((), (), s32[]{:S(2)}) async-start(), calls=%async_computation.3 | async-start | bytes 10813440 | tf_op jit(solution)/shard_map/reduce_scatter | solution.py:89
  52.2 1.0 copy-start.6
  92.9 2.0 copy-start.2
  137.4 2.7 copy-start.1
  140.1 40.7 %copy-start.5 = (f32[512]{0:T(512)S(1)}, f32[512]{0:T(512)}, u32[]{:S(2)}) copy-start(f32[512]{0:T(512)} %param.12) | copy-start | bytes 6148
  140.1 40.7 %copy-start.4 = (f32[512]{0:T(512)S(1)}, f32[512]{0:T(512)}, u32[]{:S(2)}) copy-start(f32[512]{0:T(512)} %param.13) | copy-start | bytes 6148
Sparse Core Ops, SparseCore 0:
  10.9 71.9 all-gather.1
  196.5 152.7 reduce-scatter.1
where the time goes:
time: 359 us; the launch traced here: 358 us
  waiting for transfers between devices  190 us (53%)
  blocking collectives  79.5 us (22%)
  matrix products  34.6 us (10%)
  local copies, waits for them, and re-layouts  24.1 us (7%)
  between operations  14.2 us (4%)
  other arithmetic  7.69 us (2%)
  starting transfers between devices  7.38 us (2%)
    reduce_scatter x1, waiting for transfers between devices, on_device(): lax.psum_scatter(lax.dot_general(grad_logits, head_weight, (((1,), (1,)),...  127 us
    psum x1, blocking collectives, on_device(): lax.psum((parts[0], parts[1], parts[2], parts[3], parts[4], parts[5]), 'v...  39.9 us
    pmax x1, blocking collectives, on_device(): student_max, teacher_max = lax.pmax((local_smax, local_tmax), 'vocab')  39.6 us
    all_to_all x1, waiting for transfers between devices, on_device(): lax.all_to_all(outgoing, 'vocab', split_axis=1, concat_axis=2, tiled=True)  33.2 us
    all_gather x1, waiting for transfers between devices, on_device(): gathered = lax.all_gather(hidden_states, 'vocab', axis=0, tiled=True)  29.2 us
    unnamed x16, local copies, waits for them, and re-layouts  16.7 us
    dot_general x1, matrix products, on_device(): lax.dot_general(grad_logits, head_weight, (((1,), (1,)), ((), ())), prefe...  12.2 us
    dot_general x1, matrix products, on_device(): lax.dot_general(gathered, grad_logits, (((0,), (0,)), ((), ())), preferre...  10.7 us
  transfers between devices with their start and end apart: 3, of which 3 were waited for; matrix products, arithmetic and copies ran while one was open for 9% of the time, Pallas kernels for 0%

commit v1 on v0

--- a/solution.py
+++ b/solution.py
@@ -1,6 +1,8 @@
 import jax
 import jax.numpy as jnp
 from jax import lax
+from jax.experimental import pallas as pl
+from jax.experimental.pallas import tpu as pltpu
 from jax.sharding import PartitionSpec as P
 
 
@@ -15,7 +17,7 @@
     )
 
 
-def on_device(
+def plain_plan(
     hidden_states, head_weight, teacher_logits, block_lists, row_reader, tail_mass, token_weight
 ):
     blocks, listed_count, stored_rows, block_side = teacher_logits.shape
@@ -97,6 +99,440 @@
     return (token_loss, grad_head, grad_hidden)
 
 
+CORES = 2
+CHIPS = 4
+GROUP = CORES * CHIPS
+SLOTS = 4
+VMEM_LIMIT = 48 * 1024 * 1024
+
+
+def kernel_params():
+    return pltpu.CompilerParams(vmem_limit_bytes=VMEM_LIMIT)
+
+
+def vmem_spec():
+    return pl.BlockSpec(memory_space=pltpu.VMEM)
+
+
+def smem_spec():
+    return pl.BlockSpec(memory_space=pltpu.SMEM)
+
+
+def shift(x, distance):
+    n = lax.axis_size("vocab")
+    return lax.ppermute(x, "vocab", [(i, i ^ distance) for i in range(n)])
+
+
+def tile_of(size):
+    return 512 if size % 512 == 0 else 128
+
+
+def token_places(place, rows, side):
+    row = lax.broadcasted_iota(jnp.int32, (side, 1), 0)
+    group = row // rows
+    chip = (group % CHIPS) ^ place[1]
+    core = (group // CHIPS) ^ place[0]
+    return (chip * CORES + core) * rows + row % rows
+
+
+def pick_column(match, values):
+    return jnp.sum(jnp.where(match, values, 0.0), axis=1, keepdims=True)
+
+
+def teacher_kernel(
+    unlisted, rows, pos_ref, place_ref, blocks_ref, stat_ref, reader_ref, tail_ref, prob_ref, entropy_ref
+):
+    layers, slots, side, _ = blocks_ref.shape
+    pos = [pos_ref[i] for i in range(3)]
+    lane = lax.broadcasted_iota(jnp.int32, (1, side), 1)
+    where_token = token_places(pos, rows, side)
+    for k in range(layers):
+        block = pos[2] ^ k
+        match = reader_ref[block] == where_token
+        onehot = jnp.where(match, 1.0, 0.0).astype(jnp.bfloat16)
+        normaliser = pick_column(match, stat_ref[0, block])
+        tail = pick_column(lane == where_token, tail_ref[block])
+        kept = 1.0 - tail
+        rest = tail / unlisted
+        span = pl.ds(k * side, side)
+        prob_ref[span, :] = jnp.broadcast_to(rest, (side, prob_ref.shape[1]))
+        for s in range(slots):
+            place = place_ref[block, s]
+            values = jnp.dot(onehot, blocks_ref[block, s], preferred_element_type=jnp.float32)
+            prob = kept * jnp.exp(values - normaliser)
+
+            @pl.when(place >= 0)
+            def _():
+                prob_ref[span, pl.ds(pl.multiple_of(place * side, side), side)] = prob
+
+        if k == 0:
+            mean = pick_column(match, stat_ref[1, block])
+            entropy = kept * (jnp.log(kept) - normaliser + mean) + tail * jnp.log(rest)
+            entropy_ref[...] = jnp.broadcast_to(entropy[:rows], entropy_ref.shape)
+
+
+def assemble(pieces, rows, out_ref):
+    layers = pieces[0].shape[0] // rows
+    for k in range(layers):
+        for p, piece in enumerate(pieces):
+            out_ref[pl.ds((k * GROUP + p) * rows, rows), :] = piece[pl.ds(k * rows, rows), :]
+
+
+def logits_kernel(rows, *refs):
+    pieces = refs[:GROUP]
+    w_ref, prob_ref, logits_ref, stat_ref, hidden = refs[GROUP:]
+    step = pl.program_id(0)
+    assemble(pieces, rows, hidden)
+    part = jnp.dot(hidden[...], w_ref[...], preferred_element_type=jnp.float32)
+
+    @pl.when(step == 0)
+    def _():
+        logits_ref[...] = part
+
+    @pl.when(step > 0)
+    def _():
+        logits_ref[...] += part
+
+    @pl.when(step == pl.num_programs(0) - 1)
+    def _():
+        logits = logits_ref[...]
+        top = jnp.max(logits, axis=1, keepdims=True)
+        norm = top + jnp.log(jnp.sum(jnp.exp(logits - top), axis=1, keepdims=True))
+        cross = jnp.sum(prob_ref[...] * logits, axis=1, keepdims=True)
+        lane = lax.broadcasted_iota(jnp.int32, (1, 128), 1)
+        both = jnp.where(lane == 0, norm, jnp.where(lane == 1, cross, 0.0))
+        stat_ref[...] = both.T[:2]
+
+
+def grad_kernel(
+    rows, pos_ref, own_ref, sib_ref, logits_ref, prob_ref, weight_ref, entropy_ref, grad_ref, loss_ref
+):
+    tokens = logits_ref.shape[0]
+    devices = tokens // rows
+    layers, _, side = weight_ref.shape
+    layer_bits = (devices // GROUP).bit_length() - 1
+    pos = [pos_ref[i] for i in range(3)]
+    lane = lax.broadcasted_iota(jnp.int32, (1, 128), 1)
+    stat = jnp.concatenate(
+        [own_ref[...], sib_ref[...], jnp.zeros((128 - 2 * devices, tokens), jnp.float32)], axis=0
+    ).T
+    pairs = [(1 + i, 3 + i) for i in range(layer_bits)]
+    pairs += [(1 + layer_bits, 0), (2 + layer_bits, 1), (3 + layer_bits, 2)]
+    for lane_bit, block_bit in pairs:
+        halves = stat.reshape(devices >> (block_bit + 1), 2, rows << block_bit, 128)
+        swapped = jnp.stack([halves[:, 1], halves[:, 0]], axis=1).reshape(tokens, 128)
+        stat = jnp.where((lane >> lane_bit) & 1 == 1, swapped, stat)
+    used = lane < 2 * devices
+    is_norm = used & (lane % 2 == 0)
+    top = jnp.max(jnp.where(is_norm, stat, -jnp.inf), axis=1, keepdims=True)
+    total = jnp.sum(jnp.where(is_norm, jnp.exp(stat - top), 0.0), axis=1, keepdims=True)
+    log_norm = top + jnp.log(total)
+    cross = jnp.sum(jnp.where(used & (lane % 2 == 1), stat, 0.0), axis=1, keepdims=True)
+    loss_ref[...] = entropy_ref[...] - cross[:rows] + log_norm[:rows]
+    where_token = token_places(pos, rows, side)
+    for k in range(layers):
+        span = pl.ds(k * side, side)
+        weight = pick_column(lane == where_token, weight_ref[pos[2] ^ k])
+        student = jnp.exp(logits_ref[span, :] - log_norm[k * side : (k + 1) * side])
+        grad_ref[span, :] = (weight * (student - prob_ref[span, :])).astype(grad_ref.dtype)
+
+
+def partial_kernel(rows, core_ref, grad_ref, sib_ref, w_ref, sib_w_ref, *refs):
+    outs, swapped = refs[:CHIPS], refs[CHIPS]
+    layers = outs[0].shape[0]
+    half = CHIPS * rows
+
+    @pl.when(pl.program_id(0) == 0)
+    def _():
+        for k in range(layers):
+            for core in range(CORES):
+                swapped[pl.ds((k * CORES + core) * half, half), :] = sib_ref[
+                    pl.ds((k * CORES + 1 - core) * half, half), :
+                ]
+
+    contract = (((1,), (1,)), ((), ()))
+    total = lax.dot_general(
+        grad_ref[...], w_ref[...], contract, preferred_element_type=jnp.float32
+    ) + lax.dot_general(
+        swapped[...], sib_w_ref[...], contract, preferred_element_type=jnp.float32
+    )
+    for j, out in enumerate(outs):
+        for k in range(layers):
+            for core in range(CORES):
+                start = (k * GROUP + core * CHIPS + j) * rows
+                out[k, core] = total[start : start + rows].astype(out.dtype)
+
+
+def head_kernel(rows, *refs):
+    pieces = refs[:GROUP]
+    grad_ref, out_ref, hidden = refs[GROUP:]
+    assemble(pieces, rows, hidden)
+    out_ref[...] = lax.dot_general(
+        hidden[...], grad_ref[...], (((0,), (0,)), ((), ())), preferred_element_type=jnp.float32
+    ).astype(out_ref.dtype)
+
+
+def chip_sum_kernel(own_ref, *refs):
+    arrived, outs = refs[: CHIPS - 1], refs[CHIPS - 1 :]
+    for k, out in enumerate(outs):
+        total = own_ref[k]
+        for part in arrived:
+            total = total + part[k].astype(jnp.float32)
+        out[...] = total.astype(out.dtype)
+
+
+def layer_sum_kernel(own_ref, *refs):
+    arrived, (mine, theirs) = refs[:-2], refs[-2:]
+    total = own_ref[...]
+    for part in arrived:
+        total = total + part[...].astype(jnp.float32)
+    mine[...] = total[0].astype(mine.dtype)
+    theirs[...] = total[1].astype(theirs.dtype)
+
+
+def split_three(x):
+    high = lax.reduce_precision(x, 8, 7)
+    middle = lax.reduce_precision(x - high, 8, 7)
+    low = x - high - middle
+    return jnp.stack([high, middle, low]).astype(jnp.bfloat16)
+
+
+def send_teacher(teacher_logits, block_lists, places):
+    blocks, listed_count, stored, side = teacher_logits.shape
+    n = lax.axis_size("vocab")
+    rank = lax.axis_index("vocab")
+    owner = block_lists // places
+    earlier = jnp.tril(jnp.ones((listed_count, listed_count), jnp.bool_), -1)
+    slot = jnp.sum((owner[:, :, None] == owner[:, None, :]) & earlier, axis=2, dtype=jnp.int32)
+    code = owner * SLOTS + slot
+    picker = (code[:, None, :] == jnp.arange(n * SLOTS, dtype=jnp.int32)[None, :, None]).astype(jnp.bfloat16)
+    packed = jnp.einsum(
+        "tsk,tkrc->tsrc", picker, teacher_logits, preferred_element_type=jnp.float32
+    ).astype(jnp.bfloat16)
+    packed = packed.reshape(blocks, n, SLOTS * stored, side).transpose(1, 0, 2, 3)
+    values = teacher_logits.astype(jnp.float32)
+    top = jnp.max(values, axis=(1, 3))
+    powers = jnp.exp(values - top[:, None, :, None])
+    total = jnp.sum(powers, axis=(1, 3))
+    mean = jnp.sum(powers * values, axis=(1, 3)) / total
+    stat = split_three(jnp.stack([top + jnp.log(total), mean])).reshape(-1)
+    stat = jnp.pad(stat, (0, side - stat.shape[0]))
+    payload = jnp.concatenate(
+        [packed.reshape(n, -1, side), jnp.broadcast_to(stat, (n, 1, side))], axis=1
+    )
+    arrived = lax.all_to_all(payload, "vocab", split_axis=0, concat_axis=0, tiled=True)
+    arrived_blocks = (
+        arrived[:, :-1]
+        .reshape(n, blocks, SLOTS, stored, side)
+        .transpose(1, 2, 0, 3, 4)
+        .reshape(blocks, SLOTS, n * stored, side)
+    )
+    arrived_stat = (
+        arrived[:, -1, : 6 * blocks * stored]
+        .astype(jnp.float32)
+        .reshape(n, 3, 2, blocks, stored)
+        .sum(axis=1)
+        .transpose(1, 2, 0, 3)
+        .reshape(2, blocks, 1, n * stored)
+    )
+    mine = code[:, None, :] == rank * SLOTS + jnp.arange(SLOTS, dtype=jnp.int32)[None, :, None]
+    place = jnp.sum(jnp.where(mine, (block_lists % places + 1)[:, None, :], 0), axis=2) - 1
+    return arrived_blocks, arrived_stat, place.astype(jnp.int32)
+
+
+def levels_plan(
+    hidden_states, head_weight, teacher_logits, block_lists, row_reader, tail_mass, token_weight
+):
+    blocks, listed_count, stored, side = teacher_logits.shape
+    rows, depth = hidden_states.shape
+    slab = head_weight.shape[1]
+    n = lax.axis_size("vocab")
+    rank = lax.axis_index("vocab")
+    tokens = n * rows
+    layers = n // GROUP
+    half = depth // CORES
+    bf16, f32 = jnp.bfloat16, jnp.float32
+    core, chip, layer = rank % CORES, (rank // CORES) % CHIPS, rank // GROUP
+    pos = jnp.stack([core, chip, layer]).astype(jnp.int32)
+    unlisted = float(n * slab - side * listed_count)
+
+    column = [hidden_states] + [shift(hidden_states, k * GROUP) for k in range(1, layers)]
+    column = jnp.concatenate(column, axis=0)
+    pieces = [column] + [shift(column, j * CORES) for j in range(1, CHIPS)]
+    pieces = pieces + [shift(piece, 1) for piece in pieces]
+
+    arrived_blocks, arrived_stat, place = send_teacher(teacher_logits, block_lists, slab // side)
+    sib_w = shift(lax.dynamic_slice(head_weight, ((1 - core) * half, 0), (half, slab)), 1)
+
+    prob, entropy = pl.pallas_call(
+        lambda *refs: teacher_kernel(unlisted, rows, *refs),
+        out_shape=(
+            jax.ShapeDtypeStruct((tokens, slab), f32),
+            jax.ShapeDtypeStruct((rows, side), f32),
+        ),
+        in_specs=[smem_spec(), smem_spec()] + [vmem_spec()] * 4,
+        out_specs=(vmem_spec(), vmem_spec()),
+        compiler_params=kernel_params(),
+        cost_estimate=pl.CostEstimate(
+            flops=2 * tokens * side * side * SLOTS, bytes_accessed=4 * tokens * slab, transcendentals=0
+        ),
+        name="teacher_prob",
+    )(
+        pos,
+        place,
+        arrived_blocks,
+        arrived_stat,
+        row_reader.reshape(blocks, 1, side),
+        tail_mass.reshape(blocks, 1, side),
+    )
+
+    tile = tile_of(depth)
+    piece_specs = [pl.BlockSpec((layers * rows, tile), lambda t: (0, t)) for _ in range(GROUP)]
+    whole = lambda t: (0, 0)
+    logits, stat = pl.pallas_call(
+        lambda *refs: logits_kernel(rows, *refs),
+        grid=(depth // tile,),
+        out_shape=(
+            jax.ShapeDtypeStruct((tokens, slab), f32),
+            jax.ShapeDtypeStruct((2, tokens), f32),
+        ),
+        in_specs=piece_specs
+        + [pl.BlockSpec((tile, slab), lambda t: (t, 0)), pl.BlockSpec((tokens, slab), whole)],
+        out_specs=(pl.BlockSpec((tokens, slab), whole), pl.BlockSpec((2, tokens), whole)),
+        scratch_shapes=[pltpu.VMEM((tokens, tile), bf16)],
+        compiler_params=kernel_params(),
+        cost_estimate=pl.CostEstimate(
+            flops=2 * tokens * depth * slab,
+            bytes_accessed=2 * depth * (slab + tokens) + 4 * tokens * slab,
+            transcendentals=tokens * slab,
+        ),
+        name="logits",
+    )(*pieces, head_weight, prob)
+
+    stat = jnp.concatenate([stat] + [shift(stat, k * GROUP) for k in range(1, layers)], axis=0)
+    stat = jnp.concatenate([stat] + [shift(stat, j * CORES) for j in range(1, CHIPS)], axis=0)
+    sib_stat = shift(stat, 1)
+
+    grad, loss = pl.pallas_call(
+        lambda *refs: grad_kernel(rows, *refs),
+        out_shape=(
+            jax.ShapeDtypeStruct((tokens, slab), bf16),
+            jax.ShapeDtypeStruct((rows, side), f32),
+        ),
+        in_specs=[smem_spec()] + [vmem_spec()] * 6,
+        out_specs=(vmem_spec(), vmem_spec()),
+        compiler_params=kernel_params(),
+        cost_estimate=pl.CostEstimate(
+            flops=4 * tokens * slab, bytes_accessed=10 * tokens * slab, transcendentals=tokens * slab
+        ),
+        name="grad_logits",
+    )(pos, stat, sib_stat, logits, prob, token_weight.reshape(blocks, 1, side), entropy)
+    sib_grad = shift(grad, 1)
+
+    tile = tile_of(half)
+    steps = half // tile
+    out_block = pl.BlockSpec((layers, CORES, rows, tile), lambda t, core: (0, 0, 0, t))
+    partial = pl.pallas_call(
+        lambda *refs: partial_kernel(rows, *refs),
+        grid_spec=pltpu.PrefetchScalarGridSpec(
+            num_scalar_prefetch=1,
+            grid=(steps,),
+            in_specs=[
+                pl.BlockSpec((tokens, slab), lambda t, core: (0, 0)),
+                pl.BlockSpec((tokens, slab), lambda t, core: (0, 0)),
+                pl.BlockSpec((tile, slab), lambda t, core: (core[0] * steps + t, 0)),
+                pl.BlockSpec((tile, slab), lambda t, core: (t, 0)),
+            ],
+            out_specs=[out_block] * CHIPS,
+            scratch_shapes=[pltpu.VMEM((tokens, slab), bf16)],
+        ),
+        out_shape=[
+            jax.ShapeDtypeStruct((layers, CORES, rows, half), f32 if j == 0 else bf16)
+            for j in range(CHIPS)
+        ],
+        compiler_params=kernel_params(),
+        cost_estimate=pl.CostEstimate(
+            flops=4 * tokens * half * slab, bytes_accessed=4 * half * slab, transcendentals=0
+        ),
+        name="grad_hidden_partial",
+    )(pos[:1], grad, sib_grad, head_weight, sib_w)
+
+    arrived = [shift(partial[j], j * CORES) for j in range(1, CHIPS)]
+    chip_block = pl.BlockSpec((layers, CORES, rows, tile), lambda t: (0, 0, 0, t))
+    layer_block = pl.BlockSpec((CORES, rows, tile), lambda t: (0, 0, t))
+    summed = pl.pallas_call(
+        chip_sum_kernel,
+        grid=(steps,),
+        in_specs=[chip_block] * CHIPS,
+        out_specs=[layer_block] * layers,
+        out_shape=[
+            jax.ShapeDtypeStruct((CORES, rows, half), f32 if k == 0 else bf16) for k in range(layers)
+        ],
+        compiler_params=kernel_params(),
+        cost_estimate=pl.CostEstimate(
+            flops=tokens * half, bytes_accessed=3 * tokens * half, transcendentals=0
+        ),
+        name="chip_sum",
+    )(partial[0], *arrived)
+    arrived = [shift(summed[k], k * GROUP) for k in range(1, layers)]
+    row_block = pl.BlockSpec((rows, tile), lambda t: (0, t))
+    mine, theirs = pl.pallas_call(
+        layer_sum_kernel,
+        grid=(steps,),
+        in_specs=[layer_block] * layers,
+        out_specs=[row_block] * CORES,
+        out_shape=[jax.ShapeDtypeStruct((rows, half), bf16)] * CORES,
+        compiler_params=kernel_params(),
+        cost_estimate=pl.CostEstimate(
+            flops=CORES * layers * rows * half, bytes_accessed=3 * CORES * layers * rows * half, transcendentals=0
+        ),
+        name="layer_sum",
+    )(summed[0], *arrived)
+    other = shift(theirs, 1)
+
+    tile = tile_of(depth)
+    grad_head = pl.pallas_call(
+        lambda *refs: head_kernel(rows, *refs),
+        grid=(depth // tile,),
+        in_specs=piece_specs + [pl.BlockSpec((tokens, slab), whole)],
+        out_specs=pl.BlockSpec((tile, slab), lambda t: (t, 0)),
+        out_shape=jax.ShapeDtypeStruct((depth, slab), bf16),
+        scratch_shapes=[pltpu.VMEM((tokens, tile), bf16)],
+        compiler_params=kernel_params(),
+        cost_estimate=pl.CostEstimate(
+            flops=2 * tokens * depth * slab, bytes_accessed=2 * depth * (slab + tokens), transcendentals=0
+        ),
+        name="grad_head",
+    )(*pieces, grad)
+
+    low, high = jnp.where(core == 0, mine, other), jnp.where(core == 0, other, mine)
+    return loss[:, 0], grad_head, jnp.concatenate([low, high], axis=1)
+
+
+def fits_levels(hidden_states, teacher_logits):
+    n = lax.axis_size("vocab")
+    rows = hidden_states.shape[0]
+    blocks, _, stored, side = teacher_logits.shape
+    return (
+        n == blocks * GROUP
+        and blocks & (blocks - 1) == 0
+        and rows * GROUP == side
+        and rows % 16 == 0
+        and 2 * n <= side
+        and 6 * blocks * stored <= side
+        and hidden_states.shape[1] % (CORES * 128) == 0
+    )
+
+
+def on_device(
+    hidden_states, head_weight, teacher_logits, block_lists, row_reader, tail_mass, token_weight
+):
+    plan = levels_plan if fits_levels(hidden_states, teacher_logits) else plain_plan
+    return plan(
+        hidden_states, head_weight, teacher_logits, block_lists, row_reader, tail_mass, token_weight
+    )
+
+
 def solution(mesh):
     in_specs = (
         P("vocab", None),

time: 359 us -> 172 us (0.48)
  waiting for transfers between devices: 190 us -> 70.2 us
  blocking collectives: 79.5 us -> 0 us
  Pallas kernels: 0 us -> 42.8 us
  matrix products: 34.6 us -> 0.45 us
  starting transfers between devices: 7.38 us -> 34.2 us
  between operations: 14.2 us -> 1.04 us
  local copies, waits for them, and re-layouts: 24.1 us -> 19.1 us
  other arithmetic: 7.69 us -> 3.02 us
    reduce_scatter x1 -> x0, waiting for transfers between devices: 127 us -> none  [on_device(): lax.psum_scatter(lax.dot_general(grad_logits, head_weight, (((1,), (1,)),...]
    ppermute x0 -> x26, waiting for transfers between devices: none -> 69.6 us  [shift(): return lax.ppermute(x, 'vocab', [(i, i ^ distance) for i in range(n)])]
    pallas_call x0 -> x7, Pallas kernels: none -> 42.8 us  [the longest x1 15.5 us: levels_plan(): pl.pallas_call(lambda *refs: logits_kernel(rows, *refs), grid=(depth // t...]
    psum x1 -> x0, blocking collectives: 39.9 us -> none  [on_device(): lax.psum((parts[0], parts[1], parts[2], parts[3], parts[4], parts[5]), 'v...]
    pmax x1 -> x0, blocking collectives: 39.6 us -> none  [on_device(): student_max, teacher_max = lax.pmax((local_smax, local_tmax), 'vocab')]
    dot_general x4 -> x1, matrix products: 34.1 us -> 0.45 us  [send_teacher(): jnp.einsum('tsk,tkrc->tsrc', picker, teacher_logits, preferred_element_ty...]
    all_to_all x1, waiting for transfers between devices: 33.2 us -> 0.55 us  [send_teacher(): lax.all_to_all(payload, 'vocab', split_axis=0, concat_axis=0, tiled=True)]
    all_gather x1 -> x0, waiting for transfers between devices: 29.2 us -> none  [on_device(): gathered = lax.all_gather(hidden_states, 'vocab', axis=0, tiled=True)]
  transfers between devices with their start and end apart: 3 -> 27, of which waited for: 3 -> 15; matrix products, arithmetic and copies ran while one was open for 9% -> 7% of each run, Pallas kernels for 0% -> 19%
where the time goes in v1:
time: 172 us; the launch traced here: 171 us
  waiting for transfers between devices  70.2 us (41%)
  Pallas kernels  42.8 us (25%)
  starting transfers between devices  34.2 us (20%)
  local copies, waits for them, and re-layouts  19.1 us (11%)
  other arithmetic  3.02 us (2%)
    ppermute x26, waiting for transfers between devices, shift(): return lax.ppermute(x, 'vocab', [(i, i ^ distance) for i in range(n)])  69.6 us
    ppermute x26, starting transfers between devices, shift(): return lax.ppermute(x, 'vocab', [(i, i ^ distance) for i in range(n)])  28.2 us
    pallas_call x1, Pallas kernels, levels_plan(): pl.pallas_call(lambda *refs: logits_kernel(rows, *refs), grid=(depth // t...  15.5 us
    pallas_call x1, Pallas kernels, levels_plan(): pl.pallas_call(lambda *refs: head_kernel(rows, *refs), grid=(depth // til...  12.3 us
    unnamed x44, local copies, waits for them, and re-layouts  9.85 us
    pallas_call x1, Pallas kernels, levels_plan(): pl.pallas_call(lambda *refs: partial_kernel(rows, *refs), grid_spec=pltpu...  9.65 us
    all_to_all x1, starting transfers between devices, send_teacher(): lax.all_to_all(payload, 'vocab', split_axis=0, concat_axis=0, tiled=True)  5.99 us
    dynamic_slice x1, local copies, waits for them, and re-layouts, levels_plan(): lax.dynamic_slice(head_weight, ((1 - core) * half, 0), (half, slab))  5.47 us
  transfers between devices with their start and end apart: 27, of which 15 were waited for; matrix products, arithmetic and copies ran while one was open for 7% of the time, Pallas kernels for 19%

profile of v1, /device:TPU:0, one launch (start us, length us, event | category | flops | bytes accessed | tf_op | source)
XLA Modules:
  0.0 170.7 jit_solution(12242532554057298222)
XLA Ops:
  0.6 3.1 %collective-permute-start = (bf16[16,5120]{1,0:T(8,128)(2,1)}, bf16[16,5120]{1,0:T(8,128)(2,1)S(1)}, u32[]{:S(2)}, u32[]{:S(2)}) collective-permute-start(bf16[16,5120]{1,0:T(8,128)(2,1)} %param.7), channel_id=1, source_target_pairs={{0,8},{1,9},{2,10},{3,11},{4,12},{5,13},{6,14},{7,15},{8,0},{9,1},... | collective-permute-start | bytes 491528 | tf_op jit(solution)/shard_map/ppermute | solution.py:123
  3.7 2.6 %collective-permute-start.1 = (bf16[16,5120]{1,0:T(8,128)(2,1)}, bf16[16,5120]{1,0:T(8,128)(2,1)S(1)}, u32[]{:S(2)}, u32[]{:S(2)}) collective-permute-start(bf16[16,5120]{1,0:T(8,128)(2,1)} %param.7), channel_id=1, source_target_pairs={{0,16},{1,17},{2,18},{3,19},{4,20},{5,21},{6,22},{7,23},{8,24},{9,... | collective-permute-start | bytes 491528 | tf_op jit(solution)/shard_map/ppermute | solution.py:123
  6.3 5.5 %constant_dynamic-slice_fusion = bf16[2560,1024]{1,0:T(8,128)(2,1)} fusion(bf16[5120,1024]{1,0:T(8,128)(2,1)} %refs_3_.1, s32[]{:T(128)S(6)} %select_n.58), kind=kLoop, calls=%fused_computation.47 | loop fusion | bytes 10485764 | tf_op jit(solution)/shard_map/dynamic_slice | solution.py:365
  11.9 0.2 reduce_max.14
  12.1 0.5 fusion.1
  12.9 0.2 convert_reduce_fusion
  13.1 0.4 convolution_convert_fusion
  13.6 0.4 copy.43
  14.1 4.9 %collective-permute-done.1 = bf16[16,5120]{1,0:T(8,128)(2,1)S(1)} collective-permute-done((bf16[16,5120]{1,0:T(8,128)(2,1)}, bf16[16,5120]{1,0:T(8,128)(2,1)S(1)}, u32[]{:S(2)}, u32[]{:S(2)}) %collective-permute-start.1) | collective-permute-done | bytes 163872 | tf_op jit(solution)/shard_map/ppermute | solution.py:123
  19.0 1.6 collective-permute-start.3
  20.6 1.5 collective-permute-start.4
  22.1 0.5 collective-permute-start.5
  22.6 0.9 pad_maximum_fusion
  23.5 6.0 %all-to-all-start = ((bf16[32,65,128]{2,1,0:T(8,128)(2,1)}), bf16[32,65,128]{2,1,0:T(8,128)(2,1)}, u32[]{:S(2)}, u32[]{:S(2)}) async-start(bf16[32,65,128]{2,1,0:T(8,128)(2,1)} %pad_maximum_fusion), calls=%async_computation | async-start | bytes 1179648 | tf_op jit(solution)/shard_map/all_to_all | solution.py:323
  29.5 0.3 collective-permute-start.6
  29.8 10.2 %collective-permute-done.3.refs_1_ = bf16[64,5120]{1,0:T(8,128)(2,1)S(1)} collective-permute-done((bf16[64,5120]{1,0:T(8,128)(2,1)S(1)}, bf16[64,5120]{1,0:T(8,128)(2,1)S(1)}, u32[]{:S(2)}, u32[]{:S(2)}) %collective-permute-start.3) | collective-permute-done | bytes 655392 | tf_op jit(solution)/shard_map/ppermute | solution.py:123
  39.9 13.4 %collective-permute-done.4.refs_2_ = bf16[64,5120]{1,0:T(8,128)(2,1)S(1)} collective-permute-done((bf16[64,5120]{1,0:T(8,128)(2,1)S(1)}, bf16[64,5120]{1,0:T(8,128)(2,1)S(1)}, u32[]{:S(2)}, u32[]{:S(2)}) %collective-permute-start.4) | collective-permute-done | bytes 655392 | tf_op jit(solution)/shard_map/ppermute | solution.py:123
  53.3 0.6 collective-permute-done.5.refs_3_
  54.0 0.2 select_reduce_fusion
  54.2 0.6 all-to-all-done
  54.8 1.1 slice.12
  55.8 0.3 copy.52
  56.2 0.3 copy.46
  56.5 0.9 slice.13
  57.7 3.1 %teacher_prob.1 = (f32[512,1024]{1,0:T(8,128)S(1)}, f32[16,128]{1,0:T(8,128)S(1)}) custom-call(s32[3]{0:T(128)S(1)} %pad_add_fusion.refs_0_, s32[4,4]{1,0:T(4,128)S(1)} %broadcast_add_fusion.refs_1_, bf16[4,4,128,128]{3,2,1,0:T(8,128)(2,1)S(1)} %bitcast.28, f32[2,4,1,128]{3,2,1,0:T(1,128)S(1)} %bitcast.29, s32[4,1,128]{2,1,0:T(1,128)S(1)} %bitcast.30, ...), custom_call_target="tpu_custom_call" | custom-call | flops 67108864 | bytes 2097152 | tf_op jit(solution)/shard_map/teacher_prob/pallas_call | solution.py:367
  60.8 1.3 copy-done
  62.2 1.1 copy-done.12
  63.2 1.1 copy-done.15
  64.3 15.5 %logits.1 = (f32[512,1024]{1,0:T(8,128)}, f32[2,512]{1,0:T(2,128)S(1)}) custom-call(bf16[64,5120]{1,0:T(8,128)(2,1)S(1)} %constant_dynamic-update-slice_fusion.refs_0_, bf16[64,5120]{1,0:T(8,128)(2,1)S(1)} %collective-permute-done.3.refs_1_, bf16[64,5120]{1,0:T(8,128)(2,1)S(1)} %copy-done.12, bf16[64,5120]{1,0:T(8,128)(2,1)S(1)} %copy-done.15, ...), custom_call_target="tpu_custom_call" | custom-call | flops 5368709120 | bytes 17825792 | tf_op jit(solution)/shard_map/logits/pallas_call | solution.py:392
  79.8 4.2 %collective-permute-start.10 = (f32[2,512]{1,0:T(2,128)S(1)}, f32[2,512]{1,0:T(2,128)S(1)}, u32[]{:S(2)}, u32[]{:S(2)}) collective-permute-start(f32[2,512]{1,0:T(2,128)S(1)} %get-tuple-element.20), channel_id=1, source_target_pairs={{0,8},{1,9},{2,10},{3,11},{4,12},{5,13},{6,14},{7,15},{8,0},{9,1},... | collective-permute-start | bytes 12296 | tf_op jit(solution)/shard_map/ppermute | solution.py:123
  84.0 1.2 collective-permute-start.11
  85.3 1.4 collective-permute-start.12
  86.7 1.9 %collective-permute-done.11 = f32[2,512]{1,0:T(2,128)S(1)} collective-permute-done((f32[2,512]{1,0:T(2,128)S(1)}, f32[2,512]{1,0:T(2,128)S(1)}, u32[]{:S(2)}, u32[]{:S(2)}) %collective-permute-start.11) | collective-permute-done | bytes 4128 | tf_op jit(solution)/shard_map/ppermute | solution.py:123
  88.5 2.1 %collective-permute-done.12 = f32[2,512]{1,0:T(2,128)S(1)} collective-permute-done((f32[2,512]{1,0:T(2,128)S(1)}, f32[2,512]{1,0:T(2,128)S(1)}, u32[]{:S(2)}, u32[]{:S(2)}) %collective-permute-start.12) | collective-permute-done | bytes 4128 | tf_op jit(solution)/shard_map/ppermute | solution.py:123
  90.7 0.7 collective-permute-start.13
  91.4 1.6 collective-permute-start.14
  93.0 1.2 collective-permute-start.15
  94.2 0.2 collective-permute-done.13
  94.5 0.7 collective-permute-done.14
  95.2 2.5 %collective-permute-done.15 = f32[8,512]{1,0:T(8,128)S(1)} collective-permute-done((f32[8,512]{1,0:T(8,128)S(1)}, f32[8,512]{1,0:T(8,128)S(1)}, u32[]{:S(2)}, u32[]{:S(2)}) %collective-permute-start.15) | collective-permute-done | bytes 16416 | tf_op jit(solution)/shard_map/ppermute | solution.py:123
  97.7 1.2 collective-permute-done.16.refs_2_
  99.0 1.6 copy-done.2
  100.6 1.3 grad_logits.1
  101.9 0.2 collective-permute-start.17
  102.1 2.5 %collective-permute-done.17.refs_2_ = bf16[512,1024]{1,0:T(8,128)(2,1)S(1)} collective-permute-done((bf16[512,1024]{1,0:T(8,128)(2,1)S(1)}, bf16[512,1024]{1,0:T(8,128)(2,1)S(1)}, u32[]{:S(2)}, u32[]{:S(2)}) %collective-permute-start.17) | collective-permute-done | bytes 1048608 | tf_op jit(solution)/shard_map/ppermute | solution.py:123
  104.6 9.7 %grad_hidden_partial.1 = (f32[4,2,16,2560]{3,2,1,0:T(8,128)S(1)}, bf16[4,2,16,2560]{3,2,1,0:T(8,128)(2,1)}, bf16[4,2,16,2560]{3,2,1,0:T(8,128)(2,1)}, bf16[4,2,16,2560]{3,2,1,0:T(8,128)(2,1)}) custom-call(s32[1]{0:T(128)} %bitcast.refs_0_, bf16[512,1024]{1,0:T(8,128)(2,1)S(1)} %get-tuple-element.24.refs_8_.refs_1_, ...), custom_call_target="tpu_custom_call" | custom-call | flops 5368709120 | bytes 10485760 | tf_op jit(solution)/shard_map/grad_hidden_partial/pallas_call | solution.py:435
  114.3 1.5 collective-permute-start.19
  115.8 0.3 collective-permute-start.20
  116.1 1.7 collective-permute-start.21
  117.8 14.3 %collective-permute-done.19.refs_0_ = bf16[4,2,16,2560]{3,2,1,0:T(8,128)(2,1)S(1)} collective-permute-done((bf16[4,2,16,2560]{3,2,1,0:T(8,128)(2,1)}, bf16[4,2,16,2560]{3,2,1,0:T(8,128)(2,1)S(1)}, u32[]{:S(2)}, u32[]{:S(2)}) %collective-permute-start.19) | collective-permute-done | bytes 655392 | tf_op jit(solution)/shard_map/ppermute | solution.py:123
  132.1 14.5 %collective-permute-done.20.refs_1_ = bf16[4,2,16,2560]{3,2,1,0:T(8,128)(2,1)S(1)} collective-permute-done((bf16[4,2,16,2560]{3,2,1,0:T(8,128)(2,1)}, bf16[4,2,16,2560]{3,2,1,0:T(8,128)(2,1)S(1)}, u32[]{:S(2)}, u32[]{:S(2)}) %collective-permute-start.20) | collective-permute-done | bytes 655392 | tf_op jit(solution)/shard_map/ppermute | solution.py:123
  146.6 0.7 chip_sum.1
  147.3 0.2 collective-permute-start.22
  147.5 1.8 %collective-permute-start.23 = (bf16[2,16,2560]{2,1,0:T(8,128)(2,1)S(1)}, bf16[2,16,2560]{2,1,0:T(8,128)(2,1)S(1)}, u32[]{:S(2)}, u32[]{:S(2)}) collective-permute-start(bf16[2,16,2560]{2,1,0:T(8,128)(2,1)S(1)} %get-tuple-element.31), channel_id=1, source_target_pairs={{0,16},{1,17},{2,18},{3,19},{4,20},{5,21},{6,22},{7,23},{8,24},{9,... | collective-permute-start | bytes 491528 | tf_op jit(solution)/shard_map/ppermute | solution.py:123
  149.3 2.4 %collective-permute-start.24 = (bf16[2,16,2560]{2,1,0:T(8,128)(2,1)S(1)}, bf16[2,16,2560]{2,1,0:T(8,128)(2,1)S(1)}, u32[]{:S(2)}, u32[]{:S(2)}) collective-permute-start(bf16[2,16,2560]{2,1,0:T(8,128)(2,1)S(1)} %get-tuple-element.32), channel_id=1, source_target_pairs={{0,24},{1,25},{2,26},{3,27},{4,28},{5,29},{6,30},{7,31},{8,16},{9,... | collective-permute-start | bytes 491528 | tf_op jit(solution)/shard_map/ppermute | solution.py:123
  151.7 1.1 copy-done.4
  152.8 1.1 copy-done.10
  153.9 1.1 copy-done.13
  155.0 1.1 copy-done.16
  156.1 12.3 %grad_head.1 = bf16[5120,1024]{1,0:T(8,128)(2,1)} custom-call(bf16[64,5120]{1,0:T(8,128)(2,1)S(1)} %copy-done.4, bf16[64,5120]{1,0:T(8,128)(2,1)S(1)} %copy-done.10, bf16[64,5120]{1,0:T(8,128)(2,1)S(1)} %copy-done.13, bf16[64,5120]{1,0:T(8,128)(2,1)S(1)} %copy-done.16, bf16[64,5120]{1,0:T(8,128)(2,1)} %collective-permute-done.6.refs_4_, ...), custom_call_target="tpu_custom_call" | custom-call | flops 5368709120 | bytes 15728640 | tf_op jit(solution)/shard_map/grad_head/pallas_call | solution.py:494
  168.4 0.3 layer_sum.1
  168.8 0.6 slice_reduce_fusion
  169.4 0.6 collective-permute-done.25
  170.1 0.7 pad_maximum_fusion.1
  (78 shorter events, 1.1 us)
Async XLA Ops:
  0.6 13.4 %collective-permute-start = (bf16[16,5120]{1,0:T(8,128)(2,1)}, bf16[16,5120]{1,0:T(8,128)(2,1)S(1)}, u32[]{:S(2)}, u32[]{:S(2)}) collective-permute-start(bf16[16,5120]{1,0:T(8,128)(2,1)} %param.7), channel_id=1, source_target_pairs={{0,8},{1,9},{2,10},{3,11},{4,12},{5,13},{6,14},{7,15},{8,0},{9,1},... | collective-permute-start | bytes 491528 | tf_op jit(solution)/shard_map/ppermute | solution.py:123
  3.7 15.3 %collective-permute-start.1 = (bf16[16,5120]{1,0:T(8,128)(2,1)}, bf16[16,5120]{1,0:T(8,128)(2,1)S(1)}, u32[]{:S(2)}, u32[]{:S(2)}) collective-permute-start(bf16[16,5120]{1,0:T(8,128)(2,1)} %param.7), channel_id=1, source_target_pairs={{0,16},{1,17},{2,18},{3,19},{4,20},{5,21},{6,22},{7,23},{8,24},{9,... | collective-permute-start | bytes 491528 | tf_op jit(solution)/shard_map/ppermute | solution.py:123
  6.3 12.7 %collective-permute-start.2 = (bf16[16,5120]{1,0:T(8,128)(2,1)}, bf16[16,5120]{1,0:T(8,128)(2,1)S(1)}, u32[]{:S(2)}, u32[]{:S(2)}) collective-permute-start(bf16[16,5120]{1,0:T(8,128)(2,1)} %param.7), channel_id=1, source_target_pairs={{0,24},{1,25},{2,26},{3,27},{4,28},{5,29},{6,30},{7,31},{8,16},{9,... | collective-permute-start | bytes 491528 | tf_op jit(solution)/shard_map/ppermute | solution.py:123
  6.3 5.5 %copy-start.18 = (bf16[16,5120]{1,0:T(8,128)(2,1)S(1)}, bf16[16,5120]{1,0:T(8,128)(2,1)}, u32[]{:S(2)}) copy-start(bf16[16,5120]{1,0:T(8,128)(2,1)} %param.7) | copy-start | bytes 491524
  6.3 5.5 %copy-start.17 = (bf16[4,64,4,128]{3,2,1,0:T(4,128)(2,1)S(1)}, bf16[4,64,4,128]{3,2,1,0:T(4,128)(2,1)}, u32[]{:S(2)}) copy-start(bf16[4,64,4,128]{3,2,1,0:T(4,128)(2,1)} %param.9) | copy-start | bytes 786436
  6.3 6.5 %copy-start.19 = (s32[4,64]{1,0:T(4,128)S(1)}, s32[4,64]{1,0:T(4,128)}, u32[]{:S(2)}) copy-start(s32[4,64]{1,0:T(4,128)} %param.10) | copy-start | bytes 3076
  11.8 92.8 %collective-permute-start.18 = (bf16[2560,1024]{1,0:T(8,128)(2,1)}, bf16[2560,1024]{1,0:T(8,128)(2,1)}, u32[]{:S(2)}, u32[]{:S(2)}) collective-permute-start(bf16[2560,1024]{1,0:T(8,128)(2,1)} %constant_dynamic-slice_fusion), channel_id=1, source_target_pairs={{0,1},{1,0},{2,3},{3,2},{4,5},{5,4},{6,7},{7,6},{8,9},{9,8},{10,11... | collective-permute-start | bytes 15728648 | tf_op jit(solution)/shard_map/ppermute | solution.py:123
  11.8 45.9 %copy-start.5 = (s32[4,128]{1,0:T(4,128)S(1)}, s32[4,128]{1,0:T(4,128)}, u32[]{:S(2)}) copy-start(s32[4,128]{1,0:T(4,128)} %param.11) | copy-start | bytes 6148
  11.9 45.9 %copy-start.6 = (f32[512]{0:T(512)S(1)}, f32[512]{0:T(512)}, u32[]{:S(2)}) copy-start(f32[512]{0:T(512)} %param.12) | copy-start | bytes 6148
  19.0 60.8 %copy-start.3 = (bf16[64,5120]{1,0:T(8,128)(2,1)}, bf16[64,5120]{1,0:T(8,128)(2,1)S(1)}, u32[]{:S(2)}) copy-start(bf16[64,5120]{1,0:T(8,128)(2,1)S(1)} %constant_dynamic-update-slice_fusion.refs_0_) | copy-start | bytes 1966084
  19.0 20.9 %collective-permute-start.3 = (bf16[64,5120]{1,0:T(8,128)(2,1)S(1)}, bf16[64,5120]{1,0:T(8,128)(2,1)S(1)}, u32[]{:S(2)}, u32[]{:S(2)}) collective-permute-start(bf16[64,5120]{1,0:T(8,128)(2,1)S(1)} %constant_dynamic-update-slice_fusion.refs_0_), channel_id=1, source_target_pairs={{0,2},{1,3},{2,0},{3,1},{4,6},{5,7},{6,4},{7,5},{8,10},{9,11},{10,... | collective-permute-start | bytes 1966088 | tf_op jit(solution)/shard_map/ppermute | solution.py:123
  20.6 32.7 %collective-permute-start.4 = (bf16[64,5120]{1,0:T(8,128)(2,1)S(1)}, bf16[64,5120]{1,0:T(8,128)(2,1)S(1)}, u32[]{:S(2)}, u32[]{:S(2)}) collective-permute-start(bf16[64,5120]{1,0:T(8,128)(2,1)S(1)} %constant_dynamic-update-slice_fusion.refs_0_), channel_id=1, source_target_pairs={{0,4},{1,5},{2,6},{3,7},{4,0},{5,1},{6,2},{7,3},{8,12},{9,13},{10,... | collective-permute-start | bytes 1966088 | tf_op jit(solution)/shard_map/ppermute | solution.py:123
  22.1 31.8 %collective-permute-start.5 = (bf16[64,5120]{1,0:T(8,128)(2,1)S(1)}, bf16[64,5120]{1,0:T(8,128)(2,1)S(1)}, u32[]{:S(2)}, u32[]{:S(2)}) collective-permute-start(bf16[64,5120]{1,0:T(8,128)(2,1)S(1)} %constant_dynamic-update-slice_fusion.refs_0_), channel_id=1, source_target_pairs={{0,6},{1,7},{2,4},{3,5},{4,2},{5,3},{6,0},{7,1},{8,14},{9,15},{10,... | collective-permute-start | bytes 1966088 | tf_op jit(solution)/shard_map/ppermute | solution.py:123
  23.5 31.3 %all-to-all-start = ((bf16[32,65,128]{2,1,0:T(8,128)(2,1)}), bf16[32,65,128]{2,1,0:T(8,128)(2,1)}, u32[]{:S(2)}, u32[]{:S(2)}) async-start(bf16[32,65,128]{2,1,0:T(8,128)(2,1)} %pad_maximum_fusion), calls=%async_computation | async-start | bytes 1179648 | tf_op jit(solution)/shard_map/all_to_all | solution.py:323
  29.5 32.6 %collective-permute-start.6 = (bf16[64,5120]{1,0:T(8,128)(2,1)S(1)}, bf16[64,5120]{1,0:T(8,128)(2,1)}, u32[]{:S(2)}, u32[]{:S(2)}) collective-permute-start(bf16[64,5120]{1,0:T(8,128)(2,1)S(1)} %constant_dynamic-update-slice_fusion.refs_0_), channel_id=1, source_target_pairs={{0,1},{1,0},{2,3},{3,2},{4,5},{5,4},{6,7},{7,6},{8,9},{9,8},{10,11... | collective-permute-start | bytes 1966088 | tf_op jit(solution)/shard_map/ppermute | solution.py:123
  39.9 39.9 %copy-start.9 = (bf16[64,5120]{1,0:T(8,128)(2,1)}, bf16[64,5120]{1,0:T(8,128)(2,1)S(1)}, u32[]{:S(2)}) copy-start(bf16[64,5120]{1,0:T(8,128)(2,1)S(1)} %collective-permute-done.3.refs_1_) | copy-start | bytes 1966084
  39.9 22.2 %collective-permute-start.7 = (bf16[64,5120]{1,0:T(8,128)(2,1)S(1)}, bf16[64,5120]{1,0:T(8,128)(2,1)}, u32[]{:S(2)}, u32[]{:S(2)}) collective-permute-start(bf16[64,5120]{1,0:T(8,128)(2,1)S(1)} %collective-permute-done.3.refs_1_), channel_id=1, source_target_pairs={{0,1},{1,0},{2,3},{3,2},{4,5},{5,4},{6,7},{7,6},{8,9},{9,8},{10,11... | collective-permute-start | bytes 1966088 | tf_op jit(solution)/shard_map/ppermute | solution.py:123
  53.3 8.8 %copy-start.11 = (bf16[64,5120]{1,0:T(8,128)(2,1)}, bf16[64,5120]{1,0:T(8,128)(2,1)S(1)}, u32[]{:S(2)}) copy-start(bf16[64,5120]{1,0:T(8,128)(2,1)S(1)} %collective-permute-done.4.refs_2_) | copy-start | bytes 1966084
  53.3 8.8 %collective-permute-start.8 = (bf16[64,5120]{1,0:T(8,128)(2,1)S(1)}, bf16[64,5120]{1,0:T(8,128)(2,1)}, u32[]{:S(2)}, u32[]{:S(2)}) collective-permute-start(bf16[64,5120]{1,0:T(8,128)(2,1)S(1)} %collective-permute-done.4.refs_2_), channel_id=1, source_target_pairs={{0,1},{1,0},{2,3},{3,2},{4,5},{5,4},{6,7},{7,6},{8,9},{9,8},{10,11... | collective-permute-start | bytes 1966088 | tf_op jit(solution)/shard_map/ppermute | solution.py:123
  53.9 8.2 %copy-start.14 = (bf16[64,5120]{1,0:T(8,128)(2,1)}, bf16[64,5120]{1,0:T(8,128)(2,1)S(1)}, u32[]{:S(2)}) copy-start(bf16[64,5120]{1,0:T(8,128)(2,1)S(1)} %collective-permute-done.5.refs_3_) | copy-start | bytes 1966084
  53.9 8.2 %collective-permute-start.9 = (bf16[64,5120]{1,0:T(8,128)(2,1)S(1)}, bf16[64,5120]{1,0:T(8,128)(2,1)}, u32[]{:S(2)}, u32[]{:S(2)}) collective-permute-start(bf16[64,5120]{1,0:T(8,128)(2,1)S(1)} %collective-permute-done.5.refs_3_), channel_id=1, source_target_pairs={{0,1},{1,0},{2,3},{3,2},{4,5},{5,4},{6,7},{7,6},{8,9},{9,8},{10,11... | collective-permute-start | bytes 1966088 | tf_op jit(solution)/shard_map/ppermute | solution.py:123
  60.8 1.3 copy-start
  62.1 1.1 copy-start.12
  63.2 1.1 copy-start.15
  64.3 34.7 %copy-start.1 = (f32[512,1024]{1,0:T(8,128)S(1)}, f32[512,1024]{1,0:T(8,128)}, u32[]{:S(2)}) copy-start(f32[512,1024]{1,0:T(8,128)} %copy-done) | copy-start | bytes 6291460
  64.3 34.7 %copy-start.7 = (f32[512]{0:T(512)S(1)}, f32[512]{0:T(512)}, u32[]{:S(2)}) copy-start(f32[512]{0:T(512)} %param.13) | copy-start | bytes 6148
  79.8 6.8 %collective-permute-start.10 = (f32[2,512]{1,0:T(2,128)S(1)}, f32[2,512]{1,0:T(2,128)S(1)}, u32[]{:S(2)}, u32[]{:S(2)}) collective-permute-start(f32[2,512]{1,0:T(2,128)S(1)} %get-tuple-element.20), channel_id=1, source_target_pairs={{0,8},{1,9},{2,10},{3,11},{4,12},{5,13},{6,14},{7,15},{8,0},{9,1},... | collective-permute-start | bytes 12296 | tf_op jit(solution)/shard_map/ppermute | solution.py:123
  84.0 4.5 %collective-permute-start.11 = (f32[2,512]{1,0:T(2,128)S(1)}, f32[2,512]{1,0:T(2,128)S(1)}, u32[]{:S(2)}, u32[]{:S(2)}) collective-permute-start(f32[2,512]{1,0:T(2,128)S(1)} %get-tuple-element.20), channel_id=1, source_target_pairs={{0,16},{1,17},{2,18},{3,19},{4,20},{5,21},{6,22},{7,23},{8,24},{9,... | collective-permute-start | bytes 12296 | tf_op jit(solution)/shard_map/ppermute | solution.py:123
  85.3 5.4 %collective-permute-start.12 = (f32[2,512]{1,0:T(2,128)S(1)}, f32[2,512]{1,0:T(2,128)S(1)}, u32[]{:S(2)}, u32[]{:S(2)}) collective-permute-start(f32[2,512]{1,0:T(2,128)S(1)} %get-tuple-element.20), channel_id=1, source_target_pairs={{0,24},{1,25},{2,26},{3,27},{4,28},{5,29},{6,30},{7,31},{8,16},{9,... | collective-permute-start | bytes 12296 | tf_op jit(solution)/shard_map/ppermute | solution.py:123
  90.7 3.8 %collective-permute-start.13 = (f32[8,512]{1,0:T(8,128)S(1)}, f32[8,512]{1,0:T(8,128)S(1)}, u32[]{:S(2)}, u32[]{:S(2)}) collective-permute-start(f32[8,512]{1,0:T(8,128)S(1)} %pad_maximum_fusion.2), channel_id=1, source_target_pairs={{0,2},{1,3},{2,0},{3,1},{4,6},{5,7},{6,4},{7,5},{8,10},{9,11},{10,... | collective-permute-start | bytes 49160 | tf_op jit(solution)/shard_map/ppermute | solution.py:123
  91.4 3.7 %collective-permute-start.14 = (f32[8,512]{1,0:T(8,128)S(1)}, f32[8,512]{1,0:T(8,128)S(1)}, u32[]{:S(2)}, u32[]{:S(2)}) collective-permute-start(f32[8,512]{1,0:T(8,128)S(1)} %pad_maximum_fusion.2), channel_id=1, source_target_pairs={{0,4},{1,5},{2,6},{3,7},{4,0},{5,1},{6,2},{7,3},{8,12},{9,13},{10,... | collective-permute-start | bytes 49160 | tf_op jit(solution)/shard_map/ppermute | solution.py:123
  93.0 4.6 %collective-permute-start.15 = (f32[8,512]{1,0:T(8,128)S(1)}, f32[8,512]{1,0:T(8,128)S(1)}, u32[]{:S(2)}, u32[]{:S(2)}) collective-permute-start(f32[8,512]{1,0:T(8,128)S(1)} %pad_maximum_fusion.2), channel_id=1, source_target_pairs={{0,6},{1,7},{2,4},{3,5},{4,2},{5,3},{6,0},{7,1},{8,14},{9,15},{10,... | collective-permute-start | bytes 49160 | tf_op jit(solution)/shard_map/ppermute | solution.py:123
  97.7 1.3 collective-permute-start.16
  99.0 1.6 copy-start.2
  101.9 12.4 %copy-start.8 = (bf16[512,1024]{1,0:T(8,128)(2,1)}, bf16[512,1024]{1,0:T(8,128)(2,1)S(1)}, u32[]{:S(2)}) copy-start(bf16[512,1024]{1,0:T(8,128)(2,1)S(1)} %get-tuple-element.24.refs_8_.refs_1_) | copy-start | bytes 3145732
  101.9 2.7 %collective-permute-start.17 = (bf16[512,1024]{1,0:T(8,128)(2,1)S(1)}, bf16[512,1024]{1,0:T(8,128)(2,1)S(1)}, u32[]{:S(2)}, u32[]{:S(2)}) collective-permute-start(bf16[512,1024]{1,0:T(8,128)(2,1)S(1)} %get-tuple-element.24.refs_8_.refs_1_), channel_id=1, source_target_pairs={{0,1},{1,0},{2,3},{3,2},{4,5},{5,4},{6,7},{7,6},{8,9},{9,8},{10,11... | collective-permute-start | bytes 3145736 | tf_op jit(solution)/shard_map/ppermute | solution.py:123
  114.3 17.8 %collective-permute-start.19 = (bf16[4,2,16,2560]{3,2,1,0:T(8,128)(2,1)}, bf16[4,2,16,2560]{3,2,1,0:T(8,128)(2,1)S(1)}, u32[]{:S(2)}, u32[]{:S(2)}) collective-permute-start(bf16[4,2,16,2560]{3,2,1,0:T(8,128)(2,1)} %get-tuple-element.26), channel_id=1, source_target_pairs={{0,2},{1,3},{2,0},{3,1},{4,6},{5,7},{6,4},{7,5},{8,10},{9,11},{10,... | collective-permute-start | bytes 1966088 | tf_op jit(solution)/shard_map/ppermute | solution.py:123
  115.8 30.8 %collective-permute-start.20 = (bf16[4,2,16,2560]{3,2,1,0:T(8,128)(2,1)}, bf16[4,2,16,2560]{3,2,1,0:T(8,128)(2,1)S(1)}, u32[]{:S(2)}, u32[]{:S(2)}) collective-permute-start(bf16[4,2,16,2560]{3,2,1,0:T(8,128)(2,1)} %get-tuple-element.27), channel_id=1, source_target_pairs={{0,4},{1,5},{2,6},{3,7},{4,0},{5,1},{6,2},{7,3},{8,12},{9,13},{10,... | collective-permute-start | bytes 1966088 | tf_op jit(solution)/shard_map/ppermute | solution.py:123
  116.1 30.5 %collective-permute-start.21 = (bf16[4,2,16,2560]{3,2,1,0:T(8,128)(2,1)}, bf16[4,2,16,2560]{3,2,1,0:T(8,128)(2,1)S(1)}, u32[]{:S(2)}, u32[]{:S(2)}) collective-permute-start(bf16[4,2,16,2560]{3,2,1,0:T(8,128)(2,1)} %get-tuple-element.28), channel_id=1, source_target_pairs={{0,6},{1,7},{2,4},{3,5},{4,2},{5,3},{6,0},{7,1},{8,14},{9,15},{10,... | collective-permute-start | bytes 1966088 | tf_op jit(solution)/shard_map/ppermute | solution.py:123
  147.3 21.1 %collective-permute-start.22 = (bf16[2,16,2560]{2,1,0:T(8,128)(2,1)S(1)}, bf16[2,16,2560]{2,1,0:T(8,128)(2,1)S(1)}, u32[]{:S(2)}, u32[]{:S(2)}) collective-permute-start(bf16[2,16,2560]{2,1,0:T(8,128)(2,1)S(1)} %get-tuple-element.30), channel_id=1, source_target_pairs={{0,8},{1,9},{2,10},{3,11},{4,12},{5,13},{6,14},{7,15},{8,0},{9,1},... | collective-permute-start | bytes 491528 | tf_op jit(solution)/shard_map/ppermute | solution.py:123
  147.5 20.9 %collective-permute-start.23 = (bf16[2,16,2560]{2,1,0:T(8,128)(2,1)S(1)}, bf16[2,16,2560]{2,1,0:T(8,128)(2,1)S(1)}, u32[]{:S(2)}, u32[]{:S(2)}) collective-permute-start(bf16[2,16,2560]{2,1,0:T(8,128)(2,1)S(1)} %get-tuple-element.31), channel_id=1, source_target_pairs={{0,16},{1,17},{2,18},{3,19},{4,20},{5,21},{6,22},{7,23},{8,24},{9,... | collective-permute-start | bytes 491528 | tf_op jit(solution)/shard_map/ppermute | solution.py:123
  149.3 19.1 %collective-permute-start.24 = (bf16[2,16,2560]{2,1,0:T(8,128)(2,1)S(1)}, bf16[2,16,2560]{2,1,0:T(8,128)(2,1)S(1)}, u32[]{:S(2)}, u32[]{:S(2)}) collective-permute-start(bf16[2,16,2560]{2,1,0:T(8,128)(2,1)S(1)} %get-tuple-element.32), channel_id=1, source_target_pairs={{0,24},{1,25},{2,26},{3,27},{4,28},{5,29},{6,30},{7,31},{8,16},{9,... | collective-permute-start | bytes 491528 | tf_op jit(solution)/shard_map/ppermute | solution.py:123
  151.7 1.1 copy-start.4
  152.8 1.1 copy-start.10
  153.9 1.1 copy-start.13
  155.0 1.1 copy-start.16
  168.7 1.3 collective-permute-start.25

commit v2 on v1

--- a/solution.py
+++ b/solution.py
@@ -1,3 +1,5 @@
+import functools
+
 import jax
 import jax.numpy as jnp
 from jax import lax
@@ -103,7 +105,9 @@
 CHIPS = 4
 GROUP = CORES * CHIPS
 SLOTS = 4
-VMEM_LIMIT = 48 * 1024 * 1024
+VMEM_LIMIT = 30 * 1024 * 1024
+HIDDEN_CHUNKS = 2
+PARTIAL_CHUNKS = (3, 2)
 
 
 def kernel_params():
@@ -178,27 +182,44 @@
             out_ref[pl.ds((k * GROUP + p) * rows, rows), :] = piece[pl.ds(k * rows, rows), :]
 
 
-def logits_kernel(rows, *refs):
-    pieces = refs[:GROUP]
-    w_ref, prob_ref, logits_ref, stat_ref, hidden = refs[GROUP:]
+def logits_kernel(rows, last, *refs):
+    pieces, w_ref, refs = refs[:GROUP], refs[GROUP], refs[GROUP + 1 :]
+    if last:
+        before_ref, prob_ref, logits_ref, stat_ref, hidden, cross_ref = refs
+    else:
+        logits_ref, hidden = refs
     step = pl.program_id(0)
-    assemble(pieces, rows, hidden)
-    part = jnp.dot(hidden[...], w_ref[...], preferred_element_type=jnp.float32)
 
     @pl.when(step == 0)
     def _():
+        assemble(pieces, rows, hidden)
+
+    part = jnp.dot(hidden[...], w_ref[...], preferred_element_type=jnp.float32)
+    if not last:
         logits_ref[...] = part
+        return
+    part = part + before_ref[...]
+    width = part.shape[1]
+    logits_ref[:, pl.ds(pl.multiple_of(step * width, width), width)] = part
+    product = part * prob_ref[...]
+    folded = product[:, :128]
+    for i in range(1, width // 128):
+        folded = folded + product[:, i * 128 : (i + 1) * 128]
+
+    @pl.when(step == 0)
+    def _():
+        cross_ref[...] = folded
 
     @pl.when(step > 0)
     def _():
-        logits_ref[...] += part
+        cross_ref[...] += folded
 
     @pl.when(step == pl.num_programs(0) - 1)
     def _():
         logits = logits_ref[...]
         top = jnp.max(logits, axis=1, keepdims=True)
         norm = top + jnp.log(jnp.sum(jnp.exp(logits - top), axis=1, keepdims=True))
-        cross = jnp.sum(prob_ref[...] * logits, axis=1, keepdims=True)
+        cross = jnp.sum(cross_ref[...], axis=1, keepdims=True)
         lane = lax.broadcasted_iota(jnp.int32, (1, 128), 1)
         both = jnp.where(lane == 0, norm, jnp.where(lane == 1, cross, 0.0))
         stat_ref[...] = both.T[:2]
@@ -263,10 +284,15 @@
                 out[k, core] = total[start : start + rows].astype(out.dtype)
 
 
-def head_kernel(rows, *refs):
-    pieces = refs[:GROUP]
-    grad_ref, out_ref, hidden = refs[GROUP:]
-    assemble(pieces, rows, hidden)
+def head_kernel(rows, chunk_steps, *refs):
+    pieces, (grad_ref, out_ref, hidden) = refs[:-3], refs[-3:]
+    chunk = pl.program_id(0) // chunk_steps
+    for i in range(len(pieces) // GROUP):
+
+        @pl.when(chunk == i)
+        def _():
+            assemble(pieces[i * GROUP : (i + 1) * GROUP], rows, hidden)
+
     out_ref[...] = lax.dot_general(
         hidden[...], grad_ref[...], (((0,), (0,)), ((), ())), preferred_element_type=jnp.float32
     ).astype(out_ref.dtype)
@@ -356,10 +382,15 @@
     pos = jnp.stack([core, chip, layer]).astype(jnp.int32)
     unlisted = float(n * slab - side * listed_count)
 
-    column = [hidden_states] + [shift(hidden_states, k * GROUP) for k in range(1, layers)]
-    column = jnp.concatenate(column, axis=0)
-    pieces = [column] + [shift(column, j * CORES) for j in range(1, CHIPS)]
-    pieces = pieces + [shift(piece, 1) for piece in pieces]
+    chunks = HIDDEN_CHUNKS if depth % (HIDDEN_CHUNKS * 256) == 0 else 1
+    chunk = depth // chunks
+    pieces = []
+    for i in range(chunks):
+        own = hidden_states[:, i * chunk : (i + 1) * chunk]
+        column = [own] + [shift(own, k * GROUP) for k in range(1, layers)]
+        column = jnp.concatenate(column, axis=0)
+        plane = [column] + [shift(column, j * CORES) for j in range(1, CHIPS)]
+        pieces.append(plane + [shift(piece, 1) for piece in plane])
 
     arrived_blocks, arrived_stat, place = send_teacher(teacher_logits, block_lists, slab // side)
     sib_w = shift(lax.dynamic_slice(head_weight, ((1 - core) * half, 0), (half, slab)), 1)
@@ -386,31 +417,47 @@
         tail_mass.reshape(blocks, 1, side),
     )
 
-    tile = tile_of(depth)
-    piece_specs = [pl.BlockSpec((layers * rows, tile), lambda t: (0, t)) for _ in range(GROUP)]
-    whole = lambda t: (0, 0)
-    logits, stat = pl.pallas_call(
-        lambda *refs: logits_kernel(rows, *refs),
-        grid=(depth // tile,),
-        out_shape=(
-            jax.ShapeDtypeStruct((tokens, slab), f32),
-            jax.ShapeDtypeStruct((2, tokens), f32),
-        ),
-        in_specs=piece_specs
-        + [pl.BlockSpec((tile, slab), lambda t: (t, 0)), pl.BlockSpec((tokens, slab), whole)],
-        out_specs=(pl.BlockSpec((tokens, slab), whole), pl.BlockSpec((2, tokens), whole)),
-        scratch_shapes=[pltpu.VMEM((tokens, tile), bf16)],
-        compiler_params=kernel_params(),
-        cost_estimate=pl.CostEstimate(
-            flops=2 * tokens * depth * slab,
-            bytes_accessed=2 * depth * (slab + tokens) + 4 * tokens * slab,
-            transcendentals=tokens * slab,
-        ),
-        name="logits",
-    )(*pieces, head_weight, prob)
-
-    stat = jnp.concatenate([stat] + [shift(stat, k * GROUP) for k in range(1, layers)], axis=0)
-    stat = jnp.concatenate([stat] + [shift(stat, j * CORES) for j in range(1, CHIPS)], axis=0)
+    width = 256 if slab % 256 == 0 else 128
+    logits = None
+    for i in range(chunks):
+        last = i == chunks - 1
+        whole = lambda t: (0, 0)
+        across = pl.BlockSpec((tokens, width), lambda t: (0, t))
+        in_specs = [pl.BlockSpec((layers * rows, chunk), whole) for _ in range(GROUP)]
+        in_specs.append(pl.BlockSpec((chunk, width), lambda t, i=i: (i, t)))
+        operands = pieces[i] + [head_weight]
+        scratch = [pltpu.VMEM((tokens, chunk), bf16)]
+        out_shape = [jax.ShapeDtypeStruct((tokens, slab), f32)]
+        out_specs = [across]
+        if last:
+            before = jnp.zeros((tokens, slab), f32) if logits is None else logits
+            in_specs += [across, across]
+            operands += [before, prob]
+            scratch.append(pltpu.VMEM((tokens, 128), f32))
+            out_shape.append(jax.ShapeDtypeStruct((2, tokens), f32))
+            out_specs = [pl.BlockSpec((tokens, slab), whole), pl.BlockSpec((2, tokens), whole)]
+        outs = pl.pallas_call(
+            functools.partial(logits_kernel, rows, last),
+            grid=(slab // width,),
+            out_shape=out_shape,
+            in_specs=in_specs,
+            out_specs=out_specs,
+            scratch_shapes=scratch,
+            compiler_params=kernel_params(),
+            cost_estimate=pl.CostEstimate(
+                flops=2 * tokens * chunk * slab,
+                bytes_accessed=2 * chunk * (slab + tokens) + 4 * tokens * slab,
+                transcendentals=tokens * slab if last else 0,
+            ),
+            name="logits",
+        )(*operands)
+        logits = outs[0]
+    stat = outs[1]
+
+    distances = [1 << i for i in range((n // GROUP).bit_length() - 1)]
+    distances = [d * GROUP for d in distances] + [CORES, 2 * CORES]
+    for distance in distances:
+        stat = jnp.concatenate([stat, shift(stat, distance)], axis=0)
     sib_stat = shift(stat, 1)
 
     grad, loss = pl.pallas_call(
@@ -431,79 +478,100 @@
 
     tile = tile_of(half)
     steps = half // tile
-    out_block = pl.BlockSpec((layers, CORES, rows, tile), lambda t, core: (0, 0, 0, t))
-    partial = pl.pallas_call(
-        lambda *refs: partial_kernel(rows, *refs),
-        grid_spec=pltpu.PrefetchScalarGridSpec(
-            num_scalar_prefetch=1,
-            grid=(steps,),
-            in_specs=[
-                pl.BlockSpec((tokens, slab), lambda t, core: (0, 0)),
-                pl.BlockSpec((tokens, slab), lambda t, core: (0, 0)),
-                pl.BlockSpec((tile, slab), lambda t, core: (core[0] * steps + t, 0)),
-                pl.BlockSpec((tile, slab), lambda t, core: (t, 0)),
+    sizes = PARTIAL_CHUNKS if sum(PARTIAL_CHUNKS) == steps else (steps,)
+    sent = []
+    for i, size in enumerate(sizes):
+        first = sum(sizes[:i])
+        out_block = pl.BlockSpec((layers, CORES, rows, tile), lambda t, core: (0, 0, 0, t))
+        partial = pl.pallas_call(
+            functools.partial(partial_kernel, rows),
+            grid_spec=pltpu.PrefetchScalarGridSpec(
+                num_scalar_prefetch=1,
+                grid=(size,),
+                in_specs=[
+                    pl.BlockSpec((tokens, slab), lambda t, core: (0, 0)),
+                    pl.BlockSpec((tokens, slab), lambda t, core: (0, 0)),
+                    pl.BlockSpec((tile, slab), lambda t, core, first=first: (core[0] * steps + first + t, 0)),
+                    pl.BlockSpec((tile, slab), lambda t, core, first=first: (first + t, 0)),
+                ],
+                out_specs=[out_block] * CHIPS,
+                scratch_shapes=[pltpu.VMEM((tokens, slab), bf16)],
+            ),
+            out_shape=[
+                jax.ShapeDtypeStruct((layers, CORES, rows, size * tile), f32 if j == 0 else bf16)
+                for j in range(CHIPS)
             ],
-            out_specs=[out_block] * CHIPS,
-            scratch_shapes=[pltpu.VMEM((tokens, slab), bf16)],
-        ),
-        out_shape=[
-            jax.ShapeDtypeStruct((layers, CORES, rows, half), f32 if j == 0 else bf16)
-            for j in range(CHIPS)
-        ],
-        compiler_params=kernel_params(),
-        cost_estimate=pl.CostEstimate(
-            flops=4 * tokens * half * slab, bytes_accessed=4 * half * slab, transcendentals=0
-        ),
-        name="grad_hidden_partial",
-    )(pos[:1], grad, sib_grad, head_weight, sib_w)
-
-    arrived = [shift(partial[j], j * CORES) for j in range(1, CHIPS)]
-    chip_block = pl.BlockSpec((layers, CORES, rows, tile), lambda t: (0, 0, 0, t))
-    layer_block = pl.BlockSpec((CORES, rows, tile), lambda t: (0, 0, t))
-    summed = pl.pallas_call(
-        chip_sum_kernel,
-        grid=(steps,),
-        in_specs=[chip_block] * CHIPS,
-        out_specs=[layer_block] * layers,
-        out_shape=[
-            jax.ShapeDtypeStruct((CORES, rows, half), f32 if k == 0 else bf16) for k in range(layers)
-        ],
-        compiler_params=kernel_params(),
-        cost_estimate=pl.CostEstimate(
-            flops=tokens * half, bytes_accessed=3 * tokens * half, transcendentals=0
-        ),
-        name="chip_sum",
-    )(partial[0], *arrived)
-    arrived = [shift(summed[k], k * GROUP) for k in range(1, layers)]
-    row_block = pl.BlockSpec((rows, tile), lambda t: (0, t))
-    mine, theirs = pl.pallas_call(
-        layer_sum_kernel,
-        grid=(steps,),
-        in_specs=[layer_block] * layers,
-        out_specs=[row_block] * CORES,
-        out_shape=[jax.ShapeDtypeStruct((rows, half), bf16)] * CORES,
-        compiler_params=kernel_params(),
-        cost_estimate=pl.CostEstimate(
-            flops=CORES * layers * rows * half, bytes_accessed=3 * CORES * layers * rows * half, transcendentals=0
-        ),
-        name="layer_sum",
-    )(summed[0], *arrived)
-    other = shift(theirs, 1)
-
-    tile = tile_of(depth)
+            compiler_params=kernel_params(),
+            cost_estimate=pl.CostEstimate(
+                flops=4 * tokens * size * tile * slab, bytes_accessed=4 * size * tile * slab, transcendentals=0
+            ),
+            name="grad_hidden_partial",
+        )(pos[:1], grad, sib_grad, head_weight, sib_w)
+        sent.append([partial[0]] + [shift(partial[j], j * CORES) for j in range(1, CHIPS)])
+
+    head_tile = chunk // 2 if chunk % 512 == 0 else chunk
+    per_chunk = chunk // head_tile
+    piece_specs = [
+        pl.BlockSpec(
+            (layers * rows, head_tile),
+            lambda t, i=i: (0, jnp.clip(t - i * per_chunk, 0, per_chunk - 1)),
+        )
+        for i in range(chunks)
+        for _ in range(GROUP)
+    ]
     grad_head = pl.pallas_call(
-        lambda *refs: head_kernel(rows, *refs),
-        grid=(depth // tile,),
-        in_specs=piece_specs + [pl.BlockSpec((tokens, slab), whole)],
-        out_specs=pl.BlockSpec((tile, slab), lambda t: (t, 0)),
+        functools.partial(head_kernel, rows, per_chunk),
+        grid=(depth // head_tile,),
+        in_specs=piece_specs + [pl.BlockSpec((tokens, slab), lambda t: (0, 0))],
+        out_specs=pl.BlockSpec((head_tile, slab), lambda t: (t, 0)),
         out_shape=jax.ShapeDtypeStruct((depth, slab), bf16),
-        scratch_shapes=[pltpu.VMEM((tokens, tile), bf16)],
+        scratch_shapes=[pltpu.VMEM((tokens, head_tile), bf16)],
         compiler_params=kernel_params(),
         cost_estimate=pl.CostEstimate(
             flops=2 * tokens * depth * slab, bytes_accessed=2 * depth * (slab + tokens), transcendentals=0
         ),
         name="grad_head",
-    )(*pieces, grad)
+    )(*[piece for some in pieces for piece in some], grad)
+    sent, grad_head = lax.optimization_barrier((sent, grad_head))
+
+    mine, other = [], []
+    for size, parts in zip(sizes, sent):
+        chip_block = pl.BlockSpec((layers, CORES, rows, tile), lambda t: (0, 0, 0, t))
+        layer_block = pl.BlockSpec((CORES, rows, tile), lambda t: (0, 0, t))
+        summed = pl.pallas_call(
+            chip_sum_kernel,
+            grid=(size,),
+            in_specs=[chip_block] * CHIPS,
+            out_specs=[layer_block] * layers,
+            out_shape=[
+                jax.ShapeDtypeStruct((CORES, rows, size * tile), f32 if k == 0 else bf16)
+                for k in range(layers)
+            ],
+            compiler_params=kernel_params(),
+            cost_estimate=pl.CostEstimate(
+                flops=tokens * size * tile, bytes_accessed=3 * tokens * size * tile, transcendentals=0
+            ),
+            name="chip_sum",
+        )(*parts)
+        arrived = [shift(summed[k], k * GROUP) for k in range(1, layers)]
+        row_block = pl.BlockSpec((rows, tile), lambda t: (0, t))
+        ours, theirs = pl.pallas_call(
+            layer_sum_kernel,
+            grid=(size,),
+            in_specs=[layer_block] * layers,
+            out_specs=[row_block] * CORES,
+            out_shape=[jax.ShapeDtypeStruct((rows, size * tile), bf16)] * CORES,
+            compiler_params=kernel_params(),
+            cost_estimate=pl.CostEstimate(
+                flops=CORES * layers * rows * size * tile,
+                bytes_accessed=3 * CORES * layers * rows * size * tile,
+                transcendentals=0,
+            ),
+            name="layer_sum",
+        )(summed[0], *arrived)
+        mine.append(ours)
+        other.append(shift(theirs, 1))
+    mine, other = jnp.concatenate(mine, axis=1), jnp.concatenate(other, axis=1)
 
     low, high = jnp.where(core == 0, mine, other), jnp.where(core == 0, other, mine)
     return loss[:, 0], grad_head, jnp.concatenate([low, high], axis=1)

time: 172 us -> 189 us (1.099)
  starting transfers between devices: 34.2 us -> 46.6 us
  local copies, waits for them, and re-layouts: 19.1 us -> 29.5 us
  Pallas kernels: 42.8 us -> 36.2 us
    ppermute x26 -> x41, starting transfers between devices: 28.2 us -> 43.6 us  [shift(): return lax.ppermute(x, 'vocab', [(i, i ^ distance) for i in range(n)])]
    unnamed x44 -> x55, local copies, waits for them, and re-layouts: 9.85 us -> 21.2 us
    pallas_call x5 -> x9, Pallas kernels: 38.4 us -> 31.7 us  [the longest x2 11 us: levels_plan(): pl.pallas_call(functools.partial(logits_kernel, rows, last), grid=(slab /...]
    all_to_all x1, starting transfers between devices: 5.99 us -> 2.92 us  [send_teacher(): lax.all_to_all(payload, 'vocab', split_axis=0, concat_axis=0, tiled=True)]
    ppermute x26 -> x41, waiting for transfers between devices: 69.6 us -> 71.9 us  [shift(): return lax.ppermute(x, 'vocab', [(i, i ^ distance) for i in range(n)])]
  transfers between devices with their start and end apart: 27 -> 42, of which waited for: 15 -> 14; matrix products, arithmetic and copies ran while one was open for 7% -> 6% of each run, Pallas kernels for 19% -> 17%
where the time goes in v2:
time: 189 us
  waiting for transfers between devices  71.9 us (38%)
  starting transfers between devices  46.6 us (25%)
  Pallas kernels  36.2 us (19%)
  local copies, waits for them, and re-layouts  29.5 us (16%)
  other arithmetic  3.13 us (2%)
    ppermute x41, waiting for transfers between devices, shift(): return lax.ppermute(x, 'vocab', [(i, i ^ distance) for i in range(n)])  71.9 us
    ppermute x41, starting transfers between devices, shift(): return lax.ppermute(x, 'vocab', [(i, i ^ distance) for i in range(n)])  43.6 us
    unnamed x55, local copies, waits for them, and re-layouts  21.2 us
    pallas_call x2, Pallas kernels, levels_plan(): pl.pallas_call(functools.partial(logits_kernel, rows, last), grid=(slab /...  11 us
    pallas_call x1, Pallas kernels, levels_plan(): pl.pallas_call(functools.partial(head_kernel, rows, per_chunk), grid=(dep...  10.3 us
    pallas_call x2, Pallas kernels, levels_plan(): pl.pallas_call(functools.partial(partial_kernel, rows), grid_spec=pltpu.P...  9.27 us
    dynamic_slice x1, local copies, waits for them, and re-layouts, levels_plan(): lax.dynamic_slice(head_weight, ((1 - core) * half, 0), (half, slab))  5.46 us
  transfers between devices with their start and end apart: 42, of which 14 were waited for; matrix products, arithmetic and copies ran while one was open for 6% of the time, Pallas kernels for 17%

profile of v2, /device:TPU:0, one launch (start us, length us, event | category | flops | bytes accessed | tf_op | source)
XLA Modules:
  0.0 188.9 jit_solution(4841537772019908197)
XLA Ops:
  0.6 0.9 fusion.10
  1.6 5.1 %collective-permute-start.2 = (bf16[16,2560]{1,0:T(8,128)(2,1)S(1)}, bf16[16,2560]{1,0:T(8,128)(2,1)S(1)}, u32[]{:S(2)}, u32[]{:S(2)}) collective-permute-start(bf16[16,2560]{1,0:T(8,128)(2,1)S(1)} %get-tuple-element.78), channel_id=1, source_target_pairs={{0,24},{1,25},{2,26},{3,27},{4,28},{5,29},{6,30},{7,31},{8,16},{9,... | collective-permute-start | bytes 245768 | tf_op jit(solution)/shard_map/ppermute | solution.py:127
  6.7 0.6 collective-permute-start
  7.3 3.7 %collective-permute-start.12 = (bf16[16,2560]{1,0:T(8,128)(2,1)S(1)}, bf16[16,2560]{1,0:T(8,128)(2,1)S(1)}, u32[]{:S(2)}, u32[]{:S(2)}) collective-permute-start(bf16[16,2560]{1,0:T(8,128)(2,1)S(1)} %get-tuple-element.77), channel_id=1, source_target_pairs={{0,24},{1,25},{2,26},{3,27},{4,28},{5,29},{6,30},{7,31},{8,16},{9,... | collective-permute-start | bytes 245768 | tf_op jit(solution)/shard_map/ppermute | solution.py:127
  11.1 5.5 %constant_dynamic-slice_fusion = bf16[2560,1024]{1,0:T(8,128)(2,1)} fusion(bf16[5120,1024]{1,0:T(8,128)(2,1)} %w_ref.3, s32[]{:T(128)S(6)} %select_n.57), kind=kLoop, calls=%fused_computation.51 | loop fusion | bytes 10485764 | tf_op jit(solution)/shard_map/dynamic_slice | solution.py:396
  16.8 0.5 fusion.1
  18.8 0.9 pad_maximum_fusion
  19.7 2.9 %all-to-all-start = ((bf16[32,65,128]{2,1,0:T(8,128)(2,1)}), bf16[32,65,128]{2,1,0:T(8,128)(2,1)S(1)}, u32[]{:S(2)}, u32[]{:S(2)}) async-start(bf16[32,65,128]{2,1,0:T(8,128)(2,1)} %pad_maximum_fusion), calls=%async_computation | async-start | bytes 1179648 | tf_op jit(solution)/shard_map/all_to_all | solution.py:349
  22.6 2.7 %collective-permute-start.11 = (bf16[16,2560]{1,0:T(8,128)(2,1)S(1)}, bf16[16,2560]{1,0:T(8,128)(2,1)S(1)}, u32[]{:S(2)}, u32[]{:S(2)}) collective-permute-start(bf16[16,2560]{1,0:T(8,128)(2,1)S(1)} %get-tuple-element.77), channel_id=1, source_target_pairs={{0,16},{1,17},{2,18},{3,19},{4,20},{5,21},{6,22},{7,23},{8,24},{9,... | collective-permute-start | bytes 245768 | tf_op jit(solution)/shard_map/ppermute | solution.py:127
  25.4 1.5 collective-permute-start.10
  26.9 1.5 collective-permute-start.3
  28.5 1.5 collective-permute-start.4
  30.0 12.6 %collective-permute-done.11 = bf16[16,2560]{1,0:T(8,128)(2,1)S(1)} collective-permute-done((bf16[16,2560]{1,0:T(8,128)(2,1)S(1)}, bf16[16,2560]{1,0:T(8,128)(2,1)S(1)}, u32[]{:S(2)}, u32[]{:S(2)}) %collective-permute-start.11) | collective-permute-done | bytes 81952 | tf_op jit(solution)/shard_map/ppermute | solution.py:127
  42.5 2.4 %collective-permute-start.5 = (bf16[64,2560]{1,0:T(8,128)(2,1)S(1)}, bf16[64,2560]{1,0:T(8,128)(2,1)}, u32[]{:S(2)}, u32[]{:S(2)}) collective-permute-start(bf16[64,2560]{1,0:T(8,128)(2,1)S(1)} %pad_maximum_fusion.1.refs_0_.refs_8_), channel_id=1, source_target_pairs={{0,6},{1,7},{2,4},{3,5},{4,2},{5,3},{6,0},{7,1},{8,14},{9,15},{10,... | collective-permute-start | bytes 983048 | tf_op jit(solution)/shard_map/ppermute | solution.py:127
  45.0 0.6 collective-permute-start.13
  45.6 0.6 collective-permute-start.14
  46.1 2.4 %collective-permute-start.15 = (bf16[64,2560]{1,0:T(8,128)(2,1)S(1)}, bf16[64,2560]{1,0:T(8,128)(2,1)S(1)}, u32[]{:S(2)}, u32[]{:S(2)}) collective-permute-start(bf16[64,2560]{1,0:T(8,128)(2,1)S(1)} %pad_maximum_fusion.2.refs_0_), channel_id=1, source_target_pairs={{0,6},{1,7},{2,4},{3,5},{4,2},{5,3},{6,0},{7,1},{8,14},{9,15},{10,... | collective-permute-start | bytes 983048 | tf_op jit(solution)/shard_map/ppermute | solution.py:127
  48.7 5.5 %collective-permute-done.5.refs_3_.refs_11_ = bf16[64,2560]{1,0:T(8,128)(2,1)} collective-permute-done((bf16[64,2560]{1,0:T(8,128)(2,1)S(1)}, bf16[64,2560]{1,0:T(8,128)(2,1)}, u32[]{:S(2)}, u32[]{:S(2)}) %collective-permute-start.5) | collective-permute-done | bytes 327712 | tf_op jit(solution)/shard_map/ppermute | solution.py:127
  54.2 6.9 %collective-permute-done.13.refs_1_ = bf16[64,2560]{1,0:T(8,128)(2,1)S(1)} collective-permute-done((bf16[64,2560]{1,0:T(8,128)(2,1)S(1)}, bf16[64,2560]{1,0:T(8,128)(2,1)S(1)}, u32[]{:S(2)}, u32[]{:S(2)}) %collective-permute-start.13) | collective-permute-done | bytes 327712 | tf_op jit(solution)/shard_map/ppermute | solution.py:127
  61.2 0.5 collective-permute-start.18
  61.7 5.1 %collective-permute-done.15.refs_3_ = bf16[64,2560]{1,0:T(8,128)(2,1)S(1)} collective-permute-done((bf16[64,2560]{1,0:T(8,128)(2,1)S(1)}, bf16[64,2560]{1,0:T(8,128)(2,1)S(1)}, u32[]{:S(2)}, u32[]{:S(2)}) %collective-permute-start.15) | collective-permute-done | bytes 327712 | tf_op jit(solution)/shard_map/ppermute | solution.py:127
  66.9 0.6 collective-permute-start.6
  68.5 4.0 %copy-done = bf16[5120,1024]{1,0:T(8,128)(2,1)S(1)} copy-done((bf16[5120,1024]{1,0:T(8,128)(2,1)S(1)}, bf16[5120,1024]{1,0:T(8,128)(2,1)}, u32[]{:S(2)}) %copy-start) | copy-done | bytes 10485784
  72.5 4.4 %logits.2.refs_9_ = f32[512,1024]{1,0:T(8,128)S(1)} custom-call(bf16[64,2560]{1,0:T(8,128)(2,1)S(1)} %pad_maximum_fusion.2.refs_0_, bf16[64,2560]{1,0:T(8,128)(2,1)S(1)} %collective-permute-done.13.refs_1_, bf16[64,2560]{1,0:T(8,128)(2,1)S(1)} %collective-permute-done.14.refs_2_, bf16[64,2560]{1,0:T(8,128)(2,1)S(1)} %collective-permute-done.15.refs_3_, ...), custom_call_target="tpu_custom_call" | custom-call | flops 2684354560 | bytes 9961472 | tf_op jit(solution)/shard_map/logits/pallas_call | solution.py:439
  77.0 1.3 copy-done.3
  78.3 0.7 copy-done.13
  79.0 0.7 copy-done.15
  79.8 0.8 copy-done.17
  80.5 0.7 copy-done.19
  82.4 3.2 %teacher_prob.1 = (f32[512,1024]{1,0:T(8,128)S(1)}, f32[16,128]{1,0:T(8,128)S(1)}) custom-call(s32[3]{0:T(128)S(1)} %pad_add_fusion.refs_0_, s32[4,4]{1,0:T(4,128)S(1)} %broadcast_add_fusion.refs_1_, bf16[4,4,128,128]{3,2,1,0:T(8,128)(2,1)S(1)} %bitcast.28, f32[2,4,1,128]{3,2,1,0:T(1,128)S(1)} %bitcast.29, s32[4,1,128]{2,1,0:T(1,128)S(1)} %bitcast.30, ...), custom_call_target="tpu_custom_call" | custom-call | flops 67108864 | bytes 2097152 | tf_op jit(solution)/shard_map/teacher_prob/pallas_call | solution.py:398
  85.7 4.0 %copy-done.1 = bf16[5120,1024]{1,0:T(8,128)(2,1)S(1)} copy-done((bf16[5120,1024]{1,0:T(8,128)(2,1)S(1)}, bf16[5120,1024]{1,0:T(8,128)(2,1)}, u32[]{:S(2)}) %copy-start.1) | copy-done | bytes 10485784
  89.7 1.6 copy-done.4
  91.2 6.6 %logits.3 = (f32[512,1024]{1,0:T(8,128)S(1)}, f32[2,512]{1,0:T(2,128)S(1)}) custom-call(bf16[64,2560]{1,0:T(8,128)(2,1)S(1)} %pad_maximum_fusion.1.refs_0_.refs_8_, bf16[64,2560]{1,0:T(8,128)(2,1)} %collective-permute-done.3.refs_1_.refs_9_, bf16[64,2560]{1,0:T(8,128)(2,1)} %collective-permute-done.4.refs_2_.refs_10_, ...), custom_call_target="tpu_custom_call" | custom-call | flops 2684354560 | bytes 9961472 | tf_op jit(solution)/shard_map/logits/pallas_call | solution.py:439
  97.9 1.3 copy-done.5
  99.2 3.6 %collective-permute-done.20 = f32[2,512]{1,0:T(2,128)S(1)} collective-permute-done((f32[2,512]{1,0:T(2,128)S(1)}, f32[2,512]{1,0:T(2,128)S(1)}, u32[]{:S(2)}, u32[]{:S(2)}) %collective-permute-start.20) | collective-permute-done | bytes 4128 | tf_op jit(solution)/shard_map/ppermute | solution.py:127
  103.0 4.5 %collective-permute-done.21 = f32[4,512]{1,0:T(4,128)S(1)} collective-permute-done((f32[4,512]{1,0:T(4,128)S(1)}, f32[4,512]{1,0:T(4,128)S(1)}, u32[]{:S(2)}, u32[]{:S(2)}) %collective-permute-start.21) | collective-permute-done | bytes 8224 | tf_op jit(solution)/shard_map/ppermute | solution.py:127
  107.5 1.5 collective-permute-start.22
  109.0 2.3 %collective-permute-done.22 = f32[8,512]{1,0:T(8,128)S(1)} collective-permute-done((f32[8,512]{1,0:T(8,128)S(1)}, f32[8,512]{1,0:T(8,128)S(1)}, u32[]{:S(2)}, u32[]{:S(2)}) %collective-permute-start.22) | collective-permute-done | bytes 16416 | tf_op jit(solution)/shard_map/ppermute | solution.py:127
  111.3 1.5 collective-permute-start.23
  112.9 2.4 %collective-permute-done.23 = f32[16,512]{1,0:T(8,128)S(1)} collective-permute-done((f32[16,512]{1,0:T(8,128)S(1)}, f32[16,512]{1,0:T(8,128)S(1)}, u32[]{:S(2)}, u32[]{:S(2)}) %collective-permute-start.23) | collective-permute-done | bytes 32800 | tf_op jit(solution)/shard_map/ppermute | solution.py:127
  115.4 1.2 collective-permute-done.24.refs_2_
  116.6 1.6 copy-done.6
  118.2 1.3 grad_logits.1
  119.7 2.5 %collective-permute-done.25.sib_ref = bf16[512,1024]{1,0:T(8,128)(2,1)S(1)} collective-permute-done((bf16[512,1024]{1,0:T(8,128)(2,1)S(1)}, bf16[512,1024]{1,0:T(8,128)(2,1)S(1)}, u32[]{:S(2)}, u32[]{:S(2)}) %collective-permute-start.25) | collective-permute-done | bytes 1048608 | tf_op jit(solution)/shard_map/ppermute | solution.py:127
  122.2 4.0 %copy-done.2 = bf16[5120,1024]{1,0:T(8,128)(2,1)S(1)} copy-done((bf16[5120,1024]{1,0:T(8,128)(2,1)S(1)}, bf16[5120,1024]{1,0:T(8,128)(2,1)}, u32[]{:S(2)}) %copy-start.2) | copy-done | bytes 10485784
  126.2 4.0 %grad_hidden_partial.3 = (f32[4,2,16,1024]{3,2,1,0:T(8,128)S(1)}, bf16[4,2,16,1024]{3,2,1,0:T(8,128)(2,1)S(1)}, bf16[4,2,16,1024]{3,2,1,0:T(8,128)(2,1)S(1)}, bf16[4,2,16,1024]{3,2,1,0:T(8,128)(2,1)S(1)}) custom-call(s32[1]{0:T(128)} %bitcast.core_ref, bf16[512,1024]{1,0:T(8,128)(2,1)S(1)} %get-tuple-element.43.grad_ref.refs_16_, ...), custom_call_target="tpu_custom_call" | custom-call | flops 2147483648 | bytes 4194304 | tf_op jit(solution)/shard_map/grad_hidden_partial/pallas_call | solution.py:486
  130.2 1.5 collective-permute-start.30
  131.8 5.3 %grad_hidden_partial.2 = (f32[4,2,16,1536]{3,2,1,0:T(8,128)S(1)}, bf16[4,2,16,1536]{3,2,1,0:T(8,128)(2,1)S(1)}, bf16[4,2,16,1536]{3,2,1,0:T(8,128)(2,1)S(1)}, bf16[4,2,16,1536]{3,2,1,0:T(8,128)(2,1)S(1)}) custom-call(s32[1]{0:T(128)} %bitcast.core_ref, bf16[512,1024]{1,0:T(8,128)(2,1)S(1)} %get-tuple-element.43.grad_ref.refs_16_, ...), custom_call_target="tpu_custom_call" | custom-call | flops 3221225472 | bytes 6291456 | tf_op jit(solution)/shard_map/grad_hidden_partial/pallas_call | solution.py:486
  137.1 0.6 collective-permute-start.27
  137.7 1.5 collective-permute-start.28
  139.2 1.4 collective-permute-start.29
  140.6 1.5 collective-permute-start.31
  142.1 0.5 collective-permute-start.32
  142.7 10.3 %grad_head.1 = bf16[5120,1024]{1,0:T(8,128)(2,1)} custom-call(bf16[64,2560]{1,0:T(8,128)(2,1)S(1)} %pad_maximum_fusion.2.refs_0_, bf16[64,2560]{1,0:T(8,128)(2,1)S(1)} %copy-done.8, bf16[64,2560]{1,0:T(8,128)(2,1)S(1)} %copy-done.10, bf16[64,2560]{1,0:T(8,128)(2,1)S(1)} %copy-done.12, bf16[64,2560]{1,0:T(8,128)(2,1)S(1)} %copy-done.14, ...), custom_call_target="tpu_custom_call" | custom-call | flops 5368709120 | bytes 15728640 | tf_op jit(solution)/shard_map/grad_head/pallas_call | solution.py:522
  153.1 15.1 %collective-permute-done.31.refs_1_ = bf16[4,2,16,1024]{3,2,1,0:T(8,128)(2,1)S(1)} collective-permute-done((bf16[4,2,16,1024]{3,2,1,0:T(8,128)(2,1)S(1)}, bf16[4,2,16,1024]{3,2,1,0:T(8,128)(2,1)S(1)}, u32[]{:S(2)}, u32[]{:S(2)}) %collective-permute-start.31) | collective-permute-done | bytes 262176 | tf_op jit(solution)/shard_map/ppermute | solution.py:127
  169.1 2.1 %collective-permute-start.33 = (bf16[2,16,1536]{2,1,0:T(8,128)(2,1)S(1)}, bf16[2,16,1536]{2,1,0:T(8,128)(2,1)S(1)}, u32[]{:S(2)}, u32[]{:S(2)}) collective-permute-start(bf16[2,16,1536]{2,1,0:T(8,128)(2,1)S(1)} %get-tuple-element.58), channel_id=1, source_target_pairs={{0,8},{1,9},{2,10},{3,11},{4,12},{5,13},{6,14},{7,15},{8,0},{9,1},... | collective-permute-start | bytes 294920 | tf_op jit(solution)/shard_map/ppermute | solution.py:127
  171.3 2.3 %collective-permute-start.35 = (bf16[2,16,1536]{2,1,0:T(8,128)(2,1)S(1)}, bf16[2,16,1536]{2,1,0:T(8,128)(2,1)S(1)}, u32[]{:S(2)}, u32[]{:S(2)}) collective-permute-start(bf16[2,16,1536]{2,1,0:T(8,128)(2,1)S(1)} %get-tuple-element.60), channel_id=1, source_target_pairs={{0,24},{1,25},{2,26},{3,27},{4,28},{5,29},{6,30},{7,31},{8,16},{9,... | collective-permute-start | bytes 294920 | tf_op jit(solution)/shard_map/ppermute | solution.py:127
  173.6 1.1 collective-permute-start.37
  174.7 2.3 %collective-permute-start.38 = (bf16[2,16,1024]{2,1,0:T(8,128)(2,1)S(1)}, bf16[2,16,1024]{2,1,0:T(8,128)(2,1)S(1)}, u32[]{:S(2)}, u32[]{:S(2)}) collective-permute-start(bf16[2,16,1024]{2,1,0:T(8,128)(2,1)S(1)} %get-tuple-element.69), channel_id=1, source_target_pairs={{0,24},{1,25},{2,26},{3,27},{4,28},{5,29},{6,30},{7,31},{8,16},{9,... | collective-permute-start | bytes 196616 | tf_op jit(solution)/shard_map/ppermute | solution.py:127
  177.0 0.6 slice_reduce_fusion
  177.6 8.7 %collective-permute-done.37.refs_1_ = bf16[2,16,1024]{2,1,0:T(8,128)(2,1)S(1)} collective-permute-done((bf16[2,16,1024]{2,1,0:T(8,128)(2,1)S(1)}, bf16[2,16,1024]{2,1,0:T(8,128)(2,1)S(1)}, u32[]{:S(2)}, u32[]{:S(2)}) %collective-permute-start.37) | collective-permute-done | bytes 65568 | tf_op jit(solution)/shard_map/ppermute | solution.py:127
  186.8 0.5 collective-permute-start.39
  187.3 0.9 collective-permute-done.39
  188.3 0.7 pad_maximum_fusion.3
  (129 shorter events, 6.1 us)
Async XLA Ops:
  1.6 21.0 %collective-permute-start.2 = (bf16[16,2560]{1,0:T(8,128)(2,1)S(1)}, bf16[16,2560]{1,0:T(8,128)(2,1)S(1)}, u32[]{:S(2)}, u32[]{:S(2)}) collective-permute-start(bf16[16,2560]{1,0:T(8,128)(2,1)S(1)} %get-tuple-element.78), channel_id=1, source_target_pairs={{0,24},{1,25},{2,26},{3,27},{4,28},{5,29},{6,30},{7,31},{8,16},{9,... | collective-permute-start | bytes 245768 | tf_op jit(solution)/shard_map/ppermute | solution.py:127
  6.7 18.7 %collective-permute-start.1 = (bf16[16,2560]{1,0:T(8,128)(2,1)S(1)}, bf16[16,2560]{1,0:T(8,128)(2,1)S(1)}, u32[]{:S(2)}, u32[]{:S(2)}) collective-permute-start(bf16[16,2560]{1,0:T(8,128)(2,1)S(1)} %get-tuple-element.78), channel_id=1, source_target_pairs={{0,16},{1,17},{2,18},{3,19},{4,20},{5,21},{6,22},{7,23},{8,24},{9,... | collective-permute-start | bytes 245768 | tf_op jit(solution)/shard_map/ppermute | solution.py:127
  6.7 20.2 %collective-permute-start = (bf16[16,2560]{1,0:T(8,128)(2,1)S(1)}, bf16[16,2560]{1,0:T(8,128)(2,1)S(1)}, u32[]{:S(2)}, u32[]{:S(2)}) collective-permute-start(bf16[16,2560]{1,0:T(8,128)(2,1)S(1)} %get-tuple-element.78), channel_id=1, source_target_pairs={{0,8},{1,9},{2,10},{3,11},{4,12},{5,13},{6,14},{7,15},{8,0},{9,1},... | collective-permute-start | bytes 245768 | tf_op jit(solution)/shard_map/ppermute | solution.py:127
  7.3 21.1 %collective-permute-start.12 = (bf16[16,2560]{1,0:T(8,128)(2,1)S(1)}, bf16[16,2560]{1,0:T(8,128)(2,1)S(1)}, u32[]{:S(2)}, u32[]{:S(2)}) collective-permute-start(bf16[16,2560]{1,0:T(8,128)(2,1)S(1)} %get-tuple-element.77), channel_id=1, source_target_pairs={{0,24},{1,25},{2,26},{3,27},{4,28},{5,29},{6,30},{7,31},{8,16},{9,... | collective-permute-start | bytes 245768 | tf_op jit(solution)/shard_map/ppermute | solution.py:127
  11.1 5.5 %copy-start.24 = (bf16[4,64,4,128]{3,2,1,0:T(4,128)(2,1)S(1)}, bf16[4,64,4,128]{3,2,1,0:T(4,128)(2,1)}, u32[]{:S(2)}) copy-start(bf16[4,64,4,128]{3,2,1,0:T(4,128)(2,1)} %param.9) | copy-start | bytes 786436
  11.1 6.4 %copy-start.25 = (s32[4,64]{1,0:T(4,128)S(1)}, s32[4,64]{1,0:T(4,128)}, u32[]{:S(2)}) copy-start(s32[4,64]{1,0:T(4,128)} %param.10) | copy-start | bytes 3076
  16.5 105.7 %collective-permute-start.26 = (bf16[2560,1024]{1,0:T(8,128)(2,1)}, bf16[2560,1024]{1,0:T(8,128)(2,1)}, u32[]{:S(2)}, u32[]{:S(2)}) collective-permute-start(bf16[2560,1024]{1,0:T(8,128)(2,1)} %constant_dynamic-slice_fusion), channel_id=1, source_target_pairs={{0,1},{1,0},{2,3},{3,2},{4,5},{5,4},{6,7},{7,6},{8,9},{9,8},{10,11... | collective-permute-start | bytes 15728648 | tf_op jit(solution)/shard_map/ppermute | solution.py:127
  19.7 61.6 %all-to-all-start = ((bf16[32,65,128]{2,1,0:T(8,128)(2,1)}), bf16[32,65,128]{2,1,0:T(8,128)(2,1)S(1)}, u32[]{:S(2)}, u32[]{:S(2)}) async-start(bf16[32,65,128]{2,1,0:T(8,128)(2,1)} %pad_maximum_fusion), calls=%async_computation | async-start | bytes 1179648 | tf_op jit(solution)/shard_map/all_to_all | solution.py:349
  22.6 19.9 %collective-permute-start.11 = (bf16[16,2560]{1,0:T(8,128)(2,1)S(1)}, bf16[16,2560]{1,0:T(8,128)(2,1)S(1)}, u32[]{:S(2)}, u32[]{:S(2)}) collective-permute-start(bf16[16,2560]{1,0:T(8,128)(2,1)S(1)} %get-tuple-element.77), channel_id=1, source_target_pairs={{0,16},{1,17},{2,18},{3,19},{4,20},{5,21},{6,22},{7,23},{8,24},{9,... | collective-permute-start | bytes 245768 | tf_op jit(solution)/shard_map/ppermute | solution.py:127
  25.4 19.6 %collective-permute-start.10 = (bf16[16,2560]{1,0:T(8,128)(2,1)S(1)}, bf16[16,2560]{1,0:T(8,128)(2,1)S(1)}, u32[]{:S(2)}, u32[]{:S(2)}) collective-permute-start(bf16[16,2560]{1,0:T(8,128)(2,1)S(1)} %get-tuple-element.77), channel_id=1, source_target_pairs={{0,8},{1,9},{2,10},{3,11},{4,12},{5,13},{6,14},{7,15},{8,0},{9,1},... | collective-permute-start | bytes 245768 | tf_op jit(solution)/shard_map/ppermute | solution.py:127
  26.9 18.7 %collective-permute-start.3 = (bf16[64,2560]{1,0:T(8,128)(2,1)S(1)}, bf16[64,2560]{1,0:T(8,128)(2,1)}, u32[]{:S(2)}, u32[]{:S(2)}) collective-permute-start(bf16[64,2560]{1,0:T(8,128)(2,1)S(1)} %pad_maximum_fusion.1.refs_0_.refs_8_), channel_id=1, source_target_pairs={{0,2},{1,3},{2,0},{3,1},{4,6},{5,7},{6,4},{7,5},{8,10},{9,11},{10,... | collective-permute-start | bytes 983048 | tf_op jit(solution)/shard_map/ppermute | solution.py:127
  28.5 17.7 %collective-permute-start.4 = (bf16[64,2560]{1,0:T(8,128)(2,1)S(1)}, bf16[64,2560]{1,0:T(8,128)(2,1)}, u32[]{:S(2)}, u32[]{:S(2)}) collective-permute-start(bf16[64,2560]{1,0:T(8,128)(2,1)S(1)} %pad_maximum_fusion.1.refs_0_.refs_8_), channel_id=1, source_target_pairs={{0,4},{1,5},{2,6},{3,7},{4,0},{5,1},{6,2},{7,3},{8,12},{9,13},{10,... | collective-permute-start | bytes 983048 | tf_op jit(solution)/shard_map/ppermute | solution.py:127
  42.5 11.7 %collective-permute-start.5 = (bf16[64,2560]{1,0:T(8,128)(2,1)S(1)}, bf16[64,2560]{1,0:T(8,128)(2,1)}, u32[]{:S(2)}, u32[]{:S(2)}) collective-permute-start(bf16[64,2560]{1,0:T(8,128)(2,1)S(1)} %pad_maximum_fusion.1.refs_0_.refs_8_), channel_id=1, source_target_pairs={{0,6},{1,7},{2,4},{3,5},{4,2},{5,3},{6,0},{7,1},{8,14},{9,15},{10,... | collective-permute-start | bytes 983048 | tf_op jit(solution)/shard_map/ppermute | solution.py:127
  45.0 16.2 %collective-permute-start.13 = (bf16[64,2560]{1,0:T(8,128)(2,1)S(1)}, bf16[64,2560]{1,0:T(8,128)(2,1)S(1)}, u32[]{:S(2)}, u32[]{:S(2)}) collective-permute-start(bf16[64,2560]{1,0:T(8,128)(2,1)S(1)} %pad_maximum_fusion.2.refs_0_), channel_id=1, source_target_pairs={{0,2},{1,3},{2,0},{3,1},{4,6},{5,7},{6,4},{7,5},{8,10},{9,11},{10,... | collective-permute-start | bytes 983048 | tf_op jit(solution)/shard_map/ppermute | solution.py:127
  45.6 15.6 %collective-permute-start.14 = (bf16[64,2560]{1,0:T(8,128)(2,1)S(1)}, bf16[64,2560]{1,0:T(8,128)(2,1)S(1)}, u32[]{:S(2)}, u32[]{:S(2)}) collective-permute-start(bf16[64,2560]{1,0:T(8,128)(2,1)S(1)} %pad_maximum_fusion.2.refs_0_), channel_id=1, source_target_pairs={{0,4},{1,5},{2,6},{3,7},{4,0},{5,1},{6,2},{7,3},{8,12},{9,13},{10,... | collective-permute-start | bytes 983048 | tf_op jit(solution)/shard_map/ppermute | solution.py:127
  46.1 20.6 %collective-permute-start.15 = (bf16[64,2560]{1,0:T(8,128)(2,1)S(1)}, bf16[64,2560]{1,0:T(8,128)(2,1)S(1)}, u32[]{:S(2)}, u32[]{:S(2)}) collective-permute-start(bf16[64,2560]{1,0:T(8,128)(2,1)S(1)} %pad_maximum_fusion.2.refs_0_), channel_id=1, source_target_pairs={{0,6},{1,7},{2,4},{3,5},{4,2},{5,3},{6,0},{7,1},{8,14},{9,15},{10,... | collective-permute-start | bytes 983048 | tf_op jit(solution)/shard_map/ppermute | solution.py:127
  54.2 12.7 %collective-permute-start.16 = (bf16[64,2560]{1,0:T(8,128)(2,1)S(1)}, bf16[64,2560]{1,0:T(8,128)(2,1)S(1)}, u32[]{:S(2)}, u32[]{:S(2)}) collective-permute-start(bf16[64,2560]{1,0:T(8,128)(2,1)S(1)} %pad_maximum_fusion.2.refs_0_), channel_id=1, source_target_pairs={{0,1},{1,0},{2,3},{3,2},{4,5},{5,4},{6,7},{7,6},{8,9},{9,8},{10,11... | collective-permute-start | bytes 983048 | tf_op jit(solution)/shard_map/ppermute | solution.py:127
  61.1 15.8 %copy-start.7 = (bf16[64,2560]{1,0:T(8,128)(2,1)}, bf16[64,2560]{1,0:T(8,128)(2,1)S(1)}, u32[]{:S(2)}) copy-start(bf16[64,2560]{1,0:T(8,128)(2,1)S(1)} %collective-permute-done.13.refs_1_) | copy-start | bytes 983044
  61.1 6.3 %collective-permute-start.17 = (bf16[64,2560]{1,0:T(8,128)(2,1)S(1)}, bf16[64,2560]{1,0:T(8,128)(2,1)S(1)}, u32[]{:S(2)}, u32[]{:S(2)}) collective-permute-start(bf16[64,2560]{1,0:T(8,128)(2,1)S(1)} %collective-permute-done.13.refs_1_), channel_id=1, source_target_pairs={{0,1},{1,0},{2,3},{3,2},{4,5},{5,4},{6,7},{7,6},{8,9},{9,8},{10,11... | collective-permute-start | bytes 983048 | tf_op jit(solution)/shard_map/ppermute | solution.py:127
  61.2 15.8 %copy-start.9 = (bf16[64,2560]{1,0:T(8,128)(2,1)}, bf16[64,2560]{1,0:T(8,128)(2,1)S(1)}, u32[]{:S(2)}) copy-start(bf16[64,2560]{1,0:T(8,128)(2,1)S(1)} %collective-permute-done.14.refs_2_) | copy-start | bytes 983044
  61.2 6.4 %collective-permute-start.18 = (bf16[64,2560]{1,0:T(8,128)(2,1)S(1)}, bf16[64,2560]{1,0:T(8,128)(2,1)S(1)}, u32[]{:S(2)}, u32[]{:S(2)}) collective-permute-start(bf16[64,2560]{1,0:T(8,128)(2,1)S(1)} %collective-permute-done.14.refs_2_), channel_id=1, source_target_pairs={{0,1},{1,0},{2,3},{3,2},{4,5},{5,4},{6,7},{7,6},{8,9},{9,8},{10,11... | collective-permute-start | bytes 983048 | tf_op jit(solution)/shard_map/ppermute | solution.py:127
  66.8 10.2 %copy-start.11 = (bf16[64,2560]{1,0:T(8,128)(2,1)}, bf16[64,2560]{1,0:T(8,128)(2,1)S(1)}, u32[]{:S(2)}) copy-start(bf16[64,2560]{1,0:T(8,128)(2,1)S(1)} %collective-permute-done.15.refs_3_) | copy-start | bytes 983044
  66.8 1.6 collective-permute-start.19
  66.9 15.5 %copy-start.21 = (s32[4,128]{1,0:T(4,128)S(1)}, s32[4,128]{1,0:T(4,128)}, u32[]{:S(2)}) copy-start(s32[4,128]{1,0:T(4,128)} %param.11) | copy-start | bytes 6148
  66.9 15.5 %copy-start.22 = (f32[512]{0:T(512)S(1)}, f32[512]{0:T(512)}, u32[]{:S(2)}) copy-start(f32[512]{0:T(512)} %param.12) | copy-start | bytes 6148
  66.9 18.8 %collective-permute-start.6 = (bf16[64,2560]{1,0:T(8,128)(2,1)S(1)}, bf16[64,2560]{1,0:T(8,128)(2,1)}, u32[]{:S(2)}, u32[]{:S(2)}) collective-permute-start(bf16[64,2560]{1,0:T(8,128)(2,1)S(1)} %pad_maximum_fusion.1.refs_0_.refs_8_), channel_id=1, source_target_pairs={{0,1},{1,0},{2,3},{3,2},{4,5},{5,4},{6,7},{7,6},{8,9},{9,8},{10,11... | collective-permute-start | bytes 983048 | tf_op jit(solution)/shard_map/ppermute | solution.py:127
  67.4 18.2 %collective-permute-start.7 = (bf16[64,2560]{1,0:T(8,128)(2,1)}, bf16[64,2560]{1,0:T(8,128)(2,1)}, u32[]{:S(2)}, u32[]{:S(2)}) collective-permute-start(bf16[64,2560]{1,0:T(8,128)(2,1)} %collective-permute-done.3.refs_1_.refs_9_), channel_id=1, source_target_pairs={{0,1},{1,0},{2,3},{3,2},{4,5},{5,4},{6,7},{7,6},{8,9},{9,8},{10,11... | collective-permute-start | bytes 983048 | tf_op jit(solution)/shard_map/ppermute | solution.py:127
  67.5 18.1 %collective-permute-start.8 = (bf16[64,2560]{1,0:T(8,128)(2,1)}, bf16[64,2560]{1,0:T(8,128)(2,1)}, u32[]{:S(2)}, u32[]{:S(2)}) collective-permute-start(bf16[64,2560]{1,0:T(8,128)(2,1)} %collective-permute-done.4.refs_2_.refs_10_), channel_id=1, source_target_pairs={{0,1},{1,0},{2,3},{3,2},{4,5},{5,4},{6,7},{7,6},{8,9},{9,8},{10,11... | collective-permute-start | bytes 983048 | tf_op jit(solution)/shard_map/ppermute | solution.py:127
  68.4 17.3 %collective-permute-start.9 = (bf16[64,2560]{1,0:T(8,128)(2,1)}, bf16[64,2560]{1,0:T(8,128)(2,1)}, u32[]{:S(2)}, u32[]{:S(2)}) collective-permute-start(bf16[64,2560]{1,0:T(8,128)(2,1)} %collective-permute-done.5.refs_3_.refs_11_), channel_id=1, source_target_pairs={{0,1},{1,0},{2,3},{3,2},{4,5},{5,4},{6,7},{7,6},{8,9},{9,8},{10,11... | collective-permute-start | bytes 983048 | tf_op jit(solution)/shard_map/ppermute | solution.py:127
  68.5 4.0 %copy-start = (bf16[5120,1024]{1,0:T(8,128)(2,1)S(1)}, bf16[5120,1024]{1,0:T(8,128)(2,1)}, u32[]{:S(2)}) copy-start(bf16[5120,1024]{1,0:T(8,128)(2,1)} %w_ref.3) | copy-start | bytes 31457284
  77.0 1.3 copy-start.3
  85.7 4.0 %copy-start.1 = (bf16[5120,1024]{1,0:T(8,128)(2,1)S(1)}, bf16[5120,1024]{1,0:T(8,128)(2,1)}, u32[]{:S(2)}) copy-start(bf16[5120,1024]{1,0:T(8,128)(2,1)} %w_ref.3) | copy-start | bytes 31457284
  89.7 1.6 copy-start.4
  91.2 25.4 %copy-start.23 = (f32[512]{0:T(512)S(1)}, f32[512]{0:T(512)}, u32[]{:S(2)}) copy-start(f32[512]{0:T(512)} %param.13) | copy-start | bytes 6148
  97.9 1.3 copy-start.5
  99.2 3.6 %collective-permute-start.20 = (f32[2,512]{1,0:T(2,128)S(1)}, f32[2,512]{1,0:T(2,128)S(1)}, u32[]{:S(2)}, u32[]{:S(2)}) collective-permute-start(f32[2,512]{1,0:T(2,128)S(1)} %get-tuple-element.39), channel_id=1, source_target_pairs={{0,8},{1,9},{2,10},{3,11},{4,12},{5,13},{6,14},{7,15},{8,0},{9,1},... | collective-permute-start | bytes 12296 | tf_op jit(solution)/shard_map/ppermute | solution.py:127
  102.9 4.6 %collective-permute-start.21 = (f32[4,512]{1,0:T(4,128)S(1)}, f32[4,512]{1,0:T(4,128)S(1)}, u32[]{:S(2)}, u32[]{:S(2)}) collective-permute-start(f32[4,512]{1,0:T(4,128)S(1)} %pad_maximum_fusion.6), channel_id=1, source_target_pairs={{0,16},{1,17},{2,18},{3,19},{4,20},{5,21},{6,22},{7,23},{8,24},{9,... | collective-permute-start | bytes 24584 | tf_op jit(solution)/shard_map/ppermute | solution.py:127
  107.5 3.8 %collective-permute-start.22 = (f32[8,512]{1,0:T(8,128)S(1)}, f32[8,512]{1,0:T(8,128)S(1)}, u32[]{:S(2)}, u32[]{:S(2)}) collective-permute-start(f32[8,512]{1,0:T(8,128)S(1)} %pad_maximum_fusion.5), channel_id=1, source_target_pairs={{0,2},{1,3},{2,0},{3,1},{4,6},{5,7},{6,4},{7,5},{8,10},{9,11},{10,... | collective-permute-start | bytes 49160 | tf_op jit(solution)/shard_map/ppermute | solution.py:127
  111.3 4.0 %collective-permute-start.23 = (f32[16,512]{1,0:T(8,128)S(1)}, f32[16,512]{1,0:T(8,128)S(1)}, u32[]{:S(2)}, u32[]{:S(2)}) collective-permute-start(f32[16,512]{1,0:T(8,128)S(1)} %pad_maximum_fusion.4), channel_id=1, source_target_pairs={{0,4},{1,5},{2,6},{3,7},{4,0},{5,1},{6,2},{7,3},{8,12},{9,13},{10,... | collective-permute-start | bytes 98312 | tf_op jit(solution)/shard_map/ppermute | solution.py:127
  115.3 1.3 collective-permute-start.24
  116.6 1.6 copy-start.6
  119.5 2.7 %collective-permute-start.25 = (bf16[512,1024]{1,0:T(8,128)(2,1)S(1)}, bf16[512,1024]{1,0:T(8,128)(2,1)S(1)}, u32[]{:S(2)}, u32[]{:S(2)}) collective-permute-start(bf16[512,1024]{1,0:T(8,128)(2,1)S(1)} %get-tuple-element.43.grad_ref.refs_16_), channel_id=1, source_target_pairs={{0,1},{1,0},{2,3},{3,2},{4,5},{5,4},{6,7},{7,6},{8,9},{9,8},{10,11... | collective-permute-start | bytes 3145736 | tf_op jit(solution)/shard_map/ppermute | solution.py:127
  122.2 4.0 %copy-start.2 = (bf16[5120,1024]{1,0:T(8,128)(2,1)S(1)}, bf16[5120,1024]{1,0:T(8,128)(2,1)}, u32[]{:S(2)}) copy-start(bf16[5120,1024]{1,0:T(8,128)(2,1)} %w_ref.3) | copy-start | bytes 31457284
  130.2 12.5 %copy-start.8 = (bf16[64,2560]{1,0:T(8,128)(2,1)S(1)}, bf16[64,2560]{1,0:T(8,128)(2,1)}, u32[]{:S(2)}) copy-start(bf16[64,2560]{1,0:T(8,128)(2,1)} %copy-done.7) | copy-start | bytes 983044
  130.2 12.5 %copy-start.10 = (bf16[64,2560]{1,0:T(8,128)(2,1)S(1)}, bf16[64,2560]{1,0:T(8,128)(2,1)}, u32[]{:S(2)}) copy-start(bf16[64,2560]{1,0:T(8,128)(2,1)} %copy-done.9) | copy-start | bytes 983044
  130.2 12.5 %copy-start.12 = (bf16[64,2560]{1,0:T(8,128)(2,1)S(1)}, bf16[64,2560]{1,0:T(8,128)(2,1)}, u32[]{:S(2)}) copy-start(bf16[64,2560]{1,0:T(8,128)(2,1)} %copy-done.11) | copy-start | bytes 983044
  130.2 12.5 %copy-start.14 = (bf16[64,2560]{1,0:T(8,128)(2,1)S(1)}, bf16[64,2560]{1,0:T(8,128)(2,1)}, u32[]{:S(2)}) copy-start(bf16[64,2560]{1,0:T(8,128)(2,1)} %copy-done.13) | copy-start | bytes 983044
  130.2 12.5 %copy-start.16 = (bf16[64,2560]{1,0:T(8,128)(2,1)S(1)}, bf16[64,2560]{1,0:T(8,128)(2,1)}, u32[]{:S(2)}) copy-start(bf16[64,2560]{1,0:T(8,128)(2,1)} %copy-done.15) | copy-start | bytes 983044
  130.2 12.5 %copy-start.18 = (bf16[64,2560]{1,0:T(8,128)(2,1)S(1)}, bf16[64,2560]{1,0:T(8,128)(2,1)}, u32[]{:S(2)}) copy-start(bf16[64,2560]{1,0:T(8,128)(2,1)} %copy-done.17) | copy-start | bytes 983044
  130.2 12.5 %copy-start.20 = (bf16[64,2560]{1,0:T(8,128)(2,1)S(1)}, bf16[64,2560]{1,0:T(8,128)(2,1)}, u32[]{:S(2)}) copy-start(bf16[64,2560]{1,0:T(8,128)(2,1)} %copy-done.19) | copy-start | bytes 983044
  130.2 11.9 %collective-permute-start.30 = (bf16[4,2,16,1024]{3,2,1,0:T(8,128)(2,1)S(1)}, bf16[4,2,16,1024]{3,2,1,0:T(8,128)(2,1)S(1)}, u32[]{:S(2)}, u32[]{:S(2)}) collective-permute-start(bf16[4,2,16,1024]{3,2,1,0:T(8,128)(2,1)S(1)} %get-tuple-element.49), channel_id=1, source_target_pairs={{0,2},{1,3},{2,0},{3,1},{4,6},{5,7},{6,4},{7,5},{8,10},{9,11},{10,... | collective-permute-start | bytes 786440 | tf_op jit(solution)/shard_map/ppermute | solution.py:127
  137.1 31.1 %collective-permute-start.27 = (bf16[4,2,16,1536]{3,2,1,0:T(8,128)(2,1)S(1)}, bf16[4,2,16,1536]{3,2,1,0:T(8,128)(2,1)S(1)}, u32[]{:S(2)}, u32[]{:S(2)}) collective-permute-start(bf16[4,2,16,1536]{3,2,1,0:T(8,128)(2,1)S(1)} %get-tuple-element.45), channel_id=1, source_target_pairs={{0,2},{1,3},{2,0},{3,1},{4,6},{5,7},{6,4},{7,5},{8,10},{9,11},{10,... | collective-permute-start | bytes 1179656 | tf_op jit(solution)/shard_map/ppermute | solution.py:127
  137.7 30.5 %collective-permute-start.28 = (bf16[4,2,16,1536]{3,2,1,0:T(8,128)(2,1)S(1)}, bf16[4,2,16,1536]{3,2,1,0:T(8,128)(2,1)S(1)}, u32[]{:S(2)}, u32[]{:S(2)}) collective-permute-start(bf16[4,2,16,1536]{3,2,1,0:T(8,128)(2,1)S(1)} %get-tuple-element.46), channel_id=1, source_target_pairs={{0,4},{1,5},{2,6},{3,7},{4,0},{5,1},{6,2},{7,3},{8,12},{9,13},{10,... | collective-permute-start | bytes 1179656 | tf_op jit(solution)/shard_map/ppermute | solution.py:127
  139.2 29.0 %collective-permute-start.29 = (bf16[4,2,16,1536]{3,2,1,0:T(8,128)(2,1)S(1)}, bf16[4,2,16,1536]{3,2,1,0:T(8,128)(2,1)S(1)}, u32[]{:S(2)}, u32[]{:S(2)}) collective-permute-start(bf16[4,2,16,1536]{3,2,1,0:T(8,128)(2,1)S(1)} %get-tuple-element.47), channel_id=1, source_target_pairs={{0,6},{1,7},{2,4},{3,5},{4,2},{5,3},{6,0},{7,1},{8,14},{9,15},{10,... | collective-permute-start | bytes 1179656 | tf_op jit(solution)/shard_map/ppermute | solution.py:127
  140.6 27.6 %collective-permute-start.31 = (bf16[4,2,16,1024]{3,2,1,0:T(8,128)(2,1)S(1)}, bf16[4,2,16,1024]{3,2,1,0:T(8,128)(2,1)S(1)}, u32[]{:S(2)}, u32[]{:S(2)}) collective-permute-start(bf16[4,2,16,1024]{3,2,1,0:T(8,128)(2,1)S(1)} %get-tuple-element.50), channel_id=1, source_target_pairs={{0,4},{1,5},{2,6},{3,7},{4,0},{5,1},{6,2},{7,3},{8,12},{9,13},{10,... | collective-permute-start | bytes 786440 | tf_op jit(solution)/shard_map/ppermute | solution.py:127
  142.1 26.1 %collective-permute-start.32 = (bf16[4,2,16,1024]{3,2,1,0:T(8,128)(2,1)S(1)}, bf16[4,2,16,1024]{3,2,1,0:T(8,128)(2,1)S(1)}, u32[]{:S(2)}, u32[]{:S(2)}) collective-permute-start(bf16[4,2,16,1024]{3,2,1,0:T(8,128)(2,1)S(1)} %get-tuple-element.51), channel_id=1, source_target_pairs={{0,6},{1,7},{2,4},{3,5},{4,2},{5,3},{6,0},{7,1},{8,14},{9,15},{10,... | collective-permute-start | bytes 786440 | tf_op jit(solution)/shard_map/ppermute | solution.py:127
  168.5 6.1 %collective-permute-start.36 = (bf16[2,16,1024]{2,1,0:T(8,128)(2,1)S(1)}, bf16[2,16,1024]{2,1,0:T(8,128)(2,1)S(1)}, u32[]{:S(2)}, u32[]{:S(2)}) collective-permute-start(bf16[2,16,1024]{2,1,0:T(8,128)(2,1)S(1)} %get-tuple-element.67), channel_id=1, source_target_pairs={{0,8},{1,9},{2,10},{3,11},{4,12},{5,13},{6,14},{7,15},{8,0},{9,1},... | collective-permute-start | bytes 196616 | tf_op jit(solution)/shard_map/ppermute | solution.py:127
  169.1 17.5 %collective-permute-start.33 = (bf16[2,16,1536]{2,1,0:T(8,128)(2,1)S(1)}, bf16[2,16,1536]{2,1,0:T(8,128)(2,1)S(1)}, u32[]{:S(2)}, u32[]{:S(2)}) collective-permute-start(bf16[2,16,1536]{2,1,0:T(8,128)(2,1)S(1)} %get-tuple-element.58), channel_id=1, source_target_pairs={{0,8},{1,9},{2,10},{3,11},{4,12},{5,13},{6,14},{7,15},{8,0},{9,1},... | collective-permute-start | bytes 294920 | tf_op jit(solution)/shard_map/ppermute | solution.py:127
  171.1 15.4 %collective-permute-start.34 = (bf16[2,16,1536]{2,1,0:T(8,128)(2,1)S(1)}, bf16[2,16,1536]{2,1,0:T(8,128)(2,1)S(1)}, u32[]{:S(2)}, u32[]{:S(2)}) collective-permute-start(bf16[2,16,1536]{2,1,0:T(8,128)(2,1)S(1)} %get-tuple-element.59), channel_id=1, source_target_pairs={{0,16},{1,17},{2,18},{3,19},{4,20},{5,21},{6,22},{7,23},{8,24},{9,... | collective-permute-start | bytes 294920 | tf_op jit(solution)/shard_map/ppermute | solution.py:127
  171.3 15.3 %collective-permute-start.35 = (bf16[2,16,1536]{2,1,0:T(8,128)(2,1)S(1)}, bf16[2,16,1536]{2,1,0:T(8,128)(2,1)S(1)}, u32[]{:S(2)}, u32[]{:S(2)}) collective-permute-start(bf16[2,16,1536]{2,1,0:T(8,128)(2,1)S(1)} %get-tuple-element.60), channel_id=1, source_target_pairs={{0,24},{1,25},{2,26},{3,27},{4,28},{5,29},{6,30},{7,31},{8,16},{9,... | collective-permute-start | bytes 294920 | tf_op jit(solution)/shard_map/ppermute | solution.py:127
  173.6 12.8 %collective-permute-start.37 = (bf16[2,16,1024]{2,1,0:T(8,128)(2,1)S(1)}, bf16[2,16,1024]{2,1,0:T(8,128)(2,1)S(1)}, u32[]{:S(2)}, u32[]{:S(2)}) collective-permute-start(bf16[2,16,1024]{2,1,0:T(8,128)(2,1)S(1)} %get-tuple-element.68), channel_id=1, source_target_pairs={{0,16},{1,17},{2,18},{3,19},{4,20},{5,21},{6,22},{7,23},{8,24},{9,... | collective-permute-start | bytes 196616 | tf_op jit(solution)/shard_map/ppermute | solution.py:127
  174.7 11.7 %collective-permute-start.38 = (bf16[2,16,1024]{2,1,0:T(8,128)(2,1)S(1)}, bf16[2,16,1024]{2,1,0:T(8,128)(2,1)S(1)}, u32[]{:S(2)}, u32[]{:S(2)}) collective-permute-start(bf16[2,16,1024]{2,1,0:T(8,128)(2,1)S(1)} %get-tuple-element.69), channel_id=1, source_target_pairs={{0,24},{1,25},{2,26},{3,27},{4,28},{5,29},{6,30},{7,31},{8,16},{9,... | collective-permute-start | bytes 196616 | tf_op jit(solution)/shard_map/ppermute | solution.py:127
  186.5 1.8 collective-permute-start.40
  186.8 1.4 collective-permute-start.39
  (4 other events, 3.0 us)

commit v3 on v2

--- a/solution.py
+++ b/solution.py
@@ -105,9 +105,7 @@
 CHIPS = 4
 GROUP = CORES * CHIPS
 SLOTS = 4
-VMEM_LIMIT = 30 * 1024 * 1024
-HIDDEN_CHUNKS = 2
-PARTIAL_CHUNKS = (3, 2)
+VMEM_LIMIT = 56 * 1024 * 1024
 
 
 def kernel_params():
@@ -125,10 +123,6 @@
 def shift(x, distance):
     n = lax.axis_size("vocab")
     return lax.ppermute(x, "vocab", [(i, i ^ distance) for i in range(n)])
-
-
-def tile_of(size):
-    return 512 if size % 512 == 0 else 128
 
 
 def token_places(place, rows, side):
@@ -175,15 +169,15 @@
             entropy_ref[...] = jnp.broadcast_to(entropy[:rows], entropy_ref.shape)
 
 
-def assemble(pieces, rows, out_ref):
-    layers = pieces[0].shape[0] // rows
-    for k in range(layers):
-        for p, piece in enumerate(pieces):
-            out_ref[pl.ds((k * GROUP + p) * rows, rows), :] = piece[pl.ds(k * rows, rows), :]
-
-
-def logits_kernel(rows, last, *refs):
-    pieces, w_ref, refs = refs[:GROUP], refs[GROUP], refs[GROUP + 1 :]
+def assemble(pieces, places, rows, out_ref):
+    for piece, blocks in zip(pieces, places):
+        for i, block in enumerate(blocks):
+            out_ref[pl.ds(block * rows, rows), :] = piece[pl.ds(i * rows, rows), :]
+
+
+def logits_kernel(rows, places, last, *refs):
+    count = len(places)
+    pieces, w_ref, refs = refs[:count], refs[count], refs[count + 1 :]
     if last:
         before_ref, prob_ref, logits_ref, stat_ref, hidden, cross_ref = refs
     else:
@@ -192,7 +186,7 @@
 
     @pl.when(step == 0)
     def _():
-        assemble(pieces, rows, hidden)
+        assemble(pieces, places, rows, hidden)
 
     part = jnp.dot(hidden[...], w_ref[...], preferred_element_type=jnp.float32)
     if not last:
@@ -222,33 +216,40 @@
         cross = jnp.sum(cross_ref[...], axis=1, keepdims=True)
         lane = lax.broadcasted_iota(jnp.int32, (1, 128), 1)
         both = jnp.where(lane == 0, norm, jnp.where(lane == 1, cross, 0.0))
-        stat_ref[...] = both.T[:2]
+        both = both.T
+        tokens = logits.shape[0]
+        packed = [both[i : i + 1, t : t + 128] for i in range(2) for t in range(0, tokens, 128)]
+        stat_ref[...] = jnp.broadcast_to(jnp.concatenate(packed, axis=0)[None], stat_ref.shape)
 
 
 def grad_kernel(
-    rows, pos_ref, own_ref, sib_ref, logits_ref, prob_ref, weight_ref, entropy_ref, grad_ref, loss_ref
+    rows, pos_ref, stat_ref, logits_ref, prob_ref, weight_ref, entropy_ref, grad_ref, loss_ref
 ):
     tokens = logits_ref.shape[0]
     devices = tokens // rows
     layers, _, side = weight_ref.shape
     layer_bits = (devices // GROUP).bit_length() - 1
     pos = [pos_ref[i] for i in range(3)]
+    rank = pos_ref[3]
     lane = lax.broadcasted_iota(jnp.int32, (1, 128), 1)
+    per_stat = stat_ref.shape[1] // 2
+    norms, crosses = [
+        jnp.concatenate([stat_ref[:, i * per_stat + t, :] for t in range(per_stat)], axis=1) for i in range(2)
+    ]
     stat = jnp.concatenate(
-        [own_ref[...], sib_ref[...], jnp.zeros((128 - 2 * devices, tokens), jnp.float32)], axis=0
+        [norms, crosses, jnp.zeros((128 - 2 * devices, tokens), jnp.float32)], axis=0
     ).T
-    pairs = [(1 + i, 3 + i) for i in range(layer_bits)]
-    pairs += [(1 + layer_bits, 0), (2 + layer_bits, 1), (3 + layer_bits, 2)]
-    for lane_bit, block_bit in pairs:
+    pairs = [(0, 2), (1, 0), (2, 1)] + [(3 + i, 3 + i) for i in range(layer_bits)]
+    for index_bit, block_bit in pairs:
         halves = stat.reshape(devices >> (block_bit + 1), 2, rows << block_bit, 128)
         swapped = jnp.stack([halves[:, 1], halves[:, 0]], axis=1).reshape(tokens, 128)
-        stat = jnp.where((lane >> lane_bit) & 1 == 1, swapped, stat)
-    used = lane < 2 * devices
-    is_norm = used & (lane % 2 == 0)
+        stat = jnp.where(((lane ^ rank) >> index_bit) & 1 == 1, swapped, stat)
+    is_norm = lane < devices
+    is_cross = (lane >= devices) & (lane < 2 * devices)
     top = jnp.max(jnp.where(is_norm, stat, -jnp.inf), axis=1, keepdims=True)
     total = jnp.sum(jnp.where(is_norm, jnp.exp(stat - top), 0.0), axis=1, keepdims=True)
     log_norm = top + jnp.log(total)
-    cross = jnp.sum(jnp.where(used & (lane % 2 == 1), stat, 0.0), axis=1, keepdims=True)
+    cross = jnp.sum(jnp.where(is_cross, stat, 0.0), axis=1, keepdims=True)
     loss_ref[...] = entropy_ref[...] - cross[:rows] + log_norm[:rows]
     where_token = token_places(pos, rows, side)
     for k in range(layers):
@@ -258,9 +259,8 @@
         grad_ref[span, :] = (weight * (student - prob_ref[span, :])).astype(grad_ref.dtype)
 
 
-def partial_kernel(rows, core_ref, grad_ref, sib_ref, w_ref, sib_w_ref, *refs):
-    outs, swapped = refs[:CHIPS], refs[CHIPS]
-    layers = outs[0].shape[0]
+def partial_kernel(rows, by_layer, pos_ref, grad_ref, sib_ref, w_ref, sib_w_ref, out_ref, swapped):
+    layers = out_ref.shape[0] if by_layer else out_ref.shape[1]
     half = CHIPS * rows
 
     @pl.when(pl.program_id(0) == 0)
@@ -277,43 +277,55 @@
     ) + lax.dot_general(
         swapped[...], sib_w_ref[...], contract, preferred_element_type=jnp.float32
     )
-    for j, out in enumerate(outs):
-        for k in range(layers):
+    for k in range(layers):
+        for j in range(CHIPS):
             for core in range(CORES):
                 start = (k * GROUP + core * CHIPS + j) * rows
-                out[k, core] = total[start : start + rows].astype(out.dtype)
-
-
-def head_kernel(rows, chunk_steps, *refs):
+                part = total[start : start + rows].astype(out_ref.dtype)
+                if by_layer:
+                    out_ref[pos_ref[2] ^ k, j, core] = part
+                else:
+                    out_ref[pos_ref[1] ^ j, k, core] = part
+
+
+def head_kernel(rows, places, *refs):
     pieces, (grad_ref, out_ref, hidden) = refs[:-3], refs[-3:]
-    chunk = pl.program_id(0) // chunk_steps
-    for i in range(len(pieces) // GROUP):
-
-        @pl.when(chunk == i)
+    step = pl.program_id(0)
+    done, first = 0, 0
+    for blocks, steps in places:
+        some = pieces[done : done + len(blocks)]
+
+        @pl.when((step >= first) & (step < first + steps))
         def _():
-            assemble(pieces[i * GROUP : (i + 1) * GROUP], rows, hidden)
-
+            assemble(some, blocks, rows, hidden)
+
+        done, first = done + len(blocks), first + steps
     out_ref[...] = lax.dot_general(
         hidden[...], grad_ref[...], (((0,), (0,)), ((), ())), preferred_element_type=jnp.float32
     ).astype(out_ref.dtype)
 
 
-def chip_sum_kernel(own_ref, *refs):
-    arrived, outs = refs[: CHIPS - 1], refs[CHIPS - 1 :]
-    for k, out in enumerate(outs):
-        total = own_ref[k]
-        for part in arrived:
-            total = total + part[k].astype(jnp.float32)
-        out[...] = total.astype(out.dtype)
-
-
-def layer_sum_kernel(own_ref, *refs):
-    arrived, (mine, theirs) = refs[:-2], refs[-2:]
-    total = own_ref[...]
-    for part in arrived:
-        total = total + part[...].astype(jnp.float32)
-    mine[...] = total[0].astype(mine.dtype)
-    theirs[...] = total[1].astype(theirs.dtype)
+def total_of(parts_ref, index=()):
+    total = parts_ref[(0, *index)].astype(jnp.float32)
+    for i in range(1, parts_ref.shape[0]):
+        total = total + parts_ref[(i, *index)].astype(jnp.float32)
+    return total
+
+
+def first_sum_kernel(axis, pos_ref, parts_ref, out_ref):
+    for i in range(out_ref.shape[0]):
+        out_ref[pos_ref[axis] ^ i] = total_of(parts_ref, (i,)).astype(out_ref.dtype)
+
+
+def last_sum_kernel(*refs):
+    parts, (mine, theirs) = refs[:-2], refs[-2:]
+    first = 0
+    for part in parts:
+        total = total_of(part)
+        span = pl.ds(first, total.shape[-1])
+        mine[:, span] = total[0].astype(mine.dtype)
+        theirs[:, span] = total[1].astype(theirs.dtype)
+        first += total.shape[-1]
 
 
 def split_three(x):
@@ -379,21 +391,40 @@
     half = depth // CORES
     bf16, f32 = jnp.bfloat16, jnp.float32
     core, chip, layer = rank % CORES, (rank // CORES) % CHIPS, rank // GROUP
-    pos = jnp.stack([core, chip, layer]).astype(jnp.int32)
+    pos = jnp.stack([core, chip, layer, rank]).astype(jnp.int32)
     unlisted = float(n * slab - side * listed_count)
-
-    chunks = HIDDEN_CHUNKS if depth % (HIDDEN_CHUNKS * 256) == 0 else 1
-    chunk = depth // chunks
-    pieces = []
-    for i in range(chunks):
-        own = hidden_states[:, i * chunk : (i + 1) * chunk]
-        column = [own] + [shift(own, k * GROUP) for k in range(1, layers)]
-        column = jnp.concatenate(column, axis=0)
-        plane = [column] + [shift(column, j * CORES) for j in range(1, CHIPS)]
-        pieces.append(plane + [shift(piece, 1) for piece in plane])
+    in_layer = [[(o * CHIPS + q) * CORES + c for q in range(CHIPS)] for o in range(layers) for c in range(CORES)]
+    across = [[o * GROUP + i for o in range(layers)] for i in range(GROUP)]
+
+    wide = depth * 3 // 4
+    own = hidden_states[:, :wide]
+    column = [own] + [shift(own, k * GROUP) for k in range(1, layers)]
+    column = jnp.concatenate(column, axis=0)
+    plane = hidden_states[:, wide:]
+    for j in (1, 2):
+        plane = jnp.concatenate([plane, shift(plane, j * CORES)], axis=0)
 
     arrived_blocks, arrived_stat, place = send_teacher(teacher_logits, block_lists, slab // side)
-    sib_w = shift(lax.dynamic_slice(head_weight, ((1 - core) * half, 0), (half, slab)), 1)
+
+    column, plane, late_weight = lax.optimization_barrier((column, plane, head_weight))
+    wide_pieces = [column] + [shift(column, j * CORES) for j in range(1, CHIPS)]
+    wide_pieces += [shift(piece, 1) for piece in wide_pieces]
+    wide_places = [[k * GROUP + p for k in range(layers)] for p in range(GROUP)]
+    narrow_pieces = [plane]
+    narrow_layers = [[0]]
+    for k in [1 << i for i in reversed(range((layers - 1).bit_length()))]:
+        if k > 1:
+            narrow_pieces = [jnp.concatenate([plane, shift(plane, k * GROUP)], axis=0)]
+            plane = narrow_pieces[0]
+            narrow_layers = [narrow_layers[0] + [i ^ k for i in narrow_layers[0]]]
+        else:
+            narrow_pieces.append(shift(plane, GROUP))
+            narrow_layers.append([i ^ 1 for i in narrow_layers[0]])
+    narrow_pieces += [shift(piece, 1) for piece in narrow_pieces]
+    narrow_places = [
+        [k * GROUP + c * CHIPS + j for k in some for j in range(CHIPS)] for c in range(CORES) for some in narrow_layers
+    ]
+    sib_w = shift(lax.dynamic_slice(late_weight, ((1 - core) * half, 0), (half, slab)), 1)
 
     prob, entropy = pl.pallas_call(
         lambda *refs: teacher_kernel(unlisted, rows, *refs),
@@ -418,29 +449,29 @@
     )
 
     width = 256 if slab % 256 == 0 else 128
-    logits = None
-    for i in range(chunks):
-        last = i == chunks - 1
-        whole = lambda t: (0, 0)
-        across = pl.BlockSpec((tokens, width), lambda t: (0, t))
-        in_specs = [pl.BlockSpec((layers * rows, chunk), whole) for _ in range(GROUP)]
-        in_specs.append(pl.BlockSpec((chunk, width), lambda t, i=i: (i, t)))
-        operands = pieces[i] + [head_weight]
+    whole = lambda t: (0, 0)
+    tile_out = pl.BlockSpec((tokens, width), lambda t: (0, t))
+    narrow = depth - wide
+
+    def logits_call(pieces, places, chunk, first, before=None):
+        last = before is not None
+        out_shape = [jax.ShapeDtypeStruct((tokens, slab), f32)]
+        out_specs = [tile_out]
         scratch = [pltpu.VMEM((tokens, chunk), bf16)]
-        out_shape = [jax.ShapeDtypeStruct((tokens, slab), f32)]
-        out_specs = [across]
         if last:
-            before = jnp.zeros((tokens, slab), f32) if logits is None else logits
-            in_specs += [across, across]
-            operands += [before, prob]
             scratch.append(pltpu.VMEM((tokens, 128), f32))
-            out_shape.append(jax.ShapeDtypeStruct((2, tokens), f32))
-            out_specs = [pl.BlockSpec((tokens, slab), whole), pl.BlockSpec((2, tokens), whole)]
-        outs = pl.pallas_call(
-            functools.partial(logits_kernel, rows, last),
+            out_shape.append(jax.ShapeDtypeStruct((n, 2 * tokens // 128, 128), f32))
+            out_specs = [
+                pl.BlockSpec((tokens, slab), whole),
+                pl.BlockSpec((n, 2 * tokens // 128, 128), lambda t: (0, 0, 0)),
+            ]
+        return pl.pallas_call(
+            functools.partial(logits_kernel, rows, places, last),
             grid=(slab // width,),
             out_shape=out_shape,
-            in_specs=in_specs,
+            in_specs=[pl.BlockSpec(piece.shape, whole) for piece in pieces]
+            + [pl.BlockSpec((chunk, width), lambda t: (first // chunk, t))]
+            + [tile_out] * (2 * last),
             out_specs=out_specs,
             scratch_shapes=scratch,
             compiler_params=kernel_params(),
@@ -450,15 +481,11 @@
                 transcendentals=tokens * slab if last else 0,
             ),
             name="logits",
-        )(*operands)
-        logits = outs[0]
-    stat = outs[1]
-
-    distances = [1 << i for i in range((n // GROUP).bit_length() - 1)]
-    distances = [d * GROUP for d in distances] + [CORES, 2 * CORES]
-    for distance in distances:
-        stat = jnp.concatenate([stat, shift(stat, distance)], axis=0)
-    sib_stat = shift(stat, 1)
+        )(*pieces, head_weight, *((before, prob) if last else ()))
+
+    (logits,) = logits_call(narrow_pieces, narrow_places, narrow, wide)
+    logits, stat = logits_call(wide_pieces, wide_places, wide, 0, logits)
+    stat = lax.all_to_all(stat, "vocab", split_axis=0, concat_axis=0, tiled=True)
 
     grad, loss = pl.pallas_call(
         lambda *refs: grad_kernel(rows, *refs),
@@ -466,63 +493,70 @@
             jax.ShapeDtypeStruct((tokens, slab), bf16),
             jax.ShapeDtypeStruct((rows, side), f32),
         ),
-        in_specs=[smem_spec()] + [vmem_spec()] * 6,
+        in_specs=[smem_spec()] + [vmem_spec()] * 5,
         out_specs=(vmem_spec(), vmem_spec()),
         compiler_params=kernel_params(),
         cost_estimate=pl.CostEstimate(
             flops=4 * tokens * slab, bytes_accessed=10 * tokens * slab, transcendentals=tokens * slab
         ),
         name="grad_logits",
-    )(pos, stat, sib_stat, logits, prob, token_weight.reshape(blocks, 1, side), entropy)
+    )(pos, stat, logits, prob, token_weight.reshape(blocks, 1, side), entropy)
     sib_grad = shift(grad, 1)
 
-    tile = tile_of(half)
-    steps = half // tile
-    sizes = PARTIAL_CHUNKS if sum(PARTIAL_CHUNKS) == steps else (steps,)
+    back = half // 10 * 3 // 256 * 256
     sent = []
-    for i, size in enumerate(sizes):
-        first = sum(sizes[:i])
-        out_block = pl.BlockSpec((layers, CORES, rows, tile), lambda t, core: (0, 0, 0, t))
+    for first, size, by_layer in ((0, half - back, False), (half - back, back, True)):
+        tile = size // 2 if size % 256 == 0 and size > 1024 else size
+        steps = size // tile
+        shape = (layers, CHIPS, CORES, rows) if by_layer else (CHIPS, layers, CORES, rows)
         partial = pl.pallas_call(
-            functools.partial(partial_kernel, rows),
+            functools.partial(partial_kernel, rows, by_layer),
             grid_spec=pltpu.PrefetchScalarGridSpec(
                 num_scalar_prefetch=1,
-                grid=(size,),
+                grid=(steps,),
                 in_specs=[
-                    pl.BlockSpec((tokens, slab), lambda t, core: (0, 0)),
-                    pl.BlockSpec((tokens, slab), lambda t, core: (0, 0)),
-                    pl.BlockSpec((tile, slab), lambda t, core, first=first: (core[0] * steps + first + t, 0)),
-                    pl.BlockSpec((tile, slab), lambda t, core, first=first: (first + t, 0)),
+                    pl.BlockSpec((tokens, slab), lambda t, pos: (0, 0)),
+                    pl.BlockSpec((tokens, slab), lambda t, pos: (0, 0)),
+                    pl.BlockSpec(
+                        (pl.Element(tile), pl.Element(slab)),
+                        lambda t, pos, first=first, tile=tile: (pl.multiple_of(pos[0] * half + first + t * tile, 128), 0),
+                    ),
+                    pl.BlockSpec(
+                        (pl.Element(tile), pl.Element(slab)),
+                        lambda t, pos, first=first, tile=tile: (pl.multiple_of(first + t * tile, 128), 0),
+                    ),
                 ],
-                out_specs=[out_block] * CHIPS,
+                out_specs=pl.BlockSpec((*shape, tile), lambda t, pos: (0, 0, 0, 0, t)),
                 scratch_shapes=[pltpu.VMEM((tokens, slab), bf16)],
             ),
-            out_shape=[
-                jax.ShapeDtypeStruct((layers, CORES, rows, size * tile), f32 if j == 0 else bf16)
-                for j in range(CHIPS)
-            ],
+            out_shape=jax.ShapeDtypeStruct((*shape, size), bf16),
             compiler_params=kernel_params(),
             cost_estimate=pl.CostEstimate(
-                flops=4 * tokens * size * tile * slab, bytes_accessed=4 * size * tile * slab, transcendentals=0
+                flops=4 * tokens * size * slab, bytes_accessed=4 * size * slab, transcendentals=0
             ),
             name="grad_hidden_partial",
-        )(pos[:1], grad, sib_grad, head_weight, sib_w)
-        sent.append([partial[0]] + [shift(partial[j], j * CORES) for j in range(1, CHIPS)])
-
-    head_tile = chunk // 2 if chunk % 512 == 0 else chunk
-    per_chunk = chunk // head_tile
+        )(pos, grad, sib_grad, head_weight, sib_w)
+        groups = across if by_layer else in_layer
+        sent.append(
+            lax.all_to_all(
+                partial, "vocab", split_axis=0, concat_axis=0, axis_index_groups=groups, tiled=True
+            )
+        )
+
+    _, late_grad = lax.optimization_barrier((partial, grad))
+    head_tile = narrow
+    places = [(wide_places, wide // head_tile), (narrow_places, narrow // head_tile)]
     piece_specs = [
-        pl.BlockSpec(
-            (layers * rows, head_tile),
-            lambda t, i=i: (0, jnp.clip(t - i * per_chunk, 0, per_chunk - 1)),
-        )
-        for i in range(chunks)
-        for _ in range(GROUP)
+        pl.BlockSpec((piece.shape[0], head_tile), lambda t: (0, jnp.minimum(t, wide // head_tile - 1)))
+        for piece in wide_pieces
+    ] + [
+        pl.BlockSpec((piece.shape[0], head_tile), lambda t: (0, jnp.maximum(t - wide // head_tile, 0)))
+        for piece in narrow_pieces
     ]
     grad_head = pl.pallas_call(
-        functools.partial(head_kernel, rows, per_chunk),
+        functools.partial(head_kernel, rows, places),
         grid=(depth // head_tile,),
-        in_specs=piece_specs + [pl.BlockSpec((tokens, slab), lambda t: (0, 0))],
+        in_specs=piece_specs + [pl.BlockSpec((tokens, slab), whole)],
         out_specs=pl.BlockSpec((head_tile, slab), lambda t: (t, 0)),
         out_shape=jax.ShapeDtypeStruct((depth, slab), bf16),
         scratch_shapes=[pltpu.VMEM((tokens, head_tile), bf16)],
@@ -531,47 +565,47 @@
             flops=2 * tokens * depth * slab, bytes_accessed=2 * depth * (slab + tokens), transcendentals=0
         ),
         name="grad_head",
-    )(*[piece for some in pieces for piece in some], grad)
+    )(*wide_pieces, *narrow_pieces, late_grad)
     sent, grad_head = lax.optimization_barrier((sent, grad_head))
 
-    mine, other = [], []
-    for size, parts in zip(sizes, sent):
-        chip_block = pl.BlockSpec((layers, CORES, rows, tile), lambda t: (0, 0, 0, t))
-        layer_block = pl.BlockSpec((CORES, rows, tile), lambda t: (0, 0, t))
+    arrived = []
+    for parts, by_layer in zip(sent, (False, True)):
+        size = parts.shape[-1]
+        tile = size // 2 if size % 256 == 0 and size > 1024 else size
+        count = parts.shape[1]
         summed = pl.pallas_call(
-            chip_sum_kernel,
-            grid=(size,),
-            in_specs=[chip_block] * CHIPS,
-            out_specs=[layer_block] * layers,
-            out_shape=[
-                jax.ShapeDtypeStruct((CORES, rows, size * tile), f32 if k == 0 else bf16)
-                for k in range(layers)
+            functools.partial(first_sum_kernel, 1 if by_layer else 2),
+            grid=(size // tile,),
+            in_specs=[
+                smem_spec(),
+                pl.BlockSpec((*parts.shape[:-1], tile), lambda t: (0, 0, 0, 0, t)),
             ],
+            out_specs=pl.BlockSpec((count, CORES, rows, tile), lambda t: (0, 0, 0, t)),
+            out_shape=jax.ShapeDtypeStruct((count, CORES, rows, size), bf16),
             compiler_params=kernel_params(),
             cost_estimate=pl.CostEstimate(
-                flops=tokens * size * tile, bytes_accessed=3 * tokens * size * tile, transcendentals=0
+                flops=tokens * size, bytes_accessed=3 * tokens * size, transcendentals=0
             ),
-            name="chip_sum",
-        )(*parts)
-        arrived = [shift(summed[k], k * GROUP) for k in range(1, layers)]
-        row_block = pl.BlockSpec((rows, tile), lambda t: (0, t))
-        ours, theirs = pl.pallas_call(
-            layer_sum_kernel,
-            grid=(size,),
-            in_specs=[layer_block] * layers,
-            out_specs=[row_block] * CORES,
-            out_shape=[jax.ShapeDtypeStruct((rows, size * tile), bf16)] * CORES,
-            compiler_params=kernel_params(),
-            cost_estimate=pl.CostEstimate(
-                flops=CORES * layers * rows * size * tile,
-                bytes_accessed=3 * CORES * layers * rows * size * tile,
-                transcendentals=0,
-            ),
-            name="layer_sum",
-        )(summed[0], *arrived)
-        mine.append(ours)
-        other.append(shift(theirs, 1))
-    mine, other = jnp.concatenate(mine, axis=1), jnp.concatenate(other, axis=1)
+            name="first_sum",
+        )(pos, parts)
+        groups = in_layer if by_layer else across
+        arrived.append(
+            lax.all_to_all(
+                summed, "vocab", split_axis=0, concat_axis=0, axis_index_groups=groups, tiled=True
+            )
+        )
+    mine, theirs = pl.pallas_call(
+        last_sum_kernel,
+        in_specs=[vmem_spec()] * 2,
+        out_specs=[vmem_spec()] * 2,
+        out_shape=[jax.ShapeDtypeStruct((rows, half), bf16)] * 2,
+        compiler_params=kernel_params(),
+        cost_estimate=pl.CostEstimate(
+            flops=CORES * layers * rows * half, bytes_accessed=3 * CORES * layers * rows * half, transcendentals=0
+        ),
+        name="last_sum",
+    )(*arrived)
+    other = shift(theirs, 1)
 
     low, high = jnp.where(core == 0, mine, other), jnp.where(core == 0, other, mine)
     return loss[:, 0], grad_head, jnp.concatenate([low, high], axis=1)
@@ -588,7 +622,7 @@
         and rows % 16 == 0
         and 2 * n <= side
         and 6 * blocks * stored <= side
-        and hidden_states.shape[1] % (CORES * 128) == 0
+        and hidden_states.shape[1] % (CORES * 1280) == 0
     )
 
 

time: 189 us -> 212 us (1.12)
  Pallas kernels: 36.2 us -> 58.4 us
  local copies, waits for them, and re-layouts: 29.5 us -> 13.7 us
  starting transfers between devices: 46.6 us -> 31.8 us
  waiting for transfers between devices: 71.9 us -> 86.5 us
  blocking collectives: 0 us -> 12.8 us
  other arithmetic: 3.13 us -> 6.06 us
    all_to_all x0 -> x4, waiting for transfers between devices: none -> 36.1 us  [the longest x2 21.9 us: levels_plan(): lax.all_to_all(partial, 'vocab', split_axis=0, concat_axis=0, axis_index_...]
    ppermute x41 -> x19, starting transfers between devices: 43.6 us -> 14.3 us  [shift(): return lax.ppermute(x, 'vocab', [(i, i ^ distance) for i in range(n)])]
    ppermute x41 -> x19, waiting for transfers between devices: 71.9 us -> 50.4 us  [shift(): return lax.ppermute(x, 'vocab', [(i, i ^ distance) for i in range(n)])]
    unnamed x55 -> x32, local copies, waits for them, and re-layouts: 21.2 us -> 3.12 us
    pallas_call x9 -> x8, Pallas kernels: 31.7 us -> 49.4 us  [the longest x2 16.4 us: logits_call(): pl.pallas_call(functools.partial(logits_kernel, rows, places, last), grid...]
    all_to_all x0 -> x4, starting transfers between devices: none -> 14.2 us  [the longest x2 7.26 us: levels_plan(): lax.all_to_all(partial, 'vocab', split_axis=0, concat_axis=0, axis_index_...]
    all_to_all x0 -> x1, blocking collectives: none -> 12.8 us  [levels_plan(): lax.all_to_all(stat, 'vocab', split_axis=0, concat_axis=0, tiled=True)]
    pallas_call x1, Pallas kernels: 1.25 us -> 4.1 us  [levels_plan(): pl.pallas_call(lambda *refs: grad_kernel(rows, *refs), out_shape=(jax.Sha...]
  transfers between devices with their start and end apart: 42 -> 24, of which waited for: 14 -> 14; matrix products, arithmetic and copies ran while one was open for 6% -> 4% of each run, Pallas kernels for 17% -> 23%
where the time goes in v3:
time: 212 us; the launch traced here: 211 us
  waiting for transfers between devices  86.5 us (41%)
  Pallas kernels  58.4 us (28%)
  starting transfers between devices  31.8 us (15%)
  local copies, waits for them, and re-layouts  13.7 us (6%)
  blocking collectives  12.8 us (6%)
  other arithmetic  6.06 us (3%)
    ppermute x19, waiting for transfers between devices, shift(): return lax.ppermute(x, 'vocab', [(i, i ^ distance) for i in range(n)])  50.4 us
    all_to_all x2, waiting for transfers between devices, levels_plan(): lax.all_to_all(partial, 'vocab', split_axis=0, concat_axis=0, axis_index_...  21.9 us
    pallas_call x2, Pallas kernels, logits_call(): pl.pallas_call(functools.partial(logits_kernel, rows, places, last), grid...  16.4 us
    pallas_call x2, Pallas kernels, levels_plan(): pl.pallas_call(functools.partial(partial_kernel, rows, by_layer), grid_sp...  15.1 us
    ppermute x19, starting transfers between devices, shift(): return lax.ppermute(x, 'vocab', [(i, i ^ distance) for i in range(n)])  14.3 us
    all_to_all x2, waiting for transfers between devices, levels_plan(): lax.all_to_all(summed, 'vocab', split_axis=0, concat_axis=0, axis_index_g...  14.2 us
    all_to_all x1, blocking collectives, levels_plan(): lax.all_to_all(stat, 'vocab', split_axis=0, concat_axis=0, tiled=True)  12.8 us
    pallas_call x1, Pallas kernels, levels_plan(): pl.pallas_call(functools.partial(head_kernel, rows, places), grid=(depth...  11.3 us
  transfers between devices with their start and end apart: 24, of which 14 were waited for; matrix products, arithmetic and copies ran while one was open for 4% of the time, Pallas kernels for 23%

profile of v3, /device:TPU:0, one launch (start us, length us, event | category | flops | bytes accessed | tf_op | source)
XLA Modules:
  0.0 210.6 jit_solution(4959066692395935329)
XLA Ops:
  0.6 0.8 slice.16
  1.4 2.9 %collective-permute-start.3 = (bf16[16,1280]{1,0:T(8,128)(2,1)S(1)}, bf16[16,1280]{1,0:T(8,128)(2,1)S(1)}, u32[]{:S(2)}, u32[]{:S(2)}) collective-permute-start(bf16[16,1280]{1,0:T(8,128)(2,1)S(1)} %slice.16), channel_id=1, source_target_pairs={{0,2},{1,3},{2,0},{3,1},{4,6},{5,7},{6,4},{7,5},{8,10},{9,11},{10,... | collective-permute-start | bytes 122888 | tf_op jit(solution)/shard_map/ppermute | solution.py:125
  4.4 2.0 collective-permute-done.3
  6.3 2.1 collective-permute-start.4
  8.4 0.9 slice.15
  9.3 3.7 %collective-permute-start.2 = (bf16[16,3840]{1,0:T(8,128)(2,1)S(1)}, bf16[16,3840]{1,0:T(8,128)(2,1)S(1)}, u32[]{:S(2)}, u32[]{:S(2)}) collective-permute-start(bf16[16,3840]{1,0:T(8,128)(2,1)S(1)} %slice.15), channel_id=1, source_target_pairs={{0,24},{1,25},{2,26},{3,27},{4,28},{5,29},{6,30},{7,31},{8,16},{9,... | collective-permute-start | bytes 368648 | tf_op jit(solution)/shard_map/ppermute | solution.py:125
  13.0 0.8 collective-permute-start
  13.8 1.2 reduce_max.14
  14.9 1.8 collective-permute-done.2
  16.7 5.2 %collective-permute-done.1 = bf16[16,3840]{1,0:T(8,128)(2,1)S(1)} collective-permute-done((bf16[16,3840]{1,0:T(8,128)(2,1)S(1)}, bf16[16,3840]{1,0:T(8,128)(2,1)S(1)}, u32[]{:S(2)}, u32[]{:S(2)}) %collective-permute-start.1) | collective-permute-done | bytes 122912 | tf_op jit(solution)/shard_map/ppermute | solution.py:125
  22.0 5.6 %constant_dynamic-slice_fusion = bf16[2560,1024]{1,0:T(8,128)(2,1)} fusion(bf16[5120,1024]{1,0:T(8,128)(2,1)} %w_ref.3, s32[]{:T(128)S(6)} %select_n.57), kind=kLoop, calls=%fused_computation.47 | loop fusion | bytes 10485764 | tf_op jit(solution)/shard_map/dynamic_slice | solution.py:427
  27.6 0.5 fusion.1
  28.4 0.2 convert_reduce_fusion
  28.6 0.3 collective-permute-start.12
  29.0 10.6 %collective-permute-done.12 = bf16[64,1280]{1,0:T(8,128)(2,1)S(1)} collective-permute-done((bf16[64,1280]{1,0:T(8,128)(2,1)S(1)}, bf16[64,1280]{1,0:T(8,128)(2,1)S(1)}, u32[]{:S(2)}, u32[]{:S(2)}) %collective-permute-start.12) | collective-permute-done | bytes 163872 | tf_op jit(solution)/shard_map/ppermute | solution.py:125
  39.6 0.1 collective-permute-start.14
  39.7 0.4 convolution_convert_fusion
  40.2 0.4 copy.43
  40.8 0.9 pad_maximum_fusion
  41.6 3.3 %all-to-all-start = ((bf16[32,65,128]{2,1,0:T(8,128)(2,1)}), bf16[32,65,128]{2,1,0:T(8,128)(2,1)S(1)}, u32[]{:S(2)}, u32[]{:S(2)}) async-start(bf16[32,65,128]{2,1,0:T(8,128)(2,1)} %pad_maximum_fusion), calls=%async_computation | async-start | bytes 1179648 | tf_op jit(solution)/shard_map/all_to_all | solution.py:361
  44.9 2.7 %collective-permute-start.7 = (bf16[64,3840]{1,0:T(8,128)(2,1)S(1)}, bf16[64,3840]{1,0:T(8,128)(2,1)S(1)}, u32[]{:S(2)}, u32[]{:S(2)}) collective-permute-start(bf16[64,3840]{1,0:T(8,128)(2,1)S(1)} %pad_maximum_fusion.1.refs_0_), channel_id=1, source_target_pairs={{0,6},{1,7},{2,4},{3,5},{4,2},{5,3},{6,0},{7,1},{8,14},{9,15},{10,... | collective-permute-start | bytes 1474568 | tf_op jit(solution)/shard_map/ppermute | solution.py:125
  47.7 0.6 collective-permute-start.6
  48.2 0.3 collective-permute-start.5
  48.5 5.3 %collective-permute-done.13.refs_1_.refs_9_ = bf16[128,1280]{1,0:T(8,128)(2,1)} collective-permute-done((bf16[128,1280]{1,0:T(8,128)(2,1)S(1)}, bf16[128,1280]{1,0:T(8,128)(2,1)}, u32[]{:S(2)}, u32[]{:S(2)}) %collective-permute-start.13) | collective-permute-done | bytes 327712 | tf_op jit(solution)/shard_map/ppermute | solution.py:125
  53.8 0.2 select_reduce_fusion
  54.0 12.5 %collective-permute-done.7.refs_3_ = bf16[64,3840]{1,0:T(8,128)(2,1)S(1)} collective-permute-done((bf16[64,3840]{1,0:T(8,128)(2,1)S(1)}, bf16[64,3840]{1,0:T(8,128)(2,1)S(1)}, u32[]{:S(2)}, u32[]{:S(2)}) %collective-permute-start.7) | collective-permute-done | bytes 491552 | tf_op jit(solution)/shard_map/ppermute | solution.py:125
  66.5 9.2 %collective-permute-done.6.refs_2_ = bf16[64,3840]{1,0:T(8,128)(2,1)S(1)} collective-permute-done((bf16[64,3840]{1,0:T(8,128)(2,1)S(1)}, bf16[64,3840]{1,0:T(8,128)(2,1)S(1)}, u32[]{:S(2)}, u32[]{:S(2)}) %collective-permute-start.6) | collective-permute-done | bytes 491552 | tf_op jit(solution)/shard_map/ppermute | solution.py:125
  75.8 0.3 collective-permute-done.5.refs_1_
  76.1 0.2 collective-permute-start.10
  76.3 0.3 collective-permute-start.9
  76.6 0.6 broadcast_add_fusion.refs_1_
  77.2 0.7 pad_add_fusion.refs_0_.pos_ref
  77.8 5.4 %logits.2.refs_9_ = f32[512,1024]{1,0:T(8,128)} custom-call(bf16[128,1280]{1,0:T(8,128)(2,1)} %copy-done.7, bf16[128,1280]{1,0:T(8,128)(2,1)} %collective-permute-done.13.refs_1_.refs_9_, bf16[128,1280]{1,0:T(8,128)(2,1)} %collective-permute-done.14.refs_2_.refs_10_, bf16[128,1280]{1,0:T(8,128)(2,1)} %collective-permute-done.15.refs_3_.refs_11_, ...), custom_call_target="tpu_custom_call" | custom-call | flops 1342177280 | bytes 6029312 | tf_op jit(solution)/shard_map/logits/pallas_call | solution.py:468
  83.4 0.3 copy.52
  83.7 1.1 copy.46
  85.0 0.7 reshape.196
  85.8 4.9 %teacher_prob.1 = (f32[512,1024]{1,0:T(8,128)}, f32[16,128]{1,0:T(8,128)}) custom-call(s32[4]{0:T(128)} %pad_add_fusion.refs_0_.pos_ref, s32[4,4]{1,0:T(4,128)} %broadcast_add_fusion.refs_1_, bf16[4,4,128,128]{3,2,1,0:T(8,128)(2,1)} %bitcast.29, f32[2,4,1,128]{3,2,1,0:T(1,128)} %bitcast.35, s32[4,1,128]{2,1,0:T(1,128)} %bitcast.36, f32[4,1,128]{2,1,0:T(1,128)} %bitcast.37), custom_call_target="tpu_custom_call" | custom-call | flops 67108864 | bytes 2097152 | tf_op jit(solution)/shard_map/teacher_prob/pallas_call | solution.py:429
  90.7 0.7 copy-done.11
  91.4 0.2 copy-done.12
  91.6 11.0 %logits.3 = (f32[512,1024]{1,0:T(8,128)}, f32[32,8,128]{2,1,0:T(8,128)}) custom-call(bf16[64,3840]{1,0:T(8,128)(2,1)} %copy-done.4, bf16[64,3840]{1,0:T(8,128)(2,1)} %copy-done.10, bf16[64,3840]{1,0:T(8,128)(2,1)} %copy-done.9, bf16[64,3840]{1,0:T(8,128)(2,1)} %copy-done.8, bf16[64,3840]{1,0:T(8,128)(2,1)} %copy-done.11, ...), custom_call_target="tpu_custom_call" | custom-call | flops 4026531840 | bytes 13893632 | tf_op jit(solution)/shard_map/logits/pallas_call | solution.py:468
  102.6 12.8 %all_to_all.30.refs_1_ = f32[32,8,128]{2,1,0:T(8,128)} all-to-all(f32[32,8,128]{2,1,0:T(8,128)} %get-tuple-element.21), channel_id=1, replica_groups=mesh['vocab'=32] {'vocab'}, dimensions={0} | all-to-all | bytes 262144 | tf_op jit(solution)/shard_map/all_to_all | solution.py:488
  115.4 4.1 %grad_logits.1 = (bf16[512,1024]{1,0:T(8,128)(2,1)}, f32[16,128]{1,0:T(8,128)}) custom-call(s32[4]{0:T(128)} %pad_add_fusion.refs_0_.pos_ref, f32[32,8,128]{2,1,0:T(8,128)} %all_to_all.30.refs_1_, f32[512,1024]{1,0:T(8,128)} %get-tuple-element.22.refs_2_, f32[512,1024]{1,0:T(8,128)} %get-tuple-element.20.refs_10_.refs_3_, f32[4,1,128]{2,1,0:T(1,128)} %bitcast.38, ...), custom_call_target="tpu_custom_call" | custom-call | flops 2097152 | bytes 5242880 | tf_op jit(solution)/shard_map/grad_logits/pallas_call | solution.py:490
  119.5 0.2 collective-permute-start.16
  119.7 2.7 %collective-permute-done.16.sib_ref = bf16[512,1024]{1,0:T(8,128)(2,1)S(1)} collective-permute-done((bf16[512,1024]{1,0:T(8,128)(2,1)}, bf16[512,1024]{1,0:T(8,128)(2,1)S(1)}, u32[]{:S(2)}, u32[]{:S(2)}) %collective-permute-start.16) | collective-permute-done | bytes 1048608 | tf_op jit(solution)/shard_map/ppermute | solution.py:125
  122.4 1.0 copy-done.1
  123.4 5.9 %grad_hidden_partial.3 = bf16[4,4,2,16,768]{4,3,2,1,0:T(8,128)(2,1)} custom-call(s32[4]{0:T(128)} %pad_add_fusion.refs_0_.pos_ref, bf16[512,1024]{1,0:T(8,128)(2,1)} %get-tuple-element.27.grad_ref.refs_12_, bf16[512,1024]{1,0:T(8,128)(2,1)} %copy-done.1, bf16[5120,1024]{1,0:T(8,128)(2,1)} %w_ref.3, bf16[2560,1024]{1,0:T(8,128)(2,1)} %collective-permute-done.17.sib_w_ref), custom_call_target="tpu_custom_call" | custom-call | flops 1610612736 | bytes 3145728 | tf_op jit(solution)/shard_map/grad_hidden_partial/pallas_call | solution.py:512
  129.3 3.7 %all-to-all-start.3 = ((bf16[4,4,2,16,768]{4,3,2,1,0:T(8,128)(2,1)}), bf16[4,4,2,16,768]{4,3,2,1,0:T(8,128)(2,1)S(1)}, u32[]{:S(2)}, u32[]{:S(2)}) async-start(bf16[4,4,2,16,768]{4,3,2,1,0:T(8,128)(2,1)} %grad_hidden_partial.3), calls=%async_computation.3 | async-start | bytes 1572864 | tf_op jit(solution)/shard_map/all_to_all | solution.py:541
  133.0 9.2 %grad_hidden_partial.2 = bf16[4,4,2,16,1792]{4,3,2,1,0:T(8,128)(2,1)} custom-call(s32[4]{0:T(128)} %pad_add_fusion.refs_0_.pos_ref, bf16[512,1024]{1,0:T(8,128)(2,1)} %get-tuple-element.27.grad_ref.refs_12_, bf16[512,1024]{1,0:T(8,128)(2,1)} %copy-done.1, bf16[5120,1024]{1,0:T(8,128)(2,1)} %w_ref.3, bf16[2560,1024]{1,0:T(8,128)(2,1)} %collective-permute-done.17.sib_w_ref), custom_call_target="tpu_custom_call" | custom-call | flops 3758096384 | bytes 7340032 | tf_op jit(solution)/shard_map/grad_hidden_partial/pallas_call | solution.py:512
  142.2 11.4 %all-to-all-done.3.parts_ref = bf16[4,4,2,16,768]{4,3,2,1,0:T(8,128)(2,1)S(1)} async-done(((bf16[4,4,2,16,768]{4,3,2,1,0:T(8,128)(2,1)}), bf16[4,4,2,16,768]{4,3,2,1,0:T(8,128)(2,1)S(1)}, u32[]{:S(2)}, u32[]{:S(2)}) %all-to-all-start.3) | async-done | bytes 786464 | tf_op jit(solution)/shard_map/all_to_all | solution.py:541
  153.5 3.6 %all-to-all-start.2 = ((bf16[4,4,2,16,1792]{4,3,2,1,0:T(8,128)(2,1)}), bf16[4,4,2,16,1792]{4,3,2,1,0:T(8,128)(2,1)S(1)}, u32[]{:S(2)}, u32[]{:S(2)}) async-start(bf16[4,4,2,16,1792]{4,3,2,1,0:T(8,128)(2,1)} %grad_hidden_partial.2), calls=%async_computation.2 | async-start | bytes 3670016 | tf_op jit(solution)/shard_map/all_to_all | solution.py:541
  157.1 11.3 %grad_head.1 = bf16[5120,1024]{1,0:T(8,128)(2,1)} custom-call(bf16[64,3840]{1,0:T(8,128)(2,1)} %copy-done.4, bf16[64,3840]{1,0:T(8,128)(2,1)} %copy-done.10, bf16[64,3840]{1,0:T(8,128)(2,1)} %copy-done.9, bf16[64,3840]{1,0:T(8,128)(2,1)} %copy-done.8, bf16[64,3840]{1,0:T(8,128)(2,1)} %copy-done.11, bf16[64,3840]{1,0:T(8,128)(2,1)} %collective-permute-done.9.refs_5_, ...), custom_call_target="tpu_custom_call" | custom-call | flops 5368709120 | bytes 15728640 | tf_op jit(solution)/shard_map/grad_head/pallas_call | solution.py:556
  168.4 10.6 %all-to-all-done.2.parts_ref = bf16[4,4,2,16,1792]{4,3,2,1,0:T(8,128)(2,1)S(1)} async-done(((bf16[4,4,2,16,1792]{4,3,2,1,0:T(8,128)(2,1)}), bf16[4,4,2,16,1792]{4,3,2,1,0:T(8,128)(2,1)S(1)}, u32[]{:S(2)}, u32[]{:S(2)}) %all-to-all-start.2) | async-done | bytes 1835040 | tf_op jit(solution)/shard_map/all_to_all | solution.py:541
  179.0 2.5 %first_sum.3 = bf16[4,2,16,768]{3,2,1,0:T(8,128)(2,1)} custom-call(s32[4]{0:T(128)} %pad_add_fusion.refs_0_.pos_ref, bf16[4,4,2,16,768]{4,3,2,1,0:T(8,128)(2,1)} %copy-done.2), custom_call_target="tpu_custom_call" | custom-call | flops 393216 | bytes 1179648 | tf_op jit(solution)/shard_map/first_sum/pallas_call | solution.py:576
  181.5 3.5 %all-to-all-start.5 = ((bf16[4,2,16,768]{3,2,1,0:T(8,128)(2,1)}), bf16[4,2,16,768]{3,2,1,0:T(8,128)(2,1)S(1)}, u32[]{:S(2)}, u32[]{:S(2)}) async-start(bf16[4,2,16,768]{3,2,1,0:T(8,128)(2,1)} %first_sum.3), calls=%async_computation.5 | async-start | bytes 393216 | tf_op jit(solution)/shard_map/all_to_all | solution.py:593
  185.0 2.3 %first_sum.2 = bf16[4,2,16,1792]{3,2,1,0:T(8,128)(2,1)} custom-call(s32[4]{0:T(128)} %pad_add_fusion.refs_0_.pos_ref, bf16[4,4,2,16,1792]{4,3,2,1,0:T(8,128)(2,1)} %copy-done), custom_call_target="tpu_custom_call" | custom-call | flops 917504 | bytes 2752512 | tf_op jit(solution)/shard_map/first_sum/pallas_call | solution.py:576
  187.3 2.8 %all-to-all-done.5.refs_1_ = bf16[4,2,16,768]{3,2,1,0:T(8,128)(2,1)S(1)} async-done(((bf16[4,2,16,768]{3,2,1,0:T(8,128)(2,1)}), bf16[4,2,16,768]{3,2,1,0:T(8,128)(2,1)S(1)}, u32[]{:S(2)}, u32[]{:S(2)}) %all-to-all-start.5) | async-done | bytes 196640 | tf_op jit(solution)/shard_map/all_to_all | solution.py:593
  190.2 3.5 %all-to-all-start.4 = ((bf16[4,2,16,1792]{3,2,1,0:T(8,128)(2,1)}), bf16[4,2,16,1792]{3,2,1,0:T(8,128)(2,1)S(1)}, u32[]{:S(2)}, u32[]{:S(2)}) async-start(bf16[4,2,16,1792]{3,2,1,0:T(8,128)(2,1)} %first_sum.2), calls=%async_computation.4 | async-start | bytes 917504 | tf_op jit(solution)/shard_map/all_to_all | solution.py:593
  193.7 11.3 %all-to-all-done.4.refs_0_ = bf16[4,2,16,1792]{3,2,1,0:T(8,128)(2,1)S(1)} async-done(((bf16[4,2,16,1792]{3,2,1,0:T(8,128)(2,1)}), bf16[4,2,16,1792]{3,2,1,0:T(8,128)(2,1)S(1)}, u32[]{:S(2)}, u32[]{:S(2)}) %all-to-all-start.4) | async-done | bytes 458784 | tf_op jit(solution)/shard_map/all_to_all | solution.py:593
  205.0 0.8 copy-done.5
  205.8 1.8 last_sum.1
  207.6 0.6 slice_reduce_fusion
  208.2 0.9 collective-permute-done.18
  209.1 0.9 broadcast_select_fusion.1
  210.0 0.7 pad_maximum_fusion.3
  (67 shorter events, 0.9 us)
Async XLA Ops:
  1.4 4.9 %collective-permute-start.3 = (bf16[16,1280]{1,0:T(8,128)(2,1)S(1)}, bf16[16,1280]{1,0:T(8,128)(2,1)S(1)}, u32[]{:S(2)}, u32[]{:S(2)}) collective-permute-start(bf16[16,1280]{1,0:T(8,128)(2,1)S(1)} %slice.16), channel_id=1, source_target_pairs={{0,2},{1,3},{2,0},{3,1},{4,6},{5,7},{6,4},{7,5},{8,10},{9,11},{10,... | collective-permute-start | bytes 122888 | tf_op jit(solution)/shard_map/ppermute | solution.py:125
  6.3 8.6 %collective-permute-start.4 = (bf16[32,1280]{1,0:T(8,128)(2,1)S(1)}, bf16[32,1280]{1,0:T(8,128)(2,1)S(1)}, u32[]{:S(2)}, u32[]{:S(2)}) collective-permute-start(bf16[32,1280]{1,0:T(8,128)(2,1)S(1)} %pad_maximum_fusion.4), channel_id=1, source_target_pairs={{0,4},{1,5},{2,6},{3,7},{4,0},{5,1},{6,2},{7,3},{8,12},{9,13},{10,... | collective-permute-start | bytes 245768 | tf_op jit(solution)/shard_map/ppermute | solution.py:125
  9.3 7.4 %collective-permute-start.2 = (bf16[16,3840]{1,0:T(8,128)(2,1)S(1)}, bf16[16,3840]{1,0:T(8,128)(2,1)S(1)}, u32[]{:S(2)}, u32[]{:S(2)}) collective-permute-start(bf16[16,3840]{1,0:T(8,128)(2,1)S(1)} %slice.15), channel_id=1, source_target_pairs={{0,24},{1,25},{2,26},{3,27},{4,28},{5,29},{6,30},{7,31},{8,16},{9,... | collective-permute-start | bytes 368648 | tf_op jit(solution)/shard_map/ppermute | solution.py:125
  13.0 8.9 %collective-permute-start.1 = (bf16[16,3840]{1,0:T(8,128)(2,1)S(1)}, bf16[16,3840]{1,0:T(8,128)(2,1)S(1)}, u32[]{:S(2)}, u32[]{:S(2)}) collective-permute-start(bf16[16,3840]{1,0:T(8,128)(2,1)S(1)} %slice.15), channel_id=1, source_target_pairs={{0,16},{1,17},{2,18},{3,19},{4,20},{5,21},{6,22},{7,23},{8,24},{9,... | collective-permute-start | bytes 368648 | tf_op jit(solution)/shard_map/ppermute | solution.py:125
  13.0 8.9 %collective-permute-start = (bf16[16,3840]{1,0:T(8,128)(2,1)S(1)}, bf16[16,3840]{1,0:T(8,128)(2,1)S(1)}, u32[]{:S(2)}, u32[]{:S(2)}) collective-permute-start(bf16[16,3840]{1,0:T(8,128)(2,1)S(1)} %slice.15), channel_id=1, source_target_pairs={{0,8},{1,9},{2,10},{3,11},{4,12},{5,13},{6,14},{7,15},{8,0},{9,1},... | collective-permute-start | bytes 368648 | tf_op jit(solution)/shard_map/ppermute | solution.py:125
  21.9 44.6 %copy-start.4 = (bf16[64,3840]{1,0:T(8,128)(2,1)}, bf16[64,3840]{1,0:T(8,128)(2,1)S(1)}, u32[]{:S(2)}) copy-start(bf16[64,3840]{1,0:T(8,128)(2,1)S(1)} %pad_maximum_fusion.1.refs_0_) | copy-start | bytes 1474564
  22.0 5.6 %copy-start.3 = (bf16[4,64,4,128]{3,2,1,0:T(4,128)(2,1)S(1)}, bf16[4,64,4,128]{3,2,1,0:T(4,128)(2,1)}, u32[]{:S(2)}) copy-start(bf16[4,64,4,128]{3,2,1,0:T(4,128)(2,1)} %param.9) | copy-start | bytes 786436
  22.0 6.3 %copy-start.14 = (s32[4,64]{1,0:T(4,128)S(1)}, s32[4,64]{1,0:T(4,128)}, u32[]{:S(2)}) copy-start(s32[4,64]{1,0:T(4,128)} %param.10) | copy-start | bytes 3076
  27.6 94.8 %collective-permute-start.17 = (bf16[2560,1024]{1,0:T(8,128)(2,1)}, bf16[2560,1024]{1,0:T(8,128)(2,1)}, u32[]{:S(2)}, u32[]{:S(2)}) collective-permute-start(bf16[2560,1024]{1,0:T(8,128)(2,1)} %constant_dynamic-slice_fusion), channel_id=1, source_target_pairs={{0,1},{1,0},{2,3},{3,2},{4,5},{5,4},{6,7},{7,6},{8,9},{9,8},{10,11... | collective-permute-start | bytes 15728648 | tf_op jit(solution)/shard_map/ppermute | solution.py:125
  28.6 10.9 %collective-permute-start.12 = (bf16[64,1280]{1,0:T(8,128)(2,1)S(1)}, bf16[64,1280]{1,0:T(8,128)(2,1)S(1)}, u32[]{:S(2)}, u32[]{:S(2)}) collective-permute-start(bf16[64,1280]{1,0:T(8,128)(2,1)S(1)} %pad_maximum_fusion.2), channel_id=1, source_target_pairs={{0,16},{1,17},{2,18},{3,19},{4,20},{5,21},{6,22},{7,23},{8,24},{9,... | collective-permute-start | bytes 491528 | tf_op jit(solution)/shard_map/ppermute | solution.py:125
  39.6 2.1 copy-start.7
  39.6 8.7 %collective-permute-start.14 = (bf16[128,1280]{1,0:T(8,128)(2,1)S(1)}, bf16[128,1280]{1,0:T(8,128)(2,1)}, u32[]{:S(2)}, u32[]{:S(2)}) collective-permute-start(bf16[128,1280]{1,0:T(8,128)(2,1)S(1)} %constant_dynamic-update-slice_fusion.refs_0_.refs_8_), channel_id=1, source_target_pairs={{0,1},{1,0},{2,3},{3,2},{4,5},{5,4},{6,7},{7,6},{8,9},{9,8},{10,11... | collective-permute-start | bytes 983048 | tf_op jit(solution)/shard_map/ppermute | solution.py:125
  40.7 13.2 %collective-permute-start.13 = (bf16[128,1280]{1,0:T(8,128)(2,1)S(1)}, bf16[128,1280]{1,0:T(8,128)(2,1)}, u32[]{:S(2)}, u32[]{:S(2)}) collective-permute-start(bf16[128,1280]{1,0:T(8,128)(2,1)S(1)} %constant_dynamic-update-slice_fusion.refs_0_.refs_8_), channel_id=1, source_target_pairs={{0,8},{1,9},{2,10},{3,11},{4,12},{5,13},{6,14},{7,15},{8,0},{9,1},... | collective-permute-start | bytes 983048 | tf_op jit(solution)/shard_map/ppermute | solution.py:125
  41.6 41.6 %all-to-all-start = ((bf16[32,65,128]{2,1,0:T(8,128)(2,1)}), bf16[32,65,128]{2,1,0:T(8,128)(2,1)S(1)}, u32[]{:S(2)}, u32[]{:S(2)}) async-start(bf16[32,65,128]{2,1,0:T(8,128)(2,1)} %pad_maximum_fusion), calls=%async_computation | async-start | bytes 1179648 | tf_op jit(solution)/shard_map/all_to_all | solution.py:361
  44.9 21.6 %collective-permute-start.7 = (bf16[64,3840]{1,0:T(8,128)(2,1)S(1)}, bf16[64,3840]{1,0:T(8,128)(2,1)S(1)}, u32[]{:S(2)}, u32[]{:S(2)}) collective-permute-start(bf16[64,3840]{1,0:T(8,128)(2,1)S(1)} %pad_maximum_fusion.1.refs_0_), channel_id=1, source_target_pairs={{0,6},{1,7},{2,4},{3,5},{4,2},{5,3},{6,0},{7,1},{8,14},{9,15},{10,... | collective-permute-start | bytes 1474568 | tf_op jit(solution)/shard_map/ppermute | solution.py:125
  47.7 28.1 %collective-permute-start.6 = (bf16[64,3840]{1,0:T(8,128)(2,1)S(1)}, bf16[64,3840]{1,0:T(8,128)(2,1)S(1)}, u32[]{:S(2)}, u32[]{:S(2)}) collective-permute-start(bf16[64,3840]{1,0:T(8,128)(2,1)S(1)} %pad_maximum_fusion.1.refs_0_), channel_id=1, source_target_pairs={{0,4},{1,5},{2,6},{3,7},{4,0},{5,1},{6,2},{7,3},{8,12},{9,13},{10,... | collective-permute-start | bytes 1474568 | tf_op jit(solution)/shard_map/ppermute | solution.py:125
  48.2 27.8 %collective-permute-start.5 = (bf16[64,3840]{1,0:T(8,128)(2,1)S(1)}, bf16[64,3840]{1,0:T(8,128)(2,1)S(1)}, u32[]{:S(2)}, u32[]{:S(2)}) collective-permute-start(bf16[64,3840]{1,0:T(8,128)(2,1)S(1)} %pad_maximum_fusion.1.refs_0_), channel_id=1, source_target_pairs={{0,2},{1,3},{2,0},{3,1},{4,6},{5,7},{6,4},{7,5},{8,10},{9,11},{10,... | collective-permute-start | bytes 1474568 | tf_op jit(solution)/shard_map/ppermute | solution.py:125
  53.8 22.5 %collective-permute-start.15 = (bf16[128,1280]{1,0:T(8,128)(2,1)}, bf16[128,1280]{1,0:T(8,128)(2,1)}, u32[]{:S(2)}, u32[]{:S(2)}) collective-permute-start(bf16[128,1280]{1,0:T(8,128)(2,1)} %collective-permute-done.13.refs_1_.refs_9_), channel_id=1, source_target_pairs={{0,1},{1,0},{2,3},{3,2},{4,5},{5,4},{6,7},{7,6},{8,9},{9,8},{10,11... | collective-permute-start | bytes 983048 | tf_op jit(solution)/shard_map/ppermute | solution.py:125
  66.5 16.7 %copy-start.8 = (bf16[64,3840]{1,0:T(8,128)(2,1)}, bf16[64,3840]{1,0:T(8,128)(2,1)S(1)}, u32[]{:S(2)}) copy-start(bf16[64,3840]{1,0:T(8,128)(2,1)S(1)} %collective-permute-done.7.refs_3_) | copy-start | bytes 1474564
  66.5 24.1 %collective-permute-start.8 = (bf16[64,3840]{1,0:T(8,128)(2,1)S(1)}, bf16[64,3840]{1,0:T(8,128)(2,1)S(1)}, u32[]{:S(2)}, u32[]{:S(2)}) collective-permute-start(bf16[64,3840]{1,0:T(8,128)(2,1)S(1)} %pad_maximum_fusion.1.refs_0_), channel_id=1, source_target_pairs={{0,1},{1,0},{2,3},{3,2},{4,5},{5,4},{6,7},{7,6},{8,9},{9,8},{10,11... | collective-permute-start | bytes 1474568 | tf_op jit(solution)/shard_map/ppermute | solution.py:125
  75.8 7.5 %copy-start.9 = (bf16[64,3840]{1,0:T(8,128)(2,1)}, bf16[64,3840]{1,0:T(8,128)(2,1)S(1)}, u32[]{:S(2)}) copy-start(bf16[64,3840]{1,0:T(8,128)(2,1)S(1)} %collective-permute-done.6.refs_2_) | copy-start | bytes 1474564
  75.8 14.9 %collective-permute-start.11 = (bf16[64,3840]{1,0:T(8,128)(2,1)S(1)}, bf16[64,3840]{1,0:T(8,128)(2,1)S(1)}, u32[]{:S(2)}, u32[]{:S(2)}) collective-permute-start(bf16[64,3840]{1,0:T(8,128)(2,1)S(1)} %collective-permute-done.7.refs_3_), channel_id=1, source_target_pairs={{0,1},{1,0},{2,3},{3,2},{4,5},{5,4},{6,7},{7,6},{8,9},{9,8},{10,11... | collective-permute-start | bytes 1474568 | tf_op jit(solution)/shard_map/ppermute | solution.py:125
  76.1 7.2 %copy-start.10 = (bf16[64,3840]{1,0:T(8,128)(2,1)}, bf16[64,3840]{1,0:T(8,128)(2,1)S(1)}, u32[]{:S(2)}) copy-start(bf16[64,3840]{1,0:T(8,128)(2,1)S(1)} %collective-permute-done.5.refs_1_) | copy-start | bytes 1474564
  76.1 14.6 %collective-permute-start.10 = (bf16[64,3840]{1,0:T(8,128)(2,1)S(1)}, bf16[64,3840]{1,0:T(8,128)(2,1)}, u32[]{:S(2)}, u32[]{:S(2)}) collective-permute-start(bf16[64,3840]{1,0:T(8,128)(2,1)S(1)} %collective-permute-done.6.refs_2_), channel_id=1, source_target_pairs={{0,1},{1,0},{2,3},{3,2},{4,5},{5,4},{6,7},{7,6},{8,9},{9,8},{10,11... | collective-permute-start | bytes 1474568 | tf_op jit(solution)/shard_map/ppermute | solution.py:125
  76.3 14.4 %collective-permute-start.9 = (bf16[64,3840]{1,0:T(8,128)(2,1)S(1)}, bf16[64,3840]{1,0:T(8,128)(2,1)}, u32[]{:S(2)}, u32[]{:S(2)}) collective-permute-start(bf16[64,3840]{1,0:T(8,128)(2,1)S(1)} %collective-permute-done.5.refs_1_), channel_id=1, source_target_pairs={{0,1},{1,0},{2,3},{3,2},{4,5},{5,4},{6,7},{7,6},{8,9},{9,8},{10,11... | collective-permute-start | bytes 1474568 | tf_op jit(solution)/shard_map/ppermute | solution.py:125
  90.6 0.8 copy-start.11
  90.7 0.9 copy-start.12
  119.5 2.9 %collective-permute-start.16 = (bf16[512,1024]{1,0:T(8,128)(2,1)}, bf16[512,1024]{1,0:T(8,128)(2,1)S(1)}, u32[]{:S(2)}, u32[]{:S(2)}) collective-permute-start(bf16[512,1024]{1,0:T(8,128)(2,1)} %get-tuple-element.27.grad_ref.refs_12_), channel_id=1, source_target_pairs={{0,1},{1,0},{2,3},{3,2},{4,5},{5,4},{6,7},{7,6},{8,9},{9,8},{10,11... | collective-permute-start | bytes 3145736 | tf_op jit(solution)/shard_map/ppermute | solution.py:125
  122.4 1.0 copy-start.1
  129.3 24.2 %all-to-all-start.3 = ((bf16[4,4,2,16,768]{4,3,2,1,0:T(8,128)(2,1)}), bf16[4,4,2,16,768]{4,3,2,1,0:T(8,128)(2,1)S(1)}, u32[]{:S(2)}, u32[]{:S(2)}) async-start(bf16[4,4,2,16,768]{4,3,2,1,0:T(8,128)(2,1)} %grad_hidden_partial.3), calls=%async_computation.3 | async-start | bytes 1572864 | tf_op jit(solution)/shard_map/all_to_all | solution.py:541
  153.5 14.9 %copy-start.2 = (bf16[4,4,2,16,768]{4,3,2,1,0:T(8,128)(2,1)}, bf16[4,4,2,16,768]{4,3,2,1,0:T(8,128)(2,1)S(1)}, u32[]{:S(2)}) copy-start(bf16[4,4,2,16,768]{4,3,2,1,0:T(8,128)(2,1)S(1)} %all-to-all-done.3.parts_ref) | copy-start | bytes 2359300
  153.5 25.5 %all-to-all-start.2 = ((bf16[4,4,2,16,1792]{4,3,2,1,0:T(8,128)(2,1)}), bf16[4,4,2,16,1792]{4,3,2,1,0:T(8,128)(2,1)S(1)}, u32[]{:S(2)}, u32[]{:S(2)}) async-start(bf16[4,4,2,16,1792]{4,3,2,1,0:T(8,128)(2,1)} %grad_hidden_partial.2), calls=%async_computation.2 | async-start | bytes 3670016 | tf_op jit(solution)/shard_map/all_to_all | solution.py:541
  179.0 6.0 %copy-start = (bf16[4,4,2,16,1792]{4,3,2,1,0:T(8,128)(2,1)}, bf16[4,4,2,16,1792]{4,3,2,1,0:T(8,128)(2,1)S(1)}, u32[]{:S(2)}) copy-start(bf16[4,4,2,16,1792]{4,3,2,1,0:T(8,128)(2,1)S(1)} %all-to-all-done.2.parts_ref) | copy-start | bytes 5505028
  181.5 26.1 %copy-start.13 = (f32[16,128]{1,0:T(8,128)S(1)}, f32[16,128]{1,0:T(8,128)}, u32[]{:S(2)}) copy-start(f32[16,128]{1,0:T(8,128)} %get-tuple-element.24) | copy-start | bytes 24580
  181.5 8.7 %all-to-all-start.5 = ((bf16[4,2,16,768]{3,2,1,0:T(8,128)(2,1)}), bf16[4,2,16,768]{3,2,1,0:T(8,128)(2,1)S(1)}, u32[]{:S(2)}, u32[]{:S(2)}) async-start(bf16[4,2,16,768]{3,2,1,0:T(8,128)(2,1)} %first_sum.3), calls=%async_computation.5 | async-start | bytes 393216 | tf_op jit(solution)/shard_map/all_to_all | solution.py:593
  190.2 14.8 %copy-start.6 = (bf16[4,2,16,768]{3,2,1,0:T(8,128)(2,1)}, bf16[4,2,16,768]{3,2,1,0:T(8,128)(2,1)S(1)}, u32[]{:S(2)}) copy-start(bf16[4,2,16,768]{3,2,1,0:T(8,128)(2,1)S(1)} %all-to-all-done.5.refs_1_) | copy-start | bytes 589828
  190.2 14.8 %all-to-all-start.4 = ((bf16[4,2,16,1792]{3,2,1,0:T(8,128)(2,1)}), bf16[4,2,16,1792]{3,2,1,0:T(8,128)(2,1)S(1)}, u32[]{:S(2)}, u32[]{:S(2)}) async-start(bf16[4,2,16,1792]{3,2,1,0:T(8,128)(2,1)} %first_sum.2), calls=%async_computation.4 | async-start | bytes 917504 | tf_op jit(solution)/shard_map/all_to_all | solution.py:593
  205.0 0.8 copy-start.5
  207.6 1.5 collective-permute-start.18

commit v4 on v3

--- a/solution.py
+++ b/solution.py
@@ -105,7 +105,7 @@
 CHIPS = 4
 GROUP = CORES * CHIPS
 SLOTS = 4
-VMEM_LIMIT = 56 * 1024 * 1024
+VMEM_LIMIT = 30 * 1024 * 1024
 
 
 def kernel_params():
@@ -114,6 +114,10 @@
 
 def vmem_spec():
     return pl.BlockSpec(memory_space=pltpu.VMEM)
+
+
+def hbm_spec():
+    return pl.BlockSpec(memory_space=pltpu.HBM)
 
 
 def smem_spec():
@@ -169,31 +173,49 @@
             entropy_ref[...] = jnp.broadcast_to(entropy[:rows], entropy_ref.shape)
 
 
-def assemble(pieces, places, rows, out_ref):
-    for piece, blocks in zip(pieces, places):
-        for i, block in enumerate(blocks):
-            out_ref[pl.ds(block * rows, rows), :] = piece[pl.ds(i * rows, rows), :]
-
-
-def logits_kernel(rows, places, last, *refs):
-    count = len(places)
-    pieces, w_ref, refs = refs[:count], refs[count], refs[count + 1 :]
+def assemble(pieces, layer, rows, out_ref):
+    layers = out_ref.shape[0] // (GROUP * rows)
+    for core, piece in enumerate(pieces):
+        for chip in range(CHIPS):
+            for i in range(layers):
+                block = (layer ^ i) * GROUP + core * CHIPS + chip
+                out_ref[pl.ds(pl.multiple_of(block * rows, rows), rows), :] = piece[
+                    pl.ds((chip * layers + i) * rows, rows), :
+                ]
+
+
+def logits_kernel(rows, by_rank, first, last, pos_ref, *refs):
+    pieces, w_ref, refs = refs[:CORES], refs[CORES], refs[CORES + 1 :]
     if last:
-        before_ref, prob_ref, logits_ref, stat_ref, hidden, cross_ref = refs
+        before_ref, prob_ref, logits_ref, stat_ref, hidden, tiles, sems, cross_ref = refs
     else:
-        logits_ref, hidden = refs
-    step = pl.program_id(0)
+        logits_ref, hidden, tiles, sems = refs
+    step, steps = pl.program_id(0), w_ref.shape[1] // tiles.shape[2]
+    chunk, width = tiles.shape[1:]
+
+    def copy(t, slot):
+        column = pl.multiple_of(t * width, width)
+        return pltpu.make_async_copy(
+            w_ref.at[pl.ds(first, chunk), pl.ds(column, width)], tiles.at[slot], sems.at[slot]
+        )
 
     @pl.when(step == 0)
     def _():
-        assemble(pieces, places, rows, hidden)
-
-    part = jnp.dot(hidden[...], w_ref[...], preferred_element_type=jnp.float32)
+        for t in range(min(2, steps)):
+            copy(t, t).start()
+        assemble(pieces, pos_ref[2] if by_rank else 0, rows, hidden)
+
+    copy(step, step % 2).wait()
+    part = jnp.dot(hidden[...], tiles[step % 2], preferred_element_type=jnp.float32)
+
+    @pl.when(step + 2 < steps)
+    def _():
+        copy(step + 2, step % 2).start()
+
     if not last:
         logits_ref[...] = part
         return
     part = part + before_ref[...]
-    width = part.shape[1]
     logits_ref[:, pl.ds(pl.multiple_of(step * width, width), width)] = part
     product = part * prob_ref[...]
     folded = product[:, :128]
@@ -259,12 +281,23 @@
         grad_ref[span, :] = (weight * (student - prob_ref[span, :])).astype(grad_ref.dtype)
 
 
-def partial_kernel(rows, by_layer, pos_ref, grad_ref, sib_ref, w_ref, sib_w_ref, out_ref, swapped):
-    layers = out_ref.shape[0] if by_layer else out_ref.shape[1]
+def partial_kernel(rows, first, steps, stacked, pos_ref, grad_ref, sib_ref, w_ref, sib_w_ref, *refs):
+    outs, (swapped, tiles, sems) = refs[:-3], refs[-3:]
+    tokens = grad_ref.shape[0]
+    layers = tokens // (GROUP * rows)
     half = CHIPS * rows
-
-    @pl.when(pl.program_id(0) == 0)
-    def _():
+    step = pl.program_id(0)
+    tile = tiles.shape[1]
+    start = pos_ref[0] * (w_ref.shape[0] // CORES) + first
+
+    def copy(t, slot):
+        row = pl.multiple_of(start + t * tile, 128)
+        return pltpu.make_async_copy(w_ref.at[pl.ds(row, tile), :], tiles.at[slot], sems.at[slot])
+
+    @pl.when(step == 0)
+    def _():
+        for t in range(min(2, steps)):
+            copy(t, t).start()
         for k in range(layers):
             for core in range(CORES):
                 swapped[pl.ds((k * CORES + core) * half, half), :] = sib_ref[
@@ -272,34 +305,38 @@
                 ]
 
     contract = (((1,), (1,)), ((), ()))
-    total = lax.dot_general(
-        grad_ref[...], w_ref[...], contract, preferred_element_type=jnp.float32
-    ) + lax.dot_general(
-        swapped[...], sib_w_ref[...], contract, preferred_element_type=jnp.float32
-    )
-    for k in range(layers):
-        for j in range(CHIPS):
+    span = pl.ds(pl.multiple_of(first + step * tile, tile), tile)
+    total = lax.dot_general(swapped[...], sib_w_ref[span, :], contract, preferred_element_type=jnp.float32)
+    copy(step, step % 2).wait()
+    total += lax.dot_general(grad_ref[...], tiles[step % 2], contract, preferred_element_type=jnp.float32)
+
+    @pl.when(step + 2 < steps)
+    def _():
+        copy(step + 2, step % 2).start()
+
+    for j in range(CHIPS):
+        for k in range(layers):
             for core in range(CORES):
-                start = (k * GROUP + core * CHIPS + j) * rows
-                part = total[start : start + rows].astype(out_ref.dtype)
-                if by_layer:
-                    out_ref[pos_ref[2] ^ k, j, core] = part
+                row = (k * GROUP + core * CHIPS + j) * rows
+                part = total[row : row + rows]
+                if stacked:
+                    outs[0][pos_ref[1] ^ j, k, core] = part.astype(outs[0].dtype)
                 else:
-                    out_ref[pos_ref[1] ^ j, k, core] = part
-
-
-def head_kernel(rows, places, *refs):
+                    outs[j][k, core] = part.astype(outs[j].dtype)
+
+
+def head_kernel(rows, chunk_steps, pos_ref, *refs):
     pieces, (grad_ref, out_ref, hidden) = refs[:-3], refs[-3:]
-    step = pl.program_id(0)
-    done, first = 0, 0
-    for blocks, steps in places:
-        some = pieces[done : done + len(blocks)]
-
-        @pl.when((step >= first) & (step < first + steps))
-        def _():
-            assemble(some, blocks, rows, hidden)
-
-        done, first = done + len(blocks), first + steps
+    chunk = pl.program_id(0) // chunk_steps
+
+    @pl.when(chunk == 0)
+    def _():
+        assemble(pieces[:CORES], 0, rows, hidden)
+
+    @pl.when(chunk == 1)
+    def _():
+        assemble(pieces[CORES:], pos_ref[2], rows, hidden)
+
     out_ref[...] = lax.dot_general(
         hidden[...], grad_ref[...], (((0,), (0,)), ((), ())), preferred_element_type=jnp.float32
     ).astype(out_ref.dtype)
@@ -312,20 +349,30 @@
     return total
 
 
-def first_sum_kernel(axis, pos_ref, parts_ref, out_ref):
-    for i in range(out_ref.shape[0]):
-        out_ref[pos_ref[axis] ^ i] = total_of(parts_ref, (i,)).astype(out_ref.dtype)
-
-
-def last_sum_kernel(*refs):
-    parts, (mine, theirs) = refs[:-2], refs[-2:]
-    first = 0
-    for part in parts:
-        total = total_of(part)
-        span = pl.ds(first, total.shape[-1])
-        mine[:, span] = total[0].astype(mine.dtype)
-        theirs[:, span] = total[1].astype(theirs.dtype)
-        first += total.shape[-1]
+def chip_sum_kernel(own_ref, *refs):
+    arrived, outs = refs[: CHIPS - 1], refs[CHIPS - 1 :]
+    for k, out in enumerate(outs):
+        total = own_ref[k]
+        for part in arrived:
+            total = total + part[k].astype(jnp.float32)
+        out[...] = total.astype(out.dtype)
+
+
+def chip_sum_stacked_kernel(pos_ref, parts_ref, out_ref):
+    for k in range(out_ref.shape[0]):
+        out_ref[pos_ref[2] ^ k] = total_of(parts_ref, (k,)).astype(out_ref.dtype)
+
+
+def last_sum_kernel(own_ref, *refs):
+    arrived, (stacked_ref, mine, theirs) = refs[:-3], refs[-3:]
+    first = own_ref[...]
+    for part in arrived:
+        first = first + part[...].astype(jnp.float32)
+    second = total_of(stacked_ref)
+    split, end = first.shape[-1], mine.shape[1]
+    for core, out in enumerate((mine, theirs)):
+        out[:, :split] = first[core].astype(out.dtype)
+        out[:, split:end] = second[core].astype(out.dtype)
 
 
 def split_three(x):
@@ -335,7 +382,7 @@
     return jnp.stack([high, middle, low]).astype(jnp.bfloat16)
 
 
-def send_teacher(teacher_logits, block_lists, places):
+def send_teacher(teacher_logits, block_lists, places, after):
     blocks, listed_count, stored, side = teacher_logits.shape
     n = lax.axis_size("vocab")
     rank = lax.axis_index("vocab")
@@ -358,6 +405,7 @@
     payload = jnp.concatenate(
         [packed.reshape(n, -1, side), jnp.broadcast_to(stat, (n, 1, side))], axis=1
     )
+    payload, _ = lax.optimization_barrier((payload, after))
     arrived = lax.all_to_all(payload, "vocab", split_axis=0, concat_axis=0, tiled=True)
     arrived_blocks = (
         arrived[:, :-1]
@@ -396,35 +444,27 @@
     in_layer = [[(o * CHIPS + q) * CORES + c for q in range(CHIPS)] for o in range(layers) for c in range(CORES)]
     across = [[o * GROUP + i for o in range(layers)] for i in range(GROUP)]
 
-    wide = depth * 3 // 4
-    own = hidden_states[:, :wide]
-    column = [own] + [shift(own, k * GROUP) for k in range(1, layers)]
-    column = jnp.concatenate(column, axis=0)
-    plane = hidden_states[:, wide:]
-    for j in (1, 2):
-        plane = jnp.concatenate([plane, shift(plane, j * CORES)], axis=0)
-
-    arrived_blocks, arrived_stat, place = send_teacher(teacher_logits, block_lists, slab // side)
-
-    column, plane, late_weight = lax.optimization_barrier((column, plane, head_weight))
-    wide_pieces = [column] + [shift(column, j * CORES) for j in range(1, CHIPS)]
-    wide_pieces += [shift(piece, 1) for piece in wide_pieces]
-    wide_places = [[k * GROUP + p for k in range(layers)] for p in range(GROUP)]
-    narrow_pieces = [plane]
-    narrow_layers = [[0]]
-    for k in [1 << i for i in reversed(range((layers - 1).bit_length()))]:
-        if k > 1:
-            narrow_pieces = [jnp.concatenate([plane, shift(plane, k * GROUP)], axis=0)]
-            plane = narrow_pieces[0]
-            narrow_layers = [narrow_layers[0] + [i ^ k for i in narrow_layers[0]]]
-        else:
-            narrow_pieces.append(shift(plane, GROUP))
-            narrow_layers.append([i ^ 1 for i in narrow_layers[0]])
-    narrow_pieces += [shift(piece, 1) for piece in narrow_pieces]
-    narrow_places = [
-        [k * GROUP + c * CHIPS + j for k in some for j in range(CHIPS)] for c in range(CORES) for some in narrow_layers
-    ]
-    sib_w = shift(lax.dynamic_slice(late_weight, ((1 - core) * half, 0), (half, slab)), 1)
+    chunk = depth // 2
+    column = hidden_states[:, :chunk]
+    column = jnp.concatenate([column] + [shift(column, k * GROUP) for k in range(1, layers)], axis=0)
+    late_column = jnp.broadcast_to(hidden_states[None, :, chunk:], (layers, rows, chunk))
+    late_column = lax.all_to_all(
+        late_column.reshape(layers * rows, chunk),
+        "vocab",
+        split_axis=0,
+        concat_axis=0,
+        axis_index_groups=across,
+        tiled=True,
+    )
+    sib_w = shift(lax.dynamic_slice(head_weight, ((1 - core) * half, 0), (half, slab)), 1)
+    plane = [column] + [shift(column, j * CORES) for j in range(1, CHIPS)]
+    arrived_blocks, arrived_stat, place = send_teacher(
+        teacher_logits, block_lists, slab // side, late_column
+    )
+    late_column, plane[1], sib_w = lax.optimization_barrier((late_column, plane[1], sib_w))
+    late_plane = [late_column] + [shift(late_column, j * CORES) for j in range(1, CHIPS)]
+    plane = jnp.concatenate(plane, axis=0)
+    hidden = [plane, shift(plane, 1)]
 
     prob, entropy = pl.pallas_call(
         lambda *refs: teacher_kernel(unlisted, rows, *refs),
@@ -451,13 +491,16 @@
     width = 256 if slab % 256 == 0 else 128
     whole = lambda t: (0, 0)
     tile_out = pl.BlockSpec((tokens, width), lambda t: (0, t))
-    narrow = depth - wide
-
-    def logits_call(pieces, places, chunk, first, before=None):
+
+    def logits_call(pieces, first, before=None):
         last = before is not None
         out_shape = [jax.ShapeDtypeStruct((tokens, slab), f32)]
         out_specs = [tile_out]
-        scratch = [pltpu.VMEM((tokens, chunk), bf16)]
+        scratch = [
+            pltpu.VMEM((tokens, chunk), bf16),
+            pltpu.VMEM((2, chunk, width), bf16),
+            pltpu.SemaphoreType.DMA((2,)),
+        ]
         if last:
             scratch.append(pltpu.VMEM((tokens, 128), f32))
             out_shape.append(jax.ShapeDtypeStruct((n, 2 * tokens // 128, 128), f32))
@@ -466,12 +509,10 @@
                 pl.BlockSpec((n, 2 * tokens // 128, 128), lambda t: (0, 0, 0)),
             ]
         return pl.pallas_call(
-            functools.partial(logits_kernel, rows, places, last),
+            functools.partial(logits_kernel, rows, last, first, last),
             grid=(slab // width,),
             out_shape=out_shape,
-            in_specs=[pl.BlockSpec(piece.shape, whole) for piece in pieces]
-            + [pl.BlockSpec((chunk, width), lambda t: (first // chunk, t))]
-            + [tile_out] * (2 * last),
+            in_specs=[smem_spec()] + [vmem_spec()] * CORES + [hbm_spec()] + [tile_out] * (2 * last),
             out_specs=out_specs,
             scratch_shapes=scratch,
             compiler_params=kernel_params(),
@@ -481,10 +522,13 @@
                 transcendentals=tokens * slab if last else 0,
             ),
             name="logits",
-        )(*pieces, head_weight, *((before, prob) if last else ()))
-
-    (logits,) = logits_call(narrow_pieces, narrow_places, narrow, wide)
-    logits, stat = logits_call(wide_pieces, wide_places, wide, 0, logits)
+        )(pos, *pieces, head_weight, *((before, prob) if last else ()))
+
+    (logits,) = logits_call(hidden, 0)
+    late_plane, logits, prob = lax.optimization_barrier((late_plane, logits, prob))
+    late_plane = jnp.concatenate(late_plane, axis=0)
+    late_hidden = [late_plane, shift(late_plane, 1)]
+    logits, stat = logits_call(late_hidden, chunk, logits)
     stat = lax.all_to_all(stat, "vocab", split_axis=0, concat_axis=0, tiled=True)
 
     grad, loss = pl.pallas_call(
@@ -503,60 +547,55 @@
     )(pos, stat, logits, prob, token_weight.reshape(blocks, 1, side), entropy)
     sib_grad = shift(grad, 1)
 
-    back = half // 10 * 3 // 256 * 256
-    sent = []
-    for first, size, by_layer in ((0, half - back, False), (half - back, back, True)):
-        tile = size // 2 if size % 256 == 0 and size > 1024 else size
-        steps = size // tile
-        shape = (layers, CHIPS, CORES, rows) if by_layer else (CHIPS, layers, CORES, rows)
-        partial = pl.pallas_call(
-            functools.partial(partial_kernel, rows, by_layer),
-            grid_spec=pltpu.PrefetchScalarGridSpec(
-                num_scalar_prefetch=1,
-                grid=(steps,),
-                in_specs=[
-                    pl.BlockSpec((tokens, slab), lambda t, pos: (0, 0)),
-                    pl.BlockSpec((tokens, slab), lambda t, pos: (0, 0)),
-                    pl.BlockSpec(
-                        (pl.Element(tile), pl.Element(slab)),
-                        lambda t, pos, first=first, tile=tile: (pl.multiple_of(pos[0] * half + first + t * tile, 128), 0),
-                    ),
-                    pl.BlockSpec(
-                        (pl.Element(tile), pl.Element(slab)),
-                        lambda t, pos, first=first, tile=tile: (pl.multiple_of(first + t * tile, 128), 0),
-                    ),
-                ],
-                out_specs=pl.BlockSpec((*shape, tile), lambda t, pos: (0, 0, 0, 0, t)),
-                scratch_shapes=[pltpu.VMEM((tokens, slab), bf16)],
-            ),
-            out_shape=jax.ShapeDtypeStruct((*shape, size), bf16),
+    tile = half // 5
+    sizes = (3 * tile, 2 * tile)
+    late_grad, later_sib_w = grad, sib_w
+    partials = []
+    for i, size in enumerate(sizes):
+        first = sum(sizes[:i])
+        stacked = i == 1
+        if stacked:
+            shapes = [(CHIPS, layers, CORES, rows)]
+        else:
+            shapes = [(layers, CORES, rows)] * CHIPS
+        outs = pl.pallas_call(
+            functools.partial(partial_kernel, rows, first, size // tile, stacked),
+            grid=(size // tile,),
+            in_specs=[smem_spec(), vmem_spec(), vmem_spec(), hbm_spec(), vmem_spec()],
+            out_specs=[
+                pl.BlockSpec((*shape, tile), lambda t, count=len(shape): (0,) * count + (t,)) for shape in shapes
+            ],
+            out_shape=[
+                jax.ShapeDtypeStruct((*shape, size), f32 if j == 0 and not stacked else bf16)
+                for j, shape in enumerate(shapes)
+            ],
+            scratch_shapes=[
+                pltpu.VMEM((tokens, slab), bf16),
+                pltpu.VMEM((2, tile, slab), bf16),
+                pltpu.SemaphoreType.DMA((2,)),
+            ],
             compiler_params=kernel_params(),
             cost_estimate=pl.CostEstimate(
                 flops=4 * tokens * size * slab, bytes_accessed=4 * size * slab, transcendentals=0
             ),
             name="grad_hidden_partial",
-        )(pos, grad, sib_grad, head_weight, sib_w)
-        groups = across if by_layer else in_layer
-        sent.append(
-            lax.all_to_all(
-                partial, "vocab", split_axis=0, concat_axis=0, axis_index_groups=groups, tiled=True
-            )
-        )
-
-    _, late_grad = lax.optimization_barrier((partial, grad))
-    head_tile = narrow
-    places = [(wide_places, wide // head_tile), (narrow_places, narrow // head_tile)]
+        )(pos, late_grad, sib_grad, head_weight, later_sib_w)
+        *outs, late_grad, later_sib_w = lax.optimization_barrier((*outs, late_grad, later_sib_w))
+        partials.append(outs)
+    arrived = [shift(partials[0][j], j * CORES) for j in range(1, CHIPS)]
+    late_arrived = lax.all_to_all(
+        partials[1][0], "vocab", split_axis=0, concat_axis=0, axis_index_groups=in_layer, tiled=True
+    )
+
+    head_tile = chunk // 2
     piece_specs = [
-        pl.BlockSpec((piece.shape[0], head_tile), lambda t: (0, jnp.minimum(t, wide // head_tile - 1)))
-        for piece in wide_pieces
-    ] + [
-        pl.BlockSpec((piece.shape[0], head_tile), lambda t: (0, jnp.maximum(t - wide // head_tile, 0)))
-        for piece in narrow_pieces
+        pl.BlockSpec((tokens // CORES, head_tile), lambda t, i=i: (0, jnp.clip(t - 2 * i, 0, 1)))
+        for i in (0, 0, 1, 1)
     ]
     grad_head = pl.pallas_call(
-        functools.partial(head_kernel, rows, places),
-        grid=(depth // head_tile,),
-        in_specs=piece_specs + [pl.BlockSpec((tokens, slab), whole)],
+        functools.partial(head_kernel, rows, 2),
+        grid=(4,),
+        in_specs=[smem_spec()] + piece_specs + [vmem_spec()],
         out_specs=pl.BlockSpec((head_tile, slab), lambda t: (t, 0)),
         out_shape=jax.ShapeDtypeStruct((depth, slab), bf16),
         scratch_shapes=[pltpu.VMEM((tokens, head_tile), bf16)],
@@ -565,38 +604,40 @@
             flops=2 * tokens * depth * slab, bytes_accessed=2 * depth * (slab + tokens), transcendentals=0
         ),
         name="grad_head",
-    )(*wide_pieces, *narrow_pieces, late_grad)
-    sent, grad_head = lax.optimization_barrier((sent, grad_head))
-
-    arrived = []
-    for parts, by_layer in zip(sent, (False, True)):
-        size = parts.shape[-1]
-        tile = size // 2 if size % 256 == 0 and size > 1024 else size
-        count = parts.shape[1]
-        summed = pl.pallas_call(
-            functools.partial(first_sum_kernel, 1 if by_layer else 2),
-            grid=(size // tile,),
-            in_specs=[
-                smem_spec(),
-                pl.BlockSpec((*parts.shape[:-1], tile), lambda t: (0, 0, 0, 0, t)),
-            ],
-            out_specs=pl.BlockSpec((count, CORES, rows, tile), lambda t: (0, 0, 0, t)),
-            out_shape=jax.ShapeDtypeStruct((count, CORES, rows, size), bf16),
-            compiler_params=kernel_params(),
-            cost_estimate=pl.CostEstimate(
-                flops=tokens * size, bytes_accessed=3 * tokens * size, transcendentals=0
-            ),
-            name="first_sum",
-        )(pos, parts)
-        groups = in_layer if by_layer else across
-        arrived.append(
-            lax.all_to_all(
-                summed, "vocab", split_axis=0, concat_axis=0, axis_index_groups=groups, tiled=True
-            )
-        )
+    )(pos, *hidden, *late_hidden, late_grad)
+    arrived, grad_head = lax.optimization_barrier((arrived, grad_head))
+
+    summed = pl.pallas_call(
+        chip_sum_kernel,
+        in_specs=[vmem_spec()] * CHIPS,
+        out_specs=[vmem_spec()] * layers,
+        out_shape=[
+            jax.ShapeDtypeStruct((CORES, rows, sizes[0]), f32 if k == 0 else bf16) for k in range(layers)
+        ],
+        compiler_params=kernel_params(),
+        cost_estimate=pl.CostEstimate(
+            flops=tokens * sizes[0], bytes_accessed=3 * tokens * sizes[0], transcendentals=0
+        ),
+        name="chip_sum",
+    )(partials[0][0], *arrived)
+    arrived = [shift(summed[k], k * GROUP) for k in range(1, layers)]
+    late_summed = pl.pallas_call(
+        chip_sum_stacked_kernel,
+        in_specs=[smem_spec(), vmem_spec()],
+        out_specs=vmem_spec(),
+        out_shape=jax.ShapeDtypeStruct((layers, CORES, rows, sizes[1]), bf16),
+        compiler_params=kernel_params(),
+        cost_estimate=pl.CostEstimate(
+            flops=tokens * sizes[1], bytes_accessed=3 * tokens * sizes[1], transcendentals=0
+        ),
+        name="chip_sum",
+    )(pos, late_arrived)
+    late_arrived = lax.all_to_all(
+        late_summed, "vocab", split_axis=0, concat_axis=0, axis_index_groups=across, tiled=True
+    )
     mine, theirs = pl.pallas_call(
         last_sum_kernel,
-        in_specs=[vmem_spec()] * 2,
+        in_specs=[vmem_spec()] * (layers + 1),
         out_specs=[vmem_spec()] * 2,
         out_shape=[jax.ShapeDtypeStruct((rows, half), bf16)] * 2,
         compiler_params=kernel_params(),
@@ -604,7 +645,7 @@
             flops=CORES * layers * rows * half, bytes_accessed=3 * CORES * layers * rows * half, transcendentals=0
         ),
         name="last_sum",
-    )(*arrived)
+    )(summed[0], *arrived, late_arrived)
     other = shift(theirs, 1)
 
     low, high = jnp.where(core == 0, mine, other), jnp.where(core == 0, other, mine)

time: 212 us -> 179 us (0.84)
  waiting for transfers between devices: 86.5 us -> 52.2 us
  Pallas kernels: 58.4 us -> 41.9 us
  local copies, waits for them, and re-layouts: 13.7 us -> 27.7 us
  starting transfers between devices: 31.8 us -> 38.4 us
    ppermute x19 -> x20, waiting for transfers between devices: 50.4 us -> 24.4 us  [shift(): return lax.ppermute(x, 'vocab', [(i, i ^ distance) for i in range(n)])]
    all_to_all x4 -> x3, waiting for transfers between devices: 36.1 us -> 11.4 us  [the longest x1 11.4 us: levels_plan(): lax.all_to_all(partials[1][0], 'vocab', split_axis=0, concat_axis=0, axis...]
    all_to_all x1, waiting for transfers between devices: 0.01 us -> 16.4 us  [send_teacher(): lax.all_to_all(payload, 'vocab', split_axis=0, concat_axis=0, tiled=True)]
    unnamed x32 -> x64, local copies, waits for them, and re-layouts: 3.12 us -> 15.3 us
    pallas_call x8, Pallas kernels: 49.4 us -> 37.6 us  [the longest x2 14.2 us: levels_plan(): pl.pallas_call(functools.partial(partial_kernel, rows, first, size // til...]
    ppermute x19 -> x20, starting transfers between devices: 14.3 us -> 21.3 us  [shift(): return lax.ppermute(x, 'vocab', [(i, i ^ distance) for i in range(n)])]
    pallas_call x1, Pallas kernels: 4.1 us -> 1.28 us  [levels_plan(): pl.pallas_call(lambda *refs: grad_kernel(rows, *refs), out_shape=(jax.Sha...]
    all_to_all x4 -> x3, starting transfers between devices: 14.2 us -> 12 us  [the longest x1 5.09 us: levels_plan(): lax.all_to_all(late_column.reshape(layers * rows, chunk), 'vocab', split_...]
  transfers between devices with their start and end apart: 24 -> 24, of which waited for: 14 -> 8; matrix products, arithmetic and copies ran while one was open for 4% -> 7% of each run, Pallas kernels for 23% -> 11%
where the time goes in v4:
time: 179 us; the launch traced here: 178 us
  waiting for transfers between devices  52.2 us (29%)
  Pallas kernels  41.9 us (23%)
  starting transfers between devices  38.4 us (21%)
  local copies, waits for them, and re-layouts  27.7 us (15%)
  blocking collectives  11.3 us (6%)
  other arithmetic  4.58 us (3%)
    ppermute x20, waiting for transfers between devices, shift(): return lax.ppermute(x, 'vocab', [(i, i ^ distance) for i in range(n)])  24.4 us
    ppermute x20, starting transfers between devices, shift(): return lax.ppermute(x, 'vocab', [(i, i ^ distance) for i in range(n)])  21.3 us
    all_to_all x1, waiting for transfers between devices, send_teacher(): lax.all_to_all(payload, 'vocab', split_axis=0, concat_axis=0, tiled=True)  16.4 us
    unnamed x64, local copies, waits for them, and re-layouts  15.3 us
    pallas_call x2, Pallas kernels, levels_plan(): pl.pallas_call(functools.partial(partial_kernel, rows, first, size // til...  14.2 us
    pallas_call x2, Pallas kernels, logits_call(): pl.pallas_call(functools.partial(logits_kernel, rows, last, first, last),...  12 us
    all_to_all x1, waiting for transfers between devices, levels_plan(): lax.all_to_all(partials[1][0], 'vocab', split_axis=0, concat_axis=0, axis...  11.4 us
    all_to_all x1, blocking collectives, levels_plan(): lax.all_to_all(stat, 'vocab', split_axis=0, concat_axis=0, tiled=True)  11.3 us
  transfers between devices with their start and end apart: 24, of which 8 were waited for; matrix products, arithmetic and copies ran while one was open for 7% of the time, Pallas kernels for 11%

profile of v4, /device:TPU:0, one launch (start us, length us, event | category | flops | bytes accessed | tf_op | source)
XLA Modules:
  0.0 177.8 jit_solution(15184062876849372012)
XLA Ops:
  0.7 5.5 %constant_dynamic-slice_fusion = bf16[2560,1024]{1,0:T(8,128)(2,1)} fusion(bf16[5120,1024]{1,0:T(8,128)(2,1)} %w_ref.3, s32[]{:T(128)S(6)} %select_n.54), kind=kLoop, calls=%fused_computation.54 | loop fusion | bytes 10485764 | tf_op jit(solution)/shard_map/dynamic_slice | solution.py:459
  6.1 0.5 collective-permute-start.4
  6.6 0.7 constant_dynamic-update-slice_fusion.6
  7.2 4.6 %collective-permute-start.2 = (bf16[16,2560]{1,0:T(8,128)(2,1)}, bf16[16,2560]{1,0:T(8,128)(2,1)S(1)}, u32[]{:S(2)}, u32[]{:S(2)}) collective-permute-start(bf16[16,2560]{1,0:T(8,128)(2,1)} %get-tuple-element.84), channel_id=1, source_target_pairs={{0,24},{1,25},{2,26},{3,27},{4,28},{5,29},{6,30},{7,31},{8,16},{9,... | collective-permute-start | bytes 245768 | tf_op jit(solution)/shard_map/ppermute | solution.py:129
  11.8 0.6 collective-permute-start
  12.4 0.7 broadcast_in_dim.14
  13.1 5.1 %all-to-all-start = ((bf16[4,16,2560]{2,1,0:T(8,128)(2,1)}), bf16[4,16,2560]{2,1,0:T(8,128)(2,1)S(1)}, u32[]{:S(2)}, u32[]{:S(2)}) async-start(bf16[4,16,2560]{2,1,0:T(8,128)(2,1)} %broadcast_in_dim.14), calls=%async_computation | async-start | bytes 655360 | tf_op jit(solution)/shard_map/all_to_all | solution.py:451
  18.5 0.5 fusion.1
  19.0 0.6 add_select_fusion.1
  19.9 0.4 convolution_convert_fusion
  20.6 0.4 copy.43
  21.1 0.6 pad.4
  21.7 1.0 pad_maximum_fusion.1
  22.7 2.5 %collective-permute-start.9 = (bf16[64,2560]{1,0:T(8,128)(2,1)S(1)}, bf16[64,2560]{1,0:T(8,128)(2,1)S(1)}, u32[]{:S(2)}, u32[]{:S(2)}) collective-permute-start(bf16[64,2560]{1,0:T(8,128)(2,1)S(1)} %pad_maximum_fusion.1), channel_id=1, source_target_pairs={{0,6},{1,7},{2,4},{3,5},{4,2},{5,3},{6,0},{7,1},{8,14},{9,15},{10,... | collective-permute-start | bytes 983048 | tf_op jit(solution)/shard_map/ppermute | solution.py:129
  25.2 0.5 collective-permute-start.8
  25.7 0.5 collective-permute-start.3
  26.3 0.9 constant_dynamic-update-slice_fusion.5
  27.2 0.9 constant_dynamic-update-slice_fusion.4
  28.1 11.7 %collective-permute-done.3 = bf16[64,2560]{1,0:T(8,128)(2,1)S(1)} collective-permute-done((bf16[64,2560]{1,0:T(8,128)(2,1)S(1)}, bf16[64,2560]{1,0:T(8,128)(2,1)S(1)}, u32[]{:S(2)}, u32[]{:S(2)}) %collective-permute-start.3) | collective-permute-done | bytes 327712 | tf_op jit(solution)/shard_map/ppermute | solution.py:129
  40.0 0.7 broadcast_in_dim.17
  40.7 0.9 pad_maximum_fusion
  41.6 5.1 %all-to-all-start.1 = ((bf16[32,65,128]{2,1,0:T(8,128)(2,1)}), bf16[32,65,128]{2,1,0:T(8,128)(2,1)}, u32[]{:S(2)}, u32[]{:S(2)}) async-start(bf16[32,65,128]{2,1,0:T(8,128)(2,1)} %pad_maximum_fusion), calls=%async_computation.1 | async-start | bytes 1179648 | tf_op jit(solution)/shard_map/all_to_all | solution.py:409
  47.1 16.4 %all-to-all-done.1 = bf16[32,65,128]{2,1,0:T(8,128)(2,1)} async-done(((bf16[32,65,128]{2,1,0:T(8,128)(2,1)}), bf16[32,65,128]{2,1,0:T(8,128)(2,1)}, u32[]{:S(2)}, u32[]{:S(2)}) %all-to-all-start.1) | async-done | bytes 532512 | tf_op jit(solution)/shard_map/all_to_all | solution.py:409
  63.5 0.9 slice.21
  64.3 2.1 %collective-permute-start.7 = (bf16[64,2560]{1,0:T(8,128)(2,1)}, bf16[64,2560]{1,0:T(8,128)(2,1)}, u32[]{:S(2)}, u32[]{:S(2)}) collective-permute-start(bf16[64,2560]{1,0:T(8,128)(2,1)} %bitcast.40), channel_id=1, source_target_pairs={{0,6},{1,7},{2,4},{3,5},{4,2},{5,3},{6,0},{7,1},{8,14},{9,15},{10,... | collective-permute-start | bytes 983048 | tf_op jit(solution)/shard_map/ppermute | solution.py:129
  66.5 0.5 collective-permute-start.6
  67.0 0.9 collective-permute-start.5
  67.9 1.1 slice.20
  69.0 0.3 copy.52
  70.0 3.0 %teacher_prob.1 = (f32[512,1024]{1,0:T(8,128)S(1)}, f32[16,128]{1,0:T(8,128)S(1)}) custom-call(s32[4]{0:T(128)S(1)} %pad_add_fusion.pos_ref.refs_0_, s32[4,4]{1,0:T(4,128)S(1)} %broadcast_add_fusion.refs_1_, bf16[4,4,128,128]{3,2,1,0:T(8,128)(2,1)S(1)} %bitcast.32, f32[2,4,1,128]{3,2,1,0:T(1,128)S(1)} %bitcast.33, s32[4,1,128]{2,1,0:T(1,128)S(1)} %bitcast.34, ...), custom_call_target="tpu_custom_call" | custom-call | flops 67108864 | bytes 2097152 | tf_op jit(solution)/shard_map/teacher_prob/pallas_call | solution.py:469
  73.1 4.0 %copy-done = bf16[5120,1024]{1,0:T(8,128)(2,1)S(1)} copy-done((bf16[5120,1024]{1,0:T(8,128)(2,1)S(1)}, bf16[5120,1024]{1,0:T(8,128)(2,1)}, u32[]{:S(2)}) %copy-start) | copy-done | bytes 10485784
  77.1 5.2 %logits.2.refs_3_ = f32[512,1024]{1,0:T(8,128)S(1)} custom-call(s32[4]{0:T(128)S(1)} %pad_add_fusion.pos_ref.refs_0_, bf16[256,2560]{1,0:T(8,128)(2,1)S(1)} %constant_dynamic-update-slice_fusion.refs_0_, bf16[256,2560]{1,0:T(8,128)(2,1)S(1)} %collective-permute-done.10.refs_1_, bf16[5120,1024]{1,0:T(8,128)(2,1)S(1)} %copy-done), custom_call_target="tpu_custom_call" | custom-call | flops 2684354560 | bytes 9961472 | tf_op jit(solution)/shard_map/logits/pallas_call | solution.py:511
  82.3 1.0 constant_dynamic-update-slice_fusion.9
  83.3 1.0 constant_dynamic-update-slice_fusion.8
  84.3 1.1 constant_dynamic-update-slice_fusion.7.refs_0_.refs_2_
  85.6 3.0 %collective-permute-done.11.refs_1_.refs_3_ = bf16[256,2560]{1,0:T(8,128)(2,1)S(1)} collective-permute-done((bf16[256,2560]{1,0:T(8,128)(2,1)S(1)}, bf16[256,2560]{1,0:T(8,128)(2,1)S(1)}, u32[]{:S(2)}, u32[]{:S(2)}) %collective-permute-start.11) | collective-permute-done | bytes 1310752 | tf_op jit(solution)/shard_map/ppermute | solution.py:129
  88.6 6.9 %logits.3 = (f32[512,1024]{1,0:T(8,128)S(1)}, f32[32,8,128]{2,1,0:T(8,128)S(1)}) custom-call(s32[4]{0:T(128)S(1)} %pad_add_fusion.pos_ref.refs_0_, bf16[256,2560]{1,0:T(8,128)(2,1)S(1)} %constant_dynamic-update-slice_fusion.7.refs_0_.refs_2_, bf16[256,2560]{1,0:T(8,128)(2,1)S(1)} %collective-permute-done.11.refs_1_.refs_3_, bf16[5120,1024]{1,0:T(8,128)(2,1)S(1)} %copy-done, ...), custom_call_target="tpu_custom_call" | custom-call | flops 2684354560 | bytes 9961472 | tf_op jit(solution)/shard_map/logits/pallas_call | solution.py:511
  95.5 11.3 %all_to_all.29.refs_1_ = f32[32,8,128]{2,1,0:T(8,128)S(1)} all-to-all(f32[32,8,128]{2,1,0:T(8,128)S(1)} %get-tuple-element.51), channel_id=1, replica_groups=mesh['vocab'=32] {'vocab'}, dimensions={0} | all-to-all | bytes 262144 | tf_op jit(solution)/shard_map/all_to_all | solution.py:532
  106.8 1.3 grad_logits.1
  108.1 0.3 collective-permute-start.12
  108.4 2.4 %collective-permute-done.12.sib_ref = bf16[512,1024]{1,0:T(8,128)(2,1)S(1)} collective-permute-done((bf16[512,1024]{1,0:T(8,128)(2,1)S(1)}, bf16[512,1024]{1,0:T(8,128)(2,1)S(1)}, u32[]{:S(2)}, u32[]{:S(2)}) %collective-permute-start.12) | collective-permute-done | bytes 1048608 | tf_op jit(solution)/shard_map/ppermute | solution.py:129
  110.9 7.4 %grad_hidden_partial.2 = (f32[4,2,16,1536]{3,2,1,0:T(8,128)S(1)}, bf16[4,2,16,1536]{3,2,1,0:T(8,128)(2,1)S(1)}, bf16[4,2,16,1536]{3,2,1,0:T(8,128)(2,1)S(1)}, bf16[4,2,16,1536]{3,2,1,0:T(8,128)(2,1)S(1)}) custom-call(s32[4]{0:T(128)S(1)} %pad_add_fusion.pos_ref.refs_0_, bf16[512,1024]{1,0:T(8,128)(2,1)S(1)} %get-tuple-element.66.grad_ref.refs_4_, ...), custom_call_target="tpu_custom_call" | custom-call | flops 3221225472 | bytes 6291456 | tf_op jit(solution)/shard_map/grad_hidden_partial/pallas_call | solution.py:561
  118.3 0.9 copy-done.8
  119.2 0.8 copy-done.15
  119.9 6.8 %grad_hidden_partial.3 = bf16[4,4,2,16,1024]{4,3,2,1,0:T(8,128)(2,1)} custom-call(s32[4]{0:T(128)S(1)} %pad_add_fusion.pos_ref.refs_0_, bf16[512,1024]{1,0:T(8,128)(2,1)S(1)} %get-tuple-element.66.grad_ref.refs_4_, bf16[512,1024]{1,0:T(8,128)(2,1)S(1)} %collective-permute-done.12.sib_ref, bf16[5120,1024]{1,0:T(8,128)(2,1)S(1)} %bitcast.31, ...), custom_call_target="tpu_custom_call" | custom-call | flops 2147483648 | bytes 4194304 | tf_op jit(solution)/shard_map/grad_hidden_partial/pallas_call | solution.py:561
  126.8 3.5 %all-to-all-start.3 = ((bf16[4,4,2,16,1024]{4,3,2,1,0:T(8,128)(2,1)}), bf16[4,4,2,16,1024]{4,3,2,1,0:T(8,128)(2,1)S(1)}, u32[]{:S(2)}, u32[]{:S(2)}) async-start(bf16[4,4,2,16,1024]{4,3,2,1,0:T(8,128)(2,1)} %grad_hidden_partial.3), calls=%async_computation.3 | async-start | bytes 2097152 | tf_op jit(solution)/shard_map/all_to_all | solution.py:586
  130.3 2.0 %collective-permute-start.13 = (bf16[4,2,16,1536]{3,2,1,0:T(8,128)(2,1)}, bf16[4,2,16,1536]{3,2,1,0:T(8,128)(2,1)}, u32[]{:S(2)}, u32[]{:S(2)}) collective-permute-start(bf16[4,2,16,1536]{3,2,1,0:T(8,128)(2,1)} %copy-done.15), channel_id=1, source_target_pairs={{0,2},{1,3},{2,0},{3,1},{4,6},{5,7},{6,4},{7,5},{8,10},{9,11},{10,... | collective-permute-start | bytes 1179656 | tf_op jit(solution)/shard_map/ppermute | solution.py:129
  132.3 1.5 collective-permute-start.14
  133.9 11.4 %all-to-all-done.3.parts_ref = bf16[4,4,2,16,1024]{4,3,2,1,0:T(8,128)(2,1)S(1)} async-done(((bf16[4,4,2,16,1024]{4,3,2,1,0:T(8,128)(2,1)}), bf16[4,4,2,16,1024]{4,3,2,1,0:T(8,128)(2,1)S(1)}, u32[]{:S(2)}, u32[]{:S(2)}) %all-to-all-start.3) | async-done | bytes 1048608 | tf_op jit(solution)/shard_map/all_to_all | solution.py:586
  145.3 0.7 chip_sum.3
  146.0 0.7 copy-done.7
  146.7 3.4 %all-to-all-start.4 = ((bf16[4,2,16,1024]{3,2,1,0:T(8,128)(2,1)}), bf16[4,2,16,1024]{3,2,1,0:T(8,128)(2,1)S(1)}, u32[]{:S(2)}, u32[]{:S(2)}) async-start(bf16[4,2,16,1024]{3,2,1,0:T(8,128)(2,1)} %copy-done.7), calls=%async_computation.4 | async-start | bytes 524288 | tf_op jit(solution)/shard_map/all_to_all | solution.py:635
  150.1 1.3 copy-done.2
  151.4 1.3 copy-done.4
  152.7 1.3 copy-done.6
  154.0 9.1 %grad_head.1 = bf16[5120,1024]{1,0:T(8,128)(2,1)} custom-call(s32[4]{0:T(128)S(1)} %pad_add_fusion.pos_ref.refs_0_, bf16[256,2560]{1,0:T(8,128)(2,1)S(1)} %copy-done.2, bf16[256,2560]{1,0:T(8,128)(2,1)S(1)} %copy-done.4, bf16[256,2560]{1,0:T(8,128)(2,1)S(1)} %constant_dynamic-update-slice_fusion.7.refs_0_.refs_2_, bf16[256,2560]{1,0:T(8,128)(2,1)S(1)} %copy-done.6, ...), custom_call_target="tpu_custom_call" | custom-call | flops 5368709120 | bytes 15728640 | tf_op jit(solution)/shard_map/grad_head/pallas_call | solution.py:595
  163.2 1.4 chip_sum.2
  164.6 2.0 %collective-permute-start.16 = (bf16[2,16,1536]{2,1,0:T(8,128)(2,1)S(1)}, bf16[2,16,1536]{2,1,0:T(8,128)(2,1)S(1)}, u32[]{:S(2)}, u32[]{:S(2)}) collective-permute-start(bf16[2,16,1536]{2,1,0:T(8,128)(2,1)S(1)} %get-tuple-element.73), channel_id=1, source_target_pairs={{0,8},{1,9},{2,10},{3,11},{4,12},{5,13},{6,14},{7,15},{8,0},{9,1},... | collective-permute-start | bytes 294920 | tf_op jit(solution)/shard_map/ppermute | solution.py:129
  166.7 2.4 %collective-permute-start.17 = (bf16[2,16,1536]{2,1,0:T(8,128)(2,1)S(1)}, bf16[2,16,1536]{2,1,0:T(8,128)(2,1)S(1)}, u32[]{:S(2)}, u32[]{:S(2)}) collective-permute-start(bf16[2,16,1536]{2,1,0:T(8,128)(2,1)S(1)} %get-tuple-element.74), channel_id=1, source_target_pairs={{0,16},{1,17},{2,18},{3,19},{4,20},{5,21},{6,22},{7,23},{8,24},{9,... | collective-permute-start | bytes 294920 | tf_op jit(solution)/shard_map/ppermute | solution.py:129
  169.1 1.1 collective-permute-done.16.refs_0_
  170.2 5.5 %collective-permute-done.17.refs_1_ = bf16[2,16,1536]{2,1,0:T(8,128)(2,1)S(1)} collective-permute-done((bf16[2,16,1536]{2,1,0:T(8,128)(2,1)S(1)}, bf16[2,16,1536]{2,1,0:T(8,128)(2,1)S(1)}, u32[]{:S(2)}, u32[]{:S(2)}) %collective-permute-start.17) | collective-permute-done | bytes 98336 | tf_op jit(solution)/shard_map/ppermute | solution.py:129
  175.8 0.6 slice_reduce_fusion
  176.4 0.6 collective-permute-done.19
  177.1 0.7 pad_maximum_fusion.2
  (98 shorter events, 2.5 us)
Async XLA Ops:
  0.6 5.9 %copy-start.19 = (bf16[16,5120]{1,0:T(8,128)(2,1)S(1)}, bf16[16,5120]{1,0:T(8,128)(2,1)}, u32[]{:S(2)}) copy-start(bf16[16,5120]{1,0:T(8,128)(2,1)} %param.7) | copy-start | bytes 491524
  6.1 12.1 %copy-start.16 = (bf16[4,64,4,128]{3,2,1,0:T(4,128)(2,1)S(1)}, bf16[4,64,4,128]{3,2,1,0:T(4,128)(2,1)}, u32[]{:S(2)}) copy-start(bf16[4,64,4,128]{3,2,1,0:T(4,128)(2,1)} %param.9) | copy-start | bytes 786436
  6.1 12.9 %copy-start.23 = (s32[4,64]{1,0:T(4,128)S(1)}, s32[4,64]{1,0:T(4,128)}, u32[]{:S(2)}) copy-start(s32[4,64]{1,0:T(4,128)} %param.10) | copy-start | bytes 3076
  6.1 33.7 %collective-permute-start.4 = (bf16[2560,1024]{1,0:T(8,128)(2,1)}, bf16[2560,1024]{1,0:T(8,128)(2,1)}, u32[]{:S(2)}, u32[]{:S(2)}) collective-permute-start(bf16[2560,1024]{1,0:T(8,128)(2,1)} %constant_dynamic-slice_fusion), channel_id=1, source_target_pairs={{0,1},{1,0},{2,3},{3,2},{4,5},{5,4},{6,7},{7,6},{8,9},{9,8},{10,11... | collective-permute-start | bytes 15728648 | tf_op jit(solution)/shard_map/ppermute | solution.py:129
  7.2 14.5 %collective-permute-start.2 = (bf16[16,2560]{1,0:T(8,128)(2,1)}, bf16[16,2560]{1,0:T(8,128)(2,1)S(1)}, u32[]{:S(2)}, u32[]{:S(2)}) collective-permute-start(bf16[16,2560]{1,0:T(8,128)(2,1)} %get-tuple-element.84), channel_id=1, source_target_pairs={{0,24},{1,25},{2,26},{3,27},{4,28},{5,29},{6,30},{7,31},{8,16},{9,... | collective-permute-start | bytes 245768 | tf_op jit(solution)/shard_map/ppermute | solution.py:129
  11.8 9.9 %collective-permute-start.1 = (bf16[16,2560]{1,0:T(8,128)(2,1)}, bf16[16,2560]{1,0:T(8,128)(2,1)}, u32[]{:S(2)}, u32[]{:S(2)}) collective-permute-start(bf16[16,2560]{1,0:T(8,128)(2,1)} %get-tuple-element.84), channel_id=1, source_target_pairs={{0,16},{1,17},{2,18},{3,19},{4,20},{5,21},{6,22},{7,23},{8,24},{9,... | collective-permute-start | bytes 245768 | tf_op jit(solution)/shard_map/ppermute | solution.py:129
  11.8 9.9 %collective-permute-start = (bf16[16,2560]{1,0:T(8,128)(2,1)}, bf16[16,2560]{1,0:T(8,128)(2,1)}, u32[]{:S(2)}, u32[]{:S(2)}) collective-permute-start(bf16[16,2560]{1,0:T(8,128)(2,1)} %get-tuple-element.84), channel_id=1, source_target_pairs={{0,8},{1,9},{2,10},{3,11},{4,12},{5,13},{6,14},{7,15},{8,0},{9,1},... | collective-permute-start | bytes 245768 | tf_op jit(solution)/shard_map/ppermute | solution.py:129
  13.1 26.7 %all-to-all-start = ((bf16[4,16,2560]{2,1,0:T(8,128)(2,1)}), bf16[4,16,2560]{2,1,0:T(8,128)(2,1)S(1)}, u32[]{:S(2)}, u32[]{:S(2)}) async-start(bf16[4,16,2560]{2,1,0:T(8,128)(2,1)} %broadcast_in_dim.14), calls=%async_computation | async-start | bytes 655360 | tf_op jit(solution)/shard_map/all_to_all | solution.py:451
  19.9 0.6 copy-start.20
  22.7 17.2 %collective-permute-start.9 = (bf16[64,2560]{1,0:T(8,128)(2,1)S(1)}, bf16[64,2560]{1,0:T(8,128)(2,1)S(1)}, u32[]{:S(2)}, u32[]{:S(2)}) collective-permute-start(bf16[64,2560]{1,0:T(8,128)(2,1)S(1)} %pad_maximum_fusion.1), channel_id=1, source_target_pairs={{0,6},{1,7},{2,4},{3,5},{4,2},{5,3},{6,0},{7,1},{8,14},{9,15},{10,... | collective-permute-start | bytes 983048 | tf_op jit(solution)/shard_map/ppermute | solution.py:129
  25.2 14.6 %collective-permute-start.8 = (bf16[64,2560]{1,0:T(8,128)(2,1)S(1)}, bf16[64,2560]{1,0:T(8,128)(2,1)S(1)}, u32[]{:S(2)}, u32[]{:S(2)}) collective-permute-start(bf16[64,2560]{1,0:T(8,128)(2,1)S(1)} %pad_maximum_fusion.1), channel_id=1, source_target_pairs={{0,4},{1,5},{2,6},{3,7},{4,0},{5,1},{6,2},{7,3},{8,12},{9,13},{10,... | collective-permute-start | bytes 983048 | tf_op jit(solution)/shard_map/ppermute | solution.py:129
  25.7 14.1 %collective-permute-start.3 = (bf16[64,2560]{1,0:T(8,128)(2,1)S(1)}, bf16[64,2560]{1,0:T(8,128)(2,1)S(1)}, u32[]{:S(2)}, u32[]{:S(2)}) collective-permute-start(bf16[64,2560]{1,0:T(8,128)(2,1)S(1)} %pad_maximum_fusion.1), channel_id=1, source_target_pairs={{0,2},{1,3},{2,0},{3,1},{4,6},{5,7},{6,4},{7,5},{8,10},{9,11},{10,... | collective-permute-start | bytes 983048 | tf_op jit(solution)/shard_map/ppermute | solution.py:129
  39.8 1.8 %copy-start.17 = (bf16[4,16,2560]{2,1,0:T(8,128)(2,1)}, bf16[4,16,2560]{2,1,0:T(8,128)(2,1)S(1)}, u32[]{:S(2)}) copy-start(bf16[4,16,2560]{2,1,0:T(8,128)(2,1)S(1)} %all-to-all-done) | copy-start | bytes 983044
  39.9 33.1 %copy-start.1 = (bf16[256,2560]{1,0:T(8,128)(2,1)}, bf16[256,2560]{1,0:T(8,128)(2,1)S(1)}, u32[]{:S(2)}) copy-start(bf16[256,2560]{1,0:T(8,128)(2,1)S(1)} %constant_dynamic-update-slice_fusion.refs_0_) | copy-start | bytes 3932164
  39.9 6.9 %copy-start.21 = (s32[4,64]{1,0:T(4,128)S(1)}, s32[4,64]{1,0:T(4,128)}, u32[]{:S(2)}) copy-start(s32[4,64]{1,0:T(4,128)} %copy-done.20) | copy-start | bytes 3076
  39.9 6.9 %copy-start.22 = (s32[4,64]{1,0:T(4,128)S(1)}, s32[4,64]{1,0:T(4,128)}, u32[]{:S(2)}) copy-start(s32[4,64]{1,0:T(4,128)} %get-tuple-element.92) | copy-start | bytes 3076
  40.0 33.1 %collective-permute-start.10 = (bf16[256,2560]{1,0:T(8,128)(2,1)S(1)}, bf16[256,2560]{1,0:T(8,128)(2,1)S(1)}, u32[]{:S(2)}, u32[]{:S(2)}) collective-permute-start(bf16[256,2560]{1,0:T(8,128)(2,1)S(1)} %constant_dynamic-update-slice_fusion.refs_0_), channel_id=1, source_target_pairs={{0,1},{1,0},{2,3},{3,2},{4,5},{5,4},{6,7},{7,6},{8,9},{9,8},{10,11... | collective-permute-start | bytes 3932168 | tf_op jit(solution)/shard_map/ppermute | solution.py:129
  41.6 21.9 %all-to-all-start.1 = ((bf16[32,65,128]{2,1,0:T(8,128)(2,1)}), bf16[32,65,128]{2,1,0:T(8,128)(2,1)}, u32[]{:S(2)}, u32[]{:S(2)}) async-start(bf16[32,65,128]{2,1,0:T(8,128)(2,1)} %pad_maximum_fusion), calls=%async_computation.1 | async-start | bytes 1179648 | tf_op jit(solution)/shard_map/all_to_all | solution.py:409
  64.3 17.9 %collective-permute-start.7 = (bf16[64,2560]{1,0:T(8,128)(2,1)}, bf16[64,2560]{1,0:T(8,128)(2,1)}, u32[]{:S(2)}, u32[]{:S(2)}) collective-permute-start(bf16[64,2560]{1,0:T(8,128)(2,1)} %bitcast.40), channel_id=1, source_target_pairs={{0,6},{1,7},{2,4},{3,5},{4,2},{5,3},{6,0},{7,1},{8,14},{9,15},{10,... | collective-permute-start | bytes 983048 | tf_op jit(solution)/shard_map/ppermute | solution.py:129
  66.5 15.8 %collective-permute-start.6 = (bf16[64,2560]{1,0:T(8,128)(2,1)}, bf16[64,2560]{1,0:T(8,128)(2,1)}, u32[]{:S(2)}, u32[]{:S(2)}) collective-permute-start(bf16[64,2560]{1,0:T(8,128)(2,1)} %bitcast.41), channel_id=1, source_target_pairs={{0,4},{1,5},{2,6},{3,7},{4,0},{5,1},{6,2},{7,3},{8,12},{9,13},{10,... | collective-permute-start | bytes 983048 | tf_op jit(solution)/shard_map/ppermute | solution.py:129
  67.0 15.3 %collective-permute-start.5 = (bf16[64,2560]{1,0:T(8,128)(2,1)}, bf16[64,2560]{1,0:T(8,128)(2,1)}, u32[]{:S(2)}, u32[]{:S(2)}) collective-permute-start(bf16[64,2560]{1,0:T(8,128)(2,1)} %bitcast.42), channel_id=1, source_target_pairs={{0,2},{1,3},{2,0},{3,1},{4,6},{5,7},{6,4},{7,5},{8,10},{9,11},{10,... | collective-permute-start | bytes 983048 | tf_op jit(solution)/shard_map/ppermute | solution.py:129
  69.0 1.0 copy-start.10
  69.0 1.0 copy-start.11
  73.1 4.0 %copy-start = (bf16[5120,1024]{1,0:T(8,128)(2,1)S(1)}, bf16[5120,1024]{1,0:T(8,128)(2,1)}, u32[]{:S(2)}) copy-start(bf16[5120,1024]{1,0:T(8,128)(2,1)} %w_ref.3) | copy-start | bytes 31457284
  77.1 5.2 %copy-start.3 = (bf16[256,2560]{1,0:T(8,128)(2,1)}, bf16[256,2560]{1,0:T(8,128)(2,1)S(1)}, u32[]{:S(2)}) copy-start(bf16[256,2560]{1,0:T(8,128)(2,1)S(1)} %collective-permute-done.10.refs_1_) | copy-start | bytes 3932164
  77.1 5.2 %copy-start.18 = (bf16[4,16,2560]{2,1,0:T(8,128)(2,1)S(1)}, bf16[4,16,2560]{2,1,0:T(8,128)(2,1)}, u32[]{:S(2)}) copy-start(bf16[4,16,2560]{2,1,0:T(8,128)(2,1)} %copy-done.17) | copy-start | bytes 983044
  84.3 26.5 %slice-start = ((s8[10485760]{0:T(1024)(128)(4,1)}), s8[4194304]{0:T(1024)(128)(4,1)S(1)}, s32[]{:S(2)}) async-start(s8[10485760]{0:T(1024)(128)(4,1)} %bitcast.30), calls=%async_computation.5 | async-start | bytes 8388608
  85.5 21.4 %copy-start.12 = (f32[512]{0:T(512)S(1)}, f32[512]{0:T(512)}, u32[]{:S(2)}) copy-start(f32[512]{0:T(512)} %param.13) | copy-start | bytes 6148
  85.5 25.4 %slice-start.1 = ((s8[10485760]{0:T(1024)(128)(4,1)}), s8[4194304]{0:T(1024)(128)(4,1)S(1)}, s32[]{:S(2)}) async-start(s8[10485760]{0:T(1024)(128)(4,1)} %bitcast.30), calls=%async_computation.6 | async-start | bytes 8388608
  85.5 25.4 %slice-start.2 = ((s8[10485760]{0:T(1024)(128)(4,1)}), s8[2097152]{0:T(1024)(128)(4,1)S(1)}, s32[]{:S(2)}) async-start(s8[10485760]{0:T(1024)(128)(4,1)} %bitcast.30), calls=%async_computation.7 | async-start | bytes 4194304
  85.5 3.1 %collective-permute-start.11 = (bf16[256,2560]{1,0:T(8,128)(2,1)S(1)}, bf16[256,2560]{1,0:T(8,128)(2,1)S(1)}, u32[]{:S(2)}, u32[]{:S(2)}) collective-permute-start(bf16[256,2560]{1,0:T(8,128)(2,1)S(1)} %constant_dynamic-update-slice_fusion.7.refs_0_.refs_2_), channel_id=1, source_target_pairs={{0,1},{1,0},{2,3},{3,2},{4,5},{5,4},{6,7},{7,6},{8,9},{9,8},{10,11... | collective-permute-start | bytes 3932168 | tf_op jit(solution)/shard_map/ppermute | solution.py:129
  88.6 6.9 %copy-start.5 = (bf16[256,2560]{1,0:T(8,128)(2,1)}, bf16[256,2560]{1,0:T(8,128)(2,1)S(1)}, u32[]{:S(2)}) copy-start(bf16[256,2560]{1,0:T(8,128)(2,1)S(1)} %collective-permute-done.11.refs_1_.refs_3_) | copy-start | bytes 3932164
  108.1 2.7 %collective-permute-start.12 = (bf16[512,1024]{1,0:T(8,128)(2,1)S(1)}, bf16[512,1024]{1,0:T(8,128)(2,1)S(1)}, u32[]{:S(2)}, u32[]{:S(2)}) collective-permute-start(bf16[512,1024]{1,0:T(8,128)(2,1)S(1)} %get-tuple-element.66.grad_ref.refs_4_), channel_id=1, source_target_pairs={{0,1},{1,0},{2,3},{3,2},{4,5},{5,4},{6,7},{7,6},{8,9},{9,8},{10,11... | collective-permute-start | bytes 3145736 | tf_op jit(solution)/shard_map/ppermute | solution.py:129
  118.3 0.9 copy-start.8
  119.2 0.8 copy-start.15
  119.9 6.8 %copy-start.13 = (bf16[4,2,16,1536]{3,2,1,0:T(8,128)(2,1)}, bf16[4,2,16,1536]{3,2,1,0:T(8,128)(2,1)S(1)}, u32[]{:S(2)}) copy-start(bf16[4,2,16,1536]{3,2,1,0:T(8,128)(2,1)S(1)} %get-tuple-element.63) | copy-start | bytes 1179652
  119.9 6.8 %copy-start.14 = (bf16[4,2,16,1536]{3,2,1,0:T(8,128)(2,1)}, bf16[4,2,16,1536]{3,2,1,0:T(8,128)(2,1)S(1)}, u32[]{:S(2)}) copy-start(bf16[4,2,16,1536]{3,2,1,0:T(8,128)(2,1)S(1)} %get-tuple-element.62) | copy-start | bytes 1179652
  126.8 18.5 %all-to-all-start.3 = ((bf16[4,4,2,16,1024]{4,3,2,1,0:T(8,128)(2,1)}), bf16[4,4,2,16,1024]{4,3,2,1,0:T(8,128)(2,1)S(1)}, u32[]{:S(2)}, u32[]{:S(2)}) async-start(bf16[4,4,2,16,1024]{4,3,2,1,0:T(8,128)(2,1)} %grad_hidden_partial.3), calls=%async_computation.3 | async-start | bytes 2097152 | tf_op jit(solution)/shard_map/all_to_all | solution.py:586
  130.3 32.8 %collective-permute-start.13 = (bf16[4,2,16,1536]{3,2,1,0:T(8,128)(2,1)}, bf16[4,2,16,1536]{3,2,1,0:T(8,128)(2,1)}, u32[]{:S(2)}, u32[]{:S(2)}) collective-permute-start(bf16[4,2,16,1536]{3,2,1,0:T(8,128)(2,1)} %copy-done.15), channel_id=1, source_target_pairs={{0,2},{1,3},{2,0},{3,1},{4,6},{5,7},{6,4},{7,5},{8,10},{9,11},{10,... | collective-permute-start | bytes 1179656 | tf_op jit(solution)/shard_map/ppermute | solution.py:129
  132.3 30.9 %collective-permute-start.14 = (bf16[4,2,16,1536]{3,2,1,0:T(8,128)(2,1)}, bf16[4,2,16,1536]{3,2,1,0:T(8,128)(2,1)}, u32[]{:S(2)}, u32[]{:S(2)}) collective-permute-start(bf16[4,2,16,1536]{3,2,1,0:T(8,128)(2,1)} %copy-done.14), channel_id=1, source_target_pairs={{0,4},{1,5},{2,6},{3,7},{4,0},{5,1},{6,2},{7,3},{8,12},{9,13},{10,... | collective-permute-start | bytes 1179656 | tf_op jit(solution)/shard_map/ppermute | solution.py:129
  133.8 29.4 %collective-permute-start.15 = (bf16[4,2,16,1536]{3,2,1,0:T(8,128)(2,1)}, bf16[4,2,16,1536]{3,2,1,0:T(8,128)(2,1)}, u32[]{:S(2)}, u32[]{:S(2)}) collective-permute-start(bf16[4,2,16,1536]{3,2,1,0:T(8,128)(2,1)} %copy-done.13), channel_id=1, source_target_pairs={{0,6},{1,7},{2,4},{3,5},{4,2},{5,3},{6,0},{7,1},{8,14},{9,15},{10,... | collective-permute-start | bytes 1179656 | tf_op jit(solution)/shard_map/ppermute | solution.py:129
  146.0 0.7 copy-start.7
  146.7 29.0 %all-to-all-start.4 = ((bf16[4,2,16,1024]{3,2,1,0:T(8,128)(2,1)}), bf16[4,2,16,1024]{3,2,1,0:T(8,128)(2,1)S(1)}, u32[]{:S(2)}, u32[]{:S(2)}) async-start(bf16[4,2,16,1024]{3,2,1,0:T(8,128)(2,1)} %copy-done.7), calls=%async_computation.4 | async-start | bytes 524288 | tf_op jit(solution)/shard_map/all_to_all | solution.py:635
  150.1 1.3 copy-start.2
  151.4 1.3 copy-start.4
  152.7 1.3 copy-start.6
  154.0 9.1 %copy-start.9 = (f32[4,2,16,1536]{3,2,1,0:T(8,128)S(1)}, f32[4,2,16,1536]{3,2,1,0:T(8,128)}, u32[]{:S(2)}) copy-start(f32[4,2,16,1536]{3,2,1,0:T(8,128)} %copy-done.8) | copy-start | bytes 2359300
  164.6 5.6 %collective-permute-start.16 = (bf16[2,16,1536]{2,1,0:T(8,128)(2,1)S(1)}, bf16[2,16,1536]{2,1,0:T(8,128)(2,1)S(1)}, u32[]{:S(2)}, u32[]{:S(2)}) collective-permute-start(bf16[2,16,1536]{2,1,0:T(8,128)(2,1)S(1)} %get-tuple-element.73), channel_id=1, source_target_pairs={{0,8},{1,9},{2,10},{3,11},{4,12},{5,13},{6,14},{7,15},{8,0},{9,1},... | collective-permute-start | bytes 294920 | tf_op jit(solution)/shard_map/ppermute | solution.py:129
  166.7 9.0 %collective-permute-start.17 = (bf16[2,16,1536]{2,1,0:T(8,128)(2,1)S(1)}, bf16[2,16,1536]{2,1,0:T(8,128)(2,1)S(1)}, u32[]{:S(2)}, u32[]{:S(2)}) collective-permute-start(bf16[2,16,1536]{2,1,0:T(8,128)(2,1)S(1)} %get-tuple-element.74), channel_id=1, source_target_pairs={{0,16},{1,17},{2,18},{3,19},{4,20},{5,21},{6,22},{7,23},{8,24},{9,... | collective-permute-start | bytes 294920 | tf_op jit(solution)/shard_map/ppermute | solution.py:129
  169.0 6.6 %collective-permute-start.18 = (bf16[2,16,1536]{2,1,0:T(8,128)(2,1)S(1)}, bf16[2,16,1536]{2,1,0:T(8,128)(2,1)S(1)}, u32[]{:S(2)}, u32[]{:S(2)}) collective-permute-start(bf16[2,16,1536]{2,1,0:T(8,128)(2,1)S(1)} %get-tuple-element.75), channel_id=1, source_target_pairs={{0,24},{1,25},{2,26},{3,27},{4,28},{5,29},{6,30},{7,31},{8,16},{9,... | collective-permute-start | bytes 294920 | tf_op jit(solution)/shard_map/ppermute | solution.py:129
  175.7 1.3 collective-permute-start.19

commit v5 on v4

--- a/solution.py
+++ b/solution.py
@@ -105,11 +105,13 @@
 CHIPS = 4
 GROUP = CORES * CHIPS
 SLOTS = 4
-VMEM_LIMIT = 30 * 1024 * 1024
-
-
-def kernel_params():
-    return pltpu.CompilerParams(vmem_limit_bytes=VMEM_LIMIT)
+LIGHT = pl.CostEstimate(flops=1, bytes_accessed=1, transcendentals=0)
+SMALL_VMEM = 24 * 1024 * 1024
+LARGE_VMEM = 56 * 1024 * 1024
+
+
+def kernel_params(limit=SMALL_VMEM):
+    return pltpu.CompilerParams(vmem_limit_bytes=limit)
 
 
 def vmem_spec():
@@ -173,18 +175,18 @@
             entropy_ref[...] = jnp.broadcast_to(entropy[:rows], entropy_ref.shape)
 
 
-def assemble(pieces, layer, rows, out_ref):
+def assemble(pieces, rows, out_ref):
     layers = out_ref.shape[0] // (GROUP * rows)
     for core, piece in enumerate(pieces):
         for chip in range(CHIPS):
             for i in range(layers):
-                block = (layer ^ i) * GROUP + core * CHIPS + chip
-                out_ref[pl.ds(pl.multiple_of(block * rows, rows), rows), :] = piece[
+                block = i * GROUP + core * CHIPS + chip
+                out_ref[pl.ds(block * rows, rows), :] = piece[
                     pl.ds((chip * layers + i) * rows, rows), :
                 ]
 
 
-def logits_kernel(rows, by_rank, first, last, pos_ref, *refs):
+def logits_kernel(rows, first, last, *refs):
     pieces, w_ref, refs = refs[:CORES], refs[CORES], refs[CORES + 1 :]
     if last:
         before_ref, prob_ref, logits_ref, stat_ref, hidden, tiles, sems, cross_ref = refs
@@ -203,7 +205,7 @@
     def _():
         for t in range(min(2, steps)):
             copy(t, t).start()
-        assemble(pieces, pos_ref[2] if by_rank else 0, rows, hidden)
+        assemble(pieces, rows, hidden)
 
     copy(step, step % 2).wait()
     part = jnp.dot(hidden[...], tiles[step % 2], preferred_element_type=jnp.float32)
@@ -281,23 +283,13 @@
         grad_ref[span, :] = (weight * (student - prob_ref[span, :])).astype(grad_ref.dtype)
 
 
-def partial_kernel(rows, first, steps, stacked, pos_ref, grad_ref, sib_ref, w_ref, sib_w_ref, *refs):
-    outs, (swapped, tiles, sems) = refs[:-3], refs[-3:]
-    tokens = grad_ref.shape[0]
-    layers = tokens // (GROUP * rows)
+def partial_kernel(rows, stacked, pos_ref, grad_ref, sib_ref, w_ref, sib_w_ref, *refs):
+    outs, swapped = refs[:-1], refs[-1]
+    layers = grad_ref.shape[0] // (GROUP * rows)
     half = CHIPS * rows
-    step = pl.program_id(0)
-    tile = tiles.shape[1]
-    start = pos_ref[0] * (w_ref.shape[0] // CORES) + first
-
-    def copy(t, slot):
-        row = pl.multiple_of(start + t * tile, 128)
-        return pltpu.make_async_copy(w_ref.at[pl.ds(row, tile), :], tiles.at[slot], sems.at[slot])
-
-    @pl.when(step == 0)
-    def _():
-        for t in range(min(2, steps)):
-            copy(t, t).start()
+
+    @pl.when(pl.program_id(0) == 0)
+    def _():
         for k in range(layers):
             for core in range(CORES):
                 swapped[pl.ds((k * CORES + core) * half, half), :] = sib_ref[
@@ -305,15 +297,9 @@
                 ]
 
     contract = (((1,), (1,)), ((), ()))
-    span = pl.ds(pl.multiple_of(first + step * tile, tile), tile)
-    total = lax.dot_general(swapped[...], sib_w_ref[span, :], contract, preferred_element_type=jnp.float32)
-    copy(step, step % 2).wait()
-    total += lax.dot_general(grad_ref[...], tiles[step % 2], contract, preferred_element_type=jnp.float32)
-
-    @pl.when(step + 2 < steps)
-    def _():
-        copy(step + 2, step % 2).start()
-
+    total = lax.dot_general(
+        grad_ref[...], w_ref[...], contract, preferred_element_type=jnp.float32
+    ) + lax.dot_general(swapped[...], sib_w_ref[...], contract, preferred_element_type=jnp.float32)
     for j in range(CHIPS):
         for k in range(layers):
             for core in range(CORES):
@@ -325,17 +311,17 @@
                     outs[j][k, core] = part.astype(outs[j].dtype)
 
 
-def head_kernel(rows, chunk_steps, pos_ref, *refs):
+def head_kernel(rows, chunk_steps, *refs):
     pieces, (grad_ref, out_ref, hidden) = refs[:-3], refs[-3:]
     chunk = pl.program_id(0) // chunk_steps
 
     @pl.when(chunk == 0)
     def _():
-        assemble(pieces[:CORES], 0, rows, hidden)
+        assemble(pieces[:CORES], rows, hidden)
 
     @pl.when(chunk == 1)
     def _():
-        assemble(pieces[CORES:], pos_ref[2], rows, hidden)
+        assemble(pieces[CORES:], rows, hidden)
 
     out_ref[...] = lax.dot_general(
         hidden[...], grad_ref[...], (((0,), (0,)), ((), ())), preferred_element_type=jnp.float32
@@ -447,20 +433,12 @@
     chunk = depth // 2
     column = hidden_states[:, :chunk]
     column = jnp.concatenate([column] + [shift(column, k * GROUP) for k in range(1, layers)], axis=0)
-    late_column = jnp.broadcast_to(hidden_states[None, :, chunk:], (layers, rows, chunk))
-    late_column = lax.all_to_all(
-        late_column.reshape(layers * rows, chunk),
-        "vocab",
-        split_axis=0,
-        concat_axis=0,
-        axis_index_groups=across,
-        tiled=True,
-    )
-    sib_w = shift(lax.dynamic_slice(head_weight, ((1 - core) * half, 0), (half, slab)), 1)
+    sib_w = shift(head_weight, 1)
+    late_column, column = lax.optimization_barrier((hidden_states[:, chunk:], column))
     plane = [column] + [shift(column, j * CORES) for j in range(1, CHIPS)]
-    arrived_blocks, arrived_stat, place = send_teacher(
-        teacher_logits, block_lists, slab // side, late_column
-    )
+    for k in [1 << i for i in range((layers - 1).bit_length())]:
+        late_column = jnp.concatenate([late_column, shift(late_column, k * GROUP)], axis=0)
+    arrived_blocks, arrived_stat, place = send_teacher(teacher_logits, block_lists, slab // side, column)
     late_column, plane[1], sib_w = lax.optimization_barrier((late_column, plane[1], sib_w))
     late_plane = [late_column] + [shift(late_column, j * CORES) for j in range(1, CHIPS)]
     plane = jnp.concatenate(plane, axis=0)
@@ -475,9 +453,7 @@
         in_specs=[smem_spec(), smem_spec()] + [vmem_spec()] * 4,
         out_specs=(vmem_spec(), vmem_spec()),
         compiler_params=kernel_params(),
-        cost_estimate=pl.CostEstimate(
-            flops=2 * tokens * side * side * SLOTS, bytes_accessed=4 * tokens * slab, transcendentals=0
-        ),
+        cost_estimate=LIGHT,
         name="teacher_prob",
     )(
         pos,
@@ -509,20 +485,16 @@
                 pl.BlockSpec((n, 2 * tokens // 128, 128), lambda t: (0, 0, 0)),
             ]
         return pl.pallas_call(
-            functools.partial(logits_kernel, rows, last, first, last),
+            functools.partial(logits_kernel, rows, first, last),
             grid=(slab // width,),
             out_shape=out_shape,
-            in_specs=[smem_spec()] + [vmem_spec()] * CORES + [hbm_spec()] + [tile_out] * (2 * last),
+            in_specs=[vmem_spec()] * CORES + [hbm_spec()] + [tile_out] * (2 * last),
             out_specs=out_specs,
             scratch_shapes=scratch,
-            compiler_params=kernel_params(),
-            cost_estimate=pl.CostEstimate(
-                flops=2 * tokens * chunk * slab,
-                bytes_accessed=2 * chunk * (slab + tokens) + 4 * tokens * slab,
-                transcendentals=tokens * slab if last else 0,
-            ),
+            compiler_params=kernel_params(LARGE_VMEM),
+            cost_estimate=LIGHT,
             name="logits",
-        )(pos, *pieces, head_weight, *((before, prob) if last else ()))
+        )(*pieces, head_weight, *((before, prob) if last else ()))
 
     (logits,) = logits_call(hidden, 0)
     late_plane, logits, prob = lax.optimization_barrier((late_plane, logits, prob))
@@ -540,9 +512,7 @@
         in_specs=[smem_spec()] + [vmem_spec()] * 5,
         out_specs=(vmem_spec(), vmem_spec()),
         compiler_params=kernel_params(),
-        cost_estimate=pl.CostEstimate(
-            flops=4 * tokens * slab, bytes_accessed=10 * tokens * slab, transcendentals=tokens * slab
-        ),
+        cost_estimate=LIGHT,
         name="grad_logits",
     )(pos, stat, logits, prob, token_weight.reshape(blocks, 1, side), entropy)
     sib_grad = shift(grad, 1)
@@ -558,31 +528,33 @@
             shapes = [(CHIPS, layers, CORES, rows)]
         else:
             shapes = [(layers, CORES, rows)] * CHIPS
+        w_block = pl.BlockSpec((tile, slab), lambda t, pos, first=first: (pos[0] * 5 + first // tile + t, 0))
         outs = pl.pallas_call(
-            functools.partial(partial_kernel, rows, first, size // tile, stacked),
-            grid=(size // tile,),
-            in_specs=[smem_spec(), vmem_spec(), vmem_spec(), hbm_spec(), vmem_spec()],
-            out_specs=[
-                pl.BlockSpec((*shape, tile), lambda t, count=len(shape): (0,) * count + (t,)) for shape in shapes
-            ],
+            functools.partial(partial_kernel, rows, stacked),
+            grid_spec=pltpu.PrefetchScalarGridSpec(
+                num_scalar_prefetch=1,
+                grid=(size // tile,),
+                in_specs=[pl.BlockSpec((tokens, slab), lambda t, pos: (0, 0))] * 2 + [w_block] * 2,
+                out_specs=[
+                    pl.BlockSpec((*shape, tile), lambda t, pos, count=len(shape): (0,) * count + (t,))
+                    for shape in shapes
+                ],
+                scratch_shapes=[pltpu.VMEM((tokens, slab), bf16)],
+            ),
             out_shape=[
                 jax.ShapeDtypeStruct((*shape, size), f32 if j == 0 and not stacked else bf16)
                 for j, shape in enumerate(shapes)
             ],
-            scratch_shapes=[
-                pltpu.VMEM((tokens, slab), bf16),
-                pltpu.VMEM((2, tile, slab), bf16),
-                pltpu.SemaphoreType.DMA((2,)),
-            ],
-            compiler_params=kernel_params(),
-            cost_estimate=pl.CostEstimate(
-                flops=4 * tokens * size * slab, bytes_accessed=4 * size * slab, transcendentals=0
-            ),
+            compiler_params=kernel_params(LARGE_VMEM),
+            cost_estimate=LIGHT,
             name="grad_hidden_partial",
         )(pos, late_grad, sib_grad, head_weight, later_sib_w)
-        *outs, late_grad, later_sib_w = lax.optimization_barrier((*outs, late_grad, later_sib_w))
+        if stacked:
+            outs, late_grad = lax.optimization_barrier((outs, late_grad))
+        else:
+            arrived = [shift(outs[j], j * CORES) for j in range(1, CHIPS)]
+            arrived[1], late_grad, later_sib_w = lax.optimization_barrier((arrived[1], late_grad, later_sib_w))
         partials.append(outs)
-    arrived = [shift(partials[0][j], j * CORES) for j in range(1, CHIPS)]
     late_arrived = lax.all_to_all(
         partials[1][0], "vocab", split_axis=0, concat_axis=0, axis_index_groups=in_layer, tiled=True
     )
@@ -595,16 +567,14 @@
     grad_head = pl.pallas_call(
         functools.partial(head_kernel, rows, 2),
         grid=(4,),
-        in_specs=[smem_spec()] + piece_specs + [vmem_spec()],
+        in_specs=piece_specs + [pl.BlockSpec((tokens, slab), whole)],
         out_specs=pl.BlockSpec((head_tile, slab), lambda t: (t, 0)),
         out_shape=jax.ShapeDtypeStruct((depth, slab), bf16),
         scratch_shapes=[pltpu.VMEM((tokens, head_tile), bf16)],
-        compiler_params=kernel_params(),
-        cost_estimate=pl.CostEstimate(
-            flops=2 * tokens * depth * slab, bytes_accessed=2 * depth * (slab + tokens), transcendentals=0
-        ),
+        compiler_params=kernel_params(LARGE_VMEM),
+        cost_estimate=LIGHT,
         name="grad_head",
-    )(pos, *hidden, *late_hidden, late_grad)
+    )(*hidden, *late_hidden, late_grad)
     arrived, grad_head = lax.optimization_barrier((arrived, grad_head))
 
     summed = pl.pallas_call(
@@ -615,9 +585,7 @@
             jax.ShapeDtypeStruct((CORES, rows, sizes[0]), f32 if k == 0 else bf16) for k in range(layers)
         ],
         compiler_params=kernel_params(),
-        cost_estimate=pl.CostEstimate(
-            flops=tokens * sizes[0], bytes_accessed=3 * tokens * sizes[0], transcendentals=0
-        ),
+        cost_estimate=LIGHT,
         name="chip_sum",
     )(partials[0][0], *arrived)
     arrived = [shift(summed[k], k * GROUP) for k in range(1, layers)]
@@ -627,9 +595,7 @@
         out_specs=vmem_spec(),
         out_shape=jax.ShapeDtypeStruct((layers, CORES, rows, sizes[1]), bf16),
         compiler_params=kernel_params(),
-        cost_estimate=pl.CostEstimate(
-            flops=tokens * sizes[1], bytes_accessed=3 * tokens * sizes[1], transcendentals=0
-        ),
+        cost_estimate=LIGHT,
         name="chip_sum",
     )(pos, late_arrived)
     late_arrived = lax.all_to_all(
@@ -641,9 +607,7 @@
         out_specs=[vmem_spec()] * 2,
         out_shape=[jax.ShapeDtypeStruct((rows, half), bf16)] * 2,
         compiler_params=kernel_params(),
-        cost_estimate=pl.CostEstimate(
-            flops=CORES * layers * rows * half, bytes_accessed=3 * CORES * layers * rows * half, transcendentals=0
-        ),
+        cost_estimate=LIGHT,
         name="last_sum",
     )(summed[0], *arrived, late_arrived)
     other = shift(theirs, 1)

time: 179 us -> 175 us (0.978)
  local copies, waits for them, and re-layouts: 27.7 us -> 9.38 us
  waiting for transfers between devices: 52.2 us -> 60.9 us
  Pallas kernels: 41.9 us -> 48.7 us
  starting transfers between devices: 38.4 us -> 35.8 us
    ppermute x20 -> x22, waiting for transfers between devices: 24.4 us -> 36.5 us  [shift(): return lax.ppermute(x, 'vocab', [(i, i ^ distance) for i in range(n)])]
    unnamed x64 -> x39, local copies, waits for them, and re-layouts: 15.3 us -> 6.5 us
    dynamic_slice x1 -> x0, local copies, waits for them, and re-layouts: 5.46 us -> none  [levels_plan(): lax.dynamic_slice(head_weight, ((1 - core) * half, 0), (half, slab))]
    pallas_call x4, Pallas kernels: 26.2 us -> 31.6 us  [the longest x2 17 us: logits_call(): pl.pallas_call(functools.partial(logits_kernel, rows, first, last), grid=...]
    all_to_all x1 -> x0, starting transfers between devices: 5.09 us -> none  [levels_plan(): lax.all_to_all(late_column.reshape(layers * rows, chunk), 'vocab', split_...]
    ppermute x20 -> x22, starting transfers between devices: 21.3 us -> 25.2 us  [shift(): return lax.ppermute(x, 'vocab', [(i, i ^ distance) for i in range(n)])]
    all_to_all x1, waiting for transfers between devices: 16.4 us -> 12.9 us  [send_teacher(): lax.all_to_all(payload, 'vocab', split_axis=0, concat_axis=0, tiled=True)]
    pallas_call x1, Pallas kernels: 9.12 us -> 11 us  [levels_plan(): pl.pallas_call(functools.partial(head_kernel, rows, 2), grid=(4,), in_spe...]
  transfers between devices with their start and end apart: 24 -> 25, of which waited for: 8 -> 13; matrix products, arithmetic and copies ran while one was open for 7% -> 6% of each run, Pallas kernels for 11% -> 13%
where the time goes in v5:
time: 175 us
  waiting for transfers between devices  60.9 us (35%)
  Pallas kernels  48.7 us (28%)
  starting transfers between devices  35.8 us (20%)
  blocking collectives  11.5 us (7%)
  local copies, waits for them, and re-layouts  9.38 us (5%)
  other arithmetic  5.79 us (3%)
    ppermute x22, waiting for transfers between devices, shift(): return lax.ppermute(x, 'vocab', [(i, i ^ distance) for i in range(n)])  36.5 us
    ppermute x22, starting transfers between devices, shift(): return lax.ppermute(x, 'vocab', [(i, i ^ distance) for i in range(n)])  25.2 us
    pallas_call x2, Pallas kernels, logits_call(): pl.pallas_call(functools.partial(logits_kernel, rows, first, last), grid=...  17 us
    pallas_call x2, Pallas kernels, levels_plan(): pl.pallas_call(functools.partial(partial_kernel, rows, stacked), grid_spe...  14.6 us
    all_to_all x1, waiting for transfers between devices, send_teacher(): lax.all_to_all(payload, 'vocab', split_axis=0, concat_axis=0, tiled=True)  12.9 us
    all_to_all x1, waiting for transfers between devices, levels_plan(): lax.all_to_all(partials[1][0], 'vocab', split_axis=0, concat_axis=0, axis...  11.6 us
    all_to_all x1, blocking collectives, levels_plan(): lax.all_to_all(stat, 'vocab', split_axis=0, concat_axis=0, tiled=True)  11.5 us
    pallas_call x1, Pallas kernels, levels_plan(): pl.pallas_call(functools.partial(head_kernel, rows, 2), grid=(4,), in_spe...  11 us
  transfers between devices with their start and end apart: 25, of which 13 were waited for; matrix products, arithmetic and copies ran while one was open for 6% of the time, Pallas kernels for 13%

profile of v5, /device:TPU:0, one launch (start us, length us, event | category | flops | bytes accessed | tf_op | source)
XLA Modules:
  0.0 174.5 jit_solution(7153014801413762496)
XLA Ops:
  0.6 0.5 collective-permute-start.6
  1.1 0.9 fusion.10
  2.1 4.7 %collective-permute-start.2 = (bf16[16,2560]{1,0:T(8,128)(2,1)S(1)}, bf16[16,2560]{1,0:T(8,128)(2,1)S(1)}, u32[]{:S(2)}, u32[]{:S(2)}) collective-permute-start(bf16[16,2560]{1,0:T(8,128)(2,1)S(1)} %get-tuple-element.81), channel_id=1, source_target_pairs={{0,24},{1,25},{2,26},{3,27},{4,28},{5,29},{6,30},{7,31},{8,16},{9,... | collective-permute-start | bytes 245768 | tf_op jit(solution)/shard_map/ppermute | solution.py:131
  6.8 0.6 collective-permute-start
  7.4 1.2 reduce_max.14
  8.6 0.7 add_select_fusion.1
  9.4 0.2 convert_reduce_fusion
  9.6 1.5 fusion.1
  11.1 1.4 convolution_convert_fusion
  12.5 1.8 %collective-permute-done.1 = bf16[16,2560]{1,0:T(8,128)(2,1)S(1)} collective-permute-done((bf16[16,2560]{1,0:T(8,128)(2,1)S(1)}, bf16[16,2560]{1,0:T(8,128)(2,1)S(1)}, u32[]{:S(2)}, u32[]{:S(2)}) %collective-permute-start.1) | collective-permute-done | bytes 81952 | tf_op jit(solution)/shard_map/ppermute | solution.py:131
  14.3 0.9 collective-permute-start.3
  15.4 0.4 copy.43
  15.9 2.5 %collective-permute-start.11 = (bf16[64,2560]{1,0:T(8,128)(2,1)S(1)}, bf16[64,2560]{1,0:T(8,128)(2,1)S(1)}, u32[]{:S(2)}, u32[]{:S(2)}) collective-permute-start(bf16[64,2560]{1,0:T(8,128)(2,1)S(1)} %pad_maximum_fusion.1), channel_id=1, source_target_pairs={{0,6},{1,7},{2,4},{3,5},{4,2},{5,3},{6,0},{7,1},{8,14},{9,15},{10,... | collective-permute-start | bytes 983048 | tf_op jit(solution)/shard_map/ppermute | solution.py:131
  18.4 0.5 collective-permute-start.10
  18.9 0.5 collective-permute-start.5
  19.4 2.2 %collective-permute-start.4 = (bf16[32,2560]{1,0:T(8,128)(2,1)S(1)}, bf16[32,2560]{1,0:T(8,128)(2,1)S(1)}, u32[]{:S(2)}, u32[]{:S(2)}) collective-permute-start(bf16[32,2560]{1,0:T(8,128)(2,1)S(1)} %pad_maximum_fusion.3), channel_id=1, source_target_pairs={{0,16},{1,17},{2,18},{3,19},{4,20},{5,21},{6,22},{7,23},{8,24},{9,... | collective-permute-start | bytes 491528 | tf_op jit(solution)/shard_map/ppermute | solution.py:131
  21.7 6.9 %collective-permute-done.4 = bf16[32,2560]{1,0:T(8,128)(2,1)S(1)} collective-permute-done((bf16[32,2560]{1,0:T(8,128)(2,1)S(1)}, bf16[32,2560]{1,0:T(8,128)(2,1)S(1)}, u32[]{:S(2)}, u32[]{:S(2)}) %collective-permute-start.4) | collective-permute-done | bytes 163872 | tf_op jit(solution)/shard_map/ppermute | solution.py:131
  28.6 4.4 %collective-permute-done.5 = bf16[64,2560]{1,0:T(8,128)(2,1)S(1)} collective-permute-done((bf16[64,2560]{1,0:T(8,128)(2,1)S(1)}, bf16[64,2560]{1,0:T(8,128)(2,1)S(1)}, u32[]{:S(2)}, u32[]{:S(2)}) %collective-permute-start.5) | collective-permute-done | bytes 327712 | tf_op jit(solution)/shard_map/ppermute | solution.py:131
  33.2 1.0 pad_maximum_fusion
  34.2 3.6 %all-to-all-start = ((bf16[32,65,128]{2,1,0:T(8,128)(2,1)}), bf16[32,65,128]{2,1,0:T(8,128)(2,1)S(1)}, u32[]{:S(2)}, u32[]{:S(2)}) async-start(bf16[32,65,128]{2,1,0:T(8,128)(2,1)} %pad_maximum_fusion), calls=%async_computation | async-start | bytes 1179648 | tf_op jit(solution)/shard_map/all_to_all | solution.py:395
  37.9 0.2 select_reduce_fusion
  38.1 2.7 %collective-permute-start.9 = (bf16[64,2560]{1,0:T(8,128)(2,1)S(1)}, bf16[64,2560]{1,0:T(8,128)(2,1)S(1)}, u32[]{:S(2)}, u32[]{:S(2)}) collective-permute-start(bf16[64,2560]{1,0:T(8,128)(2,1)S(1)} %pad_maximum_fusion.2), channel_id=1, source_target_pairs={{0,6},{1,7},{2,4},{3,5},{4,2},{5,3},{6,0},{7,1},{8,14},{9,15},{10,... | collective-permute-start | bytes 983048 | tf_op jit(solution)/shard_map/ppermute | solution.py:131
  40.8 0.6 collective-permute-start.8
  41.4 0.3 collective-permute-start.7
  41.7 12.9 %all-to-all-done = bf16[32,65,128]{2,1,0:T(8,128)(2,1)S(1)} async-done(((bf16[32,65,128]{2,1,0:T(8,128)(2,1)}), bf16[32,65,128]{2,1,0:T(8,128)(2,1)S(1)}, u32[]{:S(2)}, u32[]{:S(2)}) %all-to-all-start) | async-done | bytes 532512 | tf_op jit(solution)/shard_map/all_to_all | solution.py:395
  54.7 0.3 copy.52
  55.1 0.3 copy.46
  55.5 0.1 copy.49
  55.6 0.1 reshape.196
  55.8 3.0 %teacher_prob.1 = (f32[512,1024]{1,0:T(8,128)S(1)}, f32[16,128]{1,0:T(8,128)S(1)}) custom-call(s32[4]{0:T(128)S(1)} %pad_add_fusion.refs_0_.pos_ref, s32[4,4]{1,0:T(4,128)S(1)} %broadcast_add_fusion.refs_1_, bf16[4,4,128,128]{3,2,1,0:T(8,128)(2,1)S(1)} %bitcast.29, f32[2,4,1,128]{3,2,1,0:T(1,128)S(1)} %bitcast.30, s32[4,1,128]{2,1,0:T(1,128)S(1)} %bitcast.31, ...), custom_call_target="tpu_custom_call" | custom-call | flops 1 | bytes 1 | tf_op jit(solution)/shard_map/teacher_prob/pallas_call | solution.py:447
  58.8 1.4 copy-done.1
  60.2 7.5 %logits.2.refs_3_ = f32[512,1024]{1,0:T(8,128)} custom-call(bf16[256,2560]{1,0:T(8,128)(2,1)} %copy-done.11, bf16[256,2560]{1,0:T(8,128)(2,1)} %collective-permute-done.12.refs_1_, bf16[5120,1024]{1,0:T(8,128)(2,1)} %w_ref.3), custom_call_target="tpu_custom_call" | custom-call | flops 1 | bytes 1 | tf_op jit(solution)/shard_map/logits/pallas_call | solution.py:487
  67.8 1.0 constant_dynamic-update-slice_fusion.6
  69.0 3.0 %collective-permute-done.13.refs_1_.refs_3_ = bf16[256,2560]{1,0:T(8,128)(2,1)S(1)} collective-permute-done((bf16[256,2560]{1,0:T(8,128)(2,1)S(1)}, bf16[256,2560]{1,0:T(8,128)(2,1)S(1)}, u32[]{:S(2)}, u32[]{:S(2)}) %collective-permute-start.13) | collective-permute-done | bytes 1310752 | tf_op jit(solution)/shard_map/ppermute | solution.py:131
  72.0 1.1 copy-done.12
  73.1 9.5 %logits.3 = (f32[512,1024]{1,0:T(8,128)}, f32[32,8,128]{2,1,0:T(8,128)}) custom-call(bf16[256,2560]{1,0:T(8,128)(2,1)} %copy-done.10, bf16[256,2560]{1,0:T(8,128)(2,1)} %copy-done.12, bf16[5120,1024]{1,0:T(8,128)(2,1)} %w_ref.3, f32[512,1024]{1,0:T(8,128)} %logits.2.refs_3_, f32[512,1024]{1,0:T(8,128)} %copy-done.1), custom_call_target="tpu_custom_call" | custom-call | flops 1 | bytes 1 | tf_op jit(solution)/shard_map/logits/pallas_call | solution.py:487
  82.6 11.5 %all_to_all.20.refs_1_ = f32[32,8,128]{2,1,0:T(8,128)S(1)} all-to-all(f32[32,8,128]{2,1,0:T(8,128)} %get-tuple-element.52), channel_id=1, replica_groups=mesh['vocab'=32] {'vocab'}, dimensions={0} | all-to-all | bytes 262144 | tf_op jit(solution)/shard_map/all_to_all | solution.py:504
  94.1 1.6 copy-done.3
  95.7 1.3 grad_logits.1
  97.0 0.3 collective-permute-start.14
  97.3 2.4 %collective-permute-done.14.sib_ref = bf16[512,1024]{1,0:T(8,128)(2,1)S(1)} collective-permute-done((bf16[512,1024]{1,0:T(8,128)(2,1)S(1)}, bf16[512,1024]{1,0:T(8,128)(2,1)S(1)}, u32[]{:S(2)}, u32[]{:S(2)}) %collective-permute-start.14) | collective-permute-done | bytes 1048608 | tf_op jit(solution)/shard_map/ppermute | solution.py:131
  99.7 1.0 copy-done.13
  100.7 8.2 %grad_hidden_partial.2 = (f32[4,2,16,1536]{3,2,1,0:T(8,128)}, bf16[4,2,16,1536]{3,2,1,0:T(8,128)(2,1)}, bf16[4,2,16,1536]{3,2,1,0:T(8,128)(2,1)}, bf16[4,2,16,1536]{3,2,1,0:T(8,128)(2,1)}) custom-call(s32[4]{0:T(128)} %copy-done.5, bf16[512,1024]{1,0:T(8,128)(2,1)} %copy-done, bf16[512,1024]{1,0:T(8,128)(2,1)} %copy-done.13, bf16[5120,1024]{1,0:T(8,128)(2,1)} %w_ref.3, ...), custom_call_target="tpu_custom_call" | custom-call | flops 1 | bytes 1 | tf_op jit(solution)/shard_map/grad_hidden_partial/pallas_call | solution.py:532
  108.9 0.7 collective-permute-start.16
  109.5 10.8 %collective-permute-done.16.refs_1_ = bf16[4,2,16,1536]{3,2,1,0:T(8,128)(2,1)S(1)} collective-permute-done((bf16[4,2,16,1536]{3,2,1,0:T(8,128)(2,1)}, bf16[4,2,16,1536]{3,2,1,0:T(8,128)(2,1)S(1)}, u32[]{:S(2)}, u32[]{:S(2)}) %collective-permute-start.16) | collective-permute-done | bytes 393248 | tf_op jit(solution)/shard_map/ppermute | solution.py:131
  120.3 6.4 %grad_hidden_partial.3 = bf16[4,4,2,16,1024]{4,3,2,1,0:T(8,128)(2,1)} custom-call(s32[4]{0:T(128)} %copy-done.5, bf16[512,1024]{1,0:T(8,128)(2,1)} %copy-done, bf16[512,1024]{1,0:T(8,128)(2,1)} %copy-done.13, bf16[5120,1024]{1,0:T(8,128)(2,1)} %w_ref.3, bf16[5120,1024]{1,0:T(8,128)(2,1)} %collective-permute-done.6.sib_w_ref), custom_call_target="tpu_custom_call" | custom-call | flops 1 | bytes 1 | tf_op jit(solution)/shard_map/grad_hidden_partial/pallas_call | solution.py:532
  126.8 3.7 %all-to-all-start.2 = ((bf16[4,4,2,16,1024]{4,3,2,1,0:T(8,128)(2,1)}), bf16[4,4,2,16,1024]{4,3,2,1,0:T(8,128)(2,1)S(1)}, u32[]{:S(2)}, u32[]{:S(2)}) async-start(bf16[4,4,2,16,1024]{4,3,2,1,0:T(8,128)(2,1)} %grad_hidden_partial.3), calls=%async_computation.2 | async-start | bytes 2097152 | tf_op jit(solution)/shard_map/all_to_all | solution.py:558
  130.4 2.0 %collective-permute-start.15 = (bf16[4,2,16,1536]{3,2,1,0:T(8,128)(2,1)S(1)}, bf16[4,2,16,1536]{3,2,1,0:T(8,128)(2,1)S(1)}, u32[]{:S(2)}, u32[]{:S(2)}) collective-permute-start(bf16[4,2,16,1536]{3,2,1,0:T(8,128)(2,1)S(1)} %copy-done.15), channel_id=1, source_target_pairs={{0,2},{1,3},{2,0},{3,1},{4,6},{5,7},{6,4},{7,5},{8,10},{9,11},{10,... | collective-permute-start | bytes 1179656 | tf_op jit(solution)/shard_map/ppermute | solution.py:131
  132.4 1.5 collective-permute-start.17
  133.9 11.6 %all-to-all-done.2.parts_ref = bf16[4,4,2,16,1024]{4,3,2,1,0:T(8,128)(2,1)S(1)} async-done(((bf16[4,4,2,16,1024]{4,3,2,1,0:T(8,128)(2,1)}), bf16[4,4,2,16,1024]{4,3,2,1,0:T(8,128)(2,1)S(1)}, u32[]{:S(2)}, u32[]{:S(2)}) %all-to-all-start.2) | async-done | bytes 1048608 | tf_op jit(solution)/shard_map/all_to_all | solution.py:558
  145.5 1.4 chip_sum.3
  146.8 3.4 %all-to-all-start.3 = ((bf16[4,2,16,1024]{3,2,1,0:T(8,128)(2,1)}), bf16[4,2,16,1024]{3,2,1,0:T(8,128)(2,1)S(1)}, u32[]{:S(2)}, u32[]{:S(2)}) async-start(bf16[4,2,16,1024]{3,2,1,0:T(8,128)(2,1)} %chip_sum.3), calls=%async_computation.3 | async-start | bytes 524288 | tf_op jit(solution)/shard_map/all_to_all | solution.py:601
  150.2 11.0 %grad_head.1 = bf16[5120,1024]{1,0:T(8,128)(2,1)} custom-call(bf16[256,2560]{1,0:T(8,128)(2,1)} %copy-done.11, bf16[256,2560]{1,0:T(8,128)(2,1)} %collective-permute-done.12.refs_1_, bf16[256,2560]{1,0:T(8,128)(2,1)} %copy-done.10, bf16[256,2560]{1,0:T(8,128)(2,1)} %copy-done.12, bf16[512,1024]{1,0:T(8,128)(2,1)} %copy-done), custom_call_target="tpu_custom_call" | custom-call | flops 1 | bytes 1 | tf_op jit(solution)/shard_map/grad_head/pallas_call | solution.py:567
  161.3 0.3 collective-permute-done.17.refs_2_
  161.6 0.2 chip_sum.2
  161.8 1.7 collective-permute-start.18
  163.5 2.4 %collective-permute-start.19 = (bf16[2,16,1536]{2,1,0:T(8,128)(2,1)S(1)}, bf16[2,16,1536]{2,1,0:T(8,128)(2,1)S(1)}, u32[]{:S(2)}, u32[]{:S(2)}) collective-permute-start(bf16[2,16,1536]{2,1,0:T(8,128)(2,1)S(1)} %get-tuple-element.72), channel_id=1, source_target_pairs={{0,16},{1,17},{2,18},{3,19},{4,20},{5,21},{6,22},{7,23},{8,24},{9,... | collective-permute-start | bytes 294920 | tf_op jit(solution)/shard_map/ppermute | solution.py:131
  165.9 0.4 collective-permute-start.20
  166.3 0.2 collective-permute-done.18.refs_0_
  166.5 3.8 %collective-permute-done.19.refs_1_ = bf16[2,16,1536]{2,1,0:T(8,128)(2,1)S(1)} collective-permute-done((bf16[2,16,1536]{2,1,0:T(8,128)(2,1)S(1)}, bf16[2,16,1536]{2,1,0:T(8,128)(2,1)S(1)}, u32[]{:S(2)}, u32[]{:S(2)}) %collective-permute-start.19) | collective-permute-done | bytes 98336 | tf_op jit(solution)/shard_map/ppermute | solution.py:131
  170.3 2.1 %collective-permute-done.20.refs_2_ = bf16[2,16,1536]{2,1,0:T(8,128)(2,1)S(1)} collective-permute-done((bf16[2,16,1536]{2,1,0:T(8,128)(2,1)S(1)}, bf16[2,16,1536]{2,1,0:T(8,128)(2,1)S(1)}, u32[]{:S(2)}, u32[]{:S(2)}) %collective-permute-start.20) | collective-permute-done | bytes 98336 | tf_op jit(solution)/shard_map/ppermute | solution.py:131
  172.6 0.6 slice_reduce_fusion
  173.2 0.6 collective-permute-done.21
  173.9 0.7 pad_maximum_fusion.4
  (75 shorter events, 1.2 us)
Async XLA Ops:
  0.6 32.4 %collective-permute-start.6 = (bf16[5120,1024]{1,0:T(8,128)(2,1)}, bf16[5120,1024]{1,0:T(8,128)(2,1)}, u32[]{:S(2)}, u32[]{:S(2)}) collective-permute-start(bf16[5120,1024]{1,0:T(8,128)(2,1)} %w_ref.3), channel_id=1, source_target_pairs={{0,1},{1,0},{2,3},{3,2},{4,5},{5,4},{6,7},{7,6},{8,9},{9,8},{10,11... | collective-permute-start | bytes 31457288 | tf_op jit(solution)/shard_map/ppermute | solution.py:131
  2.1 10.4 %collective-permute-start.2 = (bf16[16,2560]{1,0:T(8,128)(2,1)S(1)}, bf16[16,2560]{1,0:T(8,128)(2,1)S(1)}, u32[]{:S(2)}, u32[]{:S(2)}) collective-permute-start(bf16[16,2560]{1,0:T(8,128)(2,1)S(1)} %get-tuple-element.81), channel_id=1, source_target_pairs={{0,24},{1,25},{2,26},{3,27},{4,28},{5,29},{6,30},{7,31},{8,16},{9,... | collective-permute-start | bytes 245768 | tf_op jit(solution)/shard_map/ppermute | solution.py:131
  6.8 7.5 %collective-permute-start.1 = (bf16[16,2560]{1,0:T(8,128)(2,1)S(1)}, bf16[16,2560]{1,0:T(8,128)(2,1)S(1)}, u32[]{:S(2)}, u32[]{:S(2)}) collective-permute-start(bf16[16,2560]{1,0:T(8,128)(2,1)S(1)} %get-tuple-element.81), channel_id=1, source_target_pairs={{0,16},{1,17},{2,18},{3,19},{4,20},{5,21},{6,22},{7,23},{8,24},{9,... | collective-permute-start | bytes 245768 | tf_op jit(solution)/shard_map/ppermute | solution.py:131
  6.8 7.5 %collective-permute-start = (bf16[16,2560]{1,0:T(8,128)(2,1)S(1)}, bf16[16,2560]{1,0:T(8,128)(2,1)S(1)}, u32[]{:S(2)}, u32[]{:S(2)}) collective-permute-start(bf16[16,2560]{1,0:T(8,128)(2,1)S(1)} %get-tuple-element.81), channel_id=1, source_target_pairs={{0,8},{1,9},{2,10},{3,11},{4,12},{5,13},{6,14},{7,15},{8,0},{9,1},... | collective-permute-start | bytes 245768 | tf_op jit(solution)/shard_map/ppermute | solution.py:131
  14.3 5.1 %collective-permute-start.3 = (bf16[16,2560]{1,0:T(8,128)(2,1)S(1)}, bf16[16,2560]{1,0:T(8,128)(2,1)S(1)}, u32[]{:S(2)}, u32[]{:S(2)}) collective-permute-start(bf16[16,2560]{1,0:T(8,128)(2,1)S(1)} %get-tuple-element.40), channel_id=1, source_target_pairs={{0,8},{1,9},{2,10},{3,11},{4,12},{5,13},{6,14},{7,15},{8,0},{9,1},... | collective-permute-start | bytes 245768 | tf_op jit(solution)/shard_map/ppermute | solution.py:131
  15.9 17.2 %collective-permute-start.11 = (bf16[64,2560]{1,0:T(8,128)(2,1)S(1)}, bf16[64,2560]{1,0:T(8,128)(2,1)S(1)}, u32[]{:S(2)}, u32[]{:S(2)}) collective-permute-start(bf16[64,2560]{1,0:T(8,128)(2,1)S(1)} %pad_maximum_fusion.1), channel_id=1, source_target_pairs={{0,6},{1,7},{2,4},{3,5},{4,2},{5,3},{6,0},{7,1},{8,14},{9,15},{10,... | collective-permute-start | bytes 983048 | tf_op jit(solution)/shard_map/ppermute | solution.py:131
  18.4 14.7 %collective-permute-start.10 = (bf16[64,2560]{1,0:T(8,128)(2,1)S(1)}, bf16[64,2560]{1,0:T(8,128)(2,1)S(1)}, u32[]{:S(2)}, u32[]{:S(2)}) collective-permute-start(bf16[64,2560]{1,0:T(8,128)(2,1)S(1)} %pad_maximum_fusion.1), channel_id=1, source_target_pairs={{0,4},{1,5},{2,6},{3,7},{4,0},{5,1},{6,2},{7,3},{8,12},{9,13},{10,... | collective-permute-start | bytes 983048 | tf_op jit(solution)/shard_map/ppermute | solution.py:131
  18.9 14.1 %collective-permute-start.5 = (bf16[64,2560]{1,0:T(8,128)(2,1)S(1)}, bf16[64,2560]{1,0:T(8,128)(2,1)S(1)}, u32[]{:S(2)}, u32[]{:S(2)}) collective-permute-start(bf16[64,2560]{1,0:T(8,128)(2,1)S(1)} %pad_maximum_fusion.1), channel_id=1, source_target_pairs={{0,2},{1,3},{2,0},{3,1},{4,6},{5,7},{6,4},{7,5},{8,10},{9,11},{10,... | collective-permute-start | bytes 983048 | tf_op jit(solution)/shard_map/ppermute | solution.py:131
  19.4 9.2 %collective-permute-start.4 = (bf16[32,2560]{1,0:T(8,128)(2,1)S(1)}, bf16[32,2560]{1,0:T(8,128)(2,1)S(1)}, u32[]{:S(2)}, u32[]{:S(2)}) collective-permute-start(bf16[32,2560]{1,0:T(8,128)(2,1)S(1)} %pad_maximum_fusion.3), channel_id=1, source_target_pairs={{0,16},{1,17},{2,18},{3,19},{4,20},{5,21},{6,22},{7,23},{8,24},{9,... | collective-permute-start | bytes 491528 | tf_op jit(solution)/shard_map/ppermute | solution.py:131
  33.1 21.6 %copy-start.11 = (bf16[256,2560]{1,0:T(8,128)(2,1)}, bf16[256,2560]{1,0:T(8,128)(2,1)S(1)}, u32[]{:S(2)}) copy-start(bf16[256,2560]{1,0:T(8,128)(2,1)S(1)} %constant_dynamic-update-slice_fusion.refs_0_) | copy-start | bytes 3932164
  33.1 27.1 %collective-permute-start.12 = (bf16[256,2560]{1,0:T(8,128)(2,1)S(1)}, bf16[256,2560]{1,0:T(8,128)(2,1)}, u32[]{:S(2)}, u32[]{:S(2)}) collective-permute-start(bf16[256,2560]{1,0:T(8,128)(2,1)S(1)} %constant_dynamic-update-slice_fusion.refs_0_), channel_id=1, source_target_pairs={{0,1},{1,0},{2,3},{3,2},{4,5},{5,4},{6,7},{7,6},{8,9},{9,8},{10,11... | collective-permute-start | bytes 3932168 | tf_op jit(solution)/shard_map/ppermute | solution.py:131
  34.2 20.4 %all-to-all-start = ((bf16[32,65,128]{2,1,0:T(8,128)(2,1)}), bf16[32,65,128]{2,1,0:T(8,128)(2,1)S(1)}, u32[]{:S(2)}, u32[]{:S(2)}) async-start(bf16[32,65,128]{2,1,0:T(8,128)(2,1)} %pad_maximum_fusion), calls=%async_computation | async-start | bytes 1179648 | tf_op jit(solution)/shard_map/all_to_all | solution.py:395
  38.1 29.6 %collective-permute-start.9 = (bf16[64,2560]{1,0:T(8,128)(2,1)S(1)}, bf16[64,2560]{1,0:T(8,128)(2,1)S(1)}, u32[]{:S(2)}, u32[]{:S(2)}) collective-permute-start(bf16[64,2560]{1,0:T(8,128)(2,1)S(1)} %pad_maximum_fusion.2), channel_id=1, source_target_pairs={{0,6},{1,7},{2,4},{3,5},{4,2},{5,3},{6,0},{7,1},{8,14},{9,15},{10,... | collective-permute-start | bytes 983048 | tf_op jit(solution)/shard_map/ppermute | solution.py:131
  40.8 26.9 %collective-permute-start.8 = (bf16[64,2560]{1,0:T(8,128)(2,1)S(1)}, bf16[64,2560]{1,0:T(8,128)(2,1)S(1)}, u32[]{:S(2)}, u32[]{:S(2)}) collective-permute-start(bf16[64,2560]{1,0:T(8,128)(2,1)S(1)} %pad_maximum_fusion.2), channel_id=1, source_target_pairs={{0,4},{1,5},{2,6},{3,7},{4,0},{5,1},{6,2},{7,3},{8,12},{9,13},{10,... | collective-permute-start | bytes 983048 | tf_op jit(solution)/shard_map/ppermute | solution.py:131
  41.4 26.4 %collective-permute-start.7 = (bf16[64,2560]{1,0:T(8,128)(2,1)S(1)}, bf16[64,2560]{1,0:T(8,128)(2,1)}, u32[]{:S(2)}, u32[]{:S(2)}) collective-permute-start(bf16[64,2560]{1,0:T(8,128)(2,1)S(1)} %pad_maximum_fusion.2), channel_id=1, source_target_pairs={{0,2},{1,3},{2,0},{3,1},{4,6},{5,7},{6,4},{7,5},{8,10},{9,11},{10,... | collective-permute-start | bytes 983048 | tf_op jit(solution)/shard_map/ppermute | solution.py:131
  41.7 52.3 %copy-start.5 = (s32[4]{0:T(128)}, s32[4]{0:T(128)S(1)}, u32[]{:S(2)}) copy-start(s32[4]{0:T(128)S(1)} %pad_add_fusion.refs_0_.pos_ref) | copy-start | bytes 52
  54.7 1.1 copy-start.7
  54.7 1.1 copy-start.8
  58.8 1.4 copy-start.1
  68.9 3.1 %copy-start.10 = (bf16[256,2560]{1,0:T(8,128)(2,1)}, bf16[256,2560]{1,0:T(8,128)(2,1)S(1)}, u32[]{:S(2)}) copy-start(bf16[256,2560]{1,0:T(8,128)(2,1)S(1)} %constant_dynamic-update-slice_fusion.4.refs_0_.refs_2_) | copy-start | bytes 3932164
  68.9 25.2 %copy-start.9 = (f32[512]{0:T(512)S(1)}, f32[512]{0:T(512)}, u32[]{:S(2)}) copy-start(f32[512]{0:T(512)} %param.13) | copy-start | bytes 6148
  68.9 3.1 %collective-permute-start.13 = (bf16[256,2560]{1,0:T(8,128)(2,1)S(1)}, bf16[256,2560]{1,0:T(8,128)(2,1)S(1)}, u32[]{:S(2)}, u32[]{:S(2)}) collective-permute-start(bf16[256,2560]{1,0:T(8,128)(2,1)S(1)} %constant_dynamic-update-slice_fusion.4.refs_0_.refs_2_), channel_id=1, source_target_pairs={{0,1},{1,0},{2,3},{3,2},{4,5},{5,4},{6,7},{7,6},{8,9},{9,8},{10,11... | collective-permute-start | bytes 3932168 | tf_op jit(solution)/shard_map/ppermute | solution.py:131
  72.0 1.1 copy-start.12
  73.1 21.0 %copy-start.2 = (f32[512,1024]{1,0:T(8,128)S(1)}, f32[512,1024]{1,0:T(8,128)}, u32[]{:S(2)}) copy-start(f32[512,1024]{1,0:T(8,128)} %copy-done.1) | copy-start | bytes 6291460
  94.1 1.6 copy-start.3
  97.0 2.7 %copy-start = (bf16[512,1024]{1,0:T(8,128)(2,1)}, bf16[512,1024]{1,0:T(8,128)(2,1)S(1)}, u32[]{:S(2)}) copy-start(bf16[512,1024]{1,0:T(8,128)(2,1)S(1)} %get-tuple-element.64.grad_ref.refs_4_) | copy-start | bytes 3145732
  97.0 2.7 %collective-permute-start.14 = (bf16[512,1024]{1,0:T(8,128)(2,1)S(1)}, bf16[512,1024]{1,0:T(8,128)(2,1)S(1)}, u32[]{:S(2)}, u32[]{:S(2)}) collective-permute-start(bf16[512,1024]{1,0:T(8,128)(2,1)S(1)} %get-tuple-element.64.grad_ref.refs_4_), channel_id=1, source_target_pairs={{0,1},{1,0},{2,3},{3,2},{4,5},{5,4},{6,7},{7,6},{8,9},{9,8},{10,11... | collective-permute-start | bytes 3145736 | tf_op jit(solution)/shard_map/ppermute | solution.py:131
  99.7 1.0 copy-start.13
  108.9 11.4 %collective-permute-start.16 = (bf16[4,2,16,1536]{3,2,1,0:T(8,128)(2,1)}, bf16[4,2,16,1536]{3,2,1,0:T(8,128)(2,1)S(1)}, u32[]{:S(2)}, u32[]{:S(2)}) collective-permute-start(bf16[4,2,16,1536]{3,2,1,0:T(8,128)(2,1)} %get-tuple-element.59), channel_id=1, source_target_pairs={{0,4},{1,5},{2,6},{3,7},{4,0},{5,1},{6,2},{7,3},{8,12},{9,13},{10,... | collective-permute-start | bytes 1179656 | tf_op jit(solution)/shard_map/ppermute | solution.py:131
  126.7 3.7 %copy-start.15 = (bf16[4,2,16,1536]{3,2,1,0:T(8,128)(2,1)S(1)}, bf16[4,2,16,1536]{3,2,1,0:T(8,128)(2,1)}, u32[]{:S(2)}) copy-start(bf16[4,2,16,1536]{3,2,1,0:T(8,128)(2,1)} %get-tuple-element.58) | copy-start | bytes 1179652
  126.7 5.7 %copy-start.14 = (bf16[4,2,16,1536]{3,2,1,0:T(8,128)(2,1)S(1)}, bf16[4,2,16,1536]{3,2,1,0:T(8,128)(2,1)}, u32[]{:S(2)}) copy-start(bf16[4,2,16,1536]{3,2,1,0:T(8,128)(2,1)} %get-tuple-element.61) | copy-start | bytes 1179652
  126.7 18.7 %copy-start.6 = (s32[4]{0:T(128)S(1)}, s32[4]{0:T(128)}, u32[]{:S(2)}) copy-start(s32[4]{0:T(128)} %copy-done.5) | copy-start | bytes 52
  126.8 18.7 %all-to-all-start.2 = ((bf16[4,4,2,16,1024]{4,3,2,1,0:T(8,128)(2,1)}), bf16[4,4,2,16,1024]{4,3,2,1,0:T(8,128)(2,1)S(1)}, u32[]{:S(2)}, u32[]{:S(2)}) async-start(bf16[4,4,2,16,1024]{4,3,2,1,0:T(8,128)(2,1)} %grad_hidden_partial.3), calls=%async_computation.2 | async-start | bytes 2097152 | tf_op jit(solution)/shard_map/all_to_all | solution.py:558
  130.4 30.9 %collective-permute-start.15 = (bf16[4,2,16,1536]{3,2,1,0:T(8,128)(2,1)S(1)}, bf16[4,2,16,1536]{3,2,1,0:T(8,128)(2,1)S(1)}, u32[]{:S(2)}, u32[]{:S(2)}) collective-permute-start(bf16[4,2,16,1536]{3,2,1,0:T(8,128)(2,1)S(1)} %copy-done.15), channel_id=1, source_target_pairs={{0,2},{1,3},{2,0},{3,1},{4,6},{5,7},{6,4},{7,5},{8,10},{9,11},{10,... | collective-permute-start | bytes 1179656 | tf_op jit(solution)/shard_map/ppermute | solution.py:131
  132.4 29.2 %collective-permute-start.17 = (bf16[4,2,16,1536]{3,2,1,0:T(8,128)(2,1)S(1)}, bf16[4,2,16,1536]{3,2,1,0:T(8,128)(2,1)S(1)}, u32[]{:S(2)}, u32[]{:S(2)}) collective-permute-start(bf16[4,2,16,1536]{3,2,1,0:T(8,128)(2,1)S(1)} %copy-done.14), channel_id=1, source_target_pairs={{0,6},{1,7},{2,4},{3,5},{4,2},{5,3},{6,0},{7,1},{8,14},{9,15},{10,... | collective-permute-start | bytes 1179656 | tf_op jit(solution)/shard_map/ppermute | solution.py:131
  146.8 25.6 %all-to-all-start.3 = ((bf16[4,2,16,1024]{3,2,1,0:T(8,128)(2,1)}), bf16[4,2,16,1024]{3,2,1,0:T(8,128)(2,1)S(1)}, u32[]{:S(2)}, u32[]{:S(2)}) async-start(bf16[4,2,16,1024]{3,2,1,0:T(8,128)(2,1)} %chip_sum.3), calls=%async_computation.3 | async-start | bytes 524288 | tf_op jit(solution)/shard_map/all_to_all | solution.py:601
  150.2 11.4 %copy-start.4 = (f32[4,2,16,1536]{3,2,1,0:T(8,128)S(1)}, f32[4,2,16,1536]{3,2,1,0:T(8,128)}, u32[]{:S(2)}) copy-start(f32[4,2,16,1536]{3,2,1,0:T(8,128)} %get-tuple-element.66.own_ref) | copy-start | bytes 2359300
  161.8 4.7 %collective-permute-start.18 = (bf16[2,16,1536]{2,1,0:T(8,128)(2,1)S(1)}, bf16[2,16,1536]{2,1,0:T(8,128)(2,1)S(1)}, u32[]{:S(2)}, u32[]{:S(2)}) collective-permute-start(bf16[2,16,1536]{2,1,0:T(8,128)(2,1)S(1)} %get-tuple-element.71), channel_id=1, source_target_pairs={{0,8},{1,9},{2,10},{3,11},{4,12},{5,13},{6,14},{7,15},{8,0},{9,1},... | collective-permute-start | bytes 294920 | tf_op jit(solution)/shard_map/ppermute | solution.py:131
  163.5 6.8 %collective-permute-start.19 = (bf16[2,16,1536]{2,1,0:T(8,128)(2,1)S(1)}, bf16[2,16,1536]{2,1,0:T(8,128)(2,1)S(1)}, u32[]{:S(2)}, u32[]{:S(2)}) collective-permute-start(bf16[2,16,1536]{2,1,0:T(8,128)(2,1)S(1)} %get-tuple-element.72), channel_id=1, source_target_pairs={{0,16},{1,17},{2,18},{3,19},{4,20},{5,21},{6,22},{7,23},{8,24},{9,... | collective-permute-start | bytes 294920 | tf_op jit(solution)/shard_map/ppermute | solution.py:131
  165.9 6.5 %collective-permute-start.20 = (bf16[2,16,1536]{2,1,0:T(8,128)(2,1)S(1)}, bf16[2,16,1536]{2,1,0:T(8,128)(2,1)S(1)}, u32[]{:S(2)}, u32[]{:S(2)}) collective-permute-start(bf16[2,16,1536]{2,1,0:T(8,128)(2,1)S(1)} %get-tuple-element.73), channel_id=1, source_target_pairs={{0,24},{1,25},{2,26},{3,27},{4,28},{5,29},{6,30},{7,31},{8,16},{9,... | collective-permute-start | bytes 294920 | tf_op jit(solution)/shard_map/ppermute | solution.py:131
  172.5 1.3 collective-permute-start.21

commit v6 on v1

--- a/solution.py
+++ b/solution.py
@@ -1,3 +1,5 @@
+import functools
+
 import jax
 import jax.numpy as jnp
 from jax import lax
@@ -103,15 +105,22 @@
 CHIPS = 4
 GROUP = CORES * CHIPS
 SLOTS = 4
-VMEM_LIMIT = 48 * 1024 * 1024
-
-
-def kernel_params():
-    return pltpu.CompilerParams(vmem_limit_bytes=VMEM_LIMIT)
+LIGHT = pl.CostEstimate(flops=1, bytes_accessed=1, transcendentals=0)
+SMALL_VMEM = 16 * 1024 * 1024
+LOGITS_VMEM = 48 * 1024 * 1024
+LARGE_VMEM = 52 * 1024 * 1024
+
+
+def kernel_params(limit=SMALL_VMEM):
+    return pltpu.CompilerParams(vmem_limit_bytes=limit)
 
 
 def vmem_spec():
     return pl.BlockSpec(memory_space=pltpu.VMEM)
+
+
+def hbm_spec():
+    return pl.BlockSpec(memory_space=pltpu.HBM)
 
 
 def smem_spec():
@@ -121,10 +130,6 @@
 def shift(x, distance):
     n = lax.axis_size("vocab")
     return lax.ppermute(x, "vocab", [(i, i ^ distance) for i in range(n)])
-
-
-def tile_of(size):
-    return 512 if size % 512 == 0 else 128
 
 
 def token_places(place, rows, side):
@@ -171,63 +176,112 @@
             entropy_ref[...] = jnp.broadcast_to(entropy[:rows], entropy_ref.shape)
 
 
-def assemble(pieces, rows, out_ref):
-    layers = pieces[0].shape[0] // rows
-    for k in range(layers):
-        for p, piece in enumerate(pieces):
-            out_ref[pl.ds((k * GROUP + p) * rows, rows), :] = piece[pl.ds(k * rows, rows), :]
-
-
-def logits_kernel(rows, *refs):
-    pieces = refs[:GROUP]
-    w_ref, prob_ref, logits_ref, stat_ref, hidden = refs[GROUP:]
+def piece_blocks(layers):
+    first = [
+        [k * GROUP + core * CHIPS + x + 2 * y for x in range(2) for k in range(layers)]
+        for core in range(CORES)
+        for y in range(2)
+    ]
+    second = [
+        [k * GROUP + core * CHIPS + x + 2 * y for y in range(2) for k in range(layers)]
+        for core in range(CORES)
+        for x in range(2)
+    ]
+    return first, second
+
+
+def assemble(pieces, places, rows, out_ref, columns=slice(None)):
+    for piece, blocks in zip(pieces, places):
+        for i, block in enumerate(blocks):
+            out_ref[pl.ds(block * rows, rows), columns] = piece[pl.ds(i * rows, rows), :]
+
+
+def logits_kernel(rows, places, *refs):
+    count = 2 * len(places[0])
+    pieces, refs = refs[:count], refs[count:]
+    w_ref, prob_ref, logits_ref, stat_ref, hidden, weight, sems, cross_ref = refs
+    half, width = w_ref.shape[0] // 2, prob_ref.shape[1]
+    tiles = w_ref.shape[1] // width
     step = pl.program_id(0)
-    assemble(pieces, rows, hidden)
-    part = jnp.dot(hidden[...], w_ref[...], preferred_element_type=jnp.float32)
+
+    def copy(i):
+        span = pl.ds(i * half, half)
+        return pltpu.make_async_copy(w_ref.at[span, :], weight.at[span, :], sems.at[i])
 
     @pl.when(step == 0)
     def _():
-        logits_ref[...] = part
-
-    @pl.when(step > 0)
+        copy(0).start()
+        copy(1).start()
+        for i, some in enumerate(places):
+            mine = pieces[i * len(some) : (i + 1) * len(some)]
+            assemble(mine, some, rows, hidden, slice(i * half, (i + 1) * half))
+        copy(0).wait()
+
+    @pl.when(step == tiles)
     def _():
-        logits_ref[...] += part
-
-    @pl.when(step == pl.num_programs(0) - 1)
+        copy(1).wait()
+
+    @pl.when(step < tiles)
+    def _():
+        span = pl.ds(pl.multiple_of(step * width, width), width)
+        logits_ref[:, span] = jnp.dot(
+            hidden[:, :half], weight[:half, span], preferred_element_type=jnp.float32
+        )
+
+    @pl.when(step >= tiles)
+    def _():
+        span = pl.ds(pl.multiple_of((step - tiles) * width, width), width)
+        total = logits_ref[:, span] + jnp.dot(
+            hidden[:, half:], weight[half:, span], preferred_element_type=jnp.float32
+        )
+        logits_ref[:, span] = total
+        product = total * prob_ref[...]
+        folded = product[:, :128]
+        for i in range(1, width // 128):
+            folded = folded + product[:, i * 128 : (i + 1) * 128]
+        cross_ref[...] = jnp.where(step == tiles, 0.0, cross_ref[...]) + folded
+
+    @pl.when(step == 2 * tiles - 1)
     def _():
         logits = logits_ref[...]
         top = jnp.max(logits, axis=1, keepdims=True)
         norm = top + jnp.log(jnp.sum(jnp.exp(logits - top), axis=1, keepdims=True))
-        cross = jnp.sum(prob_ref[...] * logits, axis=1, keepdims=True)
+        cross = jnp.sum(cross_ref[...], axis=1, keepdims=True)
         lane = lax.broadcasted_iota(jnp.int32, (1, 128), 1)
-        both = jnp.where(lane == 0, norm, jnp.where(lane == 1, cross, 0.0))
-        stat_ref[...] = both.T[:2]
+        both = jnp.where(lane == 0, norm, jnp.where(lane == 1, cross, 0.0)).T
+        tokens = logits.shape[0]
+        packed = [both[i : i + 1, t : t + 128] for i in range(2) for t in range(0, tokens, 128)]
+        stat_ref[...] = jnp.broadcast_to(jnp.concatenate(packed, axis=0)[None], stat_ref.shape)
 
 
 def grad_kernel(
-    rows, pos_ref, own_ref, sib_ref, logits_ref, prob_ref, weight_ref, entropy_ref, grad_ref, loss_ref
+    rows, pos_ref, stat_ref, logits_ref, prob_ref, weight_ref, entropy_ref, grad_ref, loss_ref
 ):
     tokens = logits_ref.shape[0]
     devices = tokens // rows
     layers, _, side = weight_ref.shape
     layer_bits = (devices // GROUP).bit_length() - 1
     pos = [pos_ref[i] for i in range(3)]
+    rank = pos_ref[3]
     lane = lax.broadcasted_iota(jnp.int32, (1, 128), 1)
+    per_stat = stat_ref.shape[1] // 2
+    norms, crosses = [
+        jnp.concatenate([stat_ref[:, i * per_stat + t, :] for t in range(per_stat)], axis=1) for i in range(2)
+    ]
     stat = jnp.concatenate(
-        [own_ref[...], sib_ref[...], jnp.zeros((128 - 2 * devices, tokens), jnp.float32)], axis=0
+        [norms, crosses, jnp.zeros((128 - 2 * devices, tokens), jnp.float32)], axis=0
     ).T
-    pairs = [(1 + i, 3 + i) for i in range(layer_bits)]
-    pairs += [(1 + layer_bits, 0), (2 + layer_bits, 1), (3 + layer_bits, 2)]
-    for lane_bit, block_bit in pairs:
+    pairs = [(0, 2), (1, 0), (2, 1)] + [(3 + i, 3 + i) for i in range(layer_bits)]
+    for index_bit, block_bit in pairs:
         halves = stat.reshape(devices >> (block_bit + 1), 2, rows << block_bit, 128)
         swapped = jnp.stack([halves[:, 1], halves[:, 0]], axis=1).reshape(tokens, 128)
-        stat = jnp.where((lane >> lane_bit) & 1 == 1, swapped, stat)
-    used = lane < 2 * devices
-    is_norm = used & (lane % 2 == 0)
+        stat = jnp.where(((lane ^ rank) >> index_bit) & 1 == 1, swapped, stat)
+    is_norm = lane < devices
+    is_cross = (lane >= devices) & (lane < 2 * devices)
     top = jnp.max(jnp.where(is_norm, stat, -jnp.inf), axis=1, keepdims=True)
     total = jnp.sum(jnp.where(is_norm, jnp.exp(stat - top), 0.0), axis=1, keepdims=True)
     log_norm = top + jnp.log(total)
-    cross = jnp.sum(jnp.where(used & (lane % 2 == 1), stat, 0.0), axis=1, keepdims=True)
+    cross = jnp.sum(jnp.where(is_cross, stat, 0.0), axis=1, keepdims=True)
     loss_ref[...] = entropy_ref[...] - cross[:rows] + log_norm[:rows]
     where_token = token_places(pos, rows, side)
     for k in range(layers):
@@ -263,10 +317,15 @@
                 out[k, core] = total[start : start + rows].astype(out.dtype)
 
 
-def head_kernel(rows, *refs):
-    pieces = refs[:GROUP]
-    grad_ref, out_ref, hidden = refs[GROUP:]
-    assemble(pieces, rows, hidden)
+def head_kernel(rows, places, *refs):
+    pieces, (grad_ref, out_ref, hidden) = refs[:-3], refs[-3:]
+    half = pl.program_id(0) // 2
+    for i, some in enumerate(places):
+
+        @pl.when(half == i)
+        def _():
+            assemble(pieces[i * len(some) : (i + 1) * len(some)], some, rows, hidden)
+
     out_ref[...] = lax.dot_general(
         hidden[...], grad_ref[...], (((0,), (0,)), ((), ())), preferred_element_type=jnp.float32
     ).astype(out_ref.dtype)
@@ -297,14 +356,14 @@
     return jnp.stack([high, middle, low]).astype(jnp.bfloat16)
 
 
-def send_teacher(teacher_logits, block_lists, places):
+def pack_teacher(teacher_logits, block_lists, places, layer):
     blocks, listed_count, stored, side = teacher_logits.shape
     n = lax.axis_size("vocab")
     rank = lax.axis_index("vocab")
     owner = block_lists // places
     earlier = jnp.tril(jnp.ones((listed_count, listed_count), jnp.bool_), -1)
     slot = jnp.sum((owner[:, :, None] == owner[:, None, :]) & earlier, axis=2, dtype=jnp.int32)
-    code = owner * SLOTS + slot
+    code = (owner ^ (layer * GROUP)) * SLOTS + slot
     picker = (code[:, None, :] == jnp.arange(n * SLOTS, dtype=jnp.int32)[None, :, None]).astype(jnp.bfloat16)
     packed = jnp.einsum(
         "tsk,tkrc->tsrc", picker, teacher_logits, preferred_element_type=jnp.float32
@@ -320,7 +379,13 @@
     payload = jnp.concatenate(
         [packed.reshape(n, -1, side), jnp.broadcast_to(stat, (n, 1, side))], axis=1
     )
-    arrived = lax.all_to_all(payload, "vocab", split_axis=0, concat_axis=0, tiled=True)
+    mine = (owner * SLOTS + slot)[:, None, :] == rank * SLOTS + jnp.arange(SLOTS, dtype=jnp.int32)[None, :, None]
+    place = jnp.sum(jnp.where(mine, (block_lists % places + 1)[:, None, :], 0), axis=2) - 1
+    return payload.reshape(n // GROUP, GROUP, -1, side), place.astype(jnp.int32)
+
+
+def unpack_teacher(arrived, blocks, stored):
+    n, _, side = arrived.shape
     arrived_blocks = (
         arrived[:, :-1]
         .reshape(n, blocks, SLOTS, stored, side)
@@ -335,9 +400,15 @@
         .transpose(1, 2, 0, 3)
         .reshape(2, blocks, 1, n * stored)
     )
-    mine = code[:, None, :] == rank * SLOTS + jnp.arange(SLOTS, dtype=jnp.int32)[None, :, None]
-    place = jnp.sum(jnp.where(mine, (block_lists % places + 1)[:, None, :], 0), axis=2) - 1
-    return arrived_blocks, arrived_stat, place.astype(jnp.int32)
+    return arrived_blocks, arrived_stat
+
+
+def by_distance(x, layer, layers):
+    shape = x.shape
+    for i in range((layers - 1).bit_length()):
+        pairs = x.reshape(shape[0], layers >> (i + 1), 2, -1)
+        x = jnp.where((layer >> i) & 1 == 1, pairs[:, :, ::-1], pairs).reshape(shape)
+    return x
 
 
 def levels_plan(
@@ -353,16 +424,32 @@
     half = depth // CORES
     bf16, f32 = jnp.bfloat16, jnp.float32
     core, chip, layer = rank % CORES, (rank // CORES) % CHIPS, rank // GROUP
-    pos = jnp.stack([core, chip, layer]).astype(jnp.int32)
+    pos = jnp.stack([core, chip, layer, rank]).astype(jnp.int32)
     unlisted = float(n * slab - side * listed_count)
+    in_layer = [[o * GROUP + i for i in range(GROUP)] for o in range(layers)]
+    X, Y = CORES, 2 * CORES
 
     column = [hidden_states] + [shift(hidden_states, k * GROUP) for k in range(1, layers)]
+    sib_w = shift(head_weight, 1)
+    payload, place = pack_teacher(teacher_logits, block_lists, slab // side, layer)
+    payload = lax.all_to_all(
+        payload, "vocab", split_axis=1, concat_axis=1, axis_index_groups=in_layer, tiled=True
+    )
     column = jnp.concatenate(column, axis=0)
-    pieces = [column] + [shift(column, j * CORES) for j in range(1, CHIPS)]
-    pieces = pieces + [shift(piece, 1) for piece in pieces]
-
-    arrived_blocks, arrived_stat, place = send_teacher(teacher_logits, block_lists, slab // side)
-    sib_w = shift(lax.dynamic_slice(head_weight, ((1 - core) * half, 0), (half, slab)), 1)
+    column, payload = lax.optimization_barrier((column, payload))
+    first, second = [column[:, :half]], [column[:, half:]]
+    first_x, second_y = shift(first[0], X), shift(second[0], Y)
+    crossed = [payload[k] for k in range(layers)]
+    early = [shift(crossed[k], k * GROUP) for k in range(1, layers - 1)]
+    first_x, second_y, sib_w, *early = lax.optimization_barrier((first_x, second_y, sib_w, *early))
+    first = [jnp.concatenate([first[0], first_x], axis=0)]
+    second = [jnp.concatenate([second[0], second_y], axis=0)]
+    first.append(shift(first[0], Y))
+    second.append(shift(second[0], X))
+    late = [shift(crossed[k], k * GROUP) for k in range(max(layers - 1, 1), layers)]
+    arrived = jnp.stack([crossed[0], *early, *late]).reshape(n, -1, side)
+    arrived_blocks, arrived_stat = unpack_teacher(arrived, blocks, stored)
+    first_sib, second_sib = [shift(first[0], 1)], [shift(second[0], 1)]
 
     prob, entropy = pl.pallas_call(
         lambda *refs: teacher_kernel(unlisted, rows, *refs),
@@ -373,45 +460,52 @@
         in_specs=[smem_spec(), smem_spec()] + [vmem_spec()] * 4,
         out_specs=(vmem_spec(), vmem_spec()),
         compiler_params=kernel_params(),
-        cost_estimate=pl.CostEstimate(
-            flops=2 * tokens * side * side * SLOTS, bytes_accessed=4 * tokens * slab, transcendentals=0
-        ),
+        cost_estimate=LIGHT,
         name="teacher_prob",
     )(
         pos,
         place,
         arrived_blocks,
         arrived_stat,
-        row_reader.reshape(blocks, 1, side),
+        by_distance(row_reader, layer, layers).reshape(blocks, 1, side),
         tail_mass.reshape(blocks, 1, side),
     )
 
-    tile = tile_of(depth)
-    piece_specs = [pl.BlockSpec((layers * rows, tile), lambda t: (0, t)) for _ in range(GROUP)]
+    first[1], second[1], first_sib[0], second_sib[0], prob = lax.optimization_barrier(
+        (first[1], second[1], first_sib[0], second_sib[0], prob)
+    )
+    first_sib.append(shift(first[1], 1))
+    second_sib.append(shift(second[1], 1))
+    pieces = first + first_sib + second + second_sib
+    places = piece_blocks(layers)
+
+    width = 256 if slab % 256 == 0 else 128
+    tiles = slab // width
     whole = lambda t: (0, 0)
     logits, stat = pl.pallas_call(
-        lambda *refs: logits_kernel(rows, *refs),
-        grid=(depth // tile,),
-        out_shape=(
+        functools.partial(logits_kernel, rows, places),
+        grid=(2 * tiles,),
+        out_shape=[
             jax.ShapeDtypeStruct((tokens, slab), f32),
-            jax.ShapeDtypeStruct((2, tokens), f32),
-        ),
-        in_specs=piece_specs
-        + [pl.BlockSpec((tile, slab), lambda t: (t, 0)), pl.BlockSpec((tokens, slab), whole)],
-        out_specs=(pl.BlockSpec((tokens, slab), whole), pl.BlockSpec((2, tokens), whole)),
-        scratch_shapes=[pltpu.VMEM((tokens, tile), bf16)],
-        compiler_params=kernel_params(),
-        cost_estimate=pl.CostEstimate(
-            flops=2 * tokens * depth * slab,
-            bytes_accessed=2 * depth * (slab + tokens) + 4 * tokens * slab,
-            transcendentals=tokens * slab,
-        ),
+            jax.ShapeDtypeStruct((n, 2 * tokens // 128, 128), f32),
+        ],
+        in_specs=[vmem_spec()] * len(pieces)
+        + [hbm_spec(), pl.BlockSpec((tokens, width), lambda t: (0, jnp.maximum(t - tiles, 0)))],
+        out_specs=[
+            pl.BlockSpec((tokens, slab), whole),
+            pl.BlockSpec((n, 2 * tokens // 128, 128), lambda t: (0, 0, 0)),
+        ],
+        scratch_shapes=[
+            pltpu.VMEM((tokens, depth), bf16),
+            pltpu.VMEM((depth, slab), bf16),
+            pltpu.SemaphoreType.DMA((2,)),
+            pltpu.VMEM((tokens, 128), f32),
+        ],
+        compiler_params=kernel_params(LOGITS_VMEM),
+        cost_estimate=LIGHT,
         name="logits",
     )(*pieces, head_weight, prob)
-
-    stat = jnp.concatenate([stat] + [shift(stat, k * GROUP) for k in range(1, layers)], axis=0)
-    stat = jnp.concatenate([stat] + [shift(stat, j * CORES) for j in range(1, CHIPS)], axis=0)
-    sib_stat = shift(stat, 1)
+    stat = lax.all_to_all(stat, "vocab", split_axis=0, concat_axis=0, tiled=True)
 
     grad, loss = pl.pallas_call(
         lambda *refs: grad_kernel(rows, *refs),
@@ -419,91 +513,77 @@
             jax.ShapeDtypeStruct((tokens, slab), bf16),
             jax.ShapeDtypeStruct((rows, side), f32),
         ),
-        in_specs=[smem_spec()] + [vmem_spec()] * 6,
+        in_specs=[smem_spec()] + [vmem_spec()] * 5,
         out_specs=(vmem_spec(), vmem_spec()),
         compiler_params=kernel_params(),
-        cost_estimate=pl.CostEstimate(
-            flops=4 * tokens * slab, bytes_accessed=10 * tokens * slab, transcendentals=tokens * slab
-        ),
+        cost_estimate=LIGHT,
         name="grad_logits",
-    )(pos, stat, sib_stat, logits, prob, token_weight.reshape(blocks, 1, side), entropy)
+    )(pos, stat, logits, prob, token_weight.reshape(blocks, 1, side), entropy)
     sib_grad = shift(grad, 1)
 
-    tile = tile_of(half)
-    steps = half // tile
-    out_block = pl.BlockSpec((layers, CORES, rows, tile), lambda t, core: (0, 0, 0, t))
+    tile = half // 5
+    out_block = pl.BlockSpec((layers, CORES, rows, tile), lambda t, pos: (0, 0, 0, t))
     partial = pl.pallas_call(
-        lambda *refs: partial_kernel(rows, *refs),
+        functools.partial(partial_kernel, rows),
         grid_spec=pltpu.PrefetchScalarGridSpec(
             num_scalar_prefetch=1,
-            grid=(steps,),
-            in_specs=[
-                pl.BlockSpec((tokens, slab), lambda t, core: (0, 0)),
-                pl.BlockSpec((tokens, slab), lambda t, core: (0, 0)),
-                pl.BlockSpec((tile, slab), lambda t, core: (core[0] * steps + t, 0)),
-                pl.BlockSpec((tile, slab), lambda t, core: (t, 0)),
-            ],
+            grid=(5,),
+            in_specs=[pl.BlockSpec((tokens, slab), lambda t, pos: (0, 0))] * 2
+            + [pl.BlockSpec((tile, slab), lambda t, pos: (pos[0] * 5 + t, 0))] * 2,
             out_specs=[out_block] * CHIPS,
             scratch_shapes=[pltpu.VMEM((tokens, slab), bf16)],
         ),
         out_shape=[
-            jax.ShapeDtypeStruct((layers, CORES, rows, half), f32 if j == 0 else bf16)
-            for j in range(CHIPS)
+            jax.ShapeDtypeStruct((layers, CORES, rows, half), f32 if j == 0 else bf16) for j in range(CHIPS)
         ],
-        compiler_params=kernel_params(),
-        cost_estimate=pl.CostEstimate(
-            flops=4 * tokens * half * slab, bytes_accessed=4 * half * slab, transcendentals=0
-        ),
+        compiler_params=kernel_params(LARGE_VMEM),
+        cost_estimate=LIGHT,
         name="grad_hidden_partial",
-    )(pos[:1], grad, sib_grad, head_weight, sib_w)
-
+    )(pos, grad, sib_grad, head_weight, sib_w)
+    *partial, late_grad = lax.optimization_barrier((*partial, grad))
     arrived = [shift(partial[j], j * CORES) for j in range(1, CHIPS)]
-    chip_block = pl.BlockSpec((layers, CORES, rows, tile), lambda t: (0, 0, 0, t))
-    layer_block = pl.BlockSpec((CORES, rows, tile), lambda t: (0, 0, t))
+
+    head_tile = half // 2
+    per_half = len(pieces) // 2
+    grad_head = pl.pallas_call(
+        functools.partial(head_kernel, rows, places),
+        grid=(4,),
+        in_specs=[
+            pl.BlockSpec((piece.shape[0], head_tile), lambda t, i=i: (0, jnp.clip(t - 2 * (i // per_half), 0, 1)))
+            for i, piece in enumerate(pieces)
+        ]
+        + [pl.BlockSpec((tokens, slab), whole)],
+        out_specs=pl.BlockSpec((head_tile, slab), lambda t: (t, 0)),
+        out_shape=jax.ShapeDtypeStruct((depth, slab), bf16),
+        scratch_shapes=[pltpu.VMEM((tokens, head_tile), bf16)],
+        compiler_params=kernel_params(LARGE_VMEM),
+        cost_estimate=LIGHT,
+        name="grad_head",
+    )(*pieces, late_grad)
+    arrived, grad_head = lax.optimization_barrier((arrived, grad_head))
+
     summed = pl.pallas_call(
         chip_sum_kernel,
-        grid=(steps,),
-        in_specs=[chip_block] * CHIPS,
-        out_specs=[layer_block] * layers,
+        in_specs=[vmem_spec()] * CHIPS,
+        out_specs=[vmem_spec()] * layers,
         out_shape=[
             jax.ShapeDtypeStruct((CORES, rows, half), f32 if k == 0 else bf16) for k in range(layers)
         ],
         compiler_params=kernel_params(),
-        cost_estimate=pl.CostEstimate(
-            flops=tokens * half, bytes_accessed=3 * tokens * half, transcendentals=0
-        ),
+        cost_estimate=LIGHT,
         name="chip_sum",
     )(partial[0], *arrived)
     arrived = [shift(summed[k], k * GROUP) for k in range(1, layers)]
-    row_block = pl.BlockSpec((rows, tile), lambda t: (0, t))
     mine, theirs = pl.pallas_call(
         layer_sum_kernel,
-        grid=(steps,),
-        in_specs=[layer_block] * layers,
-        out_specs=[row_block] * CORES,
-        out_shape=[jax.ShapeDtypeStruct((rows, half), bf16)] * CORES,
+        in_specs=[vmem_spec()] * layers,
+        out_specs=[vmem_spec()] * 2,
+        out_shape=[jax.ShapeDtypeStruct((rows, half), bf16)] * 2,
         compiler_params=kernel_params(),
-        cost_estimate=pl.CostEstimate(
-            flops=CORES * layers * rows * half, bytes_accessed=3 * CORES * layers * rows * half, transcendentals=0
-        ),
+        cost_estimate=LIGHT,
         name="layer_sum",
     )(summed[0], *arrived)
     other = shift(theirs, 1)
-
-    tile = tile_of(depth)
-    grad_head = pl.pallas_call(
-        lambda *refs: head_kernel(rows, *refs),
-        grid=(depth // tile,),
-        in_specs=piece_specs + [pl.BlockSpec((tokens, slab), whole)],
-        out_specs=pl.BlockSpec((tile, slab), lambda t: (t, 0)),
-        out_shape=jax.ShapeDtypeStruct((depth, slab), bf16),
-        scratch_shapes=[pltpu.VMEM((tokens, tile), bf16)],
-        compiler_params=kernel_params(),
-        cost_estimate=pl.CostEstimate(
-            flops=2 * tokens * depth * slab, bytes_accessed=2 * depth * (slab + tokens), transcendentals=0
-        ),
-        name="grad_head",
-    )(*pieces, grad)
 
     low, high = jnp.where(core == 0, mine, other), jnp.where(core == 0, other, mine)
     return loss[:, 0], grad_head, jnp.concatenate([low, high], axis=1)
@@ -520,7 +600,7 @@
         and rows % 16 == 0
         and 2 * n <= side
         and 6 * blocks * stored <= side
-        and hidden_states.shape[1] % (CORES * 128) == 0
+        and hidden_states.shape[1] % (CORES * 1280) == 0
     )
 
 

time: 172 us -> 154 us (0.90)
  waiting for transfers between devices: 70.2 us -> 54.6 us
  blocking collectives: 0 us -> 10.2 us
  local copies, waits for them, and re-layouts: 19.1 us -> 10.5 us
  starting transfers between devices: 34.2 us -> 30.1 us
  Pallas kernels: 42.8 us -> 39.6 us
  other arithmetic: 3.02 us -> 6.03 us
    ppermute x26 -> x23, waiting for transfers between devices: 69.6 us -> 45.5 us  [shift(): return lax.ppermute(x, 'vocab', [(i, i ^ distance) for i in range(n)])]
    all_to_all x0 -> x1, blocking collectives: none -> 10.2 us  [levels_plan(): lax.all_to_all(stat, 'vocab', split_axis=0, concat_axis=0, tiled=True)]
    all_to_all x1, waiting for transfers between devices: 0.55 us -> 9.1 us  [levels_plan(): lax.all_to_all(payload, 'vocab', split_axis=1, concat_axis=1, axis_index_...]
    dynamic_slice x1 -> x0, local copies, waits for them, and re-layouts: 5.47 us -> none  [levels_plan(): lax.dynamic_slice(head_weight, ((1 - core) * half, 0), (half, slab))]
    unnamed x44 -> x36, local copies, waits for them, and re-layouts: 9.85 us -> 5.52 us
    pallas_call x5, Pallas kernels: 38.4 us -> 35.3 us  [the longest x1 13.6 us: levels_plan(): pl.pallas_call(functools.partial(logits_kernel, rows, places), grid=(2 *...]
    ppermute x26 -> x23, starting transfers between devices: 28.2 us -> 26.1 us  [shift(): return lax.ppermute(x, 'vocab', [(i, i ^ distance) for i in range(n)])]
    all_to_all x1, starting transfers between devices: 5.99 us -> 3.94 us  [levels_plan(): lax.all_to_all(payload, 'vocab', split_axis=1, concat_axis=1, axis_index_...]
  transfers between devices with their start and end apart: 27 -> 24, of which waited for: 15 -> 14; matrix products, arithmetic and copies ran while one was open for 7% -> 8% of each run, Pallas kernels for 19% -> 9%
where the time goes in v6:
time: 154 us; the launch traced here: 153 us
  waiting for transfers between devices  54.6 us (35%)
  Pallas kernels  39.6 us (26%)
  starting transfers between devices  30.1 us (20%)
  local copies, waits for them, and re-layouts  10.5 us (7%)
  blocking collectives  10.2 us (7%)
  other arithmetic  6.03 us (4%)
    ppermute x23, waiting for transfers between devices, shift(): return lax.ppermute(x, 'vocab', [(i, i ^ distance) for i in range(n)])  45.5 us
    ppermute x23, starting transfers between devices, shift(): return lax.ppermute(x, 'vocab', [(i, i ^ distance) for i in range(n)])  26.1 us
    pallas_call x1, Pallas kernels, levels_plan(): pl.pallas_call(functools.partial(logits_kernel, rows, places), grid=(2 *...  13.6 us
    pallas_call x1, Pallas kernels, levels_plan(): pl.pallas_call(functools.partial(partial_kernel, rows), grid_spec=pltpu.P...  10.7 us
    pallas_call x1, Pallas kernels, levels_plan(): pl.pallas_call(functools.partial(head_kernel, rows, places), grid=(4,), i...  10.6 us
    all_to_all x1, blocking collectives, levels_plan(): lax.all_to_all(stat, 'vocab', split_axis=0, concat_axis=0, tiled=True)  10.2 us
    all_to_all x1, waiting for transfers between devices, levels_plan(): lax.all_to_all(payload, 'vocab', split_axis=1, concat_axis=1, axis_index_...  9.1 us
    unnamed x36, local copies, waits for them, and re-layouts  5.52 us
  transfers between devices with their start and end apart: 24, of which 14 were waited for; matrix products, arithmetic and copies ran while one was open for 8% of the time, Pallas kernels for 9%

profile of v6, /device:TPU:0, one launch (start us, length us, event | category | flops | bytes accessed | tf_op | source)
XLA Modules:
  0.0 153.4 jit_solution(9994778360466330791)
XLA Ops:
  0.6 0.5 collective-permute-start.5
  1.1 3.7 %collective-permute-start.1 = (bf16[16,5120]{1,0:T(8,128)(2,1)}, bf16[16,5120]{1,0:T(8,128)(2,1)S(1)}, u32[]{:S(2)}, u32[]{:S(2)}) collective-permute-start(bf16[16,5120]{1,0:T(8,128)(2,1)} %param.7), channel_id=1, source_target_pairs={{0,16},{1,17},{2,18},{3,19},{4,20},{5,21},{6,22},{7,23},{8,24},{9,... | collective-permute-start | bytes 491528 | tf_op jit(solution)/shard_map/ppermute | solution.py:132
  4.8 1.6 %collective-permute-start = (bf16[16,5120]{1,0:T(8,128)(2,1)}, bf16[16,5120]{1,0:T(8,128)(2,1)S(1)}, u32[]{:S(2)}, u32[]{:S(2)}) collective-permute-start(bf16[16,5120]{1,0:T(8,128)(2,1)} %param.7), channel_id=1, source_target_pairs={{0,8},{1,9},{2,10},{3,11},{4,12},{5,13},{6,14},{7,15},{8,0},{9,1},... | collective-permute-start | bytes 491528 | tf_op jit(solution)/shard_map/ppermute | solution.py:132
  6.4 1.2 reduce_max.14
  7.6 1.5 fusion.1
  9.1 0.1 convert_element_type.31
  9.2 0.7 fusion.8
  10.0 0.2 convert_reduce_fusion
  10.2 1.4 convolution_convert_fusion
  11.6 0.4 copy.56
  12.2 1.2 copy.58
  13.4 3.9 %all-to-all-start = ((bf16[4,8,65,128]{3,0,2,1:T(4,128)(2,1)}), bf16[4,8,65,128]{3,0,2,1:T(4,128)(2,1)S(1)}, u32[]{:S(2)}, u32[]{:S(2)}) async-start(bf16[4,8,65,128]{3,0,2,1:T(4,128)(2,1)} %copy.58), calls=%async_computation | async-start | bytes 1064960 | tf_op jit(solution)/shard_map/all_to_all | solution.py:435
  17.5 0.1 reshape_reshape.6
  17.7 0.4 collective-permute-done.2
  18.1 9.1 %all-to-all-done = bf16[4,8,65,128]{3,0,2,1:T(4,128)(2,1)S(1)} async-done(((bf16[4,8,65,128]{3,0,2,1:T(4,128)(2,1)}), bf16[4,8,65,128]{3,0,2,1:T(4,128)(2,1)S(1)}, u32[]{:S(2)}, u32[]{:S(2)}) %all-to-all-start) | async-done | bytes 532512 | tf_op jit(solution)/shard_map/all_to_all | solution.py:435
  27.3 0.6 collective-permute-start.4
  27.9 0.6 collective-permute-start.3
  28.5 0.7 fusion.11
  29.2 1.7 %collective-permute-start.7 = (bf16[8,65,128]{2,0,1:T(8,128)(2,1)S(1)}, bf16[8,65,128]{2,0,1:T(8,128)(2,1)S(1)}, u32[]{:S(2)}, u32[]{:S(2)}) collective-permute-start(bf16[8,65,128]{2,0,1:T(8,128)(2,1)S(1)} %get-tuple-element.83), channel_id=1, source_target_pairs={{0,16},{1,17},{2,18},{3,19},{4,20},{5,21},{6,22},{7,23},{8,24},{9,... | collective-permute-start | bytes 399368 | tf_op jit(solution)/shard_map/ppermute | solution.py:132
  30.9 2.5 %collective-permute-start.6 = (bf16[8,65,128]{2,0,1:T(8,128)(2,1)S(1)}, bf16[8,65,128]{2,0,1:T(8,128)(2,1)S(1)}, u32[]{:S(2)}, u32[]{:S(2)}) collective-permute-start(bf16[8,65,128]{2,0,1:T(8,128)(2,1)S(1)} %get-tuple-element.84), channel_id=1, source_target_pairs={{0,8},{1,9},{2,10},{3,11},{4,12},{5,13},{6,14},{7,15},{8,0},{9,1},... | collective-permute-start | bytes 399368 | tf_op jit(solution)/shard_map/ppermute | solution.py:132
  33.4 0.2 select_reduce_fusion
  33.6 4.2 %collective-permute-done.7 = bf16[8,65,128]{2,0,1:T(8,128)(2,1)S(1)} collective-permute-done((bf16[8,65,128]{2,0,1:T(8,128)(2,1)S(1)}, bf16[8,65,128]{2,0,1:T(8,128)(2,1)S(1)}, u32[]{:S(2)}, u32[]{:S(2)}) %collective-permute-start.7) | collective-permute-done | bytes 133152 | tf_op jit(solution)/shard_map/ppermute | solution.py:132
  37.8 2.5 %collective-permute-start.12 = (bf16[8,65,128]{2,0,1:T(8,128)(2,1)}, bf16[8,65,128]{2,0,1:T(8,128)(2,1)}, u32[]{:S(2)}, u32[]{:S(2)}) collective-permute-start(bf16[8,65,128]{2,0,1:T(8,128)(2,1)} %get-tuple-element.82), channel_id=1, source_target_pairs={{0,24},{1,25},{2,26},{3,27},{4,28},{5,29},{6,30},{7,31},{8,16},{9,... | collective-permute-start | bytes 399368 | tf_op jit(solution)/shard_map/ppermute | solution.py:132
  40.5 0.5 copy-done.16
  41.0 2.0 %collective-permute-start.9 = (bf16[128,2560]{1,0:T(8,128)(2,1)S(1)}, bf16[128,2560]{1,0:T(8,128)(2,1)S(1)}, u32[]{:S(2)}, u32[]{:S(2)}) collective-permute-start(bf16[128,2560]{1,0:T(8,128)(2,1)S(1)} %pad_maximum_fusion.2.refs_4_), channel_id=1, source_target_pairs={{0,2},{1,3},{2,0},{3,1},{4,6},{5,7},{6,4},{7,5},{8,10},{9,11},{10,... | collective-permute-start | bytes 1966088 | tf_op jit(solution)/shard_map/ppermute | solution.py:132
  43.1 0.3 collective-permute-start.10
  43.4 1.4 collective-permute-start.8
  44.9 0.2 collective-permute-done.12
  45.0 1.1 copy_bitcast_fusion
  46.2 1.1 copy.64
  47.3 0.1 copy.65
  47.4 0.1 copy.66
  47.6 0.1 reshape.202
  47.7 1.0 copy-done.9
  48.7 3.0 %teacher_prob.1 = (f32[512,1024]{1,0:T(8,128)S(1)}, f32[16,128]{1,0:T(8,128)S(1)}) custom-call(s32[4]{0:T(128)S(1)} %pad_add_fusion.refs_0_.core_ref, s32[4,4]{1,0:T(4,128)S(1)} %broadcast_add_fusion.refs_1_, bf16[4,4,128,128]{3,2,1,0:T(8,128)(2,1)S(1)} %bitcast.44, f32[2,4,1,128]{3,2,1,0:T(1,128)S(1)} %bitcast.45, s32[4,1,128]{2,1,0:T(1,128)S(1)} %reshape_reshape.7.refs_4_, ...), custom_call_target="tpu_custom_call" | custom-call | flops 1 | bytes 1 | tf_op jit(solution)/shard_map/teacher_prob/pallas_call | solution.py:454
  51.8 1.3 copy-done
  53.1 5.3 %collective-permute-done.9.refs_5_ = bf16[128,2560]{1,0:T(8,128)(2,1)S(1)} collective-permute-done((bf16[128,2560]{1,0:T(8,128)(2,1)S(1)}, bf16[128,2560]{1,0:T(8,128)(2,1)S(1)}, u32[]{:S(2)}, u32[]{:S(2)}) %collective-permute-start.9) | collective-permute-done | bytes 655392 | tf_op jit(solution)/shard_map/ppermute | solution.py:132
  58.4 2.0 %collective-permute-done.8.refs_1_ = bf16[128,2560]{1,0:T(8,128)(2,1)} collective-permute-done((bf16[128,2560]{1,0:T(8,128)(2,1)S(1)}, bf16[128,2560]{1,0:T(8,128)(2,1)}, u32[]{:S(2)}, u32[]{:S(2)}) %collective-permute-start.8) | collective-permute-done | bytes 655392 | tf_op jit(solution)/shard_map/ppermute | solution.py:132
  60.4 0.5 collective-permute-start.14
  60.9 2.7 %collective-permute-done.13.refs_3_ = bf16[128,2560]{1,0:T(8,128)(2,1)S(1)} collective-permute-done((bf16[128,2560]{1,0:T(8,128)(2,1)}, bf16[128,2560]{1,0:T(8,128)(2,1)S(1)}, u32[]{:S(2)}, u32[]{:S(2)}) %collective-permute-start.13) | collective-permute-done | bytes 655392 | tf_op jit(solution)/shard_map/ppermute | solution.py:132
  63.6 13.6 %logits.1 = (f32[512,1024]{1,0:T(8,128)}, f32[32,8,128]{2,1,0:T(8,128)S(1)}) custom-call(bf16[128,2560]{1,0:T(8,128)(2,1)S(1)} %pad_maximum_fusion.1.refs_0_, bf16[128,2560]{1,0:T(8,128)(2,1)} %collective-permute-done.8.refs_1_, bf16[128,2560]{1,0:T(8,128)(2,1)S(1)} %collective-permute-done.10.refs_2_, ...), custom_call_target="tpu_custom_call" | custom-call | flops 1 | bytes 1 | tf_op jit(solution)/shard_map/logits/pallas_call | solution.py:485
  77.3 10.2 %all_to_all.10.refs_1_ = f32[32,8,128]{2,1,0:T(8,128)S(1)} all-to-all(f32[32,8,128]{2,1,0:T(8,128)S(1)} %get-tuple-element.52), channel_id=1, replica_groups=mesh['vocab'=32] {'vocab'}, dimensions={0} | all-to-all | bytes 262144 | tf_op jit(solution)/shard_map/all_to_all | solution.py:508
  87.6 1.6 %copy-done.8 = f32[512,1024]{1,0:T(8,128)S(1)} copy-done((f32[512,1024]{1,0:T(8,128)S(1)}, f32[512,1024]{1,0:T(8,128)}, u32[]{:S(2)}) %copy-start.8) | copy-done | bytes 2097176
  89.2 1.3 grad_logits.1
  90.5 0.3 collective-permute-start.15
  90.7 2.4 %collective-permute-done.15.sib_ref = bf16[512,1024]{1,0:T(8,128)(2,1)S(1)} collective-permute-done((bf16[512,1024]{1,0:T(8,128)(2,1)S(1)}, bf16[512,1024]{1,0:T(8,128)(2,1)S(1)}, u32[]{:S(2)}, u32[]{:S(2)}) %collective-permute-start.15) | collective-permute-done | bytes 1048608 | tf_op jit(solution)/shard_map/ppermute | solution.py:132
  93.2 1.0 copy-done.13
  94.2 10.7 %grad_hidden_partial.1 = (f32[4,2,16,2560]{3,2,1,0:T(8,128)}, bf16[4,2,16,2560]{3,2,1,0:T(8,128)(2,1)S(1)}, bf16[4,2,16,2560]{3,2,1,0:T(8,128)(2,1)S(1)}, bf16[4,2,16,2560]{3,2,1,0:T(8,128)(2,1)S(1)}) custom-call(s32[4]{0:T(128)S(1)} %pad_add_fusion.refs_0_.core_ref, bf16[512,1024]{1,0:T(8,128)(2,1)} %copy-done.3, bf16[512,1024]{1,0:T(8,128)(2,1)} %copy-done.13, ...), custom_call_target="tpu_custom_call" | custom-call | flops 1 | bytes 1 | tf_op jit(solution)/shard_map/grad_hidden_partial/pallas_call | solution.py:526
  104.8 0.4 collective-permute-start.16
  105.3 1.0 collective-permute-start.17
  106.3 2.1 %collective-permute-start.18 = (bf16[4,2,16,2560]{3,2,1,0:T(8,128)(2,1)S(1)}, bf16[4,2,16,2560]{3,2,1,0:T(8,128)(2,1)S(1)}, u32[]{:S(2)}, u32[]{:S(2)}) collective-permute-start(bf16[4,2,16,2560]{3,2,1,0:T(8,128)(2,1)S(1)} %get-tuple-element.64), channel_id=1, source_target_pairs={{0,6},{1,7},{2,4},{3,5},{4,2},{5,3},{6,0},{7,1},{8,14},{9,15},{10,... | collective-permute-start | bytes 1966088 | tf_op jit(solution)/shard_map/ppermute | solution.py:132
  108.3 10.6 %grad_head.1 = bf16[5120,1024]{1,0:T(8,128)(2,1)} custom-call(bf16[128,2560]{1,0:T(8,128)(2,1)S(1)} %pad_maximum_fusion.1.refs_0_, bf16[128,2560]{1,0:T(8,128)(2,1)} %collective-permute-done.8.refs_1_, bf16[128,2560]{1,0:T(8,128)(2,1)S(1)} %collective-permute-done.10.refs_2_, bf16[128,2560]{1,0:T(8,128)(2,1)} %copy-done.6, bf16[128,2560]{1,0:T(8,128)(2,1)} %copy-done.2, ...), custom_call_target="tpu_custom_call" | custom-call | flops 1 | bytes 1 | tf_op jit(solution)/shard_map/grad_head/pallas_call | solution.py:548
  118.9 3.5 %collective-permute-done.16.refs_0_ = bf16[4,2,16,2560]{3,2,1,0:T(8,128)(2,1)S(1)} collective-permute-done((bf16[4,2,16,2560]{3,2,1,0:T(8,128)(2,1)S(1)}, bf16[4,2,16,2560]{3,2,1,0:T(8,128)(2,1)S(1)}, u32[]{:S(2)}, u32[]{:S(2)}) %collective-permute-start.16) | collective-permute-done | bytes 655392 | tf_op jit(solution)/shard_map/ppermute | solution.py:132
  122.4 0.2 collective-permute-done.17.refs_1_
  122.6 13.2 %collective-permute-done.18.refs_2_ = bf16[4,2,16,2560]{3,2,1,0:T(8,128)(2,1)S(1)} collective-permute-done((bf16[4,2,16,2560]{3,2,1,0:T(8,128)(2,1)S(1)}, bf16[4,2,16,2560]{3,2,1,0:T(8,128)(2,1)S(1)}, u32[]{:S(2)}, u32[]{:S(2)}) %collective-permute-start.18) | collective-permute-done | bytes 655392 | tf_op jit(solution)/shard_map/ppermute | solution.py:132
  135.8 0.3 chip_sum.1
  136.1 0.7 collective-permute-start.19
  136.8 1.2 collective-permute-start.20
  138.0 2.6 %collective-permute-start.21 = (bf16[2,16,2560]{2,1,0:T(8,128)(2,1)S(1)}, bf16[2,16,2560]{2,1,0:T(8,128)(2,1)S(1)}, u32[]{:S(2)}, u32[]{:S(2)}) collective-permute-start(bf16[2,16,2560]{2,1,0:T(8,128)(2,1)S(1)} %get-tuple-element.74), channel_id=1, source_target_pairs={{0,24},{1,25},{2,26},{3,27},{4,28},{5,29},{6,30},{7,31},{8,16},{9,... | collective-permute-start | bytes 491528 | tf_op jit(solution)/shard_map/ppermute | solution.py:132
  140.6 3.3 %collective-permute-done.19.refs_0_ = bf16[2,16,2560]{2,1,0:T(8,128)(2,1)S(1)} collective-permute-done((bf16[2,16,2560]{2,1,0:T(8,128)(2,1)S(1)}, bf16[2,16,2560]{2,1,0:T(8,128)(2,1)S(1)}, u32[]{:S(2)}, u32[]{:S(2)}) %collective-permute-start.19) | collective-permute-done | bytes 163872 | tf_op jit(solution)/shard_map/ppermute | solution.py:132
  143.9 7.4 %collective-permute-done.20.refs_1_ = bf16[2,16,2560]{2,1,0:T(8,128)(2,1)S(1)} collective-permute-done((bf16[2,16,2560]{2,1,0:T(8,128)(2,1)S(1)}, bf16[2,16,2560]{2,1,0:T(8,128)(2,1)S(1)}, u32[]{:S(2)}, u32[]{:S(2)}) %collective-permute-start.20) | collective-permute-done | bytes 163872 | tf_op jit(solution)/shard_map/ppermute | solution.py:132
  151.4 0.6 slice_reduce_fusion
  152.0 0.6 collective-permute-done.22
  152.7 0.7 pad_maximum_fusion.5
  (75 shorter events, 1.2 us)
Async XLA Ops:
  0.6 39.8 %collective-permute-start.5 = (bf16[5120,1024]{1,0:T(8,128)(2,1)}, bf16[5120,1024]{1,0:T(8,128)(2,1)}, u32[]{:S(2)}, u32[]{:S(2)}) collective-permute-start(bf16[5120,1024]{1,0:T(8,128)(2,1)} %w_ref.1), channel_id=1, source_target_pairs={{0,1},{1,0},{2,3},{3,2},{4,5},{5,4},{6,7},{7,6},{8,9},{9,8},{10,11... | collective-permute-start | bytes 31457288 | tf_op jit(solution)/shard_map/ppermute | solution.py:132
  1.1 16.5 %collective-permute-start.1 = (bf16[16,5120]{1,0:T(8,128)(2,1)}, bf16[16,5120]{1,0:T(8,128)(2,1)S(1)}, u32[]{:S(2)}, u32[]{:S(2)}) collective-permute-start(bf16[16,5120]{1,0:T(8,128)(2,1)} %param.7), channel_id=1, source_target_pairs={{0,16},{1,17},{2,18},{3,19},{4,20},{5,21},{6,22},{7,23},{8,24},{9,... | collective-permute-start | bytes 491528 | tf_op jit(solution)/shard_map/ppermute | solution.py:132
  4.8 12.8 %collective-permute-start = (bf16[16,5120]{1,0:T(8,128)(2,1)}, bf16[16,5120]{1,0:T(8,128)(2,1)S(1)}, u32[]{:S(2)}, u32[]{:S(2)}) collective-permute-start(bf16[16,5120]{1,0:T(8,128)(2,1)} %param.7), channel_id=1, source_target_pairs={{0,8},{1,9},{2,10},{3,11},{4,12},{5,13},{6,14},{7,15},{8,0},{9,1},... | collective-permute-start | bytes 491528 | tf_op jit(solution)/shard_map/ppermute | solution.py:132
  6.4 11.7 %collective-permute-start.2 = (bf16[16,5120]{1,0:T(8,128)(2,1)}, bf16[16,5120]{1,0:T(8,128)(2,1)S(1)}, u32[]{:S(2)}, u32[]{:S(2)}) collective-permute-start(bf16[16,5120]{1,0:T(8,128)(2,1)} %param.7), channel_id=1, source_target_pairs={{0,24},{1,25},{2,26},{3,27},{4,28},{5,29},{6,30},{7,31},{8,16},{9,... | collective-permute-start | bytes 491528 | tf_op jit(solution)/shard_map/ppermute | solution.py:132
  12.2 5.2 %copy-start.17 = (s32[4,128]{1,0:T(4,128)S(1)}, s32[4,128]{1,0:T(4,128)}, u32[]{:S(2)}) copy-start(s32[4,128]{1,0:T(4,128)} %param.11) | copy-start | bytes 6148
  12.2 5.9 %copy-start.14 = (bf16[16,5120]{1,0:T(8,128)(2,1)S(1)}, bf16[16,5120]{1,0:T(8,128)(2,1)}, u32[]{:S(2)}) copy-start(bf16[16,5120]{1,0:T(8,128)(2,1)} %param.7) | copy-start | bytes 491524
  13.4 13.8 %all-to-all-start = ((bf16[4,8,65,128]{3,0,2,1:T(4,128)(2,1)}), bf16[4,8,65,128]{3,0,2,1:T(4,128)(2,1)S(1)}, u32[]{:S(2)}, u32[]{:S(2)}) async-start(bf16[4,8,65,128]{3,0,2,1:T(4,128)(2,1)} %copy.58), calls=%async_computation | async-start | bytes 1064960 | tf_op jit(solution)/shard_map/all_to_all | solution.py:435
  27.3 13.1 %collective-permute-start.4 = (bf16[64,2560]{1,0:T(8,128)(2,1)S(1)}, bf16[64,2560]{1,0:T(8,128)(2,1)S(1)}, u32[]{:S(2)}, u32[]{:S(2)}) collective-permute-start(bf16[64,2560]{1,0:T(8,128)(2,1)S(1)} %get-tuple-element.79), channel_id=1, source_target_pairs={{0,4},{1,5},{2,6},{3,7},{4,0},{5,1},{6,2},{7,3},{8,12},{9,13},{10,... | collective-permute-start | bytes 983048 | tf_op jit(solution)/shard_map/ppermute | solution.py:132
  27.9 12.5 %collective-permute-start.3 = (bf16[64,2560]{1,0:T(8,128)(2,1)S(1)}, bf16[64,2560]{1,0:T(8,128)(2,1)S(1)}, u32[]{:S(2)}, u32[]{:S(2)}) collective-permute-start(bf16[64,2560]{1,0:T(8,128)(2,1)S(1)} %get-tuple-element.80), channel_id=1, source_target_pairs={{0,2},{1,3},{2,0},{3,1},{4,6},{5,7},{6,4},{7,5},{8,10},{9,11},{10,... | collective-permute-start | bytes 983048 | tf_op jit(solution)/shard_map/ppermute | solution.py:132
  29.2 8.6 %collective-permute-start.7 = (bf16[8,65,128]{2,0,1:T(8,128)(2,1)S(1)}, bf16[8,65,128]{2,0,1:T(8,128)(2,1)S(1)}, u32[]{:S(2)}, u32[]{:S(2)}) collective-permute-start(bf16[8,65,128]{2,0,1:T(8,128)(2,1)S(1)} %get-tuple-element.83), channel_id=1, source_target_pairs={{0,16},{1,17},{2,18},{3,19},{4,20},{5,21},{6,22},{7,23},{8,24},{9,... | collective-permute-start | bytes 399368 | tf_op jit(solution)/shard_map/ppermute | solution.py:132
  30.9 9.5 %collective-permute-start.6 = (bf16[8,65,128]{2,0,1:T(8,128)(2,1)S(1)}, bf16[8,65,128]{2,0,1:T(8,128)(2,1)S(1)}, u32[]{:S(2)}, u32[]{:S(2)}) collective-permute-start(bf16[8,65,128]{2,0,1:T(8,128)(2,1)S(1)} %get-tuple-element.84), channel_id=1, source_target_pairs={{0,8},{1,9},{2,10},{3,11},{4,12},{5,13},{6,14},{7,15},{8,0},{9,1},... | collective-permute-start | bytes 399368 | tf_op jit(solution)/shard_map/ppermute | solution.py:132
  37.8 2.6 %copy-start.15 = (bf16[8,65,128]{2,0,1:T(8,128)(2,1)}, bf16[8,65,128]{2,0,1:T(8,128)(2,1)S(1)}, u32[]{:S(2)}) copy-start(bf16[8,65,128]{2,0,1:T(8,128)(2,1)S(1)} %collective-permute-done.7) | copy-start | bytes 399364
  37.8 7.2 %collective-permute-start.12 = (bf16[8,65,128]{2,0,1:T(8,128)(2,1)}, bf16[8,65,128]{2,0,1:T(8,128)(2,1)}, u32[]{:S(2)}, u32[]{:S(2)}) collective-permute-start(bf16[8,65,128]{2,0,1:T(8,128)(2,1)} %get-tuple-element.82), channel_id=1, source_target_pairs={{0,24},{1,25},{2,26},{3,27},{4,28},{5,29},{6,30},{7,31},{8,16},{9,... | collective-permute-start | bytes 399368 | tf_op jit(solution)/shard_map/ppermute | solution.py:132
  40.4 0.6 copy-start.16
  41.0 22.6 %copy-start.2 = (bf16[128,2560]{1,0:T(8,128)(2,1)}, bf16[128,2560]{1,0:T(8,128)(2,1)S(1)}, u32[]{:S(2)}) copy-start(bf16[128,2560]{1,0:T(8,128)(2,1)S(1)} %pad_maximum_fusion.2.refs_4_) | copy-start | bytes 1966084
  41.0 12.1 %collective-permute-start.11 = (bf16[128,2560]{1,0:T(8,128)(2,1)S(1)}, bf16[128,2560]{1,0:T(8,128)(2,1)S(1)}, u32[]{:S(2)}, u32[]{:S(2)}) collective-permute-start(bf16[128,2560]{1,0:T(8,128)(2,1)S(1)} %pad_maximum_fusion.2.refs_4_), channel_id=1, source_target_pairs={{0,1},{1,0},{2,3},{3,2},{4,5},{5,4},{6,7},{7,6},{8,9},{9,8},{10,11... | collective-permute-start | bytes 1966088 | tf_op jit(solution)/shard_map/ppermute | solution.py:132
  41.0 17.4 %collective-permute-start.9 = (bf16[128,2560]{1,0:T(8,128)(2,1)S(1)}, bf16[128,2560]{1,0:T(8,128)(2,1)S(1)}, u32[]{:S(2)}, u32[]{:S(2)}) collective-permute-start(bf16[128,2560]{1,0:T(8,128)(2,1)S(1)} %pad_maximum_fusion.2.refs_4_), channel_id=1, source_target_pairs={{0,2},{1,3},{2,0},{3,1},{4,6},{5,7},{6,4},{7,5},{8,10},{9,11},{10,... | collective-permute-start | bytes 1966088 | tf_op jit(solution)/shard_map/ppermute | solution.py:132
  43.1 15.4 %collective-permute-start.10 = (bf16[128,2560]{1,0:T(8,128)(2,1)S(1)}, bf16[128,2560]{1,0:T(8,128)(2,1)S(1)}, u32[]{:S(2)}, u32[]{:S(2)}) collective-permute-start(bf16[128,2560]{1,0:T(8,128)(2,1)S(1)} %pad_maximum_fusion.1.refs_0_), channel_id=1, source_target_pairs={{0,1},{1,0},{2,3},{3,2},{4,5},{5,4},{6,7},{7,6},{8,9},{9,8},{10,11... | collective-permute-start | bytes 1966088 | tf_op jit(solution)/shard_map/ppermute | solution.py:132
  43.4 17.0 %collective-permute-start.8 = (bf16[128,2560]{1,0:T(8,128)(2,1)S(1)}, bf16[128,2560]{1,0:T(8,128)(2,1)}, u32[]{:S(2)}, u32[]{:S(2)}) collective-permute-start(bf16[128,2560]{1,0:T(8,128)(2,1)S(1)} %pad_maximum_fusion.1.refs_0_), channel_id=1, source_target_pairs={{0,4},{1,5},{2,6},{3,7},{4,0},{5,1},{6,2},{7,3},{8,12},{9,13},{10,... | collective-permute-start | bytes 1966088 | tf_op jit(solution)/shard_map/ppermute | solution.py:132
  46.2 1.5 copy-start.11
  47.7 1.0 copy-start.9
  51.8 1.3 copy-start
  53.1 24.2 %copy-start.4 = (bf16[128,2560]{1,0:T(8,128)(2,1)}, bf16[128,2560]{1,0:T(8,128)(2,1)S(1)}, u32[]{:S(2)}) copy-start(bf16[128,2560]{1,0:T(8,128)(2,1)S(1)} %collective-permute-done.11.refs_6_) | copy-start | bytes 1966084
  58.4 18.9 %copy-start.5 = (bf16[128,2560]{1,0:T(8,128)(2,1)}, bf16[128,2560]{1,0:T(8,128)(2,1)S(1)}, u32[]{:S(2)}) copy-start(bf16[128,2560]{1,0:T(8,128)(2,1)S(1)} %collective-permute-done.9.refs_5_) | copy-start | bytes 1966084
  60.4 27.2 %copy-start.12 = (f32[512]{0:T(512)S(1)}, f32[512]{0:T(512)}, u32[]{:S(2)}) copy-start(f32[512]{0:T(512)} %param.13) | copy-start | bytes 6148
  60.4 3.2 %collective-permute-start.13 = (bf16[128,2560]{1,0:T(8,128)(2,1)}, bf16[128,2560]{1,0:T(8,128)(2,1)S(1)}, u32[]{:S(2)}, u32[]{:S(2)}) collective-permute-start(bf16[128,2560]{1,0:T(8,128)(2,1)} %collective-permute-done.8.refs_1_), channel_id=1, source_target_pairs={{0,1},{1,0},{2,3},{3,2},{4,5},{5,4},{6,7},{7,6},{8,9},{9,8},{10,11... | collective-permute-start | bytes 1966088 | tf_op jit(solution)/shard_map/ppermute | solution.py:132
  60.4 3.2 %collective-permute-start.14 = (bf16[128,2560]{1,0:T(8,128)(2,1)S(1)}, bf16[128,2560]{1,0:T(8,128)(2,1)S(1)}, u32[]{:S(2)}, u32[]{:S(2)}) collective-permute-start(bf16[128,2560]{1,0:T(8,128)(2,1)S(1)} %collective-permute-done.9.refs_5_), channel_id=1, source_target_pairs={{0,1},{1,0},{2,3},{3,2},{4,5},{5,4},{6,7},{7,6},{8,9},{9,8},{10,11... | collective-permute-start | bytes 1966088 | tf_op jit(solution)/shard_map/ppermute | solution.py:132
  63.6 13.7 %copy-start.6 = (bf16[128,2560]{1,0:T(8,128)(2,1)}, bf16[128,2560]{1,0:T(8,128)(2,1)S(1)}, u32[]{:S(2)}) copy-start(bf16[128,2560]{1,0:T(8,128)(2,1)S(1)} %collective-permute-done.13.refs_3_) | copy-start | bytes 1966084
  63.6 13.7 %copy-start.7 = (bf16[128,2560]{1,0:T(8,128)(2,1)}, bf16[128,2560]{1,0:T(8,128)(2,1)S(1)}, u32[]{:S(2)}) copy-start(bf16[128,2560]{1,0:T(8,128)(2,1)S(1)} %collective-permute-done.14.refs_7_) | copy-start | bytes 1966084
  63.6 24.0 %copy-start.1 = (f32[512,1024]{1,0:T(8,128)S(1)}, f32[512,1024]{1,0:T(8,128)}, u32[]{:S(2)}) copy-start(f32[512,1024]{1,0:T(8,128)} %copy-done) | copy-start | bytes 6291460
  87.6 1.6 %copy-start.8 = (f32[512,1024]{1,0:T(8,128)S(1)}, f32[512,1024]{1,0:T(8,128)}, u32[]{:S(2)}) copy-start(f32[512,1024]{1,0:T(8,128)} %get-tuple-element.53.refs_2_) | copy-start | bytes 6291460
  90.5 2.7 %copy-start.3 = (bf16[512,1024]{1,0:T(8,128)(2,1)}, bf16[512,1024]{1,0:T(8,128)(2,1)S(1)}, u32[]{:S(2)}) copy-start(bf16[512,1024]{1,0:T(8,128)(2,1)S(1)} %get-tuple-element.65.grad_ref.refs_8_) | copy-start | bytes 3145732
  90.5 2.7 %collective-permute-start.15 = (bf16[512,1024]{1,0:T(8,128)(2,1)S(1)}, bf16[512,1024]{1,0:T(8,128)(2,1)S(1)}, u32[]{:S(2)}, u32[]{:S(2)}) collective-permute-start(bf16[512,1024]{1,0:T(8,128)(2,1)S(1)} %get-tuple-element.65.grad_ref.refs_8_), channel_id=1, source_target_pairs={{0,1},{1,0},{2,3},{3,2},{4,5},{5,4},{6,7},{7,6},{8,9},{9,8},{10,11... | collective-permute-start | bytes 3145736 | tf_op jit(solution)/shard_map/ppermute | solution.py:132
  93.2 1.0 copy-start.13
  104.8 31.0 %copy-start.10 = (f32[4,2,16,2560]{3,2,1,0:T(8,128)S(1)}, f32[4,2,16,2560]{3,2,1,0:T(8,128)}, u32[]{:S(2)}) copy-start(f32[4,2,16,2560]{3,2,1,0:T(8,128)} %get-tuple-element.67.own_ref) | copy-start | bytes 3932164
  104.8 17.6 %collective-permute-start.16 = (bf16[4,2,16,2560]{3,2,1,0:T(8,128)(2,1)S(1)}, bf16[4,2,16,2560]{3,2,1,0:T(8,128)(2,1)S(1)}, u32[]{:S(2)}, u32[]{:S(2)}) collective-permute-start(bf16[4,2,16,2560]{3,2,1,0:T(8,128)(2,1)S(1)} %get-tuple-element.62), channel_id=1, source_target_pairs={{0,2},{1,3},{2,0},{3,1},{4,6},{5,7},{6,4},{7,5},{8,10},{9,11},{10,... | collective-permute-start | bytes 1966088 | tf_op jit(solution)/shard_map/ppermute | solution.py:132
  105.3 17.3 %collective-permute-start.17 = (bf16[4,2,16,2560]{3,2,1,0:T(8,128)(2,1)S(1)}, bf16[4,2,16,2560]{3,2,1,0:T(8,128)(2,1)S(1)}, u32[]{:S(2)}, u32[]{:S(2)}) collective-permute-start(bf16[4,2,16,2560]{3,2,1,0:T(8,128)(2,1)S(1)} %get-tuple-element.63), channel_id=1, source_target_pairs={{0,4},{1,5},{2,6},{3,7},{4,0},{5,1},{6,2},{7,3},{8,12},{9,13},{10,... | collective-permute-start | bytes 1966088 | tf_op jit(solution)/shard_map/ppermute | solution.py:132
  106.3 29.5 %collective-permute-start.18 = (bf16[4,2,16,2560]{3,2,1,0:T(8,128)(2,1)S(1)}, bf16[4,2,16,2560]{3,2,1,0:T(8,128)(2,1)S(1)}, u32[]{:S(2)}, u32[]{:S(2)}) collective-permute-start(bf16[4,2,16,2560]{3,2,1,0:T(8,128)(2,1)S(1)} %get-tuple-element.64), channel_id=1, source_target_pairs={{0,6},{1,7},{2,4},{3,5},{4,2},{5,3},{6,0},{7,1},{8,14},{9,15},{10,... | collective-permute-start | bytes 1966088 | tf_op jit(solution)/shard_map/ppermute | solution.py:132
  136.1 7.8 %collective-permute-start.19 = (bf16[2,16,2560]{2,1,0:T(8,128)(2,1)S(1)}, bf16[2,16,2560]{2,1,0:T(8,128)(2,1)S(1)}, u32[]{:S(2)}, u32[]{:S(2)}) collective-permute-start(bf16[2,16,2560]{2,1,0:T(8,128)(2,1)S(1)} %get-tuple-element.72), channel_id=1, source_target_pairs={{0,8},{1,9},{2,10},{3,11},{4,12},{5,13},{6,14},{7,15},{8,0},{9,1},... | collective-permute-start | bytes 491528 | tf_op jit(solution)/shard_map/ppermute | solution.py:132
  136.8 14.5 %collective-permute-start.20 = (bf16[2,16,2560]{2,1,0:T(8,128)(2,1)S(1)}, bf16[2,16,2560]{2,1,0:T(8,128)(2,1)S(1)}, u32[]{:S(2)}, u32[]{:S(2)}) collective-permute-start(bf16[2,16,2560]{2,1,0:T(8,128)(2,1)S(1)} %get-tuple-element.73), channel_id=1, source_target_pairs={{0,16},{1,17},{2,18},{3,19},{4,20},{5,21},{6,22},{7,23},{8,24},{9,... | collective-permute-start | bytes 491528 | tf_op jit(solution)/shard_map/ppermute | solution.py:132
  138.0 13.3 %collective-permute-start.21 = (bf16[2,16,2560]{2,1,0:T(8,128)(2,1)S(1)}, bf16[2,16,2560]{2,1,0:T(8,128)(2,1)S(1)}, u32[]{:S(2)}, u32[]{:S(2)}) collective-permute-start(bf16[2,16,2560]{2,1,0:T(8,128)(2,1)S(1)} %get-tuple-element.74), channel_id=1, source_target_pairs={{0,24},{1,25},{2,26},{3,27},{4,28},{5,29},{6,30},{7,31},{8,16},{9,... | collective-permute-start | bytes 491528 | tf_op jit(solution)/shard_map/ppermute | solution.py:132
  151.3 1.3 collective-permute-start.22

commit v7 on v6

--- a/solution.py
+++ b/solution.py
@@ -107,7 +107,7 @@
 SLOTS = 4
 LIGHT = pl.CostEstimate(flops=1, bytes_accessed=1, transcendentals=0)
 SMALL_VMEM = 16 * 1024 * 1024
-LOGITS_VMEM = 48 * 1024 * 1024
+LOGITS_VMEM = 56 * 1024 * 1024
 LARGE_VMEM = 52 * 1024 * 1024
 
 
@@ -196,11 +196,11 @@
             out_ref[pl.ds(block * rows, rows), columns] = piece[pl.ds(i * rows, rows), :]
 
 
-def logits_kernel(rows, places, *refs):
+def logits_kernel(rows, places, width, *refs):
     count = 2 * len(places[0])
     pieces, refs = refs[:count], refs[count:]
-    w_ref, prob_ref, logits_ref, stat_ref, hidden, weight, sems, cross_ref = refs
-    half, width = w_ref.shape[0] // 2, prob_ref.shape[1]
+    w_ref, logits_ref, stat_ref, hidden, weight, sems = refs
+    half = w_ref.shape[0] // 2
     tiles = w_ref.shape[1] // width
     step = pl.program_id(0)
 
@@ -235,27 +235,20 @@
             hidden[:, half:], weight[half:, span], preferred_element_type=jnp.float32
         )
         logits_ref[:, span] = total
-        product = total * prob_ref[...]
-        folded = product[:, :128]
-        for i in range(1, width // 128):
-            folded = folded + product[:, i * 128 : (i + 1) * 128]
-        cross_ref[...] = jnp.where(step == tiles, 0.0, cross_ref[...]) + folded
 
     @pl.when(step == 2 * tiles - 1)
     def _():
         logits = logits_ref[...]
         top = jnp.max(logits, axis=1, keepdims=True)
         norm = top + jnp.log(jnp.sum(jnp.exp(logits - top), axis=1, keepdims=True))
-        cross = jnp.sum(cross_ref[...], axis=1, keepdims=True)
-        lane = lax.broadcasted_iota(jnp.int32, (1, 128), 1)
-        both = jnp.where(lane == 0, norm, jnp.where(lane == 1, cross, 0.0)).T
         tokens = logits.shape[0]
-        packed = [both[i : i + 1, t : t + 128] for i in range(2) for t in range(0, tokens, 128)]
-        stat_ref[...] = jnp.broadcast_to(jnp.concatenate(packed, axis=0)[None], stat_ref.shape)
+        norm = jnp.broadcast_to(norm, (tokens, 128)).T
+        packed = jnp.concatenate([norm[:1, t : t + 128] for t in range(0, tokens, 128)], axis=0)
+        stat_ref[...] = jnp.broadcast_to(packed[None], stat_ref.shape)
 
 
 def grad_kernel(
-    rows, pos_ref, stat_ref, logits_ref, prob_ref, weight_ref, entropy_ref, grad_ref, loss_ref
+    rows, pos_ref, stat_ref, logits_ref, prob_ref, weight_ref, entropy_ref, grad_ref, loss_ref, cross_ref
 ):
     tokens = logits_ref.shape[0]
     devices = tokens // rows
@@ -264,31 +257,29 @@
     pos = [pos_ref[i] for i in range(3)]
     rank = pos_ref[3]
     lane = lax.broadcasted_iota(jnp.int32, (1, 128), 1)
-    per_stat = stat_ref.shape[1] // 2
-    norms, crosses = [
-        jnp.concatenate([stat_ref[:, i * per_stat + t, :] for t in range(per_stat)], axis=1) for i in range(2)
-    ]
-    stat = jnp.concatenate(
-        [norms, crosses, jnp.zeros((128 - 2 * devices, tokens), jnp.float32)], axis=0
-    ).T
+    norms = jnp.concatenate([stat_ref[:, t, :] for t in range(stat_ref.shape[1])], axis=1)
+    stat = jnp.concatenate([norms, jnp.zeros((128 - devices, tokens), jnp.float32)], axis=0).T
     pairs = [(0, 2), (1, 0), (2, 1)] + [(3 + i, 3 + i) for i in range(layer_bits)]
     for index_bit, block_bit in pairs:
         halves = stat.reshape(devices >> (block_bit + 1), 2, rows << block_bit, 128)
         swapped = jnp.stack([halves[:, 1], halves[:, 0]], axis=1).reshape(tokens, 128)
         stat = jnp.where(((lane ^ rank) >> index_bit) & 1 == 1, swapped, stat)
     is_norm = lane < devices
-    is_cross = (lane >= devices) & (lane < 2 * devices)
     top = jnp.max(jnp.where(is_norm, stat, -jnp.inf), axis=1, keepdims=True)
     total = jnp.sum(jnp.where(is_norm, jnp.exp(stat - top), 0.0), axis=1, keepdims=True)
     log_norm = top + jnp.log(total)
-    cross = jnp.sum(jnp.where(is_cross, stat, 0.0), axis=1, keepdims=True)
-    loss_ref[...] = entropy_ref[...] - cross[:rows] + log_norm[:rows]
+    loss_ref[...] = entropy_ref[...] + log_norm[:rows]
+    crosses = []
     where_token = token_places(pos, rows, side)
     for k in range(layers):
         span = pl.ds(k * side, side)
         weight = pick_column(lane == where_token, weight_ref[pos[2] ^ k])
-        student = jnp.exp(logits_ref[span, :] - log_norm[k * side : (k + 1) * side])
-        grad_ref[span, :] = (weight * (student - prob_ref[span, :])).astype(grad_ref.dtype)
+        logits, prob = logits_ref[span, :], prob_ref[span, :]
+        crosses.append(jnp.sum(prob * logits, axis=1, keepdims=True))
+        student = jnp.exp(logits - log_norm[k * side : (k + 1) * side])
+        grad_ref[span, :] = (weight * (student - prob)).astype(grad_ref.dtype)
+    cross = jnp.broadcast_to(jnp.concatenate(crosses, axis=0), (tokens, 128)).T
+    cross_ref[...] = cross[:1]
 
 
 def partial_kernel(rows, core_ref, grad_ref, sib_ref, w_ref, sib_w_ref, *refs):
@@ -356,14 +347,14 @@
     return jnp.stack([high, middle, low]).astype(jnp.bfloat16)
 
 
-def pack_teacher(teacher_logits, block_lists, places, layer):
+def pack_teacher(teacher_logits, block_lists, places):
     blocks, listed_count, stored, side = teacher_logits.shape
     n = lax.axis_size("vocab")
     rank = lax.axis_index("vocab")
     owner = block_lists // places
     earlier = jnp.tril(jnp.ones((listed_count, listed_count), jnp.bool_), -1)
     slot = jnp.sum((owner[:, :, None] == owner[:, None, :]) & earlier, axis=2, dtype=jnp.int32)
-    code = (owner ^ (layer * GROUP)) * SLOTS + slot
+    code = owner * SLOTS + slot
     picker = (code[:, None, :] == jnp.arange(n * SLOTS, dtype=jnp.int32)[None, :, None]).astype(jnp.bfloat16)
     packed = jnp.einsum(
         "tsk,tkrc->tsrc", picker, teacher_logits, preferred_element_type=jnp.float32
@@ -379,7 +370,7 @@
     payload = jnp.concatenate(
         [packed.reshape(n, -1, side), jnp.broadcast_to(stat, (n, 1, side))], axis=1
     )
-    mine = (owner * SLOTS + slot)[:, None, :] == rank * SLOTS + jnp.arange(SLOTS, dtype=jnp.int32)[None, :, None]
+    mine = code[:, None, :] == rank * SLOTS + jnp.arange(SLOTS, dtype=jnp.int32)[None, :, None]
     place = jnp.sum(jnp.where(mine, (block_lists % places + 1)[:, None, :], 0), axis=2) - 1
     return payload.reshape(n // GROUP, GROUP, -1, side), place.astype(jnp.int32)
 
@@ -403,11 +394,11 @@
     return arrived_blocks, arrived_stat
 
 
-def by_distance(x, layer, layers):
-    shape = x.shape
-    for i in range((layers - 1).bit_length()):
-        pairs = x.reshape(shape[0], layers >> (i + 1), 2, -1)
-        x = jnp.where((layer >> i) & 1 == 1, pairs[:, :, ::-1], pairs).reshape(shape)
+def by_device(x, rank):
+    n = x.shape[0]
+    for i in range((n - 1).bit_length()):
+        pairs = x.reshape(n >> (i + 1), 2, -1)
+        x = jnp.where((rank >> i) & 1 == 1, pairs[:, ::-1], pairs).reshape(x.shape)
     return x
 
 
@@ -426,31 +417,63 @@
     core, chip, layer = rank % CORES, (rank // CORES) % CHIPS, rank // GROUP
     pos = jnp.stack([core, chip, layer, rank]).astype(jnp.int32)
     unlisted = float(n * slab - side * listed_count)
+    across = [[o * GROUP + i for o in range(layers)] for i in range(GROUP)]
     in_layer = [[o * GROUP + i for i in range(GROUP)] for o in range(layers)]
     X, Y = CORES, 2 * CORES
 
     column = [hidden_states] + [shift(hidden_states, k * GROUP) for k in range(1, layers)]
     sib_w = shift(head_weight, 1)
-    payload, place = pack_teacher(teacher_logits, block_lists, slab // side, layer)
+    payload, place = pack_teacher(teacher_logits, block_lists, slab // side)
     payload = lax.all_to_all(
         payload, "vocab", split_axis=1, concat_axis=1, axis_index_groups=in_layer, tiled=True
     )
-    column = jnp.concatenate(column, axis=0)
-    column, payload = lax.optimization_barrier((column, payload))
+    column = lax.optimization_barrier(jnp.concatenate(column, axis=0))
     first, second = [column[:, :half]], [column[:, half:]]
     first_x, second_y = shift(first[0], X), shift(second[0], Y)
-    crossed = [payload[k] for k in range(layers)]
-    early = [shift(crossed[k], k * GROUP) for k in range(1, layers - 1)]
-    first_x, second_y, sib_w, *early = lax.optimization_barrier((first_x, second_y, sib_w, *early))
+    first_x, second_y, sib_w, payload = lax.optimization_barrier((first_x, second_y, sib_w, payload))
     first = [jnp.concatenate([first[0], first_x], axis=0)]
     second = [jnp.concatenate([second[0], second_y], axis=0)]
     first.append(shift(first[0], Y))
     second.append(shift(second[0], X))
-    late = [shift(crossed[k], k * GROUP) for k in range(max(layers - 1, 1), layers)]
-    arrived = jnp.stack([crossed[0], *early, *late]).reshape(n, -1, side)
-    arrived_blocks, arrived_stat = unpack_teacher(arrived, blocks, stored)
     first_sib, second_sib = [shift(first[0], 1)], [shift(second[0], 1)]
-
+    arrived = lax.all_to_all(
+        payload, "vocab", split_axis=0, concat_axis=0, axis_index_groups=across, tiled=True
+    )
+    first[1], second[1], first_sib[0], second_sib[0], arrived = lax.optimization_barrier(
+        (first[1], second[1], first_sib[0], second_sib[0], arrived)
+    )
+    first_sib.append(shift(first[1], 1))
+    second_sib.append(shift(second[1], 1))
+    pieces = first + first_sib + second + second_sib
+    places = piece_blocks(layers)
+    width = 256 if slab % 256 == 0 else 128
+    tiles = slab // width
+    whole = lambda t: (0, 0)
+    logits, stat = pl.pallas_call(
+        functools.partial(logits_kernel, rows, places, width),
+        grid=(2 * tiles,),
+        out_shape=[
+            jax.ShapeDtypeStruct((tokens, slab), f32),
+            jax.ShapeDtypeStruct((n, tokens // 128, 128), f32),
+        ],
+        in_specs=[vmem_spec()] * len(pieces)
+        + [hbm_spec()],
+        out_specs=[
+            pl.BlockSpec((tokens, slab), whole),
+            pl.BlockSpec((n, tokens // 128, 128), lambda t: (0, 0, 0)),
+        ],
+        scratch_shapes=[
+            pltpu.VMEM((tokens, depth), bf16),
+            pltpu.VMEM((depth, slab), bf16),
+            pltpu.SemaphoreType.DMA((2,)),
+        ],
+        compiler_params=kernel_params(LOGITS_VMEM),
+        cost_estimate=LIGHT,
+        name="logits",
+    )(*pieces, head_weight)
+    stat, arrived = lax.optimization_barrier((stat, arrived))
+    stat = lax.all_to_all(stat, "vocab", split_axis=0, concat_axis=0, tiled=True)
+    arrived_blocks, arrived_stat = unpack_teacher(arrived.reshape(n, -1, side), blocks, stored)
     prob, entropy = pl.pallas_call(
         lambda *refs: teacher_kernel(unlisted, rows, *refs),
         out_shape=(
@@ -467,54 +490,19 @@
         place,
         arrived_blocks,
         arrived_stat,
-        by_distance(row_reader, layer, layers).reshape(blocks, 1, side),
+        row_reader.reshape(blocks, 1, side),
         tail_mass.reshape(blocks, 1, side),
     )
 
-    first[1], second[1], first_sib[0], second_sib[0], prob = lax.optimization_barrier(
-        (first[1], second[1], first_sib[0], second_sib[0], prob)
-    )
-    first_sib.append(shift(first[1], 1))
-    second_sib.append(shift(second[1], 1))
-    pieces = first + first_sib + second + second_sib
-    places = piece_blocks(layers)
-
-    width = 256 if slab % 256 == 0 else 128
-    tiles = slab // width
-    whole = lambda t: (0, 0)
-    logits, stat = pl.pallas_call(
-        functools.partial(logits_kernel, rows, places),
-        grid=(2 * tiles,),
-        out_shape=[
-            jax.ShapeDtypeStruct((tokens, slab), f32),
-            jax.ShapeDtypeStruct((n, 2 * tokens // 128, 128), f32),
-        ],
-        in_specs=[vmem_spec()] * len(pieces)
-        + [hbm_spec(), pl.BlockSpec((tokens, width), lambda t: (0, jnp.maximum(t - tiles, 0)))],
-        out_specs=[
-            pl.BlockSpec((tokens, slab), whole),
-            pl.BlockSpec((n, 2 * tokens // 128, 128), lambda t: (0, 0, 0)),
-        ],
-        scratch_shapes=[
-            pltpu.VMEM((tokens, depth), bf16),
-            pltpu.VMEM((depth, slab), bf16),
-            pltpu.SemaphoreType.DMA((2,)),
-            pltpu.VMEM((tokens, 128), f32),
-        ],
-        compiler_params=kernel_params(LOGITS_VMEM),
-        cost_estimate=LIGHT,
-        name="logits",
-    )(*pieces, head_weight, prob)
-    stat = lax.all_to_all(stat, "vocab", split_axis=0, concat_axis=0, tiled=True)
-
-    grad, loss = pl.pallas_call(
+    grad, loss, cross = pl.pallas_call(
         lambda *refs: grad_kernel(rows, *refs),
         out_shape=(
             jax.ShapeDtypeStruct((tokens, slab), bf16),
             jax.ShapeDtypeStruct((rows, side), f32),
+            jax.ShapeDtypeStruct((1, tokens), f32),
         ),
         in_specs=[smem_spec()] + [vmem_spec()] * 5,
-        out_specs=(vmem_spec(), vmem_spec()),
+        out_specs=[vmem_spec()] * 3,
         compiler_params=kernel_params(),
         cost_estimate=LIGHT,
         name="grad_logits",
@@ -540,7 +528,10 @@
         cost_estimate=LIGHT,
         name="grad_hidden_partial",
     )(pos, grad, sib_grad, head_weight, sib_w)
-    *partial, late_grad = lax.optimization_barrier((*partial, grad))
+    *partial, late_grad, cross = lax.optimization_barrier((*partial, grad, cross))
+    cross = cross.reshape(layers, CORES, CHIPS, rows).transpose(0, 2, 1, 3).reshape(n, rows)
+    cross = lax.all_to_all(by_device(cross, rank), "vocab", split_axis=0, concat_axis=0, tiled=True)
+    token_loss = loss[:, 0] - jnp.sum(cross, axis=0)
     arrived = [shift(partial[j], j * CORES) for j in range(1, CHIPS)]
 
     head_tile = half // 2
@@ -560,7 +551,7 @@
         cost_estimate=LIGHT,
         name="grad_head",
     )(*pieces, late_grad)
-    arrived, grad_head = lax.optimization_barrier((arrived, grad_head))
+    arrived, grad_head, token_loss = lax.optimization_barrier((arrived, grad_head, token_loss))
 
     summed = pl.pallas_call(
         chip_sum_kernel,
@@ -586,7 +577,7 @@
     other = shift(theirs, 1)
 
     low, high = jnp.where(core == 0, mine, other), jnp.where(core == 0, other, mine)
-    return loss[:, 0], grad_head, jnp.concatenate([low, high], axis=1)
+    return token_loss, grad_head, jnp.concatenate([low, high], axis=1)
 
 
 def fits_levels(hidden_states, teacher_logits):

time: 154 us -> 164 us (1.065)
  blocking collectives: 10.2 us -> 0 us
  starting transfers between devices: 30.1 us -> 37.5 us
  waiting for transfers between devices: 54.6 us -> 61.8 us
  local copies, waits for them, and re-layouts: 10.5 us -> 13.1 us
  Pallas kernels: 39.6 us -> 41.6 us
    all_to_all x0 -> x3, waiting for transfers between devices: none -> 14.7 us  [the longest x1 12.6 us: levels_plan(): lax.all_to_all(by_device(cross, rank), 'vocab', split_axis=0, concat_axis...]
    all_to_all x0 -> x3, starting transfers between devices: none -> 13.7 us  [the longest x1 5.1 us: levels_plan(): lax.all_to_all(stat, 'vocab', split_axis=0, concat_axis=0, tiled=True)]
    all_to_all x1 -> x0, blocking collectives: 10.2 us -> none  [levels_plan(): lax.all_to_all(stat, 'vocab', split_axis=0, concat_axis=0, tiled=True)]
    ppermute x23 -> x20, starting transfers between devices: 26.1 us -> 19.9 us  [shift(): return lax.ppermute(x, 'vocab', [(i, i ^ distance) for i in range(n)])]
    ppermute x23 -> x20, waiting for transfers between devices: 45.5 us -> 40.7 us  [shift(): return lax.ppermute(x, 'vocab', [(i, i ^ distance) for i in range(n)])]
    all_to_all x1, waiting for transfers between devices: 9.1 us -> 6.41 us  [levels_plan(): lax.all_to_all(payload, 'vocab', split_axis=1, concat_axis=1, axis_index_...]
    unnamed x36 -> x40, local copies, waits for them, and re-layouts: 5.52 us -> 7.82 us
  transfers between devices with their start and end apart: 24 -> 24, of which waited for: 14 -> 13; matrix products, arithmetic and copies ran while one was open for 8% -> 6% of each run, Pallas kernels for 9% -> 8%
where the time goes in v7:
time: 164 us; the launch traced here: 163 us
  waiting for transfers between devices  61.8 us (38%)
  Pallas kernels  41.6 us (25%)
  starting transfers between devices  37.5 us (23%)
  local copies, waits for them, and re-layouts  13.1 us (8%)
  other arithmetic  6.15 us (4%)
    ppermute x20, waiting for transfers between devices, shift(): return lax.ppermute(x, 'vocab', [(i, i ^ distance) for i in range(n)])  40.7 us
    ppermute x20, starting transfers between devices, shift(): return lax.ppermute(x, 'vocab', [(i, i ^ distance) for i in range(n)])  19.9 us
    pallas_call x1, Pallas kernels, levels_plan(): pl.pallas_call(functools.partial(logits_kernel, rows, places, width), gri...  14 us
    all_to_all x1, waiting for transfers between devices, levels_plan(): lax.all_to_all(by_device(cross, rank), 'vocab', split_axis=0, concat_axis...  12.6 us
    pallas_call x1, Pallas kernels, levels_plan(): pl.pallas_call(functools.partial(partial_kernel, rows), grid_spec=pltpu.P...  10.7 us
    pallas_call x1, Pallas kernels, levels_plan(): pl.pallas_call(functools.partial(head_kernel, rows, places), grid=(4,), i...  10.6 us
    unnamed x40, local copies, waits for them, and re-layouts  7.82 us
    all_to_all x1, waiting for transfers between devices, levels_plan(): lax.all_to_all(payload, 'vocab', split_axis=1, concat_axis=1, axis_index_...  6.41 us
  transfers between devices with their start and end apart: 24, of which 13 were waited for; matrix products, arithmetic and copies ran while one was open for 6% of the time, Pallas kernels for 8%

profile of v7, /device:TPU:0, one launch (start us, length us, event | category | flops | bytes accessed | tf_op | source)
XLA Modules:
  0.0 162.6 jit_solution(7064905121555925071)
XLA Ops:
  0.6 0.5 collective-permute-start.5
  1.1 3.7 %collective-permute-start.1 = (bf16[16,5120]{1,0:T(8,128)(2,1)}, bf16[16,5120]{1,0:T(8,128)(2,1)S(1)}, u32[]{:S(2)}, u32[]{:S(2)}) collective-permute-start(bf16[16,5120]{1,0:T(8,128)(2,1)} %param.7), channel_id=1, source_target_pairs={{0,16},{1,17},{2,18},{3,19},{4,20},{5,21},{6,22},{7,23},{8,24},{9,... | collective-permute-start | bytes 491528 | tf_op jit(solution)/shard_map/ppermute | solution.py:132
  4.8 1.6 collective-permute-start
  6.4 1.2 reduce_max.14
  7.6 1.5 fusion.1
  9.1 0.7 fusion.8
  9.8 0.2 convert_reduce_fusion
  10.1 1.4 convolution_convert_fusion
  11.5 0.1 convert_element_type.31
  11.6 0.4 copy.42
  12.2 1.2 copy.44
  13.4 3.9 %all-to-all-start = ((bf16[4,8,65,128]{3,0,2,1:T(4,128)(2,1)}), bf16[4,8,65,128]{3,0,2,1:T(4,128)(2,1)S(1)}, u32[]{:S(2)}, u32[]{:S(2)}) async-start(bf16[4,8,65,128]{3,0,2,1:T(4,128)(2,1)} %copy.44), calls=%async_computation | async-start | bytes 1064960 | tf_op jit(solution)/shard_map/all_to_all | solution.py:427
  17.4 0.7 collective-permute-done.2
  18.2 1.6 collective-permute-start.4
  19.8 1.5 collective-permute-start.3
  21.2 6.4 %all-to-all-done = bf16[4,8,65,128]{3,0,2,1:T(4,128)(2,1)S(1)} async-done(((bf16[4,8,65,128]{3,0,2,1:T(4,128)(2,1)}), bf16[4,8,65,128]{3,0,2,1:T(4,128)(2,1)S(1)}, u32[]{:S(2)}, u32[]{:S(2)}) %all-to-all-start) | async-done | bytes 532512 | tf_op jit(solution)/shard_map/all_to_all | solution.py:427
  27.7 5.6 %collective-permute-done.4 = bf16[64,2560]{1,0:T(8,128)(2,1)S(1)} collective-permute-done((bf16[64,2560]{1,0:T(8,128)(2,1)S(1)}, bf16[64,2560]{1,0:T(8,128)(2,1)S(1)}, u32[]{:S(2)}, u32[]{:S(2)}) %collective-permute-start.4) | collective-permute-done | bytes 327712 | tf_op jit(solution)/shard_map/ppermute | solution.py:132
  33.5 1.5 collective-permute-start.7
  35.0 0.9 copy.45
  35.8 4.9 %all-to-all-start.1 = ((bf16[4,8,65,128]{3,1,2,0:T(8,128)(2,1)}), bf16[4,8,65,128]{3,1,2,0:T(8,128)(2,1)S(1)}, u32[]{:S(2)}, u32[]{:S(2)}) async-start(bf16[4,8,65,128]{3,1,2,0:T(8,128)(2,1)} %copy.45), calls=%async_computation.1 | async-start | bytes 1064960 | tf_op jit(solution)/shard_map/all_to_all | solution.py:439
  40.9 0.6 collective-permute-start.6
  41.5 9.2 %collective-permute-done.7.refs_5_ = bf16[128,2560]{1,0:T(8,128)(2,1)} collective-permute-done((bf16[128,2560]{1,0:T(8,128)(2,1)S(1)}, bf16[128,2560]{1,0:T(8,128)(2,1)}, u32[]{:S(2)}, u32[]{:S(2)}) %collective-permute-start.7) | collective-permute-done | bytes 655392 | tf_op jit(solution)/shard_map/ppermute | solution.py:132
  50.7 7.3 %collective-permute-done.6.refs_1_ = bf16[128,2560]{1,0:T(8,128)(2,1)S(1)} collective-permute-done((bf16[128,2560]{1,0:T(8,128)(2,1)S(1)}, bf16[128,2560]{1,0:T(8,128)(2,1)S(1)}, u32[]{:S(2)}, u32[]{:S(2)}) %collective-permute-start.6) | collective-permute-done | bytes 655392 | tf_op jit(solution)/shard_map/ppermute | solution.py:132
  58.0 0.5 collective-permute-start.11
  58.6 0.2 select_reduce_fusion
  58.8 1.5 collective-permute-done.10.refs_3_
  60.4 1.0 collective-permute-done.11.refs_7_
  61.4 14.0 %logits.1 = (f32[512,1024]{1,0:T(8,128)}, f32[32,4,128]{2,1,0:T(4,128)}) custom-call(bf16[128,2560]{1,0:T(8,128)(2,1)} %copy-done, bf16[128,2560]{1,0:T(8,128)(2,1)} %copy-done.5, bf16[128,2560]{1,0:T(8,128)(2,1)} %copy-done.3, bf16[128,2560]{1,0:T(8,128)(2,1)} %copy-done.18, bf16[128,2560]{1,0:T(8,128)(2,1)} %copy-done.17, ...), custom_call_target="tpu_custom_call" | custom-call | flops 1 | bytes 1 | tf_op jit(solution)/shard_map/logits/pallas_call | solution.py:452
  75.5 5.1 %all-to-all-start.2 = ((f32[32,4,128]{2,1,0:T(4,128)}), f32[32,4,128]{2,1,0:T(4,128)S(1)}, u32[]{:S(2)}, u32[]{:S(2)}) async-start(f32[32,4,128]{2,1,0:T(4,128)} %get-tuple-element.51), calls=%async_computation.2 | async-start | bytes 131072 | tf_op jit(solution)/shard_map/all_to_all | solution.py:475
  80.7 0.3 copy.47
  81.2 0.1 copy.49
  81.3 0.1 reshape.208
  81.4 3.1 %teacher_prob.1 = (f32[512,1024]{1,0:T(8,128)S(1)}, f32[16,128]{1,0:T(8,128)S(1)}) custom-call(s32[4]{0:T(128)S(1)} %pad_add_fusion.refs_0_.core_ref, s32[4,4]{1,0:T(4,128)S(1)} %broadcast_add_fusion.refs_1_, bf16[4,4,128,128]{3,2,1,0:T(8,128)(2,1)S(1)} %bitcast.42, f32[2,4,1,128]{3,2,1,0:T(1,128)S(1)} %bitcast.43, s32[4,1,128]{2,1,0:T(1,128)S(1)} %bitcast.44, ...), custom_call_target="tpu_custom_call" | custom-call | flops 1 | bytes 1 | tf_op jit(solution)/shard_map/teacher_prob/pallas_call | solution.py:477
  84.5 1.4 copy-done.8
  85.8 2.1 %all-to-all-done.2.refs_1_ = f32[32,4,128]{2,1,0:T(4,128)S(1)} async-done(((f32[32,4,128]{2,1,0:T(4,128)}), f32[32,4,128]{2,1,0:T(4,128)S(1)}, u32[]{:S(2)}, u32[]{:S(2)}) %all-to-all-start.2) | async-done | bytes 65568 | tf_op jit(solution)/shard_map/all_to_all | solution.py:475
  88.0 1.6 copy-done.7
  89.6 1.6 copy-done.9
  91.2 1.6 grad_logits.1
  92.8 0.2 collective-permute-start.12
  93.0 2.7 %collective-permute-done.12.sib_ref = bf16[512,1024]{1,0:T(8,128)(2,1)} collective-permute-done((bf16[512,1024]{1,0:T(8,128)(2,1)S(1)}, bf16[512,1024]{1,0:T(8,128)(2,1)}, u32[]{:S(2)}, u32[]{:S(2)}) %collective-permute-start.12) | collective-permute-done | bytes 1048608 | tf_op jit(solution)/shard_map/ppermute | solution.py:132
  95.6 10.7 %grad_hidden_partial.1 = (f32[4,2,16,2560]{3,2,1,0:T(8,128)}, bf16[4,2,16,2560]{3,2,1,0:T(8,128)(2,1)S(1)}, bf16[4,2,16,2560]{3,2,1,0:T(8,128)(2,1)S(1)}, bf16[4,2,16,2560]{3,2,1,0:T(8,128)(2,1)S(1)}) custom-call(s32[4]{0:T(128)S(1)} %pad_add_fusion.refs_0_.core_ref, bf16[512,1024]{1,0:T(8,128)(2,1)} %copy-done.2, ...), custom_call_target="tpu_custom_call" | custom-call | flops 1 | bytes 1 | tf_op jit(solution)/shard_map/grad_hidden_partial/pallas_call | solution.py:514
  106.3 0.9 copy-done.14
  107.2 0.8 copy-done.15
  108.0 0.2 copy-done.16
  108.2 0.5 broadcast.63
  108.7 0.7 reduce.7
  109.8 0.5 collective-permute-start.13
  110.3 0.9 collective-permute-start.14
  111.1 2.2 %collective-permute-start.15 = (bf16[4,2,16,2560]{3,2,1,0:T(8,128)(2,1)}, bf16[4,2,16,2560]{3,2,1,0:T(8,128)(2,1)}, u32[]{:S(2)}, u32[]{:S(2)}) collective-permute-start(bf16[4,2,16,2560]{3,2,1,0:T(8,128)(2,1)} %copy-done.14), channel_id=1, source_target_pairs={{0,6},{1,7},{2,4},{3,5},{4,2},{5,3},{6,0},{7,1},{8,14},{9,15},{10,... | collective-permute-start | bytes 1966088 | tf_op jit(solution)/shard_map/ppermute | solution.py:132
  113.6 0.7 all_to_all.18
  114.2 3.7 %all-to-all-start.3 = ((f32[32,1,16]{2,1,0:T(1,128)}), f32[32,1,16]{2,1,0:T(1,128)S(1)}, u32[]{:S(2)}, u32[]{:S(2)}) async-start(f32[32,1,16]{2,1,0:T(1,128)} %bitcast.23), calls=%async_computation.3 | async-start | bytes 32768 | tf_op jit(solution)/shard_map/all_to_all | solution.py:533
  118.0 0.1 slice_reduce_fusion
  118.1 10.6 %grad_head.1 = bf16[5120,1024]{1,0:T(8,128)(2,1)} custom-call(bf16[128,2560]{1,0:T(8,128)(2,1)S(1)} %copy-done.1, bf16[128,2560]{1,0:T(8,128)(2,1)S(1)} %copy-done.6, bf16[128,2560]{1,0:T(8,128)(2,1)S(1)} %copy-done.4, bf16[128,2560]{1,0:T(8,128)(2,1)} %copy-done.18, bf16[128,2560]{1,0:T(8,128)(2,1)} %copy-done.17, ...), custom_call_target="tpu_custom_call" | custom-call | flops 1 | bytes 1 | tf_op jit(solution)/shard_map/grad_head/pallas_call | solution.py:539
  128.7 12.6 %all-to-all-done.3 = f32[32,1,16]{2,1,0:T(1,128)S(1)} async-done(((f32[32,1,16]{2,1,0:T(1,128)}), f32[32,1,16]{2,1,0:T(1,128)S(1)}, u32[]{:S(2)}, u32[]{:S(2)}) %all-to-all-start.3) | async-done | bytes 2080 | tf_op jit(solution)/shard_map/all_to_all | solution.py:533
  141.3 0.5 sub.60
  141.9 1.3 copy-done.10
  143.2 1.6 chip_sum.1
  144.7 0.7 collective-permute-start.16
  145.5 2.4 %collective-permute-start.17 = (bf16[2,16,2560]{2,1,0:T(8,128)(2,1)S(1)}, bf16[2,16,2560]{2,1,0:T(8,128)(2,1)S(1)}, u32[]{:S(2)}, u32[]{:S(2)}) collective-permute-start(bf16[2,16,2560]{2,1,0:T(8,128)(2,1)S(1)} %get-tuple-element.77), channel_id=1, source_target_pairs={{0,16},{1,17},{2,18},{3,19},{4,20},{5,21},{6,22},{7,23},{8,24},{9,... | collective-permute-start | bytes 491528 | tf_op jit(solution)/shard_map/ppermute | solution.py:132
  147.9 1.3 collective-permute-start.18
  149.2 4.7 %collective-permute-done.16.refs_0_ = bf16[2,16,2560]{2,1,0:T(8,128)(2,1)S(1)} collective-permute-done((bf16[2,16,2560]{2,1,0:T(8,128)(2,1)S(1)}, bf16[2,16,2560]{2,1,0:T(8,128)(2,1)S(1)}, u32[]{:S(2)}, u32[]{:S(2)}) %collective-permute-start.16) | collective-permute-done | bytes 163872 | tf_op jit(solution)/shard_map/ppermute | solution.py:132
  153.9 6.7 %collective-permute-done.17.refs_1_ = bf16[2,16,2560]{2,1,0:T(8,128)(2,1)S(1)} collective-permute-done((bf16[2,16,2560]{2,1,0:T(8,128)(2,1)S(1)}, bf16[2,16,2560]{2,1,0:T(8,128)(2,1)S(1)}, u32[]{:S(2)}, u32[]{:S(2)}) %collective-permute-start.17) | collective-permute-done | bytes 163872 | tf_op jit(solution)/shard_map/ppermute | solution.py:132
  160.7 1.3 collective-permute-done.19
  162.0 0.7 pad_maximum_fusion.4
  (91 shorter events, 1.8 us)
Async XLA Ops:
  0.6 32.7 %collective-permute-start.5 = (bf16[5120,1024]{1,0:T(8,128)(2,1)}, bf16[5120,1024]{1,0:T(8,128)(2,1)}, u32[]{:S(2)}, u32[]{:S(2)}) collective-permute-start(bf16[5120,1024]{1,0:T(8,128)(2,1)} %w_ref.1), channel_id=1, source_target_pairs={{0,1},{1,0},{2,3},{3,2},{4,5},{5,4},{6,7},{7,6},{8,9},{9,8},{10,11... | collective-permute-start | bytes 31457288 | tf_op jit(solution)/shard_map/ppermute | solution.py:132
  1.1 16.2 %collective-permute-start.1 = (bf16[16,5120]{1,0:T(8,128)(2,1)}, bf16[16,5120]{1,0:T(8,128)(2,1)S(1)}, u32[]{:S(2)}, u32[]{:S(2)}) collective-permute-start(bf16[16,5120]{1,0:T(8,128)(2,1)} %param.7), channel_id=1, source_target_pairs={{0,16},{1,17},{2,18},{3,19},{4,20},{5,21},{6,22},{7,23},{8,24},{9,... | collective-permute-start | bytes 491528 | tf_op jit(solution)/shard_map/ppermute | solution.py:132
  4.8 12.5 %collective-permute-start = (bf16[16,5120]{1,0:T(8,128)(2,1)}, bf16[16,5120]{1,0:T(8,128)(2,1)S(1)}, u32[]{:S(2)}, u32[]{:S(2)}) collective-permute-start(bf16[16,5120]{1,0:T(8,128)(2,1)} %param.7), channel_id=1, source_target_pairs={{0,8},{1,9},{2,10},{3,11},{4,12},{5,13},{6,14},{7,15},{8,0},{9,1},... | collective-permute-start | bytes 491528 | tf_op jit(solution)/shard_map/ppermute | solution.py:132
  6.4 11.7 %collective-permute-start.2 = (bf16[16,5120]{1,0:T(8,128)(2,1)}, bf16[16,5120]{1,0:T(8,128)(2,1)S(1)}, u32[]{:S(2)}, u32[]{:S(2)}) collective-permute-start(bf16[16,5120]{1,0:T(8,128)(2,1)} %param.7), channel_id=1, source_target_pairs={{0,24},{1,25},{2,26},{3,27},{4,28},{5,29},{6,30},{7,31},{8,16},{9,... | collective-permute-start | bytes 491528 | tf_op jit(solution)/shard_map/ppermute | solution.py:132
  12.2 5.9 %copy-start.19 = (bf16[16,5120]{1,0:T(8,128)(2,1)S(1)}, bf16[16,5120]{1,0:T(8,128)(2,1)}, u32[]{:S(2)}) copy-start(bf16[16,5120]{1,0:T(8,128)(2,1)} %param.7) | copy-start | bytes 491524
  13.4 14.3 %all-to-all-start = ((bf16[4,8,65,128]{3,0,2,1:T(4,128)(2,1)}), bf16[4,8,65,128]{3,0,2,1:T(4,128)(2,1)S(1)}, u32[]{:S(2)}, u32[]{:S(2)}) async-start(bf16[4,8,65,128]{3,0,2,1:T(4,128)(2,1)} %copy.44), calls=%async_computation | async-start | bytes 1064960 | tf_op jit(solution)/shard_map/all_to_all | solution.py:427
  18.2 15.1 %collective-permute-start.4 = (bf16[64,2560]{1,0:T(8,128)(2,1)S(1)}, bf16[64,2560]{1,0:T(8,128)(2,1)S(1)}, u32[]{:S(2)}, u32[]{:S(2)}) collective-permute-start(bf16[64,2560]{1,0:T(8,128)(2,1)S(1)} %get-tuple-element.83), channel_id=1, source_target_pairs={{0,4},{1,5},{2,6},{3,7},{4,0},{5,1},{6,2},{7,3},{8,12},{9,13},{10,... | collective-permute-start | bytes 983048 | tf_op jit(solution)/shard_map/ppermute | solution.py:132
  19.8 13.6 %collective-permute-start.3 = (bf16[64,2560]{1,0:T(8,128)(2,1)S(1)}, bf16[64,2560]{1,0:T(8,128)(2,1)S(1)}, u32[]{:S(2)}, u32[]{:S(2)}) collective-permute-start(bf16[64,2560]{1,0:T(8,128)(2,1)S(1)} %get-tuple-element.84), channel_id=1, source_target_pairs={{0,2},{1,3},{2,0},{3,1},{4,6},{5,7},{6,4},{7,5},{8,10},{9,11},{10,... | collective-permute-start | bytes 983048 | tf_op jit(solution)/shard_map/ppermute | solution.py:132
  33.4 7.4 %copy-start.17 = (bf16[128,2560]{1,0:T(8,128)(2,1)}, bf16[128,2560]{1,0:T(8,128)(2,1)S(1)}, u32[]{:S(2)}) copy-start(bf16[128,2560]{1,0:T(8,128)(2,1)S(1)} %pad_maximum_fusion.2.refs_4_) | copy-start | bytes 1966084
  33.4 8.1 %collective-permute-start.9 = (bf16[128,2560]{1,0:T(8,128)(2,1)S(1)}, bf16[128,2560]{1,0:T(8,128)(2,1)}, u32[]{:S(2)}, u32[]{:S(2)}) collective-permute-start(bf16[128,2560]{1,0:T(8,128)(2,1)S(1)} %pad_maximum_fusion.2.refs_4_), channel_id=1, source_target_pairs={{0,1},{1,0},{2,3},{3,2},{4,5},{5,4},{6,7},{7,6},{8,9},{9,8},{10,11... | collective-permute-start | bytes 1966088 | tf_op jit(solution)/shard_map/ppermute | solution.py:132
  33.5 17.3 %collective-permute-start.7 = (bf16[128,2560]{1,0:T(8,128)(2,1)S(1)}, bf16[128,2560]{1,0:T(8,128)(2,1)}, u32[]{:S(2)}, u32[]{:S(2)}) collective-permute-start(bf16[128,2560]{1,0:T(8,128)(2,1)S(1)} %pad_maximum_fusion.2.refs_4_), channel_id=1, source_target_pairs={{0,2},{1,3},{2,0},{3,1},{4,6},{5,7},{6,4},{7,5},{8,10},{9,11},{10,... | collective-permute-start | bytes 1966088 | tf_op jit(solution)/shard_map/ppermute | solution.py:132
  35.8 22.2 %all-to-all-start.1 = ((bf16[4,8,65,128]{3,1,2,0:T(8,128)(2,1)}), bf16[4,8,65,128]{3,1,2,0:T(8,128)(2,1)S(1)}, u32[]{:S(2)}, u32[]{:S(2)}) async-start(bf16[4,8,65,128]{3,1,2,0:T(8,128)(2,1)} %copy.45), calls=%async_computation.1 | async-start | bytes 1064960 | tf_op jit(solution)/shard_map/all_to_all | solution.py:439
  40.8 20.6 %copy-start = (bf16[128,2560]{1,0:T(8,128)(2,1)}, bf16[128,2560]{1,0:T(8,128)(2,1)S(1)}, u32[]{:S(2)}) copy-start(bf16[128,2560]{1,0:T(8,128)(2,1)S(1)} %pad_maximum_fusion.1.refs_0_) | copy-start | bytes 1966084
  40.8 9.9 %collective-permute-start.8 = (bf16[128,2560]{1,0:T(8,128)(2,1)S(1)}, bf16[128,2560]{1,0:T(8,128)(2,1)S(1)}, u32[]{:S(2)}, u32[]{:S(2)}) collective-permute-start(bf16[128,2560]{1,0:T(8,128)(2,1)S(1)} %pad_maximum_fusion.1.refs_0_), channel_id=1, source_target_pairs={{0,1},{1,0},{2,3},{3,2},{4,5},{5,4},{6,7},{7,6},{8,9},{9,8},{10,11... | collective-permute-start | bytes 1966088 | tf_op jit(solution)/shard_map/ppermute | solution.py:132
  40.9 17.1 %collective-permute-start.6 = (bf16[128,2560]{1,0:T(8,128)(2,1)S(1)}, bf16[128,2560]{1,0:T(8,128)(2,1)S(1)}, u32[]{:S(2)}, u32[]{:S(2)}) collective-permute-start(bf16[128,2560]{1,0:T(8,128)(2,1)S(1)} %pad_maximum_fusion.1.refs_0_), channel_id=1, source_target_pairs={{0,4},{1,5},{2,6},{3,7},{4,0},{5,1},{6,2},{7,3},{8,12},{9,13},{10,... | collective-permute-start | bytes 1966088 | tf_op jit(solution)/shard_map/ppermute | solution.py:132
  50.7 10.7 %copy-start.3 = (bf16[128,2560]{1,0:T(8,128)(2,1)}, bf16[128,2560]{1,0:T(8,128)(2,1)S(1)}, u32[]{:S(2)}) copy-start(bf16[128,2560]{1,0:T(8,128)(2,1)S(1)} %collective-permute-done.8.refs_2_) | copy-start | bytes 1966084
  58.0 3.4 %copy-start.5 = (bf16[128,2560]{1,0:T(8,128)(2,1)}, bf16[128,2560]{1,0:T(8,128)(2,1)S(1)}, u32[]{:S(2)}) copy-start(bf16[128,2560]{1,0:T(8,128)(2,1)S(1)} %collective-permute-done.6.refs_1_) | copy-start | bytes 1966084
  58.0 2.3 %collective-permute-start.10 = (bf16[128,2560]{1,0:T(8,128)(2,1)S(1)}, bf16[128,2560]{1,0:T(8,128)(2,1)S(1)}, u32[]{:S(2)}, u32[]{:S(2)}) collective-permute-start(bf16[128,2560]{1,0:T(8,128)(2,1)S(1)} %collective-permute-done.6.refs_1_), channel_id=1, source_target_pairs={{0,1},{1,0},{2,3},{3,2},{4,5},{5,4},{6,7},{7,6},{8,9},{9,8},{10,11... | collective-permute-start | bytes 1966088 | tf_op jit(solution)/shard_map/ppermute | solution.py:132
  58.0 3.4 %collective-permute-start.11 = (bf16[128,2560]{1,0:T(8,128)(2,1)}, bf16[128,2560]{1,0:T(8,128)(2,1)}, u32[]{:S(2)}, u32[]{:S(2)}) collective-permute-start(bf16[128,2560]{1,0:T(8,128)(2,1)} %collective-permute-done.7.refs_5_), channel_id=1, source_target_pairs={{0,1},{1,0},{2,3},{3,2},{4,5},{5,4},{6,7},{7,6},{8,9},{9,8},{10,11... | collective-permute-start | bytes 1966088 | tf_op jit(solution)/shard_map/ppermute | solution.py:132
  60.4 1.1 copy-start.18
  75.5 12.5 %all-to-all-start.2 = ((f32[32,4,128]{2,1,0:T(4,128)}), f32[32,4,128]{2,1,0:T(4,128)S(1)}, u32[]{:S(2)}, u32[]{:S(2)}) async-start(f32[32,4,128]{2,1,0:T(4,128)} %get-tuple-element.51), calls=%async_computation.2 | async-start | bytes 131072 | tf_op jit(solution)/shard_map/all_to_all | solution.py:475
  80.7 0.7 copy-start.11
  80.7 0.7 copy-start.12
  80.7 7.3 %copy-start.13 = (f32[512]{0:T(512)S(1)}, f32[512]{0:T(512)}, u32[]{:S(2)}) copy-start(f32[512]{0:T(512)} %param.13) | copy-start | bytes 6148
  84.5 1.4 copy-start.8
  88.0 1.6 copy-start.7
  89.6 1.6 copy-start.9
  92.8 2.9 %copy-start.2 = (bf16[512,1024]{1,0:T(8,128)(2,1)}, bf16[512,1024]{1,0:T(8,128)(2,1)S(1)}, u32[]{:S(2)}) copy-start(bf16[512,1024]{1,0:T(8,128)(2,1)S(1)} %get-tuple-element.66.grad_ref.refs_8_) | copy-start | bytes 3145732
  92.8 2.9 %collective-permute-start.12 = (bf16[512,1024]{1,0:T(8,128)(2,1)S(1)}, bf16[512,1024]{1,0:T(8,128)(2,1)}, u32[]{:S(2)}, u32[]{:S(2)}) collective-permute-start(bf16[512,1024]{1,0:T(8,128)(2,1)S(1)} %get-tuple-element.66.grad_ref.refs_8_), channel_id=1, source_target_pairs={{0,1},{1,0},{2,3},{3,2},{4,5},{5,4},{6,7},{7,6},{8,9},{9,8},{10,11... | collective-permute-start | bytes 3145736 | tf_op jit(solution)/shard_map/ppermute | solution.py:132
  93.0 25.1 %copy-start.1 = (bf16[128,2560]{1,0:T(8,128)(2,1)S(1)}, bf16[128,2560]{1,0:T(8,128)(2,1)}, u32[]{:S(2)}) copy-start(bf16[128,2560]{1,0:T(8,128)(2,1)} %copy-done) | copy-start | bytes 1966084
  93.0 25.1 %copy-start.4 = (bf16[128,2560]{1,0:T(8,128)(2,1)S(1)}, bf16[128,2560]{1,0:T(8,128)(2,1)}, u32[]{:S(2)}) copy-start(bf16[128,2560]{1,0:T(8,128)(2,1)} %copy-done.3) | copy-start | bytes 1966084
  93.0 25.1 %copy-start.6 = (bf16[128,2560]{1,0:T(8,128)(2,1)S(1)}, bf16[128,2560]{1,0:T(8,128)(2,1)}, u32[]{:S(2)}) copy-start(bf16[128,2560]{1,0:T(8,128)(2,1)} %copy-done.5) | copy-start | bytes 1966084
  106.3 0.9 copy-start.14
  107.2 0.8 copy-start.15
  107.2 1.1 copy-start.16
  109.8 32.1 %collective-permute-start.13 = (bf16[4,2,16,2560]{3,2,1,0:T(8,128)(2,1)}, bf16[4,2,16,2560]{3,2,1,0:T(8,128)(2,1)S(1)}, u32[]{:S(2)}, u32[]{:S(2)}) collective-permute-start(bf16[4,2,16,2560]{3,2,1,0:T(8,128)(2,1)} %copy-done.16), channel_id=1, source_target_pairs={{0,2},{1,3},{2,0},{3,1},{4,6},{5,7},{6,4},{7,5},{8,10},{9,11},{10,... | collective-permute-start | bytes 1966088 | tf_op jit(solution)/shard_map/ppermute | solution.py:132
  110.3 31.6 %collective-permute-start.14 = (bf16[4,2,16,2560]{3,2,1,0:T(8,128)(2,1)}, bf16[4,2,16,2560]{3,2,1,0:T(8,128)(2,1)}, u32[]{:S(2)}, u32[]{:S(2)}) collective-permute-start(bf16[4,2,16,2560]{3,2,1,0:T(8,128)(2,1)} %copy-done.15), channel_id=1, source_target_pairs={{0,4},{1,5},{2,6},{3,7},{4,0},{5,1},{6,2},{7,3},{8,12},{9,13},{10,... | collective-permute-start | bytes 1966088 | tf_op jit(solution)/shard_map/ppermute | solution.py:132
  111.1 30.7 %collective-permute-start.15 = (bf16[4,2,16,2560]{3,2,1,0:T(8,128)(2,1)}, bf16[4,2,16,2560]{3,2,1,0:T(8,128)(2,1)}, u32[]{:S(2)}, u32[]{:S(2)}) collective-permute-start(bf16[4,2,16,2560]{3,2,1,0:T(8,128)(2,1)} %copy-done.14), channel_id=1, source_target_pairs={{0,6},{1,7},{2,4},{3,5},{4,2},{5,3},{6,0},{7,1},{8,14},{9,15},{10,... | collective-permute-start | bytes 1966088 | tf_op jit(solution)/shard_map/ppermute | solution.py:132
  114.2 27.0 %all-to-all-start.3 = ((f32[32,1,16]{2,1,0:T(1,128)}), f32[32,1,16]{2,1,0:T(1,128)S(1)}, u32[]{:S(2)}, u32[]{:S(2)}) async-start(f32[32,1,16]{2,1,0:T(1,128)} %bitcast.23), calls=%async_computation.3 | async-start | bytes 32768 | tf_op jit(solution)/shard_map/all_to_all | solution.py:533
  141.9 1.3 copy-start.10
  144.7 9.1 %collective-permute-start.16 = (bf16[2,16,2560]{2,1,0:T(8,128)(2,1)S(1)}, bf16[2,16,2560]{2,1,0:T(8,128)(2,1)S(1)}, u32[]{:S(2)}, u32[]{:S(2)}) collective-permute-start(bf16[2,16,2560]{2,1,0:T(8,128)(2,1)S(1)} %get-tuple-element.76), channel_id=1, source_target_pairs={{0,8},{1,9},{2,10},{3,11},{4,12},{5,13},{6,14},{7,15},{8,0},{9,1},... | collective-permute-start | bytes 491528 | tf_op jit(solution)/shard_map/ppermute | solution.py:132
  145.5 15.0 %collective-permute-start.17 = (bf16[2,16,2560]{2,1,0:T(8,128)(2,1)S(1)}, bf16[2,16,2560]{2,1,0:T(8,128)(2,1)S(1)}, u32[]{:S(2)}, u32[]{:S(2)}) collective-permute-start(bf16[2,16,2560]{2,1,0:T(8,128)(2,1)S(1)} %get-tuple-element.77), channel_id=1, source_target_pairs={{0,16},{1,17},{2,18},{3,19},{4,20},{5,21},{6,22},{7,23},{8,24},{9,... | collective-permute-start | bytes 491528 | tf_op jit(solution)/shard_map/ppermute | solution.py:132
  147.9 12.6 %collective-permute-start.18 = (bf16[2,16,2560]{2,1,0:T(8,128)(2,1)S(1)}, bf16[2,16,2560]{2,1,0:T(8,128)(2,1)S(1)}, u32[]{:S(2)}, u32[]{:S(2)}) collective-permute-start(bf16[2,16,2560]{2,1,0:T(8,128)(2,1)S(1)} %get-tuple-element.78), channel_id=1, source_target_pairs={{0,24},{1,25},{2,26},{3,27},{4,28},{5,29},{6,30},{7,31},{8,16},{9,... | collective-permute-start | bytes 491528 | tf_op jit(solution)/shard_map/ppermute | solution.py:132
  160.6 1.3 collective-permute-start.19

commit v8 on v6

--- a/solution.py
+++ b/solution.py
@@ -107,8 +107,9 @@
 SLOTS = 4
 LIGHT = pl.CostEstimate(flops=1, bytes_accessed=1, transcendentals=0)
 SMALL_VMEM = 16 * 1024 * 1024
-LOGITS_VMEM = 48 * 1024 * 1024
-LARGE_VMEM = 52 * 1024 * 1024
+LARGE_VMEM = 48 * 1024 * 1024
+ALL_VMEM = 60 * 1024 * 1024
+STAT_ROWS = 16
 
 
 def kernel_params(limit=SMALL_VMEM):
@@ -196,99 +197,103 @@
             out_ref[pl.ds(block * rows, rows), columns] = piece[pl.ds(i * rows, rows), :]
 
 
-def logits_kernel(rows, places, *refs):
-    count = 2 * len(places[0])
-    pieces, refs = refs[:count], refs[count:]
-    w_ref, prob_ref, logits_ref, stat_ref, hidden, weight, sems, cross_ref = refs
-    half, width = w_ref.shape[0] // 2, prob_ref.shape[1]
+def products_kernel(width, last, *refs):
+    pieces, w_ref, refs = refs[:4], refs[4], refs[5:]
+    if last:
+        rows, places, before_ref, prob_ref, logits_ref, stat_ref, hidden, weight, sems, out_ref = last + refs
+    else:
+        out_ref, hidden, weight, sems = refs
+    half = w_ref.shape[0] // 2
     tiles = w_ref.shape[1] // width
     step = pl.program_id(0)
+    i = step // tiles
 
     def copy(i):
         span = pl.ds(i * half, half)
-        return pltpu.make_async_copy(w_ref.at[span, :], weight.at[span, :], sems.at[i])
+        return pltpu.make_async_copy(w_ref.at[span, :], weight.at[i], sems.at[i])
 
     @pl.when(step == 0)
     def _():
         copy(0).start()
         copy(1).start()
-        for i, some in enumerate(places):
-            mine = pieces[i * len(some) : (i + 1) * len(some)]
-            assemble(mine, some, rows, hidden, slice(i * half, (i + 1) * half))
+        for p, piece in enumerate(pieces):
+            size = piece.shape[0]
+            hidden[p // 2, pl.ds(p % 2 * size, size), :] = piece[...]
         copy(0).wait()
 
     @pl.when(step == tiles)
     def _():
         copy(1).wait()
 
-    @pl.when(step < tiles)
-    def _():
-        span = pl.ds(pl.multiple_of(step * width, width), width)
-        logits_ref[:, span] = jnp.dot(
-            hidden[:, :half], weight[:half, span], preferred_element_type=jnp.float32
-        )
-
-    @pl.when(step >= tiles)
-    def _():
-        span = pl.ds(pl.multiple_of((step - tiles) * width, width), width)
-        total = logits_ref[:, span] + jnp.dot(
-            hidden[:, half:], weight[half:, span], preferred_element_type=jnp.float32
-        )
-        logits_ref[:, span] = total
-        product = total * prob_ref[...]
-        folded = product[:, :128]
-        for i in range(1, width // 128):
-            folded = folded + product[:, i * 128 : (i + 1) * 128]
-        cross_ref[...] = jnp.where(step == tiles, 0.0, cross_ref[...]) + folded
-
-    @pl.when(step == 2 * tiles - 1)
-    def _():
-        logits = logits_ref[...]
-        top = jnp.max(logits, axis=1, keepdims=True)
-        norm = top + jnp.log(jnp.sum(jnp.exp(logits - top), axis=1, keepdims=True))
-        cross = jnp.sum(cross_ref[...], axis=1, keepdims=True)
-        lane = lax.broadcasted_iota(jnp.int32, (1, 128), 1)
-        both = jnp.where(lane == 0, norm, jnp.where(lane == 1, cross, 0.0)).T
-        tokens = logits.shape[0]
-        packed = [both[i : i + 1, t : t + 128] for i in range(2) for t in range(0, tokens, 128)]
-        stat_ref[...] = jnp.broadcast_to(jnp.concatenate(packed, axis=0)[None], stat_ref.shape)
+    span = pl.ds(pl.multiple_of(step % tiles * width, width), width)
+    out_ref[i, :, span] = jnp.dot(hidden[i], weight[i, :, span], preferred_element_type=jnp.float32)
+
+    if last:
+
+        @pl.when(step == 2 * tiles - 1)
+        def _():
+            sources = {}
+            for i, some in enumerate(places):
+                for p, blocks in enumerate(some):
+                    for g, block in enumerate(blocks):
+                        sources.setdefault(block, []).append((i, p % 2, (p // 2 * len(blocks) + g) * rows))
+            for block, parts in sources.items():
+                total = None
+                for i, late, row in parts:
+                    part = (out_ref if late else before_ref)[i, pl.ds(row, rows), :]
+                    total = part if total is None else total + part
+                logits_ref[pl.ds(block * rows, rows), :] = total
+            logits = logits_ref[...]
+            top = jnp.max(logits, axis=1, keepdims=True)
+            norm = top + jnp.log(jnp.sum(jnp.exp(logits - top), axis=1, keepdims=True))
+            tokens = logits.shape[0]
+            cross = jnp.sum(logits * prob_ref[...], axis=1, keepdims=True)
+            lane = lax.broadcasted_iota(jnp.int32, (1, 128), 1)
+            both = jnp.where(lane == 0, norm, jnp.where(lane == 1, cross, 0.0)).T
+            packed = [both[i : i + 1, t : t + 128] for i in range(2) for t in range(0, tokens, 128)]
+            packed = jnp.concatenate(packed, axis=0)
+            stat_ref[...] = jnp.broadcast_to(packed[None], stat_ref.shape)
 
 
 def grad_kernel(
-    rows, pos_ref, stat_ref, logits_ref, prob_ref, weight_ref, entropy_ref, grad_ref, loss_ref
+    rows, pos_ref, stat_ref, logits_ref, prob_ref, weight_ref, entropy_ref, grad_ref, loss_ref, norm_ref
 ):
-    tokens = logits_ref.shape[0]
+    layers, _, side = weight_ref.shape
+    tokens = layers * side
     devices = tokens // rows
-    layers, _, side = weight_ref.shape
-    layer_bits = (devices // GROUP).bit_length() - 1
+    layer_bits = (layers - 1).bit_length()
     pos = [pos_ref[i] for i in range(3)]
     rank = pos_ref[3]
     lane = lax.broadcasted_iota(jnp.int32, (1, 128), 1)
-    per_stat = stat_ref.shape[1] // 2
-    norms, crosses = [
-        jnp.concatenate([stat_ref[:, i * per_stat + t, :] for t in range(per_stat)], axis=1) for i in range(2)
-    ]
-    stat = jnp.concatenate(
-        [norms, crosses, jnp.zeros((128 - 2 * devices, tokens), jnp.float32)], axis=0
-    ).T
-    pairs = [(0, 2), (1, 0), (2, 1)] + [(3 + i, 3 + i) for i in range(layer_bits)]
-    for index_bit, block_bit in pairs:
-        halves = stat.reshape(devices >> (block_bit + 1), 2, rows << block_bit, 128)
-        swapped = jnp.stack([halves[:, 1], halves[:, 0]], axis=1).reshape(tokens, 128)
-        stat = jnp.where(((lane ^ rank) >> index_bit) & 1 == 1, swapped, stat)
-    is_norm = lane < devices
-    is_cross = (lane >= devices) & (lane < 2 * devices)
-    top = jnp.max(jnp.where(is_norm, stat, -jnp.inf), axis=1, keepdims=True)
-    total = jnp.sum(jnp.where(is_norm, jnp.exp(stat - top), 0.0), axis=1, keepdims=True)
-    log_norm = top + jnp.log(total)
-    cross = jnp.sum(jnp.where(is_cross, stat, 0.0), axis=1, keepdims=True)
-    loss_ref[...] = entropy_ref[...] - cross[:rows] + log_norm[:rows]
-    where_token = token_places(pos, rows, side)
-    for k in range(layers):
-        span = pl.ds(k * side, side)
-        weight = pick_column(lane == where_token, weight_ref[pos[2] ^ k])
-        student = jnp.exp(logits_ref[span, :] - log_norm[k * side : (k + 1) * side])
-        grad_ref[span, :] = (weight * (student - prob_ref[span, :])).astype(grad_ref.dtype)
+    step = pl.program_id(0)
+
+    @pl.when(step == 0)
+    def _():
+        per_stat = stat_ref.shape[1] // 2
+        norms, crosses = [
+            jnp.concatenate([stat_ref[:, i * per_stat + t, :] for t in range(per_stat)], axis=1) for i in range(2)
+        ]
+        stat = jnp.concatenate(
+            [norms, crosses, jnp.zeros((128 - 2 * devices, tokens), jnp.float32)], axis=0
+        ).T
+        pairs = [(0, 2), (1, 0), (2, 1)] + [(3 + i, 3 + i) for i in range(layer_bits)]
+        for index_bit, block_bit in pairs:
+            halves = stat.reshape(devices >> (block_bit + 1), 2, rows << block_bit, 128)
+            swapped = jnp.stack([halves[:, 1], halves[:, 0]], axis=1).reshape(tokens, 128)
+            stat = jnp.where(((lane ^ rank) >> index_bit) & 1 == 1, swapped, stat)
+        is_norm = lane < devices
+        is_cross = (lane >= devices) & (lane < 2 * devices)
+        top = jnp.max(jnp.where(is_norm, stat, -jnp.inf), axis=1, keepdims=True)
+        total = jnp.sum(jnp.where(is_norm, jnp.exp(stat - top), 0.0), axis=1, keepdims=True)
+        log_norm = top + jnp.log(total)
+        cross = jnp.sum(jnp.where(is_cross, stat, 0.0), axis=1, keepdims=True)
+        loss_ref[...] = entropy_ref[...] - cross[:rows] + log_norm[:rows]
+        norm_ref[...] = jnp.broadcast_to(log_norm, norm_ref.shape)
+
+    weight = pick_column(lane == token_places(pos, rows, side), weight_ref[pos[2] ^ step])
+    norm = norm_ref[pl.ds(pl.multiple_of(step * side, side), side), :][:, :1]
+    student = jnp.exp(logits_ref[...] - norm)
+    grad_ref[...] = (weight * (student - prob_ref[...])).astype(grad_ref.dtype)
 
 
 def partial_kernel(rows, core_ref, grad_ref, sib_ref, w_ref, sib_w_ref, *refs):
@@ -349,11 +354,44 @@
     theirs[...] = total[1].astype(theirs.dtype)
 
 
-def split_three(x):
-    high = lax.reduce_precision(x, 8, 7)
-    middle = lax.reduce_precision(x - high, 8, 7)
-    low = x - high - middle
-    return jnp.stack([high, middle, low]).astype(jnp.bfloat16)
+def pack_kernel(code_ref, x_ref, out_ref):
+    blocks, count, side = x_ref.shape
+    chips, layers, size, _ = out_ref.shape
+    slot_rows = (size - STAT_ROWS) // blocks
+    stored = slot_rows // SLOTS
+    target = lax.broadcasted_iota(jnp.int32, (chips * layers * slot_rows, 1), 0)
+    row = lax.broadcasted_iota(jnp.int32, (count, 1), 0) % stored
+    lane = lax.broadcasted_iota(jnp.int32, (1, side), 1)
+    stat = jnp.zeros((1, side), jnp.float32)
+    for t in range(blocks):
+        onehot = jnp.where(code_ref[t] == target, 1.0, 0.0).astype(x_ref.dtype)
+        packed = jnp.dot(onehot, x_ref[t], preferred_element_type=jnp.float32).astype(out_ref.dtype)
+        for device in range(chips * layers):
+            out_ref[device % chips, device // chips, pl.ds(t * slot_rows, slot_rows), :] = packed[
+                device * slot_rows : (device + 1) * slot_rows
+            ]
+        values = x_ref[t].astype(jnp.float32)
+        row_top = jnp.max(values, axis=1, keepdims=True)
+        tops = [jnp.max(jnp.where(row == r, row_top, -jnp.inf), axis=0, keepdims=True) for r in range(stored)]
+        top = jnp.zeros_like(row_top)
+        for r in range(stored):
+            top = jnp.where(row == r, tops[r], top)
+        powers = jnp.exp(values - top)
+        sums = jnp.sum(powers, axis=1, keepdims=True)
+        weighted = jnp.sum(powers * values, axis=1, keepdims=True)
+        for r in range(stored):
+            total = jnp.sum(jnp.where(row == r, sums, 0.0), axis=0, keepdims=True)
+            mean = jnp.sum(jnp.where(row == r, weighted, 0.0), axis=0, keepdims=True) / total
+            stat = jnp.where(lane == t * stored + r, tops[r] + jnp.log(total), stat)
+            stat = jnp.where(lane == (blocks + t) * stored + r, mean, stat)
+    high = stat.astype(jnp.bfloat16).astype(jnp.float32)
+    middle = (stat - high).astype(jnp.bfloat16).astype(jnp.float32)
+    low = stat - high - middle
+    parts = jnp.concatenate([high, middle, low, jnp.zeros((STAT_ROWS - 3, side), jnp.float32)], axis=0)
+    parts = parts.astype(out_ref.dtype)
+    for chip in range(chips):
+        for layer in range(layers):
+            out_ref[chip, layer, pl.ds(size - STAT_ROWS, STAT_ROWS), :] = parts
 
 
 def pack_teacher(teacher_logits, block_lists, places, layer):
@@ -364,39 +402,36 @@
     earlier = jnp.tril(jnp.ones((listed_count, listed_count), jnp.bool_), -1)
     slot = jnp.sum((owner[:, :, None] == owner[:, None, :]) & earlier, axis=2, dtype=jnp.int32)
     code = (owner ^ (layer * GROUP)) * SLOTS + slot
-    picker = (code[:, None, :] == jnp.arange(n * SLOTS, dtype=jnp.int32)[None, :, None]).astype(jnp.bfloat16)
-    packed = jnp.einsum(
-        "tsk,tkrc->tsrc", picker, teacher_logits, preferred_element_type=jnp.float32
-    ).astype(jnp.bfloat16)
-    packed = packed.reshape(blocks, n, SLOTS * stored, side).transpose(1, 0, 2, 3)
-    values = teacher_logits.astype(jnp.float32)
-    top = jnp.max(values, axis=(1, 3))
-    powers = jnp.exp(values - top[:, None, :, None])
-    total = jnp.sum(powers, axis=(1, 3))
-    mean = jnp.sum(powers * values, axis=(1, 3)) / total
-    stat = split_three(jnp.stack([top + jnp.log(total), mean])).reshape(-1)
-    stat = jnp.pad(stat, (0, side - stat.shape[0]))
-    payload = jnp.concatenate(
-        [packed.reshape(n, -1, side), jnp.broadcast_to(stat, (n, 1, side))], axis=1
-    )
+    code = (code[:, :, None] * stored + jnp.arange(stored, dtype=jnp.int32)).reshape(blocks, 1, -1)
+    payload = pl.pallas_call(
+        pack_kernel,
+        in_specs=[vmem_spec()] * 2,
+        out_specs=vmem_spec(),
+        out_shape=jax.ShapeDtypeStruct(
+            (GROUP, n // GROUP, blocks * SLOTS * stored + STAT_ROWS, side), teacher_logits.dtype
+        ),
+        compiler_params=kernel_params(),
+        cost_estimate=LIGHT,
+        name="pack_teacher",
+    )(code, teacher_logits.reshape(blocks, listed_count * stored, side))
     mine = (owner * SLOTS + slot)[:, None, :] == rank * SLOTS + jnp.arange(SLOTS, dtype=jnp.int32)[None, :, None]
     place = jnp.sum(jnp.where(mine, (block_lists % places + 1)[:, None, :], 0), axis=2) - 1
-    return payload.reshape(n // GROUP, GROUP, -1, side), place.astype(jnp.int32)
+    return payload, place.astype(jnp.int32)
 
 
 def unpack_teacher(arrived, blocks, stored):
     n, _, side = arrived.shape
     arrived_blocks = (
-        arrived[:, :-1]
+        arrived[:, :-STAT_ROWS]
         .reshape(n, blocks, SLOTS, stored, side)
         .transpose(1, 2, 0, 3, 4)
         .reshape(blocks, SLOTS, n * stored, side)
     )
     arrived_stat = (
-        arrived[:, -1, : 6 * blocks * stored]
+        arrived[:, -STAT_ROWS : 3 - STAT_ROWS, : 2 * blocks * stored]
         .astype(jnp.float32)
-        .reshape(n, 3, 2, blocks, stored)
         .sum(axis=1)
+        .reshape(n, 2, blocks, stored)
         .transpose(1, 2, 0, 3)
         .reshape(2, blocks, 1, n * stored)
     )
@@ -433,13 +468,13 @@
     sib_w = shift(head_weight, 1)
     payload, place = pack_teacher(teacher_logits, block_lists, slab // side, layer)
     payload = lax.all_to_all(
-        payload, "vocab", split_axis=1, concat_axis=1, axis_index_groups=in_layer, tiled=True
+        payload, "vocab", split_axis=0, concat_axis=0, axis_index_groups=in_layer, tiled=True
     )
     column = jnp.concatenate(column, axis=0)
     column, payload = lax.optimization_barrier((column, payload))
     first, second = [column[:, :half]], [column[:, half:]]
     first_x, second_y = shift(first[0], X), shift(second[0], Y)
-    crossed = [payload[k] for k in range(layers)]
+    crossed = [payload[:, k] for k in range(layers)]
     early = [shift(crossed[k], k * GROUP) for k in range(1, layers - 1)]
     first_x, second_y, sib_w, *early = lax.optimization_barrier((first_x, second_y, sib_w, *early))
     first = [jnp.concatenate([first[0], first_x], axis=0)]
@@ -471,51 +506,66 @@
         tail_mass.reshape(blocks, 1, side),
     )
 
-    first[1], second[1], first_sib[0], second_sib[0], prob = lax.optimization_barrier(
-        (first[1], second[1], first_sib[0], second_sib[0], prob)
+    width = 256 if slab % 256 == 0 else 128
+    tiles = slab // width
+    product = jax.ShapeDtypeStruct((2, tokens // 2, slab), f32)
+    whole = lambda t: (0, 0)
+    weight_scratch = [
+        pltpu.VMEM((2, tokens // 2, half), bf16),
+        pltpu.VMEM((2, half, slab), bf16),
+        pltpu.SemaphoreType.DMA((2,)),
+    ]
+    before = pl.pallas_call(
+        functools.partial(products_kernel, width, None),
+        grid=(2 * tiles,),
+        out_shape=product,
+        in_specs=[vmem_spec()] * 4 + [hbm_spec()],
+        out_specs=pl.BlockSpec(product.shape, lambda t: (0, 0, 0)),
+        scratch_shapes=weight_scratch,
+        compiler_params=kernel_params(LARGE_VMEM),
+        cost_estimate=LIGHT,
+        name="first_products",
+    )(first[0], first_sib[0], second[0], second_sib[0], head_weight)
+    first[1], second[1], first_sib[0], second_sib[0], prob, before = lax.optimization_barrier(
+        (first[1], second[1], first_sib[0], second_sib[0], prob, before)
     )
     first_sib.append(shift(first[1], 1))
     second_sib.append(shift(second[1], 1))
     pieces = first + first_sib + second + second_sib
     places = piece_blocks(layers)
 
-    width = 256 if slab % 256 == 0 else 128
-    tiles = slab // width
-    whole = lambda t: (0, 0)
     logits, stat = pl.pallas_call(
-        functools.partial(logits_kernel, rows, places),
+        functools.partial(products_kernel, width, (rows, places)),
         grid=(2 * tiles,),
         out_shape=[
             jax.ShapeDtypeStruct((tokens, slab), f32),
             jax.ShapeDtypeStruct((n, 2 * tokens // 128, 128), f32),
         ],
-        in_specs=[vmem_spec()] * len(pieces)
-        + [hbm_spec(), pl.BlockSpec((tokens, width), lambda t: (0, jnp.maximum(t - tiles, 0)))],
+        in_specs=[vmem_spec()] * 4 + [hbm_spec()] + [vmem_spec()] * 2,
         out_specs=[
             pl.BlockSpec((tokens, slab), whole),
             pl.BlockSpec((n, 2 * tokens // 128, 128), lambda t: (0, 0, 0)),
         ],
-        scratch_shapes=[
-            pltpu.VMEM((tokens, depth), bf16),
-            pltpu.VMEM((depth, slab), bf16),
-            pltpu.SemaphoreType.DMA((2,)),
-            pltpu.VMEM((tokens, 128), f32),
-        ],
-        compiler_params=kernel_params(LOGITS_VMEM),
+        scratch_shapes=weight_scratch + [pltpu.VMEM(product.shape, f32)],
+        compiler_params=kernel_params(LARGE_VMEM),
         cost_estimate=LIGHT,
         name="logits",
-    )(*pieces, head_weight, prob)
+    )(first[1], first_sib[1], second[1], second_sib[1], head_weight, before, prob)
     stat = lax.all_to_all(stat, "vocab", split_axis=0, concat_axis=0, tiled=True)
 
+    block = pl.BlockSpec((side, slab), lambda t: (t, 0))
     grad, loss = pl.pallas_call(
-        lambda *refs: grad_kernel(rows, *refs),
+        functools.partial(grad_kernel, rows),
+        grid=(layers,),
         out_shape=(
             jax.ShapeDtypeStruct((tokens, slab), bf16),
             jax.ShapeDtypeStruct((rows, side), f32),
         ),
-        in_specs=[smem_spec()] + [vmem_spec()] * 5,
-        out_specs=(vmem_spec(), vmem_spec()),
-        compiler_params=kernel_params(),
+        in_specs=[smem_spec(), pl.BlockSpec(stat.shape, lambda t: (0, 0, 0)), block, block]
+        + [pl.BlockSpec((blocks, 1, side), lambda t: (0, 0, 0)), pl.BlockSpec((rows, side), whole)],
+        out_specs=(block, pl.BlockSpec((rows, side), whole)),
+        scratch_shapes=[pltpu.VMEM((tokens, 128), f32)],
+        compiler_params=kernel_params(ALL_VMEM),
         cost_estimate=LIGHT,
         name="grad_logits",
     )(pos, stat, logits, prob, token_weight.reshape(blocks, 1, side), entropy)

time: 154 us -> 164 us (1.065)
  Pallas kernels: 39.6 us -> 47.9 us
  local copies, waits for them, and re-layouts: 10.5 us -> 13.2 us
  other arithmetic: 6.03 us -> 3.35 us
  blocking collectives: 10.2 us -> 12.6 us
  waiting for transfers between devices: 54.6 us -> 56.3 us
    pallas_call x2 -> x4, Pallas kernels: 14.9 us -> 25.4 us  [the longest x1 10.2 us: levels_plan(): pl.pallas_call(functools.partial(products_kernel, width, (rows, places)),...]
    unnamed x36 -> x41, local copies, waits for them, and re-layouts: 5.52 us -> 8.82 us
    ppermute x23, waiting for transfers between devices: 45.5 us -> 48.4 us  [shift(): return lax.ppermute(x, 'vocab', [(i, i ^ distance) for i in range(n)])]
    all_to_all x1, blocking collectives: 10.2 us -> 12.6 us  [levels_plan(): lax.all_to_all(stat, 'vocab', split_axis=0, concat_axis=0, tiled=True)]
  transfers between devices with their start and end apart: 24 -> 24, of which waited for: 14 -> 14; matrix products, arithmetic and copies ran while one was open for 8% -> 4% of each run, Pallas kernels for 9% -> 14%
where the time goes in v8:
time: 164 us; the launch traced here: 163 us
  waiting for transfers between devices  56.3 us (34%)
  Pallas kernels  47.9 us (29%)
  starting transfers between devices  28.8 us (18%)
  local copies, waits for them, and re-layouts  13.2 us (8%)
  blocking collectives  12.6 us (8%)
  other arithmetic  3.35 us (2%)
    ppermute x23, waiting for transfers between devices, shift(): return lax.ppermute(x, 'vocab', [(i, i ^ distance) for i in range(n)])  48.4 us
    ppermute x23, starting transfers between devices, shift(): return lax.ppermute(x, 'vocab', [(i, i ^ distance) for i in range(n)])  24.9 us
    all_to_all x1, blocking collectives, levels_plan(): lax.all_to_all(stat, 'vocab', split_axis=0, concat_axis=0, tiled=True)  12.6 us
    pallas_call x1, Pallas kernels, levels_plan(): pl.pallas_call(functools.partial(products_kernel, width, (rows, places)),...  10.2 us
    pallas_call x1, Pallas kernels, levels_plan(): pl.pallas_call(functools.partial(head_kernel, rows, places), grid=(4,), i...  9.84 us
    pallas_call x1, Pallas kernels, levels_plan(): pl.pallas_call(functools.partial(partial_kernel, rows), grid_spec=pltpu.P...  9.26 us
    unnamed x41, local copies, waits for them, and re-layouts  8.82 us
    pallas_call x1, Pallas kernels, levels_plan(): pl.pallas_call(functools.partial(products_kernel, width, None), grid=(2 *...  8.26 us
  transfers between devices with their start and end apart: 24, of which 14 were waited for; matrix products, arithmetic and copies ran while one was open for 4% of the time, Pallas kernels for 14%

profile of v8, /device:TPU:0, one launch (start us, length us, event | category | flops | bytes accessed | tf_op | source)
XLA Modules:
  0.0 163.2 jit_solution(7252939094346656937)
XLA Ops:
  0.6 0.5 collective-permute-start.5
  1.1 3.7 %collective-permute-start.1 = (bf16[16,5120]{1,0:T(8,128)(2,1)}, bf16[16,5120]{1,0:T(8,128)(2,1)S(1)}, u32[]{:S(2)}, u32[]{:S(2)}) collective-permute-start(bf16[16,5120]{1,0:T(8,128)(2,1)} %param.7), channel_id=1, source_target_pairs={{0,16},{1,17},{2,18},{3,19},{4,20},{5,21},{6,22},{7,23},{8,24},{9,... | collective-permute-start | bytes 491528 | tf_op jit(solution)/shard_map/ppermute | solution.py:133
  4.8 1.6 collective-permute-start
  6.4 0.1 add.81
  6.5 0.7 fusion
  7.3 0.2 convert_reduce_fusion
  7.6 0.1 add.78
  7.7 0.1 add.89
  7.8 0.9 copy-done.9
  8.8 2.1 %pack_teacher.1 = bf16[8,4,80,128]{3,2,1,0:T(8,128)(2,1)} custom-call(s32[4,1,256]{2,1,0:T(1,128)S(1)} %broadcast_add_fusion.code_ref, bf16[4,256,128]{2,1,0:T(8,128)(2,1)S(1)} %bitcast.35), custom_call_target="tpu_custom_call" | custom-call | flops 1 | bytes 1 | tf_op jit(solution)/shard_map/pack_teacher/pallas_call | solution.py:406
  10.9 3.9 %all-to-all-start = ((bf16[8,4,80,128]{3,2,1,0:T(8,128)(2,1)}), bf16[8,4,80,128]{3,2,1,0:T(8,128)(2,1)S(1)}, u32[]{:S(2)}, u32[]{:S(2)}) async-start(bf16[8,4,80,128]{3,2,1,0:T(8,128)(2,1)} %pack_teacher.1), calls=%async_computation | async-start | bytes 1310720 | tf_op jit(solution)/shard_map/all_to_all | solution.py:470
  15.1 2.9 %collective-permute-done.2 = bf16[16,5120]{1,0:T(8,128)(2,1)S(1)} collective-permute-done((bf16[16,5120]{1,0:T(8,128)(2,1)}, bf16[16,5120]{1,0:T(8,128)(2,1)S(1)}, u32[]{:S(2)}, u32[]{:S(2)}) %collective-permute-start.2) | collective-permute-done | bytes 163872 | tf_op jit(solution)/shard_map/ppermute | solution.py:133
  18.1 7.9 %all-to-all-done = bf16[8,4,80,128]{3,2,1,0:T(8,128)(2,1)S(1)} async-done(((bf16[8,4,80,128]{3,2,1,0:T(8,128)(2,1)}), bf16[8,4,80,128]{3,2,1,0:T(8,128)(2,1)S(1)}, u32[]{:S(2)}, u32[]{:S(2)}) %all-to-all-start) | async-done | bytes 655392 | tf_op jit(solution)/shard_map/all_to_all | solution.py:470
  26.1 0.6 collective-permute-start.4
  26.7 0.6 collective-permute-start.3
  27.3 1.8 %collective-permute-start.7 = (bf16[8,80,128]{2,1,0:T(8,128)(2,1)S(1)}, bf16[8,80,128]{2,1,0:T(8,128)(2,1)S(1)}, u32[]{:S(2)}, u32[]{:S(2)}) collective-permute-start(bf16[8,80,128]{2,1,0:T(8,128)(2,1)S(1)} %get-tuple-element.80), channel_id=1, source_target_pairs={{0,16},{1,17},{2,18},{3,19},{4,20},{5,21},{6,22},{7,23},{8,24},{9,... | collective-permute-start | bytes 491528 | tf_op jit(solution)/shard_map/ppermute | solution.py:133
  29.0 2.5 %collective-permute-start.6 = (bf16[8,80,128]{2,1,0:T(8,128)(2,1)S(1)}, bf16[8,80,128]{2,1,0:T(8,128)(2,1)S(1)}, u32[]{:S(2)}, u32[]{:S(2)}) collective-permute-start(bf16[8,80,128]{2,1,0:T(8,128)(2,1)S(1)} %get-tuple-element.81), channel_id=1, source_target_pairs={{0,8},{1,9},{2,10},{3,11},{4,12},{5,13},{6,14},{7,15},{8,0},{9,1},... | collective-permute-start | bytes 491528 | tf_op jit(solution)/shard_map/ppermute | solution.py:133
  31.5 0.2 select_reduce_fusion
  31.7 5.5 %collective-permute-done.7 = bf16[8,80,128]{2,1,0:T(8,128)(2,1)S(1)} collective-permute-done((bf16[8,80,128]{2,1,0:T(8,128)(2,1)S(1)}, bf16[8,80,128]{2,1,0:T(8,128)(2,1)S(1)}, u32[]{:S(2)}, u32[]{:S(2)}) %collective-permute-start.7) | collective-permute-done | bytes 163872 | tf_op jit(solution)/shard_map/ppermute | solution.py:133
  37.4 0.6 copy-done.16
  38.1 0.4 collective-permute-start.9
  38.6 0.2 collective-permute-start.10
  38.8 1.7 %collective-permute-start.8 = (bf16[128,2560]{1,0:T(8,128)(2,1)S(1)}, bf16[128,2560]{1,0:T(8,128)(2,1)S(1)}, u32[]{:S(2)}, u32[]{:S(2)}) collective-permute-start(bf16[128,2560]{1,0:T(8,128)(2,1)S(1)} %pad_maximum_fusion.1.refs_0_), channel_id=1, source_target_pairs={{0,4},{1,5},{2,6},{3,7},{4,0},{5,1},{6,2},{7,3},{8,12},{9,13},{10,... | collective-permute-start | bytes 1966088 | tf_op jit(solution)/shard_map/ppermute | solution.py:133
  40.5 1.6 slice_bitcast_fusion.3
  42.1 2.5 %collective-permute-start.12 = (bf16[8,80,128]{2,1,0:T(8,128)(2,1)}, bf16[8,80,128]{2,1,0:T(8,128)(2,1)}, u32[]{:S(2)}, u32[]{:S(2)}) collective-permute-start(bf16[8,80,128]{2,1,0:T(8,128)(2,1)} %slice_bitcast_fusion.3), channel_id=1, source_target_pairs={{0,24},{1,25},{2,26},{3,27},{4,28},{5,29},{6,30},{7,31},{8,16},{9,... | collective-permute-start | bytes 491528 | tf_op jit(solution)/shard_map/ppermute | solution.py:133
  44.8 5.7 %collective-permute-done.12 = bf16[8,80,128]{2,1,0:T(8,128)(2,1)} collective-permute-done((bf16[8,80,128]{2,1,0:T(8,128)(2,1)}, bf16[8,80,128]{2,1,0:T(8,128)(2,1)}, u32[]{:S(2)}, u32[]{:S(2)}) %collective-permute-start.12) | collective-permute-done | bytes 163872 | tf_op jit(solution)/shard_map/ppermute | solution.py:133
  50.5 1.2 pad_maximum_fusion.3
  51.7 0.3 copy.49
  52.0 1.1 copy.45
  53.2 0.1 copy.47
  53.4 0.1 reshape.97
  53.5 1.0 copy-done.8
  54.5 3.1 %teacher_prob.1 = (f32[512,1024]{1,0:T(8,128)S(1)}, f32[16,128]{1,0:T(8,128)S(1)}) custom-call(s32[4]{0:T(128)S(1)} %pad_add_fusion.refs_0_.pos_ref.core_ref, s32[4,4]{1,0:T(4,128)S(1)} %broadcast_add_fusion.1.refs_1_, bf16[4,4,128,128]{3,2,1,0:T(8,128)(2,1)S(1)} %bitcast.34, f32[2,4,1,128]{3,2,1,0:T(1,128)S(1)} %bitcast.36, ...), custom_call_target="tpu_custom_call" | custom-call | flops 1 | bytes 1 | tf_op jit(solution)/shard_map/teacher_prob/pallas_call | solution.py:489
  57.6 1.4 copy-done
  59.0 0.6 copy-done.12
  59.6 8.3 %first_products.1.refs_5_ = f32[2,256,1024]{2,1,0:T(8,128)S(1)} custom-call(bf16[128,2560]{1,0:T(8,128)(2,1)S(1)} %pad_maximum_fusion.1.refs_0_, bf16[128,2560]{1,0:T(8,128)(2,1)} %collective-permute-done.10.refs_1_.refs_2_, bf16[128,2560]{1,0:T(8,128)(2,1)S(1)} %pad_maximum_fusion.2.refs_2_.refs_4_, ...), custom_call_target="tpu_custom_call" | custom-call | flops 1 | bytes 1 | tf_op jit(solution)/shard_map/first_products/pallas_call | solution.py:518
  67.9 1.3 copy-done.1
  69.2 0.5 collective-permute-start.14
  69.7 1.6 collective-permute-done.13.refs_1_.refs_3_
  71.3 0.9 collective-permute-done.14.refs_3_.refs_7_
  72.2 10.2 %logits.1 = (f32[512,1024]{1,0:T(8,128)S(1)}, f32[32,8,128]{2,1,0:T(8,128)S(1)}) custom-call(bf16[128,2560]{1,0:T(8,128)(2,1)S(1)} %collective-permute-done.8.refs_0_.refs_1_, bf16[128,2560]{1,0:T(8,128)(2,1)S(1)} %collective-permute-done.13.refs_1_.refs_3_, bf16[128,2560]{1,0:T(8,128)(2,1)S(1)} %collective-permute-done.9.refs_2_.refs_5_, ...), custom_call_target="tpu_custom_call" | custom-call | flops 1 | bytes 1 | tf_op jit(solution)/shard_map/logits/pallas_call | solution.py:537
  82.5 1.3 copy-done.7
  83.8 12.6 %all_to_all.10.stat_ref = f32[32,8,128]{2,1,0:T(8,128)} all-to-all(f32[32,8,128]{2,1,0:T(8,128)S(1)} %get-tuple-element.52), channel_id=1, replica_groups=mesh['vocab'=32] {'vocab'}, dimensions={0} | all-to-all | bytes 262144 | tf_op jit(solution)/shard_map/all_to_all | solution.py:554
  96.4 4.8 %grad_logits.1 = (bf16[512,1024]{1,0:T(8,128)(2,1)}, f32[16,128]{1,0:T(8,128)}) custom-call(s32[4]{0:T(128)} %copy-done.10, f32[32,8,128]{2,1,0:T(8,128)} %all_to_all.10.stat_ref, f32[512,1024]{1,0:T(8,128)} %copy-done.7, f32[512,1024]{1,0:T(8,128)} %copy-done, f32[4,1,128]{2,1,0:T(1,128)} %bitcast.47, f32[16,128]{1,0:T(8,128)} %copy-done.12), custom_call_target="tpu_custom_call" | custom-call | flops 1 | bytes 1 | tf_op jit(solution)/shard_map/grad_logits/pallas_call | solution.py:557
  101.2 0.2 collective-permute-start.15
  101.4 2.7 %collective-permute-done.15.sib_ref = bf16[512,1024]{1,0:T(8,128)(2,1)S(1)} collective-permute-done((bf16[512,1024]{1,0:T(8,128)(2,1)}, bf16[512,1024]{1,0:T(8,128)(2,1)S(1)}, u32[]{:S(2)}, u32[]{:S(2)}) %collective-permute-start.15) | collective-permute-done | bytes 1048608 | tf_op jit(solution)/shard_map/ppermute | solution.py:133
  104.1 1.2 copy-done.2
  105.3 9.3 %grad_hidden_partial.1 = (f32[4,2,16,2560]{3,2,1,0:T(8,128)S(1)}, bf16[4,2,16,2560]{3,2,1,0:T(8,128)(2,1)S(1)}, bf16[4,2,16,2560]{3,2,1,0:T(8,128)(2,1)S(1)}, bf16[4,2,16,2560]{3,2,1,0:T(8,128)(2,1)S(1)}) custom-call(s32[4]{0:T(128)S(1)} %copy-done.11, bf16[512,1024]{1,0:T(8,128)(2,1)S(1)} %copy-done.2, ...), custom_call_target="tpu_custom_call" | custom-call | flops 1 | bytes 1 | tf_op jit(solution)/shard_map/grad_hidden_partial/pallas_call | solution.py:576
  114.6 0.5 collective-permute-start.16
  115.1 1.0 collective-permute-start.17
  116.1 2.1 %collective-permute-start.18 = (bf16[4,2,16,2560]{3,2,1,0:T(8,128)(2,1)S(1)}, bf16[4,2,16,2560]{3,2,1,0:T(8,128)(2,1)S(1)}, u32[]{:S(2)}, u32[]{:S(2)}) collective-permute-start(bf16[4,2,16,2560]{3,2,1,0:T(8,128)(2,1)S(1)} %get-tuple-element.64), channel_id=1, source_target_pairs={{0,6},{1,7},{2,4},{3,5},{4,2},{5,3},{6,0},{7,1},{8,14},{9,15},{10,... | collective-permute-start | bytes 1966088 | tf_op jit(solution)/shard_map/ppermute | solution.py:133
  118.1 9.8 %grad_head.1 = bf16[5120,1024]{1,0:T(8,128)(2,1)} custom-call(bf16[128,2560]{1,0:T(8,128)(2,1)S(1)} %pad_maximum_fusion.1.refs_0_, bf16[128,2560]{1,0:T(8,128)(2,1)S(1)} %collective-permute-done.8.refs_0_.refs_1_, bf16[128,2560]{1,0:T(8,128)(2,1)} %collective-permute-done.10.refs_1_.refs_2_, bf16[128,2560]{1,0:T(8,128)(2,1)S(1)} %collective-permute-done.13.refs_1_.refs_3_, ...), custom_call_target="tpu_custom_call" | custom-call | flops 1 | bytes 1 | tf_op jit(solution)/shard_map/grad_head/pallas_call | solution.py:598
  128.0 4.2 %collective-permute-done.16.refs_0_ = bf16[4,2,16,2560]{3,2,1,0:T(8,128)(2,1)S(1)} collective-permute-done((bf16[4,2,16,2560]{3,2,1,0:T(8,128)(2,1)S(1)}, bf16[4,2,16,2560]{3,2,1,0:T(8,128)(2,1)S(1)}, u32[]{:S(2)}, u32[]{:S(2)}) %collective-permute-start.16) | collective-permute-done | bytes 655392 | tf_op jit(solution)/shard_map/ppermute | solution.py:133
  132.2 0.2 collective-permute-done.17.refs_1_
  132.4 13.2 %collective-permute-done.18.refs_2_ = bf16[4,2,16,2560]{3,2,1,0:T(8,128)(2,1)S(1)} collective-permute-done((bf16[4,2,16,2560]{3,2,1,0:T(8,128)(2,1)S(1)}, bf16[4,2,16,2560]{3,2,1,0:T(8,128)(2,1)S(1)}, u32[]{:S(2)}, u32[]{:S(2)}) %collective-permute-start.18) | collective-permute-done | bytes 655392 | tf_op jit(solution)/shard_map/ppermute | solution.py:133
  145.6 0.3 chip_sum.1
  145.9 0.7 collective-permute-start.19
  146.6 1.2 collective-permute-start.20
  147.8 2.5 %collective-permute-start.21 = (bf16[2,16,2560]{2,1,0:T(8,128)(2,1)S(1)}, bf16[2,16,2560]{2,1,0:T(8,128)(2,1)S(1)}, u32[]{:S(2)}, u32[]{:S(2)}) collective-permute-start(bf16[2,16,2560]{2,1,0:T(8,128)(2,1)S(1)} %get-tuple-element.76), channel_id=1, source_target_pairs={{0,24},{1,25},{2,26},{3,27},{4,28},{5,29},{6,30},{7,31},{8,16},{9,... | collective-permute-start | bytes 491528 | tf_op jit(solution)/shard_map/ppermute | solution.py:133
  150.3 3.3 %collective-permute-done.19.refs_0_ = bf16[2,16,2560]{2,1,0:T(8,128)(2,1)S(1)} collective-permute-done((bf16[2,16,2560]{2,1,0:T(8,128)(2,1)S(1)}, bf16[2,16,2560]{2,1,0:T(8,128)(2,1)S(1)}, u32[]{:S(2)}, u32[]{:S(2)}) %collective-permute-start.19) | collective-permute-done | bytes 163872 | tf_op jit(solution)/shard_map/ppermute | solution.py:133
  153.7 7.4 %collective-permute-done.20.refs_1_ = bf16[2,16,2560]{2,1,0:T(8,128)(2,1)S(1)} collective-permute-done((bf16[2,16,2560]{2,1,0:T(8,128)(2,1)S(1)}, bf16[2,16,2560]{2,1,0:T(8,128)(2,1)S(1)}, u32[]{:S(2)}, u32[]{:S(2)}) %collective-permute-start.20) | collective-permute-done | bytes 163872 | tf_op jit(solution)/shard_map/ppermute | solution.py:133
  161.2 0.6 slice_reduce_fusion
  161.9 0.6 collective-permute-done.22
  162.5 0.7 pad_maximum_fusion.4
  (72 shorter events, 1.3 us)
Async XLA Ops:
  0.6 36.7 %collective-permute-start.5 = (bf16[5120,1024]{1,0:T(8,128)(2,1)}, bf16[5120,1024]{1,0:T(8,128)(2,1)}, u32[]{:S(2)}, u32[]{:S(2)}) collective-permute-start(bf16[5120,1024]{1,0:T(8,128)(2,1)} %w_ref.1), channel_id=1, source_target_pairs={{0,1},{1,0},{2,3},{3,2},{4,5},{5,4},{6,7},{7,6},{8,9},{9,8},{10,11... | collective-permute-start | bytes 31457288 | tf_op jit(solution)/shard_map/ppermute | solution.py:133
  1.1 14.0 %collective-permute-start.1 = (bf16[16,5120]{1,0:T(8,128)(2,1)}, bf16[16,5120]{1,0:T(8,128)(2,1)S(1)}, u32[]{:S(2)}, u32[]{:S(2)}) collective-permute-start(bf16[16,5120]{1,0:T(8,128)(2,1)} %param.7), channel_id=1, source_target_pairs={{0,16},{1,17},{2,18},{3,19},{4,20},{5,21},{6,22},{7,23},{8,24},{9,... | collective-permute-start | bytes 491528 | tf_op jit(solution)/shard_map/ppermute | solution.py:133
  4.8 10.3 %collective-permute-start = (bf16[16,5120]{1,0:T(8,128)(2,1)}, bf16[16,5120]{1,0:T(8,128)(2,1)S(1)}, u32[]{:S(2)}, u32[]{:S(2)}) collective-permute-start(bf16[16,5120]{1,0:T(8,128)(2,1)} %param.7), channel_id=1, source_target_pairs={{0,8},{1,9},{2,10},{3,11},{4,12},{5,13},{6,14},{7,15},{8,0},{9,1},... | collective-permute-start | bytes 491528 | tf_op jit(solution)/shard_map/ppermute | solution.py:133
  6.4 11.7 %collective-permute-start.2 = (bf16[16,5120]{1,0:T(8,128)(2,1)}, bf16[16,5120]{1,0:T(8,128)(2,1)S(1)}, u32[]{:S(2)}, u32[]{:S(2)}) collective-permute-start(bf16[16,5120]{1,0:T(8,128)(2,1)} %param.7), channel_id=1, source_target_pairs={{0,24},{1,25},{2,26},{3,27},{4,28},{5,29},{6,30},{7,31},{8,16},{9,... | collective-permute-start | bytes 491528 | tf_op jit(solution)/shard_map/ppermute | solution.py:133
  6.4 8.4 %copy-start.19 = (s32[4,128]{1,0:T(4,128)S(1)}, s32[4,128]{1,0:T(4,128)}, u32[]{:S(2)}) copy-start(s32[4,128]{1,0:T(4,128)} %param.11) | copy-start | bytes 6148
  7.5 10.5 %copy-start.15 = (bf16[16,5120]{1,0:T(8,128)(2,1)S(1)}, bf16[16,5120]{1,0:T(8,128)(2,1)}, u32[]{:S(2)}) copy-start(bf16[16,5120]{1,0:T(8,128)(2,1)} %param.7) | copy-start | bytes 491524
  7.8 1.0 copy-start.9
  10.9 15.1 %all-to-all-start = ((bf16[8,4,80,128]{3,2,1,0:T(8,128)(2,1)}), bf16[8,4,80,128]{3,2,1,0:T(8,128)(2,1)S(1)}, u32[]{:S(2)}, u32[]{:S(2)}) async-start(bf16[8,4,80,128]{3,2,1,0:T(8,128)(2,1)} %pack_teacher.1), calls=%async_computation | async-start | bytes 1310720 | tf_op jit(solution)/shard_map/all_to_all | solution.py:470
  26.0 11.3 %copy-start.14 = (bf16[8,4,80,128]{3,2,1,0:T(8,128)(2,1)}, bf16[8,4,80,128]{3,2,1,0:T(8,128)(2,1)S(1)}, u32[]{:S(2)}) copy-start(bf16[8,4,80,128]{3,2,1,0:T(8,128)(2,1)S(1)} %all-to-all-done) | copy-start | bytes 1966084
  26.1 11.3 %collective-permute-start.4 = (bf16[64,2560]{1,0:T(8,128)(2,1)S(1)}, bf16[64,2560]{1,0:T(8,128)(2,1)S(1)}, u32[]{:S(2)}, u32[]{:S(2)}) collective-permute-start(bf16[64,2560]{1,0:T(8,128)(2,1)S(1)} %get-tuple-element.82), channel_id=1, source_target_pairs={{0,4},{1,5},{2,6},{3,7},{4,0},{5,1},{6,2},{7,3},{8,12},{9,13},{10,... | collective-permute-start | bytes 983048 | tf_op jit(solution)/shard_map/ppermute | solution.py:133
  26.7 10.7 %collective-permute-start.3 = (bf16[64,2560]{1,0:T(8,128)(2,1)S(1)}, bf16[64,2560]{1,0:T(8,128)(2,1)S(1)}, u32[]{:S(2)}, u32[]{:S(2)}) collective-permute-start(bf16[64,2560]{1,0:T(8,128)(2,1)S(1)} %get-tuple-element.83), channel_id=1, source_target_pairs={{0,2},{1,3},{2,0},{3,1},{4,6},{5,7},{6,4},{7,5},{8,10},{9,11},{10,... | collective-permute-start | bytes 983048 | tf_op jit(solution)/shard_map/ppermute | solution.py:133
  27.3 10.0 %collective-permute-start.7 = (bf16[8,80,128]{2,1,0:T(8,128)(2,1)S(1)}, bf16[8,80,128]{2,1,0:T(8,128)(2,1)S(1)}, u32[]{:S(2)}, u32[]{:S(2)}) collective-permute-start(bf16[8,80,128]{2,1,0:T(8,128)(2,1)S(1)} %get-tuple-element.80), channel_id=1, source_target_pairs={{0,16},{1,17},{2,18},{3,19},{4,20},{5,21},{6,22},{7,23},{8,24},{9,... | collective-permute-start | bytes 491528 | tf_op jit(solution)/shard_map/ppermute | solution.py:133
  29.0 8.3 %collective-permute-start.6 = (bf16[8,80,128]{2,1,0:T(8,128)(2,1)S(1)}, bf16[8,80,128]{2,1,0:T(8,128)(2,1)S(1)}, u32[]{:S(2)}, u32[]{:S(2)}) collective-permute-start(bf16[8,80,128]{2,1,0:T(8,128)(2,1)S(1)} %get-tuple-element.81), channel_id=1, source_target_pairs={{0,8},{1,9},{2,10},{3,11},{4,12},{5,13},{6,14},{7,15},{8,0},{9,1},... | collective-permute-start | bytes 491528 | tf_op jit(solution)/shard_map/ppermute | solution.py:133
  37.3 0.7 copy-start.16
  37.3 0.7 copy-start.17
  38.0 21.6 %collective-permute-start.11 = (bf16[128,2560]{1,0:T(8,128)(2,1)S(1)}, bf16[128,2560]{1,0:T(8,128)(2,1)S(1)}, u32[]{:S(2)}, u32[]{:S(2)}) collective-permute-start(bf16[128,2560]{1,0:T(8,128)(2,1)S(1)} %pad_maximum_fusion.2.refs_2_.refs_4_), channel_id=1, source_target_pairs={{0,1},{1,0},{2,3},{3,2},{4,5},{5,4},{6,7},{7,6},{8,9},{9,8},{10,11... | collective-permute-start | bytes 1966088 | tf_op jit(solution)/shard_map/ppermute | solution.py:133
  38.1 31.1 %collective-permute-start.9 = (bf16[128,2560]{1,0:T(8,128)(2,1)S(1)}, bf16[128,2560]{1,0:T(8,128)(2,1)S(1)}, u32[]{:S(2)}, u32[]{:S(2)}) collective-permute-start(bf16[128,2560]{1,0:T(8,128)(2,1)S(1)} %pad_maximum_fusion.2.refs_2_.refs_4_), channel_id=1, source_target_pairs={{0,2},{1,3},{2,0},{3,1},{4,6},{5,7},{6,4},{7,5},{8,10},{9,11},{10,... | collective-permute-start | bytes 1966088 | tf_op jit(solution)/shard_map/ppermute | solution.py:133
  38.6 21.0 %collective-permute-start.10 = (bf16[128,2560]{1,0:T(8,128)(2,1)S(1)}, bf16[128,2560]{1,0:T(8,128)(2,1)}, u32[]{:S(2)}, u32[]{:S(2)}) collective-permute-start(bf16[128,2560]{1,0:T(8,128)(2,1)S(1)} %pad_maximum_fusion.1.refs_0_), channel_id=1, source_target_pairs={{0,1},{1,0},{2,3},{3,2},{4,5},{5,4},{6,7},{7,6},{8,9},{9,8},{10,11... | collective-permute-start | bytes 1966088 | tf_op jit(solution)/shard_map/ppermute | solution.py:133
  38.8 30.4 %collective-permute-start.8 = (bf16[128,2560]{1,0:T(8,128)(2,1)S(1)}, bf16[128,2560]{1,0:T(8,128)(2,1)S(1)}, u32[]{:S(2)}, u32[]{:S(2)}) collective-permute-start(bf16[128,2560]{1,0:T(8,128)(2,1)S(1)} %pad_maximum_fusion.1.refs_0_), channel_id=1, source_target_pairs={{0,4},{1,5},{2,6},{3,7},{4,0},{5,1},{6,2},{7,3},{8,12},{9,13},{10,... | collective-permute-start | bytes 1966088 | tf_op jit(solution)/shard_map/ppermute | solution.py:133
  42.1 8.4 %collective-permute-start.12 = (bf16[8,80,128]{2,1,0:T(8,128)(2,1)}, bf16[8,80,128]{2,1,0:T(8,128)(2,1)}, u32[]{:S(2)}, u32[]{:S(2)}) collective-permute-start(bf16[8,80,128]{2,1,0:T(8,128)(2,1)} %slice_bitcast_fusion.3), channel_id=1, source_target_pairs={{0,24},{1,25},{2,26},{3,27},{4,28},{5,29},{6,30},{7,31},{8,16},{9,... | collective-permute-start | bytes 491528 | tf_op jit(solution)/shard_map/ppermute | solution.py:133
  44.8 8.7 %copy-start.10 = (s32[4]{0:T(128)}, s32[4]{0:T(128)S(1)}, u32[]{:S(2)}) copy-start(s32[4]{0:T(128)S(1)} %pad_add_fusion.refs_0_.pos_ref.core_ref) | copy-start | bytes 52
  51.7 1.8 %copy-start.13 = (f32[512]{0:T(512)S(1)}, f32[512]{0:T(512)}, u32[]{:S(2)}) copy-start(f32[512]{0:T(512)} %param.12) | copy-start | bytes 6148
  53.5 1.0 copy-start.8
  57.6 1.4 copy-start
  59.0 0.6 copy-start.12
  59.6 8.3 %copy-start.5 = (bf16[128,2560]{1,0:T(8,128)(2,1)}, bf16[128,2560]{1,0:T(8,128)(2,1)S(1)}, u32[]{:S(2)}) copy-start(bf16[128,2560]{1,0:T(8,128)(2,1)S(1)} %collective-permute-done.11.refs_3_.refs_6_) | copy-start | bytes 1966084
  67.9 1.3 copy-start.1
  69.2 2.1 %collective-permute-start.13 = (bf16[128,2560]{1,0:T(8,128)(2,1)S(1)}, bf16[128,2560]{1,0:T(8,128)(2,1)S(1)}, u32[]{:S(2)}, u32[]{:S(2)}) collective-permute-start(bf16[128,2560]{1,0:T(8,128)(2,1)S(1)} %collective-permute-done.8.refs_0_.refs_1_), channel_id=1, source_target_pairs={{0,1},{1,0},{2,3},{3,2},{4,5},{5,4},{6,7},{7,6},{8,9},{9,8},{10,11... | collective-permute-start | bytes 1966088 | tf_op jit(solution)/shard_map/ppermute | solution.py:133
  69.2 3.0 %collective-permute-start.14 = (bf16[128,2560]{1,0:T(8,128)(2,1)S(1)}, bf16[128,2560]{1,0:T(8,128)(2,1)S(1)}, u32[]{:S(2)}, u32[]{:S(2)}) collective-permute-start(bf16[128,2560]{1,0:T(8,128)(2,1)S(1)} %collective-permute-done.9.refs_2_.refs_5_), channel_id=1, source_target_pairs={{0,1},{1,0},{2,3},{3,2},{4,5},{5,4},{6,7},{7,6},{8,9},{9,8},{10,11... | collective-permute-start | bytes 1966088 | tf_op jit(solution)/shard_map/ppermute | solution.py:133
  72.2 10.2 %copy-start.3 = (bf16[128,2560]{1,0:T(8,128)(2,1)}, bf16[128,2560]{1,0:T(8,128)(2,1)S(1)}, u32[]{:S(2)}) copy-start(bf16[128,2560]{1,0:T(8,128)(2,1)S(1)} %collective-permute-done.14.refs_3_.refs_7_) | copy-start | bytes 1966084
  82.5 1.3 copy-start.7
  96.4 7.7 %copy-start.11 = (s32[4]{0:T(128)S(1)}, s32[4]{0:T(128)}, u32[]{:S(2)}) copy-start(s32[4]{0:T(128)} %copy-done.10) | copy-start | bytes 52
  101.2 2.9 %collective-permute-start.15 = (bf16[512,1024]{1,0:T(8,128)(2,1)}, bf16[512,1024]{1,0:T(8,128)(2,1)S(1)}, u32[]{:S(2)}, u32[]{:S(2)}) collective-permute-start(bf16[512,1024]{1,0:T(8,128)(2,1)} %get-tuple-element.67.grad_ref.refs_8_), channel_id=1, source_target_pairs={{0,1},{1,0},{2,3},{3,2},{4,5},{5,4},{6,7},{7,6},{8,9},{9,8},{10,11... | collective-permute-start | bytes 3145736 | tf_op jit(solution)/shard_map/ppermute | solution.py:133
  104.1 1.2 copy-start.2
  105.3 12.8 %copy-start.4 = (bf16[128,2560]{1,0:T(8,128)(2,1)S(1)}, bf16[128,2560]{1,0:T(8,128)(2,1)}, u32[]{:S(2)}) copy-start(bf16[128,2560]{1,0:T(8,128)(2,1)} %copy-done.3) | copy-start | bytes 1966084
  105.3 12.8 %copy-start.6 = (bf16[128,2560]{1,0:T(8,128)(2,1)S(1)}, bf16[128,2560]{1,0:T(8,128)(2,1)}, u32[]{:S(2)}) copy-start(bf16[128,2560]{1,0:T(8,128)(2,1)} %copy-done.5) | copy-start | bytes 1966084
  114.6 17.6 %collective-permute-start.16 = (bf16[4,2,16,2560]{3,2,1,0:T(8,128)(2,1)S(1)}, bf16[4,2,16,2560]{3,2,1,0:T(8,128)(2,1)S(1)}, u32[]{:S(2)}, u32[]{:S(2)}) collective-permute-start(bf16[4,2,16,2560]{3,2,1,0:T(8,128)(2,1)S(1)} %get-tuple-element.62), channel_id=1, source_target_pairs={{0,2},{1,3},{2,0},{3,1},{4,6},{5,7},{6,4},{7,5},{8,10},{9,11},{10,... | collective-permute-start | bytes 1966088 | tf_op jit(solution)/shard_map/ppermute | solution.py:133
  115.1 17.3 %collective-permute-start.17 = (bf16[4,2,16,2560]{3,2,1,0:T(8,128)(2,1)S(1)}, bf16[4,2,16,2560]{3,2,1,0:T(8,128)(2,1)S(1)}, u32[]{:S(2)}, u32[]{:S(2)}) collective-permute-start(bf16[4,2,16,2560]{3,2,1,0:T(8,128)(2,1)S(1)} %get-tuple-element.63), channel_id=1, source_target_pairs={{0,4},{1,5},{2,6},{3,7},{4,0},{5,1},{6,2},{7,3},{8,12},{9,13},{10,... | collective-permute-start | bytes 1966088 | tf_op jit(solution)/shard_map/ppermute | solution.py:133
  116.1 29.5 %collective-permute-start.18 = (bf16[4,2,16,2560]{3,2,1,0:T(8,128)(2,1)S(1)}, bf16[4,2,16,2560]{3,2,1,0:T(8,128)(2,1)S(1)}, u32[]{:S(2)}, u32[]{:S(2)}) collective-permute-start(bf16[4,2,16,2560]{3,2,1,0:T(8,128)(2,1)S(1)} %get-tuple-element.64), channel_id=1, source_target_pairs={{0,6},{1,7},{2,4},{3,5},{4,2},{5,3},{6,0},{7,1},{8,14},{9,15},{10,... | collective-permute-start | bytes 1966088 | tf_op jit(solution)/shard_map/ppermute | solution.py:133
  128.0 33.3 %copy-start.18 = (f32[16,128]{1,0:T(8,128)S(1)}, f32[16,128]{1,0:T(8,128)}, u32[]{:S(2)}) copy-start(f32[16,128]{1,0:T(8,128)} %get-tuple-element.55) | copy-start | bytes 24580
  145.9 7.8 %collective-permute-start.19 = (bf16[2,16,2560]{2,1,0:T(8,128)(2,1)S(1)}, bf16[2,16,2560]{2,1,0:T(8,128)(2,1)S(1)}, u32[]{:S(2)}, u32[]{:S(2)}) collective-permute-start(bf16[2,16,2560]{2,1,0:T(8,128)(2,1)S(1)} %get-tuple-element.74), channel_id=1, source_target_pairs={{0,8},{1,9},{2,10},{3,11},{4,12},{5,13},{6,14},{7,15},{8,0},{9,1},... | collective-permute-start | bytes 491528 | tf_op jit(solution)/shard_map/ppermute | solution.py:133
  146.6 14.5 %collective-permute-start.20 = (bf16[2,16,2560]{2,1,0:T(8,128)(2,1)S(1)}, bf16[2,16,2560]{2,1,0:T(8,128)(2,1)S(1)}, u32[]{:S(2)}, u32[]{:S(2)}) collective-permute-start(bf16[2,16,2560]{2,1,0:T(8,128)(2,1)S(1)} %get-tuple-element.75), channel_id=1, source_target_pairs={{0,16},{1,17},{2,18},{3,19},{4,20},{5,21},{6,22},{7,23},{8,24},{9,... | collective-permute-start | bytes 491528 | tf_op jit(solution)/shard_map/ppermute | solution.py:133
  147.8 13.3 %collective-permute-start.21 = (bf16[2,16,2560]{2,1,0:T(8,128)(2,1)S(1)}, bf16[2,16,2560]{2,1,0:T(8,128)(2,1)S(1)}, u32[]{:S(2)}, u32[]{:S(2)}) collective-permute-start(bf16[2,16,2560]{2,1,0:T(8,128)(2,1)S(1)} %get-tuple-element.76), channel_id=1, source_target_pairs={{0,24},{1,25},{2,26},{3,27},{4,28},{5,29},{6,30},{7,31},{8,16},{9,... | collective-permute-start | bytes 491528 | tf_op jit(solution)/shard_map/ppermute | solution.py:133
  161.1 1.3 collective-permute-start.22

commit v9 on v6

--- a/solution.py
+++ b/solution.py
@@ -107,8 +107,9 @@
 SLOTS = 4
 LIGHT = pl.CostEstimate(flops=1, bytes_accessed=1, transcendentals=0)
 SMALL_VMEM = 16 * 1024 * 1024
-LOGITS_VMEM = 48 * 1024 * 1024
-LARGE_VMEM = 52 * 1024 * 1024
+LOGITS_VMEM = 46 * 1024 * 1024
+LARGE_VMEM = 48 * 1024 * 1024
+STAT_ROWS = 16
 
 
 def kernel_params(limit=SMALL_VMEM):
@@ -176,29 +177,15 @@
             entropy_ref[...] = jnp.broadcast_to(entropy[:rows], entropy_ref.shape)
 
 
-def piece_blocks(layers):
-    first = [
-        [k * GROUP + core * CHIPS + x + 2 * y for x in range(2) for k in range(layers)]
-        for core in range(CORES)
-        for y in range(2)
-    ]
-    second = [
-        [k * GROUP + core * CHIPS + x + 2 * y for y in range(2) for k in range(layers)]
-        for core in range(CORES)
-        for x in range(2)
-    ]
-    return first, second
-
-
-def assemble(pieces, places, rows, out_ref, columns=slice(None)):
-    for piece, blocks in zip(pieces, places):
-        for i, block in enumerate(blocks):
-            out_ref[pl.ds(block * rows, rows), columns] = piece[pl.ds(i * rows, rows), :]
-
-
-def logits_kernel(rows, places, *refs):
-    count = 2 * len(places[0])
-    pieces, refs = refs[:count], refs[count:]
+def assemble(pieces, rows, out_ref):
+    layers = pieces[0].shape[0] // rows
+    for k in range(layers):
+        for p, piece in enumerate(pieces):
+            out_ref[pl.ds((k * GROUP + p) * rows, rows), :] = piece[pl.ds(k * rows, rows), :]
+
+
+def logits_kernel(rows, *refs):
+    pieces, refs = refs[:GROUP], refs[GROUP:]
     w_ref, prob_ref, logits_ref, stat_ref, hidden, weight, sems, cross_ref = refs
     half, width = w_ref.shape[0] // 2, prob_ref.shape[1]
     tiles = w_ref.shape[1] // width
@@ -212,9 +199,7 @@
     def _():
         copy(0).start()
         copy(1).start()
-        for i, some in enumerate(places):
-            mine = pieces[i * len(some) : (i + 1) * len(some)]
-            assemble(mine, some, rows, hidden, slice(i * half, (i + 1) * half))
+        assemble(pieces, rows, hidden)
         copy(0).wait()
 
     @pl.when(step == tiles)
@@ -317,15 +302,9 @@
                 out[k, core] = total[start : start + rows].astype(out.dtype)
 
 
-def head_kernel(rows, places, *refs):
+def head_kernel(rows, *refs):
     pieces, (grad_ref, out_ref, hidden) = refs[:-3], refs[-3:]
-    half = pl.program_id(0) // 2
-    for i, some in enumerate(places):
-
-        @pl.when(half == i)
-        def _():
-            assemble(pieces[i * len(some) : (i + 1) * len(some)], some, rows, hidden)
-
+    assemble(pieces, rows, hidden)
     out_ref[...] = lax.dot_general(
         hidden[...], grad_ref[...], (((0,), (0,)), ((), ())), preferred_element_type=jnp.float32
     ).astype(out_ref.dtype)
@@ -349,66 +328,87 @@
     theirs[...] = total[1].astype(theirs.dtype)
 
 
-def split_three(x):
-    high = lax.reduce_precision(x, 8, 7)
-    middle = lax.reduce_precision(x - high, 8, 7)
-    low = x - high - middle
-    return jnp.stack([high, middle, low]).astype(jnp.bfloat16)
-
-
-def pack_teacher(teacher_logits, block_lists, places, layer):
+def pack_kernel(code_ref, x_ref, out_ref):
+    blocks, count, side = x_ref.shape
+    devices, size, _ = out_ref.shape
+    slot_rows = (size - STAT_ROWS) // blocks
+    stored = slot_rows // SLOTS
+    target = lax.broadcasted_iota(jnp.int32, (devices * slot_rows, 1), 0)
+    row = lax.broadcasted_iota(jnp.int32, (count, 1), 0) % stored
+    lane = lax.broadcasted_iota(jnp.int32, (1, side), 1)
+    stat = jnp.zeros((1, side), jnp.float32)
+    for t in range(blocks):
+        onehot = jnp.where(code_ref[t] == target, 1.0, 0.0).astype(x_ref.dtype)
+        packed = jnp.dot(onehot, x_ref[t], preferred_element_type=jnp.float32).astype(out_ref.dtype)
+        for device in range(devices):
+            out_ref[device, pl.ds(t * slot_rows, slot_rows), :] = packed[
+                device * slot_rows : (device + 1) * slot_rows
+            ]
+        values = x_ref[t].astype(jnp.float32)
+        row_top = jnp.max(values, axis=1, keepdims=True)
+        tops = [jnp.max(jnp.where(row == r, row_top, -jnp.inf), axis=0, keepdims=True) for r in range(stored)]
+        top = jnp.zeros_like(row_top)
+        for r in range(stored):
+            top = jnp.where(row == r, tops[r], top)
+        powers = jnp.exp(values - top)
+        sums = jnp.sum(powers, axis=1, keepdims=True)
+        weighted = jnp.sum(powers * values, axis=1, keepdims=True)
+        for r in range(stored):
+            total = jnp.sum(jnp.where(row == r, sums, 0.0), axis=0, keepdims=True)
+            mean = jnp.sum(jnp.where(row == r, weighted, 0.0), axis=0, keepdims=True) / total
+            stat = jnp.where(lane == t * stored + r, tops[r] + jnp.log(total), stat)
+            stat = jnp.where(lane == (blocks + t) * stored + r, mean, stat)
+    high = stat.astype(jnp.bfloat16).astype(jnp.float32)
+    middle = (stat - high).astype(jnp.bfloat16).astype(jnp.float32)
+    low = stat - high - middle
+    parts = jnp.concatenate([high, middle, low, jnp.zeros((STAT_ROWS - 3, side), jnp.float32)], axis=0)
+    parts = parts.astype(out_ref.dtype)
+    for device in range(devices):
+        out_ref[device, pl.ds(size - STAT_ROWS, STAT_ROWS), :] = parts
+
+
+def pack_teacher(teacher_logits, block_lists, places):
     blocks, listed_count, stored, side = teacher_logits.shape
     n = lax.axis_size("vocab")
     rank = lax.axis_index("vocab")
     owner = block_lists // places
     earlier = jnp.tril(jnp.ones((listed_count, listed_count), jnp.bool_), -1)
     slot = jnp.sum((owner[:, :, None] == owner[:, None, :]) & earlier, axis=2, dtype=jnp.int32)
-    code = (owner ^ (layer * GROUP)) * SLOTS + slot
-    picker = (code[:, None, :] == jnp.arange(n * SLOTS, dtype=jnp.int32)[None, :, None]).astype(jnp.bfloat16)
-    packed = jnp.einsum(
-        "tsk,tkrc->tsrc", picker, teacher_logits, preferred_element_type=jnp.float32
-    ).astype(jnp.bfloat16)
-    packed = packed.reshape(blocks, n, SLOTS * stored, side).transpose(1, 0, 2, 3)
-    values = teacher_logits.astype(jnp.float32)
-    top = jnp.max(values, axis=(1, 3))
-    powers = jnp.exp(values - top[:, None, :, None])
-    total = jnp.sum(powers, axis=(1, 3))
-    mean = jnp.sum(powers * values, axis=(1, 3)) / total
-    stat = split_three(jnp.stack([top + jnp.log(total), mean])).reshape(-1)
-    stat = jnp.pad(stat, (0, side - stat.shape[0]))
-    payload = jnp.concatenate(
-        [packed.reshape(n, -1, side), jnp.broadcast_to(stat, (n, 1, side))], axis=1
-    )
-    mine = (owner * SLOTS + slot)[:, None, :] == rank * SLOTS + jnp.arange(SLOTS, dtype=jnp.int32)[None, :, None]
+    code = owner * SLOTS + slot
+    rows_code = (code[:, :, None] * stored + jnp.arange(stored, dtype=jnp.int32)).reshape(blocks, 1, -1)
+    payload = pl.pallas_call(
+        pack_kernel,
+        in_specs=[vmem_spec()] * 2,
+        out_specs=vmem_spec(),
+        out_shape=jax.ShapeDtypeStruct(
+            (n, blocks * SLOTS * stored + STAT_ROWS, side), teacher_logits.dtype
+        ),
+        compiler_params=kernel_params(),
+        cost_estimate=LIGHT,
+        name="pack_teacher",
+    )(rows_code, teacher_logits.reshape(blocks, listed_count * stored, side))
+    mine = code[:, None, :] == rank * SLOTS + jnp.arange(SLOTS, dtype=jnp.int32)[None, :, None]
     place = jnp.sum(jnp.where(mine, (block_lists % places + 1)[:, None, :], 0), axis=2) - 1
-    return payload.reshape(n // GROUP, GROUP, -1, side), place.astype(jnp.int32)
+    return payload, place.astype(jnp.int32)
 
 
 def unpack_teacher(arrived, blocks, stored):
     n, _, side = arrived.shape
     arrived_blocks = (
-        arrived[:, :-1]
+        arrived[:, :-3]
         .reshape(n, blocks, SLOTS, stored, side)
         .transpose(1, 2, 0, 3, 4)
         .reshape(blocks, SLOTS, n * stored, side)
     )
     arrived_stat = (
-        arrived[:, -1, : 6 * blocks * stored]
+        arrived[:, -3:, : 2 * blocks * stored]
         .astype(jnp.float32)
-        .reshape(n, 3, 2, blocks, stored)
         .sum(axis=1)
+        .reshape(n, 2, blocks, stored)
         .transpose(1, 2, 0, 3)
         .reshape(2, blocks, 1, n * stored)
     )
     return arrived_blocks, arrived_stat
-
-
-def by_distance(x, layer, layers):
-    shape = x.shape
-    for i in range((layers - 1).bit_length()):
-        pairs = x.reshape(shape[0], layers >> (i + 1), 2, -1)
-        x = jnp.where((layer >> i) & 1 == 1, pairs[:, :, ::-1], pairs).reshape(shape)
-    return x
 
 
 def levels_plan(
@@ -426,30 +426,17 @@
     core, chip, layer = rank % CORES, (rank // CORES) % CHIPS, rank // GROUP
     pos = jnp.stack([core, chip, layer, rank]).astype(jnp.int32)
     unlisted = float(n * slab - side * listed_count)
-    in_layer = [[o * GROUP + i for i in range(GROUP)] for o in range(layers)]
-    X, Y = CORES, 2 * CORES
 
     column = [hidden_states] + [shift(hidden_states, k * GROUP) for k in range(1, layers)]
     sib_w = shift(head_weight, 1)
-    payload, place = pack_teacher(teacher_logits, block_lists, slab // side, layer)
-    payload = lax.all_to_all(
-        payload, "vocab", split_axis=1, concat_axis=1, axis_index_groups=in_layer, tiled=True
-    )
     column = jnp.concatenate(column, axis=0)
-    column, payload = lax.optimization_barrier((column, payload))
-    first, second = [column[:, :half]], [column[:, half:]]
-    first_x, second_y = shift(first[0], X), shift(second[0], Y)
-    crossed = [payload[k] for k in range(layers)]
-    early = [shift(crossed[k], k * GROUP) for k in range(1, layers - 1)]
-    first_x, second_y, sib_w, *early = lax.optimization_barrier((first_x, second_y, sib_w, *early))
-    first = [jnp.concatenate([first[0], first_x], axis=0)]
-    second = [jnp.concatenate([second[0], second_y], axis=0)]
-    first.append(shift(first[0], Y))
-    second.append(shift(second[0], X))
-    late = [shift(crossed[k], k * GROUP) for k in range(max(layers - 1, 1), layers)]
-    arrived = jnp.stack([crossed[0], *early, *late]).reshape(n, -1, side)
+    plane = [column] + [shift(column, j * CORES) for j in range(1, CHIPS)]
+    payload, place = pack_teacher(teacher_logits, block_lists, slab // side)
+    payload, _ = lax.optimization_barrier((payload, column))
+    arrived = lax.all_to_all(
+        payload[:, : 3 - STAT_ROWS], "vocab", split_axis=0, concat_axis=0, tiled=True
+    )
     arrived_blocks, arrived_stat = unpack_teacher(arrived, blocks, stored)
-    first_sib, second_sib = [shift(first[0], 1)], [shift(second[0], 1)]
 
     prob, entropy = pl.pallas_call(
         lambda *refs: teacher_kernel(unlisted, rows, *refs),
@@ -467,23 +454,18 @@
         place,
         arrived_blocks,
         arrived_stat,
-        by_distance(row_reader, layer, layers).reshape(blocks, 1, side),
+        row_reader.reshape(blocks, 1, side),
         tail_mass.reshape(blocks, 1, side),
     )
 
-    first[1], second[1], first_sib[0], second_sib[0], prob = lax.optimization_barrier(
-        (first[1], second[1], first_sib[0], second_sib[0], prob)
-    )
-    first_sib.append(shift(first[1], 1))
-    second_sib.append(shift(second[1], 1))
-    pieces = first + first_sib + second + second_sib
-    places = piece_blocks(layers)
+    plane[-1], prob, sib_w = lax.optimization_barrier((plane[-1], prob, sib_w))
+    pieces = plane + [shift(piece, 1) for piece in plane]
 
     width = 256 if slab % 256 == 0 else 128
     tiles = slab // width
     whole = lambda t: (0, 0)
     logits, stat = pl.pallas_call(
-        functools.partial(logits_kernel, rows, places),
+        functools.partial(logits_kernel, rows),
         grid=(2 * tiles,),
         out_shape=[
             jax.ShapeDtypeStruct((tokens, slab), f32),
@@ -544,14 +526,10 @@
     arrived = [shift(partial[j], j * CORES) for j in range(1, CHIPS)]
 
     head_tile = half // 2
-    per_half = len(pieces) // 2
     grad_head = pl.pallas_call(
-        functools.partial(head_kernel, rows, places),
+        functools.partial(head_kernel, rows),
         grid=(4,),
-        in_specs=[
-            pl.BlockSpec((piece.shape[0], head_tile), lambda t, i=i: (0, jnp.clip(t - 2 * (i // per_half), 0, 1)))
-            for i, piece in enumerate(pieces)
-        ]
+        in_specs=[pl.BlockSpec((layers * rows, head_tile), lambda t: (0, t)) for _ in pieces]
         + [pl.BlockSpec((tokens, slab), whole)],
         out_specs=pl.BlockSpec((head_tile, slab), lambda t: (t, 0)),
         out_shape=jax.ShapeDtypeStruct((depth, slab), bf16),

time: 154 us -> 153 us (level)
  waiting for transfers between devices: 54.6 us -> 64.9 us
  starting transfers between devices: 30.1 us -> 25.2 us
  other arithmetic: 6.03 us -> 2.89 us
  Pallas kernels: 39.6 us -> 36.7 us
    ppermute x23 -> x19, waiting for transfers between devices: 45.5 us -> 64.9 us  [shift(): return lax.ppermute(x, 'vocab', [(i, i ^ distance) for i in range(n)])]
    all_to_all x1, waiting for transfers between devices: 9.1 us -> 0.01 us  [levels_plan(): lax.all_to_all(payload[:, :3 - STAT_ROWS], 'vocab', split_axis=0, concat_...]
    ppermute x23 -> x19, starting transfers between devices: 26.1 us -> 17.9 us  [shift(): return lax.ppermute(x, 'vocab', [(i, i ^ distance) for i in range(n)])]
    all_to_all x1, starting transfers between devices: 3.94 us -> 7.3 us  [levels_plan(): lax.all_to_all(payload[:, :3 - STAT_ROWS], 'vocab', split_axis=0, concat_...]
    pallas_call x2 -> x3, Pallas kernels: 24.2 us -> 22.7 us  [the longest x1 12 us: levels_plan(): pl.pallas_call(functools.partial(logits_kernel, rows), grid=(2 * tiles,),...]
    unnamed x36 -> x19, local copies, waits for them, and re-layouts: 5.52 us -> 5.63 us
  transfers between devices with their start and end apart: 24 -> 20, of which waited for: 14 -> 13; matrix products, arithmetic and copies ran while one was open for 8% -> 5% of each run, Pallas kernels for 9% -> 9%
where the time goes in v9:
time: 153 us; the launch traced here: 152 us
  waiting for transfers between devices  64.9 us (42%)
  Pallas kernels  36.7 us (24%)
  starting transfers between devices  25.2 us (16%)
  blocking collectives  11.7 us (8%)
  local copies, waits for them, and re-layouts  9.91 us (6%)
  other arithmetic  2.89 us (2%)
    ppermute x19, waiting for transfers between devices, shift(): return lax.ppermute(x, 'vocab', [(i, i ^ distance) for i in range(n)])  64.9 us
    ppermute x19, starting transfers between devices, shift(): return lax.ppermute(x, 'vocab', [(i, i ^ distance) for i in range(n)])  17.9 us
    pallas_call x1, Pallas kernels, levels_plan(): pl.pallas_call(functools.partial(logits_kernel, rows), grid=(2 * tiles,),...  12 us
    all_to_all x1, blocking collectives, levels_plan(): lax.all_to_all(stat, 'vocab', split_axis=0, concat_axis=0, tiled=True)  11.7 us
    pallas_call x1, Pallas kernels, levels_plan(): pl.pallas_call(functools.partial(head_kernel, rows), grid=(4,), in_specs=...  9.45 us
    pallas_call x1, Pallas kernels, levels_plan(): pl.pallas_call(functools.partial(partial_kernel, rows), grid_spec=pltpu.P...  9.26 us
    all_to_all x1, starting transfers between devices, levels_plan(): lax.all_to_all(payload[:, :3 - STAT_ROWS], 'vocab', split_axis=0, concat_...  7.3 us
    unnamed x19, local copies, waits for them, and re-layouts  5.63 us
  transfers between devices with their start and end apart: 20, of which 13 were waited for; matrix products, arithmetic and copies ran while one was open for 5% of the time, Pallas kernels for 9%

profile of v9, /device:TPU:0, one launch (start us, length us, event | category | flops | bytes accessed | tf_op | source)
XLA Modules:
  0.0 152.1 jit_solution(5882941978984227346)
XLA Ops:
  0.6 0.5 collective-permute-start.6
  1.1 3.7 %collective-permute-start.1 = (bf16[16,5120]{1,0:T(8,128)(2,1)}, bf16[16,5120]{1,0:T(8,128)(2,1)S(1)}, u32[]{:S(2)}, u32[]{:S(2)}) collective-permute-start(bf16[16,5120]{1,0:T(8,128)(2,1)} %param.7), channel_id=1, source_target_pairs={{0,16},{1,17},{2,18},{3,19},{4,20},{5,21},{6,22},{7,23},{8,24},{9,... | collective-permute-start | bytes 491528 | tf_op jit(solution)/shard_map/ppermute | solution.py:133
  4.8 1.6 %collective-permute-start = (bf16[16,5120]{1,0:T(8,128)(2,1)}, bf16[16,5120]{1,0:T(8,128)(2,1)S(1)}, u32[]{:S(2)}, u32[]{:S(2)}) collective-permute-start(bf16[16,5120]{1,0:T(8,128)(2,1)} %param.7), channel_id=1, source_target_pairs={{0,8},{1,9},{2,10},{3,11},{4,12},{5,13},{6,14},{7,15},{8,0},{9,1},... | collective-permute-start | bytes 491528 | tf_op jit(solution)/shard_map/ppermute | solution.py:133
  6.4 0.1 add.82
  6.5 0.7 add_select_fusion.1
  7.2 0.1 iota_compare_fusion
  7.3 0.2 convert_reduce_fusion
  7.5 0.1 add.79
  7.6 0.1 add.85
  7.8 0.9 constant_dynamic-update-slice_fusion.3
  8.7 0.0 copy-start.4
  8.7 0.9 copy-done.4
  9.7 1.3 pack_teacher.1
  10.9 2.7 %collective-permute-done = bf16[16,5120]{1,0:T(8,128)(2,1)S(1)} collective-permute-done((bf16[16,5120]{1,0:T(8,128)(2,1)}, bf16[16,5120]{1,0:T(8,128)(2,1)S(1)}, u32[]{:S(2)}, u32[]{:S(2)}) %collective-permute-start) | collective-permute-done | bytes 163872 | tf_op jit(solution)/shard_map/ppermute | solution.py:133
  13.6 0.0 collective-permute-done.1
  13.7 4.4 %collective-permute-done.2 = bf16[16,5120]{1,0:T(8,128)(2,1)S(1)} collective-permute-done((bf16[16,5120]{1,0:T(8,128)(2,1)}, bf16[16,5120]{1,0:T(8,128)(2,1)S(1)}, u32[]{:S(2)}, u32[]{:S(2)}) %collective-permute-start.2) | collective-permute-done | bytes 163872 | tf_op jit(solution)/shard_map/ppermute | solution.py:133
  18.1 0.9 slice.12
  18.9 7.3 %all-to-all-start = ((bf16[32,67,128]{2,1,0:T(8,128)(2,1)}), bf16[32,67,128]{2,1,0:T(8,128)(2,1)}, u32[]{:S(2)}, u32[]{:S(2)}) async-start(bf16[32,67,128]{2,1,0:T(8,128)(2,1)} %slice.12), calls=%async_computation | async-start | bytes 1179648 | tf_op jit(solution)/shard_map/all_to_all | solution.py:436
  26.2 1.8 %collective-permute-start.4 = (bf16[64,5120]{1,0:T(8,128)(2,1)S(1)}, bf16[64,5120]{1,0:T(8,128)(2,1)S(1)}, u32[]{:S(2)}, u32[]{:S(2)}) collective-permute-start(bf16[64,5120]{1,0:T(8,128)(2,1)S(1)} %constant_dynamic-update-slice_fusion.refs_0_), channel_id=1, source_target_pairs={{0,4},{1,5},{2,6},{3,7},{4,0},{5,1},{6,2},{7,3},{8,12},{9,13},{10,... | collective-permute-start | bytes 1966088 | tf_op jit(solution)/shard_map/ppermute | solution.py:133
  28.0 1.5 collective-permute-start.3
  29.5 0.3 collective-permute-start.5
  29.8 0.1 pad_add_fusion.refs_0_.core_ref
  29.9 0.2 select_reduce_fusion
  30.1 0.1 collective-permute-start.7
  30.2 19.2 %collective-permute-done.4.refs_2_ = bf16[64,5120]{1,0:T(8,128)(2,1)S(1)} collective-permute-done((bf16[64,5120]{1,0:T(8,128)(2,1)S(1)}, bf16[64,5120]{1,0:T(8,128)(2,1)S(1)}, u32[]{:S(2)}, u32[]{:S(2)}) %collective-permute-start.4) | collective-permute-done | bytes 655392 | tf_op jit(solution)/shard_map/ppermute | solution.py:133
  49.4 0.4 collective-permute-done.3.refs_1_
  49.8 0.1 collective-permute-start.8
  49.9 1.1 slice.16
  51.0 1.0 copy.27
  52.0 0.9 convert_reduce_fusion.1
  52.9 0.1 copy.28
  53.0 0.1 copy.29
  53.1 0.1 reshape.93
  53.2 1.0 copy-done.3
  54.3 0.7 copy-done.5
  55.0 0.7 copy-done.6
  55.6 3.0 %teacher_prob.1 = (f32[512,1024]{1,0:T(8,128)S(1)}, f32[16,128]{1,0:T(8,128)S(1)}) custom-call(s32[4]{0:T(128)S(1)} %pad_add_fusion.refs_0_.core_ref, s32[4,4]{1,0:T(4,128)S(1)} %broadcast_add_fusion.1.refs_1_, bf16[4,4,128,128]{3,2,1,0:T(8,128)(2,1)S(1)} %bitcast.18, f32[2,4,1,128]{3,2,1,0:T(1,128)S(1)} %bitcast.20, s32[4,1,128]{2,1,0:T(1,128)S(1)} %bitcast.21, ...), custom_call_target="tpu_custom_call" | custom-call | flops 1 | bytes 1 | tf_op jit(solution)/shard_map/teacher_prob/pallas_call | solution.py:441
  58.7 1.3 copy-done
  60.0 4.3 %collective-permute-done.5.refs_3_ = bf16[64,5120]{1,0:T(8,128)(2,1)S(1)} collective-permute-done((bf16[64,5120]{1,0:T(8,128)(2,1)S(1)}, bf16[64,5120]{1,0:T(8,128)(2,1)S(1)}, u32[]{:S(2)}, u32[]{:S(2)}) %collective-permute-start.5) | collective-permute-done | bytes 655392 | tf_op jit(solution)/shard_map/ppermute | solution.py:133
  64.3 2.1 %collective-permute-done.10.refs_7_ = bf16[64,5120]{1,0:T(8,128)(2,1)S(1)} collective-permute-done((bf16[64,5120]{1,0:T(8,128)(2,1)S(1)}, bf16[64,5120]{1,0:T(8,128)(2,1)S(1)}, u32[]{:S(2)}, u32[]{:S(2)}) %collective-permute-start.10) | collective-permute-done | bytes 655392 | tf_op jit(solution)/shard_map/ppermute | solution.py:133
  66.4 12.0 %logits.1 = (f32[512,1024]{1,0:T(8,128)S(1)}, f32[32,8,128]{2,1,0:T(8,128)S(1)}) custom-call(bf16[64,5120]{1,0:T(8,128)(2,1)S(1)} %constant_dynamic-update-slice_fusion.refs_0_, bf16[64,5120]{1,0:T(8,128)(2,1)S(1)} %collective-permute-done.3.refs_1_, bf16[64,5120]{1,0:T(8,128)(2,1)S(1)} %collective-permute-done.4.refs_2_, ...), custom_call_target="tpu_custom_call" | custom-call | flops 1 | bytes 1 | tf_op jit(solution)/shard_map/logits/pallas_call | solution.py:467
  78.4 11.7 %all_to_all.10.refs_1_ = f32[32,8,128]{2,1,0:T(8,128)S(1)} all-to-all(f32[32,8,128]{2,1,0:T(8,128)S(1)} %get-tuple-element.36), channel_id=1, replica_groups=mesh['vocab'=32] {'vocab'}, dimensions={0} | all-to-all | bytes 262144 | tf_op jit(solution)/shard_map/all_to_all | solution.py:490
  90.2 1.3 grad_logits.1
  91.5 0.3 collective-permute-start.11
  91.8 2.4 %collective-permute-done.11.sib_ref = bf16[512,1024]{1,0:T(8,128)(2,1)S(1)} collective-permute-done((bf16[512,1024]{1,0:T(8,128)(2,1)S(1)}, bf16[512,1024]{1,0:T(8,128)(2,1)S(1)}, u32[]{:S(2)}, u32[]{:S(2)}) %collective-permute-start.11) | collective-permute-done | bytes 1048608 | tf_op jit(solution)/shard_map/ppermute | solution.py:133
  94.2 9.3 %grad_hidden_partial.1 = (f32[4,2,16,2560]{3,2,1,0:T(8,128)S(1)}, bf16[4,2,16,2560]{3,2,1,0:T(8,128)(2,1)S(1)}, bf16[4,2,16,2560]{3,2,1,0:T(8,128)(2,1)S(1)}, bf16[4,2,16,2560]{3,2,1,0:T(8,128)(2,1)S(1)}) custom-call(s32[4]{0:T(128)S(1)} %pad_add_fusion.refs_0_.core_ref, bf16[512,1024]{1,0:T(8,128)(2,1)S(1)} %get-tuple-element.49.grad_ref.refs_8_, ...), custom_call_target="tpu_custom_call" | custom-call | flops 1 | bytes 1 | tf_op jit(solution)/shard_map/grad_hidden_partial/pallas_call | solution.py:508
  103.5 0.5 collective-permute-start.12
  104.0 1.0 collective-permute-start.13
  105.0 2.1 %collective-permute-start.14 = (bf16[4,2,16,2560]{3,2,1,0:T(8,128)(2,1)S(1)}, bf16[4,2,16,2560]{3,2,1,0:T(8,128)(2,1)S(1)}, u32[]{:S(2)}, u32[]{:S(2)}) collective-permute-start(bf16[4,2,16,2560]{3,2,1,0:T(8,128)(2,1)S(1)} %get-tuple-element.48), channel_id=1, source_target_pairs={{0,6},{1,7},{2,4},{3,5},{4,2},{5,3},{6,0},{7,1},{8,14},{9,15},{10,... | collective-permute-start | bytes 1966088 | tf_op jit(solution)/shard_map/ppermute | solution.py:133
  107.0 9.4 %grad_head.1 = bf16[5120,1024]{1,0:T(8,128)(2,1)} custom-call(bf16[64,5120]{1,0:T(8,128)(2,1)S(1)} %constant_dynamic-update-slice_fusion.refs_0_, bf16[64,5120]{1,0:T(8,128)(2,1)S(1)} %collective-permute-done.3.refs_1_, bf16[64,5120]{1,0:T(8,128)(2,1)S(1)} %collective-permute-done.4.refs_2_, bf16[64,5120]{1,0:T(8,128)(2,1)S(1)} %collective-permute-done.5.refs_3_, ...), custom_call_target="tpu_custom_call" | custom-call | flops 1 | bytes 1 | tf_op jit(solution)/shard_map/grad_head/pallas_call | solution.py:529
  116.5 4.6 %collective-permute-done.12.refs_0_ = bf16[4,2,16,2560]{3,2,1,0:T(8,128)(2,1)S(1)} collective-permute-done((bf16[4,2,16,2560]{3,2,1,0:T(8,128)(2,1)S(1)}, bf16[4,2,16,2560]{3,2,1,0:T(8,128)(2,1)S(1)}, u32[]{:S(2)}, u32[]{:S(2)}) %collective-permute-start.12) | collective-permute-done | bytes 655392 | tf_op jit(solution)/shard_map/ppermute | solution.py:133
  121.1 0.2 collective-permute-done.13.refs_1_
  121.3 13.2 %collective-permute-done.14.refs_2_ = bf16[4,2,16,2560]{3,2,1,0:T(8,128)(2,1)S(1)} collective-permute-done((bf16[4,2,16,2560]{3,2,1,0:T(8,128)(2,1)S(1)}, bf16[4,2,16,2560]{3,2,1,0:T(8,128)(2,1)S(1)}, u32[]{:S(2)}, u32[]{:S(2)}) %collective-permute-start.14) | collective-permute-done | bytes 655392 | tf_op jit(solution)/shard_map/ppermute | solution.py:133
  134.5 0.3 chip_sum.1
  134.8 0.7 collective-permute-start.15
  135.5 1.2 collective-permute-start.16
  136.7 2.5 %collective-permute-start.17 = (bf16[2,16,2560]{2,1,0:T(8,128)(2,1)S(1)}, bf16[2,16,2560]{2,1,0:T(8,128)(2,1)S(1)}, u32[]{:S(2)}, u32[]{:S(2)}) collective-permute-start(bf16[2,16,2560]{2,1,0:T(8,128)(2,1)S(1)} %get-tuple-element.58), channel_id=1, source_target_pairs={{0,24},{1,25},{2,26},{3,27},{4,28},{5,29},{6,30},{7,31},{8,16},{9,... | collective-permute-start | bytes 491528 | tf_op jit(solution)/shard_map/ppermute | solution.py:133
  139.3 3.3 %collective-permute-done.15.refs_0_ = bf16[2,16,2560]{2,1,0:T(8,128)(2,1)S(1)} collective-permute-done((bf16[2,16,2560]{2,1,0:T(8,128)(2,1)S(1)}, bf16[2,16,2560]{2,1,0:T(8,128)(2,1)S(1)}, u32[]{:S(2)}, u32[]{:S(2)}) %collective-permute-start.15) | collective-permute-done | bytes 163872 | tf_op jit(solution)/shard_map/ppermute | solution.py:133
  142.6 7.4 %collective-permute-done.16.refs_1_ = bf16[2,16,2560]{2,1,0:T(8,128)(2,1)S(1)} collective-permute-done((bf16[2,16,2560]{2,1,0:T(8,128)(2,1)S(1)}, bf16[2,16,2560]{2,1,0:T(8,128)(2,1)S(1)}, u32[]{:S(2)}, u32[]{:S(2)}) %collective-permute-start.16) | collective-permute-done | bytes 163872 | tf_op jit(solution)/shard_map/ppermute | solution.py:133
  150.0 0.1 layer_sum.1
  150.1 0.1 collective-permute-start.18
  150.2 0.6 slice_reduce_fusion
  150.8 0.6 collective-permute-done.18
  151.4 0.7 pad_maximum_fusion
  (29 shorter events, 0.1 us)
Async XLA Ops:
  0.6 63.7 %collective-permute-start.6 = (bf16[5120,1024]{1,0:T(8,128)(2,1)}, bf16[5120,1024]{1,0:T(8,128)(2,1)}, u32[]{:S(2)}, u32[]{:S(2)}) collective-permute-start(bf16[5120,1024]{1,0:T(8,128)(2,1)} %w_ref.1), channel_id=1, source_target_pairs={{0,1},{1,0},{2,3},{3,2},{4,5},{5,4},{6,7},{7,6},{8,9},{9,8},{10,11... | collective-permute-start | bytes 31457288 | tf_op jit(solution)/shard_map/ppermute | solution.py:133
  1.1 12.5 %collective-permute-start.1 = (bf16[16,5120]{1,0:T(8,128)(2,1)}, bf16[16,5120]{1,0:T(8,128)(2,1)S(1)}, u32[]{:S(2)}, u32[]{:S(2)}) collective-permute-start(bf16[16,5120]{1,0:T(8,128)(2,1)} %param.7), channel_id=1, source_target_pairs={{0,16},{1,17},{2,18},{3,19},{4,20},{5,21},{6,22},{7,23},{8,24},{9,... | collective-permute-start | bytes 491528 | tf_op jit(solution)/shard_map/ppermute | solution.py:133
  4.8 8.8 %collective-permute-start = (bf16[16,5120]{1,0:T(8,128)(2,1)}, bf16[16,5120]{1,0:T(8,128)(2,1)S(1)}, u32[]{:S(2)}, u32[]{:S(2)}) collective-permute-start(bf16[16,5120]{1,0:T(8,128)(2,1)} %param.7), channel_id=1, source_target_pairs={{0,8},{1,9},{2,10},{3,11},{4,12},{5,13},{6,14},{7,15},{8,0},{9,1},... | collective-permute-start | bytes 491528 | tf_op jit(solution)/shard_map/ppermute | solution.py:133
  6.4 11.7 %collective-permute-start.2 = (bf16[16,5120]{1,0:T(8,128)(2,1)}, bf16[16,5120]{1,0:T(8,128)(2,1)S(1)}, u32[]{:S(2)}, u32[]{:S(2)}) collective-permute-start(bf16[16,5120]{1,0:T(8,128)(2,1)} %param.7), channel_id=1, source_target_pairs={{0,24},{1,25},{2,26},{3,27},{4,28},{5,29},{6,30},{7,31},{8,16},{9,... | collective-permute-start | bytes 491528 | tf_op jit(solution)/shard_map/ppermute | solution.py:133
  8.7 1.0 copy-start.4
  18.9 30.9 %all-to-all-start = ((bf16[32,67,128]{2,1,0:T(8,128)(2,1)}), bf16[32,67,128]{2,1,0:T(8,128)(2,1)}, u32[]{:S(2)}, u32[]{:S(2)}) async-start(bf16[32,67,128]{2,1,0:T(8,128)(2,1)} %slice.12), calls=%async_computation | async-start | bytes 1179648 | tf_op jit(solution)/shard_map/all_to_all | solution.py:436
  26.2 23.1 %collective-permute-start.4 = (bf16[64,5120]{1,0:T(8,128)(2,1)S(1)}, bf16[64,5120]{1,0:T(8,128)(2,1)S(1)}, u32[]{:S(2)}, u32[]{:S(2)}) collective-permute-start(bf16[64,5120]{1,0:T(8,128)(2,1)S(1)} %constant_dynamic-update-slice_fusion.refs_0_), channel_id=1, source_target_pairs={{0,4},{1,5},{2,6},{3,7},{4,0},{5,1},{6,2},{7,3},{8,12},{9,13},{10,... | collective-permute-start | bytes 1966088 | tf_op jit(solution)/shard_map/ppermute | solution.py:133
  28.0 21.8 %collective-permute-start.3 = (bf16[64,5120]{1,0:T(8,128)(2,1)S(1)}, bf16[64,5120]{1,0:T(8,128)(2,1)S(1)}, u32[]{:S(2)}, u32[]{:S(2)}) collective-permute-start(bf16[64,5120]{1,0:T(8,128)(2,1)S(1)} %constant_dynamic-update-slice_fusion.refs_0_), channel_id=1, source_target_pairs={{0,2},{1,3},{2,0},{3,1},{4,6},{5,7},{6,4},{7,5},{8,10},{9,11},{10,... | collective-permute-start | bytes 1966088 | tf_op jit(solution)/shard_map/ppermute | solution.py:133
  29.5 34.8 %collective-permute-start.5 = (bf16[64,5120]{1,0:T(8,128)(2,1)S(1)}, bf16[64,5120]{1,0:T(8,128)(2,1)S(1)}, u32[]{:S(2)}, u32[]{:S(2)}) collective-permute-start(bf16[64,5120]{1,0:T(8,128)(2,1)S(1)} %constant_dynamic-update-slice_fusion.refs_0_), channel_id=1, source_target_pairs={{0,6},{1,7},{2,4},{3,5},{4,2},{5,3},{6,0},{7,1},{8,14},{9,15},{10,... | collective-permute-start | bytes 1966088 | tf_op jit(solution)/shard_map/ppermute | solution.py:133
  30.1 60.1 %copy-start.7 = (f32[512]{0:T(512)S(1)}, f32[512]{0:T(512)}, u32[]{:S(2)}) copy-start(f32[512]{0:T(512)} %param.13) | copy-start | bytes 6148
  30.1 34.2 %collective-permute-start.7 = (bf16[64,5120]{1,0:T(8,128)(2,1)S(1)}, bf16[64,5120]{1,0:T(8,128)(2,1)S(1)}, u32[]{:S(2)}, u32[]{:S(2)}) collective-permute-start(bf16[64,5120]{1,0:T(8,128)(2,1)S(1)} %constant_dynamic-update-slice_fusion.refs_0_), channel_id=1, source_target_pairs={{0,1},{1,0},{2,3},{3,2},{4,5},{5,4},{6,7},{7,6},{8,9},{9,8},{10,11... | collective-permute-start | bytes 1966088 | tf_op jit(solution)/shard_map/ppermute | solution.py:133
  49.4 15.0 %collective-permute-start.9 = (bf16[64,5120]{1,0:T(8,128)(2,1)S(1)}, bf16[64,5120]{1,0:T(8,128)(2,1)}, u32[]{:S(2)}, u32[]{:S(2)}) collective-permute-start(bf16[64,5120]{1,0:T(8,128)(2,1)S(1)} %collective-permute-done.4.refs_2_), channel_id=1, source_target_pairs={{0,1},{1,0},{2,3},{3,2},{4,5},{5,4},{6,7},{7,6},{8,9},{9,8},{10,11... | collective-permute-start | bytes 1966088 | tf_op jit(solution)/shard_map/ppermute | solution.py:133
  49.8 14.6 %collective-permute-start.8 = (bf16[64,5120]{1,0:T(8,128)(2,1)S(1)}, bf16[64,5120]{1,0:T(8,128)(2,1)}, u32[]{:S(2)}, u32[]{:S(2)}) collective-permute-start(bf16[64,5120]{1,0:T(8,128)(2,1)S(1)} %collective-permute-done.3.refs_1_), channel_id=1, source_target_pairs={{0,1},{1,0},{2,3},{3,2},{4,5},{5,4},{6,7},{7,6},{8,9},{9,8},{10,11... | collective-permute-start | bytes 1966088 | tf_op jit(solution)/shard_map/ppermute | solution.py:133
  53.2 1.0 copy-start.3
  54.3 0.7 copy-start.5
  55.0 0.7 copy-start.6
  58.7 1.3 copy-start
  64.3 25.9 %copy-start.1 = (f32[512,1024]{1,0:T(8,128)S(1)}, f32[512,1024]{1,0:T(8,128)}, u32[]{:S(2)}) copy-start(f32[512,1024]{1,0:T(8,128)} %copy-done) | copy-start | bytes 6291460
  64.3 2.1 %collective-permute-start.10 = (bf16[64,5120]{1,0:T(8,128)(2,1)S(1)}, bf16[64,5120]{1,0:T(8,128)(2,1)S(1)}, u32[]{:S(2)}, u32[]{:S(2)}) collective-permute-start(bf16[64,5120]{1,0:T(8,128)(2,1)S(1)} %collective-permute-done.5.refs_3_), channel_id=1, source_target_pairs={{0,1},{1,0},{2,3},{3,2},{4,5},{5,4},{6,7},{7,6},{8,9},{9,8},{10,11... | collective-permute-start | bytes 1966088 | tf_op jit(solution)/shard_map/ppermute | solution.py:133
  91.5 12.0 %copy-start.2 = (bf16[512,1024]{1,0:T(8,128)(2,1)}, bf16[512,1024]{1,0:T(8,128)(2,1)S(1)}, u32[]{:S(2)}) copy-start(bf16[512,1024]{1,0:T(8,128)(2,1)S(1)} %get-tuple-element.49.grad_ref.refs_8_) | copy-start | bytes 3145732
  91.5 2.7 %collective-permute-start.11 = (bf16[512,1024]{1,0:T(8,128)(2,1)S(1)}, bf16[512,1024]{1,0:T(8,128)(2,1)S(1)}, u32[]{:S(2)}, u32[]{:S(2)}) collective-permute-start(bf16[512,1024]{1,0:T(8,128)(2,1)S(1)} %get-tuple-element.49.grad_ref.refs_8_), channel_id=1, source_target_pairs={{0,1},{1,0},{2,3},{3,2},{4,5},{5,4},{6,7},{7,6},{8,9},{9,8},{10,11... | collective-permute-start | bytes 3145736 | tf_op jit(solution)/shard_map/ppermute | solution.py:133
  103.5 17.6 %collective-permute-start.12 = (bf16[4,2,16,2560]{3,2,1,0:T(8,128)(2,1)S(1)}, bf16[4,2,16,2560]{3,2,1,0:T(8,128)(2,1)S(1)}, u32[]{:S(2)}, u32[]{:S(2)}) collective-permute-start(bf16[4,2,16,2560]{3,2,1,0:T(8,128)(2,1)S(1)} %get-tuple-element.46), channel_id=1, source_target_pairs={{0,2},{1,3},{2,0},{3,1},{4,6},{5,7},{6,4},{7,5},{8,10},{9,11},{10,... | collective-permute-start | bytes 1966088 | tf_op jit(solution)/shard_map/ppermute | solution.py:133
  104.0 17.3 %collective-permute-start.13 = (bf16[4,2,16,2560]{3,2,1,0:T(8,128)(2,1)S(1)}, bf16[4,2,16,2560]{3,2,1,0:T(8,128)(2,1)S(1)}, u32[]{:S(2)}, u32[]{:S(2)}) collective-permute-start(bf16[4,2,16,2560]{3,2,1,0:T(8,128)(2,1)S(1)} %get-tuple-element.47), channel_id=1, source_target_pairs={{0,4},{1,5},{2,6},{3,7},{4,0},{5,1},{6,2},{7,3},{8,12},{9,13},{10,... | collective-permute-start | bytes 1966088 | tf_op jit(solution)/shard_map/ppermute | solution.py:133
  105.0 29.5 %collective-permute-start.14 = (bf16[4,2,16,2560]{3,2,1,0:T(8,128)(2,1)S(1)}, bf16[4,2,16,2560]{3,2,1,0:T(8,128)(2,1)S(1)}, u32[]{:S(2)}, u32[]{:S(2)}) collective-permute-start(bf16[4,2,16,2560]{3,2,1,0:T(8,128)(2,1)S(1)} %get-tuple-element.48), channel_id=1, source_target_pairs={{0,6},{1,7},{2,4},{3,5},{4,2},{5,3},{6,0},{7,1},{8,14},{9,15},{10,... | collective-permute-start | bytes 1966088 | tf_op jit(solution)/shard_map/ppermute | solution.py:133
  134.8 7.8 %collective-permute-start.15 = (bf16[2,16,2560]{2,1,0:T(8,128)(2,1)S(1)}, bf16[2,16,2560]{2,1,0:T(8,128)(2,1)S(1)}, u32[]{:S(2)}, u32[]{:S(2)}) collective-permute-start(bf16[2,16,2560]{2,1,0:T(8,128)(2,1)S(1)} %get-tuple-element.56), channel_id=1, source_target_pairs={{0,8},{1,9},{2,10},{3,11},{4,12},{5,13},{6,14},{7,15},{8,0},{9,1},... | collective-permute-start | bytes 491528 | tf_op jit(solution)/shard_map/ppermute | solution.py:133
  135.5 14.5 %collective-permute-start.16 = (bf16[2,16,2560]{2,1,0:T(8,128)(2,1)S(1)}, bf16[2,16,2560]{2,1,0:T(8,128)(2,1)S(1)}, u32[]{:S(2)}, u32[]{:S(2)}) collective-permute-start(bf16[2,16,2560]{2,1,0:T(8,128)(2,1)S(1)} %get-tuple-element.57), channel_id=1, source_target_pairs={{0,16},{1,17},{2,18},{3,19},{4,20},{5,21},{6,22},{7,23},{8,24},{9,... | collective-permute-start | bytes 491528 | tf_op jit(solution)/shard_map/ppermute | solution.py:133
  136.7 13.3 %collective-permute-start.17 = (bf16[2,16,2560]{2,1,0:T(8,128)(2,1)S(1)}, bf16[2,16,2560]{2,1,0:T(8,128)(2,1)S(1)}, u32[]{:S(2)}, u32[]{:S(2)}) collective-permute-start(bf16[2,16,2560]{2,1,0:T(8,128)(2,1)S(1)} %get-tuple-element.58), channel_id=1, source_target_pairs={{0,24},{1,25},{2,26},{3,27},{4,28},{5,29},{6,30},{7,31},{8,16},{9,... | collective-permute-start | bytes 491528 | tf_op jit(solution)/shard_map/ppermute | solution.py:133
  150.1 1.3 collective-permute-start.18

commit v10 on v9

--- a/solution.py
+++ b/solution.py
@@ -177,29 +177,37 @@
             entropy_ref[...] = jnp.broadcast_to(entropy[:rows], entropy_ref.shape)
 
 
-def assemble(pieces, rows, out_ref):
-    layers = pieces[0].shape[0] // rows
-    for k in range(layers):
-        for p, piece in enumerate(pieces):
-            out_ref[pl.ds((k * GROUP + p) * rows, rows), :] = piece[pl.ds(k * rows, rows), :]
-
-
-def logits_kernel(rows, *refs):
-    pieces, refs = refs[:GROUP], refs[GROUP:]
+def assemble(pieces, by_layer, rows, out_ref, columns=slice(None)):
+    count = len(pieces) // CORES
+    groups = pieces[0].shape[0] // rows
+    for p, piece in enumerate(pieces):
+        core, i = p // count, p % count
+        for g in range(groups):
+            layer, chip = (i, g) if by_layer else (g, i)
+            block = layer * GROUP + core * CHIPS + chip
+            out_ref[pl.ds(block * rows, rows), columns] = piece[pl.ds(g * rows, rows), :]
+
+
+def logits_kernel(rows, wide_count, *refs):
+    pieces, refs = refs[:-8], refs[-8:]
     w_ref, prob_ref, logits_ref, stat_ref, hidden, weight, sems, cross_ref = refs
-    half, width = w_ref.shape[0] // 2, prob_ref.shape[1]
+    wide_pieces, narrow_pieces = pieces[:wide_count], pieces[wide_count:]
+    depth = w_ref.shape[0]
+    wide, width = wide_pieces[0].shape[1], prob_ref.shape[1]
     tiles = w_ref.shape[1] // width
     step = pl.program_id(0)
+    parts = [slice(wide, depth), slice(0, wide)]
 
     def copy(i):
-        span = pl.ds(i * half, half)
+        span = pl.ds(parts[i].start, parts[i].stop - parts[i].start)
         return pltpu.make_async_copy(w_ref.at[span, :], weight.at[span, :], sems.at[i])
 
     @pl.when(step == 0)
     def _():
         copy(0).start()
         copy(1).start()
-        assemble(pieces, rows, hidden)
+        assemble(narrow_pieces, True, rows, hidden, parts[0])
+        assemble(wide_pieces, False, rows, hidden, parts[1])
         copy(0).wait()
 
     @pl.when(step == tiles)
@@ -210,14 +218,14 @@
     def _():
         span = pl.ds(pl.multiple_of(step * width, width), width)
         logits_ref[:, span] = jnp.dot(
-            hidden[:, :half], weight[:half, span], preferred_element_type=jnp.float32
+            hidden[:, parts[0]], weight[parts[0], span], preferred_element_type=jnp.float32
         )
 
     @pl.when(step >= tiles)
     def _():
         span = pl.ds(pl.multiple_of((step - tiles) * width, width), width)
         total = logits_ref[:, span] + jnp.dot(
-            hidden[:, half:], weight[half:, span], preferred_element_type=jnp.float32
+            hidden[:, parts[1]], weight[parts[1], span], preferred_element_type=jnp.float32
         )
         logits_ref[:, span] = total
         product = total * prob_ref[...]
@@ -276,12 +284,14 @@
         grad_ref[span, :] = (weight * (student - prob_ref[span, :])).astype(grad_ref.dtype)
 
 
-def partial_kernel(rows, core_ref, grad_ref, sib_ref, w_ref, sib_w_ref, *refs):
-    outs, swapped = refs[:CHIPS], refs[CHIPS]
-    layers = outs[0].shape[0]
+def partial_kernel(rows, wide_steps, core_ref, grad_ref, sib_ref, w_ref, sib_w_ref, *refs):
+    outs, swapped = refs[:-1], refs[-1]
+    wide_outs, narrow_outs = outs[:CHIPS], outs[CHIPS:]
+    layers = len(narrow_outs)
     half = CHIPS * rows
-
-    @pl.when(pl.program_id(0) == 0)
+    step = pl.program_id(0)
+
+    @pl.when(step == 0)
     def _():
         for k in range(layers):
             for core in range(CORES):
@@ -292,40 +302,65 @@
     contract = (((1,), (1,)), ((), ()))
     total = lax.dot_general(
         grad_ref[...], w_ref[...], contract, preferred_element_type=jnp.float32
-    ) + lax.dot_general(
-        swapped[...], sib_w_ref[...], contract, preferred_element_type=jnp.float32
-    )
-    for j, out in enumerate(outs):
+    ) + lax.dot_general(swapped[...], sib_w_ref[...], contract, preferred_element_type=jnp.float32)
+
+    def parts():
         for k in range(layers):
             for core in range(CORES):
-                start = (k * GROUP + core * CHIPS + j) * rows
-                out[k, core] = total[start : start + rows].astype(out.dtype)
-
-
-def head_kernel(rows, *refs):
+                for j in range(CHIPS):
+                    start = (k * GROUP + core * CHIPS + j) * rows
+                    yield k, core, j, total[start : start + rows]
+
+    @pl.when(step < wide_steps)
+    def _():
+        for k, core, j, part in parts():
+            wide_outs[j][k, core] = part.astype(wide_outs[j].dtype)
+
+    @pl.when(step >= wide_steps)
+    def _():
+        for k, core, j, part in parts():
+            narrow_outs[k][j, core] = part.astype(narrow_outs[k].dtype)
+
+
+def head_kernel(rows, wide_count, wide_steps, *refs):
     pieces, (grad_ref, out_ref, hidden) = refs[:-3], refs[-3:]
-    assemble(pieces, rows, hidden)
+    step = pl.program_id(0)
+
+    @pl.when(step < wide_steps)
+    def _():
+        assemble(pieces[:wide_count], False, rows, hidden)
+
+    @pl.when(step >= wide_steps)
+    def _():
+        assemble(pieces[wide_count:], True, rows, hidden)
+
     out_ref[...] = lax.dot_general(
         hidden[...], grad_ref[...], (((0,), (0,)), ((), ())), preferred_element_type=jnp.float32
     ).astype(out_ref.dtype)
 
 
-def chip_sum_kernel(own_ref, *refs):
-    arrived, outs = refs[: CHIPS - 1], refs[CHIPS - 1 :]
-    for k, out in enumerate(outs):
-        total = own_ref[k]
-        for part in arrived:
-            total = total + part[k].astype(jnp.float32)
-        out[...] = total.astype(out.dtype)
-
-
-def layer_sum_kernel(own_ref, *refs):
-    arrived, (mine, theirs) = refs[:-2], refs[-2:]
-    total = own_ref[...]
-    for part in arrived:
-        total = total + part[...].astype(jnp.float32)
-    mine[...] = total[0].astype(mine.dtype)
-    theirs[...] = total[1].astype(theirs.dtype)
+def sum_of(parts, index=...):
+    total = parts[0][index]
+    for part in parts[1:]:
+        total = total + part[index].astype(jnp.float32)
+    return total
+
+
+def first_sum_kernel(layers, *refs):
+    wide, narrow, outs = refs[:CHIPS], refs[CHIPS : CHIPS + layers], refs[CHIPS + layers :]
+    for k, out in enumerate(outs[:layers]):
+        out[...] = sum_of(wide, k).astype(out.dtype)
+    for j, out in enumerate(outs[layers:]):
+        out[...] = sum_of(narrow, j).astype(out.dtype)
+
+
+def last_sum_kernel(layers, *refs):
+    wide, narrow, (mine, theirs) = refs[:layers], refs[layers:-2], refs[-2:]
+    split = wide[0].shape[-1]
+    for parts, columns in ((wide, slice(0, split)), (narrow, slice(split, mine.shape[1]))):
+        total = sum_of(parts)
+        mine[:, columns] = total[0].astype(mine.dtype)
+        theirs[:, columns] = total[1].astype(theirs.dtype)
 
 
 def pack_kernel(code_ref, x_ref, out_ref):
@@ -427,15 +462,19 @@
     pos = jnp.stack([core, chip, layer, rank]).astype(jnp.int32)
     unlisted = float(n * slab - side * listed_count)
 
-    column = [hidden_states] + [shift(hidden_states, k * GROUP) for k in range(1, layers)]
-    sib_w = shift(head_weight, 1)
-    column = jnp.concatenate(column, axis=0)
-    plane = [column] + [shift(column, j * CORES) for j in range(1, CHIPS)]
+    narrow = depth * 3 // 10 // 512 * 512
+    wide = depth - narrow
+    column = [hidden_states[:, :wide]]
+    column += [shift(column[0], k * GROUP) for k in range(1, layers)]
+    plane = [hidden_states[:, wide:]]
+    plane += [shift(plane[0], j * CORES) for j in range(1, CHIPS)]
     payload, place = pack_teacher(teacher_logits, block_lists, slab // side)
-    payload, _ = lax.optimization_barrier((payload, column))
-    arrived = lax.all_to_all(
-        payload[:, : 3 - STAT_ROWS], "vocab", split_axis=0, concat_axis=0, tiled=True
-    )
+    column, plane = jnp.concatenate(column, axis=0), jnp.concatenate(plane, axis=0)
+    column, plane, payload = lax.optimization_barrier((column, plane, payload[:, : 3 - STAT_ROWS]))
+    wide_pieces = [column] + [shift(column, j * CORES) for j in range(1, CHIPS)]
+    narrow_pieces = [plane] + [shift(plane, k * GROUP) for k in range(1, layers)]
+    narrow_pieces[1], payload = lax.optimization_barrier((narrow_pieces[1], payload))
+    arrived = lax.all_to_all(payload, "vocab", split_axis=0, concat_axis=0, tiled=True)
     arrived_blocks, arrived_stat = unpack_teacher(arrived, blocks, stored)
 
     prob, entropy = pl.pallas_call(
@@ -458,14 +497,18 @@
         tail_mass.reshape(blocks, 1, side),
     )
 
-    plane[-1], prob, sib_w = lax.optimization_barrier((plane[-1], prob, sib_w))
-    pieces = plane + [shift(piece, 1) for piece in plane]
+    wide_pieces, narrow_pieces, prob = lax.optimization_barrier((wide_pieces, narrow_pieces, prob))
+    wide_pieces = list(wide_pieces) + [shift(piece, 1) for piece in wide_pieces]
+    narrow_pieces = list(narrow_pieces) + [shift(piece, 1) for piece in narrow_pieces]
+    wide_pieces, narrow_pieces, late_weight = lax.optimization_barrier((wide_pieces, narrow_pieces, head_weight))
+    sib_w = shift(late_weight, 1)
+    pieces = wide_pieces + narrow_pieces
 
     width = 256 if slab % 256 == 0 else 128
     tiles = slab // width
     whole = lambda t: (0, 0)
     logits, stat = pl.pallas_call(
-        functools.partial(logits_kernel, rows),
+        functools.partial(logits_kernel, rows, len(wide_pieces)),
         grid=(2 * tiles,),
         out_shape=[
             jax.ShapeDtypeStruct((tokens, slab), f32),
@@ -504,32 +547,49 @@
     sib_grad = shift(grad, 1)
 
     tile = half // 5
-    out_block = pl.BlockSpec((layers, CORES, rows, tile), lambda t, pos: (0, 0, 0, t))
+    wide_steps = 3
+    sizes = (wide_steps * tile, half - wide_steps * tile)
+    wide_block = pl.BlockSpec(
+        (layers, CORES, rows, tile), lambda t, pos: (0, 0, 0, jnp.minimum(t, wide_steps - 1))
+    )
+    narrow_block = pl.BlockSpec(
+        (CHIPS, CORES, rows, tile), lambda t, pos: (0, 0, 0, jnp.maximum(t - wide_steps, 0))
+    )
     partial = pl.pallas_call(
-        functools.partial(partial_kernel, rows),
+        functools.partial(partial_kernel, rows, wide_steps),
         grid_spec=pltpu.PrefetchScalarGridSpec(
             num_scalar_prefetch=1,
             grid=(5,),
             in_specs=[pl.BlockSpec((tokens, slab), lambda t, pos: (0, 0))] * 2
             + [pl.BlockSpec((tile, slab), lambda t, pos: (pos[0] * 5 + t, 0))] * 2,
-            out_specs=[out_block] * CHIPS,
+            out_specs=[wide_block] * CHIPS + [narrow_block] * layers,
             scratch_shapes=[pltpu.VMEM((tokens, slab), bf16)],
         ),
         out_shape=[
-            jax.ShapeDtypeStruct((layers, CORES, rows, half), f32 if j == 0 else bf16) for j in range(CHIPS)
-        ],
+            jax.ShapeDtypeStruct((layers, CORES, rows, sizes[0]), bf16 if j else f32) for j in range(CHIPS)
+        ]
+        + [jax.ShapeDtypeStruct((CHIPS, CORES, rows, sizes[1]), bf16 if k else f32) for k in range(layers)],
         compiler_params=kernel_params(LARGE_VMEM),
         cost_estimate=LIGHT,
         name="grad_hidden_partial",
     )(pos, grad, sib_grad, head_weight, sib_w)
     *partial, late_grad = lax.optimization_barrier((*partial, grad))
-    arrived = [shift(partial[j], j * CORES) for j in range(1, CHIPS)]
-
-    head_tile = half // 2
+    wide_sums = [shift(partial[j], j * CORES) for j in range(1, CHIPS)]
+    narrow_sums = [shift(partial[CHIPS + k], k * GROUP) for k in range(1, layers)]
+
+    head_tile = 512
+    head_steps = wide // head_tile
     grad_head = pl.pallas_call(
-        functools.partial(head_kernel, rows),
-        grid=(4,),
-        in_specs=[pl.BlockSpec((layers * rows, head_tile), lambda t: (0, t)) for _ in pieces]
+        functools.partial(head_kernel, rows, len(wide_pieces), head_steps),
+        grid=(depth // head_tile,),
+        in_specs=[
+            pl.BlockSpec((piece.shape[0], head_tile), lambda t: (0, jnp.minimum(t, head_steps - 1)))
+            for piece in wide_pieces
+        ]
+        + [
+            pl.BlockSpec((piece.shape[0], head_tile), lambda t: (0, jnp.maximum(t - head_steps, 0)))
+            for piece in narrow_pieces
+        ]
         + [pl.BlockSpec((tokens, slab), whole)],
         out_specs=pl.BlockSpec((head_tile, slab), lambda t: (t, 0)),
         out_shape=jax.ShapeDtypeStruct((depth, slab), bf16),
@@ -538,29 +598,29 @@
         cost_estimate=LIGHT,
         name="grad_head",
     )(*pieces, late_grad)
-    arrived, grad_head = lax.optimization_barrier((arrived, grad_head))
+    wide_sums, narrow_sums, grad_head = lax.optimization_barrier((wide_sums, narrow_sums, grad_head))
 
     summed = pl.pallas_call(
-        chip_sum_kernel,
-        in_specs=[vmem_spec()] * CHIPS,
-        out_specs=[vmem_spec()] * layers,
-        out_shape=[
-            jax.ShapeDtypeStruct((CORES, rows, half), f32 if k == 0 else bf16) for k in range(layers)
-        ],
+        functools.partial(first_sum_kernel, layers),
+        in_specs=[vmem_spec()] * (CHIPS + layers),
+        out_specs=[vmem_spec()] * (CHIPS + layers),
+        out_shape=[jax.ShapeDtypeStruct((CORES, rows, sizes[0]), bf16 if k else f32) for k in range(layers)]
+        + [jax.ShapeDtypeStruct((CORES, rows, sizes[1]), bf16 if j else f32) for j in range(CHIPS)],
         compiler_params=kernel_params(),
         cost_estimate=LIGHT,
-        name="chip_sum",
-    )(partial[0], *arrived)
-    arrived = [shift(summed[k], k * GROUP) for k in range(1, layers)]
+        name="first_sum",
+    )(partial[0], *wide_sums, partial[CHIPS], *narrow_sums)
+    wide_sums = [shift(summed[k], k * GROUP) for k in range(1, layers)]
+    narrow_sums = [shift(summed[layers + j], j * CORES) for j in range(1, CHIPS)]
     mine, theirs = pl.pallas_call(
-        layer_sum_kernel,
-        in_specs=[vmem_spec()] * layers,
+        functools.partial(last_sum_kernel, layers),
+        in_specs=[vmem_spec()] * (CHIPS + layers),
         out_specs=[vmem_spec()] * 2,
         out_shape=[jax.ShapeDtypeStruct((rows, half), bf16)] * 2,
         compiler_params=kernel_params(),
         cost_estimate=LIGHT,
-        name="layer_sum",
-    )(summed[0], *arrived)
+        name="last_sum",
+    )(summed[0], *wide_sums, summed[layers], *narrow_sums)
     other = shift(theirs, 1)
 
     low, high = jnp.where(core == 0, mine, other), jnp.where(core == 0, other, mine)

time: 153 us -> 149 us (0.974)
  waiting for transfers between devices: 64.9 us -> 46.3 us
  starting transfers between devices: 25.2 us -> 40.9 us
    ppermute x19 -> x35, waiting for transfers between devices: 64.9 us -> 28.6 us  [shift(): return lax.ppermute(x, 'vocab', [(i, i ^ distance) for i in range(n)])]
    ppermute x19 -> x35, starting transfers between devices: 17.9 us -> 36.8 us  [shift(): return lax.ppermute(x, 'vocab', [(i, i ^ distance) for i in range(n)])]
    all_to_all x1, waiting for transfers between devices: 0.01 us -> 17.7 us  [levels_plan(): lax.all_to_all(payload, 'vocab', split_axis=0, concat_axis=0, tiled=True)]
    all_to_all x1, starting transfers between devices: 7.3 us -> 4.14 us  [levels_plan(): lax.all_to_all(payload, 'vocab', split_axis=0, concat_axis=0, tiled=True)]
    slice x0 -> x2, local copies, waits for them, and re-layouts: none -> 1.71 us  [the longest x1 0.91 us: levels_plan(): column = [hidden_states[:, :wide]]]
    unnamed x19 -> x16, local copies, waits for them, and re-layouts: 5.63 us -> 4.38 us
  transfers between devices with their start and end apart: 20 -> 36, of which waited for: 13 -> 15; matrix products, arithmetic and copies ran while one was open for 5% -> 4% of each run, Pallas kernels for 9% -> 19%
where the time goes in v10:
time: 149 us
  waiting for transfers between devices  46.3 us (31%)
  starting transfers between devices  40.9 us (27%)
  Pallas kernels  37.5 us (25%)
  blocking collectives  11.6 us (8%)
  local copies, waits for them, and re-layouts  8.53 us (6%)
  other arithmetic  2.93 us (2%)
    ppermute x35, starting transfers between devices, shift(): return lax.ppermute(x, 'vocab', [(i, i ^ distance) for i in range(n)])  36.8 us
    ppermute x35, waiting for transfers between devices, shift(): return lax.ppermute(x, 'vocab', [(i, i ^ distance) for i in range(n)])  28.6 us
    all_to_all x1, waiting for transfers between devices, levels_plan(): lax.all_to_all(payload, 'vocab', split_axis=0, concat_axis=0, tiled=True)  17.7 us
    all_to_all x1, blocking collectives, levels_plan(): lax.all_to_all(stat, 'vocab', split_axis=0, concat_axis=0, tiled=True)  11.6 us
    pallas_call x1, Pallas kernels, levels_plan(): pl.pallas_call(functools.partial(head_kernel, rows, len(wide_pieces), hea...  11.3 us
    pallas_call x1, Pallas kernels, levels_plan(): pl.pallas_call(functools.partial(logits_kernel, rows, len(wide_pieces)),...  10.7 us
    pallas_call x1, Pallas kernels, levels_plan(): pl.pallas_call(functools.partial(partial_kernel, rows, wide_steps), grid_...  9.55 us
    unnamed x16, local copies, waits for them, and re-layouts  4.38 us
  transfers between devices with their start and end apart: 36, of which 15 were waited for; matrix products, arithmetic and copies ran while one was open for 4% of the time, Pallas kernels for 19%

profile of v10, /device:TPU:0, one launch (start us, length us, event | category | flops | bytes accessed | tf_op | source)
XLA Modules:
  0.0 148.7 jit_solution(7976217801120310325)
XLA Ops:
  0.6 0.8 slice.19
  1.4 3.9 %collective-permute-start.5 = (bf16[16,1536]{1,0:T(8,128)(2,1)S(1)}, bf16[16,1536]{1,0:T(8,128)(2,1)S(1)}, u32[]{:S(2)}, u32[]{:S(2)}) collective-permute-start(bf16[16,1536]{1,0:T(8,128)(2,1)S(1)} %slice.19), channel_id=1, source_target_pairs={{0,6},{1,7},{2,4},{3,5},{4,2},{5,3},{6,0},{7,1},{8,14},{9,15},{10,... | collective-permute-start | bytes 147464 | tf_op jit(solution)/shard_map/ppermute | solution.py:133
  5.3 0.5 collective-permute-start.4
  5.9 0.9 slice.18
  6.8 4.1 %collective-permute-start.2 = (bf16[16,3584]{1,0:T(8,128)(2,1)S(1)}, bf16[16,3584]{1,0:T(8,128)(2,1)S(1)}, u32[]{:S(2)}, u32[]{:S(2)}) collective-permute-start(bf16[16,3584]{1,0:T(8,128)(2,1)S(1)} %slice.18), channel_id=1, source_target_pairs={{0,24},{1,25},{2,26},{3,27},{4,28},{5,29},{6,30},{7,31},{8,16},{9,... | collective-permute-start | bytes 344072 | tf_op jit(solution)/shard_map/ppermute | solution.py:133
  10.9 0.7 fusion
  11.7 0.2 convert_reduce_fusion
  12.3 0.9 copy-done.3
  13.2 1.3 pack_teacher.1
  14.5 0.9 slice.24
  15.4 0.6 collective-permute-start
  16.0 3.8 %collective-permute-done.1 = bf16[16,3584]{1,0:T(8,128)(2,1)S(1)} collective-permute-done((bf16[16,3584]{1,0:T(8,128)(2,1)S(1)}, bf16[16,3584]{1,0:T(8,128)(2,1)S(1)}, u32[]{:S(2)}, u32[]{:S(2)}) %collective-permute-start.1) | collective-permute-done | bytes 114720 | tf_op jit(solution)/shard_map/ppermute | solution.py:133
  19.8 1.6 %collective-permute-done = bf16[16,3584]{1,0:T(8,128)(2,1)S(1)} collective-permute-done((bf16[16,3584]{1,0:T(8,128)(2,1)S(1)}, bf16[16,3584]{1,0:T(8,128)(2,1)S(1)}, u32[]{:S(2)}, u32[]{:S(2)}) %collective-permute-start) | collective-permute-done | bytes 114720 | tf_op jit(solution)/shard_map/ppermute | solution.py:133
  21.5 5.9 %collective-permute-done.9.refs_9_ = bf16[64,1536]{1,0:T(8,128)(2,1)S(1)} collective-permute-done((bf16[64,1536]{1,0:T(8,128)(2,1)S(1)}, bf16[64,1536]{1,0:T(8,128)(2,1)S(1)}, u32[]{:S(2)}, u32[]{:S(2)}) %collective-permute-start.9) | collective-permute-done | bytes 196640 | tf_op jit(solution)/shard_map/ppermute | solution.py:133
  27.4 4.1 %all-to-all-start = ((bf16[32,67,128]{2,1,0:T(8,128)(2,1)}), bf16[32,67,128]{2,1,0:T(8,128)(2,1)S(1)}, u32[]{:S(2)}, u32[]{:S(2)}) async-start(bf16[32,67,128]{2,1,0:T(8,128)(2,1)} %slice.24), calls=%async_computation | async-start | bytes 1179648 | tf_op jit(solution)/shard_map/all_to_all | solution.py:477
  31.6 2.7 %collective-permute-start.8 = (bf16[64,3584]{1,0:T(8,128)(2,1)S(1)}, bf16[64,3584]{1,0:T(8,128)(2,1)S(1)}, u32[]{:S(2)}, u32[]{:S(2)}) collective-permute-start(bf16[64,3584]{1,0:T(8,128)(2,1)S(1)} %pad_maximum_fusion.refs_0_), channel_id=1, source_target_pairs={{0,6},{1,7},{2,4},{3,5},{4,2},{5,3},{6,0},{7,1},{8,14},{9,15},{10,... | collective-permute-start | bytes 1376264 | tf_op jit(solution)/shard_map/ppermute | solution.py:133
  34.3 0.6 collective-permute-start.7
  34.9 0.3 collective-permute-start.6
  35.1 0.2 select_reduce_fusion
  35.4 3.7 %collective-permute-start.11 = (bf16[64,1536]{1,0:T(8,128)(2,1)S(1)}, bf16[64,1536]{1,0:T(8,128)(2,1)S(1)}, u32[]{:S(2)}, u32[]{:S(2)}) collective-permute-start(bf16[64,1536]{1,0:T(8,128)(2,1)S(1)} %pad_maximum_fusion.1.refs_8_), channel_id=1, source_target_pairs={{0,24},{1,25},{2,26},{3,27},{4,28},{5,29},{6,30},{7,31},{8,16},{9,... | collective-permute-start | bytes 589832 | tf_op jit(solution)/shard_map/ppermute | solution.py:133
  39.2 17.7 %all-to-all-done = bf16[32,67,128]{2,1,0:T(8,128)(2,1)S(1)} async-done(((bf16[32,67,128]{2,1,0:T(8,128)(2,1)}), bf16[32,67,128]{2,1,0:T(8,128)(2,1)S(1)}, u32[]{:S(2)}, u32[]{:S(2)}) %all-to-all-start) | async-done | bytes 548896 | tf_op jit(solution)/shard_map/all_to_all | solution.py:477
  56.9 0.8 copy-done.7
  57.7 0.2 copy.27
  57.9 0.9 convert_reduce_fusion.1
  59.2 0.7 copy-done.4
  59.8 0.7 copy-done.5
  60.5 3.0 %teacher_prob.1 = (f32[512,1024]{1,0:T(8,128)S(1)}, f32[16,128]{1,0:T(8,128)S(1)}) custom-call(s32[4]{0:T(128)S(1)} %pad_add_fusion.refs_0_.core_ref, s32[4,4]{1,0:T(4,128)S(1)} %broadcast_add_fusion.1.refs_1_, bf16[4,4,128,128]{3,2,1,0:T(8,128)(2,1)S(1)} %bitcast.18, f32[2,4,1,128]{3,2,1,0:T(1,128)S(1)} %bitcast.20, s32[4,1,128]{2,1,0:T(1,128)S(1)} %bitcast.21, ...), custom_call_target="tpu_custom_call" | custom-call | flops 1 | bytes 1 | tf_op jit(solution)/shard_map/teacher_prob/pallas_call | solution.py:480
  63.6 1.3 copy-done
  65.0 0.5 collective-permute-start.17
  65.6 0.4 collective-permute-start.13
  66.1 0.3 collective-permute-done.16.refs_12_
  66.6 0.1 collective-permute-done.17.refs_13_
  66.7 0.2 collective-permute-start.18
  67.0 2.7 %collective-permute-done.18.refs_14_ = bf16[64,1536]{1,0:T(8,128)(2,1)S(1)} collective-permute-done((bf16[64,1536]{1,0:T(8,128)(2,1)S(1)}, bf16[64,1536]{1,0:T(8,128)(2,1)S(1)}, u32[]{:S(2)}, u32[]{:S(2)}) %collective-permute-start.18) | collective-permute-done | bytes 196640 | tf_op jit(solution)/shard_map/ppermute | solution.py:133
  69.6 0.2 collective-permute-start.19
  69.9 1.2 collective-permute-done.19.refs_15_
  71.1 0.3 collective-permute-start.21
  71.4 10.7 %logits.1 = (f32[512,1024]{1,0:T(8,128)S(1)}, f32[32,8,128]{2,1,0:T(8,128)S(1)}) custom-call(bf16[64,3584]{1,0:T(8,128)(2,1)S(1)} %pad_maximum_fusion.refs_0_, bf16[64,3584]{1,0:T(8,128)(2,1)S(1)} %collective-permute-done.6.refs_1_, bf16[64,3584]{1,0:T(8,128)(2,1)S(1)} %collective-permute-done.7.refs_2_, ...), custom_call_target="tpu_custom_call" | custom-call | flops 1 | bytes 1 | tf_op jit(solution)/shard_map/logits/pallas_call | solution.py:510
  82.1 11.6 %all_to_all.10.refs_1_ = f32[32,8,128]{2,1,0:T(8,128)S(1)} all-to-all(f32[32,8,128]{2,1,0:T(8,128)S(1)} %get-tuple-element.105), channel_id=1, replica_groups=mesh['vocab'=32] {'vocab'}, dimensions={0} | all-to-all | bytes 262144 | tf_op jit(solution)/shard_map/all_to_all | solution.py:533
  93.7 1.3 grad_logits.1
  95.0 0.3 collective-permute-start.20
  95.3 2.4 %collective-permute-done.20.sib_ref = bf16[512,1024]{1,0:T(8,128)(2,1)S(1)} collective-permute-done((bf16[512,1024]{1,0:T(8,128)(2,1)S(1)}, bf16[512,1024]{1,0:T(8,128)(2,1)S(1)}, u32[]{:S(2)}, u32[]{:S(2)}) %collective-permute-start.20) | collective-permute-done | bytes 1048608 | tf_op jit(solution)/shard_map/ppermute | solution.py:133
  97.7 9.6 %grad_hidden_partial.1 = (f32[4,2,16,1536]{3,2,1,0:T(8,128)S(1)}, bf16[4,2,16,1536]{3,2,1,0:T(8,128)(2,1)S(1)}, bf16[4,2,16,1536]{3,2,1,0:T(8,128)(2,1)S(1)}, bf...) custom-call(s32[4]{0:T(128)S(1)} %pad_add_fusion.refs_0_.core_ref, ...), custom_call_target="tpu_custom_call" | custom-call | flops 1 | bytes 1 | tf_op jit(solution)/shard_map/grad_hidden_partial/pallas_call | solution.py:558
  107.3 0.7 collective-permute-start.25
  108.0 0.2 collective-permute-start.22
  108.2 1.3 collective-permute-start.23
  109.5 2.0 %collective-permute-start.24 = (bf16[4,2,16,1536]{3,2,1,0:T(8,128)(2,1)S(1)}, bf16[4,2,16,1536]{3,2,1,0:T(8,128)(2,1)S(1)}, u32[]{:S(2)}, u32[]{:S(2)}) collective-permute-start(bf16[4,2,16,1536]{3,2,1,0:T(8,128)(2,1)S(1)} %get-tuple-element.121), channel_id=1, source_target_pairs={{0,6},{1,7},{2,4},{3,5},{4,2},{5,3},{6,0},{7,1},{8,14},{9,15},{10,... | collective-permute-start | bytes 1179656 | tf_op jit(solution)/shard_map/ppermute | solution.py:133
  111.5 1.2 collective-permute-start.26
  112.7 5.0 %collective-permute-done.25.refs_5_ = bf16[4,2,16,1024]{3,2,1,0:T(8,128)(2,1)S(1)} collective-permute-done((bf16[4,2,16,1024]{3,2,1,0:T(8,128)(2,1)S(1)}, bf16[4,2,16,1024]{3,2,1,0:T(8,128)(2,1)S(1)}, u32[]{:S(2)}, u32[]{:S(2)}) %collective-permute-start.25) | collective-permute-done | bytes 262176 | tf_op jit(solution)/shard_map/ppermute | solution.py:133
  117.8 1.9 %collective-permute-start.27 = (bf16[4,2,16,1024]{3,2,1,0:T(8,128)(2,1)S(1)}, bf16[4,2,16,1024]{3,2,1,0:T(8,128)(2,1)S(1)}, u32[]{:S(2)}, u32[]{:S(2)}) collective-permute-start(bf16[4,2,16,1024]{3,2,1,0:T(8,128)(2,1)S(1)} %get-tuple-element.124), channel_id=1, source_target_pairs={{0,24},{1,25},{2,26},{3,27},{4,28},{5,29},{6,30},{7,31},{8,16},{9,... | collective-permute-start | bytes 786440 | tf_op jit(solution)/shard_map/ppermute | solution.py:133
  119.6 11.3 %grad_head.1 = bf16[5120,1024]{1,0:T(8,128)(2,1)} custom-call(bf16[64,3584]{1,0:T(8,128)(2,1)S(1)} %pad_maximum_fusion.refs_0_, bf16[64,3584]{1,0:T(8,128)(2,1)S(1)} %collective-permute-done.6.refs_1_, bf16[64,3584]{1,0:T(8,128)(2,1)S(1)} %collective-permute-done.7.refs_2_, bf16[64,3584]{1,0:T(8,128)(2,1)S(1)} %collective-permute-done.8.refs_3_, ...), custom_call_target="tpu_custom_call" | custom-call | flops 1 | bytes 1 | tf_op jit(solution)/shard_map/grad_head/pallas_call | solution.py:582
  130.9 1.5 %collective-permute-done.26.refs_6_ = bf16[4,2,16,1024]{3,2,1,0:T(8,128)(2,1)S(1)} collective-permute-done((bf16[4,2,16,1024]{3,2,1,0:T(8,128)(2,1)S(1)}, bf16[4,2,16,1024]{3,2,1,0:T(8,128)(2,1)S(1)}, u32[]{:S(2)}, u32[]{:S(2)}) %collective-permute-start.26) | collective-permute-done | bytes 262176 | tf_op jit(solution)/shard_map/ppermute | solution.py:133
  132.5 0.3 first_sum.1
  132.8 0.4 collective-permute-start.31
  133.2 4.7 %collective-permute-start.28 = (bf16[2,16,1536]{2,1,0:T(8,128)(2,1)S(1)}, bf16[2,16,1536]{2,1,0:T(8,128)(2,1)S(1)}, u32[]{:S(2)}, u32[]{:S(2)}) collective-permute-start(bf16[2,16,1536]{2,1,0:T(8,128)(2,1)S(1)} %get-tuple-element.136), channel_id=1, source_target_pairs={{0,8},{1,9},{2,10},{3,11},{4,12},{5,13},{6,14},{7,15},{8,0},{9,1},... | collective-permute-start | bytes 294920 | tf_op jit(solution)/shard_map/ppermute | solution.py:133
  138.0 2.3 %collective-permute-start.30 = (bf16[2,16,1536]{2,1,0:T(8,128)(2,1)S(1)}, bf16[2,16,1536]{2,1,0:T(8,128)(2,1)S(1)}, u32[]{:S(2)}, u32[]{:S(2)}) collective-permute-start(bf16[2,16,1536]{2,1,0:T(8,128)(2,1)S(1)} %get-tuple-element.138), channel_id=1, source_target_pairs={{0,24},{1,25},{2,26},{3,27},{4,28},{5,29},{6,30},{7,31},{8,16},{9,... | collective-permute-start | bytes 294920 | tf_op jit(solution)/shard_map/ppermute | solution.py:133
  140.2 1.0 collective-permute-start.32
  141.3 2.1 %collective-permute-start.33 = (bf16[2,16,1024]{2,1,0:T(8,128)(2,1)S(1)}, bf16[2,16,1024]{2,1,0:T(8,128)(2,1)S(1)}, u32[]{:S(2)}, u32[]{:S(2)}) collective-permute-start(bf16[2,16,1024]{2,1,0:T(8,128)(2,1)S(1)} %get-tuple-element.142), channel_id=1, source_target_pairs={{0,6},{1,7},{2,4},{3,5},{4,2},{5,3},{6,0},{7,1},{8,14},{9,15},{10,... | collective-permute-start | bytes 196616 | tf_op jit(solution)/shard_map/ppermute | solution.py:133
  143.3 1.2 collective-permute-done.32.refs_6_
  144.5 1.9 %collective-permute-done.33.refs_7_ = bf16[2,16,1024]{2,1,0:T(8,128)(2,1)S(1)} collective-permute-done((bf16[2,16,1024]{2,1,0:T(8,128)(2,1)S(1)}, bf16[2,16,1024]{2,1,0:T(8,128)(2,1)S(1)}, u32[]{:S(2)}, u32[]{:S(2)}) %collective-permute-start.33) | collective-permute-done | bytes 65568 | tf_op jit(solution)/shard_map/ppermute | solution.py:133
  146.4 0.2 collective-permute-done.29.refs_2_
  146.7 0.6 slice_reduce_fusion
  147.4 0.6 collective-permute-done.34
  148.0 0.7 pad_maximum_fusion.2
  (61 shorter events, 1.8 us)
Async XLA Ops:
  1.4 13.9 %collective-permute-start.5 = (bf16[16,1536]{1,0:T(8,128)(2,1)S(1)}, bf16[16,1536]{1,0:T(8,128)(2,1)S(1)}, u32[]{:S(2)}, u32[]{:S(2)}) collective-permute-start(bf16[16,1536]{1,0:T(8,128)(2,1)S(1)} %slice.19), channel_id=1, source_target_pairs={{0,6},{1,7},{2,4},{3,5},{4,2},{5,3},{6,0},{7,1},{8,14},{9,15},{10,... | collective-permute-start | bytes 147464 | tf_op jit(solution)/shard_map/ppermute | solution.py:133
  5.3 10.7 %collective-permute-start.4 = (bf16[16,1536]{1,0:T(8,128)(2,1)S(1)}, bf16[16,1536]{1,0:T(8,128)(2,1)S(1)}, u32[]{:S(2)}, u32[]{:S(2)}) collective-permute-start(bf16[16,1536]{1,0:T(8,128)(2,1)S(1)} %slice.19), channel_id=1, source_target_pairs={{0,4},{1,5},{2,6},{3,7},{4,0},{5,1},{6,2},{7,3},{8,12},{9,13},{10,... | collective-permute-start | bytes 147464 | tf_op jit(solution)/shard_map/ppermute | solution.py:133
  5.8 10.2 %collective-permute-start.3 = (bf16[16,1536]{1,0:T(8,128)(2,1)S(1)}, bf16[16,1536]{1,0:T(8,128)(2,1)S(1)}, u32[]{:S(2)}, u32[]{:S(2)}) collective-permute-start(bf16[16,1536]{1,0:T(8,128)(2,1)S(1)} %slice.19), channel_id=1, source_target_pairs={{0,2},{1,3},{2,0},{3,1},{4,6},{5,7},{6,4},{7,5},{8,10},{9,11},{10,... | collective-permute-start | bytes 147464 | tf_op jit(solution)/shard_map/ppermute | solution.py:133
  6.8 9.2 %collective-permute-start.2 = (bf16[16,3584]{1,0:T(8,128)(2,1)S(1)}, bf16[16,3584]{1,0:T(8,128)(2,1)S(1)}, u32[]{:S(2)}, u32[]{:S(2)}) collective-permute-start(bf16[16,3584]{1,0:T(8,128)(2,1)S(1)} %slice.18), channel_id=1, source_target_pairs={{0,24},{1,25},{2,26},{3,27},{4,28},{5,29},{6,30},{7,31},{8,16},{9,... | collective-permute-start | bytes 344072 | tf_op jit(solution)/shard_map/ppermute | solution.py:133
  10.9 8.9 %collective-permute-start.1 = (bf16[16,3584]{1,0:T(8,128)(2,1)S(1)}, bf16[16,3584]{1,0:T(8,128)(2,1)S(1)}, u32[]{:S(2)}, u32[]{:S(2)}) collective-permute-start(bf16[16,3584]{1,0:T(8,128)(2,1)S(1)} %slice.18), channel_id=1, source_target_pairs={{0,16},{1,17},{2,18},{3,19},{4,20},{5,21},{6,22},{7,23},{8,24},{9,... | collective-permute-start | bytes 344072 | tf_op jit(solution)/shard_map/ppermute | solution.py:133
  12.3 1.0 copy-start.3
  15.4 6.0 %collective-permute-start = (bf16[16,3584]{1,0:T(8,128)(2,1)S(1)}, bf16[16,3584]{1,0:T(8,128)(2,1)S(1)}, u32[]{:S(2)}, u32[]{:S(2)}) collective-permute-start(bf16[16,3584]{1,0:T(8,128)(2,1)S(1)} %slice.18), channel_id=1, source_target_pairs={{0,8},{1,9},{2,10},{3,11},{4,12},{5,13},{6,14},{7,15},{8,0},{9,1},... | collective-permute-start | bytes 344072 | tf_op jit(solution)/shard_map/ppermute | solution.py:133
  21.4 6.0 %collective-permute-start.9 = (bf16[64,1536]{1,0:T(8,128)(2,1)S(1)}, bf16[64,1536]{1,0:T(8,128)(2,1)S(1)}, u32[]{:S(2)}, u32[]{:S(2)}) collective-permute-start(bf16[64,1536]{1,0:T(8,128)(2,1)S(1)} %pad_maximum_fusion.1.refs_8_), channel_id=1, source_target_pairs={{0,8},{1,9},{2,10},{3,11},{4,12},{5,13},{6,14},{7,15},{8,0},{9,1},... | collective-permute-start | bytes 589832 | tf_op jit(solution)/shard_map/ppermute | solution.py:133
  27.4 29.4 %all-to-all-start = ((bf16[32,67,128]{2,1,0:T(8,128)(2,1)}), bf16[32,67,128]{2,1,0:T(8,128)(2,1)S(1)}, u32[]{:S(2)}, u32[]{:S(2)}) async-start(bf16[32,67,128]{2,1,0:T(8,128)(2,1)} %slice.24), calls=%async_computation | async-start | bytes 1179648 | tf_op jit(solution)/shard_map/all_to_all | solution.py:477
  31.6 33.3 %collective-permute-start.8 = (bf16[64,3584]{1,0:T(8,128)(2,1)S(1)}, bf16[64,3584]{1,0:T(8,128)(2,1)S(1)}, u32[]{:S(2)}, u32[]{:S(2)}) collective-permute-start(bf16[64,3584]{1,0:T(8,128)(2,1)S(1)} %pad_maximum_fusion.refs_0_), channel_id=1, source_target_pairs={{0,6},{1,7},{2,4},{3,5},{4,2},{5,3},{6,0},{7,1},{8,14},{9,15},{10,... | collective-permute-start | bytes 1376264 | tf_op jit(solution)/shard_map/ppermute | solution.py:133
  34.3 30.6 %collective-permute-start.7 = (bf16[64,3584]{1,0:T(8,128)(2,1)S(1)}, bf16[64,3584]{1,0:T(8,128)(2,1)S(1)}, u32[]{:S(2)}, u32[]{:S(2)}) collective-permute-start(bf16[64,3584]{1,0:T(8,128)(2,1)S(1)} %pad_maximum_fusion.refs_0_), channel_id=1, source_target_pairs={{0,4},{1,5},{2,6},{3,7},{4,0},{5,1},{6,2},{7,3},{8,12},{9,13},{10,... | collective-permute-start | bytes 1376264 | tf_op jit(solution)/shard_map/ppermute | solution.py:133
  34.9 30.0 %collective-permute-start.6 = (bf16[64,3584]{1,0:T(8,128)(2,1)S(1)}, bf16[64,3584]{1,0:T(8,128)(2,1)S(1)}, u32[]{:S(2)}, u32[]{:S(2)}) collective-permute-start(bf16[64,3584]{1,0:T(8,128)(2,1)S(1)} %pad_maximum_fusion.refs_0_), channel_id=1, source_target_pairs={{0,2},{1,3},{2,0},{3,1},{4,6},{5,7},{6,4},{7,5},{8,10},{9,11},{10,... | collective-permute-start | bytes 1376264 | tf_op jit(solution)/shard_map/ppermute | solution.py:133
  35.4 29.5 %collective-permute-start.11 = (bf16[64,1536]{1,0:T(8,128)(2,1)S(1)}, bf16[64,1536]{1,0:T(8,128)(2,1)S(1)}, u32[]{:S(2)}, u32[]{:S(2)}) collective-permute-start(bf16[64,1536]{1,0:T(8,128)(2,1)S(1)} %pad_maximum_fusion.1.refs_8_), channel_id=1, source_target_pairs={{0,24},{1,25},{2,26},{3,27},{4,28},{5,29},{6,30},{7,31},{8,16},{9,... | collective-permute-start | bytes 589832 | tf_op jit(solution)/shard_map/ppermute | solution.py:133
  39.1 25.8 %collective-permute-start.10 = (bf16[64,1536]{1,0:T(8,128)(2,1)S(1)}, bf16[64,1536]{1,0:T(8,128)(2,1)S(1)}, u32[]{:S(2)}, u32[]{:S(2)}) collective-permute-start(bf16[64,1536]{1,0:T(8,128)(2,1)S(1)} %pad_maximum_fusion.1.refs_8_), channel_id=1, source_target_pairs={{0,16},{1,17},{2,18},{3,19},{4,20},{5,21},{6,22},{7,23},{8,24},{9,... | collective-permute-start | bytes 589832 | tf_op jit(solution)/shard_map/ppermute | solution.py:133
  39.2 54.5 %copy-start.6 = (f32[512]{0:T(512)S(1)}, f32[512]{0:T(512)}, u32[]{:S(2)}) copy-start(f32[512]{0:T(512)} %param.13) | copy-start | bytes 6148
  56.9 0.8 copy-start.7
  59.2 0.7 copy-start.4
  59.8 0.7 copy-start.5
  63.6 1.3 copy-start
  64.9 28.8 %copy-start.1 = (f32[512,1024]{1,0:T(8,128)S(1)}, f32[512,1024]{1,0:T(8,128)}, u32[]{:S(2)}) copy-start(f32[512,1024]{1,0:T(8,128)} %copy-done) | copy-start | bytes 6291460
  64.9 1.5 %collective-permute-start.16 = (bf16[64,1536]{1,0:T(8,128)(2,1)S(1)}, bf16[64,1536]{1,0:T(8,128)(2,1)S(1)}, u32[]{:S(2)}, u32[]{:S(2)}) collective-permute-start(bf16[64,1536]{1,0:T(8,128)(2,1)S(1)} %pad_maximum_fusion.1.refs_8_), channel_id=1, source_target_pairs={{0,1},{1,0},{2,3},{3,2},{4,5},{5,4},{6,7},{7,6},{8,9},{9,8},{10,11... | collective-permute-start | bytes 589832 | tf_op jit(solution)/shard_map/ppermute | solution.py:133
  65.0 1.7 %collective-permute-start.17 = (bf16[64,1536]{1,0:T(8,128)(2,1)S(1)}, bf16[64,1536]{1,0:T(8,128)(2,1)S(1)}, u32[]{:S(2)}, u32[]{:S(2)}) collective-permute-start(bf16[64,1536]{1,0:T(8,128)(2,1)S(1)} %collective-permute-done.9.refs_9_), channel_id=1, source_target_pairs={{0,1},{1,0},{2,3},{3,2},{4,5},{5,4},{6,7},{7,6},{8,9},{9,8},{10,11... | collective-permute-start | bytes 589832 | tf_op jit(solution)/shard_map/ppermute | solution.py:133
  65.5 5.6 %collective-permute-start.12 = (bf16[64,3584]{1,0:T(8,128)(2,1)S(1)}, bf16[64,3584]{1,0:T(8,128)(2,1)S(1)}, u32[]{:S(2)}, u32[]{:S(2)}) collective-permute-start(bf16[64,3584]{1,0:T(8,128)(2,1)S(1)} %pad_maximum_fusion.refs_0_), channel_id=1, source_target_pairs={{0,1},{1,0},{2,3},{3,2},{4,5},{5,4},{6,7},{7,6},{8,9},{9,8},{10,11... | collective-permute-start | bytes 1376264 | tf_op jit(solution)/shard_map/ppermute | solution.py:133
  65.6 5.5 %collective-permute-start.13 = (bf16[64,3584]{1,0:T(8,128)(2,1)S(1)}, bf16[64,3584]{1,0:T(8,128)(2,1)S(1)}, u32[]{:S(2)}, u32[]{:S(2)}) collective-permute-start(bf16[64,3584]{1,0:T(8,128)(2,1)S(1)} %collective-permute-done.6.refs_1_), channel_id=1, source_target_pairs={{0,1},{1,0},{2,3},{3,2},{4,5},{5,4},{6,7},{7,6},{8,9},{9,8},{10,11... | collective-permute-start | bytes 1376264 | tf_op jit(solution)/shard_map/ppermute | solution.py:133
  66.0 5.1 %collective-permute-start.14 = (bf16[64,3584]{1,0:T(8,128)(2,1)S(1)}, bf16[64,3584]{1,0:T(8,128)(2,1)S(1)}, u32[]{:S(2)}, u32[]{:S(2)}) collective-permute-start(bf16[64,3584]{1,0:T(8,128)(2,1)S(1)} %collective-permute-done.7.refs_2_), channel_id=1, source_target_pairs={{0,1},{1,0},{2,3},{3,2},{4,5},{5,4},{6,7},{7,6},{8,9},{9,8},{10,11... | collective-permute-start | bytes 1376264 | tf_op jit(solution)/shard_map/ppermute | solution.py:133
  66.4 4.6 %collective-permute-start.15 = (bf16[64,3584]{1,0:T(8,128)(2,1)S(1)}, bf16[64,3584]{1,0:T(8,128)(2,1)S(1)}, u32[]{:S(2)}, u32[]{:S(2)}) collective-permute-start(bf16[64,3584]{1,0:T(8,128)(2,1)S(1)} %collective-permute-done.8.refs_3_), channel_id=1, source_target_pairs={{0,1},{1,0},{2,3},{3,2},{4,5},{5,4},{6,7},{7,6},{8,9},{9,8},{10,11... | collective-permute-start | bytes 1376264 | tf_op jit(solution)/shard_map/ppermute | solution.py:133
  66.7 2.9 %collective-permute-start.18 = (bf16[64,1536]{1,0:T(8,128)(2,1)S(1)}, bf16[64,1536]{1,0:T(8,128)(2,1)S(1)}, u32[]{:S(2)}, u32[]{:S(2)}) collective-permute-start(bf16[64,1536]{1,0:T(8,128)(2,1)S(1)} %collective-permute-done.10.refs_10_), channel_id=1, source_target_pairs={{0,1},{1,0},{2,3},{3,2},{4,5},{5,4},{6,7},{7,6},{8,9},{9,8},{10,11... | collective-permute-start | bytes 589832 | tf_op jit(solution)/shard_map/ppermute | solution.py:133
  69.6 1.4 collective-permute-start.19
  71.1 26.6 %collective-permute-start.21 = (bf16[5120,1024]{1,0:T(8,128)(2,1)}, bf16[5120,1024]{1,0:T(8,128)(2,1)}, u32[]{:S(2)}, u32[]{:S(2)}) collective-permute-start(bf16[5120,1024]{1,0:T(8,128)(2,1)} %w_ref.1), channel_id=1, source_target_pairs={{0,1},{1,0},{2,3},{3,2},{4,5},{5,4},{6,7},{7,6},{8,9},{9,8},{10,11... | collective-permute-start | bytes 31457288 | tf_op jit(solution)/shard_map/ppermute | solution.py:133
  95.0 12.3 %copy-start.2 = (bf16[512,1024]{1,0:T(8,128)(2,1)}, bf16[512,1024]{1,0:T(8,128)(2,1)S(1)}, u32[]{:S(2)}) copy-start(bf16[512,1024]{1,0:T(8,128)(2,1)S(1)} %get-tuple-element.125.grad_ref.refs_16_) | copy-start | bytes 3145732
  95.0 2.7 %collective-permute-start.20 = (bf16[512,1024]{1,0:T(8,128)(2,1)S(1)}, bf16[512,1024]{1,0:T(8,128)(2,1)S(1)}, u32[]{:S(2)}, u32[]{:S(2)}) collective-permute-start(bf16[512,1024]{1,0:T(8,128)(2,1)S(1)} %get-tuple-element.125.grad_ref.refs_16_), channel_id=1, source_target_pairs={{0,1},{1,0},{2,3},{3,2},{4,5},{5,4},{6,7},{7,6},{8,9},{9,8},{10,11... | collective-permute-start | bytes 3145736 | tf_op jit(solution)/shard_map/ppermute | solution.py:133
  107.3 10.5 %collective-permute-start.25 = (bf16[4,2,16,1024]{3,2,1,0:T(8,128)(2,1)S(1)}, bf16[4,2,16,1024]{3,2,1,0:T(8,128)(2,1)S(1)}, u32[]{:S(2)}, u32[]{:S(2)}) collective-permute-start(bf16[4,2,16,1024]{3,2,1,0:T(8,128)(2,1)S(1)} %get-tuple-element.122), channel_id=1, source_target_pairs={{0,8},{1,9},{2,10},{3,11},{4,12},{5,13},{6,14},{7,15},{8,0},{9,1},... | collective-permute-start | bytes 786440 | tf_op jit(solution)/shard_map/ppermute | solution.py:133
  108.0 24.5 %collective-permute-start.22 = (bf16[4,2,16,1536]{3,2,1,0:T(8,128)(2,1)S(1)}, bf16[4,2,16,1536]{3,2,1,0:T(8,128)(2,1)S(1)}, u32[]{:S(2)}, u32[]{:S(2)}) collective-permute-start(bf16[4,2,16,1536]{3,2,1,0:T(8,128)(2,1)S(1)} %get-tuple-element.119), channel_id=1, source_target_pairs={{0,2},{1,3},{2,0},{3,1},{4,6},{5,7},{6,4},{7,5},{8,10},{9,11},{10,... | collective-permute-start | bytes 1179656 | tf_op jit(solution)/shard_map/ppermute | solution.py:133
  108.2 24.3 %collective-permute-start.23 = (bf16[4,2,16,1536]{3,2,1,0:T(8,128)(2,1)S(1)}, bf16[4,2,16,1536]{3,2,1,0:T(8,128)(2,1)S(1)}, u32[]{:S(2)}, u32[]{:S(2)}) collective-permute-start(bf16[4,2,16,1536]{3,2,1,0:T(8,128)(2,1)S(1)} %get-tuple-element.120), channel_id=1, source_target_pairs={{0,4},{1,5},{2,6},{3,7},{4,0},{5,1},{6,2},{7,3},{8,12},{9,13},{10,... | collective-permute-start | bytes 1179656 | tf_op jit(solution)/shard_map/ppermute | solution.py:133
  109.5 23.0 %collective-permute-start.24 = (bf16[4,2,16,1536]{3,2,1,0:T(8,128)(2,1)S(1)}, bf16[4,2,16,1536]{3,2,1,0:T(8,128)(2,1)S(1)}, u32[]{:S(2)}, u32[]{:S(2)}) collective-permute-start(bf16[4,2,16,1536]{3,2,1,0:T(8,128)(2,1)S(1)} %get-tuple-element.121), channel_id=1, source_target_pairs={{0,6},{1,7},{2,4},{3,5},{4,2},{5,3},{6,0},{7,1},{8,14},{9,15},{10,... | collective-permute-start | bytes 1179656 | tf_op jit(solution)/shard_map/ppermute | solution.py:133
  111.5 21.0 %collective-permute-start.26 = (bf16[4,2,16,1024]{3,2,1,0:T(8,128)(2,1)S(1)}, bf16[4,2,16,1024]{3,2,1,0:T(8,128)(2,1)S(1)}, u32[]{:S(2)}, u32[]{:S(2)}) collective-permute-start(bf16[4,2,16,1024]{3,2,1,0:T(8,128)(2,1)S(1)} %get-tuple-element.123), channel_id=1, source_target_pairs={{0,16},{1,17},{2,18},{3,19},{4,20},{5,21},{6,22},{7,23},{8,24},{9,... | collective-permute-start | bytes 786440 | tf_op jit(solution)/shard_map/ppermute | solution.py:133
  117.8 14.7 %collective-permute-start.27 = (bf16[4,2,16,1024]{3,2,1,0:T(8,128)(2,1)S(1)}, bf16[4,2,16,1024]{3,2,1,0:T(8,128)(2,1)S(1)}, u32[]{:S(2)}, u32[]{:S(2)}) collective-permute-start(bf16[4,2,16,1024]{3,2,1,0:T(8,128)(2,1)S(1)} %get-tuple-element.124), channel_id=1, source_target_pairs={{0,24},{1,25},{2,26},{3,27},{4,28},{5,29},{6,30},{7,31},{8,16},{9,... | collective-permute-start | bytes 786440 | tf_op jit(solution)/shard_map/ppermute | solution.py:133
  132.8 8.5 %collective-permute-start.31 = (bf16[2,16,1024]{2,1,0:T(8,128)(2,1)S(1)}, bf16[2,16,1024]{2,1,0:T(8,128)(2,1)S(1)}, u32[]{:S(2)}, u32[]{:S(2)}) collective-permute-start(bf16[2,16,1024]{2,1,0:T(8,128)(2,1)S(1)} %get-tuple-element.140), channel_id=1, source_target_pairs={{0,2},{1,3},{2,0},{3,1},{4,6},{5,7},{6,4},{7,5},{8,10},{9,11},{10,... | collective-permute-start | bytes 196616 | tf_op jit(solution)/shard_map/ppermute | solution.py:133
  133.2 13.3 %collective-permute-start.28 = (bf16[2,16,1536]{2,1,0:T(8,128)(2,1)S(1)}, bf16[2,16,1536]{2,1,0:T(8,128)(2,1)S(1)}, u32[]{:S(2)}, u32[]{:S(2)}) collective-permute-start(bf16[2,16,1536]{2,1,0:T(8,128)(2,1)S(1)} %get-tuple-element.136), channel_id=1, source_target_pairs={{0,8},{1,9},{2,10},{3,11},{4,12},{5,13},{6,14},{7,15},{8,0},{9,1},... | collective-permute-start | bytes 294920 | tf_op jit(solution)/shard_map/ppermute | solution.py:133
  137.9 8.7 %collective-permute-start.29 = (bf16[2,16,1536]{2,1,0:T(8,128)(2,1)S(1)}, bf16[2,16,1536]{2,1,0:T(8,128)(2,1)S(1)}, u32[]{:S(2)}, u32[]{:S(2)}) collective-permute-start(bf16[2,16,1536]{2,1,0:T(8,128)(2,1)S(1)} %get-tuple-element.137), channel_id=1, source_target_pairs={{0,16},{1,17},{2,18},{3,19},{4,20},{5,21},{6,22},{7,23},{8,24},{9,... | collective-permute-start | bytes 294920 | tf_op jit(solution)/shard_map/ppermute | solution.py:133
  138.0 8.6 %collective-permute-start.30 = (bf16[2,16,1536]{2,1,0:T(8,128)(2,1)S(1)}, bf16[2,16,1536]{2,1,0:T(8,128)(2,1)S(1)}, u32[]{:S(2)}, u32[]{:S(2)}) collective-permute-start(bf16[2,16,1536]{2,1,0:T(8,128)(2,1)S(1)} %get-tuple-element.138), channel_id=1, source_target_pairs={{0,24},{1,25},{2,26},{3,27},{4,28},{5,29},{6,30},{7,31},{8,16},{9,... | collective-permute-start | bytes 294920 | tf_op jit(solution)/shard_map/ppermute | solution.py:133
  140.2 4.3 %collective-permute-start.32 = (bf16[2,16,1024]{2,1,0:T(8,128)(2,1)S(1)}, bf16[2,16,1024]{2,1,0:T(8,128)(2,1)S(1)}, u32[]{:S(2)}, u32[]{:S(2)}) collective-permute-start(bf16[2,16,1024]{2,1,0:T(8,128)(2,1)S(1)} %get-tuple-element.141), channel_id=1, source_target_pairs={{0,4},{1,5},{2,6},{3,7},{4,0},{5,1},{6,2},{7,3},{8,12},{9,13},{10,... | collective-permute-start | bytes 196616 | tf_op jit(solution)/shard_map/ppermute | solution.py:133
  141.3 5.2 %collective-permute-start.33 = (bf16[2,16,1024]{2,1,0:T(8,128)(2,1)S(1)}, bf16[2,16,1024]{2,1,0:T(8,128)(2,1)S(1)}, u32[]{:S(2)}, u32[]{:S(2)}) collective-permute-start(bf16[2,16,1024]{2,1,0:T(8,128)(2,1)S(1)} %get-tuple-element.142), channel_id=1, source_target_pairs={{0,6},{1,7},{2,4},{3,5},{4,2},{5,3},{6,0},{7,1},{8,14},{9,15},{10,... | collective-permute-start | bytes 196616 | tf_op jit(solution)/shard_map/ppermute | solution.py:133
  146.7 1.3 collective-permute-start.34

commit v11 on v10

--- a/solution.py
+++ b/solution.py
@@ -186,6 +186,12 @@
             layer, chip = (i, g) if by_layer else (g, i)
             block = layer * GROUP + core * CHIPS + chip
             out_ref[pl.ds(block * rows, rows), columns] = piece[pl.ds(g * rows, rows), :]
+
+
+def cut_kernel(x_ref, narrow_ref, wide_ref):
+    split = wide_ref.shape[1]
+    wide_ref[...] = x_ref[:, :split]
+    narrow_ref[...] = x_ref[:, split:]
 
 
 def logits_kernel(rows, wide_count, *refs):
@@ -462,19 +468,27 @@
     pos = jnp.stack([core, chip, layer, rank]).astype(jnp.int32)
     unlisted = float(n * slab - side * listed_count)
 
-    narrow = depth * 3 // 10 // 512 * 512
+    narrow = depth // 4
     wide = depth - narrow
-    column = [hidden_states[:, :wide]]
-    column += [shift(column[0], k * GROUP) for k in range(1, layers)]
-    plane = [hidden_states[:, wide:]]
-    plane += [shift(plane[0], j * CORES) for j in range(1, CHIPS)]
+    own_narrow, own_wide = pl.pallas_call(
+        cut_kernel,
+        in_specs=[vmem_spec()],
+        out_specs=[vmem_spec()] * 2,
+        out_shape=[jax.ShapeDtypeStruct((rows, size), bf16) for size in (narrow, wide)],
+        compiler_params=kernel_params(),
+        cost_estimate=LIGHT,
+        name="cut_columns",
+    )(hidden_states)
+    plane = [own_narrow] + [shift(own_narrow, j * CORES) for j in range(1, CHIPS)]
+    column = [own_wide] + [shift(own_wide, k * GROUP) for k in range(1, layers)]
     payload, place = pack_teacher(teacher_logits, block_lists, slab // side)
-    column, plane = jnp.concatenate(column, axis=0), jnp.concatenate(plane, axis=0)
-    column, plane, payload = lax.optimization_barrier((column, plane, payload[:, : 3 - STAT_ROWS]))
+    arrived = lax.all_to_all(
+        payload[:, : 3 - STAT_ROWS], "vocab", split_axis=0, concat_axis=0, tiled=True
+    )
+    plane, column = jnp.concatenate(plane, axis=0), jnp.concatenate(column, axis=0)
+    plane, column = lax.optimization_barrier((plane, column))
     wide_pieces = [column] + [shift(column, j * CORES) for j in range(1, CHIPS)]
     narrow_pieces = [plane] + [shift(plane, k * GROUP) for k in range(1, layers)]
-    narrow_pieces[1], payload = lax.optimization_barrier((narrow_pieces[1], payload))
-    arrived = lax.all_to_all(payload, "vocab", split_axis=0, concat_axis=0, tiled=True)
     arrived_blocks, arrived_stat = unpack_teacher(arrived, blocks, stored)
 
     prob, entropy = pl.pallas_call(
@@ -577,7 +591,7 @@
     wide_sums = [shift(partial[j], j * CORES) for j in range(1, CHIPS)]
     narrow_sums = [shift(partial[CHIPS + k], k * GROUP) for k in range(1, layers)]
 
-    head_tile = 512
+    head_tile = narrow
     head_steps = wide // head_tile
     grad_head = pl.pallas_call(
         functools.partial(head_kernel, rows, len(wide_pieces), head_steps),

time: 149 us -> 146 us (0.980)
  waiting for transfers between devices: 46.3 us -> 34.6 us
  starting transfers between devices: 40.9 us -> 50.1 us
  blocking collectives: 11.6 us -> 13.5 us
  Pallas kernels: 37.5 us -> 35.8 us
    all_to_all x1, waiting for transfers between devices: 17.7 us -> 0.01 us  [levels_plan(): lax.all_to_all(payload[:, :3 - STAT_ROWS], 'vocab', split_axis=0, concat_...]
    ppermute x35, starting transfers between devices: 36.8 us -> 45 us  [shift(): return lax.ppermute(x, 'vocab', [(i, i ^ distance) for i in range(n)])]
    ppermute x35, waiting for transfers between devices: 28.6 us -> 34.6 us  [shift(): return lax.ppermute(x, 'vocab', [(i, i ^ distance) for i in range(n)])]
    all_to_all x1, blocking collectives: 11.6 us -> 13.5 us  [levels_plan(): lax.all_to_all(stat, 'vocab', split_axis=0, concat_axis=0, tiled=True)]
    slice x2 -> x0, local copies, waits for them, and re-layouts: 1.71 us -> none  [the longest x1 0.91 us: levels_plan(): column = [hidden_states[:, :wide]]]
    pallas_call x1, Pallas kernels: 11.3 us -> 9.69 us  [levels_plan(): pl.pallas_call(functools.partial(head_kernel, rows, len(wide_pieces), hea...]
    unnamed x16 -> x18, local copies, waits for them, and re-layouts: 4.38 us -> 5.29 us
  transfers between devices with their start and end apart: 36 -> 36, of which waited for: 15 -> 13; matrix products, arithmetic and copies ran while one was open for 4% -> 3% of each run, Pallas kernels for 19% -> 18%
where the time goes in v11:
time: 146 us
  starting transfers between devices  50.1 us (34%)
  Pallas kernels  35.8 us (25%)
  waiting for transfers between devices  34.6 us (24%)
  blocking collectives  13.5 us (9%)
  local copies, waits for them, and re-layouts  7.72 us (5%)
  other arithmetic  2.94 us (2%)
    ppermute x35, starting transfers between devices, shift(): return lax.ppermute(x, 'vocab', [(i, i ^ distance) for i in range(n)])  45 us
    ppermute x35, waiting for transfers between devices, shift(): return lax.ppermute(x, 'vocab', [(i, i ^ distance) for i in range(n)])  34.6 us
    all_to_all x1, blocking collectives, levels_plan(): lax.all_to_all(stat, 'vocab', split_axis=0, concat_axis=0, tiled=True)  13.5 us
    pallas_call x1, Pallas kernels, levels_plan(): pl.pallas_call(functools.partial(logits_kernel, rows, len(wide_pieces)),...  10.6 us
    pallas_call x1, Pallas kernels, levels_plan(): pl.pallas_call(functools.partial(head_kernel, rows, len(wide_pieces), hea...  9.69 us
    pallas_call x1, Pallas kernels, levels_plan(): pl.pallas_call(functools.partial(partial_kernel, rows, wide_steps), grid_...  9.55 us
    unnamed x18, local copies, waits for them, and re-layouts  5.29 us
    all_to_all x1, starting transfers between devices, levels_plan(): lax.all_to_all(payload[:, :3 - STAT_ROWS], 'vocab', split_axis=0, concat_...  5.17 us
  transfers between devices with their start and end apart: 36, of which 13 were waited for; matrix products, arithmetic and copies ran while one was open for 3% of the time, Pallas kernels for 18%

profile of v11, /device:TPU:0, one launch (start us, length us, event | category | flops | bytes accessed | tf_op | source)
XLA Modules:
  0.0 145.8 jit_solution(8867652231825290875)
XLA Ops:
  0.6 0.9 copy-done.4
  1.6 4.0 %collective-permute-start.2 = (bf16[16,1280]{1,0:T(8,128)(2,1)S(1)}, bf16[16,1280]{1,0:T(8,128)(2,1)S(1)}, u32[]{:S(2)}, u32[]{:S(2)}) collective-permute-start(bf16[16,1280]{1,0:T(8,128)(2,1)S(1)} %get-tuple-element.73), channel_id=1, source_target_pairs={{0,6},{1,7},{2,4},{3,5},{4,2},{5,3},{6,0},{7,1},{8,14},{9,15},{10,... | collective-permute-start | bytes 122888 | tf_op jit(solution)/shard_map/ppermute | solution.py:133
  5.5 0.5 collective-permute-start.1
  6.0 0.1 collective-permute-start
  6.2 4.0 %collective-permute-start.5 = (bf16[16,3840]{1,0:T(8,128)(2,1)S(1)}, bf16[16,3840]{1,0:T(8,128)(2,1)S(1)}, u32[]{:S(2)}, u32[]{:S(2)}) collective-permute-start(bf16[16,3840]{1,0:T(8,128)(2,1)S(1)} %get-tuple-element.74), channel_id=1, source_target_pairs={{0,24},{1,25},{2,26},{3,27},{4,28},{5,29},{6,30},{7,31},{8,16},{9,... | collective-permute-start | bytes 368648 | tf_op jit(solution)/shard_map/ppermute | solution.py:133
  10.2 0.7 add_select_fusion.1
  10.9 0.2 convert_reduce_fusion
  11.6 0.9 copy-done.3
  12.5 1.3 pack_teacher.1
  13.8 0.9 slice.16
  14.6 5.2 %all-to-all-start = ((bf16[32,67,128]{2,1,0:T(8,128)(2,1)}), bf16[32,67,128]{2,1,0:T(8,128)(2,1)S(1)}, u32[]{:S(2)}, u32[]{:S(2)}) async-start(bf16[32,67,128]{2,1,0:T(8,128)(2,1)} %slice.16), calls=%async_computation | async-start | bytes 1179648 | tf_op jit(solution)/shard_map/all_to_all | solution.py:485
  19.8 1.8 %collective-permute-start.3 = (bf16[16,3840]{1,0:T(8,128)(2,1)S(1)}, bf16[16,3840]{1,0:T(8,128)(2,1)S(1)}, u32[]{:S(2)}, u32[]{:S(2)}) collective-permute-start(bf16[16,3840]{1,0:T(8,128)(2,1)S(1)} %get-tuple-element.74), channel_id=1, source_target_pairs={{0,8},{1,9},{2,10},{3,11},{4,12},{5,13},{6,14},{7,15},{8,0},{9,1},... | collective-permute-start | bytes 368648 | tf_op jit(solution)/shard_map/ppermute | solution.py:133
  21.7 11.5 %collective-permute-done.3 = bf16[16,3840]{1,0:T(8,128)(2,1)S(1)} collective-permute-done((bf16[16,3840]{1,0:T(8,128)(2,1)S(1)}, bf16[16,3840]{1,0:T(8,128)(2,1)S(1)}, u32[]{:S(2)}, u32[]{:S(2)}) %collective-permute-start.3) | collective-permute-done | bytes 122912 | tf_op jit(solution)/shard_map/ppermute | solution.py:133
  33.3 2.6 %collective-permute-start.8 = (bf16[64,3840]{1,0:T(8,128)(2,1)S(1)}, bf16[64,3840]{1,0:T(8,128)(2,1)S(1)}, u32[]{:S(2)}, u32[]{:S(2)}) collective-permute-start(bf16[64,3840]{1,0:T(8,128)(2,1)S(1)} %pad_maximum_fusion.refs_0_), channel_id=1, source_target_pairs={{0,6},{1,7},{2,4},{3,5},{4,2},{5,3},{6,0},{7,1},{8,14},{9,15},{10,... | collective-permute-start | bytes 1474568 | tf_op jit(solution)/shard_map/ppermute | solution.py:133
  35.9 0.6 collective-permute-start.7
  36.5 0.3 collective-permute-start.6
  36.8 0.2 select_reduce_fusion
  37.1 3.2 %collective-permute-start.11 = (bf16[64,1280]{1,0:T(8,128)(2,1)S(1)}, bf16[64,1280]{1,0:T(8,128)(2,1)S(1)}, u32[]{:S(2)}, u32[]{:S(2)}) collective-permute-start(bf16[64,1280]{1,0:T(8,128)(2,1)S(1)} %pad_maximum_fusion.1.refs_8_), channel_id=1, source_target_pairs={{0,24},{1,25},{2,26},{3,27},{4,28},{5,29},{6,30},{7,31},{8,16},{9,... | collective-permute-start | bytes 491528 | tf_op jit(solution)/shard_map/ppermute | solution.py:133
  40.2 1.0 collective-permute-start.10
  41.2 4.2 %collective-permute-done.11.refs_11_ = bf16[64,1280]{1,0:T(8,128)(2,1)S(1)} collective-permute-done((bf16[64,1280]{1,0:T(8,128)(2,1)S(1)}, bf16[64,1280]{1,0:T(8,128)(2,1)S(1)}, u32[]{:S(2)}, u32[]{:S(2)}) %collective-permute-start.11) | collective-permute-done | bytes 163872 | tf_op jit(solution)/shard_map/ppermute | solution.py:133
  45.5 6.5 %collective-permute-start.9 = (bf16[64,1280]{1,0:T(8,128)(2,1)S(1)}, bf16[64,1280]{1,0:T(8,128)(2,1)S(1)}, u32[]{:S(2)}, u32[]{:S(2)}) collective-permute-start(bf16[64,1280]{1,0:T(8,128)(2,1)S(1)} %pad_maximum_fusion.1.refs_8_), channel_id=1, source_target_pairs={{0,8},{1,9},{2,10},{3,11},{4,12},{5,13},{6,14},{7,15},{8,0},{9,1},... | collective-permute-start | bytes 491528 | tf_op jit(solution)/shard_map/ppermute | solution.py:133
  52.1 0.8 copy-done.8
  52.8 0.2 copy.27
  53.1 0.9 convert_reduce_fusion.1
  54.3 0.7 copy-done.5
  55.0 0.7 copy-done.6
  55.7 3.1 %teacher_prob.1 = (f32[512,1024]{1,0:T(8,128)S(1)}, f32[16,128]{1,0:T(8,128)S(1)}) custom-call(s32[4]{0:T(128)S(1)} %pad_add_fusion.refs_0_.core_ref, s32[4,4]{1,0:T(4,128)S(1)} %broadcast_add_fusion.1.refs_1_, bf16[4,4,128,128]{3,2,1,0:T(8,128)(2,1)S(1)} %bitcast.18, f32[2,4,1,128]{3,2,1,0:T(1,128)S(1)} %bitcast.20, s32[4,1,128]{2,1,0:T(1,128)S(1)} %bitcast.21, ...), custom_call_target="tpu_custom_call" | custom-call | flops 1 | bytes 1 | tf_op jit(solution)/shard_map/teacher_prob/pallas_call | solution.py:494
  58.7 1.3 copy-done
  60.2 0.5 collective-permute-start.17
  60.7 0.4 collective-permute-start.13
  61.2 0.3 collective-permute-done.16.refs_12_
  61.5 0.1 collective-permute-start.15
  61.8 0.3 collective-permute-start.18
  62.1 2.8 %collective-permute-done.18.refs_14_ = bf16[64,1280]{1,0:T(8,128)(2,1)S(1)} collective-permute-done((bf16[64,1280]{1,0:T(8,128)(2,1)S(1)}, bf16[64,1280]{1,0:T(8,128)(2,1)S(1)}, u32[]{:S(2)}, u32[]{:S(2)}) %collective-permute-start.18) | collective-permute-done | bytes 163872 | tf_op jit(solution)/shard_map/ppermute | solution.py:133
  64.9 0.2 collective-permute-start.19
  65.1 1.2 collective-permute-done.19.refs_15_
  66.3 0.3 collective-permute-start.21
  66.6 10.6 %logits.1 = (f32[512,1024]{1,0:T(8,128)S(1)}, f32[32,8,128]{2,1,0:T(8,128)S(1)}) custom-call(bf16[64,3840]{1,0:T(8,128)(2,1)S(1)} %pad_maximum_fusion.refs_0_, bf16[64,3840]{1,0:T(8,128)(2,1)S(1)} %collective-permute-done.6.refs_1_, bf16[64,3840]{1,0:T(8,128)(2,1)S(1)} %collective-permute-done.7.refs_2_, ...), custom_call_target="tpu_custom_call" | custom-call | flops 1 | bytes 1 | tf_op jit(solution)/shard_map/logits/pallas_call | solution.py:524
  77.2 13.5 %all_to_all.10.refs_1_ = f32[32,8,128]{2,1,0:T(8,128)S(1)} all-to-all(f32[32,8,128]{2,1,0:T(8,128)S(1)} %get-tuple-element.103), channel_id=1, replica_groups=mesh['vocab'=32] {'vocab'}, dimensions={0} | all-to-all | bytes 262144 | tf_op jit(solution)/shard_map/all_to_all | solution.py:547
  90.8 1.3 grad_logits.1
  92.1 0.3 collective-permute-start.20
  92.3 2.4 %collective-permute-done.20.sib_ref = bf16[512,1024]{1,0:T(8,128)(2,1)S(1)} collective-permute-done((bf16[512,1024]{1,0:T(8,128)(2,1)S(1)}, bf16[512,1024]{1,0:T(8,128)(2,1)S(1)}, u32[]{:S(2)}, u32[]{:S(2)}) %collective-permute-start.20) | collective-permute-done | bytes 1048608 | tf_op jit(solution)/shard_map/ppermute | solution.py:133
  94.8 9.6 %grad_hidden_partial.1 = (f32[4,2,16,1536]{3,2,1,0:T(8,128)S(1)}, bf16[4,2,16,1536]{3,2,1,0:T(8,128)(2,1)S(1)}, bf16[4,2,16,1536]{3,2,1,0:T(8,128)(2,1)S(1)}, bf...) custom-call(s32[4]{0:T(128)S(1)} %pad_add_fusion.refs_0_.core_ref, ...), custom_call_target="tpu_custom_call" | custom-call | flops 1 | bytes 1 | tf_op jit(solution)/shard_map/grad_hidden_partial/pallas_call | solution.py:572
  104.4 0.7 collective-permute-start.25
  105.1 0.2 collective-permute-start.22
  105.3 1.3 collective-permute-start.23
  106.5 2.0 %collective-permute-start.24 = (bf16[4,2,16,1536]{3,2,1,0:T(8,128)(2,1)S(1)}, bf16[4,2,16,1536]{3,2,1,0:T(8,128)(2,1)S(1)}, u32[]{:S(2)}, u32[]{:S(2)}) collective-permute-start(bf16[4,2,16,1536]{3,2,1,0:T(8,128)(2,1)S(1)} %get-tuple-element.119), channel_id=1, source_target_pairs={{0,6},{1,7},{2,4},{3,5},{4,2},{5,3},{6,0},{7,1},{8,14},{9,15},{10,... | collective-permute-start | bytes 1179656 | tf_op jit(solution)/shard_map/ppermute | solution.py:133
  108.6 1.3 collective-permute-start.26
  109.8 5.0 %collective-permute-done.25.refs_5_ = bf16[4,2,16,1024]{3,2,1,0:T(8,128)(2,1)S(1)} collective-permute-done((bf16[4,2,16,1024]{3,2,1,0:T(8,128)(2,1)S(1)}, bf16[4,2,16,1024]{3,2,1,0:T(8,128)(2,1)S(1)}, u32[]{:S(2)}, u32[]{:S(2)}) %collective-permute-start.25) | collective-permute-done | bytes 262176 | tf_op jit(solution)/shard_map/ppermute | solution.py:133
  114.8 1.9 %collective-permute-start.27 = (bf16[4,2,16,1024]{3,2,1,0:T(8,128)(2,1)S(1)}, bf16[4,2,16,1024]{3,2,1,0:T(8,128)(2,1)S(1)}, u32[]{:S(2)}, u32[]{:S(2)}) collective-permute-start(bf16[4,2,16,1024]{3,2,1,0:T(8,128)(2,1)S(1)} %get-tuple-element.122), channel_id=1, source_target_pairs={{0,24},{1,25},{2,26},{3,27},{4,28},{5,29},{6,30},{7,31},{8,16},{9,... | collective-permute-start | bytes 786440 | tf_op jit(solution)/shard_map/ppermute | solution.py:133
  116.7 9.7 %grad_head.1 = bf16[5120,1024]{1,0:T(8,128)(2,1)} custom-call(bf16[64,3840]{1,0:T(8,128)(2,1)S(1)} %pad_maximum_fusion.refs_0_, bf16[64,3840]{1,0:T(8,128)(2,1)S(1)} %collective-permute-done.6.refs_1_, bf16[64,3840]{1,0:T(8,128)(2,1)S(1)} %collective-permute-done.7.refs_2_, bf16[64,3840]{1,0:T(8,128)(2,1)S(1)} %collective-permute-done.8.refs_3_, ...), custom_call_target="tpu_custom_call" | custom-call | flops 1 | bytes 1 | tf_op jit(solution)/shard_map/grad_head/pallas_call | solution.py:596
  126.4 3.1 %collective-permute-done.26.refs_6_ = bf16[4,2,16,1024]{3,2,1,0:T(8,128)(2,1)S(1)} collective-permute-done((bf16[4,2,16,1024]{3,2,1,0:T(8,128)(2,1)S(1)}, bf16[4,2,16,1024]{3,2,1,0:T(8,128)(2,1)S(1)}, u32[]{:S(2)}, u32[]{:S(2)}) %collective-permute-start.26) | collective-permute-done | bytes 262176 | tf_op jit(solution)/shard_map/ppermute | solution.py:133
  129.5 0.3 first_sum.1
  129.8 0.4 collective-permute-start.31
  130.2 4.7 %collective-permute-start.28 = (bf16[2,16,1536]{2,1,0:T(8,128)(2,1)S(1)}, bf16[2,16,1536]{2,1,0:T(8,128)(2,1)S(1)}, u32[]{:S(2)}, u32[]{:S(2)}) collective-permute-start(bf16[2,16,1536]{2,1,0:T(8,128)(2,1)S(1)} %get-tuple-element.134), channel_id=1, source_target_pairs={{0,8},{1,9},{2,10},{3,11},{4,12},{5,13},{6,14},{7,15},{8,0},{9,1},... | collective-permute-start | bytes 294920 | tf_op jit(solution)/shard_map/ppermute | solution.py:133
  135.0 2.3 %collective-permute-start.30 = (bf16[2,16,1536]{2,1,0:T(8,128)(2,1)S(1)}, bf16[2,16,1536]{2,1,0:T(8,128)(2,1)S(1)}, u32[]{:S(2)}, u32[]{:S(2)}) collective-permute-start(bf16[2,16,1536]{2,1,0:T(8,128)(2,1)S(1)} %get-tuple-element.136), channel_id=1, source_target_pairs={{0,24},{1,25},{2,26},{3,27},{4,28},{5,29},{6,30},{7,31},{8,16},{9,... | collective-permute-start | bytes 294920 | tf_op jit(solution)/shard_map/ppermute | solution.py:133
  137.3 1.0 collective-permute-start.32
  138.3 2.1 %collective-permute-start.33 = (bf16[2,16,1024]{2,1,0:T(8,128)(2,1)S(1)}, bf16[2,16,1024]{2,1,0:T(8,128)(2,1)S(1)}, u32[]{:S(2)}, u32[]{:S(2)}) collective-permute-start(bf16[2,16,1024]{2,1,0:T(8,128)(2,1)S(1)} %get-tuple-element.140), channel_id=1, source_target_pairs={{0,6},{1,7},{2,4},{3,5},{4,2},{5,3},{6,0},{7,1},{8,14},{9,15},{10,... | collective-permute-start | bytes 196616 | tf_op jit(solution)/shard_map/ppermute | solution.py:133
  140.4 1.2 collective-permute-done.32.refs_6_
  141.6 1.9 %collective-permute-done.33.refs_7_ = bf16[2,16,1024]{2,1,0:T(8,128)(2,1)S(1)} collective-permute-done((bf16[2,16,1024]{2,1,0:T(8,128)(2,1)S(1)}, bf16[2,16,1024]{2,1,0:T(8,128)(2,1)S(1)}, u32[]{:S(2)}, u32[]{:S(2)}) %collective-permute-start.33) | collective-permute-done | bytes 65568 | tf_op jit(solution)/shard_map/ppermute | solution.py:133
  143.5 0.2 collective-permute-done.29.refs_2_
  143.8 0.6 slice_reduce_fusion
  144.4 0.6 collective-permute-done.34
  145.1 0.7 pad_maximum_fusion.2
  (62 shorter events, 1.6 us)
Async XLA Ops:
  0.6 0.9 copy-start.4
  1.6 18.3 %collective-permute-start.2 = (bf16[16,1280]{1,0:T(8,128)(2,1)S(1)}, bf16[16,1280]{1,0:T(8,128)(2,1)S(1)}, u32[]{:S(2)}, u32[]{:S(2)}) collective-permute-start(bf16[16,1280]{1,0:T(8,128)(2,1)S(1)} %get-tuple-element.73), channel_id=1, source_target_pairs={{0,6},{1,7},{2,4},{3,5},{4,2},{5,3},{6,0},{7,1},{8,14},{9,15},{10,... | collective-permute-start | bytes 122888 | tf_op jit(solution)/shard_map/ppermute | solution.py:133
  5.5 16.2 %collective-permute-start.1 = (bf16[16,1280]{1,0:T(8,128)(2,1)S(1)}, bf16[16,1280]{1,0:T(8,128)(2,1)S(1)}, u32[]{:S(2)}, u32[]{:S(2)}) collective-permute-start(bf16[16,1280]{1,0:T(8,128)(2,1)S(1)} %get-tuple-element.73), channel_id=1, source_target_pairs={{0,4},{1,5},{2,6},{3,7},{4,0},{5,1},{6,2},{7,3},{8,12},{9,13},{10,... | collective-permute-start | bytes 122888 | tf_op jit(solution)/shard_map/ppermute | solution.py:133
  6.0 15.7 %collective-permute-start = (bf16[16,1280]{1,0:T(8,128)(2,1)S(1)}, bf16[16,1280]{1,0:T(8,128)(2,1)S(1)}, u32[]{:S(2)}, u32[]{:S(2)}) collective-permute-start(bf16[16,1280]{1,0:T(8,128)(2,1)S(1)} %get-tuple-element.73), channel_id=1, source_target_pairs={{0,2},{1,3},{2,0},{3,1},{4,6},{5,7},{6,4},{7,5},{8,10},{9,11},{10,... | collective-permute-start | bytes 122888 | tf_op jit(solution)/shard_map/ppermute | solution.py:133
  6.2 15.5 %collective-permute-start.5 = (bf16[16,3840]{1,0:T(8,128)(2,1)S(1)}, bf16[16,3840]{1,0:T(8,128)(2,1)S(1)}, u32[]{:S(2)}, u32[]{:S(2)}) collective-permute-start(bf16[16,3840]{1,0:T(8,128)(2,1)S(1)} %get-tuple-element.74), channel_id=1, source_target_pairs={{0,24},{1,25},{2,26},{3,27},{4,28},{5,29},{6,30},{7,31},{8,16},{9,... | collective-permute-start | bytes 368648 | tf_op jit(solution)/shard_map/ppermute | solution.py:133
  10.2 11.6 %collective-permute-start.4 = (bf16[16,3840]{1,0:T(8,128)(2,1)S(1)}, bf16[16,3840]{1,0:T(8,128)(2,1)S(1)}, u32[]{:S(2)}, u32[]{:S(2)}) collective-permute-start(bf16[16,3840]{1,0:T(8,128)(2,1)S(1)} %get-tuple-element.74), channel_id=1, source_target_pairs={{0,16},{1,17},{2,18},{3,19},{4,20},{5,21},{6,22},{7,23},{8,24},{9,... | collective-permute-start | bytes 368648 | tf_op jit(solution)/shard_map/ppermute | solution.py:133
  11.5 1.0 copy-start.3
  14.6 37.4 %all-to-all-start = ((bf16[32,67,128]{2,1,0:T(8,128)(2,1)}), bf16[32,67,128]{2,1,0:T(8,128)(2,1)S(1)}, u32[]{:S(2)}, u32[]{:S(2)}) async-start(bf16[32,67,128]{2,1,0:T(8,128)(2,1)} %slice.16), calls=%async_computation | async-start | bytes 1179648 | tf_op jit(solution)/shard_map/all_to_all | solution.py:485
  19.8 13.4 %collective-permute-start.3 = (bf16[16,3840]{1,0:T(8,128)(2,1)S(1)}, bf16[16,3840]{1,0:T(8,128)(2,1)S(1)}, u32[]{:S(2)}, u32[]{:S(2)}) collective-permute-start(bf16[16,3840]{1,0:T(8,128)(2,1)S(1)} %get-tuple-element.74), channel_id=1, source_target_pairs={{0,8},{1,9},{2,10},{3,11},{4,12},{5,13},{6,14},{7,15},{8,0},{9,1},... | collective-permute-start | bytes 368648 | tf_op jit(solution)/shard_map/ppermute | solution.py:133
  33.3 26.8 %collective-permute-start.8 = (bf16[64,3840]{1,0:T(8,128)(2,1)S(1)}, bf16[64,3840]{1,0:T(8,128)(2,1)S(1)}, u32[]{:S(2)}, u32[]{:S(2)}) collective-permute-start(bf16[64,3840]{1,0:T(8,128)(2,1)S(1)} %pad_maximum_fusion.refs_0_), channel_id=1, source_target_pairs={{0,6},{1,7},{2,4},{3,5},{4,2},{5,3},{6,0},{7,1},{8,14},{9,15},{10,... | collective-permute-start | bytes 1474568 | tf_op jit(solution)/shard_map/ppermute | solution.py:133
  35.9 24.2 %collective-permute-start.7 = (bf16[64,3840]{1,0:T(8,128)(2,1)S(1)}, bf16[64,3840]{1,0:T(8,128)(2,1)S(1)}, u32[]{:S(2)}, u32[]{:S(2)}) collective-permute-start(bf16[64,3840]{1,0:T(8,128)(2,1)S(1)} %pad_maximum_fusion.refs_0_), channel_id=1, source_target_pairs={{0,4},{1,5},{2,6},{3,7},{4,0},{5,1},{6,2},{7,3},{8,12},{9,13},{10,... | collective-permute-start | bytes 1474568 | tf_op jit(solution)/shard_map/ppermute | solution.py:133
  36.5 23.6 %collective-permute-start.6 = (bf16[64,3840]{1,0:T(8,128)(2,1)S(1)}, bf16[64,3840]{1,0:T(8,128)(2,1)S(1)}, u32[]{:S(2)}, u32[]{:S(2)}) collective-permute-start(bf16[64,3840]{1,0:T(8,128)(2,1)S(1)} %pad_maximum_fusion.refs_0_), channel_id=1, source_target_pairs={{0,2},{1,3},{2,0},{3,1},{4,6},{5,7},{6,4},{7,5},{8,10},{9,11},{10,... | collective-permute-start | bytes 1474568 | tf_op jit(solution)/shard_map/ppermute | solution.py:133
  37.1 8.4 %collective-permute-start.11 = (bf16[64,1280]{1,0:T(8,128)(2,1)S(1)}, bf16[64,1280]{1,0:T(8,128)(2,1)S(1)}, u32[]{:S(2)}, u32[]{:S(2)}) collective-permute-start(bf16[64,1280]{1,0:T(8,128)(2,1)S(1)} %pad_maximum_fusion.1.refs_8_), channel_id=1, source_target_pairs={{0,24},{1,25},{2,26},{3,27},{4,28},{5,29},{6,30},{7,31},{8,16},{9,... | collective-permute-start | bytes 491528 | tf_op jit(solution)/shard_map/ppermute | solution.py:133
  40.2 19.8 %collective-permute-start.10 = (bf16[64,1280]{1,0:T(8,128)(2,1)S(1)}, bf16[64,1280]{1,0:T(8,128)(2,1)S(1)}, u32[]{:S(2)}, u32[]{:S(2)}) collective-permute-start(bf16[64,1280]{1,0:T(8,128)(2,1)S(1)} %pad_maximum_fusion.1.refs_8_), channel_id=1, source_target_pairs={{0,16},{1,17},{2,18},{3,19},{4,20},{5,21},{6,22},{7,23},{8,24},{9,... | collective-permute-start | bytes 491528 | tf_op jit(solution)/shard_map/ppermute | solution.py:133
  45.5 14.6 %collective-permute-start.9 = (bf16[64,1280]{1,0:T(8,128)(2,1)S(1)}, bf16[64,1280]{1,0:T(8,128)(2,1)S(1)}, u32[]{:S(2)}, u32[]{:S(2)}) collective-permute-start(bf16[64,1280]{1,0:T(8,128)(2,1)S(1)} %pad_maximum_fusion.1.refs_8_), channel_id=1, source_target_pairs={{0,8},{1,9},{2,10},{3,11},{4,12},{5,13},{6,14},{7,15},{8,0},{9,1},... | collective-permute-start | bytes 491528 | tf_op jit(solution)/shard_map/ppermute | solution.py:133
  52.0 38.8 %copy-start.7 = (f32[512]{0:T(512)S(1)}, f32[512]{0:T(512)}, u32[]{:S(2)}) copy-start(f32[512]{0:T(512)} %param.13) | copy-start | bytes 6148
  52.0 0.8 copy-start.8
  54.3 0.7 copy-start.5
  55.0 0.7 copy-start.6
  58.7 1.3 copy-start
  60.0 30.7 %copy-start.1 = (f32[512,1024]{1,0:T(8,128)S(1)}, f32[512,1024]{1,0:T(8,128)}, u32[]{:S(2)}) copy-start(f32[512,1024]{1,0:T(8,128)} %copy-done) | copy-start | bytes 6291460
  60.1 1.5 %collective-permute-start.16 = (bf16[64,1280]{1,0:T(8,128)(2,1)S(1)}, bf16[64,1280]{1,0:T(8,128)(2,1)S(1)}, u32[]{:S(2)}, u32[]{:S(2)}) collective-permute-start(bf16[64,1280]{1,0:T(8,128)(2,1)S(1)} %pad_maximum_fusion.1.refs_8_), channel_id=1, source_target_pairs={{0,1},{1,0},{2,3},{3,2},{4,5},{5,4},{6,7},{7,6},{8,9},{9,8},{10,11... | collective-permute-start | bytes 491528 | tf_op jit(solution)/shard_map/ppermute | solution.py:133
  60.2 1.6 %collective-permute-start.17 = (bf16[64,1280]{1,0:T(8,128)(2,1)S(1)}, bf16[64,1280]{1,0:T(8,128)(2,1)S(1)}, u32[]{:S(2)}, u32[]{:S(2)}) collective-permute-start(bf16[64,1280]{1,0:T(8,128)(2,1)S(1)} %collective-permute-done.9.refs_9_), channel_id=1, source_target_pairs={{0,1},{1,0},{2,3},{3,2},{4,5},{5,4},{6,7},{7,6},{8,9},{9,8},{10,11... | collective-permute-start | bytes 491528 | tf_op jit(solution)/shard_map/ppermute | solution.py:133
  60.7 5.6 %collective-permute-start.12 = (bf16[64,3840]{1,0:T(8,128)(2,1)S(1)}, bf16[64,3840]{1,0:T(8,128)(2,1)S(1)}, u32[]{:S(2)}, u32[]{:S(2)}) collective-permute-start(bf16[64,3840]{1,0:T(8,128)(2,1)S(1)} %pad_maximum_fusion.refs_0_), channel_id=1, source_target_pairs={{0,1},{1,0},{2,3},{3,2},{4,5},{5,4},{6,7},{7,6},{8,9},{9,8},{10,11... | collective-permute-start | bytes 1474568 | tf_op jit(solution)/shard_map/ppermute | solution.py:133
  60.7 5.5 %collective-permute-start.13 = (bf16[64,3840]{1,0:T(8,128)(2,1)S(1)}, bf16[64,3840]{1,0:T(8,128)(2,1)S(1)}, u32[]{:S(2)}, u32[]{:S(2)}) collective-permute-start(bf16[64,3840]{1,0:T(8,128)(2,1)S(1)} %collective-permute-done.6.refs_1_), channel_id=1, source_target_pairs={{0,1},{1,0},{2,3},{3,2},{4,5},{5,4},{6,7},{7,6},{8,9},{9,8},{10,11... | collective-permute-start | bytes 1474568 | tf_op jit(solution)/shard_map/ppermute | solution.py:133
  61.2 5.1 %collective-permute-start.14 = (bf16[64,3840]{1,0:T(8,128)(2,1)S(1)}, bf16[64,3840]{1,0:T(8,128)(2,1)S(1)}, u32[]{:S(2)}, u32[]{:S(2)}) collective-permute-start(bf16[64,3840]{1,0:T(8,128)(2,1)S(1)} %collective-permute-done.7.refs_2_), channel_id=1, source_target_pairs={{0,1},{1,0},{2,3},{3,2},{4,5},{5,4},{6,7},{7,6},{8,9},{9,8},{10,11... | collective-permute-start | bytes 1474568 | tf_op jit(solution)/shard_map/ppermute | solution.py:133
  61.5 4.7 %collective-permute-start.15 = (bf16[64,3840]{1,0:T(8,128)(2,1)S(1)}, bf16[64,3840]{1,0:T(8,128)(2,1)S(1)}, u32[]{:S(2)}, u32[]{:S(2)}) collective-permute-start(bf16[64,3840]{1,0:T(8,128)(2,1)S(1)} %collective-permute-done.8.refs_3_), channel_id=1, source_target_pairs={{0,1},{1,0},{2,3},{3,2},{4,5},{5,4},{6,7},{7,6},{8,9},{9,8},{10,11... | collective-permute-start | bytes 1474568 | tf_op jit(solution)/shard_map/ppermute | solution.py:133
  61.8 3.1 %collective-permute-start.18 = (bf16[64,1280]{1,0:T(8,128)(2,1)S(1)}, bf16[64,1280]{1,0:T(8,128)(2,1)S(1)}, u32[]{:S(2)}, u32[]{:S(2)}) collective-permute-start(bf16[64,1280]{1,0:T(8,128)(2,1)S(1)} %collective-permute-done.10.refs_10_), channel_id=1, source_target_pairs={{0,1},{1,0},{2,3},{3,2},{4,5},{5,4},{6,7},{7,6},{8,9},{9,8},{10,11... | collective-permute-start | bytes 491528 | tf_op jit(solution)/shard_map/ppermute | solution.py:133
  64.9 1.4 collective-permute-start.19
  66.3 28.5 %collective-permute-start.21 = (bf16[5120,1024]{1,0:T(8,128)(2,1)}, bf16[5120,1024]{1,0:T(8,128)(2,1)}, u32[]{:S(2)}, u32[]{:S(2)}) collective-permute-start(bf16[5120,1024]{1,0:T(8,128)(2,1)} %w_ref.1), channel_id=1, source_target_pairs={{0,1},{1,0},{2,3},{3,2},{4,5},{5,4},{6,7},{7,6},{8,9},{9,8},{10,11... | collective-permute-start | bytes 31457288 | tf_op jit(solution)/shard_map/ppermute | solution.py:133
  92.0 12.3 %copy-start.2 = (bf16[512,1024]{1,0:T(8,128)(2,1)}, bf16[512,1024]{1,0:T(8,128)(2,1)S(1)}, u32[]{:S(2)}) copy-start(bf16[512,1024]{1,0:T(8,128)(2,1)S(1)} %get-tuple-element.123.grad_ref.refs_16_) | copy-start | bytes 3145732
  92.1 2.7 %collective-permute-start.20 = (bf16[512,1024]{1,0:T(8,128)(2,1)S(1)}, bf16[512,1024]{1,0:T(8,128)(2,1)S(1)}, u32[]{:S(2)}, u32[]{:S(2)}) collective-permute-start(bf16[512,1024]{1,0:T(8,128)(2,1)S(1)} %get-tuple-element.123.grad_ref.refs_16_), channel_id=1, source_target_pairs={{0,1},{1,0},{2,3},{3,2},{4,5},{5,4},{6,7},{7,6},{8,9},{9,8},{10,11... | collective-permute-start | bytes 3145736 | tf_op jit(solution)/shard_map/ppermute | solution.py:133
  104.4 10.5 %collective-permute-start.25 = (bf16[4,2,16,1024]{3,2,1,0:T(8,128)(2,1)S(1)}, bf16[4,2,16,1024]{3,2,1,0:T(8,128)(2,1)S(1)}, u32[]{:S(2)}, u32[]{:S(2)}) collective-permute-start(bf16[4,2,16,1024]{3,2,1,0:T(8,128)(2,1)S(1)} %get-tuple-element.120), channel_id=1, source_target_pairs={{0,8},{1,9},{2,10},{3,11},{4,12},{5,13},{6,14},{7,15},{8,0},{9,1},... | collective-permute-start | bytes 786440 | tf_op jit(solution)/shard_map/ppermute | solution.py:133
  105.1 24.5 %collective-permute-start.22 = (bf16[4,2,16,1536]{3,2,1,0:T(8,128)(2,1)S(1)}, bf16[4,2,16,1536]{3,2,1,0:T(8,128)(2,1)S(1)}, u32[]{:S(2)}, u32[]{:S(2)}) collective-permute-start(bf16[4,2,16,1536]{3,2,1,0:T(8,128)(2,1)S(1)} %get-tuple-element.117), channel_id=1, source_target_pairs={{0,2},{1,3},{2,0},{3,1},{4,6},{5,7},{6,4},{7,5},{8,10},{9,11},{10,... | collective-permute-start | bytes 1179656 | tf_op jit(solution)/shard_map/ppermute | solution.py:133
  105.3 24.3 %collective-permute-start.23 = (bf16[4,2,16,1536]{3,2,1,0:T(8,128)(2,1)S(1)}, bf16[4,2,16,1536]{3,2,1,0:T(8,128)(2,1)S(1)}, u32[]{:S(2)}, u32[]{:S(2)}) collective-permute-start(bf16[4,2,16,1536]{3,2,1,0:T(8,128)(2,1)S(1)} %get-tuple-element.118), channel_id=1, source_target_pairs={{0,4},{1,5},{2,6},{3,7},{4,0},{5,1},{6,2},{7,3},{8,12},{9,13},{10,... | collective-permute-start | bytes 1179656 | tf_op jit(solution)/shard_map/ppermute | solution.py:133
  106.5 23.0 %collective-permute-start.24 = (bf16[4,2,16,1536]{3,2,1,0:T(8,128)(2,1)S(1)}, bf16[4,2,16,1536]{3,2,1,0:T(8,128)(2,1)S(1)}, u32[]{:S(2)}, u32[]{:S(2)}) collective-permute-start(bf16[4,2,16,1536]{3,2,1,0:T(8,128)(2,1)S(1)} %get-tuple-element.119), channel_id=1, source_target_pairs={{0,6},{1,7},{2,4},{3,5},{4,2},{5,3},{6,0},{7,1},{8,14},{9,15},{10,... | collective-permute-start | bytes 1179656 | tf_op jit(solution)/shard_map/ppermute | solution.py:133
  108.6 21.0 %collective-permute-start.26 = (bf16[4,2,16,1024]{3,2,1,0:T(8,128)(2,1)S(1)}, bf16[4,2,16,1024]{3,2,1,0:T(8,128)(2,1)S(1)}, u32[]{:S(2)}, u32[]{:S(2)}) collective-permute-start(bf16[4,2,16,1024]{3,2,1,0:T(8,128)(2,1)S(1)} %get-tuple-element.121), channel_id=1, source_target_pairs={{0,16},{1,17},{2,18},{3,19},{4,20},{5,21},{6,22},{7,23},{8,24},{9,... | collective-permute-start | bytes 786440 | tf_op jit(solution)/shard_map/ppermute | solution.py:133
  114.8 14.7 %collective-permute-start.27 = (bf16[4,2,16,1024]{3,2,1,0:T(8,128)(2,1)S(1)}, bf16[4,2,16,1024]{3,2,1,0:T(8,128)(2,1)S(1)}, u32[]{:S(2)}, u32[]{:S(2)}) collective-permute-start(bf16[4,2,16,1024]{3,2,1,0:T(8,128)(2,1)S(1)} %get-tuple-element.122), channel_id=1, source_target_pairs={{0,24},{1,25},{2,26},{3,27},{4,28},{5,29},{6,30},{7,31},{8,16},{9,... | collective-permute-start | bytes 786440 | tf_op jit(solution)/shard_map/ppermute | solution.py:133
  129.8 8.5 %collective-permute-start.31 = (bf16[2,16,1024]{2,1,0:T(8,128)(2,1)S(1)}, bf16[2,16,1024]{2,1,0:T(8,128)(2,1)S(1)}, u32[]{:S(2)}, u32[]{:S(2)}) collective-permute-start(bf16[2,16,1024]{2,1,0:T(8,128)(2,1)S(1)} %get-tuple-element.138), channel_id=1, source_target_pairs={{0,2},{1,3},{2,0},{3,1},{4,6},{5,7},{6,4},{7,5},{8,10},{9,11},{10,... | collective-permute-start | bytes 196616 | tf_op jit(solution)/shard_map/ppermute | solution.py:133
  130.2 13.2 %collective-permute-start.28 = (bf16[2,16,1536]{2,1,0:T(8,128)(2,1)S(1)}, bf16[2,16,1536]{2,1,0:T(8,128)(2,1)S(1)}, u32[]{:S(2)}, u32[]{:S(2)}) collective-permute-start(bf16[2,16,1536]{2,1,0:T(8,128)(2,1)S(1)} %get-tuple-element.134), channel_id=1, source_target_pairs={{0,8},{1,9},{2,10},{3,11},{4,12},{5,13},{6,14},{7,15},{8,0},{9,1},... | collective-permute-start | bytes 294920 | tf_op jit(solution)/shard_map/ppermute | solution.py:133
  134.9 8.7 %collective-permute-start.29 = (bf16[2,16,1536]{2,1,0:T(8,128)(2,1)S(1)}, bf16[2,16,1536]{2,1,0:T(8,128)(2,1)S(1)}, u32[]{:S(2)}, u32[]{:S(2)}) collective-permute-start(bf16[2,16,1536]{2,1,0:T(8,128)(2,1)S(1)} %get-tuple-element.135), channel_id=1, source_target_pairs={{0,16},{1,17},{2,18},{3,19},{4,20},{5,21},{6,22},{7,23},{8,24},{9,... | collective-permute-start | bytes 294920 | tf_op jit(solution)/shard_map/ppermute | solution.py:133
  135.0 8.6 %collective-permute-start.30 = (bf16[2,16,1536]{2,1,0:T(8,128)(2,1)S(1)}, bf16[2,16,1536]{2,1,0:T(8,128)(2,1)S(1)}, u32[]{:S(2)}, u32[]{:S(2)}) collective-permute-start(bf16[2,16,1536]{2,1,0:T(8,128)(2,1)S(1)} %get-tuple-element.136), channel_id=1, source_target_pairs={{0,24},{1,25},{2,26},{3,27},{4,28},{5,29},{6,30},{7,31},{8,16},{9,... | collective-permute-start | bytes 294920 | tf_op jit(solution)/shard_map/ppermute | solution.py:133
  137.3 4.3 %collective-permute-start.32 = (bf16[2,16,1024]{2,1,0:T(8,128)(2,1)S(1)}, bf16[2,16,1024]{2,1,0:T(8,128)(2,1)S(1)}, u32[]{:S(2)}, u32[]{:S(2)}) collective-permute-start(bf16[2,16,1024]{2,1,0:T(8,128)(2,1)S(1)} %get-tuple-element.139), channel_id=1, source_target_pairs={{0,4},{1,5},{2,6},{3,7},{4,0},{5,1},{6,2},{7,3},{8,12},{9,13},{10,... | collective-permute-start | bytes 196616 | tf_op jit(solution)/shard_map/ppermute | solution.py:133
  138.3 5.2 %collective-permute-start.33 = (bf16[2,16,1024]{2,1,0:T(8,128)(2,1)S(1)}, bf16[2,16,1024]{2,1,0:T(8,128)(2,1)S(1)}, u32[]{:S(2)}, u32[]{:S(2)}) collective-permute-start(bf16[2,16,1024]{2,1,0:T(8,128)(2,1)S(1)} %get-tuple-element.140), channel_id=1, source_target_pairs={{0,6},{1,7},{2,4},{3,5},{4,2},{5,3},{6,0},{7,1},{8,14},{9,15},{10,... | collective-permute-start | bytes 196616 | tf_op jit(solution)/shard_map/ppermute | solution.py:133
  143.7 1.3 collective-permute-start.34

commit v12 on v10

--- a/solution.py
+++ b/solution.py
@@ -177,37 +177,29 @@
             entropy_ref[...] = jnp.broadcast_to(entropy[:rows], entropy_ref.shape)
 
 
-def assemble(pieces, by_layer, rows, out_ref, columns=slice(None)):
-    count = len(pieces) // CORES
-    groups = pieces[0].shape[0] // rows
-    for p, piece in enumerate(pieces):
-        core, i = p // count, p % count
-        for g in range(groups):
-            layer, chip = (i, g) if by_layer else (g, i)
-            block = layer * GROUP + core * CHIPS + chip
-            out_ref[pl.ds(block * rows, rows), columns] = piece[pl.ds(g * rows, rows), :]
-
-
-def logits_kernel(rows, wide_count, *refs):
-    pieces, refs = refs[:-8], refs[-8:]
+def assemble(pieces, rows, out_ref):
+    layers = pieces[0].shape[0] // rows
+    for k in range(layers):
+        for p, piece in enumerate(pieces):
+            out_ref[pl.ds((k * GROUP + p) * rows, rows), :] = piece[pl.ds(k * rows, rows), :]
+
+
+def logits_kernel(rows, *refs):
+    pieces, refs = refs[:GROUP], refs[GROUP:]
     w_ref, prob_ref, logits_ref, stat_ref, hidden, weight, sems, cross_ref = refs
-    wide_pieces, narrow_pieces = pieces[:wide_count], pieces[wide_count:]
-    depth = w_ref.shape[0]
-    wide, width = wide_pieces[0].shape[1], prob_ref.shape[1]
+    half, width = w_ref.shape[0] // 2, prob_ref.shape[1]
     tiles = w_ref.shape[1] // width
     step = pl.program_id(0)
-    parts = [slice(wide, depth), slice(0, wide)]
 
     def copy(i):
-        span = pl.ds(parts[i].start, parts[i].stop - parts[i].start)
+        span = pl.ds(i * half, half)
         return pltpu.make_async_copy(w_ref.at[span, :], weight.at[span, :], sems.at[i])
 
     @pl.when(step == 0)
     def _():
         copy(0).start()
         copy(1).start()
-        assemble(narrow_pieces, True, rows, hidden, parts[0])
-        assemble(wide_pieces, False, rows, hidden, parts[1])
+        assemble(pieces, rows, hidden)
         copy(0).wait()
 
     @pl.when(step == tiles)
@@ -218,14 +210,14 @@
     def _():
         span = pl.ds(pl.multiple_of(step * width, width), width)
         logits_ref[:, span] = jnp.dot(
-            hidden[:, parts[0]], weight[parts[0], span], preferred_element_type=jnp.float32
+            hidden[:, :half], weight[:half, span], preferred_element_type=jnp.float32
         )
 
     @pl.when(step >= tiles)
     def _():
         span = pl.ds(pl.multiple_of((step - tiles) * width, width), width)
         total = logits_ref[:, span] + jnp.dot(
-            hidden[:, parts[1]], weight[parts[1], span], preferred_element_type=jnp.float32
+            hidden[:, half:], weight[half:, span], preferred_element_type=jnp.float32
         )
         logits_ref[:, span] = total
         product = total * prob_ref[...]
@@ -322,18 +314,9 @@
             narrow_outs[k][j, core] = part.astype(narrow_outs[k].dtype)
 
 
-def head_kernel(rows, wide_count, wide_steps, *refs):
+def head_kernel(rows, *refs):
     pieces, (grad_ref, out_ref, hidden) = refs[:-3], refs[-3:]
-    step = pl.program_id(0)
-
-    @pl.when(step < wide_steps)
-    def _():
-        assemble(pieces[:wide_count], False, rows, hidden)
-
-    @pl.when(step >= wide_steps)
-    def _():
-        assemble(pieces[wide_count:], True, rows, hidden)
-
+    assemble(pieces, rows, hidden)
     out_ref[...] = lax.dot_general(
         hidden[...], grad_ref[...], (((0,), (0,)), ((), ())), preferred_element_type=jnp.float32
     ).astype(out_ref.dtype)
@@ -462,19 +445,13 @@
     pos = jnp.stack([core, chip, layer, rank]).astype(jnp.int32)
     unlisted = float(n * slab - side * listed_count)
 
-    narrow = depth * 3 // 10 // 512 * 512
-    wide = depth - narrow
-    column = [hidden_states[:, :wide]]
-    column += [shift(column[0], k * GROUP) for k in range(1, layers)]
-    plane = [hidden_states[:, wide:]]
-    plane += [shift(plane[0], j * CORES) for j in range(1, CHIPS)]
+    column = [hidden_states] + [shift(hidden_states, k * GROUP) for k in range(1, layers)]
+    column = jnp.concatenate(column, axis=0)
+    plane = [column] + [shift(column, j * CORES) for j in range(1, CHIPS)]
     payload, place = pack_teacher(teacher_logits, block_lists, slab // side)
-    column, plane = jnp.concatenate(column, axis=0), jnp.concatenate(plane, axis=0)
-    column, plane, payload = lax.optimization_barrier((column, plane, payload[:, : 3 - STAT_ROWS]))
-    wide_pieces = [column] + [shift(column, j * CORES) for j in range(1, CHIPS)]
-    narrow_pieces = [plane] + [shift(plane, k * GROUP) for k in range(1, layers)]
-    narrow_pieces[1], payload = lax.optimization_barrier((narrow_pieces[1], payload))
-    arrived = lax.all_to_all(payload, "vocab", split_axis=0, concat_axis=0, tiled=True)
+    arrived = lax.all_to_all(
+        payload[:, : 3 - STAT_ROWS], "vocab", split_axis=0, concat_axis=0, tiled=True
+    )
     arrived_blocks, arrived_stat = unpack_teacher(arrived, blocks, stored)
 
     prob, entropy = pl.pallas_call(
@@ -497,18 +474,16 @@
         tail_mass.reshape(blocks, 1, side),
     )
 
-    wide_pieces, narrow_pieces, prob = lax.optimization_barrier((wide_pieces, narrow_pieces, prob))
-    wide_pieces = list(wide_pieces) + [shift(piece, 1) for piece in wide_pieces]
-    narrow_pieces = list(narrow_pieces) + [shift(piece, 1) for piece in narrow_pieces]
-    wide_pieces, narrow_pieces, late_weight = lax.optimization_barrier((wide_pieces, narrow_pieces, head_weight))
+    plane[-1], prob = lax.optimization_barrier((plane[-1], prob))
+    pieces = plane + [shift(piece, 1) for piece in plane]
+    pieces, late_weight = lax.optimization_barrier((pieces, head_weight))
     sib_w = shift(late_weight, 1)
-    pieces = wide_pieces + narrow_pieces
 
     width = 256 if slab % 256 == 0 else 128
     tiles = slab // width
     whole = lambda t: (0, 0)
     logits, stat = pl.pallas_call(
-        functools.partial(logits_kernel, rows, len(wide_pieces)),
+        functools.partial(logits_kernel, rows),
         grid=(2 * tiles,),
         out_shape=[
             jax.ShapeDtypeStruct((tokens, slab), f32),
@@ -577,19 +552,11 @@
     wide_sums = [shift(partial[j], j * CORES) for j in range(1, CHIPS)]
     narrow_sums = [shift(partial[CHIPS + k], k * GROUP) for k in range(1, layers)]
 
-    head_tile = 512
-    head_steps = wide // head_tile
+    head_tile = half // 2
     grad_head = pl.pallas_call(
-        functools.partial(head_kernel, rows, len(wide_pieces), head_steps),
-        grid=(depth // head_tile,),
-        in_specs=[
-            pl.BlockSpec((piece.shape[0], head_tile), lambda t: (0, jnp.minimum(t, head_steps - 1)))
-            for piece in wide_pieces
-        ]
-        + [
-            pl.BlockSpec((piece.shape[0], head_tile), lambda t: (0, jnp.maximum(t - head_steps, 0)))
-            for piece in narrow_pieces
-        ]
+        functools.partial(head_kernel, rows),
+        grid=(4,),
+        in_specs=[pl.BlockSpec((layers * rows, head_tile), lambda t: (0, t)) for _ in pieces]
         + [pl.BlockSpec((tokens, slab), whole)],
         out_specs=pl.BlockSpec((head_tile, slab), lambda t: (t, 0)),
         out_shape=jax.ShapeDtypeStruct((depth, slab), bf16),

time: 149 us -> 139 us (0.933)
  starting transfers between devices: 40.9 us -> 33.9 us
  waiting for transfers between devices: 46.3 us -> 39.7 us
  blocking collectives: 11.6 us -> 13.8 us
    all_to_all x1, waiting for transfers between devices: 17.7 us -> 0.01 us  [levels_plan(): lax.all_to_all(payload[:, :3 - STAT_ROWS], 'vocab', split_axis=0, concat_...]
    ppermute x35 -> x25, waiting for transfers between devices: 28.6 us -> 39.7 us  [shift(): return lax.ppermute(x, 'vocab', [(i, i ^ distance) for i in range(n)])]
    ppermute x35 -> x25, starting transfers between devices: 36.8 us -> 27.7 us  [shift(): return lax.ppermute(x, 'vocab', [(i, i ^ distance) for i in range(n)])]
    all_to_all x1, blocking collectives: 11.6 us -> 13.8 us  [levels_plan(): lax.all_to_all(stat, 'vocab', split_axis=0, concat_axis=0, tiled=True)]
    all_to_all x1, starting transfers between devices: 4.14 us -> 6.18 us  [levels_plan(): lax.all_to_all(payload[:, :3 - STAT_ROWS], 'vocab', split_axis=0, concat_...]
    slice x2 -> x0, local copies, waits for them, and re-layouts: 1.71 us -> none  [the longest x1 0.91 us: levels_plan(): column = [hidden_states[:, :wide]]]
    unnamed x16 -> x19, local copies, waits for them, and re-layouts: 4.38 us -> 5.63 us
  transfers between devices with their start and end apart: 36 -> 26, of which waited for: 15 -> 11; matrix products, arithmetic and copies ran while one was open for 4% -> 5% of each run, Pallas kernels for 19% -> 20%
where the time goes in v12:
time: 139 us; the launch traced here: 138 us
  waiting for transfers between devices  39.7 us (29%)
  Pallas kernels  37 us (27%)
  starting transfers between devices  33.9 us (24%)
  blocking collectives  13.8 us (10%)
  local copies, waits for them, and re-layouts  9.91 us (7%)
  other arithmetic  2.89 us (2%)
    ppermute x25, waiting for transfers between devices, shift(): return lax.ppermute(x, 'vocab', [(i, i ^ distance) for i in range(n)])  39.7 us
    ppermute x25, starting transfers between devices, shift(): return lax.ppermute(x, 'vocab', [(i, i ^ distance) for i in range(n)])  27.7 us
    all_to_all x1, blocking collectives, levels_plan(): lax.all_to_all(stat, 'vocab', split_axis=0, concat_axis=0, tiled=True)  13.8 us
    pallas_call x1, Pallas kernels, levels_plan(): pl.pallas_call(functools.partial(logits_kernel, rows), grid=(2 * tiles,),...  12 us
    pallas_call x1, Pallas kernels, levels_plan(): pl.pallas_call(functools.partial(partial_kernel, rows, wide_steps), grid_...  9.56 us
    pallas_call x1, Pallas kernels, levels_plan(): pl.pallas_call(functools.partial(head_kernel, rows), grid=(4,), in_specs=...  9.45 us
    all_to_all x1, starting transfers between devices, levels_plan(): lax.all_to_all(payload[:, :3 - STAT_ROWS], 'vocab', split_axis=0, concat_...  6.18 us
    unnamed x19, local copies, waits for them, and re-layouts  5.63 us
  transfers between devices with their start and end apart: 26, of which 11 were waited for; matrix products, arithmetic and copies ran while one was open for 5% of the time, Pallas kernels for 20%

profile of v12, /device:TPU:0, one launch (start us, length us, event | category | flops | bytes accessed | tf_op | source)
XLA Modules:
  0.0 138.1 jit_solution(9816537110648920476)
XLA Ops:
  0.6 4.1 %collective-permute-start.1 = (bf16[16,5120]{1,0:T(8,128)(2,1)}, bf16[16,5120]{1,0:T(8,128)(2,1)S(1)}, u32[]{:S(2)}, u32[]{:S(2)}) collective-permute-start(bf16[16,5120]{1,0:T(8,128)(2,1)} %param.7), channel_id=1, source_target_pairs={{0,16},{1,17},{2,18},{3,19},{4,20},{5,21},{6,22},{7,23},{8,24},{9,... | collective-permute-start | bytes 491528 | tf_op jit(solution)/shard_map/ppermute | solution.py:133
  4.7 1.6 %collective-permute-start = (bf16[16,5120]{1,0:T(8,128)(2,1)}, bf16[16,5120]{1,0:T(8,128)(2,1)S(1)}, u32[]{:S(2)}, u32[]{:S(2)}) collective-permute-start(bf16[16,5120]{1,0:T(8,128)(2,1)} %param.7), channel_id=1, source_target_pairs={{0,8},{1,9},{2,10},{3,11},{4,12},{5,13},{6,14},{7,15},{8,0},{9,1},... | collective-permute-start | bytes 491528 | tf_op jit(solution)/shard_map/ppermute | solution.py:133
  6.3 0.7 add_select_fusion.1
  7.0 0.1 iota_compare_fusion
  7.1 0.2 convert_reduce_fusion
  7.3 0.1 add.82
  7.4 0.1 add.79
  7.5 0.1 add.85
  7.7 0.9 copy-done.4
  8.6 1.3 pack_teacher.1
  9.9 0.9 slice.16
  10.8 6.2 %all-to-all-start = ((bf16[32,67,128]{2,1,0:T(8,128)(2,1)}), bf16[32,67,128]{2,1,0:T(8,128)(2,1)}, u32[]{:S(2)}, u32[]{:S(2)}) async-start(bf16[32,67,128]{2,1,0:T(8,128)(2,1)} %slice.16), calls=%async_computation | async-start | bytes 1179648 | tf_op jit(solution)/shard_map/all_to_all | solution.py:452
  17.0 0.9 constant_dynamic-update-slice_fusion.3
  18.0 1.8 %collective-permute-start.4 = (bf16[64,5120]{1,0:T(8,128)(2,1)S(1)}, bf16[64,5120]{1,0:T(8,128)(2,1)S(1)}, u32[]{:S(2)}, u32[]{:S(2)}) collective-permute-start(bf16[64,5120]{1,0:T(8,128)(2,1)S(1)} %constant_dynamic-update-slice_fusion.refs_0_), channel_id=1, source_target_pairs={{0,4},{1,5},{2,6},{3,7},{4,0},{5,1},{6,2},{7,3},{8,12},{9,13},{10,... | collective-permute-start | bytes 1966088 | tf_op jit(solution)/shard_map/ppermute | solution.py:133
  19.8 1.5 %collective-permute-start.3 = (bf16[64,5120]{1,0:T(8,128)(2,1)S(1)}, bf16[64,5120]{1,0:T(8,128)(2,1)S(1)}, u32[]{:S(2)}, u32[]{:S(2)}) collective-permute-start(bf16[64,5120]{1,0:T(8,128)(2,1)S(1)} %constant_dynamic-update-slice_fusion.refs_0_), channel_id=1, source_target_pairs={{0,2},{1,3},{2,0},{3,1},{4,6},{5,7},{6,4},{7,5},{8,10},{9,11},{10,... | collective-permute-start | bytes 1966088 | tf_op jit(solution)/shard_map/ppermute | solution.py:133
  21.2 0.3 collective-permute-start.5
  21.6 0.1 pad_add_fusion.refs_0_.core_ref
  21.6 0.2 select_reduce_fusion
  21.9 18.4 %collective-permute-done.4.refs_2_ = bf16[64,5120]{1,0:T(8,128)(2,1)S(1)} collective-permute-done((bf16[64,5120]{1,0:T(8,128)(2,1)S(1)}, bf16[64,5120]{1,0:T(8,128)(2,1)S(1)}, u32[]{:S(2)}, u32[]{:S(2)}) %collective-permute-start.4) | collective-permute-done | bytes 655392 | tf_op jit(solution)/shard_map/ppermute | solution.py:133
  40.4 0.6 collective-permute-done.3.refs_1_
  41.0 1.1 slice.17
  42.1 1.0 copy.27
  43.1 0.9 convert_reduce_fusion.1
  44.0 0.1 copy.28
  44.1 0.1 copy.29
  44.2 0.1 reshape.93
  44.4 1.0 copy-done.3
  45.4 0.7 copy-done.5
  46.1 0.7 copy-done.6
  46.8 3.1 %teacher_prob.1 = (f32[512,1024]{1,0:T(8,128)S(1)}, f32[16,128]{1,0:T(8,128)S(1)}) custom-call(s32[4]{0:T(128)S(1)} %pad_add_fusion.refs_0_.core_ref, s32[4,4]{1,0:T(4,128)S(1)} %broadcast_add_fusion.1.refs_1_, bf16[4,4,128,128]{3,2,1,0:T(8,128)(2,1)S(1)} %bitcast.18, f32[2,4,1,128]{3,2,1,0:T(1,128)S(1)} %bitcast.20, s32[4,1,128]{2,1,0:T(1,128)S(1)} %bitcast.21, ...), custom_call_target="tpu_custom_call" | custom-call | flops 1 | bytes 1 | tf_op jit(solution)/shard_map/teacher_prob/pallas_call | solution.py:457
  49.8 1.3 copy-done
  51.1 3.9 %collective-permute-done.5.refs_3_ = bf16[64,5120]{1,0:T(8,128)(2,1)S(1)} collective-permute-done((bf16[64,5120]{1,0:T(8,128)(2,1)S(1)}, bf16[64,5120]{1,0:T(8,128)(2,1)S(1)}, u32[]{:S(2)}, u32[]{:S(2)}) %collective-permute-start.5) | collective-permute-done | bytes 655392 | tf_op jit(solution)/shard_map/ppermute | solution.py:133
  55.1 2.1 %collective-permute-done.9.refs_7_ = bf16[64,5120]{1,0:T(8,128)(2,1)S(1)} collective-permute-done((bf16[64,5120]{1,0:T(8,128)(2,1)S(1)}, bf16[64,5120]{1,0:T(8,128)(2,1)S(1)}, u32[]{:S(2)}, u32[]{:S(2)}) %collective-permute-start.9) | collective-permute-done | bytes 655392 | tf_op jit(solution)/shard_map/ppermute | solution.py:133
  57.1 0.1 collective-permute-start.11
  57.3 12.0 %logits.1 = (f32[512,1024]{1,0:T(8,128)S(1)}, f32[32,8,128]{2,1,0:T(8,128)S(1)}) custom-call(bf16[64,5120]{1,0:T(8,128)(2,1)S(1)} %constant_dynamic-update-slice_fusion.refs_0_, bf16[64,5120]{1,0:T(8,128)(2,1)S(1)} %collective-permute-done.3.refs_1_, bf16[64,5120]{1,0:T(8,128)(2,1)S(1)} %collective-permute-done.4.refs_2_, ...), custom_call_target="tpu_custom_call" | custom-call | flops 1 | bytes 1 | tf_op jit(solution)/shard_map/logits/pallas_call | solution.py:485
  69.3 13.8 %all_to_all.10.refs_1_ = f32[32,8,128]{2,1,0:T(8,128)S(1)} all-to-all(f32[32,8,128]{2,1,0:T(8,128)S(1)} %get-tuple-element.65), channel_id=1, replica_groups=mesh['vocab'=32] {'vocab'}, dimensions={0} | all-to-all | bytes 262144 | tf_op jit(solution)/shard_map/all_to_all | solution.py:508
  83.0 1.3 grad_logits.1
  84.3 0.3 collective-permute-start.10
  84.6 2.4 %collective-permute-done.10.sib_ref = bf16[512,1024]{1,0:T(8,128)(2,1)S(1)} collective-permute-done((bf16[512,1024]{1,0:T(8,128)(2,1)S(1)}, bf16[512,1024]{1,0:T(8,128)(2,1)S(1)}, u32[]{:S(2)}, u32[]{:S(2)}) %collective-permute-start.10) | collective-permute-done | bytes 1048608 | tf_op jit(solution)/shard_map/ppermute | solution.py:133
  87.1 9.6 %grad_hidden_partial.1 = (f32[4,2,16,1536]{3,2,1,0:T(8,128)S(1)}, bf16[4,2,16,1536]{3,2,1,0:T(8,128)(2,1)S(1)}, bf16[4,2,16,1536]{3,2,1,0:T(8,128)(2,1)S(1)}, bf...) custom-call(s32[4]{0:T(128)S(1)} %pad_add_fusion.refs_0_.core_ref, ...), custom_call_target="tpu_custom_call" | custom-call | flops 1 | bytes 1 | tf_op jit(solution)/shard_map/grad_hidden_partial/pallas_call | solution.py:533
  96.7 0.7 collective-permute-start.15
  97.4 0.2 collective-permute-start.12
  97.6 1.3 collective-permute-start.13
  98.8 2.0 %collective-permute-start.14 = (bf16[4,2,16,1536]{3,2,1,0:T(8,128)(2,1)S(1)}, bf16[4,2,16,1536]{3,2,1,0:T(8,128)(2,1)S(1)}, u32[]{:S(2)}, u32[]{:S(2)}) collective-permute-start(bf16[4,2,16,1536]{3,2,1,0:T(8,128)(2,1)S(1)} %get-tuple-element.81), channel_id=1, source_target_pairs={{0,6},{1,7},{2,4},{3,5},{4,2},{5,3},{6,0},{7,1},{8,14},{9,15},{10,... | collective-permute-start | bytes 1179656 | tf_op jit(solution)/shard_map/ppermute | solution.py:133
  100.9 1.2 collective-permute-start.16
  102.1 5.0 %collective-permute-done.15.refs_5_ = bf16[4,2,16,1024]{3,2,1,0:T(8,128)(2,1)S(1)} collective-permute-done((bf16[4,2,16,1024]{3,2,1,0:T(8,128)(2,1)S(1)}, bf16[4,2,16,1024]{3,2,1,0:T(8,128)(2,1)S(1)}, u32[]{:S(2)}, u32[]{:S(2)}) %collective-permute-start.15) | collective-permute-done | bytes 262176 | tf_op jit(solution)/shard_map/ppermute | solution.py:133
  107.1 1.9 %collective-permute-start.17 = (bf16[4,2,16,1024]{3,2,1,0:T(8,128)(2,1)S(1)}, bf16[4,2,16,1024]{3,2,1,0:T(8,128)(2,1)S(1)}, u32[]{:S(2)}, u32[]{:S(2)}) collective-permute-start(bf16[4,2,16,1024]{3,2,1,0:T(8,128)(2,1)S(1)} %get-tuple-element.84), channel_id=1, source_target_pairs={{0,24},{1,25},{2,26},{3,27},{4,28},{5,29},{6,30},{7,31},{8,16},{9,... | collective-permute-start | bytes 786440 | tf_op jit(solution)/shard_map/ppermute | solution.py:133
  109.0 9.4 %grad_head.1 = bf16[5120,1024]{1,0:T(8,128)(2,1)} custom-call(bf16[64,5120]{1,0:T(8,128)(2,1)S(1)} %constant_dynamic-update-slice_fusion.refs_0_, bf16[64,5120]{1,0:T(8,128)(2,1)S(1)} %collective-permute-done.3.refs_1_, bf16[64,5120]{1,0:T(8,128)(2,1)S(1)} %collective-permute-done.4.refs_2_, bf16[64,5120]{1,0:T(8,128)(2,1)S(1)} %collective-permute-done.5.refs_3_, ...), custom_call_target="tpu_custom_call" | custom-call | flops 1 | bytes 1 | tf_op jit(solution)/shard_map/grad_head/pallas_call | solution.py:556
  118.5 3.3 %collective-permute-done.16.refs_6_ = bf16[4,2,16,1024]{3,2,1,0:T(8,128)(2,1)S(1)} collective-permute-done((bf16[4,2,16,1024]{3,2,1,0:T(8,128)(2,1)S(1)}, bf16[4,2,16,1024]{3,2,1,0:T(8,128)(2,1)S(1)}, u32[]{:S(2)}, u32[]{:S(2)}) %collective-permute-start.16) | collective-permute-done | bytes 262176 | tf_op jit(solution)/shard_map/ppermute | solution.py:133
  121.8 0.3 first_sum.1
  122.1 0.4 collective-permute-start.21
  122.5 4.7 %collective-permute-start.18 = (bf16[2,16,1536]{2,1,0:T(8,128)(2,1)S(1)}, bf16[2,16,1536]{2,1,0:T(8,128)(2,1)S(1)}, u32[]{:S(2)}, u32[]{:S(2)}) collective-permute-start(bf16[2,16,1536]{2,1,0:T(8,128)(2,1)S(1)} %get-tuple-element.96), channel_id=1, source_target_pairs={{0,8},{1,9},{2,10},{3,11},{4,12},{5,13},{6,14},{7,15},{8,0},{9,1},... | collective-permute-start | bytes 294920 | tf_op jit(solution)/shard_map/ppermute | solution.py:133
  127.2 0.1 collective-permute-start.19
  127.3 2.3 %collective-permute-start.20 = (bf16[2,16,1536]{2,1,0:T(8,128)(2,1)S(1)}, bf16[2,16,1536]{2,1,0:T(8,128)(2,1)S(1)}, u32[]{:S(2)}, u32[]{:S(2)}) collective-permute-start(bf16[2,16,1536]{2,1,0:T(8,128)(2,1)S(1)} %get-tuple-element.98), channel_id=1, source_target_pairs={{0,24},{1,25},{2,26},{3,27},{4,28},{5,29},{6,30},{7,31},{8,16},{9,... | collective-permute-start | bytes 294920 | tf_op jit(solution)/shard_map/ppermute | solution.py:133
  129.6 1.0 collective-permute-start.22
  130.6 2.1 %collective-permute-start.23 = (bf16[2,16,1024]{2,1,0:T(8,128)(2,1)S(1)}, bf16[2,16,1024]{2,1,0:T(8,128)(2,1)S(1)}, u32[]{:S(2)}, u32[]{:S(2)}) collective-permute-start(bf16[2,16,1024]{2,1,0:T(8,128)(2,1)S(1)} %get-tuple-element.102), channel_id=1, source_target_pairs={{0,6},{1,7},{2,4},{3,5},{4,2},{5,3},{6,0},{7,1},{8,14},{9,15},{10,... | collective-permute-start | bytes 196616 | tf_op jit(solution)/shard_map/ppermute | solution.py:133
  132.7 1.2 collective-permute-done.22.refs_6_
  133.9 1.9 %collective-permute-done.23.refs_7_ = bf16[2,16,1024]{2,1,0:T(8,128)(2,1)S(1)} collective-permute-done((bf16[2,16,1024]{2,1,0:T(8,128)(2,1)S(1)}, bf16[2,16,1024]{2,1,0:T(8,128)(2,1)S(1)}, u32[]{:S(2)}, u32[]{:S(2)}) %collective-permute-start.23) | collective-permute-done | bytes 65568 | tf_op jit(solution)/shard_map/ppermute | solution.py:133
  135.8 0.2 collective-permute-done.19.refs_2_
  136.0 0.1 last_sum.1
  136.0 0.1 collective-permute-start.24
  136.1 0.6 slice_reduce_fusion
  136.7 0.6 collective-permute-done.24
  137.4 0.7 pad_maximum_fusion
  (41 shorter events, 0.3 us)
Async XLA Ops:
  0.6 17.3 %collective-permute-start.1 = (bf16[16,5120]{1,0:T(8,128)(2,1)}, bf16[16,5120]{1,0:T(8,128)(2,1)S(1)}, u32[]{:S(2)}, u32[]{:S(2)}) collective-permute-start(bf16[16,5120]{1,0:T(8,128)(2,1)} %param.7), channel_id=1, source_target_pairs={{0,16},{1,17},{2,18},{3,19},{4,20},{5,21},{6,22},{7,23},{8,24},{9,... | collective-permute-start | bytes 491528 | tf_op jit(solution)/shard_map/ppermute | solution.py:133
  4.7 13.2 %collective-permute-start = (bf16[16,5120]{1,0:T(8,128)(2,1)}, bf16[16,5120]{1,0:T(8,128)(2,1)S(1)}, u32[]{:S(2)}, u32[]{:S(2)}) collective-permute-start(bf16[16,5120]{1,0:T(8,128)(2,1)} %param.7), channel_id=1, source_target_pairs={{0,8},{1,9},{2,10},{3,11},{4,12},{5,13},{6,14},{7,15},{8,0},{9,1},... | collective-permute-start | bytes 491528 | tf_op jit(solution)/shard_map/ppermute | solution.py:133
  6.3 11.7 %collective-permute-start.2 = (bf16[16,5120]{1,0:T(8,128)(2,1)}, bf16[16,5120]{1,0:T(8,128)(2,1)S(1)}, u32[]{:S(2)}, u32[]{:S(2)}) collective-permute-start(bf16[16,5120]{1,0:T(8,128)(2,1)} %param.7), channel_id=1, source_target_pairs={{0,24},{1,25},{2,26},{3,27},{4,28},{5,29},{6,30},{7,31},{8,16},{9,... | collective-permute-start | bytes 491528 | tf_op jit(solution)/shard_map/ppermute | solution.py:133
  7.7 1.0 copy-start.4
  10.8 30.2 %all-to-all-start = ((bf16[32,67,128]{2,1,0:T(8,128)(2,1)}), bf16[32,67,128]{2,1,0:T(8,128)(2,1)}, u32[]{:S(2)}, u32[]{:S(2)}) async-start(bf16[32,67,128]{2,1,0:T(8,128)(2,1)} %slice.16), calls=%async_computation | async-start | bytes 1179648 | tf_op jit(solution)/shard_map/all_to_all | solution.py:452
  18.0 22.4 %collective-permute-start.4 = (bf16[64,5120]{1,0:T(8,128)(2,1)S(1)}, bf16[64,5120]{1,0:T(8,128)(2,1)S(1)}, u32[]{:S(2)}, u32[]{:S(2)}) collective-permute-start(bf16[64,5120]{1,0:T(8,128)(2,1)S(1)} %constant_dynamic-update-slice_fusion.refs_0_), channel_id=1, source_target_pairs={{0,4},{1,5},{2,6},{3,7},{4,0},{5,1},{6,2},{7,3},{8,12},{9,13},{10,... | collective-permute-start | bytes 1966088 | tf_op jit(solution)/shard_map/ppermute | solution.py:133
  19.8 21.2 %collective-permute-start.3 = (bf16[64,5120]{1,0:T(8,128)(2,1)S(1)}, bf16[64,5120]{1,0:T(8,128)(2,1)S(1)}, u32[]{:S(2)}, u32[]{:S(2)}) collective-permute-start(bf16[64,5120]{1,0:T(8,128)(2,1)S(1)} %constant_dynamic-update-slice_fusion.refs_0_), channel_id=1, source_target_pairs={{0,2},{1,3},{2,0},{3,1},{4,6},{5,7},{6,4},{7,5},{8,10},{9,11},{10,... | collective-permute-start | bytes 1966088 | tf_op jit(solution)/shard_map/ppermute | solution.py:133
  21.2 33.8 %collective-permute-start.5 = (bf16[64,5120]{1,0:T(8,128)(2,1)S(1)}, bf16[64,5120]{1,0:T(8,128)(2,1)S(1)}, u32[]{:S(2)}, u32[]{:S(2)}) collective-permute-start(bf16[64,5120]{1,0:T(8,128)(2,1)S(1)} %constant_dynamic-update-slice_fusion.refs_0_), channel_id=1, source_target_pairs={{0,6},{1,7},{2,4},{3,5},{4,2},{5,3},{6,0},{7,1},{8,14},{9,15},{10,... | collective-permute-start | bytes 1966088 | tf_op jit(solution)/shard_map/ppermute | solution.py:133
  21.9 61.2 %copy-start.7 = (f32[512]{0:T(512)S(1)}, f32[512]{0:T(512)}, u32[]{:S(2)}) copy-start(f32[512]{0:T(512)} %param.13) | copy-start | bytes 6148
  21.9 33.2 %collective-permute-start.6 = (bf16[64,5120]{1,0:T(8,128)(2,1)S(1)}, bf16[64,5120]{1,0:T(8,128)(2,1)S(1)}, u32[]{:S(2)}, u32[]{:S(2)}) collective-permute-start(bf16[64,5120]{1,0:T(8,128)(2,1)S(1)} %constant_dynamic-update-slice_fusion.refs_0_), channel_id=1, source_target_pairs={{0,1},{1,0},{2,3},{3,2},{4,5},{5,4},{6,7},{7,6},{8,9},{9,8},{10,11... | collective-permute-start | bytes 1966088 | tf_op jit(solution)/shard_map/ppermute | solution.py:133
  40.4 14.6 %collective-permute-start.8 = (bf16[64,5120]{1,0:T(8,128)(2,1)S(1)}, bf16[64,5120]{1,0:T(8,128)(2,1)}, u32[]{:S(2)}, u32[]{:S(2)}) collective-permute-start(bf16[64,5120]{1,0:T(8,128)(2,1)S(1)} %collective-permute-done.4.refs_2_), channel_id=1, source_target_pairs={{0,1},{1,0},{2,3},{3,2},{4,5},{5,4},{6,7},{7,6},{8,9},{9,8},{10,11... | collective-permute-start | bytes 1966088 | tf_op jit(solution)/shard_map/ppermute | solution.py:133
  41.0 14.1 %collective-permute-start.7 = (bf16[64,5120]{1,0:T(8,128)(2,1)S(1)}, bf16[64,5120]{1,0:T(8,128)(2,1)}, u32[]{:S(2)}, u32[]{:S(2)}) collective-permute-start(bf16[64,5120]{1,0:T(8,128)(2,1)S(1)} %collective-permute-done.3.refs_1_), channel_id=1, source_target_pairs={{0,1},{1,0},{2,3},{3,2},{4,5},{5,4},{6,7},{7,6},{8,9},{9,8},{10,11... | collective-permute-start | bytes 1966088 | tf_op jit(solution)/shard_map/ppermute | solution.py:133
  44.3 1.0 copy-start.3
  45.4 0.7 copy-start.5
  46.1 0.7 copy-start.6
  49.8 1.3 copy-start
  55.0 28.0 %copy-start.1 = (f32[512,1024]{1,0:T(8,128)S(1)}, f32[512,1024]{1,0:T(8,128)}, u32[]{:S(2)}) copy-start(f32[512,1024]{1,0:T(8,128)} %copy-done) | copy-start | bytes 6291460
  55.0 2.1 %collective-permute-start.9 = (bf16[64,5120]{1,0:T(8,128)(2,1)S(1)}, bf16[64,5120]{1,0:T(8,128)(2,1)S(1)}, u32[]{:S(2)}, u32[]{:S(2)}) collective-permute-start(bf16[64,5120]{1,0:T(8,128)(2,1)S(1)} %collective-permute-done.5.refs_3_), channel_id=1, source_target_pairs={{0,1},{1,0},{2,3},{3,2},{4,5},{5,4},{6,7},{7,6},{8,9},{9,8},{10,11... | collective-permute-start | bytes 1966088 | tf_op jit(solution)/shard_map/ppermute | solution.py:133
  57.1 29.9 %collective-permute-start.11 = (bf16[5120,1024]{1,0:T(8,128)(2,1)}, bf16[5120,1024]{1,0:T(8,128)(2,1)}, u32[]{:S(2)}, u32[]{:S(2)}) collective-permute-start(bf16[5120,1024]{1,0:T(8,128)(2,1)} %w_ref.1), channel_id=1, source_target_pairs={{0,1},{1,0},{2,3},{3,2},{4,5},{5,4},{6,7},{7,6},{8,9},{9,8},{10,11... | collective-permute-start | bytes 31457288 | tf_op jit(solution)/shard_map/ppermute | solution.py:133
  84.3 12.3 %copy-start.2 = (bf16[512,1024]{1,0:T(8,128)(2,1)}, bf16[512,1024]{1,0:T(8,128)(2,1)S(1)}, u32[]{:S(2)}) copy-start(bf16[512,1024]{1,0:T(8,128)(2,1)S(1)} %get-tuple-element.85.grad_ref.refs_8_) | copy-start | bytes 3145732
  84.3 2.7 %collective-permute-start.10 = (bf16[512,1024]{1,0:T(8,128)(2,1)S(1)}, bf16[512,1024]{1,0:T(8,128)(2,1)S(1)}, u32[]{:S(2)}, u32[]{:S(2)}) collective-permute-start(bf16[512,1024]{1,0:T(8,128)(2,1)S(1)} %get-tuple-element.85.grad_ref.refs_8_), channel_id=1, source_target_pairs={{0,1},{1,0},{2,3},{3,2},{4,5},{5,4},{6,7},{7,6},{8,9},{9,8},{10,11... | collective-permute-start | bytes 3145736 | tf_op jit(solution)/shard_map/ppermute | solution.py:133
  96.7 10.5 %collective-permute-start.15 = (bf16[4,2,16,1024]{3,2,1,0:T(8,128)(2,1)S(1)}, bf16[4,2,16,1024]{3,2,1,0:T(8,128)(2,1)S(1)}, u32[]{:S(2)}, u32[]{:S(2)}) collective-permute-start(bf16[4,2,16,1024]{3,2,1,0:T(8,128)(2,1)S(1)} %get-tuple-element.82), channel_id=1, source_target_pairs={{0,8},{1,9},{2,10},{3,11},{4,12},{5,13},{6,14},{7,15},{8,0},{9,1},... | collective-permute-start | bytes 786440 | tf_op jit(solution)/shard_map/ppermute | solution.py:133
  97.4 24.4 %collective-permute-start.12 = (bf16[4,2,16,1536]{3,2,1,0:T(8,128)(2,1)S(1)}, bf16[4,2,16,1536]{3,2,1,0:T(8,128)(2,1)S(1)}, u32[]{:S(2)}, u32[]{:S(2)}) collective-permute-start(bf16[4,2,16,1536]{3,2,1,0:T(8,128)(2,1)S(1)} %get-tuple-element.79), channel_id=1, source_target_pairs={{0,2},{1,3},{2,0},{3,1},{4,6},{5,7},{6,4},{7,5},{8,10},{9,11},{10,... | collective-permute-start | bytes 1179656 | tf_op jit(solution)/shard_map/ppermute | solution.py:133
  97.6 24.3 %collective-permute-start.13 = (bf16[4,2,16,1536]{3,2,1,0:T(8,128)(2,1)S(1)}, bf16[4,2,16,1536]{3,2,1,0:T(8,128)(2,1)S(1)}, u32[]{:S(2)}, u32[]{:S(2)}) collective-permute-start(bf16[4,2,16,1536]{3,2,1,0:T(8,128)(2,1)S(1)} %get-tuple-element.80), channel_id=1, source_target_pairs={{0,4},{1,5},{2,6},{3,7},{4,0},{5,1},{6,2},{7,3},{8,12},{9,13},{10,... | collective-permute-start | bytes 1179656 | tf_op jit(solution)/shard_map/ppermute | solution.py:133
  98.8 23.0 %collective-permute-start.14 = (bf16[4,2,16,1536]{3,2,1,0:T(8,128)(2,1)S(1)}, bf16[4,2,16,1536]{3,2,1,0:T(8,128)(2,1)S(1)}, u32[]{:S(2)}, u32[]{:S(2)}) collective-permute-start(bf16[4,2,16,1536]{3,2,1,0:T(8,128)(2,1)S(1)} %get-tuple-element.81), channel_id=1, source_target_pairs={{0,6},{1,7},{2,4},{3,5},{4,2},{5,3},{6,0},{7,1},{8,14},{9,15},{10,... | collective-permute-start | bytes 1179656 | tf_op jit(solution)/shard_map/ppermute | solution.py:133
  100.9 21.0 %collective-permute-start.16 = (bf16[4,2,16,1024]{3,2,1,0:T(8,128)(2,1)S(1)}, bf16[4,2,16,1024]{3,2,1,0:T(8,128)(2,1)S(1)}, u32[]{:S(2)}, u32[]{:S(2)}) collective-permute-start(bf16[4,2,16,1024]{3,2,1,0:T(8,128)(2,1)S(1)} %get-tuple-element.83), channel_id=1, source_target_pairs={{0,16},{1,17},{2,18},{3,19},{4,20},{5,21},{6,22},{7,23},{8,24},{9,... | collective-permute-start | bytes 786440 | tf_op jit(solution)/shard_map/ppermute | solution.py:133
  107.1 14.7 %collective-permute-start.17 = (bf16[4,2,16,1024]{3,2,1,0:T(8,128)(2,1)S(1)}, bf16[4,2,16,1024]{3,2,1,0:T(8,128)(2,1)S(1)}, u32[]{:S(2)}, u32[]{:S(2)}) collective-permute-start(bf16[4,2,16,1024]{3,2,1,0:T(8,128)(2,1)S(1)} %get-tuple-element.84), channel_id=1, source_target_pairs={{0,24},{1,25},{2,26},{3,27},{4,28},{5,29},{6,30},{7,31},{8,16},{9,... | collective-permute-start | bytes 786440 | tf_op jit(solution)/shard_map/ppermute | solution.py:133
  122.1 8.5 %collective-permute-start.21 = (bf16[2,16,1024]{2,1,0:T(8,128)(2,1)S(1)}, bf16[2,16,1024]{2,1,0:T(8,128)(2,1)S(1)}, u32[]{:S(2)}, u32[]{:S(2)}) collective-permute-start(bf16[2,16,1024]{2,1,0:T(8,128)(2,1)S(1)} %get-tuple-element.100), channel_id=1, source_target_pairs={{0,2},{1,3},{2,0},{3,1},{4,6},{5,7},{6,4},{7,5},{8,10},{9,11},{10,... | collective-permute-start | bytes 196616 | tf_op jit(solution)/shard_map/ppermute | solution.py:133
  122.5 13.3 %collective-permute-start.18 = (bf16[2,16,1536]{2,1,0:T(8,128)(2,1)S(1)}, bf16[2,16,1536]{2,1,0:T(8,128)(2,1)S(1)}, u32[]{:S(2)}, u32[]{:S(2)}) collective-permute-start(bf16[2,16,1536]{2,1,0:T(8,128)(2,1)S(1)} %get-tuple-element.96), channel_id=1, source_target_pairs={{0,8},{1,9},{2,10},{3,11},{4,12},{5,13},{6,14},{7,15},{8,0},{9,1},... | collective-permute-start | bytes 294920 | tf_op jit(solution)/shard_map/ppermute | solution.py:133
  127.2 8.7 %collective-permute-start.19 = (bf16[2,16,1536]{2,1,0:T(8,128)(2,1)S(1)}, bf16[2,16,1536]{2,1,0:T(8,128)(2,1)S(1)}, u32[]{:S(2)}, u32[]{:S(2)}) collective-permute-start(bf16[2,16,1536]{2,1,0:T(8,128)(2,1)S(1)} %get-tuple-element.97), channel_id=1, source_target_pairs={{0,16},{1,17},{2,18},{3,19},{4,20},{5,21},{6,22},{7,23},{8,24},{9,... | collective-permute-start | bytes 294920 | tf_op jit(solution)/shard_map/ppermute | solution.py:133
  127.3 8.6 %collective-permute-start.20 = (bf16[2,16,1536]{2,1,0:T(8,128)(2,1)S(1)}, bf16[2,16,1536]{2,1,0:T(8,128)(2,1)S(1)}, u32[]{:S(2)}, u32[]{:S(2)}) collective-permute-start(bf16[2,16,1536]{2,1,0:T(8,128)(2,1)S(1)} %get-tuple-element.98), channel_id=1, source_target_pairs={{0,24},{1,25},{2,26},{3,27},{4,28},{5,29},{6,30},{7,31},{8,16},{9,... | collective-permute-start | bytes 294920 | tf_op jit(solution)/shard_map/ppermute | solution.py:133
  129.6 4.3 %collective-permute-start.22 = (bf16[2,16,1024]{2,1,0:T(8,128)(2,1)S(1)}, bf16[2,16,1024]{2,1,0:T(8,128)(2,1)S(1)}, u32[]{:S(2)}, u32[]{:S(2)}) collective-permute-start(bf16[2,16,1024]{2,1,0:T(8,128)(2,1)S(1)} %get-tuple-element.101), channel_id=1, source_target_pairs={{0,4},{1,5},{2,6},{3,7},{4,0},{5,1},{6,2},{7,3},{8,12},{9,13},{10,... | collective-permute-start | bytes 196616 | tf_op jit(solution)/shard_map/ppermute | solution.py:133
  130.6 5.2 %collective-permute-start.23 = (bf16[2,16,1024]{2,1,0:T(8,128)(2,1)S(1)}, bf16[2,16,1024]{2,1,0:T(8,128)(2,1)S(1)}, u32[]{:S(2)}, u32[]{:S(2)}) collective-permute-start(bf16[2,16,1024]{2,1,0:T(8,128)(2,1)S(1)} %get-tuple-element.102), channel_id=1, source_target_pairs={{0,6},{1,7},{2,4},{3,5},{4,2},{5,3},{6,0},{7,1},{8,14},{9,15},{10,... | collective-permute-start | bytes 196616 | tf_op jit(solution)/shard_map/ppermute | solution.py:133
  136.0 1.3 collective-permute-start.24

commit v13 on v12

--- a/solution.py
+++ b/solution.py
@@ -178,21 +178,32 @@
 
 
 def assemble(pieces, rows, out_ref):
+    per_core = len(pieces) // CORES
     layers = pieces[0].shape[0] // rows
-    for k in range(layers):
-        for p, piece in enumerate(pieces):
-            out_ref[pl.ds((k * GROUP + p) * rows, rows), :] = piece[pl.ds(k * rows, rows), :]
+    for core in range(CORES):
+        mine = pieces[core * per_core : (core + 1) * per_core]
+        for k in range(layers):
+            span = pl.ds(k * rows, rows)
+            for j, piece in enumerate(mine[:CHIPS]):
+                at = pl.ds((k * GROUP + core * CHIPS + j) * rows, rows)
+                columns = slice(0, piece.shape[1])
+                out_ref[at, columns] = piece[span, :]
+            if per_core > CHIPS:
+                piece = mine[CHIPS]
+                columns = slice(out_ref.shape[1] - piece.shape[1], out_ref.shape[1])
+                out_ref[at, columns] = piece[span, :]
 
 
 def logits_kernel(rows, *refs):
-    pieces, refs = refs[:GROUP], refs[GROUP:]
+    pieces, refs = refs[:-8], refs[-8:]
     w_ref, prob_ref, logits_ref, stat_ref, hidden, weight, sems, cross_ref = refs
-    half, width = w_ref.shape[0] // 2, prob_ref.shape[1]
+    depth, width = w_ref.shape[0], prob_ref.shape[1]
+    parts = [slice(0, depth // 4), slice(depth // 4, depth)]
     tiles = w_ref.shape[1] // width
     step = pl.program_id(0)
 
     def copy(i):
-        span = pl.ds(i * half, half)
+        span = pl.ds(parts[i].start, parts[i].stop - parts[i].start)
         return pltpu.make_async_copy(w_ref.at[span, :], weight.at[span, :], sems.at[i])
 
     @pl.when(step == 0)
@@ -210,14 +221,14 @@
     def _():
         span = pl.ds(pl.multiple_of(step * width, width), width)
         logits_ref[:, span] = jnp.dot(
-            hidden[:, :half], weight[:half, span], preferred_element_type=jnp.float32
+            hidden[:, parts[0]], weight[parts[0], span], preferred_element_type=jnp.float32
         )
 
     @pl.when(step >= tiles)
     def _():
         span = pl.ds(pl.multiple_of((step - tiles) * width, width), width)
         total = logits_ref[:, span] + jnp.dot(
-            hidden[:, half:], weight[half:, span], preferred_element_type=jnp.float32
+            hidden[:, parts[1]], weight[parts[1], span], preferred_element_type=jnp.float32
         )
         logits_ref[:, span] = total
         product = total * prob_ref[...]
@@ -316,7 +327,15 @@
 
 def head_kernel(rows, *refs):
     pieces, (grad_ref, out_ref, hidden) = refs[:-3], refs[-3:]
-    assemble(pieces, rows, hidden)
+    per_core = CHIPS + 1
+    late = pl.program_id(0) >= pl.num_programs(0) // 2
+    for i in range(2):
+
+        @pl.when(late == (i == 1))
+        def _():
+            mine = [pieces[c * per_core : (c + 1) * per_core] for c in range(CORES)]
+            assemble([p for some in mine for p in (*some[: CHIPS - 1], some[CHIPS - 1 + i])], rows, hidden)
+
     out_ref[...] = lax.dot_general(
         hidden[...], grad_ref[...], (((0,), (0,)), ((), ())), preferred_element_type=jnp.float32
     ).astype(out_ref.dtype)
@@ -447,7 +466,9 @@
 
     column = [hidden_states] + [shift(hidden_states, k * GROUP) for k in range(1, layers)]
     column = jnp.concatenate(column, axis=0)
-    plane = [column] + [shift(column, j * CORES) for j in range(1, CHIPS)]
+    X, Y = CORES, 2 * CORES
+    plane = [column, shift(column, X), shift(column, Y)]
+    plane += [shift(plane[1][:, :half], Y), shift(plane[2][:, half:], X)]
     payload, place = pack_teacher(teacher_logits, block_lists, slab // side)
     arrived = lax.all_to_all(
         payload[:, : 3 - STAT_ROWS], "vocab", split_axis=0, concat_axis=0, tiled=True
@@ -474,10 +495,11 @@
         tail_mass.reshape(blocks, 1, side),
     )
 
-    plane[-1], prob = lax.optimization_barrier((plane[-1], prob))
+    sent_w = lax.dynamic_slice(head_weight, ((1 - core) * half, 0), (half, slab))
+    plane[-2], plane[-1], prob, sent_w = lax.optimization_barrier((plane[-2], plane[-1], prob, sent_w))
     pieces = plane + [shift(piece, 1) for piece in plane]
-    pieces, late_weight = lax.optimization_barrier((pieces, head_weight))
-    sib_w = shift(late_weight, 1)
+    pieces, sent_w = lax.optimization_barrier((pieces, sent_w))
+    sib_w = shift(sent_w, 1)
 
     width = 256 if slab % 256 == 0 else 128
     tiles = slab // width
@@ -536,7 +558,8 @@
             num_scalar_prefetch=1,
             grid=(5,),
             in_specs=[pl.BlockSpec((tokens, slab), lambda t, pos: (0, 0))] * 2
-            + [pl.BlockSpec((tile, slab), lambda t, pos: (pos[0] * 5 + t, 0))] * 2,
+            + [pl.BlockSpec((tile, slab), lambda t, pos: (pos[0] * 5 + t, 0))]
+            + [pl.BlockSpec((tile, slab), lambda t, pos: (t, 0))],
             out_specs=[wide_block] * CHIPS + [narrow_block] * layers,
             scratch_shapes=[pltpu.VMEM((tokens, slab), bf16)],
         ),
@@ -556,7 +579,13 @@
     grad_head = pl.pallas_call(
         functools.partial(head_kernel, rows),
         grid=(4,),
-        in_specs=[pl.BlockSpec((layers * rows, head_tile), lambda t: (0, t)) for _ in pieces]
+        in_specs=[
+            pl.BlockSpec(
+                (layers * rows, head_tile),
+                lambda t, i=i % (CHIPS + 1): (0, (t, jnp.minimum(t, 1), jnp.maximum(t - 2, 0))[max(i - 2, 0)]),
+            )
+            for i in range(len(pieces))
+        ]
         + [pl.BlockSpec((tokens, slab), whole)],
         out_specs=pl.BlockSpec((head_tile, slab), lambda t: (t, 0)),
         out_shape=jax.ShapeDtypeStruct((depth, slab), bf16),

time: 139 us -> 138 us (level)
  waiting for transfers between devices: 39.7 us -> 29.4 us
  local copies, waits for them, and re-layouts: 9.91 us -> 17.9 us
  starting transfers between devices: 33.9 us -> 36.1 us
    ppermute x25 -> x27, waiting for transfers between devices: 39.7 us -> 29.4 us  [shift(): return lax.ppermute(x, 'vocab', [(i, i ^ distance) for i in range(n)])]
    dynamic_slice x0 -> x1, local copies, waits for them, and re-layouts: none -> 5.43 us  [levels_plan(): lax.dynamic_slice(head_weight, ((1 - core) * half, 0), (half, slab))]
    ppermute x25 -> x27, starting transfers between devices: 27.7 us -> 29.9 us  [shift(): return lax.ppermute(x, 'vocab', [(i, i ^ distance) for i in range(n)])]
    slice x0 -> x2, local copies, waits for them, and re-layouts: none -> 1.49 us  [levels_plan(): plane += [shift(plane[1][:, :half], Y), shift(plane[2][:, half:], X)]]
    unnamed x19 -> x21, local copies, waits for them, and re-layouts: 5.63 us -> 6.66 us
  transfers between devices with their start and end apart: 26 -> 28, of which waited for: 11 -> 10; matrix products, arithmetic and copies ran while one was open for 5% -> 10% of each run, Pallas kernels for 20% -> 19%
where the time goes in v13:
time: 138 us
  Pallas kernels  36.5 us (26%)
  starting transfers between devices  36.1 us (26%)
  waiting for transfers between devices  29.4 us (21%)
  local copies, waits for them, and re-layouts  17.9 us (13%)
  blocking collectives  13.9 us (10%)
  other arithmetic  2.88 us (2%)
    ppermute x27, starting transfers between devices, shift(): return lax.ppermute(x, 'vocab', [(i, i ^ distance) for i in range(n)])  29.9 us
    ppermute x27, waiting for transfers between devices, shift(): return lax.ppermute(x, 'vocab', [(i, i ^ distance) for i in range(n)])  29.4 us
    all_to_all x1, blocking collectives, levels_plan(): lax.all_to_all(stat, 'vocab', split_axis=0, concat_axis=0, tiled=True)  13.9 us
    pallas_call x1, Pallas kernels, levels_plan(): pl.pallas_call(functools.partial(logits_kernel, rows), grid=(2 * tiles,),...  11 us
    pallas_call x1, Pallas kernels, levels_plan(): pl.pallas_call(functools.partial(head_kernel, rows), grid=(4,), in_specs=...  9.96 us
    pallas_call x1, Pallas kernels, levels_plan(): pl.pallas_call(functools.partial(partial_kernel, rows, wide_steps), grid_...  9.55 us
    unnamed x21, local copies, waits for them, and re-layouts  6.66 us
    all_to_all x1, starting transfers between devices, levels_plan(): lax.all_to_all(payload[:, :3 - STAT_ROWS], 'vocab', split_axis=0, concat_...  6.18 us
  transfers between devices with their start and end apart: 28, of which 10 were waited for; matrix products, arithmetic and copies ran while one was open for 10% of the time, Pallas kernels for 19%

profile of v13, /device:TPU:0, one launch (start us, length us, event | category | flops | bytes accessed | tf_op | source)
XLA Modules:
  0.0 137.7 jit_solution(4728383007284200895)
XLA Ops:
  0.6 4.1 %collective-permute-start.1 = (bf16[16,5120]{1,0:T(8,128)(2,1)}, bf16[16,5120]{1,0:T(8,128)(2,1)S(1)}, u32[]{:S(2)}, u32[]{:S(2)}) collective-permute-start(bf16[16,5120]{1,0:T(8,128)(2,1)} %param.7), channel_id=1, source_target_pairs={{0,16},{1,17},{2,18},{3,19},{4,20},{5,21},{6,22},{7,23},{8,24},{9,... | collective-permute-start | bytes 491528 | tf_op jit(solution)/shard_map/ppermute | solution.py:133
  4.7 1.6 %collective-permute-start = (bf16[16,5120]{1,0:T(8,128)(2,1)}, bf16[16,5120]{1,0:T(8,128)(2,1)S(1)}, u32[]{:S(2)}, u32[]{:S(2)}) collective-permute-start(bf16[16,5120]{1,0:T(8,128)(2,1)} %param.7), channel_id=1, source_target_pairs={{0,8},{1,9},{2,10},{3,11},{4,12},{5,13},{6,14},{7,15},{8,0},{9,1},... | collective-permute-start | bytes 491528 | tf_op jit(solution)/shard_map/ppermute | solution.py:133
  6.3 0.7 add_select_fusion.1
  7.1 0.2 convert_reduce_fusion
  7.3 0.1 add.85
  7.4 0.1 add.82
  7.5 0.1 add.89
  7.7 0.9 copy-done.4
  8.6 1.3 pack_teacher.1
  9.9 0.9 slice.26
  10.8 6.2 %all-to-all-start = ((bf16[32,67,128]{2,1,0:T(8,128)(2,1)}), bf16[32,67,128]{2,1,0:T(8,128)(2,1)}, u32[]{:S(2)}, u32[]{:S(2)}) async-start(bf16[32,67,128]{2,1,0:T(8,128)(2,1)} %slice.26), calls=%async_computation | async-start | bytes 1179648 | tf_op jit(solution)/shard_map/all_to_all | solution.py:473
  17.0 0.9 constant_dynamic-update-slice_fusion.3
  18.1 1.8 %collective-permute-start.4 = (bf16[64,5120]{1,0:T(8,128)(2,1)S(1)}, bf16[64,5120]{1,0:T(8,128)(2,1)S(1)}, u32[]{:S(2)}, u32[]{:S(2)}) collective-permute-start(bf16[64,5120]{1,0:T(8,128)(2,1)S(1)} %constant_dynamic-update-slice_fusion.refs_0_), channel_id=1, source_target_pairs={{0,4},{1,5},{2,6},{3,7},{4,0},{5,1},{6,2},{7,3},{8,12},{9,13},{10,... | collective-permute-start | bytes 1966088 | tf_op jit(solution)/shard_map/ppermute | solution.py:133
  19.9 1.5 %collective-permute-start.3 = (bf16[64,5120]{1,0:T(8,128)(2,1)S(1)}, bf16[64,5120]{1,0:T(8,128)(2,1)S(1)}, u32[]{:S(2)}, u32[]{:S(2)}) collective-permute-start(bf16[64,5120]{1,0:T(8,128)(2,1)S(1)} %constant_dynamic-update-slice_fusion.refs_0_), channel_id=1, source_target_pairs={{0,2},{1,3},{2,0},{3,1},{4,6},{5,7},{6,4},{7,5},{8,10},{9,11},{10,... | collective-permute-start | bytes 1966088 | tf_op jit(solution)/shard_map/ppermute | solution.py:133
  21.3 0.1 pad_add_fusion.refs_0_.core_ref
  21.4 0.2 select_reduce_fusion
  21.6 5.4 %constant_dynamic-slice_fusion = bf16[2560,1024]{1,0:T(8,128)(2,1)} fusion(bf16[5120,1024]{1,0:T(8,128)(2,1)} %w_ref.1, s32[]{:T(128)S(6)} %select_n.57), kind=kLoop, calls=%fused_computation.28 | loop fusion | bytes 10485764 | tf_op jit(solution)/shard_map/dynamic_slice | solution.py:498
  27.1 13.4 %collective-permute-done.4.refs_2_ = bf16[64,5120]{1,0:T(8,128)(2,1)S(1)} collective-permute-done((bf16[64,5120]{1,0:T(8,128)(2,1)S(1)}, bf16[64,5120]{1,0:T(8,128)(2,1)S(1)}, u32[]{:S(2)}, u32[]{:S(2)}) %collective-permute-start.4) | collective-permute-done | bytes 655392 | tf_op jit(solution)/shard_map/ppermute | solution.py:133
  40.4 0.7 slice.25
  41.2 1.2 collective-permute-start.6
  42.3 0.7 slice.24
  43.1 0.4 collective-permute-start.5
  43.4 0.5 collective-permute-start.8
  44.0 1.1 slice.27
  45.0 1.1 copy.27
  46.1 0.9 convert_reduce_fusion.1
  47.1 0.1 copy.29
  47.2 0.1 reshape.93
  47.4 1.0 copy-done.3
  48.4 3.1 %teacher_prob.1 = (f32[512,1024]{1,0:T(8,128)S(1)}, f32[16,128]{1,0:T(8,128)S(1)}) custom-call(s32[4]{0:T(128)S(1)} %pad_add_fusion.refs_0_.core_ref, s32[4,4]{1,0:T(4,128)S(1)} %broadcast_add_fusion.1.refs_1_, bf16[4,4,128,128]{3,2,1,0:T(8,128)(2,1)S(1)} %bitcast.18, f32[2,4,1,128]{3,2,1,0:T(1,128)S(1)} %bitcast.20, s32[4,1,128]{2,1,0:T(1,128)S(1)} %bitcast.21, ...), custom_call_target="tpu_custom_call" | custom-call | flops 1 | bytes 1 | tf_op jit(solution)/shard_map/teacher_prob/pallas_call | solution.py:478
  51.5 1.3 copy-done
  52.9 0.5 collective-permute-start.11
  53.4 1.3 collective-permute-done.10.refs_8_
  54.7 0.5 collective-permute-done.11.refs_9_
  55.2 0.1 collective-permute-start.13
  55.3 11.0 %logits.1 = (f32[512,1024]{1,0:T(8,128)S(1)}, f32[32,8,128]{2,1,0:T(8,128)S(1)}) custom-call(bf16[64,5120]{1,0:T(8,128)(2,1)S(1)} %constant_dynamic-update-slice_fusion.refs_0_, bf16[64,5120]{1,0:T(8,128)(2,1)S(1)} %collective-permute-done.3.refs_1_, bf16[64,5120]{1,0:T(8,128)(2,1)S(1)} %collective-permute-done.4.refs_2_, ...), custom_call_target="tpu_custom_call" | custom-call | flops 1 | bytes 1 | tf_op jit(solution)/shard_map/logits/pallas_call | solution.py:507
  66.4 13.9 %all_to_all.10.refs_1_ = f32[32,8,128]{2,1,0:T(8,128)S(1)} all-to-all(f32[32,8,128]{2,1,0:T(8,128)S(1)} %get-tuple-element.73), channel_id=1, replica_groups=mesh['vocab'=32] {'vocab'}, dimensions={0} | all-to-all | bytes 262144 | tf_op jit(solution)/shard_map/all_to_all | solution.py:530
  80.3 1.3 grad_logits.1
  81.6 0.3 collective-permute-start.12
  81.9 2.4 %collective-permute-done.12.sib_ref = bf16[512,1024]{1,0:T(8,128)(2,1)S(1)} collective-permute-done((bf16[512,1024]{1,0:T(8,128)(2,1)S(1)}, bf16[512,1024]{1,0:T(8,128)(2,1)S(1)}, u32[]{:S(2)}, u32[]{:S(2)}) %collective-permute-start.12) | collective-permute-done | bytes 1048608 | tf_op jit(solution)/shard_map/ppermute | solution.py:133
  84.3 2.4 %copy-done.8 = bf16[2560,1024]{1,0:T(8,128)(2,1)} copy-done((bf16[2560,1024]{1,0:T(8,128)(2,1)}, bf16[2560,1024]{1,0:T(8,128)(2,1)S(1)}, u32[]{:S(2)}) %copy-start.8) | copy-done | bytes 5242904
  86.7 9.6 %grad_hidden_partial.1 = (f32[4,2,16,1536]{3,2,1,0:T(8,128)S(1)}, bf16[4,2,16,1536]{3,2,1,0:T(8,128)(2,1)S(1)}, bf16[4,2,16,1536]{3,2,1,0:T(8,128)(2,1)S(1)}, bf...) custom-call(s32[4]{0:T(128)S(1)} %pad_add_fusion.refs_0_.core_ref, ...), custom_call_target="tpu_custom_call" | custom-call | flops 1 | bytes 1 | tf_op jit(solution)/shard_map/grad_hidden_partial/pallas_call | solution.py:555
  96.2 0.7 collective-permute-start.17
  97.0 0.2 collective-permute-start.14
  97.2 1.3 collective-permute-start.15
  98.4 2.0 %collective-permute-start.16 = (bf16[4,2,16,1536]{3,2,1,0:T(8,128)(2,1)S(1)}, bf16[4,2,16,1536]{3,2,1,0:T(8,128)(2,1)S(1)}, u32[]{:S(2)}, u32[]{:S(2)}) collective-permute-start(bf16[4,2,16,1536]{3,2,1,0:T(8,128)(2,1)S(1)} %get-tuple-element.89), channel_id=1, source_target_pairs={{0,6},{1,7},{2,4},{3,5},{4,2},{5,3},{6,0},{7,1},{8,14},{9,15},{10,... | collective-permute-start | bytes 1179656 | tf_op jit(solution)/shard_map/ppermute | solution.py:133
  100.5 1.2 collective-permute-start.18
  101.7 5.0 %collective-permute-done.17.refs_5_ = bf16[4,2,16,1024]{3,2,1,0:T(8,128)(2,1)S(1)} collective-permute-done((bf16[4,2,16,1024]{3,2,1,0:T(8,128)(2,1)S(1)}, bf16[4,2,16,1024]{3,2,1,0:T(8,128)(2,1)S(1)}, u32[]{:S(2)}, u32[]{:S(2)}) %collective-permute-start.17) | collective-permute-done | bytes 262176 | tf_op jit(solution)/shard_map/ppermute | solution.py:133
  106.7 1.9 %collective-permute-start.19 = (bf16[4,2,16,1024]{3,2,1,0:T(8,128)(2,1)S(1)}, bf16[4,2,16,1024]{3,2,1,0:T(8,128)(2,1)S(1)}, u32[]{:S(2)}, u32[]{:S(2)}) collective-permute-start(bf16[4,2,16,1024]{3,2,1,0:T(8,128)(2,1)S(1)} %get-tuple-element.92), channel_id=1, source_target_pairs={{0,24},{1,25},{2,26},{3,27},{4,28},{5,29},{6,30},{7,31},{8,16},{9,... | collective-permute-start | bytes 786440 | tf_op jit(solution)/shard_map/ppermute | solution.py:133
  108.6 10.0 %grad_head.1 = bf16[5120,1024]{1,0:T(8,128)(2,1)} custom-call(bf16[64,5120]{1,0:T(8,128)(2,1)S(1)} %constant_dynamic-update-slice_fusion.refs_0_, bf16[64,5120]{1,0:T(8,128)(2,1)S(1)} %collective-permute-done.3.refs_1_, bf16[64,5120]{1,0:T(8,128)(2,1)S(1)} %collective-permute-done.4.refs_2_, bf16[64,2560]{1,0:T(8,128)(2,1)} %collective-permute-done.5.refs_3_, ...), custom_call_target="tpu_custom_call" | custom-call | flops 1 | bytes 1 | tf_op jit(solution)/shard_map/grad_head/pallas_call | solution.py:579
  118.6 2.8 %collective-permute-done.18.refs_6_ = bf16[4,2,16,1024]{3,2,1,0:T(8,128)(2,1)S(1)} collective-permute-done((bf16[4,2,16,1024]{3,2,1,0:T(8,128)(2,1)S(1)}, bf16[4,2,16,1024]{3,2,1,0:T(8,128)(2,1)S(1)}, u32[]{:S(2)}, u32[]{:S(2)}) %collective-permute-start.18) | collective-permute-done | bytes 262176 | tf_op jit(solution)/shard_map/ppermute | solution.py:133
  121.4 0.3 first_sum.1
  121.7 0.4 collective-permute-start.23
  122.1 4.7 %collective-permute-start.20 = (bf16[2,16,1536]{2,1,0:T(8,128)(2,1)S(1)}, bf16[2,16,1536]{2,1,0:T(8,128)(2,1)S(1)}, u32[]{:S(2)}, u32[]{:S(2)}) collective-permute-start(bf16[2,16,1536]{2,1,0:T(8,128)(2,1)S(1)} %get-tuple-element.104), channel_id=1, source_target_pairs={{0,8},{1,9},{2,10},{3,11},{4,12},{5,13},{6,14},{7,15},{8,0},{9,1},... | collective-permute-start | bytes 294920 | tf_op jit(solution)/shard_map/ppermute | solution.py:133
  126.8 0.1 collective-permute-start.21
  126.9 2.3 %collective-permute-start.22 = (bf16[2,16,1536]{2,1,0:T(8,128)(2,1)S(1)}, bf16[2,16,1536]{2,1,0:T(8,128)(2,1)S(1)}, u32[]{:S(2)}, u32[]{:S(2)}) collective-permute-start(bf16[2,16,1536]{2,1,0:T(8,128)(2,1)S(1)} %get-tuple-element.106), channel_id=1, source_target_pairs={{0,24},{1,25},{2,26},{3,27},{4,28},{5,29},{6,30},{7,31},{8,16},{9,... | collective-permute-start | bytes 294920 | tf_op jit(solution)/shard_map/ppermute | solution.py:133
  129.2 1.0 collective-permute-start.24
  130.2 2.1 %collective-permute-start.25 = (bf16[2,16,1024]{2,1,0:T(8,128)(2,1)S(1)}, bf16[2,16,1024]{2,1,0:T(8,128)(2,1)S(1)}, u32[]{:S(2)}, u32[]{:S(2)}) collective-permute-start(bf16[2,16,1024]{2,1,0:T(8,128)(2,1)S(1)} %get-tuple-element.110), channel_id=1, source_target_pairs={{0,6},{1,7},{2,4},{3,5},{4,2},{5,3},{6,0},{7,1},{8,14},{9,15},{10,... | collective-permute-start | bytes 196616 | tf_op jit(solution)/shard_map/ppermute | solution.py:133
  132.3 1.2 collective-permute-done.24.refs_6_
  133.5 1.9 %collective-permute-done.25.refs_7_ = bf16[2,16,1024]{2,1,0:T(8,128)(2,1)S(1)} collective-permute-done((bf16[2,16,1024]{2,1,0:T(8,128)(2,1)S(1)}, bf16[2,16,1024]{2,1,0:T(8,128)(2,1)S(1)}, u32[]{:S(2)}, u32[]{:S(2)}) %collective-permute-start.25) | collective-permute-done | bytes 65568 | tf_op jit(solution)/shard_map/ppermute | solution.py:133
  135.4 0.2 collective-permute-done.21.refs_2_
  135.7 0.6 slice_reduce_fusion
  136.3 0.6 collective-permute-done.26
  137.0 0.7 pad_maximum_fusion
  (50 shorter events, 0.5 us)
Async XLA Ops:
  0.6 17.4 %collective-permute-start.1 = (bf16[16,5120]{1,0:T(8,128)(2,1)}, bf16[16,5120]{1,0:T(8,128)(2,1)S(1)}, u32[]{:S(2)}, u32[]{:S(2)}) collective-permute-start(bf16[16,5120]{1,0:T(8,128)(2,1)} %param.7), channel_id=1, source_target_pairs={{0,16},{1,17},{2,18},{3,19},{4,20},{5,21},{6,22},{7,23},{8,24},{9,... | collective-permute-start | bytes 491528 | tf_op jit(solution)/shard_map/ppermute | solution.py:133
  4.7 13.3 %collective-permute-start = (bf16[16,5120]{1,0:T(8,128)(2,1)}, bf16[16,5120]{1,0:T(8,128)(2,1)S(1)}, u32[]{:S(2)}, u32[]{:S(2)}) collective-permute-start(bf16[16,5120]{1,0:T(8,128)(2,1)} %param.7), channel_id=1, source_target_pairs={{0,8},{1,9},{2,10},{3,11},{4,12},{5,13},{6,14},{7,15},{8,0},{9,1},... | collective-permute-start | bytes 491528 | tf_op jit(solution)/shard_map/ppermute | solution.py:133
  6.3 11.8 %collective-permute-start.2 = (bf16[16,5120]{1,0:T(8,128)(2,1)}, bf16[16,5120]{1,0:T(8,128)(2,1)S(1)}, u32[]{:S(2)}, u32[]{:S(2)}) collective-permute-start(bf16[16,5120]{1,0:T(8,128)(2,1)} %param.7), channel_id=1, source_target_pairs={{0,24},{1,25},{2,26},{3,27},{4,28},{5,29},{6,30},{7,31},{8,16},{9,... | collective-permute-start | bytes 491528 | tf_op jit(solution)/shard_map/ppermute | solution.py:133
  7.7 1.0 copy-start.4
  10.8 33.1 %all-to-all-start = ((bf16[32,67,128]{2,1,0:T(8,128)(2,1)}), bf16[32,67,128]{2,1,0:T(8,128)(2,1)}, u32[]{:S(2)}, u32[]{:S(2)}) async-start(bf16[32,67,128]{2,1,0:T(8,128)(2,1)} %slice.26), calls=%async_computation | async-start | bytes 1179648 | tf_op jit(solution)/shard_map/all_to_all | solution.py:473
  18.1 22.3 %collective-permute-start.4 = (bf16[64,5120]{1,0:T(8,128)(2,1)S(1)}, bf16[64,5120]{1,0:T(8,128)(2,1)S(1)}, u32[]{:S(2)}, u32[]{:S(2)}) collective-permute-start(bf16[64,5120]{1,0:T(8,128)(2,1)S(1)} %constant_dynamic-update-slice_fusion.refs_0_), channel_id=1, source_target_pairs={{0,4},{1,5},{2,6},{3,7},{4,0},{5,1},{6,2},{7,3},{8,12},{9,13},{10,... | collective-permute-start | bytes 1966088 | tf_op jit(solution)/shard_map/ppermute | solution.py:133
  19.9 22.5 %collective-permute-start.3 = (bf16[64,5120]{1,0:T(8,128)(2,1)S(1)}, bf16[64,5120]{1,0:T(8,128)(2,1)S(1)}, u32[]{:S(2)}, u32[]{:S(2)}) collective-permute-start(bf16[64,5120]{1,0:T(8,128)(2,1)S(1)} %constant_dynamic-update-slice_fusion.refs_0_), channel_id=1, source_target_pairs={{0,2},{1,3},{2,0},{3,1},{4,6},{5,7},{6,4},{7,5},{8,10},{9,11},{10,... | collective-permute-start | bytes 1966088 | tf_op jit(solution)/shard_map/ppermute | solution.py:133
  21.6 25.7 %copy-start.5 = (s32[4,128]{1,0:T(4,128)S(1)}, s32[4,128]{1,0:T(4,128)}, u32[]{:S(2)}) copy-start(s32[4,128]{1,0:T(4,128)} %param.11) | copy-start | bytes 6148
  21.6 25.7 %copy-start.6 = (f32[512]{0:T(512)S(1)}, f32[512]{0:T(512)}, u32[]{:S(2)}) copy-start(f32[512]{0:T(512)} %param.12) | copy-start | bytes 6148
  27.1 26.3 %collective-permute-start.7 = (bf16[64,5120]{1,0:T(8,128)(2,1)S(1)}, bf16[64,5120]{1,0:T(8,128)(2,1)S(1)}, u32[]{:S(2)}, u32[]{:S(2)}) collective-permute-start(bf16[64,5120]{1,0:T(8,128)(2,1)S(1)} %constant_dynamic-update-slice_fusion.refs_0_), channel_id=1, source_target_pairs={{0,1},{1,0},{2,3},{3,2},{4,5},{5,4},{6,7},{7,6},{8,9},{9,8},{10,11... | collective-permute-start | bytes 1966088 | tf_op jit(solution)/shard_map/ppermute | solution.py:133
  41.2 11.6 %collective-permute-start.6 = (bf16[64,2560]{1,0:T(8,128)(2,1)}, bf16[64,2560]{1,0:T(8,128)(2,1)}, u32[]{:S(2)}, u32[]{:S(2)}) collective-permute-start(bf16[64,2560]{1,0:T(8,128)(2,1)} %slice.25), channel_id=1, source_target_pairs={{0,2},{1,3},{2,0},{3,1},{4,6},{5,7},{6,4},{7,5},{8,10},{9,11},{10,... | collective-permute-start | bytes 983048 | tf_op jit(solution)/shard_map/ppermute | solution.py:133
  43.1 9.7 %collective-permute-start.5 = (bf16[64,2560]{1,0:T(8,128)(2,1)}, bf16[64,2560]{1,0:T(8,128)(2,1)}, u32[]{:S(2)}, u32[]{:S(2)}) collective-permute-start(bf16[64,2560]{1,0:T(8,128)(2,1)} %slice.24), channel_id=1, source_target_pairs={{0,4},{1,5},{2,6},{3,7},{4,0},{5,1},{6,2},{7,3},{8,12},{9,13},{10,... | collective-permute-start | bytes 983048 | tf_op jit(solution)/shard_map/ppermute | solution.py:133
  43.4 11.8 %collective-permute-start.9 = (bf16[64,5120]{1,0:T(8,128)(2,1)S(1)}, bf16[64,5120]{1,0:T(8,128)(2,1)S(1)}, u32[]{:S(2)}, u32[]{:S(2)}) collective-permute-start(bf16[64,5120]{1,0:T(8,128)(2,1)S(1)} %collective-permute-done.4.refs_2_), channel_id=1, source_target_pairs={{0,1},{1,0},{2,3},{3,2},{4,5},{5,4},{6,7},{7,6},{8,9},{9,8},{10,11... | collective-permute-start | bytes 1966088 | tf_op jit(solution)/shard_map/ppermute | solution.py:133
  43.4 11.8 %collective-permute-start.8 = (bf16[64,5120]{1,0:T(8,128)(2,1)S(1)}, bf16[64,5120]{1,0:T(8,128)(2,1)}, u32[]{:S(2)}, u32[]{:S(2)}) collective-permute-start(bf16[64,5120]{1,0:T(8,128)(2,1)S(1)} %collective-permute-done.3.refs_1_), channel_id=1, source_target_pairs={{0,1},{1,0},{2,3},{3,2},{4,5},{5,4},{6,7},{7,6},{8,9},{9,8},{10,11... | collective-permute-start | bytes 1966088 | tf_op jit(solution)/shard_map/ppermute | solution.py:133
  47.3 1.0 copy-start.3
  51.5 1.3 copy-start
  52.8 27.5 %copy-start.1 = (f32[512,1024]{1,0:T(8,128)S(1)}, f32[512,1024]{1,0:T(8,128)}, u32[]{:S(2)}) copy-start(f32[512,1024]{1,0:T(8,128)} %copy-done) | copy-start | bytes 6291460
  52.8 27.5 %copy-start.7 = (f32[512]{0:T(512)S(1)}, f32[512]{0:T(512)}, u32[]{:S(2)}) copy-start(f32[512]{0:T(512)} %param.13) | copy-start | bytes 6148
  52.8 1.9 %collective-permute-start.10 = (bf16[64,2560]{1,0:T(8,128)(2,1)}, bf16[64,2560]{1,0:T(8,128)(2,1)S(1)}, u32[]{:S(2)}, u32[]{:S(2)}) collective-permute-start(bf16[64,2560]{1,0:T(8,128)(2,1)} %collective-permute-done.5.refs_3_), channel_id=1, source_target_pairs={{0,1},{1,0},{2,3},{3,2},{4,5},{5,4},{6,7},{7,6},{8,9},{9,8},{10,11... | collective-permute-start | bytes 983048 | tf_op jit(solution)/shard_map/ppermute | solution.py:133
  52.9 2.3 %collective-permute-start.11 = (bf16[64,2560]{1,0:T(8,128)(2,1)}, bf16[64,2560]{1,0:T(8,128)(2,1)S(1)}, u32[]{:S(2)}, u32[]{:S(2)}) collective-permute-start(bf16[64,2560]{1,0:T(8,128)(2,1)} %collective-permute-done.6.refs_4_), channel_id=1, source_target_pairs={{0,1},{1,0},{2,3},{3,2},{4,5},{5,4},{6,7},{7,6},{8,9},{9,8},{10,11... | collective-permute-start | bytes 983048 | tf_op jit(solution)/shard_map/ppermute | solution.py:133
  55.2 29.1 %collective-permute-start.13 = (bf16[2560,1024]{1,0:T(8,128)(2,1)}, bf16[2560,1024]{1,0:T(8,128)(2,1)S(1)}, u32[]{:S(2)}, u32[]{:S(2)}) collective-permute-start(bf16[2560,1024]{1,0:T(8,128)(2,1)} %constant_dynamic-slice_fusion), channel_id=1, source_target_pairs={{0,1},{1,0},{2,3},{3,2},{4,5},{5,4},{6,7},{7,6},{8,9},{9,8},{10,11... | collective-permute-start | bytes 15728648 | tf_op jit(solution)/shard_map/ppermute | solution.py:133
  81.6 14.7 %copy-start.2 = (bf16[512,1024]{1,0:T(8,128)(2,1)}, bf16[512,1024]{1,0:T(8,128)(2,1)S(1)}, u32[]{:S(2)}) copy-start(bf16[512,1024]{1,0:T(8,128)(2,1)S(1)} %get-tuple-element.93.grad_ref.refs_10_) | copy-start | bytes 3145732
  81.6 2.7 %collective-permute-start.12 = (bf16[512,1024]{1,0:T(8,128)(2,1)S(1)}, bf16[512,1024]{1,0:T(8,128)(2,1)S(1)}, u32[]{:S(2)}, u32[]{:S(2)}) collective-permute-start(bf16[512,1024]{1,0:T(8,128)(2,1)S(1)} %get-tuple-element.93.grad_ref.refs_10_), channel_id=1, source_target_pairs={{0,1},{1,0},{2,3},{3,2},{4,5},{5,4},{6,7},{7,6},{8,9},{9,8},{10,11... | collective-permute-start | bytes 3145736 | tf_op jit(solution)/shard_map/ppermute | solution.py:133
  84.3 2.4 %copy-start.8 = (bf16[2560,1024]{1,0:T(8,128)(2,1)}, bf16[2560,1024]{1,0:T(8,128)(2,1)S(1)}, u32[]{:S(2)}) copy-start(bf16[2560,1024]{1,0:T(8,128)(2,1)S(1)} %collective-permute-done.13.sib_w_ref) | copy-start | bytes 15728644
  96.2 10.5 %collective-permute-start.17 = (bf16[4,2,16,1024]{3,2,1,0:T(8,128)(2,1)S(1)}, bf16[4,2,16,1024]{3,2,1,0:T(8,128)(2,1)S(1)}, u32[]{:S(2)}, u32[]{:S(2)}) collective-permute-start(bf16[4,2,16,1024]{3,2,1,0:T(8,128)(2,1)S(1)} %get-tuple-element.90), channel_id=1, source_target_pairs={{0,8},{1,9},{2,10},{3,11},{4,12},{5,13},{6,14},{7,15},{8,0},{9,1},... | collective-permute-start | bytes 786440 | tf_op jit(solution)/shard_map/ppermute | solution.py:133
  97.0 24.5 %collective-permute-start.14 = (bf16[4,2,16,1536]{3,2,1,0:T(8,128)(2,1)S(1)}, bf16[4,2,16,1536]{3,2,1,0:T(8,128)(2,1)S(1)}, u32[]{:S(2)}, u32[]{:S(2)}) collective-permute-start(bf16[4,2,16,1536]{3,2,1,0:T(8,128)(2,1)S(1)} %get-tuple-element.87), channel_id=1, source_target_pairs={{0,2},{1,3},{2,0},{3,1},{4,6},{5,7},{6,4},{7,5},{8,10},{9,11},{10,... | collective-permute-start | bytes 1179656 | tf_op jit(solution)/shard_map/ppermute | solution.py:133
  97.2 24.3 %collective-permute-start.15 = (bf16[4,2,16,1536]{3,2,1,0:T(8,128)(2,1)S(1)}, bf16[4,2,16,1536]{3,2,1,0:T(8,128)(2,1)S(1)}, u32[]{:S(2)}, u32[]{:S(2)}) collective-permute-start(bf16[4,2,16,1536]{3,2,1,0:T(8,128)(2,1)S(1)} %get-tuple-element.88), channel_id=1, source_target_pairs={{0,4},{1,5},{2,6},{3,7},{4,0},{5,1},{6,2},{7,3},{8,12},{9,13},{10,... | collective-permute-start | bytes 1179656 | tf_op jit(solution)/shard_map/ppermute | solution.py:133
  98.4 23.0 %collective-permute-start.16 = (bf16[4,2,16,1536]{3,2,1,0:T(8,128)(2,1)S(1)}, bf16[4,2,16,1536]{3,2,1,0:T(8,128)(2,1)S(1)}, u32[]{:S(2)}, u32[]{:S(2)}) collective-permute-start(bf16[4,2,16,1536]{3,2,1,0:T(8,128)(2,1)S(1)} %get-tuple-element.89), channel_id=1, source_target_pairs={{0,6},{1,7},{2,4},{3,5},{4,2},{5,3},{6,0},{7,1},{8,14},{9,15},{10,... | collective-permute-start | bytes 1179656 | tf_op jit(solution)/shard_map/ppermute | solution.py:133
  100.5 21.0 %collective-permute-start.18 = (bf16[4,2,16,1024]{3,2,1,0:T(8,128)(2,1)S(1)}, bf16[4,2,16,1024]{3,2,1,0:T(8,128)(2,1)S(1)}, u32[]{:S(2)}, u32[]{:S(2)}) collective-permute-start(bf16[4,2,16,1024]{3,2,1,0:T(8,128)(2,1)S(1)} %get-tuple-element.91), channel_id=1, source_target_pairs={{0,16},{1,17},{2,18},{3,19},{4,20},{5,21},{6,22},{7,23},{8,24},{9,... | collective-permute-start | bytes 786440 | tf_op jit(solution)/shard_map/ppermute | solution.py:133
  106.7 14.7 %collective-permute-start.19 = (bf16[4,2,16,1024]{3,2,1,0:T(8,128)(2,1)S(1)}, bf16[4,2,16,1024]{3,2,1,0:T(8,128)(2,1)S(1)}, u32[]{:S(2)}, u32[]{:S(2)}) collective-permute-start(bf16[4,2,16,1024]{3,2,1,0:T(8,128)(2,1)S(1)} %get-tuple-element.92), channel_id=1, source_target_pairs={{0,24},{1,25},{2,26},{3,27},{4,28},{5,29},{6,30},{7,31},{8,16},{9,... | collective-permute-start | bytes 786440 | tf_op jit(solution)/shard_map/ppermute | solution.py:133
  121.7 8.5 %collective-permute-start.23 = (bf16[2,16,1024]{2,1,0:T(8,128)(2,1)S(1)}, bf16[2,16,1024]{2,1,0:T(8,128)(2,1)S(1)}, u32[]{:S(2)}, u32[]{:S(2)}) collective-permute-start(bf16[2,16,1024]{2,1,0:T(8,128)(2,1)S(1)} %get-tuple-element.108), channel_id=1, source_target_pairs={{0,2},{1,3},{2,0},{3,1},{4,6},{5,7},{6,4},{7,5},{8,10},{9,11},{10,... | collective-permute-start | bytes 196616 | tf_op jit(solution)/shard_map/ppermute | solution.py:133
  122.1 13.3 %collective-permute-start.20 = (bf16[2,16,1536]{2,1,0:T(8,128)(2,1)S(1)}, bf16[2,16,1536]{2,1,0:T(8,128)(2,1)S(1)}, u32[]{:S(2)}, u32[]{:S(2)}) collective-permute-start(bf16[2,16,1536]{2,1,0:T(8,128)(2,1)S(1)} %get-tuple-element.104), channel_id=1, source_target_pairs={{0,8},{1,9},{2,10},{3,11},{4,12},{5,13},{6,14},{7,15},{8,0},{9,1},... | collective-permute-start | bytes 294920 | tf_op jit(solution)/shard_map/ppermute | solution.py:133
  126.8 8.7 %collective-permute-start.21 = (bf16[2,16,1536]{2,1,0:T(8,128)(2,1)S(1)}, bf16[2,16,1536]{2,1,0:T(8,128)(2,1)S(1)}, u32[]{:S(2)}, u32[]{:S(2)}) collective-permute-start(bf16[2,16,1536]{2,1,0:T(8,128)(2,1)S(1)} %get-tuple-element.105), channel_id=1, source_target_pairs={{0,16},{1,17},{2,18},{3,19},{4,20},{5,21},{6,22},{7,23},{8,24},{9,... | collective-permute-start | bytes 294920 | tf_op jit(solution)/shard_map/ppermute | solution.py:133
  126.9 8.6 %collective-permute-start.22 = (bf16[2,16,1536]{2,1,0:T(8,128)(2,1)S(1)}, bf16[2,16,1536]{2,1,0:T(8,128)(2,1)S(1)}, u32[]{:S(2)}, u32[]{:S(2)}) collective-permute-start(bf16[2,16,1536]{2,1,0:T(8,128)(2,1)S(1)} %get-tuple-element.106), channel_id=1, source_target_pairs={{0,24},{1,25},{2,26},{3,27},{4,28},{5,29},{6,30},{7,31},{8,16},{9,... | collective-permute-start | bytes 294920 | tf_op jit(solution)/shard_map/ppermute | solution.py:133
  129.2 4.3 %collective-permute-start.24 = (bf16[2,16,1024]{2,1,0:T(8,128)(2,1)S(1)}, bf16[2,16,1024]{2,1,0:T(8,128)(2,1)S(1)}, u32[]{:S(2)}, u32[]{:S(2)}) collective-permute-start(bf16[2,16,1024]{2,1,0:T(8,128)(2,1)S(1)} %get-tuple-element.109), channel_id=1, source_target_pairs={{0,4},{1,5},{2,6},{3,7},{4,0},{5,1},{6,2},{7,3},{8,12},{9,13},{10,... | collective-permute-start | bytes 196616 | tf_op jit(solution)/shard_map/ppermute | solution.py:133
  130.2 5.2 %collective-permute-start.25 = (bf16[2,16,1024]{2,1,0:T(8,128)(2,1)S(1)}, bf16[2,16,1024]{2,1,0:T(8,128)(2,1)S(1)}, u32[]{:S(2)}, u32[]{:S(2)}) collective-permute-start(bf16[2,16,1024]{2,1,0:T(8,128)(2,1)S(1)} %get-tuple-element.110), channel_id=1, source_target_pairs={{0,6},{1,7},{2,4},{3,5},{4,2},{5,3},{6,0},{7,1},{8,14},{9,15},{10,... | collective-permute-start | bytes 196616 | tf_op jit(solution)/shard_map/ppermute | solution.py:133
  135.6 1.3 collective-permute-start.26

commit v14 on v13

--- a/solution.py
+++ b/solution.py
@@ -107,7 +107,8 @@
 SLOTS = 4
 LIGHT = pl.CostEstimate(flops=1, bytes_accessed=1, transcendentals=0)
 SMALL_VMEM = 16 * 1024 * 1024
-LOGITS_VMEM = 46 * 1024 * 1024
+LOGITS_VMEM = 40 * 1024 * 1024
+PARTIAL_VMEM = 42 * 1024 * 1024
 LARGE_VMEM = 48 * 1024 * 1024
 STAT_ROWS = 16
 
@@ -287,7 +288,7 @@
         grad_ref[span, :] = (weight * (student - prob_ref[span, :])).astype(grad_ref.dtype)
 
 
-def partial_kernel(rows, wide_steps, core_ref, grad_ref, sib_ref, w_ref, sib_w_ref, *refs):
+def partial_kernel(rows, core_ref, grad_ref, sib_ref, w_ref, sib_w_ref, *refs):
     outs, swapped = refs[:-1], refs[-1]
     wide_outs, narrow_outs = outs[:CHIPS], outs[CHIPS:]
     layers = len(narrow_outs)
@@ -307,22 +308,37 @@
         grad_ref[...], w_ref[...], contract, preferred_element_type=jnp.float32
     ) + lax.dot_general(swapped[...], sib_w_ref[...], contract, preferred_element_type=jnp.float32)
 
-    def parts():
+    def store(outs, by_layer, columns, source):
         for k in range(layers):
             for core in range(CORES):
                 for j in range(CHIPS):
                     start = (k * GROUP + core * CHIPS + j) * rows
-                    yield k, core, j, total[start : start + rows]
-
-    @pl.when(step < wide_steps)
-    def _():
-        for k, core, j, part in parts():
-            wide_outs[j][k, core] = part.astype(wide_outs[j].dtype)
-
-    @pl.when(step >= wide_steps)
-    def _():
-        for k, core, j, part in parts():
-            narrow_outs[k][j, core] = part.astype(narrow_outs[k].dtype)
+                    out, i = (outs[k], j) if by_layer else (outs[j], k)
+                    out[i, core, :, columns] = total[start : start + rows, source].astype(out.dtype)
+
+    tile = w_ref.shape[0]
+    wide = wide_outs[0].shape[-1]
+    whole_steps, rest = wide // tile, wide % tile
+    everything = slice(0, tile)
+
+    @pl.when(step < whole_steps)
+    def _():
+        store(wide_outs, False, pl.ds(pl.multiple_of(step * tile, tile), tile), everything)
+
+    if rest:
+
+        @pl.when(step == whole_steps)
+        def _():
+            store(wide_outs, False, slice(whole_steps * tile, wide), slice(0, rest))
+            store(narrow_outs, True, slice(0, tile - rest), slice(rest, tile))
+
+    first = whole_steps + 1 if rest else whole_steps
+    offset = tile - rest if rest else 0
+
+    @pl.when(step >= first)
+    def _():
+        columns = pl.ds(pl.multiple_of(offset + (step - first) * tile, 128), tile)
+        store(narrow_outs, True, columns, everything)
 
 
 def head_kernel(rows, *refs):
@@ -544,16 +560,11 @@
     sib_grad = shift(grad, 1)
 
     tile = half // 5
-    wide_steps = 3
-    sizes = (wide_steps * tile, half - wide_steps * tile)
-    wide_block = pl.BlockSpec(
-        (layers, CORES, rows, tile), lambda t, pos: (0, 0, 0, jnp.minimum(t, wide_steps - 1))
-    )
-    narrow_block = pl.BlockSpec(
-        (CHIPS, CORES, rows, tile), lambda t, pos: (0, 0, 0, jnp.maximum(t - wide_steps, 0))
-    )
+    sizes = (half * 7 // 10, half - half * 7 // 10)
+    wide_block = pl.BlockSpec((layers, CORES, rows, sizes[0]), lambda t, pos: (0, 0, 0, 0))
+    narrow_block = pl.BlockSpec((CHIPS, CORES, rows, sizes[1]), lambda t, pos: (0, 0, 0, 0))
     partial = pl.pallas_call(
-        functools.partial(partial_kernel, rows, wide_steps),
+        functools.partial(partial_kernel, rows),
         grid_spec=pltpu.PrefetchScalarGridSpec(
             num_scalar_prefetch=1,
             grid=(5,),
@@ -567,7 +578,7 @@
             jax.ShapeDtypeStruct((layers, CORES, rows, sizes[0]), bf16 if j else f32) for j in range(CHIPS)
         ]
         + [jax.ShapeDtypeStruct((CHIPS, CORES, rows, sizes[1]), bf16 if k else f32) for k in range(layers)],
-        compiler_params=kernel_params(LARGE_VMEM),
+        compiler_params=kernel_params(PARTIAL_VMEM),
         cost_estimate=LIGHT,
         name="grad_hidden_partial",
     )(pos, grad, sib_grad, head_weight, sib_w)

time: 138 us -> 134 us (0.971)
  waiting for transfers between devices: 29.4 us -> 33.6 us
  local copies, waits for them, and re-layouts: 17.9 us -> 14.2 us
  starting transfers between devices: 36.1 us -> 32.5 us
    ppermute x27, waiting for transfers between devices: 29.4 us -> 33.6 us  [shift(): return lax.ppermute(x, 'vocab', [(i, i ^ distance) for i in range(n)])]
    unnamed x21 -> x15, local copies, waits for them, and re-layouts: 6.66 us -> 2.96 us
    ppermute x27, starting transfers between devices: 29.9 us -> 26.3 us  [shift(): return lax.ppermute(x, 'vocab', [(i, i ^ distance) for i in range(n)])]
  transfers between devices with their start and end apart: 28 -> 28, of which waited for: 10 -> 9; matrix products, arithmetic and copies ran while one was open for 10% -> 11% of each run, Pallas kernels for 19% -> 20%
where the time goes in v14:
time: 134 us; the launch traced here: 133 us
  Pallas kernels  36.3 us (27%)
  waiting for transfers between devices  33.6 us (25%)
  starting transfers between devices  32.5 us (24%)
  local copies, waits for them, and re-layouts  14.2 us (11%)
  blocking collectives  12.9 us (10%)
  other arithmetic  2.88 us (2%)
    ppermute x27, waiting for transfers between devices, shift(): return lax.ppermute(x, 'vocab', [(i, i ^ distance) for i in range(n)])  33.6 us
    ppermute x27, starting transfers between devices, shift(): return lax.ppermute(x, 'vocab', [(i, i ^ distance) for i in range(n)])  26.3 us
    all_to_all x1, blocking collectives, levels_plan(): lax.all_to_all(stat, 'vocab', split_axis=0, concat_axis=0, tiled=True)  12.9 us
    pallas_call x1, Pallas kernels, levels_plan(): pl.pallas_call(functools.partial(logits_kernel, rows), grid=(2 * tiles,),...  11 us
    pallas_call x1, Pallas kernels, levels_plan(): pl.pallas_call(functools.partial(head_kernel, rows), grid=(4,), in_specs=...  9.96 us
    pallas_call x1, Pallas kernels, levels_plan(): pl.pallas_call(functools.partial(partial_kernel, rows), grid_spec=pltpu.P...  9.41 us
    all_to_all x1, starting transfers between devices, levels_plan(): lax.all_to_all(payload[:, :3 - STAT_ROWS], 'vocab', split_axis=0, concat_...  6.18 us
    dynamic_slice x1, local copies, waits for them, and re-layouts, levels_plan(): lax.dynamic_slice(head_weight, ((1 - core) * half, 0), (half, slab))  5.43 us
  transfers between devices with their start and end apart: 28, of which 9 were waited for; matrix products, arithmetic and copies ran while one was open for 11% of the time, Pallas kernels for 20%

profile of v14, /device:TPU:0, one launch (start us, length us, event | category | flops | bytes accessed | tf_op | source)
XLA Modules:
  0.0 133.3 jit_solution(14520671201487523838)
XLA Ops:
  0.6 4.1 %collective-permute-start.1 = (bf16[16,5120]{1,0:T(8,128)(2,1)}, bf16[16,5120]{1,0:T(8,128)(2,1)S(1)}, u32[]{:S(2)}, u32[]{:S(2)}) collective-permute-start(bf16[16,5120]{1,0:T(8,128)(2,1)} %param.7), channel_id=1, source_target_pairs={{0,16},{1,17},{2,18},{3,19},{4,20},{5,21},{6,22},{7,23},{8,24},{9,... | collective-permute-start | bytes 491528 | tf_op jit(solution)/shard_map/ppermute | solution.py:134
  4.7 1.6 %collective-permute-start = (bf16[16,5120]{1,0:T(8,128)(2,1)}, bf16[16,5120]{1,0:T(8,128)(2,1)S(1)}, u32[]{:S(2)}, u32[]{:S(2)}) collective-permute-start(bf16[16,5120]{1,0:T(8,128)(2,1)} %param.7), channel_id=1, source_target_pairs={{0,8},{1,9},{2,10},{3,11},{4,12},{5,13},{6,14},{7,15},{8,0},{9,1},... | collective-permute-start | bytes 491528 | tf_op jit(solution)/shard_map/ppermute | solution.py:134
  6.3 0.7 add_select_fusion.1
  7.0 0.1 iota_compare_fusion
  7.1 0.2 convert_reduce_fusion
  7.3 0.1 add.85
  7.4 0.1 add.82
  7.5 0.1 add.89
  7.7 0.9 copy-done.2
  8.6 1.3 pack_teacher.1
  9.9 0.9 slice.26
  10.8 6.2 %all-to-all-start = ((bf16[32,67,128]{2,1,0:T(8,128)(2,1)}), bf16[32,67,128]{2,1,0:T(8,128)(2,1)}, u32[]{:S(2)}, u32[]{:S(2)}) async-start(bf16[32,67,128]{2,1,0:T(8,128)(2,1)} %slice.26), calls=%async_computation | async-start | bytes 1179648 | tf_op jit(solution)/shard_map/all_to_all | solution.py:489
  17.0 0.9 constant_dynamic-update-slice_fusion.3
  18.1 1.8 %collective-permute-start.4 = (bf16[64,5120]{1,0:T(8,128)(2,1)S(1)}, bf16[64,5120]{1,0:T(8,128)(2,1)S(1)}, u32[]{:S(2)}, u32[]{:S(2)}) collective-permute-start(bf16[64,5120]{1,0:T(8,128)(2,1)S(1)} %constant_dynamic-update-slice_fusion.refs_0_), channel_id=1, source_target_pairs={{0,4},{1,5},{2,6},{3,7},{4,0},{5,1},{6,2},{7,3},{8,12},{9,13},{10,... | collective-permute-start | bytes 1966088 | tf_op jit(solution)/shard_map/ppermute | solution.py:134
  19.8 1.5 %collective-permute-start.3 = (bf16[64,5120]{1,0:T(8,128)(2,1)S(1)}, bf16[64,5120]{1,0:T(8,128)(2,1)S(1)}, u32[]{:S(2)}, u32[]{:S(2)}) collective-permute-start(bf16[64,5120]{1,0:T(8,128)(2,1)S(1)} %constant_dynamic-update-slice_fusion.refs_0_), channel_id=1, source_target_pairs={{0,2},{1,3},{2,0},{3,1},{4,6},{5,7},{6,4},{7,5},{8,10},{9,11},{10,... | collective-permute-start | bytes 1966088 | tf_op jit(solution)/shard_map/ppermute | solution.py:134
  21.3 0.1 pad_add_fusion.refs_0_.core_ref
  21.4 0.2 select_reduce_fusion
  21.6 5.4 %constant_dynamic-slice_fusion = bf16[2560,1024]{1,0:T(8,128)(2,1)} fusion(bf16[5120,1024]{1,0:T(8,128)(2,1)} %w_ref.1, s32[]{:T(128)S(6)} %select_n.57), kind=kLoop, calls=%fused_computation.28 | loop fusion | bytes 10485764 | tf_op jit(solution)/shard_map/dynamic_slice | solution.py:514
  27.0 13.4 %collective-permute-done.4.refs_2_ = bf16[64,5120]{1,0:T(8,128)(2,1)S(1)} collective-permute-done((bf16[64,5120]{1,0:T(8,128)(2,1)S(1)}, bf16[64,5120]{1,0:T(8,128)(2,1)S(1)}, u32[]{:S(2)}, u32[]{:S(2)}) %collective-permute-start.4) | collective-permute-done | bytes 655392 | tf_op jit(solution)/shard_map/ppermute | solution.py:134
  40.4 0.7 slice.25
  41.1 1.2 collective-permute-start.6
  42.3 0.7 slice.24
  43.0 0.4 collective-permute-start.5
  43.4 0.5 collective-permute-start.8
  43.9 1.1 slice.27
  45.0 1.1 copy.27
  46.1 0.9 convert_reduce_fusion.1
  47.0 0.1 copy.28
  47.0 0.1 copy.29
  47.2 0.1 reshape.93
  47.3 1.0 copy-done.1
  48.3 3.1 %teacher_prob.1 = (f32[512,1024]{1,0:T(8,128)S(1)}, f32[16,128]{1,0:T(8,128)S(1)}) custom-call(s32[4]{0:T(128)S(1)} %pad_add_fusion.refs_0_.core_ref, s32[4,4]{1,0:T(4,128)S(1)} %broadcast_add_fusion.1.refs_1_, bf16[4,4,128,128]{3,2,1,0:T(8,128)(2,1)S(1)} %bitcast.18, f32[2,4,1,128]{3,2,1,0:T(1,128)S(1)} %bitcast.20, s32[4,1,128]{2,1,0:T(1,128)S(1)} %bitcast.21, ...), custom_call_target="tpu_custom_call" | custom-call | flops 1 | bytes 1 | tf_op jit(solution)/shard_map/teacher_prob/pallas_call | solution.py:494
  51.4 1.2 collective-permute-done.5.refs_3_
  52.6 0.5 collective-permute-start.11
  53.1 1.3 collective-permute-done.10.refs_8_
  54.4 0.5 collective-permute-done.11.refs_9_
  54.9 0.1 collective-permute-start.13
  55.1 11.0 %logits.1 = (f32[512,1024]{1,0:T(8,128)S(1)}, f32[32,8,128]{2,1,0:T(8,128)S(1)}) custom-call(bf16[64,5120]{1,0:T(8,128)(2,1)S(1)} %constant_dynamic-update-slice_fusion.refs_0_, bf16[64,5120]{1,0:T(8,128)(2,1)S(1)} %collective-permute-done.3.refs_1_, bf16[64,5120]{1,0:T(8,128)(2,1)S(1)} %collective-permute-done.4.refs_2_, ...), custom_call_target="tpu_custom_call" | custom-call | flops 1 | bytes 1 | tf_op jit(solution)/shard_map/logits/pallas_call | solution.py:523
  66.1 12.9 %all_to_all.10.refs_1_ = f32[32,8,128]{2,1,0:T(8,128)S(1)} all-to-all(f32[32,8,128]{2,1,0:T(8,128)S(1)} %get-tuple-element.73), channel_id=1, replica_groups=mesh['vocab'=32] {'vocab'}, dimensions={0} | all-to-all | bytes 262144 | tf_op jit(solution)/shard_map/all_to_all | solution.py:546
  79.0 1.3 grad_logits.1
  80.3 0.3 collective-permute-start.12
  80.6 2.4 %collective-permute-done.12.sib_ref = bf16[512,1024]{1,0:T(8,128)(2,1)S(1)} collective-permute-done((bf16[512,1024]{1,0:T(8,128)(2,1)S(1)}, bf16[512,1024]{1,0:T(8,128)(2,1)S(1)}, u32[]{:S(2)}, u32[]{:S(2)}) %collective-permute-start.12) | collective-permute-done | bytes 1048608 | tf_op jit(solution)/shard_map/ppermute | solution.py:134
  83.0 9.4 %grad_hidden_partial.1 = (f32[4,2,16,1792]{3,2,1,0:T(8,128)S(1)}, bf16[4,2,16,1792]{3,2,1,0:T(8,128)(2,1)}, bf16[4,2,16,1792]{3,2,1,0:T(8,128)(2,1)S(1)}, bf16[4...) custom-call(s32[4]{0:T(128)S(1)} %pad_add_fusion.refs_0_.core_ref, ...), custom_call_target="tpu_custom_call" | custom-call | flops 1 | bytes 1 | tf_op jit(solution)/shard_map/grad_hidden_partial/pallas_call | solution.py:566
  92.4 0.4 collective-permute-start.14
  92.9 1.0 collective-permute-start.15
  93.8 2.1 %collective-permute-start.16 = (bf16[4,2,16,1792]{3,2,1,0:T(8,128)(2,1)S(1)}, bf16[4,2,16,1792]{3,2,1,0:T(8,128)(2,1)S(1)}, u32[]{:S(2)}, u32[]{:S(2)}) collective-permute-start(bf16[4,2,16,1792]{3,2,1,0:T(8,128)(2,1)S(1)} %get-tuple-element.89), channel_id=1, source_target_pairs={{0,6},{1,7},{2,4},{3,5},{4,2},{5,3},{6,0},{7,1},{8,14},{9,15},{10,... | collective-permute-start | bytes 1376264 | tf_op jit(solution)/shard_map/ppermute | solution.py:134
  95.9 0.7 collective-permute-start.17
  96.6 1.2 collective-permute-start.18
  97.8 7.5 %collective-permute-done.17.refs_5_ = bf16[4,2,16,768]{3,2,1,0:T(8,128)(2,1)S(1)} collective-permute-done((bf16[4,2,16,768]{3,2,1,0:T(8,128)(2,1)S(1)}, bf16[4,2,16,768]{3,2,1,0:T(8,128)(2,1)S(1)}, u32[]{:S(2)}, u32[]{:S(2)}) %collective-permute-start.17) | collective-permute-done | bytes 196640 | tf_op jit(solution)/shard_map/ppermute | solution.py:134
  105.3 1.8 %collective-permute-start.19 = (bf16[4,2,16,768]{3,2,1,0:T(8,128)(2,1)S(1)}, bf16[4,2,16,768]{3,2,1,0:T(8,128)(2,1)S(1)}, u32[]{:S(2)}, u32[]{:S(2)}) collective-permute-start(bf16[4,2,16,768]{3,2,1,0:T(8,128)(2,1)S(1)} %get-tuple-element.92), channel_id=1, source_target_pairs={{0,24},{1,25},{2,26},{3,27},{4,28},{5,29},{6,30},{7,31},{8,16},{9,... | collective-permute-start | bytes 589832 | tf_op jit(solution)/shard_map/ppermute | solution.py:134
  107.1 10.0 %grad_head.1 = bf16[5120,1024]{1,0:T(8,128)(2,1)} custom-call(bf16[64,5120]{1,0:T(8,128)(2,1)S(1)} %constant_dynamic-update-slice_fusion.refs_0_, bf16[64,5120]{1,0:T(8,128)(2,1)S(1)} %collective-permute-done.3.refs_1_, bf16[64,5120]{1,0:T(8,128)(2,1)S(1)} %collective-permute-done.4.refs_2_, bf16[64,2560]{1,0:T(8,128)(2,1)} %collective-permute-done.5.refs_3_, ...), custom_call_target="tpu_custom_call" | custom-call | flops 1 | bytes 1 | tf_op jit(solution)/shard_map/grad_head/pallas_call | solution.py:590
  117.1 0.3 first_sum.1
  117.4 0.1 collective-permute-start.20
  117.5 2.5 %collective-permute-start.21 = (bf16[2,16,1792]{2,1,0:T(8,128)(2,1)S(1)}, bf16[2,16,1792]{2,1,0:T(8,128)(2,1)S(1)}, u32[]{:S(2)}, u32[]{:S(2)}) collective-permute-start(bf16[2,16,1792]{2,1,0:T(8,128)(2,1)S(1)} %get-tuple-element.105), channel_id=1, source_target_pairs={{0,16},{1,17},{2,18},{3,19},{4,20},{5,21},{6,22},{7,23},{8,24},{9,... | collective-permute-start | bytes 344072 | tf_op jit(solution)/shard_map/ppermute | solution.py:134
  120.0 1.8 %collective-permute-start.22 = (bf16[2,16,1792]{2,1,0:T(8,128)(2,1)S(1)}, bf16[2,16,1792]{2,1,0:T(8,128)(2,1)S(1)}, u32[]{:S(2)}, u32[]{:S(2)}) collective-permute-start(bf16[2,16,1792]{2,1,0:T(8,128)(2,1)S(1)} %get-tuple-element.106), channel_id=1, source_target_pairs={{0,24},{1,25},{2,26},{3,27},{4,28},{5,29},{6,30},{7,31},{8,16},{9,... | collective-permute-start | bytes 344072 | tf_op jit(solution)/shard_map/ppermute | solution.py:134
  121.9 0.5 collective-permute-start.23
  122.4 1.2 collective-permute-start.24
  123.6 2.6 %collective-permute-done.23.refs_5_ = bf16[2,16,768]{2,1,0:T(8,128)(2,1)S(1)} collective-permute-done((bf16[2,16,768]{2,1,0:T(8,128)(2,1)S(1)}, bf16[2,16,768]{2,1,0:T(8,128)(2,1)S(1)}, u32[]{:S(2)}, u32[]{:S(2)}) %collective-permute-start.23) | collective-permute-done | bytes 49184 | tf_op jit(solution)/shard_map/ppermute | solution.py:134
  126.2 1.0 collective-permute-start.25
  127.1 4.0 %collective-permute-done.25.refs_7_ = bf16[2,16,768]{2,1,0:T(8,128)(2,1)S(1)} collective-permute-done((bf16[2,16,768]{2,1,0:T(8,128)(2,1)S(1)}, bf16[2,16,768]{2,1,0:T(8,128)(2,1)S(1)}, u32[]{:S(2)}, u32[]{:S(2)}) %collective-permute-start.25) | collective-permute-done | bytes 49184 | tf_op jit(solution)/shard_map/ppermute | solution.py:134
  131.2 0.1 last_sum.1
  131.3 0.6 slice_reduce_fusion
  132.0 0.6 collective-permute-done.26
  132.6 0.7 pad_maximum_fusion
  (44 shorter events, 0.2 us)
Async XLA Ops:
  0.6 17.4 %collective-permute-start.1 = (bf16[16,5120]{1,0:T(8,128)(2,1)}, bf16[16,5120]{1,0:T(8,128)(2,1)S(1)}, u32[]{:S(2)}, u32[]{:S(2)}) collective-permute-start(bf16[16,5120]{1,0:T(8,128)(2,1)} %param.7), channel_id=1, source_target_pairs={{0,16},{1,17},{2,18},{3,19},{4,20},{5,21},{6,22},{7,23},{8,24},{9,... | collective-permute-start | bytes 491528 | tf_op jit(solution)/shard_map/ppermute | solution.py:134
  4.7 13.2 %collective-permute-start = (bf16[16,5120]{1,0:T(8,128)(2,1)}, bf16[16,5120]{1,0:T(8,128)(2,1)S(1)}, u32[]{:S(2)}, u32[]{:S(2)}) collective-permute-start(bf16[16,5120]{1,0:T(8,128)(2,1)} %param.7), channel_id=1, source_target_pairs={{0,8},{1,9},{2,10},{3,11},{4,12},{5,13},{6,14},{7,15},{8,0},{9,1},... | collective-permute-start | bytes 491528 | tf_op jit(solution)/shard_map/ppermute | solution.py:134
  6.3 11.7 %collective-permute-start.2 = (bf16[16,5120]{1,0:T(8,128)(2,1)}, bf16[16,5120]{1,0:T(8,128)(2,1)S(1)}, u32[]{:S(2)}, u32[]{:S(2)}) collective-permute-start(bf16[16,5120]{1,0:T(8,128)(2,1)} %param.7), channel_id=1, source_target_pairs={{0,24},{1,25},{2,26},{3,27},{4,28},{5,29},{6,30},{7,31},{8,16},{9,... | collective-permute-start | bytes 491528 | tf_op jit(solution)/shard_map/ppermute | solution.py:134
  7.7 1.0 copy-start.2
  10.8 33.1 %all-to-all-start = ((bf16[32,67,128]{2,1,0:T(8,128)(2,1)}), bf16[32,67,128]{2,1,0:T(8,128)(2,1)}, u32[]{:S(2)}, u32[]{:S(2)}) async-start(bf16[32,67,128]{2,1,0:T(8,128)(2,1)} %slice.26), calls=%async_computation | async-start | bytes 1179648 | tf_op jit(solution)/shard_map/all_to_all | solution.py:489
  18.1 22.3 %collective-permute-start.4 = (bf16[64,5120]{1,0:T(8,128)(2,1)S(1)}, bf16[64,5120]{1,0:T(8,128)(2,1)S(1)}, u32[]{:S(2)}, u32[]{:S(2)}) collective-permute-start(bf16[64,5120]{1,0:T(8,128)(2,1)S(1)} %constant_dynamic-update-slice_fusion.refs_0_), channel_id=1, source_target_pairs={{0,4},{1,5},{2,6},{3,7},{4,0},{5,1},{6,2},{7,3},{8,12},{9,13},{10,... | collective-permute-start | bytes 1966088 | tf_op jit(solution)/shard_map/ppermute | solution.py:134
  19.8 22.5 %collective-permute-start.3 = (bf16[64,5120]{1,0:T(8,128)(2,1)S(1)}, bf16[64,5120]{1,0:T(8,128)(2,1)S(1)}, u32[]{:S(2)}, u32[]{:S(2)}) collective-permute-start(bf16[64,5120]{1,0:T(8,128)(2,1)S(1)} %constant_dynamic-update-slice_fusion.refs_0_), channel_id=1, source_target_pairs={{0,2},{1,3},{2,0},{3,1},{4,6},{5,7},{6,4},{7,5},{8,10},{9,11},{10,... | collective-permute-start | bytes 1966088 | tf_op jit(solution)/shard_map/ppermute | solution.py:134
  21.6 25.7 %copy-start.3 = (s32[4,128]{1,0:T(4,128)S(1)}, s32[4,128]{1,0:T(4,128)}, u32[]{:S(2)}) copy-start(s32[4,128]{1,0:T(4,128)} %param.11) | copy-start | bytes 6148
  21.6 25.7 %copy-start.4 = (f32[512]{0:T(512)S(1)}, f32[512]{0:T(512)}, u32[]{:S(2)}) copy-start(f32[512]{0:T(512)} %param.12) | copy-start | bytes 6148
  27.0 26.1 %collective-permute-start.7 = (bf16[64,5120]{1,0:T(8,128)(2,1)S(1)}, bf16[64,5120]{1,0:T(8,128)(2,1)S(1)}, u32[]{:S(2)}, u32[]{:S(2)}) collective-permute-start(bf16[64,5120]{1,0:T(8,128)(2,1)S(1)} %constant_dynamic-update-slice_fusion.refs_0_), channel_id=1, source_target_pairs={{0,1},{1,0},{2,3},{3,2},{4,5},{5,4},{6,7},{7,6},{8,9},{9,8},{10,11... | collective-permute-start | bytes 1966088 | tf_op jit(solution)/shard_map/ppermute | solution.py:134
  41.1 10.3 %collective-permute-start.6 = (bf16[64,2560]{1,0:T(8,128)(2,1)}, bf16[64,2560]{1,0:T(8,128)(2,1)}, u32[]{:S(2)}, u32[]{:S(2)}) collective-permute-start(bf16[64,2560]{1,0:T(8,128)(2,1)} %slice.25), channel_id=1, source_target_pairs={{0,2},{1,3},{2,0},{3,1},{4,6},{5,7},{6,4},{7,5},{8,10},{9,11},{10,... | collective-permute-start | bytes 983048 | tf_op jit(solution)/shard_map/ppermute | solution.py:134
  43.0 9.6 %collective-permute-start.5 = (bf16[64,2560]{1,0:T(8,128)(2,1)}, bf16[64,2560]{1,0:T(8,128)(2,1)}, u32[]{:S(2)}, u32[]{:S(2)}) collective-permute-start(bf16[64,2560]{1,0:T(8,128)(2,1)} %slice.24), channel_id=1, source_target_pairs={{0,4},{1,5},{2,6},{3,7},{4,0},{5,1},{6,2},{7,3},{8,12},{9,13},{10,... | collective-permute-start | bytes 983048 | tf_op jit(solution)/shard_map/ppermute | solution.py:134
  43.4 11.5 %collective-permute-start.9 = (bf16[64,5120]{1,0:T(8,128)(2,1)S(1)}, bf16[64,5120]{1,0:T(8,128)(2,1)S(1)}, u32[]{:S(2)}, u32[]{:S(2)}) collective-permute-start(bf16[64,5120]{1,0:T(8,128)(2,1)S(1)} %collective-permute-done.4.refs_2_), channel_id=1, source_target_pairs={{0,1},{1,0},{2,3},{3,2},{4,5},{5,4},{6,7},{7,6},{8,9},{9,8},{10,11... | collective-permute-start | bytes 1966088 | tf_op jit(solution)/shard_map/ppermute | solution.py:134
  43.4 11.5 %collective-permute-start.8 = (bf16[64,5120]{1,0:T(8,128)(2,1)S(1)}, bf16[64,5120]{1,0:T(8,128)(2,1)}, u32[]{:S(2)}, u32[]{:S(2)}) collective-permute-start(bf16[64,5120]{1,0:T(8,128)(2,1)S(1)} %collective-permute-done.3.refs_1_), channel_id=1, source_target_pairs={{0,1},{1,0},{2,3},{3,2},{4,5},{5,4},{6,7},{7,6},{8,9},{9,8},{10,11... | collective-permute-start | bytes 1966088 | tf_op jit(solution)/shard_map/ppermute | solution.py:134
  47.3 1.0 copy-start.1
  52.6 26.4 %copy-start.5 = (f32[512]{0:T(512)S(1)}, f32[512]{0:T(512)}, u32[]{:S(2)}) copy-start(f32[512]{0:T(512)} %param.13) | copy-start | bytes 6148
  52.6 1.8 %collective-permute-start.10 = (bf16[64,2560]{1,0:T(8,128)(2,1)}, bf16[64,2560]{1,0:T(8,128)(2,1)S(1)}, u32[]{:S(2)}, u32[]{:S(2)}) collective-permute-start(bf16[64,2560]{1,0:T(8,128)(2,1)} %collective-permute-done.5.refs_3_), channel_id=1, source_target_pairs={{0,1},{1,0},{2,3},{3,2},{4,5},{5,4},{6,7},{7,6},{8,9},{9,8},{10,11... | collective-permute-start | bytes 983048 | tf_op jit(solution)/shard_map/ppermute | solution.py:134
  52.6 2.3 %collective-permute-start.11 = (bf16[64,2560]{1,0:T(8,128)(2,1)}, bf16[64,2560]{1,0:T(8,128)(2,1)S(1)}, u32[]{:S(2)}, u32[]{:S(2)}) collective-permute-start(bf16[64,2560]{1,0:T(8,128)(2,1)} %collective-permute-done.6.refs_4_), channel_id=1, source_target_pairs={{0,1},{1,0},{2,3},{3,2},{4,5},{5,4},{6,7},{7,6},{8,9},{9,8},{10,11... | collective-permute-start | bytes 983048 | tf_op jit(solution)/shard_map/ppermute | solution.py:134
  54.9 28.1 %collective-permute-start.13 = (bf16[2560,1024]{1,0:T(8,128)(2,1)}, bf16[2560,1024]{1,0:T(8,128)(2,1)S(1)}, u32[]{:S(2)}, u32[]{:S(2)}) collective-permute-start(bf16[2560,1024]{1,0:T(8,128)(2,1)} %constant_dynamic-slice_fusion), channel_id=1, source_target_pairs={{0,1},{1,0},{2,3},{3,2},{4,5},{5,4},{6,7},{7,6},{8,9},{9,8},{10,11... | collective-permute-start | bytes 15728648 | tf_op jit(solution)/shard_map/ppermute | solution.py:134
  80.3 12.2 %copy-start = (bf16[512,1024]{1,0:T(8,128)(2,1)}, bf16[512,1024]{1,0:T(8,128)(2,1)S(1)}, u32[]{:S(2)}) copy-start(bf16[512,1024]{1,0:T(8,128)(2,1)S(1)} %get-tuple-element.93.grad_ref.refs_10_) | copy-start | bytes 3145732
  80.3 2.7 %collective-permute-start.12 = (bf16[512,1024]{1,0:T(8,128)(2,1)S(1)}, bf16[512,1024]{1,0:T(8,128)(2,1)S(1)}, u32[]{:S(2)}, u32[]{:S(2)}) collective-permute-start(bf16[512,1024]{1,0:T(8,128)(2,1)S(1)} %get-tuple-element.93.grad_ref.refs_10_), channel_id=1, source_target_pairs={{0,1},{1,0},{2,3},{3,2},{4,5},{5,4},{6,7},{7,6},{8,9},{9,8},{10,11... | collective-permute-start | bytes 3145736 | tf_op jit(solution)/shard_map/ppermute | solution.py:134
  92.4 24.7 %collective-permute-start.14 = (bf16[4,2,16,1792]{3,2,1,0:T(8,128)(2,1)}, bf16[4,2,16,1792]{3,2,1,0:T(8,128)(2,1)S(1)}, u32[]{:S(2)}, u32[]{:S(2)}) collective-permute-start(bf16[4,2,16,1792]{3,2,1,0:T(8,128)(2,1)} %get-tuple-element.87), channel_id=1, source_target_pairs={{0,2},{1,3},{2,0},{3,1},{4,6},{5,7},{6,4},{7,5},{8,10},{9,11},{10,... | collective-permute-start | bytes 1376264 | tf_op jit(solution)/shard_map/ppermute | solution.py:134
  92.9 24.3 %collective-permute-start.15 = (bf16[4,2,16,1792]{3,2,1,0:T(8,128)(2,1)S(1)}, bf16[4,2,16,1792]{3,2,1,0:T(8,128)(2,1)S(1)}, u32[]{:S(2)}, u32[]{:S(2)}) collective-permute-start(bf16[4,2,16,1792]{3,2,1,0:T(8,128)(2,1)S(1)} %get-tuple-element.88), channel_id=1, source_target_pairs={{0,4},{1,5},{2,6},{3,7},{4,0},{5,1},{6,2},{7,3},{8,12},{9,13},{10,... | collective-permute-start | bytes 1376264 | tf_op jit(solution)/shard_map/ppermute | solution.py:134
  93.8 23.3 %collective-permute-start.16 = (bf16[4,2,16,1792]{3,2,1,0:T(8,128)(2,1)S(1)}, bf16[4,2,16,1792]{3,2,1,0:T(8,128)(2,1)S(1)}, u32[]{:S(2)}, u32[]{:S(2)}) collective-permute-start(bf16[4,2,16,1792]{3,2,1,0:T(8,128)(2,1)S(1)} %get-tuple-element.89), channel_id=1, source_target_pairs={{0,6},{1,7},{2,4},{3,5},{4,2},{5,3},{6,0},{7,1},{8,14},{9,15},{10,... | collective-permute-start | bytes 1376264 | tf_op jit(solution)/shard_map/ppermute | solution.py:134
  95.9 9.4 %collective-permute-start.17 = (bf16[4,2,16,768]{3,2,1,0:T(8,128)(2,1)S(1)}, bf16[4,2,16,768]{3,2,1,0:T(8,128)(2,1)S(1)}, u32[]{:S(2)}, u32[]{:S(2)}) collective-permute-start(bf16[4,2,16,768]{3,2,1,0:T(8,128)(2,1)S(1)} %get-tuple-element.90), channel_id=1, source_target_pairs={{0,8},{1,9},{2,10},{3,11},{4,12},{5,13},{6,14},{7,15},{8,0},{9,1},... | collective-permute-start | bytes 589832 | tf_op jit(solution)/shard_map/ppermute | solution.py:134
  96.6 20.6 %collective-permute-start.18 = (bf16[4,2,16,768]{3,2,1,0:T(8,128)(2,1)S(1)}, bf16[4,2,16,768]{3,2,1,0:T(8,128)(2,1)S(1)}, u32[]{:S(2)}, u32[]{:S(2)}) collective-permute-start(bf16[4,2,16,768]{3,2,1,0:T(8,128)(2,1)S(1)} %get-tuple-element.91), channel_id=1, source_target_pairs={{0,16},{1,17},{2,18},{3,19},{4,20},{5,21},{6,22},{7,23},{8,24},{9,... | collective-permute-start | bytes 589832 | tf_op jit(solution)/shard_map/ppermute | solution.py:134
  105.3 11.8 %collective-permute-start.19 = (bf16[4,2,16,768]{3,2,1,0:T(8,128)(2,1)S(1)}, bf16[4,2,16,768]{3,2,1,0:T(8,128)(2,1)S(1)}, u32[]{:S(2)}, u32[]{:S(2)}) collective-permute-start(bf16[4,2,16,768]{3,2,1,0:T(8,128)(2,1)S(1)} %get-tuple-element.92), channel_id=1, source_target_pairs={{0,24},{1,25},{2,26},{3,27},{4,28},{5,29},{6,30},{7,31},{8,16},{9,... | collective-permute-start | bytes 589832 | tf_op jit(solution)/shard_map/ppermute | solution.py:134
  117.4 13.7 %collective-permute-start.20 = (bf16[2,16,1792]{2,1,0:T(8,128)(2,1)S(1)}, bf16[2,16,1792]{2,1,0:T(8,128)(2,1)S(1)}, u32[]{:S(2)}, u32[]{:S(2)}) collective-permute-start(bf16[2,16,1792]{2,1,0:T(8,128)(2,1)S(1)} %get-tuple-element.104), channel_id=1, source_target_pairs={{0,8},{1,9},{2,10},{3,11},{4,12},{5,13},{6,14},{7,15},{8,0},{9,1},... | collective-permute-start | bytes 344072 | tf_op jit(solution)/shard_map/ppermute | solution.py:134
  117.5 13.7 %collective-permute-start.21 = (bf16[2,16,1792]{2,1,0:T(8,128)(2,1)S(1)}, bf16[2,16,1792]{2,1,0:T(8,128)(2,1)S(1)}, u32[]{:S(2)}, u32[]{:S(2)}) collective-permute-start(bf16[2,16,1792]{2,1,0:T(8,128)(2,1)S(1)} %get-tuple-element.105), channel_id=1, source_target_pairs={{0,16},{1,17},{2,18},{3,19},{4,20},{5,21},{6,22},{7,23},{8,24},{9,... | collective-permute-start | bytes 344072 | tf_op jit(solution)/shard_map/ppermute | solution.py:134
  120.0 11.1 %collective-permute-start.22 = (bf16[2,16,1792]{2,1,0:T(8,128)(2,1)S(1)}, bf16[2,16,1792]{2,1,0:T(8,128)(2,1)S(1)}, u32[]{:S(2)}, u32[]{:S(2)}) collective-permute-start(bf16[2,16,1792]{2,1,0:T(8,128)(2,1)S(1)} %get-tuple-element.106), channel_id=1, source_target_pairs={{0,24},{1,25},{2,26},{3,27},{4,28},{5,29},{6,30},{7,31},{8,16},{9,... | collective-permute-start | bytes 344072 | tf_op jit(solution)/shard_map/ppermute | solution.py:134
  121.9 4.3 %collective-permute-start.23 = (bf16[2,16,768]{2,1,0:T(8,128)(2,1)S(1)}, bf16[2,16,768]{2,1,0:T(8,128)(2,1)S(1)}, u32[]{:S(2)}, u32[]{:S(2)}) collective-permute-start(bf16[2,16,768]{2,1,0:T(8,128)(2,1)S(1)} %get-tuple-element.108), channel_id=1, source_target_pairs={{0,2},{1,3},{2,0},{3,1},{4,6},{5,7},{6,4},{7,5},{8,10},{9,11},{10,... | collective-permute-start | bytes 147464 | tf_op jit(solution)/shard_map/ppermute | solution.py:134
  122.4 4.8 %collective-permute-start.24 = (bf16[2,16,768]{2,1,0:T(8,128)(2,1)S(1)}, bf16[2,16,768]{2,1,0:T(8,128)(2,1)S(1)}, u32[]{:S(2)}, u32[]{:S(2)}) collective-permute-start(bf16[2,16,768]{2,1,0:T(8,128)(2,1)S(1)} %get-tuple-element.109), channel_id=1, source_target_pairs={{0,4},{1,5},{2,6},{3,7},{4,0},{5,1},{6,2},{7,3},{8,12},{9,13},{10,... | collective-permute-start | bytes 147464 | tf_op jit(solution)/shard_map/ppermute | solution.py:134
  126.2 5.0 %collective-permute-start.25 = (bf16[2,16,768]{2,1,0:T(8,128)(2,1)S(1)}, bf16[2,16,768]{2,1,0:T(8,128)(2,1)S(1)}, u32[]{:S(2)}, u32[]{:S(2)}) collective-permute-start(bf16[2,16,768]{2,1,0:T(8,128)(2,1)S(1)} %get-tuple-element.110), channel_id=1, source_target_pairs={{0,6},{1,7},{2,4},{3,5},{4,2},{5,3},{6,0},{7,1},{8,14},{9,15},{10,... | collective-permute-start | bytes 147464 | tf_op jit(solution)/shard_map/ppermute | solution.py:134
  131.3 1.3 %collective-permute-start.26 = (bf16[16,2560]{1,0:T(8,128)(2,1)S(1)}, bf16[16,2560]{1,0:T(8,128)(2,1)S(1)}, u32[]{:S(2)}, u32[]{:S(2)}) collective-permute-start(bf16[16,2560]{1,0:T(8,128)(2,1)S(1)} %get-tuple-element.112), channel_id=1, source_target_pairs={{0,1},{1,0},{2,3},{3,2},{4,5},{5,4},{6,7},{7,6},{8,9},{9,8},{10,11... | collective-permute-start | bytes 245768 | tf_op jit(solution)/shard_map/ppermute | solution.py:134

commit v15 on v14

--- a/solution.py
+++ b/solution.py
@@ -147,25 +147,37 @@
 
 
 def teacher_kernel(
-    unlisted, rows, pos_ref, place_ref, blocks_ref, stat_ref, reader_ref, tail_ref, prob_ref, entropy_ref
+    unlisted, rows, pos_ref, place_ref, arrived_ref, reader_ref, tail_ref, prob_ref, entropy_ref
 ):
-    layers, slots, side, _ = blocks_ref.shape
+    devices, size, side = arrived_ref.shape
+    blocks = reader_ref.shape[0]
+    stored = side // devices
+    per_block = SLOTS * stored
+    layers = blocks
     pos = [pos_ref[i] for i in range(3)]
     lane = lax.broadcasted_iota(jnp.int32, (1, side), 1)
+    sender_lane = lax.broadcasted_iota(jnp.int32, (1, devices), 1)
+    row_lane = lax.broadcasted_iota(jnp.int32, (1, devices * per_block), 1)
     where_token = token_places(pos, rows, side)
+    parts = [arrived_ref[:, size - 3 + i, :] for i in range(3)]
     for k in range(layers):
         block = pos[2] ^ k
-        match = reader_ref[block] == where_token
-        onehot = jnp.where(match, 1.0, 0.0).astype(jnp.bfloat16)
-        normaliser = pick_column(match, stat_ref[0, block])
+        stored_row = jnp.sum(jnp.where(reader_ref[block] == where_token, lane, 0), axis=1, keepdims=True)
+        sender, row = stored_row // stored, stored_row % stored
+        from_sender = jnp.where(sender_lane == sender, 1.0, 0.0).astype(jnp.bfloat16)
+        stat = sum(jnp.dot(from_sender, part, preferred_element_type=jnp.float32) for part in parts)
+        normaliser = pick_column(lane == block * stored + row, stat)
         tail = pick_column(lane == where_token, tail_ref[block])
         kept = 1.0 - tail
         rest = tail / unlisted
         span = pl.ds(k * side, side)
         prob_ref[span, :] = jnp.broadcast_to(rest, (side, prob_ref.shape[1]))
-        for s in range(slots):
+        all_rows = arrived_ref[:, pl.ds(pl.multiple_of(block * per_block, per_block), per_block), :]
+        all_rows = all_rows.reshape(devices * per_block, side)
+        for s in range(SLOTS):
             place = place_ref[block, s]
-            values = jnp.dot(onehot, blocks_ref[block, s], preferred_element_type=jnp.float32)
+            onehot = jnp.where(row_lane == sender * per_block + s * stored + row, 1.0, 0.0)
+            values = jnp.dot(onehot.astype(jnp.bfloat16), all_rows, preferred_element_type=jnp.float32)
             prob = kept * jnp.exp(values - normaliser)
 
             @pl.when(place >= 0)
@@ -173,7 +185,7 @@
                 prob_ref[span, pl.ds(pl.multiple_of(place * side, side), side)] = prob
 
         if k == 0:
-            mean = pick_column(match, stat_ref[1, block])
+            mean = pick_column(lane == (blocks + block) * stored + row, stat)
             entropy = kept * (jnp.log(kept) - normaliser + mean) + tail * jnp.log(rest)
             entropy_ref[...] = jnp.broadcast_to(entropy[:rows], entropy_ref.shape)
 
@@ -445,25 +457,6 @@
     return payload, place.astype(jnp.int32)
 
 
-def unpack_teacher(arrived, blocks, stored):
-    n, _, side = arrived.shape
-    arrived_blocks = (
-        arrived[:, :-3]
-        .reshape(n, blocks, SLOTS, stored, side)
-        .transpose(1, 2, 0, 3, 4)
-        .reshape(blocks, SLOTS, n * stored, side)
-    )
-    arrived_stat = (
-        arrived[:, -3:, : 2 * blocks * stored]
-        .astype(jnp.float32)
-        .sum(axis=1)
-        .reshape(n, 2, blocks, stored)
-        .transpose(1, 2, 0, 3)
-        .reshape(2, blocks, 1, n * stored)
-    )
-    return arrived_blocks, arrived_stat
-
-
 def levels_plan(
     hidden_states, head_weight, teacher_logits, block_lists, row_reader, tail_mass, token_weight
 ):
@@ -489,7 +482,6 @@
     arrived = lax.all_to_all(
         payload[:, : 3 - STAT_ROWS], "vocab", split_axis=0, concat_axis=0, tiled=True
     )
-    arrived_blocks, arrived_stat = unpack_teacher(arrived, blocks, stored)
 
     prob, entropy = pl.pallas_call(
         lambda *refs: teacher_kernel(unlisted, rows, *refs),
@@ -497,7 +489,7 @@
             jax.ShapeDtypeStruct((tokens, slab), f32),
             jax.ShapeDtypeStruct((rows, side), f32),
         ),
-        in_specs=[smem_spec(), smem_spec()] + [vmem_spec()] * 4,
+        in_specs=[smem_spec(), smem_spec()] + [vmem_spec()] * 3,
         out_specs=(vmem_spec(), vmem_spec()),
         compiler_params=kernel_params(),
         cost_estimate=LIGHT,
@@ -505,8 +497,7 @@
     )(
         pos,
         place,
-        arrived_blocks,
-        arrived_stat,
+        arrived,
         row_reader.reshape(blocks, 1, side),
         tail_mass.reshape(blocks, 1, side),
     )

time: 134 us -> 133 us (level)
  local copies, waits for them, and re-layouts: 14.2 us -> 10.7 us
  waiting for transfers between devices: 33.6 us -> 36.1 us
  Pallas kernels: 36.3 us -> 38.2 us
    ppermute x27, waiting for transfers between devices: 33.6 us -> 36.1 us  [shift(): return lax.ppermute(x, 'vocab', [(i, i ^ distance) for i in range(n)])]
    pallas_call x1, Pallas kernels: 3.05 us -> 4.93 us  [levels_plan(): pl.pallas_call(lambda *refs: teacher_kernel(unlisted, rows, *refs), out_s...]
    unnamed x15 -> x13, local copies, waits for them, and re-layouts: 2.96 us -> 1.92 us
  transfers between devices with their start and end apart: 28 -> 28, of which waited for: 9 -> 10; matrix products, arithmetic and copies ran while one was open for 11% -> 8% of each run, Pallas kernels for 20% -> 21%
where the time goes in v15:
time: 133 us
  Pallas kernels  38.2 us (29%)
  waiting for transfers between devices  36.1 us (27%)
  starting transfers between devices  32.5 us (24%)
  blocking collectives  12.6 us (9%)
  local copies, waits for them, and re-layouts  10.7 us (8%)
  other arithmetic  2 us (2%)
    ppermute x27, waiting for transfers between devices, shift(): return lax.ppermute(x, 'vocab', [(i, i ^ distance) for i in range(n)])  36.1 us
    ppermute x27, starting transfers between devices, shift(): return lax.ppermute(x, 'vocab', [(i, i ^ distance) for i in range(n)])  26.3 us
    all_to_all x1, blocking collectives, levels_plan(): lax.all_to_all(stat, 'vocab', split_axis=0, concat_axis=0, tiled=True)  12.6 us
    pallas_call x1, Pallas kernels, levels_plan(): pl.pallas_call(functools.partial(logits_kernel, rows), grid=(2 * tiles,),...  11 us
    pallas_call x1, Pallas kernels, levels_plan(): pl.pallas_call(functools.partial(head_kernel, rows), grid=(4,), in_specs=...  9.96 us
    pallas_call x1, Pallas kernels, levels_plan(): pl.pallas_call(functools.partial(partial_kernel, rows), grid_spec=pltpu.P...  9.38 us
    all_to_all x1, starting transfers between devices, levels_plan(): lax.all_to_all(payload[:, :3 - STAT_ROWS], 'vocab', split_axis=0, concat_...  6.18 us
    dynamic_slice x1, local copies, waits for them, and re-layouts, levels_plan(): lax.dynamic_slice(head_weight, ((1 - core) * half, 0), (half, slab))  5.43 us
  transfers between devices with their start and end apart: 28, of which 10 were waited for; matrix products, arithmetic and copies ran while one was open for 8% of the time, Pallas kernels for 21%

profile of v15, /device:TPU:0, one launch (start us, length us, event | category | flops | bytes accessed | tf_op | source)
XLA Modules:
  0.0 132.9 jit_solution(6241260502510794558)
XLA Ops:
  0.6 4.1 %collective-permute-start.1 = (bf16[16,5120]{1,0:T(8,128)(2,1)}, bf16[16,5120]{1,0:T(8,128)(2,1)S(1)}, u32[]{:S(2)}, u32[]{:S(2)}) collective-permute-start(bf16[16,5120]{1,0:T(8,128)(2,1)} %param.7), channel_id=1, source_target_pairs={{0,16},{1,17},{2,18},{3,19},{4,20},{5,21},{6,22},{7,23},{8,24},{9,... | collective-permute-start | bytes 491528 | tf_op jit(solution)/shard_map/ppermute | solution.py:134
  4.7 1.6 %collective-permute-start = (bf16[16,5120]{1,0:T(8,128)(2,1)}, bf16[16,5120]{1,0:T(8,128)(2,1)S(1)}, u32[]{:S(2)}, u32[]{:S(2)}) collective-permute-start(bf16[16,5120]{1,0:T(8,128)(2,1)} %param.7), channel_id=1, source_target_pairs={{0,8},{1,9},{2,10},{3,11},{4,12},{5,13},{6,14},{7,15},{8,0},{9,1},... | collective-permute-start | bytes 491528 | tf_op jit(solution)/shard_map/ppermute | solution.py:134
  6.3 0.7 add_select_fusion.1
  7.0 0.1 iota_compare_fusion
  7.1 0.2 convert_reduce_fusion
  7.3 0.1 add.85
  7.4 0.1 add.82
  7.5 0.1 add.89
  7.7 0.0 copy-start.1
  7.7 0.9 copy-done.1
  8.6 1.3 pack_teacher.1
  9.9 0.9 slice.18
  10.8 6.2 %all-to-all-start = ((bf16[32,67,128]{2,1,0:T(8,128)(2,1)}), bf16[32,67,128]{2,1,0:T(8,128)(2,1)}, u32[]{:S(2)}, u32[]{:S(2)}) async-start(bf16[32,67,128]{2,1,0:T(8,128)(2,1)} %slice.18), calls=%async_computation | async-start | bytes 1179648 | tf_op jit(solution)/shard_map/all_to_all | solution.py:482
  17.0 0.9 constant_dynamic-update-slice_fusion.3
  17.9 0.0 collective-permute-done
  17.9 0.0 collective-permute-done.1
  18.0 1.8 %collective-permute-start.4 = (bf16[64,5120]{1,0:T(8,128)(2,1)S(1)}, bf16[64,5120]{1,0:T(8,128)(2,1)S(1)}, u32[]{:S(2)}, u32[]{:S(2)}) collective-permute-start(bf16[64,5120]{1,0:T(8,128)(2,1)S(1)} %constant_dynamic-update-slice_fusion.refs_0_), channel_id=1, source_target_pairs={{0,4},{1,5},{2,6},{3,7},{4,0},{5,1},{6,2},{7,3},{8,12},{9,13},{10,... | collective-permute-start | bytes 1966088 | tf_op jit(solution)/shard_map/ppermute | solution.py:134
  19.8 1.5 %collective-permute-start.3 = (bf16[64,5120]{1,0:T(8,128)(2,1)S(1)}, bf16[64,5120]{1,0:T(8,128)(2,1)S(1)}, u32[]{:S(2)}, u32[]{:S(2)}) collective-permute-start(bf16[64,5120]{1,0:T(8,128)(2,1)S(1)} %constant_dynamic-update-slice_fusion.refs_0_), channel_id=1, source_target_pairs={{0,2},{1,3},{2,0},{3,1},{4,6},{5,7},{6,4},{7,5},{8,10},{9,11},{10,... | collective-permute-start | bytes 1966088 | tf_op jit(solution)/shard_map/ppermute | solution.py:134
  21.2 0.2 select_reduce_fusion
  21.5 0.0 copy-start.2
  21.5 0.0 copy-start.3
  21.5 5.4 %constant_dynamic-slice_fusion = bf16[2560,1024]{1,0:T(8,128)(2,1)} fusion(bf16[5120,1024]{1,0:T(8,128)(2,1)} %w_ref.1, s32[]{:T(128)S(6)} %select_n.57), kind=kLoop, calls=%fused_computation.27 | loop fusion | bytes 10485764 | tf_op jit(solution)/shard_map/dynamic_slice | solution.py:505
  26.9 13.5 %collective-permute-done.4.refs_2_ = bf16[64,5120]{1,0:T(8,128)(2,1)S(1)} collective-permute-done((bf16[64,5120]{1,0:T(8,128)(2,1)S(1)}, bf16[64,5120]{1,0:T(8,128)(2,1)S(1)}, u32[]{:S(2)}, u32[]{:S(2)}) %collective-permute-start.4) | collective-permute-done | bytes 655392 | tf_op jit(solution)/shard_map/ppermute | solution.py:134
  40.4 0.8 slice.17
  41.2 1.2 collective-permute-start.6
  42.3 0.8 slice.16
  43.1 0.4 collective-permute-start.5
  43.5 0.5 collective-permute-start.8
  44.0 0.1 pad_add_fusion.refs_0_.core_ref
  44.1 4.9 %teacher_prob.1 = (f32[512,1024]{1,0:T(8,128)S(1)}, f32[16,128]{1,0:T(8,128)S(1)}) custom-call(s32[4]{0:T(128)S(1)} %pad_add_fusion.refs_0_.core_ref, s32[4,4]{1,0:T(4,128)S(1)} %broadcast_add_fusion.1.refs_1_, bf16[32,67,128]{2,1,0:T(8,128)(2,1)} %all-to-all-done.refs_2_, s32[4,1,128]{2,1,0:T(1,128)S(1)} %bitcast.9, f32[4,1,128]{2,1,0:T(1,128)S(1)} %bitcast.10), custom_call_target="tpu_custom_call" | custom-call | flops 1 | bytes 1 | tf_op jit(solution)/shard_map/teacher_prob/pallas_call | solution.py:486
  49.0 2.1 %collective-permute-done.6.refs_4_ = bf16[64,2560]{1,0:T(8,128)(2,1)} collective-permute-done((bf16[64,2560]{1,0:T(8,128)(2,1)}, bf16[64,2560]{1,0:T(8,128)(2,1)}, u32[]{:S(2)}, u32[]{:S(2)}) %collective-permute-start.6) | collective-permute-done | bytes 327712 | tf_op jit(solution)/shard_map/ppermute | solution.py:134
  51.1 1.5 %collective-permute-done.5.refs_3_ = bf16[64,2560]{1,0:T(8,128)(2,1)} collective-permute-done((bf16[64,2560]{1,0:T(8,128)(2,1)}, bf16[64,2560]{1,0:T(8,128)(2,1)}, u32[]{:S(2)}, u32[]{:S(2)}) %collective-permute-start.5) | collective-permute-done | bytes 327712 | tf_op jit(solution)/shard_map/ppermute | solution.py:134
  52.6 0.5 collective-permute-start.11
  53.2 1.3 collective-permute-done.10.refs_8_
  54.5 0.5 collective-permute-done.11.refs_9_
  55.0 0.1 collective-permute-start.13
  55.1 11.0 %logits.1 = (f32[512,1024]{1,0:T(8,128)S(1)}, f32[32,8,128]{2,1,0:T(8,128)S(1)}) custom-call(bf16[64,5120]{1,0:T(8,128)(2,1)S(1)} %constant_dynamic-update-slice_fusion.refs_0_, bf16[64,5120]{1,0:T(8,128)(2,1)S(1)} %collective-permute-done.3.refs_1_, bf16[64,5120]{1,0:T(8,128)(2,1)S(1)} %collective-permute-done.4.refs_2_, ...), custom_call_target="tpu_custom_call" | custom-call | flops 1 | bytes 1 | tf_op jit(solution)/shard_map/logits/pallas_call | solution.py:514
  66.1 12.6 %all_to_all.10.refs_1_ = f32[32,8,128]{2,1,0:T(8,128)S(1)} all-to-all(f32[32,8,128]{2,1,0:T(8,128)S(1)} %get-tuple-element.73), channel_id=1, replica_groups=mesh['vocab'=32] {'vocab'}, dimensions={0} | all-to-all | bytes 262144 | tf_op jit(solution)/shard_map/all_to_all | solution.py:537
  78.6 1.3 grad_logits.1
  79.9 0.3 collective-permute-start.12
  80.2 2.4 %collective-permute-done.12.sib_ref = bf16[512,1024]{1,0:T(8,128)(2,1)S(1)} collective-permute-done((bf16[512,1024]{1,0:T(8,128)(2,1)S(1)}, bf16[512,1024]{1,0:T(8,128)(2,1)S(1)}, u32[]{:S(2)}, u32[]{:S(2)}) %collective-permute-start.12) | collective-permute-done | bytes 1048608 | tf_op jit(solution)/shard_map/ppermute | solution.py:134
  82.7 9.4 %grad_hidden_partial.1 = (f32[4,2,16,1792]{3,2,1,0:T(8,128)S(1)}, bf16[4,2,16,1792]{3,2,1,0:T(8,128)(2,1)}, bf16[4,2,16,1792]{3,2,1,0:T(8,128)(2,1)S(1)}, bf16[4...) custom-call(s32[4]{0:T(128)S(1)} %pad_add_fusion.refs_0_.core_ref, ...), custom_call_target="tpu_custom_call" | custom-call | flops 1 | bytes 1 | tf_op jit(solution)/shard_map/grad_hidden_partial/pallas_call | solution.py:557
  92.1 0.4 collective-permute-start.14
  92.5 1.0 collective-permute-start.15
  93.5 2.0 %collective-permute-start.16 = (bf16[4,2,16,1792]{3,2,1,0:T(8,128)(2,1)S(1)}, bf16[4,2,16,1792]{3,2,1,0:T(8,128)(2,1)S(1)}, u32[]{:S(2)}, u32[]{:S(2)}) collective-permute-start(bf16[4,2,16,1792]{3,2,1,0:T(8,128)(2,1)S(1)} %get-tuple-element.89), channel_id=1, source_target_pairs={{0,6},{1,7},{2,4},{3,5},{4,2},{5,3},{6,0},{7,1},{8,14},{9,15},{10,... | collective-permute-start | bytes 1376264 | tf_op jit(solution)/shard_map/ppermute | solution.py:134
  95.5 0.6 collective-permute-start.17
  96.2 1.3 collective-permute-start.18
  97.5 7.5 %collective-permute-done.17.refs_5_ = bf16[4,2,16,768]{3,2,1,0:T(8,128)(2,1)S(1)} collective-permute-done((bf16[4,2,16,768]{3,2,1,0:T(8,128)(2,1)S(1)}, bf16[4,2,16,768]{3,2,1,0:T(8,128)(2,1)S(1)}, u32[]{:S(2)}, u32[]{:S(2)}) %collective-permute-start.17) | collective-permute-done | bytes 196640 | tf_op jit(solution)/shard_map/ppermute | solution.py:134
  104.9 1.8 %collective-permute-start.19 = (bf16[4,2,16,768]{3,2,1,0:T(8,128)(2,1)S(1)}, bf16[4,2,16,768]{3,2,1,0:T(8,128)(2,1)S(1)}, u32[]{:S(2)}, u32[]{:S(2)}) collective-permute-start(bf16[4,2,16,768]{3,2,1,0:T(8,128)(2,1)S(1)} %get-tuple-element.92), channel_id=1, source_target_pairs={{0,24},{1,25},{2,26},{3,27},{4,28},{5,29},{6,30},{7,31},{8,16},{9,... | collective-permute-start | bytes 589832 | tf_op jit(solution)/shard_map/ppermute | solution.py:134
  106.8 10.0 %grad_head.1 = bf16[5120,1024]{1,0:T(8,128)(2,1)} custom-call(bf16[64,5120]{1,0:T(8,128)(2,1)S(1)} %constant_dynamic-update-slice_fusion.refs_0_, bf16[64,5120]{1,0:T(8,128)(2,1)S(1)} %collective-permute-done.3.refs_1_, bf16[64,5120]{1,0:T(8,128)(2,1)S(1)} %collective-permute-done.4.refs_2_, bf16[64,2560]{1,0:T(8,128)(2,1)} %collective-permute-done.5.refs_3_, ...), custom_call_target="tpu_custom_call" | custom-call | flops 1 | bytes 1 | tf_op jit(solution)/shard_map/grad_head/pallas_call | solution.py:581
  116.8 0.3 first_sum.1
  117.1 0.1 collective-permute-start.20
  117.2 2.5 %collective-permute-start.21 = (bf16[2,16,1792]{2,1,0:T(8,128)(2,1)S(1)}, bf16[2,16,1792]{2,1,0:T(8,128)(2,1)S(1)}, u32[]{:S(2)}, u32[]{:S(2)}) collective-permute-start(bf16[2,16,1792]{2,1,0:T(8,128)(2,1)S(1)} %get-tuple-element.105), channel_id=1, source_target_pairs={{0,16},{1,17},{2,18},{3,19},{4,20},{5,21},{6,22},{7,23},{8,24},{9,... | collective-permute-start | bytes 344072 | tf_op jit(solution)/shard_map/ppermute | solution.py:134
  119.7 1.8 %collective-permute-start.22 = (bf16[2,16,1792]{2,1,0:T(8,128)(2,1)S(1)}, bf16[2,16,1792]{2,1,0:T(8,128)(2,1)S(1)}, u32[]{:S(2)}, u32[]{:S(2)}) collective-permute-start(bf16[2,16,1792]{2,1,0:T(8,128)(2,1)S(1)} %get-tuple-element.106), channel_id=1, source_target_pairs={{0,24},{1,25},{2,26},{3,27},{4,28},{5,29},{6,30},{7,31},{8,16},{9,... | collective-permute-start | bytes 344072 | tf_op jit(solution)/shard_map/ppermute | solution.py:134
  121.5 0.5 collective-permute-start.23
  122.0 1.2 collective-permute-start.24
  123.3 2.5 %collective-permute-done.23.refs_5_ = bf16[2,16,768]{2,1,0:T(8,128)(2,1)S(1)} collective-permute-done((bf16[2,16,768]{2,1,0:T(8,128)(2,1)S(1)}, bf16[2,16,768]{2,1,0:T(8,128)(2,1)S(1)}, u32[]{:S(2)}, u32[]{:S(2)}) %collective-permute-start.23) | collective-permute-done | bytes 49184 | tf_op jit(solution)/shard_map/ppermute | solution.py:134
  125.8 1.0 collective-permute-start.25
  126.8 4.0 %collective-permute-done.25.refs_7_ = bf16[2,16,768]{2,1,0:T(8,128)(2,1)S(1)} collective-permute-done((bf16[2,16,768]{2,1,0:T(8,128)(2,1)S(1)}, bf16[2,16,768]{2,1,0:T(8,128)(2,1)S(1)}, u32[]{:S(2)}, u32[]{:S(2)}) %collective-permute-start.25) | collective-permute-done | bytes 49184 | tf_op jit(solution)/shard_map/ppermute | solution.py:134
  130.8 0.1 last_sum.1
  130.9 0.1 collective-permute-start.26
  131.0 0.6 slice_reduce_fusion
  131.6 0.6 collective-permute-done.26
  132.3 0.7 pad_maximum_fusion
  (36 shorter events, 0.1 us)
Async XLA Ops:
  0.6 17.3 %collective-permute-start.1 = (bf16[16,5120]{1,0:T(8,128)(2,1)}, bf16[16,5120]{1,0:T(8,128)(2,1)S(1)}, u32[]{:S(2)}, u32[]{:S(2)}) collective-permute-start(bf16[16,5120]{1,0:T(8,128)(2,1)} %param.7), channel_id=1, source_target_pairs={{0,16},{1,17},{2,18},{3,19},{4,20},{5,21},{6,22},{7,23},{8,24},{9,... | collective-permute-start | bytes 491528 | tf_op jit(solution)/shard_map/ppermute | solution.py:134
  4.7 13.2 %collective-permute-start = (bf16[16,5120]{1,0:T(8,128)(2,1)}, bf16[16,5120]{1,0:T(8,128)(2,1)S(1)}, u32[]{:S(2)}, u32[]{:S(2)}) collective-permute-start(bf16[16,5120]{1,0:T(8,128)(2,1)} %param.7), channel_id=1, source_target_pairs={{0,8},{1,9},{2,10},{3,11},{4,12},{5,13},{6,14},{7,15},{8,0},{9,1},... | collective-permute-start | bytes 491528 | tf_op jit(solution)/shard_map/ppermute | solution.py:134
  6.3 11.7 %collective-permute-start.2 = (bf16[16,5120]{1,0:T(8,128)(2,1)}, bf16[16,5120]{1,0:T(8,128)(2,1)S(1)}, u32[]{:S(2)}, u32[]{:S(2)}) collective-permute-start(bf16[16,5120]{1,0:T(8,128)(2,1)} %param.7), channel_id=1, source_target_pairs={{0,24},{1,25},{2,26},{3,27},{4,28},{5,29},{6,30},{7,31},{8,16},{9,... | collective-permute-start | bytes 491528 | tf_op jit(solution)/shard_map/ppermute | solution.py:134
  7.7 1.0 copy-start.1
  10.8 33.3 %all-to-all-start = ((bf16[32,67,128]{2,1,0:T(8,128)(2,1)}), bf16[32,67,128]{2,1,0:T(8,128)(2,1)}, u32[]{:S(2)}, u32[]{:S(2)}) async-start(bf16[32,67,128]{2,1,0:T(8,128)(2,1)} %slice.18), calls=%async_computation | async-start | bytes 1179648 | tf_op jit(solution)/shard_map/all_to_all | solution.py:482
  18.0 22.4 %collective-permute-start.4 = (bf16[64,5120]{1,0:T(8,128)(2,1)S(1)}, bf16[64,5120]{1,0:T(8,128)(2,1)S(1)}, u32[]{:S(2)}, u32[]{:S(2)}) collective-permute-start(bf16[64,5120]{1,0:T(8,128)(2,1)S(1)} %constant_dynamic-update-slice_fusion.refs_0_), channel_id=1, source_target_pairs={{0,4},{1,5},{2,6},{3,7},{4,0},{5,1},{6,2},{7,3},{8,12},{9,13},{10,... | collective-permute-start | bytes 1966088 | tf_op jit(solution)/shard_map/ppermute | solution.py:134
  19.8 22.6 %collective-permute-start.3 = (bf16[64,5120]{1,0:T(8,128)(2,1)S(1)}, bf16[64,5120]{1,0:T(8,128)(2,1)S(1)}, u32[]{:S(2)}, u32[]{:S(2)}) collective-permute-start(bf16[64,5120]{1,0:T(8,128)(2,1)S(1)} %constant_dynamic-update-slice_fusion.refs_0_), channel_id=1, source_target_pairs={{0,2},{1,3},{2,0},{3,1},{4,6},{5,7},{6,4},{7,5},{8,10},{9,11},{10,... | collective-permute-start | bytes 1966088 | tf_op jit(solution)/shard_map/ppermute | solution.py:134
  21.5 22.6 %copy-start.2 = (s32[4,128]{1,0:T(4,128)S(1)}, s32[4,128]{1,0:T(4,128)}, u32[]{:S(2)}) copy-start(s32[4,128]{1,0:T(4,128)} %param.11) | copy-start | bytes 6148
  21.5 22.6 %copy-start.3 = (f32[512]{0:T(512)S(1)}, f32[512]{0:T(512)}, u32[]{:S(2)}) copy-start(f32[512]{0:T(512)} %param.12) | copy-start | bytes 6148
  26.9 26.2 %collective-permute-start.7 = (bf16[64,5120]{1,0:T(8,128)(2,1)S(1)}, bf16[64,5120]{1,0:T(8,128)(2,1)S(1)}, u32[]{:S(2)}, u32[]{:S(2)}) collective-permute-start(bf16[64,5120]{1,0:T(8,128)(2,1)S(1)} %constant_dynamic-update-slice_fusion.refs_0_), channel_id=1, source_target_pairs={{0,1},{1,0},{2,3},{3,2},{4,5},{5,4},{6,7},{7,6},{8,9},{9,8},{10,11... | collective-permute-start | bytes 1966088 | tf_op jit(solution)/shard_map/ppermute | solution.py:134
  41.2 10.0 %collective-permute-start.6 = (bf16[64,2560]{1,0:T(8,128)(2,1)}, bf16[64,2560]{1,0:T(8,128)(2,1)}, u32[]{:S(2)}, u32[]{:S(2)}) collective-permute-start(bf16[64,2560]{1,0:T(8,128)(2,1)} %slice.17), channel_id=1, source_target_pairs={{0,2},{1,3},{2,0},{3,1},{4,6},{5,7},{6,4},{7,5},{8,10},{9,11},{10,... | collective-permute-start | bytes 983048 | tf_op jit(solution)/shard_map/ppermute | solution.py:134
  43.1 9.6 %collective-permute-start.5 = (bf16[64,2560]{1,0:T(8,128)(2,1)}, bf16[64,2560]{1,0:T(8,128)(2,1)}, u32[]{:S(2)}, u32[]{:S(2)}) collective-permute-start(bf16[64,2560]{1,0:T(8,128)(2,1)} %slice.16), channel_id=1, source_target_pairs={{0,4},{1,5},{2,6},{3,7},{4,0},{5,1},{6,2},{7,3},{8,12},{9,13},{10,... | collective-permute-start | bytes 983048 | tf_op jit(solution)/shard_map/ppermute | solution.py:134
  43.5 11.5 %collective-permute-start.9 = (bf16[64,5120]{1,0:T(8,128)(2,1)S(1)}, bf16[64,5120]{1,0:T(8,128)(2,1)S(1)}, u32[]{:S(2)}, u32[]{:S(2)}) collective-permute-start(bf16[64,5120]{1,0:T(8,128)(2,1)S(1)} %collective-permute-done.4.refs_2_), channel_id=1, source_target_pairs={{0,1},{1,0},{2,3},{3,2},{4,5},{5,4},{6,7},{7,6},{8,9},{9,8},{10,11... | collective-permute-start | bytes 1966088 | tf_op jit(solution)/shard_map/ppermute | solution.py:134
  43.5 11.5 %collective-permute-start.8 = (bf16[64,5120]{1,0:T(8,128)(2,1)S(1)}, bf16[64,5120]{1,0:T(8,128)(2,1)}, u32[]{:S(2)}, u32[]{:S(2)}) collective-permute-start(bf16[64,5120]{1,0:T(8,128)(2,1)S(1)} %collective-permute-done.3.refs_1_), channel_id=1, source_target_pairs={{0,1},{1,0},{2,3},{3,2},{4,5},{5,4},{6,7},{7,6},{8,9},{9,8},{10,11... | collective-permute-start | bytes 1966088 | tf_op jit(solution)/shard_map/ppermute | solution.py:134
  52.6 26.0 %copy-start.4 = (f32[512]{0:T(512)S(1)}, f32[512]{0:T(512)}, u32[]{:S(2)}) copy-start(f32[512]{0:T(512)} %param.13) | copy-start | bytes 6148
  52.6 1.8 %collective-permute-start.10 = (bf16[64,2560]{1,0:T(8,128)(2,1)}, bf16[64,2560]{1,0:T(8,128)(2,1)S(1)}, u32[]{:S(2)}, u32[]{:S(2)}) collective-permute-start(bf16[64,2560]{1,0:T(8,128)(2,1)} %collective-permute-done.5.refs_3_), channel_id=1, source_target_pairs={{0,1},{1,0},{2,3},{3,2},{4,5},{5,4},{6,7},{7,6},{8,9},{9,8},{10,11... | collective-permute-start | bytes 983048 | tf_op jit(solution)/shard_map/ppermute | solution.py:134
  52.6 2.3 %collective-permute-start.11 = (bf16[64,2560]{1,0:T(8,128)(2,1)}, bf16[64,2560]{1,0:T(8,128)(2,1)S(1)}, u32[]{:S(2)}, u32[]{:S(2)}) collective-permute-start(bf16[64,2560]{1,0:T(8,128)(2,1)} %collective-permute-done.6.refs_4_), channel_id=1, source_target_pairs={{0,1},{1,0},{2,3},{3,2},{4,5},{5,4},{6,7},{7,6},{8,9},{9,8},{10,11... | collective-permute-start | bytes 983048 | tf_op jit(solution)/shard_map/ppermute | solution.py:134
  55.0 27.7 %collective-permute-start.13 = (bf16[2560,1024]{1,0:T(8,128)(2,1)}, bf16[2560,1024]{1,0:T(8,128)(2,1)S(1)}, u32[]{:S(2)}, u32[]{:S(2)}) collective-permute-start(bf16[2560,1024]{1,0:T(8,128)(2,1)} %constant_dynamic-slice_fusion), channel_id=1, source_target_pairs={{0,1},{1,0},{2,3},{3,2},{4,5},{5,4},{6,7},{7,6},{8,9},{9,8},{10,11... | collective-permute-start | bytes 15728648 | tf_op jit(solution)/shard_map/ppermute | solution.py:134
  79.9 12.1 %copy-start = (bf16[512,1024]{1,0:T(8,128)(2,1)}, bf16[512,1024]{1,0:T(8,128)(2,1)S(1)}, u32[]{:S(2)}) copy-start(bf16[512,1024]{1,0:T(8,128)(2,1)S(1)} %get-tuple-element.93.grad_ref.refs_10_) | copy-start | bytes 3145732
  79.9 2.7 %collective-permute-start.12 = (bf16[512,1024]{1,0:T(8,128)(2,1)S(1)}, bf16[512,1024]{1,0:T(8,128)(2,1)S(1)}, u32[]{:S(2)}, u32[]{:S(2)}) collective-permute-start(bf16[512,1024]{1,0:T(8,128)(2,1)S(1)} %get-tuple-element.93.grad_ref.refs_10_), channel_id=1, source_target_pairs={{0,1},{1,0},{2,3},{3,2},{4,5},{5,4},{6,7},{7,6},{8,9},{9,8},{10,11... | collective-permute-start | bytes 3145736 | tf_op jit(solution)/shard_map/ppermute | solution.py:134
  92.1 24.7 %collective-permute-start.14 = (bf16[4,2,16,1792]{3,2,1,0:T(8,128)(2,1)}, bf16[4,2,16,1792]{3,2,1,0:T(8,128)(2,1)S(1)}, u32[]{:S(2)}, u32[]{:S(2)}) collective-permute-start(bf16[4,2,16,1792]{3,2,1,0:T(8,128)(2,1)} %get-tuple-element.87), channel_id=1, source_target_pairs={{0,2},{1,3},{2,0},{3,1},{4,6},{5,7},{6,4},{7,5},{8,10},{9,11},{10,... | collective-permute-start | bytes 1376264 | tf_op jit(solution)/shard_map/ppermute | solution.py:134
  92.5 24.3 %collective-permute-start.15 = (bf16[4,2,16,1792]{3,2,1,0:T(8,128)(2,1)S(1)}, bf16[4,2,16,1792]{3,2,1,0:T(8,128)(2,1)S(1)}, u32[]{:S(2)}, u32[]{:S(2)}) collective-permute-start(bf16[4,2,16,1792]{3,2,1,0:T(8,128)(2,1)S(1)} %get-tuple-element.88), channel_id=1, source_target_pairs={{0,4},{1,5},{2,6},{3,7},{4,0},{5,1},{6,2},{7,3},{8,12},{9,13},{10,... | collective-permute-start | bytes 1376264 | tf_op jit(solution)/shard_map/ppermute | solution.py:134
  93.5 23.3 %collective-permute-start.16 = (bf16[4,2,16,1792]{3,2,1,0:T(8,128)(2,1)S(1)}, bf16[4,2,16,1792]{3,2,1,0:T(8,128)(2,1)S(1)}, u32[]{:S(2)}, u32[]{:S(2)}) collective-permute-start(bf16[4,2,16,1792]{3,2,1,0:T(8,128)(2,1)S(1)} %get-tuple-element.89), channel_id=1, source_target_pairs={{0,6},{1,7},{2,4},{3,5},{4,2},{5,3},{6,0},{7,1},{8,14},{9,15},{10,... | collective-permute-start | bytes 1376264 | tf_op jit(solution)/shard_map/ppermute | solution.py:134
  95.5 9.4 %collective-permute-start.17 = (bf16[4,2,16,768]{3,2,1,0:T(8,128)(2,1)S(1)}, bf16[4,2,16,768]{3,2,1,0:T(8,128)(2,1)S(1)}, u32[]{:S(2)}, u32[]{:S(2)}) collective-permute-start(bf16[4,2,16,768]{3,2,1,0:T(8,128)(2,1)S(1)} %get-tuple-element.90), channel_id=1, source_target_pairs={{0,8},{1,9},{2,10},{3,11},{4,12},{5,13},{6,14},{7,15},{8,0},{9,1},... | collective-permute-start | bytes 589832 | tf_op jit(solution)/shard_map/ppermute | solution.py:134
  96.2 20.6 %collective-permute-start.18 = (bf16[4,2,16,768]{3,2,1,0:T(8,128)(2,1)S(1)}, bf16[4,2,16,768]{3,2,1,0:T(8,128)(2,1)S(1)}, u32[]{:S(2)}, u32[]{:S(2)}) collective-permute-start(bf16[4,2,16,768]{3,2,1,0:T(8,128)(2,1)S(1)} %get-tuple-element.91), channel_id=1, source_target_pairs={{0,16},{1,17},{2,18},{3,19},{4,20},{5,21},{6,22},{7,23},{8,24},{9,... | collective-permute-start | bytes 589832 | tf_op jit(solution)/shard_map/ppermute | solution.py:134
  104.9 11.8 %collective-permute-start.19 = (bf16[4,2,16,768]{3,2,1,0:T(8,128)(2,1)S(1)}, bf16[4,2,16,768]{3,2,1,0:T(8,128)(2,1)S(1)}, u32[]{:S(2)}, u32[]{:S(2)}) collective-permute-start(bf16[4,2,16,768]{3,2,1,0:T(8,128)(2,1)S(1)} %get-tuple-element.92), channel_id=1, source_target_pairs={{0,24},{1,25},{2,26},{3,27},{4,28},{5,29},{6,30},{7,31},{8,16},{9,... | collective-permute-start | bytes 589832 | tf_op jit(solution)/shard_map/ppermute | solution.py:134
  117.1 13.7 %collective-permute-start.20 = (bf16[2,16,1792]{2,1,0:T(8,128)(2,1)S(1)}, bf16[2,16,1792]{2,1,0:T(8,128)(2,1)S(1)}, u32[]{:S(2)}, u32[]{:S(2)}) collective-permute-start(bf16[2,16,1792]{2,1,0:T(8,128)(2,1)S(1)} %get-tuple-element.104), channel_id=1, source_target_pairs={{0,8},{1,9},{2,10},{3,11},{4,12},{5,13},{6,14},{7,15},{8,0},{9,1},... | collective-permute-start | bytes 344072 | tf_op jit(solution)/shard_map/ppermute | solution.py:134
  117.2 13.6 %collective-permute-start.21 = (bf16[2,16,1792]{2,1,0:T(8,128)(2,1)S(1)}, bf16[2,16,1792]{2,1,0:T(8,128)(2,1)S(1)}, u32[]{:S(2)}, u32[]{:S(2)}) collective-permute-start(bf16[2,16,1792]{2,1,0:T(8,128)(2,1)S(1)} %get-tuple-element.105), channel_id=1, source_target_pairs={{0,16},{1,17},{2,18},{3,19},{4,20},{5,21},{6,22},{7,23},{8,24},{9,... | collective-permute-start | bytes 344072 | tf_op jit(solution)/shard_map/ppermute | solution.py:134
  119.7 11.1 %collective-permute-start.22 = (bf16[2,16,1792]{2,1,0:T(8,128)(2,1)S(1)}, bf16[2,16,1792]{2,1,0:T(8,128)(2,1)S(1)}, u32[]{:S(2)}, u32[]{:S(2)}) collective-permute-start(bf16[2,16,1792]{2,1,0:T(8,128)(2,1)S(1)} %get-tuple-element.106), channel_id=1, source_target_pairs={{0,24},{1,25},{2,26},{3,27},{4,28},{5,29},{6,30},{7,31},{8,16},{9,... | collective-permute-start | bytes 344072 | tf_op jit(solution)/shard_map/ppermute | solution.py:134
  121.5 4.3 %collective-permute-start.23 = (bf16[2,16,768]{2,1,0:T(8,128)(2,1)S(1)}, bf16[2,16,768]{2,1,0:T(8,128)(2,1)S(1)}, u32[]{:S(2)}, u32[]{:S(2)}) collective-permute-start(bf16[2,16,768]{2,1,0:T(8,128)(2,1)S(1)} %get-tuple-element.108), channel_id=1, source_target_pairs={{0,2},{1,3},{2,0},{3,1},{4,6},{5,7},{6,4},{7,5},{8,10},{9,11},{10,... | collective-permute-start | bytes 147464 | tf_op jit(solution)/shard_map/ppermute | solution.py:134
  122.0 4.8 %collective-permute-start.24 = (bf16[2,16,768]{2,1,0:T(8,128)(2,1)S(1)}, bf16[2,16,768]{2,1,0:T(8,128)(2,1)S(1)}, u32[]{:S(2)}, u32[]{:S(2)}) collective-permute-start(bf16[2,16,768]{2,1,0:T(8,128)(2,1)S(1)} %get-tuple-element.109), channel_id=1, source_target_pairs={{0,4},{1,5},{2,6},{3,7},{4,0},{5,1},{6,2},{7,3},{8,12},{9,13},{10,... | collective-permute-start | bytes 147464 | tf_op jit(solution)/shard_map/ppermute | solution.py:134
  125.8 5.0 %collective-permute-start.25 = (bf16[2,16,768]{2,1,0:T(8,128)(2,1)S(1)}, bf16[2,16,768]{2,1,0:T(8,128)(2,1)S(1)}, u32[]{:S(2)}, u32[]{:S(2)}) collective-permute-start(bf16[2,16,768]{2,1,0:T(8,128)(2,1)S(1)} %get-tuple-element.110), channel_id=1, source_target_pairs={{0,6},{1,7},{2,4},{3,5},{4,2},{5,3},{6,0},{7,1},{8,14},{9,15},{10,... | collective-permute-start | bytes 147464 | tf_op jit(solution)/shard_map/ppermute | solution.py:134
  130.9 1.3 %collective-permute-start.26 = (bf16[16,2560]{1,0:T(8,128)(2,1)S(1)}, bf16[16,2560]{1,0:T(8,128)(2,1)S(1)}, u32[]{:S(2)}, u32[]{:S(2)}) collective-permute-start(bf16[16,2560]{1,0:T(8,128)(2,1)S(1)} %get-tuple-element.112), channel_id=1, source_target_pairs={{0,1},{1,0},{2,3},{3,2},{4,5},{5,4},{6,7},{7,6},{8,9},{9,8},{10,11... | collective-permute-start | bytes 245768 | tf_op jit(solution)/shard_map/ppermute | solution.py:134

commit v16 on v15

--- a/solution.py
+++ b/solution.py
@@ -354,16 +354,8 @@
 
 
 def head_kernel(rows, *refs):
-    pieces, (grad_ref, out_ref, hidden) = refs[:-3], refs[-3:]
-    per_core = CHIPS + 1
-    late = pl.program_id(0) >= pl.num_programs(0) // 2
-    for i in range(2):
-
-        @pl.when(late == (i == 1))
-        def _():
-            mine = [pieces[c * per_core : (c + 1) * per_core] for c in range(CORES)]
-            assemble([p for some in mine for p in (*some[: CHIPS - 1], some[CHIPS - 1 + i])], rows, hidden)
-
+    pieces, grad_ref, (out_ref, hidden) = refs[:GROUP], refs[GROUP], refs[-2:]
+    assemble(pieces, rows, hidden)
     out_ref[...] = lax.dot_general(
         hidden[...], grad_ref[...], (((0,), (0,)), ((), ())), preferred_element_type=jnp.float32
     ).astype(out_ref.dtype)
@@ -520,10 +512,7 @@
         ],
         in_specs=[vmem_spec()] * len(pieces)
         + [hbm_spec(), pl.BlockSpec((tokens, width), lambda t: (0, jnp.maximum(t - tiles, 0)))],
-        out_specs=[
-            pl.BlockSpec((tokens, slab), whole),
-            pl.BlockSpec((n, 2 * tokens // 128, 128), lambda t: (0, 0, 0)),
-        ],
+        out_specs=[vmem_spec()] * 2,
         scratch_shapes=[
             pltpu.VMEM((tokens, depth), bf16),
             pltpu.VMEM((depth, slab), bf16),
@@ -552,17 +541,15 @@
 
     tile = half // 5
     sizes = (half * 7 // 10, half - half * 7 // 10)
-    wide_block = pl.BlockSpec((layers, CORES, rows, sizes[0]), lambda t, pos: (0, 0, 0, 0))
-    narrow_block = pl.BlockSpec((CHIPS, CORES, rows, sizes[1]), lambda t, pos: (0, 0, 0, 0))
     partial = pl.pallas_call(
         functools.partial(partial_kernel, rows),
         grid_spec=pltpu.PrefetchScalarGridSpec(
             num_scalar_prefetch=1,
             grid=(5,),
-            in_specs=[pl.BlockSpec((tokens, slab), lambda t, pos: (0, 0))] * 2
+            in_specs=[vmem_spec()] * 2
             + [pl.BlockSpec((tile, slab), lambda t, pos: (pos[0] * 5 + t, 0))]
             + [pl.BlockSpec((tile, slab), lambda t, pos: (t, 0))],
-            out_specs=[wide_block] * CHIPS + [narrow_block] * layers,
+            out_specs=[vmem_spec()] * (CHIPS + layers),
             scratch_shapes=[pltpu.VMEM((tokens, slab), bf16)],
         ),
         out_shape=[
@@ -578,25 +565,32 @@
     narrow_sums = [shift(partial[CHIPS + k], k * GROUP) for k in range(1, layers)]
 
     head_tile = half // 2
-    grad_head = pl.pallas_call(
-        functools.partial(head_kernel, rows),
-        grid=(4,),
-        in_specs=[
-            pl.BlockSpec(
-                (layers * rows, head_tile),
-                lambda t, i=i % (CHIPS + 1): (0, (t, jnp.minimum(t, 1), jnp.maximum(t - 2, 0))[max(i - 2, 0)]),
-            )
-            for i in range(len(pieces))
-        ]
-        + [pl.BlockSpec((tokens, slab), whole)],
-        out_specs=pl.BlockSpec((head_tile, slab), lambda t: (t, 0)),
-        out_shape=jax.ShapeDtypeStruct((depth, slab), bf16),
-        scratch_shapes=[pltpu.VMEM((tokens, head_tile), bf16)],
-        compiler_params=kernel_params(LARGE_VMEM),
-        cost_estimate=LIGHT,
-        name="grad_head",
-    )(*pieces, late_grad)
-    wide_sums, narrow_sums, grad_head = lax.optimization_barrier((wide_sums, narrow_sums, grad_head))
+
+    def grad_head_half(i, *before):
+        some = [piece for c in range(CORES) for piece in pieces[c * (CHIPS + 1) :][: CHIPS - 1]]
+        across_chip = [pieces[c * (CHIPS + 1) + CHIPS - 1 + i] for c in range(CORES)]
+        near = pl.BlockSpec((layers * rows, head_tile), lambda t: (0, 2 * i + t))
+        far = pl.BlockSpec((layers * rows, head_tile), lambda t: (0, t))
+        operands = []
+        for c in range(CORES):
+            operands += some[c * (CHIPS - 1) : (c + 1) * (CHIPS - 1)] + [across_chip[c]]
+        return pl.pallas_call(
+            functools.partial(head_kernel, rows),
+            grid=(2,),
+            in_specs=([near] * (CHIPS - 1) + [far]) * CORES + [vmem_spec()] + [hbm_spec()] * len(before),
+            out_specs=pl.BlockSpec((head_tile, slab), lambda t: (2 * i + t, 0)),
+            out_shape=jax.ShapeDtypeStruct((depth, slab), bf16),
+            scratch_shapes=[pltpu.VMEM((tokens, head_tile), bf16)],
+            input_output_aliases={GROUP + 1: 0} if before else {},
+            compiler_params=kernel_params(LARGE_VMEM),
+            cost_estimate=LIGHT,
+            name="grad_head",
+        )(*operands, late_grad, *before)
+
+    grad_head = grad_head_half(0)
+    wide_sums, narrow_sums, grad_head, late_grad = lax.optimization_barrier(
+        (wide_sums, narrow_sums, grad_head, late_grad)
+    )
 
     summed = pl.pallas_call(
         functools.partial(first_sum_kernel, layers),
@@ -610,6 +604,8 @@
     )(partial[0], *wide_sums, partial[CHIPS], *narrow_sums)
     wide_sums = [shift(summed[k], k * GROUP) for k in range(1, layers)]
     narrow_sums = [shift(summed[layers + j], j * CORES) for j in range(1, CHIPS)]
+    grad_head = grad_head_half(1, grad_head)
+    wide_sums, narrow_sums, grad_head = lax.optimization_barrier((wide_sums, narrow_sums, grad_head))
     mine, theirs = pl.pallas_call(
         functools.partial(last_sum_kernel, layers),
         in_specs=[vmem_spec()] * (CHIPS + layers),

time: 133 us -> 137 us (1.030)
  waiting for transfers between devices: 36.1 us -> 33.4 us
  local copies, waits for them, and re-layouts: 10.7 us -> 13.4 us
  Pallas kernels: 38.2 us -> 40.6 us
  starting transfers between devices: 32.5 us -> 33.9 us
    unnamed x13 -> x33, local copies, waits for them, and re-layouts: 1.92 us -> 5.34 us
    ppermute x27, waiting for transfers between devices: 36.1 us -> 33.4 us  [shift(): return lax.ppermute(x, 'vocab', [(i, i ^ distance) for i in range(n)])]
    pallas_call x1 -> x2, Pallas kernels: 9.96 us -> 11.5 us  [grad_head_half(): pl.pallas_call(functools.partial(head_kernel, rows), grid=(2,), in_specs=...]
    ppermute x27, starting transfers between devices: 26.3 us -> 27.7 us  [shift(): return lax.ppermute(x, 'vocab', [(i, i ^ distance) for i in range(n)])]
  transfers between devices with their start and end apart: 28 -> 28, of which waited for: 10 -> 9; matrix products, arithmetic and copies ran while one was open for 8% -> 8% of each run, Pallas kernels for 21% -> 22%
where the time goes in v16:
time: 137 us
  Pallas kernels  40.6 us (30%)
  starting transfers between devices  33.9 us (25%)
  waiting for transfers between devices  33.4 us (24%)
  local copies, waits for them, and re-layouts  13.4 us (10%)
  blocking collectives  12.5 us (9%)
  other arithmetic  2 us (1%)
    ppermute x27, waiting for transfers between devices, shift(): return lax.ppermute(x, 'vocab', [(i, i ^ distance) for i in range(n)])  33.4 us
    ppermute x27, starting transfers between devices, shift(): return lax.ppermute(x, 'vocab', [(i, i ^ distance) for i in range(n)])  27.7 us
    all_to_all x1, blocking collectives, levels_plan(): lax.all_to_all(stat, 'vocab', split_axis=0, concat_axis=0, tiled=True)  12.5 us
    pallas_call x2, Pallas kernels, grad_head_half(): pl.pallas_call(functools.partial(head_kernel, rows), grid=(2,), in_specs=...  11.5 us
    pallas_call x1, Pallas kernels, levels_plan(): pl.pallas_call(functools.partial(logits_kernel, rows), grid=(2 * tiles,),...  11.1 us
    pallas_call x1, Pallas kernels, levels_plan(): pl.pallas_call(functools.partial(partial_kernel, rows), grid_spec=pltpu.P...  8.63 us
    all_to_all x1, starting transfers between devices, levels_plan(): lax.all_to_all(payload[:, :3 - STAT_ROWS], 'vocab', split_axis=0, concat_...  6.18 us
    dynamic_slice x1, local copies, waits for them, and re-layouts, levels_plan(): lax.dynamic_slice(head_weight, ((1 - core) * half, 0), (half, slab))  5.43 us
  transfers between devices with their start and end apart: 28, of which 9 were waited for; matrix products, arithmetic and copies ran while one was open for 8% of the time, Pallas kernels for 22%

profile of v16, /device:TPU:0, one launch (start us, length us, event | category | flops | bytes accessed | tf_op | source)
XLA Modules:
  0.0 136.7 jit_solution(16003291735194421120)
XLA Ops:
  0.6 4.1 %collective-permute-start.1 = (bf16[16,5120]{1,0:T(8,128)(2,1)}, bf16[16,5120]{1,0:T(8,128)(2,1)S(1)}, u32[]{:S(2)}, u32[]{:S(2)}) collective-permute-start(bf16[16,5120]{1,0:T(8,128)(2,1)} %param.7), channel_id=1, source_target_pairs={{0,16},{1,17},{2,18},{3,19},{4,20},{5,21},{6,22},{7,23},{8,24},{9,... | collective-permute-start | bytes 491528 | tf_op jit(solution)/shard_map/ppermute | solution.py:134
  4.7 1.6 %collective-permute-start = (bf16[16,5120]{1,0:T(8,128)(2,1)}, bf16[16,5120]{1,0:T(8,128)(2,1)S(1)}, u32[]{:S(2)}, u32[]{:S(2)}) collective-permute-start(bf16[16,5120]{1,0:T(8,128)(2,1)} %param.7), channel_id=1, source_target_pairs={{0,8},{1,9},{2,10},{3,11},{4,12},{5,13},{6,14},{7,15},{8,0},{9,1},... | collective-permute-start | bytes 491528 | tf_op jit(solution)/shard_map/ppermute | solution.py:134
  6.3 0.7 add_select_fusion.1
  7.0 0.1 iota_compare_fusion
  7.1 0.2 convert_reduce_fusion
  7.3 0.1 add.85
  7.4 0.1 add.82
  7.5 0.1 add.89
  7.7 0.0 copy-start.5
  7.7 0.9 copy-done.5
  8.6 1.3 pack_teacher.1
  9.9 0.9 slice.18
  10.8 6.2 %all-to-all-start = ((bf16[32,67,128]{2,1,0:T(8,128)(2,1)}), bf16[32,67,128]{2,1,0:T(8,128)(2,1)}, u32[]{:S(2)}, u32[]{:S(2)}) async-start(bf16[32,67,128]{2,1,0:T(8,128)(2,1)} %slice.18), calls=%async_computation | async-start | bytes 1179648 | tf_op jit(solution)/shard_map/all_to_all | solution.py:474
  17.0 0.9 constant_dynamic-update-slice_fusion.3
  18.0 1.8 %collective-permute-start.4 = (bf16[64,5120]{1,0:T(8,128)(2,1)S(1)}, bf16[64,5120]{1,0:T(8,128)(2,1)S(1)}, u32[]{:S(2)}, u32[]{:S(2)}) collective-permute-start(bf16[64,5120]{1,0:T(8,128)(2,1)S(1)} %constant_dynamic-update-slice_fusion.refs_0_), channel_id=1, source_target_pairs={{0,4},{1,5},{2,6},{3,7},{4,0},{5,1},{6,2},{7,3},{8,12},{9,13},{10,... | collective-permute-start | bytes 1966088 | tf_op jit(solution)/shard_map/ppermute | solution.py:134
  19.8 1.5 %collective-permute-start.3 = (bf16[64,5120]{1,0:T(8,128)(2,1)S(1)}, bf16[64,5120]{1,0:T(8,128)(2,1)S(1)}, u32[]{:S(2)}, u32[]{:S(2)}) collective-permute-start(bf16[64,5120]{1,0:T(8,128)(2,1)S(1)} %constant_dynamic-update-slice_fusion.refs_0_), channel_id=1, source_target_pairs={{0,2},{1,3},{2,0},{3,1},{4,6},{5,7},{6,4},{7,5},{8,10},{9,11},{10,... | collective-permute-start | bytes 1966088 | tf_op jit(solution)/shard_map/ppermute | solution.py:134
  21.2 0.2 select_reduce_fusion
  21.5 0.0 copy-start.12
  21.5 5.4 %constant_dynamic-slice_fusion = bf16[2560,1024]{1,0:T(8,128)(2,1)} fusion(bf16[5120,1024]{1,0:T(8,128)(2,1)} %w_ref.1, s32[]{:T(128)S(6)} %select_n.57), kind=kLoop, calls=%fused_computation.27 | loop fusion | bytes 10485764 | tf_op jit(solution)/shard_map/dynamic_slice | solution.py:497
  26.9 13.5 %collective-permute-done.4.refs_2_ = bf16[64,5120]{1,0:T(8,128)(2,1)S(1)} collective-permute-done((bf16[64,5120]{1,0:T(8,128)(2,1)S(1)}, bf16[64,5120]{1,0:T(8,128)(2,1)S(1)}, u32[]{:S(2)}, u32[]{:S(2)}) %collective-permute-start.4) | collective-permute-done | bytes 655392 | tf_op jit(solution)/shard_map/ppermute | solution.py:134
  40.4 1.2 collective-permute-start.6
  41.6 0.8 slice.16
  42.4 0.4 collective-permute-start.5
  42.8 0.5 collective-permute-start.8
  43.3 0.1 pad_add_fusion.refs_0_.core_ref
  43.4 4.9 %teacher_prob.1 = (f32[512,1024]{1,0:T(8,128)S(1)}, f32[16,128]{1,0:T(8,128)S(1)}) custom-call(s32[4]{0:T(128)S(1)} %pad_add_fusion.refs_0_.core_ref, s32[4,4]{1,0:T(4,128)S(1)} %broadcast_add_fusion.1.refs_1_, bf16[32,67,128]{2,1,0:T(8,128)(2,1)} %all-to-all-done.refs_2_, s32[4,1,128]{2,1,0:T(1,128)S(1)} %bitcast.9, f32[4,1,128]{2,1,0:T(1,128)S(1)} %bitcast.10), custom_call_target="tpu_custom_call" | custom-call | flops 1 | bytes 1 | tf_op jit(solution)/shard_map/teacher_prob/pallas_call | solution.py:478
  48.3 1.8 %collective-permute-done.6.refs_4_.refs_3_ = bf16[64,2560]{1,0:T(8,128)(2,1)S(1)} collective-permute-done((bf16[64,2560]{1,0:T(8,128)(2,1)S(1)}, bf16[64,2560]{1,0:T(8,128)(2,1)S(1)}, u32[]{:S(2)}, u32[]{:S(2)}) %collective-permute-start.6) | collective-permute-done | bytes 327712 | tf_op jit(solution)/shard_map/ppermute | solution.py:134
  50.2 1.8 %collective-permute-done.5.refs_3_ = bf16[64,2560]{1,0:T(8,128)(2,1)} collective-permute-done((bf16[64,2560]{1,0:T(8,128)(2,1)}, bf16[64,2560]{1,0:T(8,128)(2,1)}, u32[]{:S(2)}, u32[]{:S(2)}) %collective-permute-start.5) | collective-permute-done | bytes 327712 | tf_op jit(solution)/shard_map/ppermute | solution.py:134
  52.0 0.5 collective-permute-start.11
  52.5 1.8 %collective-permute-done.10.refs_8_.refs_7_ = bf16[64,2560]{1,0:T(8,128)(2,1)S(1)} collective-permute-done((bf16[64,2560]{1,0:T(8,128)(2,1)}, bf16[64,2560]{1,0:T(8,128)(2,1)S(1)}, u32[]{:S(2)}, u32[]{:S(2)}) %collective-permute-start.10) | collective-permute-done | bytes 327712 | tf_op jit(solution)/shard_map/ppermute | solution.py:134
  54.3 0.2 collective-permute-start.13
  54.5 11.1 %logits.1 = (f32[512,1024]{1,0:T(8,128)S(1)}, f32[32,8,128]{2,1,0:T(8,128)S(1)}) custom-call(bf16[64,5120]{1,0:T(8,128)(2,1)S(1)} %constant_dynamic-update-slice_fusion.refs_0_, bf16[64,5120]{1,0:T(8,128)(2,1)S(1)} %collective-permute-done.3.refs_1_, bf16[64,5120]{1,0:T(8,128)(2,1)S(1)} %collective-permute-done.4.refs_2_, ...), custom_call_target="tpu_custom_call" | custom-call | flops 1 | bytes 1 | tf_op jit(solution)/shard_map/logits/pallas_call | solution.py:506
  65.6 12.5 %all_to_all.10.refs_1_ = f32[32,8,128]{2,1,0:T(8,128)S(1)} all-to-all(f32[32,8,128]{2,1,0:T(8,128)S(1)} %get-tuple-element.81), channel_id=1, replica_groups=mesh['vocab'=32] {'vocab'}, dimensions={0} | all-to-all | bytes 262144 | tf_op jit(solution)/shard_map/all_to_all | solution.py:526
  78.1 1.3 grad_logits.1
  79.4 0.3 collective-permute-start.12
  79.7 2.4 %collective-permute-done.12.sib_ref = bf16[512,1024]{1,0:T(8,128)(2,1)S(1)} collective-permute-done((bf16[512,1024]{1,0:T(8,128)(2,1)S(1)}, bf16[512,1024]{1,0:T(8,128)(2,1)S(1)}, u32[]{:S(2)}, u32[]{:S(2)}) %collective-permute-start.12) | collective-permute-done | bytes 1048608 | tf_op jit(solution)/shard_map/ppermute | solution.py:134
  82.1 8.6 %grad_hidden_partial.1 = (f32[4,2,16,1792]{3,2,1,0:T(8,128)S(1)}, bf16[4,2,16,1792]{3,2,1,0:T(8,128)(2,1)S(1)}, bf16[4,2,16,1792]{3,2,1,0:T(8,128)(2,1)S(1)}, bf...) custom-call(s32[4]{0:T(128)S(1)} %pad_add_fusion.refs_0_.core_ref, ...), custom_call_target="tpu_custom_call" | custom-call | flops 1 | bytes 1 | tf_op jit(solution)/shard_map/grad_hidden_partial/pallas_call | solution.py:544
  90.8 0.5 collective-permute-start.14
  91.3 1.0 collective-permute-start.15
  92.3 2.1 %collective-permute-start.16 = (bf16[4,2,16,1792]{3,2,1,0:T(8,128)(2,1)S(1)}, bf16[4,2,16,1792]{3,2,1,0:T(8,128)(2,1)S(1)}, u32[]{:S(2)}, u32[]{:S(2)}) collective-permute-start(bf16[4,2,16,1792]{3,2,1,0:T(8,128)(2,1)S(1)} %get-tuple-element.98), channel_id=1, source_target_pairs={{0,6},{1,7},{2,4},{3,5},{4,2},{5,3},{6,0},{7,1},{8,14},{9,15},{10,... | collective-permute-start | bytes 1376264 | tf_op jit(solution)/shard_map/ppermute | solution.py:134
  94.3 0.7 collective-permute-start.17
  95.0 1.2 collective-permute-start.18
  96.2 7.5 %collective-permute-done.17.refs_5_ = bf16[4,2,16,768]{3,2,1,0:T(8,128)(2,1)S(1)} collective-permute-done((bf16[4,2,16,768]{3,2,1,0:T(8,128)(2,1)S(1)}, bf16[4,2,16,768]{3,2,1,0:T(8,128)(2,1)S(1)}, u32[]{:S(2)}, u32[]{:S(2)}) %collective-permute-start.17) | collective-permute-done | bytes 196640 | tf_op jit(solution)/shard_map/ppermute | solution.py:134
  103.7 1.9 %collective-permute-start.19 = (bf16[4,2,16,768]{3,2,1,0:T(8,128)(2,1)S(1)}, bf16[4,2,16,768]{3,2,1,0:T(8,128)(2,1)S(1)}, u32[]{:S(2)}, u32[]{:S(2)}) collective-permute-start(bf16[4,2,16,768]{3,2,1,0:T(8,128)(2,1)S(1)} %get-tuple-element.101), channel_id=1, source_target_pairs={{0,24},{1,25},{2,26},{3,27},{4,28},{5,29},{6,30},{7,31},{8,16},{9,... | collective-permute-start | bytes 589832 | tf_op jit(solution)/shard_map/ppermute | solution.py:134
  105.6 5.7 %grad_head.2.refs_9_ = bf16[5120,1024]{1,0:T(8,128)(2,1)} custom-call(bf16[64,5120]{1,0:T(8,128)(2,1)S(1)} %constant_dynamic-update-slice_fusion.refs_0_, bf16[64,5120]{1,0:T(8,128)(2,1)S(1)} %collective-permute-done.3.refs_1_, bf16[64,5120]{1,0:T(8,128)(2,1)S(1)} %collective-permute-done.4.refs_2_, bf16[64,2560]{1,0:T(8,128)(2,1)} %collective-permute-done.5.refs_3_, ...), custom_call_target="tpu_custom_call" | custom-call | flops 1 | bytes 1 | tf_op jit(solution)/shard_map/grad_head/pallas_call | solution.py:577
  111.3 2.0 %collective-permute-done.16.refs_3_ = bf16[4,2,16,1792]{3,2,1,0:T(8,128)(2,1)S(1)} collective-permute-done((bf16[4,2,16,1792]{3,2,1,0:T(8,128)(2,1)S(1)}, bf16[4,2,16,1792]{3,2,1,0:T(8,128)(2,1)S(1)}, u32[]{:S(2)}, u32[]{:S(2)}) %collective-permute-start.16) | collective-permute-done | bytes 458784 | tf_op jit(solution)/shard_map/ppermute | solution.py:134
  113.4 0.9 first_sum.1
  114.3 0.7 copy-done.6
  115.0 1.6 %collective-permute-start.20 = (bf16[2,16,1792]{2,1,0:T(8,128)(2,1)}, bf16[2,16,1792]{2,1,0:T(8,128)(2,1)S(1)}, u32[]{:S(2)}, u32[]{:S(2)}) collective-permute-start(bf16[2,16,1792]{2,1,0:T(8,128)(2,1)} %get-tuple-element.110), channel_id=1, source_target_pairs={{0,8},{1,9},{2,10},{3,11},{4,12},{5,13},{6,14},{7,15},{8,0},{9,1},... | collective-permute-start | bytes 344072 | tf_op jit(solution)/shard_map/ppermute | solution.py:134
  116.5 0.3 collective-permute-start.21
  116.8 2.5 %collective-permute-start.22 = (bf16[2,16,1792]{2,1,0:T(8,128)(2,1)}, bf16[2,16,1792]{2,1,0:T(8,128)(2,1)}, u32[]{:S(2)}, u32[]{:S(2)}) collective-permute-start(bf16[2,16,1792]{2,1,0:T(8,128)(2,1)} %get-tuple-element.112), channel_id=1, source_target_pairs={{0,24},{1,25},{2,26},{3,27},{4,28},{5,29},{6,30},{7,31},{8,16},{9,... | collective-permute-start | bytes 344072 | tf_op jit(solution)/shard_map/ppermute | solution.py:134
  119.4 1.7 %collective-permute-start.23 = (bf16[2,16,768]{2,1,0:T(8,128)(2,1)S(1)}, bf16[2,16,768]{2,1,0:T(8,128)(2,1)S(1)}, u32[]{:S(2)}, u32[]{:S(2)}) collective-permute-start(bf16[2,16,768]{2,1,0:T(8,128)(2,1)S(1)} %get-tuple-element.113), channel_id=1, source_target_pairs={{0,2},{1,3},{2,0},{3,1},{4,6},{5,7},{6,4},{7,5},{8,10},{9,11},{10,... | collective-permute-start | bytes 147464 | tf_op jit(solution)/shard_map/ppermute | solution.py:134
  121.0 0.6 collective-permute-start.24
  121.6 1.8 %collective-permute-done.23.refs_5_ = bf16[2,16,768]{2,1,0:T(8,128)(2,1)S(1)} collective-permute-done((bf16[2,16,768]{2,1,0:T(8,128)(2,1)S(1)}, bf16[2,16,768]{2,1,0:T(8,128)(2,1)S(1)}, u32[]{:S(2)}, u32[]{:S(2)}) %collective-permute-start.23) | collective-permute-done | bytes 49184 | tf_op jit(solution)/shard_map/ppermute | solution.py:134
  123.5 0.6 copy-done.8
  124.1 1.7 %collective-permute-start.25 = (bf16[2,16,768]{2,1,0:T(8,128)(2,1)}, bf16[2,16,768]{2,1,0:T(8,128)(2,1)}, u32[]{:S(2)}, u32[]{:S(2)}) collective-permute-start(bf16[2,16,768]{2,1,0:T(8,128)(2,1)} %get-tuple-element.115), channel_id=1, source_target_pairs={{0,6},{1,7},{2,4},{3,5},{4,2},{5,3},{6,0},{7,1},{8,14},{9,15},{10,... | collective-permute-start | bytes 147464 | tf_op jit(solution)/shard_map/ppermute | solution.py:134
  125.8 1.1 copy-done.2
  126.9 1.0 copy-done.4
  127.8 5.8 %grad_head.3 = bf16[5120,1024]{1,0:T(8,128)(2,1)} custom-call(bf16[64,5120]{1,0:T(8,128)(2,1)S(1)} %constant_dynamic-update-slice_fusion.refs_0_, bf16[64,5120]{1,0:T(8,128)(2,1)S(1)} %collective-permute-done.3.refs_1_, bf16[64,5120]{1,0:T(8,128)(2,1)S(1)} %collective-permute-done.4.refs_2_, ...), custom_call_target="tpu_custom_call", output_to_operand_aliasing={{}: (9, {})} | custom-call | flops 1 | bytes 1 | tf_op jit(solution)/shard_map/grad_head/pallas_call | solution.py:577
  133.7 1.0 last_sum.1
  134.7 0.1 collective-permute-start.26
  134.8 0.6 slice_reduce_fusion
  135.4 0.6 collective-permute-done.26
  136.1 0.7 pad_maximum_fusion
  (57 shorter events, 0.2 us)
Async XLA Ops:
  0.6 17.3 %collective-permute-start.1 = (bf16[16,5120]{1,0:T(8,128)(2,1)}, bf16[16,5120]{1,0:T(8,128)(2,1)S(1)}, u32[]{:S(2)}, u32[]{:S(2)}) collective-permute-start(bf16[16,5120]{1,0:T(8,128)(2,1)} %param.7), channel_id=1, source_target_pairs={{0,16},{1,17},{2,18},{3,19},{4,20},{5,21},{6,22},{7,23},{8,24},{9,... | collective-permute-start | bytes 491528 | tf_op jit(solution)/shard_map/ppermute | solution.py:134
  4.7 13.2 %collective-permute-start = (bf16[16,5120]{1,0:T(8,128)(2,1)}, bf16[16,5120]{1,0:T(8,128)(2,1)S(1)}, u32[]{:S(2)}, u32[]{:S(2)}) collective-permute-start(bf16[16,5120]{1,0:T(8,128)(2,1)} %param.7), channel_id=1, source_target_pairs={{0,8},{1,9},{2,10},{3,11},{4,12},{5,13},{6,14},{7,15},{8,0},{9,1},... | collective-permute-start | bytes 491528 | tf_op jit(solution)/shard_map/ppermute | solution.py:134
  6.3 11.7 %collective-permute-start.2 = (bf16[16,5120]{1,0:T(8,128)(2,1)}, bf16[16,5120]{1,0:T(8,128)(2,1)S(1)}, u32[]{:S(2)}, u32[]{:S(2)}) collective-permute-start(bf16[16,5120]{1,0:T(8,128)(2,1)} %param.7), channel_id=1, source_target_pairs={{0,24},{1,25},{2,26},{3,27},{4,28},{5,29},{6,30},{7,31},{8,16},{9,... | collective-permute-start | bytes 491528 | tf_op jit(solution)/shard_map/ppermute | solution.py:134
  7.7 1.0 copy-start.5
  10.8 32.6 %all-to-all-start = ((bf16[32,67,128]{2,1,0:T(8,128)(2,1)}), bf16[32,67,128]{2,1,0:T(8,128)(2,1)}, u32[]{:S(2)}, u32[]{:S(2)}) async-start(bf16[32,67,128]{2,1,0:T(8,128)(2,1)} %slice.18), calls=%async_computation | async-start | bytes 1179648 | tf_op jit(solution)/shard_map/all_to_all | solution.py:474
  18.0 22.4 %collective-permute-start.4 = (bf16[64,5120]{1,0:T(8,128)(2,1)S(1)}, bf16[64,5120]{1,0:T(8,128)(2,1)S(1)}, u32[]{:S(2)}, u32[]{:S(2)}) collective-permute-start(bf16[64,5120]{1,0:T(8,128)(2,1)S(1)} %constant_dynamic-update-slice_fusion.refs_0_), channel_id=1, source_target_pairs={{0,4},{1,5},{2,6},{3,7},{4,0},{5,1},{6,2},{7,3},{8,12},{9,13},{10,... | collective-permute-start | bytes 1966088 | tf_op jit(solution)/shard_map/ppermute | solution.py:134
  19.8 21.9 %collective-permute-start.3 = (bf16[64,5120]{1,0:T(8,128)(2,1)S(1)}, bf16[64,5120]{1,0:T(8,128)(2,1)S(1)}, u32[]{:S(2)}, u32[]{:S(2)}) collective-permute-start(bf16[64,5120]{1,0:T(8,128)(2,1)S(1)} %constant_dynamic-update-slice_fusion.refs_0_), channel_id=1, source_target_pairs={{0,2},{1,3},{2,0},{3,1},{4,6},{5,7},{6,4},{7,5},{8,10},{9,11},{10,... | collective-permute-start | bytes 1966088 | tf_op jit(solution)/shard_map/ppermute | solution.py:134
  21.5 21.9 %copy-start.12 = (s32[4,128]{1,0:T(4,128)S(1)}, s32[4,128]{1,0:T(4,128)}, u32[]{:S(2)}) copy-start(s32[4,128]{1,0:T(4,128)} %param.11) | copy-start | bytes 6148
  21.5 21.9 %copy-start.13 = (f32[512]{0:T(512)S(1)}, f32[512]{0:T(512)}, u32[]{:S(2)}) copy-start(f32[512]{0:T(512)} %param.12) | copy-start | bytes 6148
  26.9 25.6 %collective-permute-start.7 = (bf16[64,5120]{1,0:T(8,128)(2,1)S(1)}, bf16[64,5120]{1,0:T(8,128)(2,1)S(1)}, u32[]{:S(2)}, u32[]{:S(2)}) collective-permute-start(bf16[64,5120]{1,0:T(8,128)(2,1)S(1)} %constant_dynamic-update-slice_fusion.refs_0_), channel_id=1, source_target_pairs={{0,1},{1,0},{2,3},{3,2},{4,5},{5,4},{6,7},{7,6},{8,9},{9,8},{10,11... | collective-permute-start | bytes 1966088 | tf_op jit(solution)/shard_map/ppermute | solution.py:134
  40.4 9.7 %collective-permute-start.6 = (bf16[64,2560]{1,0:T(8,128)(2,1)S(1)}, bf16[64,2560]{1,0:T(8,128)(2,1)S(1)}, u32[]{:S(2)}, u32[]{:S(2)}) collective-permute-start(bf16[64,2560]{1,0:T(8,128)(2,1)S(1)} %slice.17), channel_id=1, source_target_pairs={{0,2},{1,3},{2,0},{3,1},{4,6},{5,7},{6,4},{7,5},{8,10},{9,11},{10,... | collective-permute-start | bytes 983048 | tf_op jit(solution)/shard_map/ppermute | solution.py:134
  42.4 9.6 %collective-permute-start.5 = (bf16[64,2560]{1,0:T(8,128)(2,1)}, bf16[64,2560]{1,0:T(8,128)(2,1)}, u32[]{:S(2)}, u32[]{:S(2)}) collective-permute-start(bf16[64,2560]{1,0:T(8,128)(2,1)} %slice.16), channel_id=1, source_target_pairs={{0,4},{1,5},{2,6},{3,7},{4,0},{5,1},{6,2},{7,3},{8,12},{9,13},{10,... | collective-permute-start | bytes 983048 | tf_op jit(solution)/shard_map/ppermute | solution.py:134
  42.8 11.5 %collective-permute-start.9 = (bf16[64,5120]{1,0:T(8,128)(2,1)S(1)}, bf16[64,5120]{1,0:T(8,128)(2,1)}, u32[]{:S(2)}, u32[]{:S(2)}) collective-permute-start(bf16[64,5120]{1,0:T(8,128)(2,1)S(1)} %collective-permute-done.4.refs_2_), channel_id=1, source_target_pairs={{0,1},{1,0},{2,3},{3,2},{4,5},{5,4},{6,7},{7,6},{8,9},{9,8},{10,11... | collective-permute-start | bytes 1966088 | tf_op jit(solution)/shard_map/ppermute | solution.py:134
  42.8 11.5 %collective-permute-start.8 = (bf16[64,5120]{1,0:T(8,128)(2,1)S(1)}, bf16[64,5120]{1,0:T(8,128)(2,1)}, u32[]{:S(2)}, u32[]{:S(2)}) collective-permute-start(bf16[64,5120]{1,0:T(8,128)(2,1)S(1)} %collective-permute-done.3.refs_1_), channel_id=1, source_target_pairs={{0,1},{1,0},{2,3},{3,2},{4,5},{5,4},{6,7},{7,6},{8,9},{9,8},{10,11... | collective-permute-start | bytes 1966088 | tf_op jit(solution)/shard_map/ppermute | solution.py:134
  52.0 26.1 %copy-start.14 = (f32[512]{0:T(512)S(1)}, f32[512]{0:T(512)}, u32[]{:S(2)}) copy-start(f32[512]{0:T(512)} %param.13) | copy-start | bytes 6148
  52.0 2.3 %collective-permute-start.10 = (bf16[64,2560]{1,0:T(8,128)(2,1)}, bf16[64,2560]{1,0:T(8,128)(2,1)S(1)}, u32[]{:S(2)}, u32[]{:S(2)}) collective-permute-start(bf16[64,2560]{1,0:T(8,128)(2,1)} %collective-permute-done.5.refs_3_), channel_id=1, source_target_pairs={{0,1},{1,0},{2,3},{3,2},{4,5},{5,4},{6,7},{7,6},{8,9},{9,8},{10,11... | collective-permute-start | bytes 983048 | tf_op jit(solution)/shard_map/ppermute | solution.py:134
  52.0 2.3 %collective-permute-start.11 = (bf16[64,2560]{1,0:T(8,128)(2,1)S(1)}, bf16[64,2560]{1,0:T(8,128)(2,1)S(1)}, u32[]{:S(2)}, u32[]{:S(2)}) collective-permute-start(bf16[64,2560]{1,0:T(8,128)(2,1)S(1)} %collective-permute-done.6.refs_4_.refs_3_), channel_id=1, source_target_pairs={{0,1},{1,0},{2,3},{3,2},{4,5},{5,4},{6,7},{7,6},{8,9},{9,8},{10,11... | collective-permute-start | bytes 983048 | tf_op jit(solution)/shard_map/ppermute | solution.py:134
  52.5 13.1 %copy-start = (bf16[64,5120]{1,0:T(8,128)(2,1)}, bf16[64,5120]{1,0:T(8,128)(2,1)S(1)}, u32[]{:S(2)}) copy-start(bf16[64,5120]{1,0:T(8,128)(2,1)S(1)} %collective-permute-done.7.refs_5_.refs_4_) | copy-start | bytes 1966084
  54.2 11.3 %copy-start.3 = (bf16[64,2560]{1,0:T(8,128)(2,1)}, bf16[64,2560]{1,0:T(8,128)(2,1)S(1)}, u32[]{:S(2)}) copy-start(bf16[64,2560]{1,0:T(8,128)(2,1)S(1)} %collective-permute-done.11.refs_9_.refs_7_) | copy-start | bytes 983044
  54.3 27.8 %collective-permute-start.13 = (bf16[2560,1024]{1,0:T(8,128)(2,1)}, bf16[2560,1024]{1,0:T(8,128)(2,1)S(1)}, u32[]{:S(2)}, u32[]{:S(2)}) collective-permute-start(bf16[2560,1024]{1,0:T(8,128)(2,1)} %constant_dynamic-slice_fusion), channel_id=1, source_target_pairs={{0,1},{1,0},{2,3},{3,2},{4,5},{5,4},{6,7},{7,6},{8,9},{9,8},{10,11... | collective-permute-start | bytes 15728648 | tf_op jit(solution)/shard_map/ppermute | solution.py:134
  79.4 11.4 %copy-start.10 = (f32[16,128]{1,0:T(8,128)}, f32[16,128]{1,0:T(8,128)S(1)}, u32[]{:S(2)}) copy-start(f32[16,128]{1,0:T(8,128)S(1)} %get-tuple-element.84) | copy-start | bytes 24580
  79.4 26.2 %copy-start.1 = (bf16[64,5120]{1,0:T(8,128)(2,1)S(1)}, bf16[64,5120]{1,0:T(8,128)(2,1)}, u32[]{:S(2)}) copy-start(bf16[64,5120]{1,0:T(8,128)(2,1)} %copy-done) | copy-start | bytes 1966084
  79.4 2.7 %collective-permute-start.12 = (bf16[512,1024]{1,0:T(8,128)(2,1)S(1)}, bf16[512,1024]{1,0:T(8,128)(2,1)S(1)}, u32[]{:S(2)}, u32[]{:S(2)}) collective-permute-start(bf16[512,1024]{1,0:T(8,128)(2,1)S(1)} %get-tuple-element.116.grad_ref.refs_8_), channel_id=1, source_target_pairs={{0,1},{1,0},{2,3},{3,2},{4,5},{5,4},{6,7},{7,6},{8,9},{9,8},{10,11... | collective-permute-start | bytes 3145736 | tf_op jit(solution)/shard_map/ppermute | solution.py:134
  90.8 20.6 %collective-permute-start.14 = (bf16[4,2,16,1792]{3,2,1,0:T(8,128)(2,1)S(1)}, bf16[4,2,16,1792]{3,2,1,0:T(8,128)(2,1)S(1)}, u32[]{:S(2)}, u32[]{:S(2)}) collective-permute-start(bf16[4,2,16,1792]{3,2,1,0:T(8,128)(2,1)S(1)} %get-tuple-element.96), channel_id=1, source_target_pairs={{0,2},{1,3},{2,0},{3,1},{4,6},{5,7},{6,4},{7,5},{8,10},{9,11},{10,... | collective-permute-start | bytes 1376264 | tf_op jit(solution)/shard_map/ppermute | solution.py:134
  91.3 20.1 %collective-permute-start.15 = (bf16[4,2,16,1792]{3,2,1,0:T(8,128)(2,1)S(1)}, bf16[4,2,16,1792]{3,2,1,0:T(8,128)(2,1)S(1)}, u32[]{:S(2)}, u32[]{:S(2)}) collective-permute-start(bf16[4,2,16,1792]{3,2,1,0:T(8,128)(2,1)S(1)} %get-tuple-element.97), channel_id=1, source_target_pairs={{0,4},{1,5},{2,6},{3,7},{4,0},{5,1},{6,2},{7,3},{8,12},{9,13},{10,... | collective-permute-start | bytes 1376264 | tf_op jit(solution)/shard_map/ppermute | solution.py:134
  92.3 21.1 %collective-permute-start.16 = (bf16[4,2,16,1792]{3,2,1,0:T(8,128)(2,1)S(1)}, bf16[4,2,16,1792]{3,2,1,0:T(8,128)(2,1)S(1)}, u32[]{:S(2)}, u32[]{:S(2)}) collective-permute-start(bf16[4,2,16,1792]{3,2,1,0:T(8,128)(2,1)S(1)} %get-tuple-element.98), channel_id=1, source_target_pairs={{0,6},{1,7},{2,4},{3,5},{4,2},{5,3},{6,0},{7,1},{8,14},{9,15},{10,... | collective-permute-start | bytes 1376264 | tf_op jit(solution)/shard_map/ppermute | solution.py:134
  94.3 9.4 %collective-permute-start.17 = (bf16[4,2,16,768]{3,2,1,0:T(8,128)(2,1)S(1)}, bf16[4,2,16,768]{3,2,1,0:T(8,128)(2,1)S(1)}, u32[]{:S(2)}, u32[]{:S(2)}) collective-permute-start(bf16[4,2,16,768]{3,2,1,0:T(8,128)(2,1)S(1)} %get-tuple-element.99), channel_id=1, source_target_pairs={{0,8},{1,9},{2,10},{3,11},{4,12},{5,13},{6,14},{7,15},{8,0},{9,1},... | collective-permute-start | bytes 589832 | tf_op jit(solution)/shard_map/ppermute | solution.py:134
  95.0 16.3 %collective-permute-start.18 = (bf16[4,2,16,768]{3,2,1,0:T(8,128)(2,1)S(1)}, bf16[4,2,16,768]{3,2,1,0:T(8,128)(2,1)S(1)}, u32[]{:S(2)}, u32[]{:S(2)}) collective-permute-start(bf16[4,2,16,768]{3,2,1,0:T(8,128)(2,1)S(1)} %get-tuple-element.100), channel_id=1, source_target_pairs={{0,16},{1,17},{2,18},{3,19},{4,20},{5,21},{6,22},{7,23},{8,24},{9,... | collective-permute-start | bytes 589832 | tf_op jit(solution)/shard_map/ppermute | solution.py:134
  103.7 7.6 %collective-permute-start.19 = (bf16[4,2,16,768]{3,2,1,0:T(8,128)(2,1)S(1)}, bf16[4,2,16,768]{3,2,1,0:T(8,128)(2,1)S(1)}, u32[]{:S(2)}, u32[]{:S(2)}) collective-permute-start(bf16[4,2,16,768]{3,2,1,0:T(8,128)(2,1)S(1)} %get-tuple-element.101), channel_id=1, source_target_pairs={{0,24},{1,25},{2,26},{3,27},{4,28},{5,29},{6,30},{7,31},{8,16},{9,... | collective-permute-start | bytes 589832 | tf_op jit(solution)/shard_map/ppermute | solution.py:134
  114.3 0.7 copy-start.6
  115.0 18.6 %collective-permute-start.20 = (bf16[2,16,1792]{2,1,0:T(8,128)(2,1)}, bf16[2,16,1792]{2,1,0:T(8,128)(2,1)S(1)}, u32[]{:S(2)}, u32[]{:S(2)}) collective-permute-start(bf16[2,16,1792]{2,1,0:T(8,128)(2,1)} %get-tuple-element.110), channel_id=1, source_target_pairs={{0,8},{1,9},{2,10},{3,11},{4,12},{5,13},{6,14},{7,15},{8,0},{9,1},... | collective-permute-start | bytes 344072 | tf_op jit(solution)/shard_map/ppermute | solution.py:134
  116.5 17.1 %collective-permute-start.21 = (bf16[2,16,1792]{2,1,0:T(8,128)(2,1)}, bf16[2,16,1792]{2,1,0:T(8,128)(2,1)}, u32[]{:S(2)}, u32[]{:S(2)}) collective-permute-start(bf16[2,16,1792]{2,1,0:T(8,128)(2,1)} %get-tuple-element.111), channel_id=1, source_target_pairs={{0,16},{1,17},{2,18},{3,19},{4,20},{5,21},{6,22},{7,23},{8,24},{9,... | collective-permute-start | bytes 344072 | tf_op jit(solution)/shard_map/ppermute | solution.py:134
  116.8 16.8 %collective-permute-start.22 = (bf16[2,16,1792]{2,1,0:T(8,128)(2,1)}, bf16[2,16,1792]{2,1,0:T(8,128)(2,1)}, u32[]{:S(2)}, u32[]{:S(2)}) collective-permute-start(bf16[2,16,1792]{2,1,0:T(8,128)(2,1)} %get-tuple-element.112), channel_id=1, source_target_pairs={{0,24},{1,25},{2,26},{3,27},{4,28},{5,29},{6,30},{7,31},{8,16},{9,... | collective-permute-start | bytes 344072 | tf_op jit(solution)/shard_map/ppermute | solution.py:134
  119.4 4.1 %collective-permute-start.23 = (bf16[2,16,768]{2,1,0:T(8,128)(2,1)S(1)}, bf16[2,16,768]{2,1,0:T(8,128)(2,1)S(1)}, u32[]{:S(2)}, u32[]{:S(2)}) collective-permute-start(bf16[2,16,768]{2,1,0:T(8,128)(2,1)S(1)} %get-tuple-element.113), channel_id=1, source_target_pairs={{0,2},{1,3},{2,0},{3,1},{4,6},{5,7},{6,4},{7,5},{8,10},{9,11},{10,... | collective-permute-start | bytes 147464 | tf_op jit(solution)/shard_map/ppermute | solution.py:134
  121.0 12.6 %collective-permute-start.24 = (bf16[2,16,768]{2,1,0:T(8,128)(2,1)}, bf16[2,16,768]{2,1,0:T(8,128)(2,1)}, u32[]{:S(2)}, u32[]{:S(2)}) collective-permute-start(bf16[2,16,768]{2,1,0:T(8,128)(2,1)} %get-tuple-element.114), channel_id=1, source_target_pairs={{0,4},{1,5},{2,6},{3,7},{4,0},{5,1},{6,2},{7,3},{8,12},{9,13},{10,... | collective-permute-start | bytes 147464 | tf_op jit(solution)/shard_map/ppermute | solution.py:134
  123.5 0.6 copy-start.8
  124.1 9.5 %collective-permute-start.25 = (bf16[2,16,768]{2,1,0:T(8,128)(2,1)}, bf16[2,16,768]{2,1,0:T(8,128)(2,1)}, u32[]{:S(2)}, u32[]{:S(2)}) collective-permute-start(bf16[2,16,768]{2,1,0:T(8,128)(2,1)} %get-tuple-element.115), channel_id=1, source_target_pairs={{0,6},{1,7},{2,4},{3,5},{4,2},{5,3},{6,0},{7,1},{8,14},{9,15},{10,... | collective-permute-start | bytes 147464 | tf_op jit(solution)/shard_map/ppermute | solution.py:134
  125.8 1.1 copy-start.2
  126.9 1.0 copy-start.4
  127.8 5.8 %copy-start.7 = (f32[2,16,1792]{2,1,0:T(8,128)S(1)}, f32[2,16,1792]{2,1,0:T(8,128)}, u32[]{:S(2)}) copy-start(f32[2,16,1792]{2,1,0:T(8,128)} %copy-done.6) | copy-start | bytes 688132
  127.8 5.8 %copy-start.9 = (bf16[2,16,768]{2,1,0:T(8,128)(2,1)S(1)}, bf16[2,16,768]{2,1,0:T(8,128)(2,1)}, u32[]{:S(2)}) copy-start(bf16[2,16,768]{2,1,0:T(8,128)(2,1)} %copy-done.8) | copy-start | bytes 147460
  127.8 6.9 %copy-start.11 = (f32[16,128]{1,0:T(8,128)S(1)}, f32[16,128]{1,0:T(8,128)}, u32[]{:S(2)}) copy-start(f32[16,128]{1,0:T(8,128)} %copy-done.10) | copy-start | bytes 24580
  134.7 1.3 collective-permute-start.26

commit v17 on v15

--- a/solution.py
+++ b/solution.py
@@ -520,10 +520,7 @@
         ],
         in_specs=[vmem_spec()] * len(pieces)
         + [hbm_spec(), pl.BlockSpec((tokens, width), lambda t: (0, jnp.maximum(t - tiles, 0)))],
-        out_specs=[
-            pl.BlockSpec((tokens, slab), whole),
-            pl.BlockSpec((n, 2 * tokens // 128, 128), lambda t: (0, 0, 0)),
-        ],
+        out_specs=[vmem_spec()] * 2,
         scratch_shapes=[
             pltpu.VMEM((tokens, depth), bf16),
             pltpu.VMEM((depth, slab), bf16),
@@ -552,17 +549,15 @@
 
     tile = half // 5
     sizes = (half * 7 // 10, half - half * 7 // 10)
-    wide_block = pl.BlockSpec((layers, CORES, rows, sizes[0]), lambda t, pos: (0, 0, 0, 0))
-    narrow_block = pl.BlockSpec((CHIPS, CORES, rows, sizes[1]), lambda t, pos: (0, 0, 0, 0))
     partial = pl.pallas_call(
         functools.partial(partial_kernel, rows),
         grid_spec=pltpu.PrefetchScalarGridSpec(
             num_scalar_prefetch=1,
             grid=(5,),
-            in_specs=[pl.BlockSpec((tokens, slab), lambda t, pos: (0, 0))] * 2
+            in_specs=[vmem_spec()] * 2
             + [pl.BlockSpec((tile, slab), lambda t, pos: (pos[0] * 5 + t, 0))]
             + [pl.BlockSpec((tile, slab), lambda t, pos: (t, 0))],
-            out_specs=[wide_block] * CHIPS + [narrow_block] * layers,
+            out_specs=[vmem_spec()] * (CHIPS + layers),
             scratch_shapes=[pltpu.VMEM((tokens, slab), bf16)],
         ),
         out_shape=[

time: 133 us -> 133 us (level)
  no operation moved by 1% of the time
where the time goes in v17:
time: 133 us
  Pallas kernels  38.1 us (29%)
  waiting for transfers between devices  36.1 us (27%)
  starting transfers between devices  32.5 us (24%)
  blocking collectives  12.6 us (9%)
  local copies, waits for them, and re-layouts  10.7 us (8%)
  other arithmetic  2 us (2%)
    ppermute x27, waiting for transfers between devices, shift(): return lax.ppermute(x, 'vocab', [(i, i ^ distance) for i in range(n)])  36.1 us
    ppermute x27, starting transfers between devices, shift(): return lax.ppermute(x, 'vocab', [(i, i ^ distance) for i in range(n)])  26.3 us
    all_to_all x1, blocking collectives, levels_plan(): lax.all_to_all(stat, 'vocab', split_axis=0, concat_axis=0, tiled=True)  12.6 us
    pallas_call x1, Pallas kernels, levels_plan(): pl.pallas_call(functools.partial(logits_kernel, rows), grid=(2 * tiles,),...  11 us
    pallas_call x1, Pallas kernels, levels_plan(): pl.pallas_call(functools.partial(head_kernel, rows), grid=(4,), in_specs=...  9.96 us
    pallas_call x1, Pallas kernels, levels_plan(): pl.pallas_call(functools.partial(partial_kernel, rows), grid_spec=pltpu.P...  9.38 us
    all_to_all x1, starting transfers between devices, levels_plan(): lax.all_to_all(payload[:, :3 - STAT_ROWS], 'vocab', split_axis=0, concat_...  6.18 us
    dynamic_slice x1, local copies, waits for them, and re-layouts, levels_plan(): lax.dynamic_slice(head_weight, ((1 - core) * half, 0), (half, slab))  5.43 us
  transfers between devices with their start and end apart: 28, of which 10 were waited for; matrix products, arithmetic and copies ran while one was open for 8% of the time, Pallas kernels for 21%

profile of v17, /device:TPU:0, one launch (start us, length us, event | category | flops | bytes accessed | tf_op | source)
XLA Modules:
  0.0 132.9 jit_solution(6241260502510794558)
XLA Ops:
  0.6 4.1 %collective-permute-start.1 = (bf16[16,5120]{1,0:T(8,128)(2,1)}, bf16[16,5120]{1,0:T(8,128)(2,1)S(1)}, u32[]{:S(2)}, u32[]{:S(2)}) collective-permute-start(bf16[16,5120]{1,0:T(8,128)(2,1)} %param.7), channel_id=1, source_target_pairs={{0,16},{1,17},{2,18},{3,19},{4,20},{5,21},{6,22},{7,23},{8,24},{9,... | collective-permute-start | bytes 491528 | tf_op jit(solution)/shard_map/ppermute | solution.py:134
  4.7 1.6 %collective-permute-start = (bf16[16,5120]{1,0:T(8,128)(2,1)}, bf16[16,5120]{1,0:T(8,128)(2,1)S(1)}, u32[]{:S(2)}, u32[]{:S(2)}) collective-permute-start(bf16[16,5120]{1,0:T(8,128)(2,1)} %param.7), channel_id=1, source_target_pairs={{0,8},{1,9},{2,10},{3,11},{4,12},{5,13},{6,14},{7,15},{8,0},{9,1},... | collective-permute-start | bytes 491528 | tf_op jit(solution)/shard_map/ppermute | solution.py:134
  6.3 0.7 add_select_fusion.1
  7.0 0.1 iota_compare_fusion
  7.1 0.2 convert_reduce_fusion
  7.3 0.1 add.85
  7.4 0.1 add.82
  7.5 0.1 add.89
  7.7 0.0 copy-start.1
  7.7 0.9 copy-done.1
  8.6 1.3 pack_teacher.1
  9.9 0.9 slice.18
  10.8 6.2 %all-to-all-start = ((bf16[32,67,128]{2,1,0:T(8,128)(2,1)}), bf16[32,67,128]{2,1,0:T(8,128)(2,1)}, u32[]{:S(2)}, u32[]{:S(2)}) async-start(bf16[32,67,128]{2,1,0:T(8,128)(2,1)} %slice.18), calls=%async_computation | async-start | bytes 1179648 | tf_op jit(solution)/shard_map/all_to_all | solution.py:482
  17.0 0.9 constant_dynamic-update-slice_fusion.3
  17.9 0.0 collective-permute-done
  17.9 0.0 collective-permute-done.1
  18.0 1.8 %collective-permute-start.4 = (bf16[64,5120]{1,0:T(8,128)(2,1)S(1)}, bf16[64,5120]{1,0:T(8,128)(2,1)S(1)}, u32[]{:S(2)}, u32[]{:S(2)}) collective-permute-start(bf16[64,5120]{1,0:T(8,128)(2,1)S(1)} %constant_dynamic-update-slice_fusion.refs_0_), channel_id=1, source_target_pairs={{0,4},{1,5},{2,6},{3,7},{4,0},{5,1},{6,2},{7,3},{8,12},{9,13},{10,... | collective-permute-start | bytes 1966088 | tf_op jit(solution)/shard_map/ppermute | solution.py:134
  19.8 1.5 %collective-permute-start.3 = (bf16[64,5120]{1,0:T(8,128)(2,1)S(1)}, bf16[64,5120]{1,0:T(8,128)(2,1)S(1)}, u32[]{:S(2)}, u32[]{:S(2)}) collective-permute-start(bf16[64,5120]{1,0:T(8,128)(2,1)S(1)} %constant_dynamic-update-slice_fusion.refs_0_), channel_id=1, source_target_pairs={{0,2},{1,3},{2,0},{3,1},{4,6},{5,7},{6,4},{7,5},{8,10},{9,11},{10,... | collective-permute-start | bytes 1966088 | tf_op jit(solution)/shard_map/ppermute | solution.py:134
  21.2 0.2 select_reduce_fusion
  21.5 0.0 copy-start.2
  21.5 0.0 copy-start.3
  21.5 5.4 %constant_dynamic-slice_fusion = bf16[2560,1024]{1,0:T(8,128)(2,1)} fusion(bf16[5120,1024]{1,0:T(8,128)(2,1)} %w_ref.1, s32[]{:T(128)S(6)} %select_n.57), kind=kLoop, calls=%fused_computation.27 | loop fusion | bytes 10485764 | tf_op jit(solution)/shard_map/dynamic_slice | solution.py:505
  26.9 13.5 %collective-permute-done.4.refs_2_ = bf16[64,5120]{1,0:T(8,128)(2,1)S(1)} collective-permute-done((bf16[64,5120]{1,0:T(8,128)(2,1)S(1)}, bf16[64,5120]{1,0:T(8,128)(2,1)S(1)}, u32[]{:S(2)}, u32[]{:S(2)}) %collective-permute-start.4) | collective-permute-done | bytes 655392 | tf_op jit(solution)/shard_map/ppermute | solution.py:134
  40.4 0.8 slice.17
  41.2 1.2 collective-permute-start.6
  42.3 0.8 slice.16
  43.1 0.4 collective-permute-start.5
  43.5 0.5 collective-permute-start.8
  44.0 0.1 pad_add_fusion.refs_0_.core_ref
  44.1 4.9 %teacher_prob.1 = (f32[512,1024]{1,0:T(8,128)S(1)}, f32[16,128]{1,0:T(8,128)S(1)}) custom-call(s32[4]{0:T(128)S(1)} %pad_add_fusion.refs_0_.core_ref, s32[4,4]{1,0:T(4,128)S(1)} %broadcast_add_fusion.1.refs_1_, bf16[32,67,128]{2,1,0:T(8,128)(2,1)} %all-to-all-done.refs_2_, s32[4,1,128]{2,1,0:T(1,128)S(1)} %bitcast.9, f32[4,1,128]{2,1,0:T(1,128)S(1)} %bitcast.10), custom_call_target="tpu_custom_call" | custom-call | flops 1 | bytes 1 | tf_op jit(solution)/shard_map/teacher_prob/pallas_call | solution.py:486
  49.0 2.2 %collective-permute-done.6.refs_4_ = bf16[64,2560]{1,0:T(8,128)(2,1)} collective-permute-done((bf16[64,2560]{1,0:T(8,128)(2,1)}, bf16[64,2560]{1,0:T(8,128)(2,1)}, u32[]{:S(2)}, u32[]{:S(2)}) %collective-permute-start.6) | collective-permute-done | bytes 327712 | tf_op jit(solution)/shard_map/ppermute | solution.py:134
  51.1 1.5 %collective-permute-done.5.refs_3_ = bf16[64,2560]{1,0:T(8,128)(2,1)} collective-permute-done((bf16[64,2560]{1,0:T(8,128)(2,1)}, bf16[64,2560]{1,0:T(8,128)(2,1)}, u32[]{:S(2)}, u32[]{:S(2)}) %collective-permute-start.5) | collective-permute-done | bytes 327712 | tf_op jit(solution)/shard_map/ppermute | solution.py:134
  52.6 0.5 collective-permute-start.11
  53.2 1.3 collective-permute-done.10.refs_8_
  54.5 0.5 collective-permute-done.11.refs_9_
  55.0 0.1 collective-permute-start.13
  55.1 11.0 %logits.1 = (f32[512,1024]{1,0:T(8,128)S(1)}, f32[32,8,128]{2,1,0:T(8,128)S(1)}) custom-call(bf16[64,5120]{1,0:T(8,128)(2,1)S(1)} %constant_dynamic-update-slice_fusion.refs_0_, bf16[64,5120]{1,0:T(8,128)(2,1)S(1)} %collective-permute-done.3.refs_1_, bf16[64,5120]{1,0:T(8,128)(2,1)S(1)} %collective-permute-done.4.refs_2_, ...), custom_call_target="tpu_custom_call" | custom-call | flops 1 | bytes 1 | tf_op jit(solution)/shard_map/logits/pallas_call | solution.py:514
  66.1 12.6 %all_to_all.10.refs_1_ = f32[32,8,128]{2,1,0:T(8,128)S(1)} all-to-all(f32[32,8,128]{2,1,0:T(8,128)S(1)} %get-tuple-element.73), channel_id=1, replica_groups=mesh['vocab'=32] {'vocab'}, dimensions={0} | all-to-all | bytes 262144 | tf_op jit(solution)/shard_map/all_to_all | solution.py:534
  78.6 1.3 grad_logits.1
  79.9 0.3 collective-permute-start.12
  80.2 2.4 %collective-permute-done.12.sib_ref = bf16[512,1024]{1,0:T(8,128)(2,1)S(1)} collective-permute-done((bf16[512,1024]{1,0:T(8,128)(2,1)S(1)}, bf16[512,1024]{1,0:T(8,128)(2,1)S(1)}, u32[]{:S(2)}, u32[]{:S(2)}) %collective-permute-start.12) | collective-permute-done | bytes 1048608 | tf_op jit(solution)/shard_map/ppermute | solution.py:134
  82.7 9.4 %grad_hidden_partial.1 = (f32[4,2,16,1792]{3,2,1,0:T(8,128)S(1)}, bf16[4,2,16,1792]{3,2,1,0:T(8,128)(2,1)}, bf16[4,2,16,1792]{3,2,1,0:T(8,128)(2,1)S(1)}, bf16[4...) custom-call(s32[4]{0:T(128)S(1)} %pad_add_fusion.refs_0_.core_ref, ...), custom_call_target="tpu_custom_call" | custom-call | flops 1 | bytes 1 | tf_op jit(solution)/shard_map/grad_hidden_partial/pallas_call | solution.py:552
  92.1 0.4 collective-permute-start.14
  92.5 1.0 collective-permute-start.15
  93.5 2.0 %collective-permute-start.16 = (bf16[4,2,16,1792]{3,2,1,0:T(8,128)(2,1)S(1)}, bf16[4,2,16,1792]{3,2,1,0:T(8,128)(2,1)S(1)}, u32[]{:S(2)}, u32[]{:S(2)}) collective-permute-start(bf16[4,2,16,1792]{3,2,1,0:T(8,128)(2,1)S(1)} %get-tuple-element.89), channel_id=1, source_target_pairs={{0,6},{1,7},{2,4},{3,5},{4,2},{5,3},{6,0},{7,1},{8,14},{9,15},{10,... | collective-permute-start | bytes 1376264 | tf_op jit(solution)/shard_map/ppermute | solution.py:134
  95.5 0.6 collective-permute-start.17
  96.2 1.3 collective-permute-start.18
  97.5 7.5 %collective-permute-done.17.refs_5_ = bf16[4,2,16,768]{3,2,1,0:T(8,128)(2,1)S(1)} collective-permute-done((bf16[4,2,16,768]{3,2,1,0:T(8,128)(2,1)S(1)}, bf16[4,2,16,768]{3,2,1,0:T(8,128)(2,1)S(1)}, u32[]{:S(2)}, u32[]{:S(2)}) %collective-permute-start.17) | collective-permute-done | bytes 196640 | tf_op jit(solution)/shard_map/ppermute | solution.py:134
  104.9 1.8 %collective-permute-start.19 = (bf16[4,2,16,768]{3,2,1,0:T(8,128)(2,1)S(1)}, bf16[4,2,16,768]{3,2,1,0:T(8,128)(2,1)S(1)}, u32[]{:S(2)}, u32[]{:S(2)}) collective-permute-start(bf16[4,2,16,768]{3,2,1,0:T(8,128)(2,1)S(1)} %get-tuple-element.92), channel_id=1, source_target_pairs={{0,24},{1,25},{2,26},{3,27},{4,28},{5,29},{6,30},{7,31},{8,16},{9,... | collective-permute-start | bytes 589832 | tf_op jit(solution)/shard_map/ppermute | solution.py:134
  106.8 10.0 %grad_head.1 = bf16[5120,1024]{1,0:T(8,128)(2,1)} custom-call(bf16[64,5120]{1,0:T(8,128)(2,1)S(1)} %constant_dynamic-update-slice_fusion.refs_0_, bf16[64,5120]{1,0:T(8,128)(2,1)S(1)} %collective-permute-done.3.refs_1_, bf16[64,5120]{1,0:T(8,128)(2,1)S(1)} %collective-permute-done.4.refs_2_, bf16[64,2560]{1,0:T(8,128)(2,1)} %collective-permute-done.5.refs_3_, ...), custom_call_target="tpu_custom_call" | custom-call | flops 1 | bytes 1 | tf_op jit(solution)/shard_map/grad_head/pallas_call | solution.py:576
  116.8 0.3 first_sum.1
  117.1 0.1 collective-permute-start.20
  117.2 2.5 %collective-permute-start.21 = (bf16[2,16,1792]{2,1,0:T(8,128)(2,1)S(1)}, bf16[2,16,1792]{2,1,0:T(8,128)(2,1)S(1)}, u32[]{:S(2)}, u32[]{:S(2)}) collective-permute-start(bf16[2,16,1792]{2,1,0:T(8,128)(2,1)S(1)} %get-tuple-element.105), channel_id=1, source_target_pairs={{0,16},{1,17},{2,18},{3,19},{4,20},{5,21},{6,22},{7,23},{8,24},{9,... | collective-permute-start | bytes 344072 | tf_op jit(solution)/shard_map/ppermute | solution.py:134
  119.7 1.8 %collective-permute-start.22 = (bf16[2,16,1792]{2,1,0:T(8,128)(2,1)S(1)}, bf16[2,16,1792]{2,1,0:T(8,128)(2,1)S(1)}, u32[]{:S(2)}, u32[]{:S(2)}) collective-permute-start(bf16[2,16,1792]{2,1,0:T(8,128)(2,1)S(1)} %get-tuple-element.106), channel_id=1, source_target_pairs={{0,24},{1,25},{2,26},{3,27},{4,28},{5,29},{6,30},{7,31},{8,16},{9,... | collective-permute-start | bytes 344072 | tf_op jit(solution)/shard_map/ppermute | solution.py:134
  121.5 0.5 collective-permute-start.23
  122.0 1.2 collective-permute-start.24
  123.3 2.5 %collective-permute-done.23.refs_5_ = bf16[2,16,768]{2,1,0:T(8,128)(2,1)S(1)} collective-permute-done((bf16[2,16,768]{2,1,0:T(8,128)(2,1)S(1)}, bf16[2,16,768]{2,1,0:T(8,128)(2,1)S(1)}, u32[]{:S(2)}, u32[]{:S(2)}) %collective-permute-start.23) | collective-permute-done | bytes 49184 | tf_op jit(solution)/shard_map/ppermute | solution.py:134
  125.8 1.0 collective-permute-start.25
  126.8 4.0 %collective-permute-done.25.refs_7_ = bf16[2,16,768]{2,1,0:T(8,128)(2,1)S(1)} collective-permute-done((bf16[2,16,768]{2,1,0:T(8,128)(2,1)S(1)}, bf16[2,16,768]{2,1,0:T(8,128)(2,1)S(1)}, u32[]{:S(2)}, u32[]{:S(2)}) %collective-permute-start.25) | collective-permute-done | bytes 49184 | tf_op jit(solution)/shard_map/ppermute | solution.py:134
  130.8 0.1 last_sum.1
  130.9 0.1 collective-permute-start.26
  131.0 0.6 slice_reduce_fusion
  131.6 0.6 collective-permute-done.26
  132.3 0.7 pad_maximum_fusion
  (36 shorter events, 0.1 us)
Async XLA Ops:
  0.6 17.3 %collective-permute-start.1 = (bf16[16,5120]{1,0:T(8,128)(2,1)}, bf16[16,5120]{1,0:T(8,128)(2,1)S(1)}, u32[]{:S(2)}, u32[]{:S(2)}) collective-permute-start(bf16[16,5120]{1,0:T(8,128)(2,1)} %param.7), channel_id=1, source_target_pairs={{0,16},{1,17},{2,18},{3,19},{4,20},{5,21},{6,22},{7,23},{8,24},{9,... | collective-permute-start | bytes 491528 | tf_op jit(solution)/shard_map/ppermute | solution.py:134
  4.7 13.2 %collective-permute-start = (bf16[16,5120]{1,0:T(8,128)(2,1)}, bf16[16,5120]{1,0:T(8,128)(2,1)S(1)}, u32[]{:S(2)}, u32[]{:S(2)}) collective-permute-start(bf16[16,5120]{1,0:T(8,128)(2,1)} %param.7), channel_id=1, source_target_pairs={{0,8},{1,9},{2,10},{3,11},{4,12},{5,13},{6,14},{7,15},{8,0},{9,1},... | collective-permute-start | bytes 491528 | tf_op jit(solution)/shard_map/ppermute | solution.py:134
  6.3 11.7 %collective-permute-start.2 = (bf16[16,5120]{1,0:T(8,128)(2,1)}, bf16[16,5120]{1,0:T(8,128)(2,1)S(1)}, u32[]{:S(2)}, u32[]{:S(2)}) collective-permute-start(bf16[16,5120]{1,0:T(8,128)(2,1)} %param.7), channel_id=1, source_target_pairs={{0,24},{1,25},{2,26},{3,27},{4,28},{5,29},{6,30},{7,31},{8,16},{9,... | collective-permute-start | bytes 491528 | tf_op jit(solution)/shard_map/ppermute | solution.py:134
  7.7 1.0 copy-start.1
  10.8 33.3 %all-to-all-start = ((bf16[32,67,128]{2,1,0:T(8,128)(2,1)}), bf16[32,67,128]{2,1,0:T(8,128)(2,1)}, u32[]{:S(2)}, u32[]{:S(2)}) async-start(bf16[32,67,128]{2,1,0:T(8,128)(2,1)} %slice.18), calls=%async_computation | async-start | bytes 1179648 | tf_op jit(solution)/shard_map/all_to_all | solution.py:482
  18.0 22.4 %collective-permute-start.4 = (bf16[64,5120]{1,0:T(8,128)(2,1)S(1)}, bf16[64,5120]{1,0:T(8,128)(2,1)S(1)}, u32[]{:S(2)}, u32[]{:S(2)}) collective-permute-start(bf16[64,5120]{1,0:T(8,128)(2,1)S(1)} %constant_dynamic-update-slice_fusion.refs_0_), channel_id=1, source_target_pairs={{0,4},{1,5},{2,6},{3,7},{4,0},{5,1},{6,2},{7,3},{8,12},{9,13},{10,... | collective-permute-start | bytes 1966088 | tf_op jit(solution)/shard_map/ppermute | solution.py:134
  19.8 22.6 %collective-permute-start.3 = (bf16[64,5120]{1,0:T(8,128)(2,1)S(1)}, bf16[64,5120]{1,0:T(8,128)(2,1)S(1)}, u32[]{:S(2)}, u32[]{:S(2)}) collective-permute-start(bf16[64,5120]{1,0:T(8,128)(2,1)S(1)} %constant_dynamic-update-slice_fusion.refs_0_), channel_id=1, source_target_pairs={{0,2},{1,3},{2,0},{3,1},{4,6},{5,7},{6,4},{7,5},{8,10},{9,11},{10,... | collective-permute-start | bytes 1966088 | tf_op jit(solution)/shard_map/ppermute | solution.py:134
  21.5 22.6 %copy-start.2 = (s32[4,128]{1,0:T(4,128)S(1)}, s32[4,128]{1,0:T(4,128)}, u32[]{:S(2)}) copy-start(s32[4,128]{1,0:T(4,128)} %param.11) | copy-start | bytes 6148
  21.5 22.6 %copy-start.3 = (f32[512]{0:T(512)S(1)}, f32[512]{0:T(512)}, u32[]{:S(2)}) copy-start(f32[512]{0:T(512)} %param.12) | copy-start | bytes 6148
  26.9 26.2 %collective-permute-start.7 = (bf16[64,5120]{1,0:T(8,128)(2,1)S(1)}, bf16[64,5120]{1,0:T(8,128)(2,1)S(1)}, u32[]{:S(2)}, u32[]{:S(2)}) collective-permute-start(bf16[64,5120]{1,0:T(8,128)(2,1)S(1)} %constant_dynamic-update-slice_fusion.refs_0_), channel_id=1, source_target_pairs={{0,1},{1,0},{2,3},{3,2},{4,5},{5,4},{6,7},{7,6},{8,9},{9,8},{10,11... | collective-permute-start | bytes 1966088 | tf_op jit(solution)/shard_map/ppermute | solution.py:134
  41.2 10.0 %collective-permute-start.6 = (bf16[64,2560]{1,0:T(8,128)(2,1)}, bf16[64,2560]{1,0:T(8,128)(2,1)}, u32[]{:S(2)}, u32[]{:S(2)}) collective-permute-start(bf16[64,2560]{1,0:T(8,128)(2,1)} %slice.17), channel_id=1, source_target_pairs={{0,2},{1,3},{2,0},{3,1},{4,6},{5,7},{6,4},{7,5},{8,10},{9,11},{10,... | collective-permute-start | bytes 983048 | tf_op jit(solution)/shard_map/ppermute | solution.py:134
  43.1 9.6 %collective-permute-start.5 = (bf16[64,2560]{1,0:T(8,128)(2,1)}, bf16[64,2560]{1,0:T(8,128)(2,1)}, u32[]{:S(2)}, u32[]{:S(2)}) collective-permute-start(bf16[64,2560]{1,0:T(8,128)(2,1)} %slice.16), channel_id=1, source_target_pairs={{0,4},{1,5},{2,6},{3,7},{4,0},{5,1},{6,2},{7,3},{8,12},{9,13},{10,... | collective-permute-start | bytes 983048 | tf_op jit(solution)/shard_map/ppermute | solution.py:134
  43.5 11.5 %collective-permute-start.9 = (bf16[64,5120]{1,0:T(8,128)(2,1)S(1)}, bf16[64,5120]{1,0:T(8,128)(2,1)S(1)}, u32[]{:S(2)}, u32[]{:S(2)}) collective-permute-start(bf16[64,5120]{1,0:T(8,128)(2,1)S(1)} %collective-permute-done.4.refs_2_), channel_id=1, source_target_pairs={{0,1},{1,0},{2,3},{3,2},{4,5},{5,4},{6,7},{7,6},{8,9},{9,8},{10,11... | collective-permute-start | bytes 1966088 | tf_op jit(solution)/shard_map/ppermute | solution.py:134
  43.5 11.5 %collective-permute-start.8 = (bf16[64,5120]{1,0:T(8,128)(2,1)S(1)}, bf16[64,5120]{1,0:T(8,128)(2,1)}, u32[]{:S(2)}, u32[]{:S(2)}) collective-permute-start(bf16[64,5120]{1,0:T(8,128)(2,1)S(1)} %collective-permute-done.3.refs_1_), channel_id=1, source_target_pairs={{0,1},{1,0},{2,3},{3,2},{4,5},{5,4},{6,7},{7,6},{8,9},{9,8},{10,11... | collective-permute-start | bytes 1966088 | tf_op jit(solution)/shard_map/ppermute | solution.py:134
  52.6 26.0 %copy-start.4 = (f32[512]{0:T(512)S(1)}, f32[512]{0:T(512)}, u32[]{:S(2)}) copy-start(f32[512]{0:T(512)} %param.13) | copy-start | bytes 6148
  52.6 1.8 %collective-permute-start.10 = (bf16[64,2560]{1,0:T(8,128)(2,1)}, bf16[64,2560]{1,0:T(8,128)(2,1)S(1)}, u32[]{:S(2)}, u32[]{:S(2)}) collective-permute-start(bf16[64,2560]{1,0:T(8,128)(2,1)} %collective-permute-done.5.refs_3_), channel_id=1, source_target_pairs={{0,1},{1,0},{2,3},{3,2},{4,5},{5,4},{6,7},{7,6},{8,9},{9,8},{10,11... | collective-permute-start | bytes 983048 | tf_op jit(solution)/shard_map/ppermute | solution.py:134
  52.6 2.3 %collective-permute-start.11 = (bf16[64,2560]{1,0:T(8,128)(2,1)}, bf16[64,2560]{1,0:T(8,128)(2,1)S(1)}, u32[]{:S(2)}, u32[]{:S(2)}) collective-permute-start(bf16[64,2560]{1,0:T(8,128)(2,1)} %collective-permute-done.6.refs_4_), channel_id=1, source_target_pairs={{0,1},{1,0},{2,3},{3,2},{4,5},{5,4},{6,7},{7,6},{8,9},{9,8},{10,11... | collective-permute-start | bytes 983048 | tf_op jit(solution)/shard_map/ppermute | solution.py:134
  55.0 27.7 %collective-permute-start.13 = (bf16[2560,1024]{1,0:T(8,128)(2,1)}, bf16[2560,1024]{1,0:T(8,128)(2,1)S(1)}, u32[]{:S(2)}, u32[]{:S(2)}) collective-permute-start(bf16[2560,1024]{1,0:T(8,128)(2,1)} %constant_dynamic-slice_fusion), channel_id=1, source_target_pairs={{0,1},{1,0},{2,3},{3,2},{4,5},{5,4},{6,7},{7,6},{8,9},{9,8},{10,11... | collective-permute-start | bytes 15728648 | tf_op jit(solution)/shard_map/ppermute | solution.py:134
  79.9 12.1 %copy-start = (bf16[512,1024]{1,0:T(8,128)(2,1)}, bf16[512,1024]{1,0:T(8,128)(2,1)S(1)}, u32[]{:S(2)}) copy-start(bf16[512,1024]{1,0:T(8,128)(2,1)S(1)} %get-tuple-element.93.grad_ref.refs_10_) | copy-start | bytes 3145732
  79.9 2.7 %collective-permute-start.12 = (bf16[512,1024]{1,0:T(8,128)(2,1)S(1)}, bf16[512,1024]{1,0:T(8,128)(2,1)S(1)}, u32[]{:S(2)}, u32[]{:S(2)}) collective-permute-start(bf16[512,1024]{1,0:T(8,128)(2,1)S(1)} %get-tuple-element.93.grad_ref.refs_10_), channel_id=1, source_target_pairs={{0,1},{1,0},{2,3},{3,2},{4,5},{5,4},{6,7},{7,6},{8,9},{9,8},{10,11... | collective-permute-start | bytes 3145736 | tf_op jit(solution)/shard_map/ppermute | solution.py:134
  92.1 24.7 %collective-permute-start.14 = (bf16[4,2,16,1792]{3,2,1,0:T(8,128)(2,1)}, bf16[4,2,16,1792]{3,2,1,0:T(8,128)(2,1)S(1)}, u32[]{:S(2)}, u32[]{:S(2)}) collective-permute-start(bf16[4,2,16,1792]{3,2,1,0:T(8,128)(2,1)} %get-tuple-element.87), channel_id=1, source_target_pairs={{0,2},{1,3},{2,0},{3,1},{4,6},{5,7},{6,4},{7,5},{8,10},{9,11},{10,... | collective-permute-start | bytes 1376264 | tf_op jit(solution)/shard_map/ppermute | solution.py:134
  92.5 24.3 %collective-permute-start.15 = (bf16[4,2,16,1792]{3,2,1,0:T(8,128)(2,1)S(1)}, bf16[4,2,16,1792]{3,2,1,0:T(8,128)(2,1)S(1)}, u32[]{:S(2)}, u32[]{:S(2)}) collective-permute-start(bf16[4,2,16,1792]{3,2,1,0:T(8,128)(2,1)S(1)} %get-tuple-element.88), channel_id=1, source_target_pairs={{0,4},{1,5},{2,6},{3,7},{4,0},{5,1},{6,2},{7,3},{8,12},{9,13},{10,... | collective-permute-start | bytes 1376264 | tf_op jit(solution)/shard_map/ppermute | solution.py:134
  93.5 23.3 %collective-permute-start.16 = (bf16[4,2,16,1792]{3,2,1,0:T(8,128)(2,1)S(1)}, bf16[4,2,16,1792]{3,2,1,0:T(8,128)(2,1)S(1)}, u32[]{:S(2)}, u32[]{:S(2)}) collective-permute-start(bf16[4,2,16,1792]{3,2,1,0:T(8,128)(2,1)S(1)} %get-tuple-element.89), channel_id=1, source_target_pairs={{0,6},{1,7},{2,4},{3,5},{4,2},{5,3},{6,0},{7,1},{8,14},{9,15},{10,... | collective-permute-start | bytes 1376264 | tf_op jit(solution)/shard_map/ppermute | solution.py:134
  95.5 9.4 %collective-permute-start.17 = (bf16[4,2,16,768]{3,2,1,0:T(8,128)(2,1)S(1)}, bf16[4,2,16,768]{3,2,1,0:T(8,128)(2,1)S(1)}, u32[]{:S(2)}, u32[]{:S(2)}) collective-permute-start(bf16[4,2,16,768]{3,2,1,0:T(8,128)(2,1)S(1)} %get-tuple-element.90), channel_id=1, source_target_pairs={{0,8},{1,9},{2,10},{3,11},{4,12},{5,13},{6,14},{7,15},{8,0},{9,1},... | collective-permute-start | bytes 589832 | tf_op jit(solution)/shard_map/ppermute | solution.py:134
  96.2 20.6 %collective-permute-start.18 = (bf16[4,2,16,768]{3,2,1,0:T(8,128)(2,1)S(1)}, bf16[4,2,16,768]{3,2,1,0:T(8,128)(2,1)S(1)}, u32[]{:S(2)}, u32[]{:S(2)}) collective-permute-start(bf16[4,2,16,768]{3,2,1,0:T(8,128)(2,1)S(1)} %get-tuple-element.91), channel_id=1, source_target_pairs={{0,16},{1,17},{2,18},{3,19},{4,20},{5,21},{6,22},{7,23},{8,24},{9,... | collective-permute-start | bytes 589832 | tf_op jit(solution)/shard_map/ppermute | solution.py:134
  104.9 11.8 %collective-permute-start.19 = (bf16[4,2,16,768]{3,2,1,0:T(8,128)(2,1)S(1)}, bf16[4,2,16,768]{3,2,1,0:T(8,128)(2,1)S(1)}, u32[]{:S(2)}, u32[]{:S(2)}) collective-permute-start(bf16[4,2,16,768]{3,2,1,0:T(8,128)(2,1)S(1)} %get-tuple-element.92), channel_id=1, source_target_pairs={{0,24},{1,25},{2,26},{3,27},{4,28},{5,29},{6,30},{7,31},{8,16},{9,... | collective-permute-start | bytes 589832 | tf_op jit(solution)/shard_map/ppermute | solution.py:134
  117.1 13.7 %collective-permute-start.20 = (bf16[2,16,1792]{2,1,0:T(8,128)(2,1)S(1)}, bf16[2,16,1792]{2,1,0:T(8,128)(2,1)S(1)}, u32[]{:S(2)}, u32[]{:S(2)}) collective-permute-start(bf16[2,16,1792]{2,1,0:T(8,128)(2,1)S(1)} %get-tuple-element.104), channel_id=1, source_target_pairs={{0,8},{1,9},{2,10},{3,11},{4,12},{5,13},{6,14},{7,15},{8,0},{9,1},... | collective-permute-start | bytes 344072 | tf_op jit(solution)/shard_map/ppermute | solution.py:134
  117.2 13.6 %collective-permute-start.21 = (bf16[2,16,1792]{2,1,0:T(8,128)(2,1)S(1)}, bf16[2,16,1792]{2,1,0:T(8,128)(2,1)S(1)}, u32[]{:S(2)}, u32[]{:S(2)}) collective-permute-start(bf16[2,16,1792]{2,1,0:T(8,128)(2,1)S(1)} %get-tuple-element.105), channel_id=1, source_target_pairs={{0,16},{1,17},{2,18},{3,19},{4,20},{5,21},{6,22},{7,23},{8,24},{9,... | collective-permute-start | bytes 344072 | tf_op jit(solution)/shard_map/ppermute | solution.py:134
  119.7 11.1 %collective-permute-start.22 = (bf16[2,16,1792]{2,1,0:T(8,128)(2,1)S(1)}, bf16[2,16,1792]{2,1,0:T(8,128)(2,1)S(1)}, u32[]{:S(2)}, u32[]{:S(2)}) collective-permute-start(bf16[2,16,1792]{2,1,0:T(8,128)(2,1)S(1)} %get-tuple-element.106), channel_id=1, source_target_pairs={{0,24},{1,25},{2,26},{3,27},{4,28},{5,29},{6,30},{7,31},{8,16},{9,... | collective-permute-start | bytes 344072 | tf_op jit(solution)/shard_map/ppermute | solution.py:134
  121.5 4.3 %collective-permute-start.23 = (bf16[2,16,768]{2,1,0:T(8,128)(2,1)S(1)}, bf16[2,16,768]{2,1,0:T(8,128)(2,1)S(1)}, u32[]{:S(2)}, u32[]{:S(2)}) collective-permute-start(bf16[2,16,768]{2,1,0:T(8,128)(2,1)S(1)} %get-tuple-element.108), channel_id=1, source_target_pairs={{0,2},{1,3},{2,0},{3,1},{4,6},{5,7},{6,4},{7,5},{8,10},{9,11},{10,... | collective-permute-start | bytes 147464 | tf_op jit(solution)/shard_map/ppermute | solution.py:134
  122.0 4.8 %collective-permute-start.24 = (bf16[2,16,768]{2,1,0:T(8,128)(2,1)S(1)}, bf16[2,16,768]{2,1,0:T(8,128)(2,1)S(1)}, u32[]{:S(2)}, u32[]{:S(2)}) collective-permute-start(bf16[2,16,768]{2,1,0:T(8,128)(2,1)S(1)} %get-tuple-element.109), channel_id=1, source_target_pairs={{0,4},{1,5},{2,6},{3,7},{4,0},{5,1},{6,2},{7,3},{8,12},{9,13},{10,... | collective-permute-start | bytes 147464 | tf_op jit(solution)/shard_map/ppermute | solution.py:134
  125.8 5.0 %collective-permute-start.25 = (bf16[2,16,768]{2,1,0:T(8,128)(2,1)S(1)}, bf16[2,16,768]{2,1,0:T(8,128)(2,1)S(1)}, u32[]{:S(2)}, u32[]{:S(2)}) collective-permute-start(bf16[2,16,768]{2,1,0:T(8,128)(2,1)S(1)} %get-tuple-element.110), channel_id=1, source_target_pairs={{0,6},{1,7},{2,4},{3,5},{4,2},{5,3},{6,0},{7,1},{8,14},{9,15},{10,... | collective-permute-start | bytes 147464 | tf_op jit(solution)/shard_map/ppermute | solution.py:134
  130.9 1.3 %collective-permute-start.26 = (bf16[16,2560]{1,0:T(8,128)(2,1)S(1)}, bf16[16,2560]{1,0:T(8,128)(2,1)S(1)}, u32[]{:S(2)}, u32[]{:S(2)}) collective-permute-start(bf16[16,2560]{1,0:T(8,128)(2,1)S(1)} %get-tuple-element.112), channel_id=1, source_target_pairs={{0,1},{1,0},{2,3},{3,2},{4,5},{5,4},{6,7},{7,6},{8,9},{9,8},{10,11... | collective-permute-start | bytes 245768 | tf_op jit(solution)/shard_map/ppermute | solution.py:134

commit v18 on v17

--- a/solution.py
+++ b/solution.py
@@ -205,6 +205,19 @@
                 piece = mine[CHIPS]
                 columns = slice(out_ref.shape[1] - piece.shape[1], out_ref.shape[1])
                 out_ref[at, columns] = piece[span, :]
+
+
+def cut_kernel(x_ref, y_ref, low_ref, high_ref):
+    half = low_ref.shape[1]
+    low_ref[...] = x_ref[:, :half]
+    high_ref[...] = y_ref[:, half:]
+
+
+def join_kernel(pos_ref, mine_ref, other_ref, out_ref):
+    half = mine_ref.shape[1]
+    own = pos_ref[0]
+    out_ref[:, pl.ds(pl.multiple_of(own * half, half), half)] = mine_ref[...]
+    out_ref[:, pl.ds(pl.multiple_of((1 - own) * half, half), half)] = other_ref[...]
 
 
 def logits_kernel(rows, *refs):
@@ -477,7 +490,18 @@
     column = jnp.concatenate(column, axis=0)
     X, Y = CORES, 2 * CORES
     plane = [column, shift(column, X), shift(column, Y)]
-    plane += [shift(plane[1][:, :half], Y), shift(plane[2][:, half:], X)]
+    sent_w = lax.dynamic_slice(head_weight, ((1 - core) * half, 0), (half, slab))
+    plane[1], plane[2], sent_w = lax.optimization_barrier((plane[1], plane[2], sent_w))
+    low, high = pl.pallas_call(
+        cut_kernel,
+        in_specs=[vmem_spec()] * 2,
+        out_specs=[vmem_spec()] * 2,
+        out_shape=[jax.ShapeDtypeStruct((layers * rows, half), bf16)] * 2,
+        compiler_params=kernel_params(),
+        cost_estimate=LIGHT,
+        name="cut_halves",
+    )(plane[1], plane[2])
+    plane += [shift(low, Y), shift(high, X)]
     payload, place = pack_teacher(teacher_logits, block_lists, slab // side)
     arrived = lax.all_to_all(
         payload[:, : 3 - STAT_ROWS], "vocab", split_axis=0, concat_axis=0, tiled=True
@@ -502,8 +526,7 @@
         tail_mass.reshape(blocks, 1, side),
     )
 
-    sent_w = lax.dynamic_slice(head_weight, ((1 - core) * half, 0), (half, slab))
-    plane[-2], plane[-1], prob, sent_w = lax.optimization_barrier((plane[-2], plane[-1], prob, sent_w))
+    plane[-2], plane[-1], prob = lax.optimization_barrier((plane[-2], plane[-1], prob))
     pieces = plane + [shift(piece, 1) for piece in plane]
     pieces, sent_w = lax.optimization_barrier((pieces, sent_w))
     sib_w = shift(sent_w, 1)
@@ -616,8 +639,16 @@
     )(summed[0], *wide_sums, summed[layers], *narrow_sums)
     other = shift(theirs, 1)
 
-    low, high = jnp.where(core == 0, mine, other), jnp.where(core == 0, other, mine)
-    return loss[:, 0], grad_head, jnp.concatenate([low, high], axis=1)
+    grad_hidden = pl.pallas_call(
+        join_kernel,
+        in_specs=[smem_spec()] + [vmem_spec()] * 2,
+        out_specs=vmem_spec(),
+        out_shape=jax.ShapeDtypeStruct((rows, depth), bf16),
+        compiler_params=kernel_params(),
+        cost_estimate=LIGHT,
+        name="join_halves",
+    )(pos, mine, other)
+    return loss[:, 0], grad_head, grad_hidden
 
 
 def fits_levels(hidden_states, teacher_logits):

time: 133 us -> 134 us (level)
  Pallas kernels: 38.1 us -> 39.6 us
  local copies, waits for them, and re-layouts: 10.7 us -> 9.23 us
    pallas_call x0 -> x2, Pallas kernels: none -> 2.1 us  [the longest x1 1.22 us: levels_plan(): pl.pallas_call(join_kernel, in_specs=[smem_spec()] + [vmem_spec()] * 2, o...]
    slice x3 -> x1, local copies, waits for them, and re-layouts: 2.15 us -> 0.63 us  [levels_plan(): return (loss[:, 0], grad_head, grad_hidden)]
  transfers between devices with their start and end apart: 28 -> 28, of which waited for: 10 -> 10; matrix products, arithmetic and copies ran while one was open for 8% -> 7% of each run, Pallas kernels for 21% -> 22%
where the time goes in v18:
time: 134 us
  Pallas kernels  39.6 us (30%)
  waiting for transfers between devices  35.9 us (27%)
  starting transfers between devices  33.2 us (25%)
  blocking collectives  13.6 us (10%)
  local copies, waits for them, and re-layouts  9.23 us (7%)
    ppermute x27, waiting for transfers between devices, shift(): return lax.ppermute(x, 'vocab', [(i, i ^ distance) for i in range(n)])  35.9 us
    ppermute x27, starting transfers between devices, shift(): return lax.ppermute(x, 'vocab', [(i, i ^ distance) for i in range(n)])  27 us
    all_to_all x1, blocking collectives, levels_plan(): lax.all_to_all(stat, 'vocab', split_axis=0, concat_axis=0, tiled=True)  13.6 us
    pallas_call x1, Pallas kernels, levels_plan(): pl.pallas_call(functools.partial(logits_kernel, rows), grid=(2 * tiles,),...  11 us
    pallas_call x1, Pallas kernels, levels_plan(): pl.pallas_call(functools.partial(head_kernel, rows), grid=(4,), in_specs=...  9.96 us
    pallas_call x1, Pallas kernels, levels_plan(): pl.pallas_call(functools.partial(partial_kernel, rows), grid_spec=pltpu.P...  8.63 us
    all_to_all x1, starting transfers between devices, levels_plan(): lax.all_to_all(payload[:, :3 - STAT_ROWS], 'vocab', split_axis=0, concat_...  6.18 us
    dynamic_slice x1, local copies, waits for them, and re-layouts, levels_plan(): lax.dynamic_slice(head_weight, ((1 - core) * half, 0), (half, slab))  5.43 us
  transfers between devices with their start and end apart: 28, of which 10 were waited for; matrix products, arithmetic and copies ran while one was open for 7% of the time, Pallas kernels for 22%

profile of v18, /device:TPU:0, one launch (start us, length us, event | category | flops | bytes accessed | tf_op | source)
XLA Modules:
  0.0 133.7 jit_solution(3540243594361098526)
XLA Ops:
  0.6 4.1 %collective-permute-start.1 = (bf16[16,5120]{1,0:T(8,128)(2,1)}, bf16[16,5120]{1,0:T(8,128)(2,1)S(1)}, u32[]{:S(2)}, u32[]{:S(2)}) collective-permute-start(bf16[16,5120]{1,0:T(8,128)(2,1)} %param.7), channel_id=1, source_target_pairs={{0,16},{1,17},{2,18},{3,19},{4,20},{5,21},{6,22},{7,23},{8,24},{9,... | collective-permute-start | bytes 491528 | tf_op jit(solution)/shard_map/ppermute | solution.py:134
  4.7 1.6 %collective-permute-start = (bf16[16,5120]{1,0:T(8,128)(2,1)}, bf16[16,5120]{1,0:T(8,128)(2,1)S(1)}, u32[]{:S(2)}, u32[]{:S(2)}) collective-permute-start(bf16[16,5120]{1,0:T(8,128)(2,1)} %param.7), channel_id=1, source_target_pairs={{0,8},{1,9},{2,10},{3,11},{4,12},{5,13},{6,14},{7,15},{8,0},{9,1},... | collective-permute-start | bytes 491528 | tf_op jit(solution)/shard_map/ppermute | solution.py:134
  6.3 0.0 collective-permute-start.2
  6.3 0.7 add_select_fusion.1
  7.0 0.1 iota_compare_fusion
  7.1 0.2 convert_reduce_fusion
  7.3 0.1 add.86
  7.4 0.1 add.83
  7.5 0.1 add.89
  7.7 0.0 copy-start.1
  7.7 0.9 copy-done.1
  8.6 1.3 pack_teacher.1
  9.9 0.9 slice.8
  10.8 6.2 %all-to-all-start = ((bf16[32,67,128]{2,1,0:T(8,128)(2,1)}), bf16[32,67,128]{2,1,0:T(8,128)(2,1)}, u32[]{:S(2)}, u32[]{:S(2)}) async-start(bf16[32,67,128]{2,1,0:T(8,128)(2,1)} %slice.8), calls=%async_computation | async-start | bytes 1179648 | tf_op jit(solution)/shard_map/all_to_all | solution.py:506
  17.0 0.9 constant_dynamic-update-slice_fusion.3
  18.0 1.8 %collective-permute-start.4 = (bf16[64,5120]{1,0:T(8,128)(2,1)S(1)}, bf16[64,5120]{1,0:T(8,128)(2,1)S(1)}, u32[]{:S(2)}, u32[]{:S(2)}) collective-permute-start(bf16[64,5120]{1,0:T(8,128)(2,1)S(1)} %constant_dynamic-update-slice_fusion.refs_0_), channel_id=1, source_target_pairs={{0,4},{1,5},{2,6},{3,7},{4,0},{5,1},{6,2},{7,3},{8,12},{9,13},{10,... | collective-permute-start | bytes 1966088 | tf_op jit(solution)/shard_map/ppermute | solution.py:134
  19.8 1.5 %collective-permute-start.3 = (bf16[64,5120]{1,0:T(8,128)(2,1)S(1)}, bf16[64,5120]{1,0:T(8,128)(2,1)S(1)}, u32[]{:S(2)}, u32[]{:S(2)}) collective-permute-start(bf16[64,5120]{1,0:T(8,128)(2,1)S(1)} %constant_dynamic-update-slice_fusion.refs_0_), channel_id=1, source_target_pairs={{0,2},{1,3},{2,0},{3,1},{4,6},{5,7},{6,4},{7,5},{8,10},{9,11},{10,... | collective-permute-start | bytes 1966088 | tf_op jit(solution)/shard_map/ppermute | solution.py:134
  21.3 0.2 select_reduce_fusion
  21.5 0.0 copy-start.2
  21.5 0.0 copy-start.3
  21.5 5.4 %constant_dynamic-slice_fusion = bf16[2560,1024]{1,0:T(8,128)(2,1)} fusion(bf16[5120,1024]{1,0:T(8,128)(2,1)} %w_ref.1, s32[]{:T(128)S(6)} %select_n.42), kind=kLoop, calls=%fused_computation.24 | loop fusion | bytes 10485764 | tf_op jit(solution)/shard_map/dynamic_slice | solution.py:493
  27.0 13.5 %collective-permute-done.4.y_ref.refs_2_ = bf16[64,5120]{1,0:T(8,128)(2,1)S(1)} collective-permute-done((bf16[64,5120]{1,0:T(8,128)(2,1)S(1)}, bf16[64,5120]{1,0:T(8,128)(2,1)S(1)}, u32[]{:S(2)}, u32[]{:S(2)}) %collective-permute-start.4) | collective-permute-done | bytes 655392 | tf_op jit(solution)/shard_map/ppermute | solution.py:134
  40.4 0.0 collective-permute-done.3.x_ref.refs_1_
  40.5 0.0 collective-permute-start.8
  40.5 0.9 cut_halves.1
  41.4 0.5 collective-permute-start.9
  41.9 1.1 collective-permute-start.5
  43.0 0.8 collective-permute-start.6
  43.8 0.1 pad_add_fusion.refs_0_.core_ref.pos_ref
  43.9 4.9 %teacher_prob.1 = (f32[512,1024]{1,0:T(8,128)S(1)}, f32[16,128]{1,0:T(8,128)S(1)}) custom-call(s32[4]{0:T(128)S(1)} %pad_add_fusion.refs_0_.core_ref.pos_ref, s32[4,4]{1,0:T(4,128)S(1)} %broadcast_add_fusion.1.refs_1_, bf16[32,67,128]{2,1,0:T(8,128)(2,1)} %all-to-all-done.refs_2_, s32[4,1,128]{2,1,0:T(1,128)S(1)} %bitcast.9, f32[4,1,128]{2,1,0:T(1,128)S(1)} %bitcast.10), custom_call_target="tpu_custom_call" | custom-call | flops 1 | bytes 1 | tf_op jit(solution)/shard_map/teacher_prob/pallas_call | solution.py:510
  48.8 3.0 %collective-permute-done.5.refs_3_ = bf16[64,2560]{1,0:T(8,128)(2,1)} collective-permute-done((bf16[64,2560]{1,0:T(8,128)(2,1)}, bf16[64,2560]{1,0:T(8,128)(2,1)}, u32[]{:S(2)}, u32[]{:S(2)}) %collective-permute-start.5) | collective-permute-done | bytes 327712 | tf_op jit(solution)/shard_map/ppermute | solution.py:134
  51.8 0.8 collective-permute-done.6.refs_4_
  52.6 0.5 collective-permute-start.11
  53.1 1.3 collective-permute-done.10.refs_8_
  54.5 0.5 collective-permute-done.11.refs_9_
  54.9 0.1 collective-permute-start.13
  55.1 11.0 %logits.1 = (f32[512,1024]{1,0:T(8,128)S(1)}, f32[32,8,128]{2,1,0:T(8,128)S(1)}) custom-call(bf16[64,5120]{1,0:T(8,128)(2,1)S(1)} %constant_dynamic-update-slice_fusion.refs_0_, bf16[64,5120]{1,0:T(8,128)(2,1)S(1)} %collective-permute-done.3.x_ref.refs_1_, bf16[64,5120]{1,0:T(8,128)(2,1)S(1)} %collective-permute-done.4.y_ref.refs_2_, ...), custom_call_target="tpu_custom_call" | custom-call | flops 1 | bytes 1 | tf_op jit(solution)/shard_map/logits/pallas_call | solution.py:537
  66.1 13.6 %all_to_all.10.refs_1_ = f32[32,8,128]{2,1,0:T(8,128)S(1)} all-to-all(f32[32,8,128]{2,1,0:T(8,128)S(1)} %get-tuple-element.81), channel_id=1, replica_groups=mesh['vocab'=32] {'vocab'}, dimensions={0} | all-to-all | bytes 262144 | tf_op jit(solution)/shard_map/all_to_all | solution.py:557
  79.7 1.3 grad_logits.1
  81.1 0.3 collective-permute-start.12
  81.4 2.4 %collective-permute-done.12.sib_ref = bf16[512,1024]{1,0:T(8,128)(2,1)S(1)} collective-permute-done((bf16[512,1024]{1,0:T(8,128)(2,1)S(1)}, bf16[512,1024]{1,0:T(8,128)(2,1)S(1)}, u32[]{:S(2)}, u32[]{:S(2)}) %collective-permute-start.12) | collective-permute-done | bytes 1048608 | tf_op jit(solution)/shard_map/ppermute | solution.py:134
  83.8 8.6 %grad_hidden_partial.1 = (f32[4,2,16,1792]{3,2,1,0:T(8,128)S(1)}, bf16[4,2,16,1792]{3,2,1,0:T(8,128)(2,1)S(1)}, bf16[4,2,16,1792]{3,2,1,0:T(8,128)(2,1)S(1)}, bf...) custom-call(s32[4]{0:T(128)S(1)} %pad_add_fusion.refs_0_.core_ref.po, ...), custom_call_target="tpu_custom_call" | custom-call | flops 1 | bytes 1 | tf_op jit(solution)/shard_map/grad_hidden_partial/pallas_call | solution.py:575
  92.5 0.5 collective-permute-start.14
  93.0 1.0 collective-permute-start.15
  94.0 2.0 %collective-permute-start.16 = (bf16[4,2,16,1792]{3,2,1,0:T(8,128)(2,1)S(1)}, bf16[4,2,16,1792]{3,2,1,0:T(8,128)(2,1)S(1)}, u32[]{:S(2)}, u32[]{:S(2)}) collective-permute-start(bf16[4,2,16,1792]{3,2,1,0:T(8,128)(2,1)S(1)} %get-tuple-element.97), channel_id=1, source_target_pairs={{0,6},{1,7},{2,4},{3,5},{4,2},{5,3},{6,0},{7,1},{8,14},{9,15},{10,... | collective-permute-start | bytes 1376264 | tf_op jit(solution)/shard_map/ppermute | solution.py:134
  96.0 0.7 collective-permute-start.17
  96.7 1.3 collective-permute-start.18
  97.9 7.5 %collective-permute-done.17.refs_5_ = bf16[4,2,16,768]{3,2,1,0:T(8,128)(2,1)S(1)} collective-permute-done((bf16[4,2,16,768]{3,2,1,0:T(8,128)(2,1)S(1)}, bf16[4,2,16,768]{3,2,1,0:T(8,128)(2,1)S(1)}, u32[]{:S(2)}, u32[]{:S(2)}) %collective-permute-start.17) | collective-permute-done | bytes 196640 | tf_op jit(solution)/shard_map/ppermute | solution.py:134
  105.4 1.9 %collective-permute-start.19 = (bf16[4,2,16,768]{3,2,1,0:T(8,128)(2,1)S(1)}, bf16[4,2,16,768]{3,2,1,0:T(8,128)(2,1)S(1)}, u32[]{:S(2)}, u32[]{:S(2)}) collective-permute-start(bf16[4,2,16,768]{3,2,1,0:T(8,128)(2,1)S(1)} %get-tuple-element.100), channel_id=1, source_target_pairs={{0,24},{1,25},{2,26},{3,27},{4,28},{5,29},{6,30},{7,31},{8,16},{9,... | collective-permute-start | bytes 589832 | tf_op jit(solution)/shard_map/ppermute | solution.py:134
  107.3 10.0 %grad_head.1 = bf16[5120,1024]{1,0:T(8,128)(2,1)} custom-call(bf16[64,5120]{1,0:T(8,128)(2,1)S(1)} %constant_dynamic-update-slice_fusion.refs_0_, bf16[64,5120]{1,0:T(8,128)(2,1)S(1)} %collective-permute-done.3.x_ref.refs_1_, bf16[64,5120]{1,0:T(8,128)(2,1)S(1)} %collective-permute-done.4.y_ref.refs_2_, bf16[64,2560]{1,0:T(8,128)(2,1)} %collective-permute-done.5.refs_3_, ...), custom_call_target="tpu_custom_call" | custom-call | flops 1 | bytes 1 | tf_op jit(solution)/shard_map/grad_head/pallas_call | solution.py:599
  117.3 0.3 first_sum.1
  117.5 0.1 collective-permute-start.20
  117.6 2.5 %collective-permute-start.21 = (bf16[2,16,1792]{2,1,0:T(8,128)(2,1)S(1)}, bf16[2,16,1792]{2,1,0:T(8,128)(2,1)S(1)}, u32[]{:S(2)}, u32[]{:S(2)}) collective-permute-start(bf16[2,16,1792]{2,1,0:T(8,128)(2,1)S(1)} %get-tuple-element.113), channel_id=1, source_target_pairs={{0,16},{1,17},{2,18},{3,19},{4,20},{5,21},{6,22},{7,23},{8,24},{9,... | collective-permute-start | bytes 344072 | tf_op jit(solution)/shard_map/ppermute | solution.py:134
  120.2 1.9 %collective-permute-start.22 = (bf16[2,16,1792]{2,1,0:T(8,128)(2,1)S(1)}, bf16[2,16,1792]{2,1,0:T(8,128)(2,1)S(1)}, u32[]{:S(2)}, u32[]{:S(2)}) collective-permute-start(bf16[2,16,1792]{2,1,0:T(8,128)(2,1)S(1)} %get-tuple-element.114), channel_id=1, source_target_pairs={{0,24},{1,25},{2,26},{3,27},{4,28},{5,29},{6,30},{7,31},{8,16},{9,... | collective-permute-start | bytes 344072 | tf_op jit(solution)/shard_map/ppermute | solution.py:134
  122.0 0.5 collective-permute-start.23
  122.5 1.2 collective-permute-start.24
  123.7 2.4 %collective-permute-done.23.refs_5_ = bf16[2,16,768]{2,1,0:T(8,128)(2,1)S(1)} collective-permute-done((bf16[2,16,768]{2,1,0:T(8,128)(2,1)S(1)}, bf16[2,16,768]{2,1,0:T(8,128)(2,1)S(1)}, u32[]{:S(2)}, u32[]{:S(2)}) %collective-permute-start.23) | collective-permute-done | bytes 49184 | tf_op jit(solution)/shard_map/ppermute | solution.py:134
  126.1 1.2 collective-permute-start.25
  127.2 3.8 %collective-permute-done.25.refs_7_ = bf16[2,16,768]{2,1,0:T(8,128)(2,1)S(1)} collective-permute-done((bf16[2,16,768]{2,1,0:T(8,128)(2,1)S(1)}, bf16[2,16,768]{2,1,0:T(8,128)(2,1)S(1)}, u32[]{:S(2)}, u32[]{:S(2)}) %collective-permute-start.25) | collective-permute-done | bytes 49184 | tf_op jit(solution)/shard_map/ppermute | solution.py:134
  131.1 0.1 last_sum.1
  131.2 0.1 collective-permute-start.26
  131.3 0.6 slice_reduce_fusion
  131.9 0.6 collective-permute-done.26.other_ref
  132.5 1.2 join_halves.1
  (34 shorter events, 0.1 us)
Async XLA Ops:
  0.6 17.4 %collective-permute-start.1 = (bf16[16,5120]{1,0:T(8,128)(2,1)}, bf16[16,5120]{1,0:T(8,128)(2,1)S(1)}, u32[]{:S(2)}, u32[]{:S(2)}) collective-permute-start(bf16[16,5120]{1,0:T(8,128)(2,1)} %param.7), channel_id=1, source_target_pairs={{0,16},{1,17},{2,18},{3,19},{4,20},{5,21},{6,22},{7,23},{8,24},{9,... | collective-permute-start | bytes 491528 | tf_op jit(solution)/shard_map/ppermute | solution.py:134
  4.7 13.2 %collective-permute-start = (bf16[16,5120]{1,0:T(8,128)(2,1)}, bf16[16,5120]{1,0:T(8,128)(2,1)S(1)}, u32[]{:S(2)}, u32[]{:S(2)}) collective-permute-start(bf16[16,5120]{1,0:T(8,128)(2,1)} %param.7), channel_id=1, source_target_pairs={{0,8},{1,9},{2,10},{3,11},{4,12},{5,13},{6,14},{7,15},{8,0},{9,1},... | collective-permute-start | bytes 491528 | tf_op jit(solution)/shard_map/ppermute | solution.py:134
  6.3 11.7 %collective-permute-start.2 = (bf16[16,5120]{1,0:T(8,128)(2,1)}, bf16[16,5120]{1,0:T(8,128)(2,1)S(1)}, u32[]{:S(2)}, u32[]{:S(2)}) collective-permute-start(bf16[16,5120]{1,0:T(8,128)(2,1)} %param.7), channel_id=1, source_target_pairs={{0,24},{1,25},{2,26},{3,27},{4,28},{5,29},{6,30},{7,31},{8,16},{9,... | collective-permute-start | bytes 491528 | tf_op jit(solution)/shard_map/ppermute | solution.py:134
  7.7 1.0 copy-start.1
  10.8 33.1 %all-to-all-start = ((bf16[32,67,128]{2,1,0:T(8,128)(2,1)}), bf16[32,67,128]{2,1,0:T(8,128)(2,1)}, u32[]{:S(2)}, u32[]{:S(2)}) async-start(bf16[32,67,128]{2,1,0:T(8,128)(2,1)} %slice.8), calls=%async_computation | async-start | bytes 1179648 | tf_op jit(solution)/shard_map/all_to_all | solution.py:506
  18.0 22.4 %collective-permute-start.4 = (bf16[64,5120]{1,0:T(8,128)(2,1)S(1)}, bf16[64,5120]{1,0:T(8,128)(2,1)S(1)}, u32[]{:S(2)}, u32[]{:S(2)}) collective-permute-start(bf16[64,5120]{1,0:T(8,128)(2,1)S(1)} %constant_dynamic-update-slice_fusion.refs_0_), channel_id=1, source_target_pairs={{0,4},{1,5},{2,6},{3,7},{4,0},{5,1},{6,2},{7,3},{8,12},{9,13},{10,... | collective-permute-start | bytes 1966088 | tf_op jit(solution)/shard_map/ppermute | solution.py:134
  19.8 20.7 %collective-permute-start.3 = (bf16[64,5120]{1,0:T(8,128)(2,1)S(1)}, bf16[64,5120]{1,0:T(8,128)(2,1)S(1)}, u32[]{:S(2)}, u32[]{:S(2)}) collective-permute-start(bf16[64,5120]{1,0:T(8,128)(2,1)S(1)} %constant_dynamic-update-slice_fusion.refs_0_), channel_id=1, source_target_pairs={{0,2},{1,3},{2,0},{3,1},{4,6},{5,7},{6,4},{7,5},{8,10},{9,11},{10,... | collective-permute-start | bytes 1966088 | tf_op jit(solution)/shard_map/ppermute | solution.py:134
  21.5 22.4 %copy-start.2 = (s32[4,128]{1,0:T(4,128)S(1)}, s32[4,128]{1,0:T(4,128)}, u32[]{:S(2)}) copy-start(s32[4,128]{1,0:T(4,128)} %param.11) | copy-start | bytes 6148
  21.5 22.4 %copy-start.3 = (f32[512]{0:T(512)S(1)}, f32[512]{0:T(512)}, u32[]{:S(2)}) copy-start(f32[512]{0:T(512)} %param.12) | copy-start | bytes 6148
  26.9 26.2 %collective-permute-start.7 = (bf16[64,5120]{1,0:T(8,128)(2,1)S(1)}, bf16[64,5120]{1,0:T(8,128)(2,1)S(1)}, u32[]{:S(2)}, u32[]{:S(2)}) collective-permute-start(bf16[64,5120]{1,0:T(8,128)(2,1)S(1)} %constant_dynamic-update-slice_fusion.refs_0_), channel_id=1, source_target_pairs={{0,1},{1,0},{2,3},{3,2},{4,5},{5,4},{6,7},{7,6},{8,9},{9,8},{10,11... | collective-permute-start | bytes 1966088 | tf_op jit(solution)/shard_map/ppermute | solution.py:134
  40.5 14.5 %collective-permute-start.8 = (bf16[64,5120]{1,0:T(8,128)(2,1)S(1)}, bf16[64,5120]{1,0:T(8,128)(2,1)S(1)}, u32[]{:S(2)}, u32[]{:S(2)}) collective-permute-start(bf16[64,5120]{1,0:T(8,128)(2,1)S(1)} %collective-permute-done.3.x_ref.refs_1_), channel_id=1, source_target_pairs={{0,1},{1,0},{2,3},{3,2},{4,5},{5,4},{6,7},{7,6},{8,9},{9,8},{10,11... | collective-permute-start | bytes 1966088 | tf_op jit(solution)/shard_map/ppermute | solution.py:134
  41.4 13.6 %collective-permute-start.9 = (bf16[64,5120]{1,0:T(8,128)(2,1)S(1)}, bf16[64,5120]{1,0:T(8,128)(2,1)}, u32[]{:S(2)}, u32[]{:S(2)}) collective-permute-start(bf16[64,5120]{1,0:T(8,128)(2,1)S(1)} %collective-permute-done.4.y_ref.refs_2_), channel_id=1, source_target_pairs={{0,1},{1,0},{2,3},{3,2},{4,5},{5,4},{6,7},{7,6},{8,9},{9,8},{10,11... | collective-permute-start | bytes 1966088 | tf_op jit(solution)/shard_map/ppermute | solution.py:134
  41.9 9.9 %collective-permute-start.5 = (bf16[64,2560]{1,0:T(8,128)(2,1)}, bf16[64,2560]{1,0:T(8,128)(2,1)}, u32[]{:S(2)}, u32[]{:S(2)}) collective-permute-start(bf16[64,2560]{1,0:T(8,128)(2,1)} %get-tuple-element.64), channel_id=1, source_target_pairs={{0,4},{1,5},{2,6},{3,7},{4,0},{5,1},{6,2},{7,3},{8,12},{9,13},{10,... | collective-permute-start | bytes 983048 | tf_op jit(solution)/shard_map/ppermute | solution.py:134
  43.0 9.7 %collective-permute-start.6 = (bf16[64,2560]{1,0:T(8,128)(2,1)}, bf16[64,2560]{1,0:T(8,128)(2,1)}, u32[]{:S(2)}, u32[]{:S(2)}) collective-permute-start(bf16[64,2560]{1,0:T(8,128)(2,1)} %get-tuple-element.65), channel_id=1, source_target_pairs={{0,2},{1,3},{2,0},{3,1},{4,6},{5,7},{6,4},{7,5},{8,10},{9,11},{10,... | collective-permute-start | bytes 983048 | tf_op jit(solution)/shard_map/ppermute | solution.py:134
  52.6 27.1 %copy-start.4 = (f32[512]{0:T(512)S(1)}, f32[512]{0:T(512)}, u32[]{:S(2)}) copy-start(f32[512]{0:T(512)} %param.13) | copy-start | bytes 6148
  52.6 1.8 %collective-permute-start.10 = (bf16[64,2560]{1,0:T(8,128)(2,1)}, bf16[64,2560]{1,0:T(8,128)(2,1)S(1)}, u32[]{:S(2)}, u32[]{:S(2)}) collective-permute-start(bf16[64,2560]{1,0:T(8,128)(2,1)} %collective-permute-done.5.refs_3_), channel_id=1, source_target_pairs={{0,1},{1,0},{2,3},{3,2},{4,5},{5,4},{6,7},{7,6},{8,9},{9,8},{10,11... | collective-permute-start | bytes 983048 | tf_op jit(solution)/shard_map/ppermute | solution.py:134
  52.6 2.3 %collective-permute-start.11 = (bf16[64,2560]{1,0:T(8,128)(2,1)}, bf16[64,2560]{1,0:T(8,128)(2,1)S(1)}, u32[]{:S(2)}, u32[]{:S(2)}) collective-permute-start(bf16[64,2560]{1,0:T(8,128)(2,1)} %collective-permute-done.6.refs_4_), channel_id=1, source_target_pairs={{0,1},{1,0},{2,3},{3,2},{4,5},{5,4},{6,7},{7,6},{8,9},{9,8},{10,11... | collective-permute-start | bytes 983048 | tf_op jit(solution)/shard_map/ppermute | solution.py:134
  54.9 28.9 %collective-permute-start.13 = (bf16[2560,1024]{1,0:T(8,128)(2,1)}, bf16[2560,1024]{1,0:T(8,128)(2,1)S(1)}, u32[]{:S(2)}, u32[]{:S(2)}) collective-permute-start(bf16[2560,1024]{1,0:T(8,128)(2,1)} %constant_dynamic-slice_fusion), channel_id=1, source_target_pairs={{0,1},{1,0},{2,3},{3,2},{4,5},{5,4},{6,7},{7,6},{8,9},{9,8},{10,11... | collective-permute-start | bytes 15728648 | tf_op jit(solution)/shard_map/ppermute | solution.py:134
  81.1 11.4 %copy-start = (bf16[512,1024]{1,0:T(8,128)(2,1)}, bf16[512,1024]{1,0:T(8,128)(2,1)S(1)}, u32[]{:S(2)}) copy-start(bf16[512,1024]{1,0:T(8,128)(2,1)S(1)} %get-tuple-element.101.grad_ref.refs_10_) | copy-start | bytes 3145732
  81.1 2.7 %collective-permute-start.12 = (bf16[512,1024]{1,0:T(8,128)(2,1)S(1)}, bf16[512,1024]{1,0:T(8,128)(2,1)S(1)}, u32[]{:S(2)}, u32[]{:S(2)}) collective-permute-start(bf16[512,1024]{1,0:T(8,128)(2,1)S(1)} %get-tuple-element.101.grad_ref.refs_10_), channel_id=1, source_target_pairs={{0,1},{1,0},{2,3},{3,2},{4,5},{5,4},{6,7},{7,6},{8,9},{9,8},{10,11... | collective-permute-start | bytes 3145736 | tf_op jit(solution)/shard_map/ppermute | solution.py:134
  92.5 24.8 %collective-permute-start.14 = (bf16[4,2,16,1792]{3,2,1,0:T(8,128)(2,1)S(1)}, bf16[4,2,16,1792]{3,2,1,0:T(8,128)(2,1)S(1)}, u32[]{:S(2)}, u32[]{:S(2)}) collective-permute-start(bf16[4,2,16,1792]{3,2,1,0:T(8,128)(2,1)S(1)} %get-tuple-element.95), channel_id=1, source_target_pairs={{0,2},{1,3},{2,0},{3,1},{4,6},{5,7},{6,4},{7,5},{8,10},{9,11},{10,... | collective-permute-start | bytes 1376264 | tf_op jit(solution)/shard_map/ppermute | solution.py:134
  93.0 24.3 %collective-permute-start.15 = (bf16[4,2,16,1792]{3,2,1,0:T(8,128)(2,1)S(1)}, bf16[4,2,16,1792]{3,2,1,0:T(8,128)(2,1)S(1)}, u32[]{:S(2)}, u32[]{:S(2)}) collective-permute-start(bf16[4,2,16,1792]{3,2,1,0:T(8,128)(2,1)S(1)} %get-tuple-element.96), channel_id=1, source_target_pairs={{0,4},{1,5},{2,6},{3,7},{4,0},{5,1},{6,2},{7,3},{8,12},{9,13},{10,... | collective-permute-start | bytes 1376264 | tf_op jit(solution)/shard_map/ppermute | solution.py:134
  94.0 23.3 %collective-permute-start.16 = (bf16[4,2,16,1792]{3,2,1,0:T(8,128)(2,1)S(1)}, bf16[4,2,16,1792]{3,2,1,0:T(8,128)(2,1)S(1)}, u32[]{:S(2)}, u32[]{:S(2)}) collective-permute-start(bf16[4,2,16,1792]{3,2,1,0:T(8,128)(2,1)S(1)} %get-tuple-element.97), channel_id=1, source_target_pairs={{0,6},{1,7},{2,4},{3,5},{4,2},{5,3},{6,0},{7,1},{8,14},{9,15},{10,... | collective-permute-start | bytes 1376264 | tf_op jit(solution)/shard_map/ppermute | solution.py:134
  96.0 9.4 %collective-permute-start.17 = (bf16[4,2,16,768]{3,2,1,0:T(8,128)(2,1)S(1)}, bf16[4,2,16,768]{3,2,1,0:T(8,128)(2,1)S(1)}, u32[]{:S(2)}, u32[]{:S(2)}) collective-permute-start(bf16[4,2,16,768]{3,2,1,0:T(8,128)(2,1)S(1)} %get-tuple-element.98), channel_id=1, source_target_pairs={{0,8},{1,9},{2,10},{3,11},{4,12},{5,13},{6,14},{7,15},{8,0},{9,1},... | collective-permute-start | bytes 589832 | tf_op jit(solution)/shard_map/ppermute | solution.py:134
  96.7 20.6 %collective-permute-start.18 = (bf16[4,2,16,768]{3,2,1,0:T(8,128)(2,1)S(1)}, bf16[4,2,16,768]{3,2,1,0:T(8,128)(2,1)S(1)}, u32[]{:S(2)}, u32[]{:S(2)}) collective-permute-start(bf16[4,2,16,768]{3,2,1,0:T(8,128)(2,1)S(1)} %get-tuple-element.99), channel_id=1, source_target_pairs={{0,16},{1,17},{2,18},{3,19},{4,20},{5,21},{6,22},{7,23},{8,24},{9,... | collective-permute-start | bytes 589832 | tf_op jit(solution)/shard_map/ppermute | solution.py:134
  105.4 11.8 %collective-permute-start.19 = (bf16[4,2,16,768]{3,2,1,0:T(8,128)(2,1)S(1)}, bf16[4,2,16,768]{3,2,1,0:T(8,128)(2,1)S(1)}, u32[]{:S(2)}, u32[]{:S(2)}) collective-permute-start(bf16[4,2,16,768]{3,2,1,0:T(8,128)(2,1)S(1)} %get-tuple-element.100), channel_id=1, source_target_pairs={{0,24},{1,25},{2,26},{3,27},{4,28},{5,29},{6,30},{7,31},{8,16},{9,... | collective-permute-start | bytes 589832 | tf_op jit(solution)/shard_map/ppermute | solution.py:134
  117.5 13.5 %collective-permute-start.20 = (bf16[2,16,1792]{2,1,0:T(8,128)(2,1)S(1)}, bf16[2,16,1792]{2,1,0:T(8,128)(2,1)S(1)}, u32[]{:S(2)}, u32[]{:S(2)}) collective-permute-start(bf16[2,16,1792]{2,1,0:T(8,128)(2,1)S(1)} %get-tuple-element.112), channel_id=1, source_target_pairs={{0,8},{1,9},{2,10},{3,11},{4,12},{5,13},{6,14},{7,15},{8,0},{9,1},... | collective-permute-start | bytes 344072 | tf_op jit(solution)/shard_map/ppermute | solution.py:134
  117.6 13.5 %collective-permute-start.21 = (bf16[2,16,1792]{2,1,0:T(8,128)(2,1)S(1)}, bf16[2,16,1792]{2,1,0:T(8,128)(2,1)S(1)}, u32[]{:S(2)}, u32[]{:S(2)}) collective-permute-start(bf16[2,16,1792]{2,1,0:T(8,128)(2,1)S(1)} %get-tuple-element.113), channel_id=1, source_target_pairs={{0,16},{1,17},{2,18},{3,19},{4,20},{5,21},{6,22},{7,23},{8,24},{9,... | collective-permute-start | bytes 344072 | tf_op jit(solution)/shard_map/ppermute | solution.py:134
  120.2 10.9 %collective-permute-start.22 = (bf16[2,16,1792]{2,1,0:T(8,128)(2,1)S(1)}, bf16[2,16,1792]{2,1,0:T(8,128)(2,1)S(1)}, u32[]{:S(2)}, u32[]{:S(2)}) collective-permute-start(bf16[2,16,1792]{2,1,0:T(8,128)(2,1)S(1)} %get-tuple-element.114), channel_id=1, source_target_pairs={{0,24},{1,25},{2,26},{3,27},{4,28},{5,29},{6,30},{7,31},{8,16},{9,... | collective-permute-start | bytes 344072 | tf_op jit(solution)/shard_map/ppermute | solution.py:134
  122.0 4.1 %collective-permute-start.23 = (bf16[2,16,768]{2,1,0:T(8,128)(2,1)S(1)}, bf16[2,16,768]{2,1,0:T(8,128)(2,1)S(1)}, u32[]{:S(2)}, u32[]{:S(2)}) collective-permute-start(bf16[2,16,768]{2,1,0:T(8,128)(2,1)S(1)} %get-tuple-element.116), channel_id=1, source_target_pairs={{0,2},{1,3},{2,0},{3,1},{4,6},{5,7},{6,4},{7,5},{8,10},{9,11},{10,... | collective-permute-start | bytes 147464 | tf_op jit(solution)/shard_map/ppermute | solution.py:134
  122.5 4.8 %collective-permute-start.24 = (bf16[2,16,768]{2,1,0:T(8,128)(2,1)S(1)}, bf16[2,16,768]{2,1,0:T(8,128)(2,1)S(1)}, u32[]{:S(2)}, u32[]{:S(2)}) collective-permute-start(bf16[2,16,768]{2,1,0:T(8,128)(2,1)S(1)} %get-tuple-element.117), channel_id=1, source_target_pairs={{0,4},{1,5},{2,6},{3,7},{4,0},{5,1},{6,2},{7,3},{8,12},{9,13},{10,... | collective-permute-start | bytes 147464 | tf_op jit(solution)/shard_map/ppermute | solution.py:134
  126.1 5.0 %collective-permute-start.25 = (bf16[2,16,768]{2,1,0:T(8,128)(2,1)S(1)}, bf16[2,16,768]{2,1,0:T(8,128)(2,1)S(1)}, u32[]{:S(2)}, u32[]{:S(2)}) collective-permute-start(bf16[2,16,768]{2,1,0:T(8,128)(2,1)S(1)} %get-tuple-element.118), channel_id=1, source_target_pairs={{0,6},{1,7},{2,4},{3,5},{4,2},{5,3},{6,0},{7,1},{8,14},{9,15},{10,... | collective-permute-start | bytes 147464 | tf_op jit(solution)/shard_map/ppermute | solution.py:134
  131.2 1.3 %collective-permute-start.26 = (bf16[16,2560]{1,0:T(8,128)(2,1)S(1)}, bf16[16,2560]{1,0:T(8,128)(2,1)S(1)}, u32[]{:S(2)}, u32[]{:S(2)}) collective-permute-start(bf16[16,2560]{1,0:T(8,128)(2,1)S(1)} %get-tuple-element.120), channel_id=1, source_target_pairs={{0,1},{1,0},{2,3},{3,2},{4,5},{5,4},{6,7},{7,6},{8,9},{9,8},{10,11... | collective-permute-start | bytes 245768 | tf_op jit(solution)/shard_map/ppermute | solution.py:134

commit v19 on v18

--- a/solution.py
+++ b/solution.py
@@ -211,13 +211,6 @@
     half = low_ref.shape[1]
     low_ref[...] = x_ref[:, :half]
     high_ref[...] = y_ref[:, half:]
-
-
-def join_kernel(pos_ref, mine_ref, other_ref, out_ref):
-    half = mine_ref.shape[1]
-    own = pos_ref[0]
-    out_ref[:, pl.ds(pl.multiple_of(own * half, half), half)] = mine_ref[...]
-    out_ref[:, pl.ds(pl.multiple_of((1 - own) * half, half), half)] = other_ref[...]
 
 
 def logits_kernel(rows, *refs):
@@ -606,7 +599,7 @@
             )
             for i in range(len(pieces))
         ]
-        + [pl.BlockSpec((tokens, slab), whole)],
+        + [vmem_spec()],
         out_specs=pl.BlockSpec((head_tile, slab), lambda t: (t, 0)),
         out_shape=jax.ShapeDtypeStruct((depth, slab), bf16),
         scratch_shapes=[pltpu.VMEM((tokens, head_tile), bf16)],
@@ -639,16 +632,8 @@
     )(summed[0], *wide_sums, summed[layers], *narrow_sums)
     other = shift(theirs, 1)
 
-    grad_hidden = pl.pallas_call(
-        join_kernel,
-        in_specs=[smem_spec()] + [vmem_spec()] * 2,
-        out_specs=vmem_spec(),
-        out_shape=jax.ShapeDtypeStruct((rows, depth), bf16),
-        compiler_params=kernel_params(),
-        cost_estimate=LIGHT,
-        name="join_halves",
-    )(pos, mine, other)
-    return loss[:, 0], grad_head, grad_hidden
+    low, high = jnp.where(core == 0, mine, other), jnp.where(core == 0, other, mine)
+    return loss[:, 0], grad_head, jnp.concatenate([low, high], axis=1)
 
 
 def fits_levels(hidden_states, teacher_logits):

time: 134 us -> 134 us (level)
  no operation moved by 1% of the time
where the time goes in v19:
time: 134 us; the launch traced here: 133 us
  Pallas kernels  38.3 us (29%)
  waiting for transfers between devices  35.9 us (27%)
  starting transfers between devices  33.2 us (25%)
  blocking collectives  13.7 us (10%)
  local copies, waits for them, and re-layouts  9.21 us (7%)
  other arithmetic  2 us (1%)
    ppermute x27, waiting for transfers between devices, shift(): return lax.ppermute(x, 'vocab', [(i, i ^ distance) for i in range(n)])  35.9 us
    ppermute x27, starting transfers between devices, shift(): return lax.ppermute(x, 'vocab', [(i, i ^ distance) for i in range(n)])  27 us
    all_to_all x1, blocking collectives, levels_plan(): lax.all_to_all(stat, 'vocab', split_axis=0, concat_axis=0, tiled=True)  13.7 us
    pallas_call x1, Pallas kernels, levels_plan(): pl.pallas_call(functools.partial(logits_kernel, rows), grid=(2 * tiles,),...  11 us
    pallas_call x1, Pallas kernels, levels_plan(): pl.pallas_call(functools.partial(head_kernel, rows), grid=(4,), in_specs=...  9.96 us
    pallas_call x1, Pallas kernels, levels_plan(): pl.pallas_call(functools.partial(partial_kernel, rows), grid_spec=pltpu.P...  8.63 us
    all_to_all x1, starting transfers between devices, levels_plan(): lax.all_to_all(payload[:, :3 - STAT_ROWS], 'vocab', split_axis=0, concat_...  6.18 us
    dynamic_slice x1, local copies, waits for them, and re-layouts, levels_plan(): lax.dynamic_slice(head_weight, ((1 - core) * half, 0), (half, slab))  5.43 us
  transfers between devices with their start and end apart: 28, of which 10 were waited for; matrix products, arithmetic and copies ran while one was open for 7% of the time, Pallas kernels for 22%

profile of v19, /device:TPU:0, one launch (start us, length us, event | category | flops | bytes accessed | tf_op | source)
XLA Modules:
  0.0 133.2 jit_solution(4272484484491738731)
XLA Ops:
  0.6 4.1 %collective-permute-start.1 = (bf16[16,5120]{1,0:T(8,128)(2,1)}, bf16[16,5120]{1,0:T(8,128)(2,1)S(1)}, u32[]{:S(2)}, u32[]{:S(2)}) collective-permute-start(bf16[16,5120]{1,0:T(8,128)(2,1)} %param.7), channel_id=1, source_target_pairs={{0,16},{1,17},{2,18},{3,19},{4,20},{5,21},{6,22},{7,23},{8,24},{9,... | collective-permute-start | bytes 491528 | tf_op jit(solution)/shard_map/ppermute | solution.py:134
  4.7 1.6 %collective-permute-start = (bf16[16,5120]{1,0:T(8,128)(2,1)}, bf16[16,5120]{1,0:T(8,128)(2,1)S(1)}, u32[]{:S(2)}, u32[]{:S(2)}) collective-permute-start(bf16[16,5120]{1,0:T(8,128)(2,1)} %param.7), channel_id=1, source_target_pairs={{0,8},{1,9},{2,10},{3,11},{4,12},{5,13},{6,14},{7,15},{8,0},{9,1},... | collective-permute-start | bytes 491528 | tf_op jit(solution)/shard_map/ppermute | solution.py:134
  6.3 0.0 collective-permute-start.2
  6.3 0.7 add_select_fusion.1
  7.0 0.1 iota_compare_fusion
  7.1 0.2 convert_reduce_fusion
  7.3 0.1 add.86
  7.4 0.1 add.83
  7.5 0.1 add.89
  7.7 0.0 copy-start.1
  7.7 0.9 copy-done.1
  8.6 1.3 pack_teacher.1
  9.9 0.9 slice.8
  10.8 6.2 %all-to-all-start = ((bf16[32,67,128]{2,1,0:T(8,128)(2,1)}), bf16[32,67,128]{2,1,0:T(8,128)(2,1)}, u32[]{:S(2)}, u32[]{:S(2)}) async-start(bf16[32,67,128]{2,1,0:T(8,128)(2,1)} %slice.8), calls=%async_computation | async-start | bytes 1179648 | tf_op jit(solution)/shard_map/all_to_all | solution.py:499
  17.0 0.9 constant_dynamic-update-slice_fusion.3
  18.0 1.8 %collective-permute-start.4 = (bf16[64,5120]{1,0:T(8,128)(2,1)S(1)}, bf16[64,5120]{1,0:T(8,128)(2,1)S(1)}, u32[]{:S(2)}, u32[]{:S(2)}) collective-permute-start(bf16[64,5120]{1,0:T(8,128)(2,1)S(1)} %constant_dynamic-update-slice_fusion.refs_0_), channel_id=1, source_target_pairs={{0,4},{1,5},{2,6},{3,7},{4,0},{5,1},{6,2},{7,3},{8,12},{9,13},{10,... | collective-permute-start | bytes 1966088 | tf_op jit(solution)/shard_map/ppermute | solution.py:134
  19.8 1.5 %collective-permute-start.3 = (bf16[64,5120]{1,0:T(8,128)(2,1)S(1)}, bf16[64,5120]{1,0:T(8,128)(2,1)S(1)}, u32[]{:S(2)}, u32[]{:S(2)}) collective-permute-start(bf16[64,5120]{1,0:T(8,128)(2,1)S(1)} %constant_dynamic-update-slice_fusion.refs_0_), channel_id=1, source_target_pairs={{0,2},{1,3},{2,0},{3,1},{4,6},{5,7},{6,4},{7,5},{8,10},{9,11},{10,... | collective-permute-start | bytes 1966088 | tf_op jit(solution)/shard_map/ppermute | solution.py:134
  21.3 0.2 select_reduce_fusion
  21.5 0.0 copy-start.2
  21.5 0.0 copy-start.3
  21.5 5.4 %constant_dynamic-slice_fusion = bf16[2560,1024]{1,0:T(8,128)(2,1)} fusion(bf16[5120,1024]{1,0:T(8,128)(2,1)} %w_ref.1, s32[]{:T(128)S(6)} %select_n.54), kind=kLoop, calls=%fused_computation.27 | loop fusion | bytes 10485764 | tf_op jit(solution)/shard_map/dynamic_slice | solution.py:486
  26.9 13.5 %collective-permute-done.4.y_ref.refs_2_ = bf16[64,5120]{1,0:T(8,128)(2,1)S(1)} collective-permute-done((bf16[64,5120]{1,0:T(8,128)(2,1)S(1)}, bf16[64,5120]{1,0:T(8,128)(2,1)S(1)}, u32[]{:S(2)}, u32[]{:S(2)}) %collective-permute-start.4) | collective-permute-done | bytes 655392 | tf_op jit(solution)/shard_map/ppermute | solution.py:134
  40.4 0.0 collective-permute-done.3.x_ref.refs_1_
  40.5 0.0 collective-permute-start.8
  40.5 0.9 cut_halves.1
  41.4 0.5 collective-permute-start.9
  41.9 1.1 collective-permute-start.5
  43.0 0.8 collective-permute-start.6
  43.8 0.1 pad_add_fusion.refs_0_.core_ref
  43.9 4.9 %teacher_prob.1 = (f32[512,1024]{1,0:T(8,128)S(1)}, f32[16,128]{1,0:T(8,128)S(1)}) custom-call(s32[4]{0:T(128)S(1)} %pad_add_fusion.refs_0_.core_ref, s32[4,4]{1,0:T(4,128)S(1)} %broadcast_add_fusion.1.refs_1_, bf16[32,67,128]{2,1,0:T(8,128)(2,1)} %all-to-all-done.refs_2_, s32[4,1,128]{2,1,0:T(1,128)S(1)} %bitcast.9, f32[4,1,128]{2,1,0:T(1,128)S(1)} %bitcast.10), custom_call_target="tpu_custom_call" | custom-call | flops 1 | bytes 1 | tf_op jit(solution)/shard_map/teacher_prob/pallas_call | solution.py:503
  48.8 3.0 %collective-permute-done.5.refs_3_ = bf16[64,2560]{1,0:T(8,128)(2,1)} collective-permute-done((bf16[64,2560]{1,0:T(8,128)(2,1)}, bf16[64,2560]{1,0:T(8,128)(2,1)}, u32[]{:S(2)}, u32[]{:S(2)}) %collective-permute-start.5) | collective-permute-done | bytes 327712 | tf_op jit(solution)/shard_map/ppermute | solution.py:134
  51.8 0.8 collective-permute-done.6.refs_4_
  52.6 0.5 collective-permute-start.11
  53.1 1.3 collective-permute-done.10.refs_8_
  54.5 0.5 collective-permute-done.11.refs_9_
  54.9 0.1 collective-permute-start.13
  55.1 11.0 %logits.1 = (f32[512,1024]{1,0:T(8,128)S(1)}, f32[32,8,128]{2,1,0:T(8,128)S(1)}) custom-call(bf16[64,5120]{1,0:T(8,128)(2,1)S(1)} %constant_dynamic-update-slice_fusion.refs_0_, bf16[64,5120]{1,0:T(8,128)(2,1)S(1)} %collective-permute-done.3.x_ref.refs_1_, bf16[64,5120]{1,0:T(8,128)(2,1)S(1)} %collective-permute-done.4.y_ref.refs_2_, ...), custom_call_target="tpu_custom_call" | custom-call | flops 1 | bytes 1 | tf_op jit(solution)/shard_map/logits/pallas_call | solution.py:530
  66.1 13.7 %all_to_all.10.refs_1_ = f32[32,8,128]{2,1,0:T(8,128)S(1)} all-to-all(f32[32,8,128]{2,1,0:T(8,128)S(1)} %get-tuple-element.81), channel_id=1, replica_groups=mesh['vocab'=32] {'vocab'}, dimensions={0} | all-to-all | bytes 262144 | tf_op jit(solution)/shard_map/all_to_all | solution.py:550
  79.8 1.3 grad_logits.1
  81.1 0.3 collective-permute-start.12
  81.3 2.4 %collective-permute-done.12.sib_ref = bf16[512,1024]{1,0:T(8,128)(2,1)S(1)} collective-permute-done((bf16[512,1024]{1,0:T(8,128)(2,1)S(1)}, bf16[512,1024]{1,0:T(8,128)(2,1)S(1)}, u32[]{:S(2)}, u32[]{:S(2)}) %collective-permute-start.12) | collective-permute-done | bytes 1048608 | tf_op jit(solution)/shard_map/ppermute | solution.py:134
  83.8 8.6 %grad_hidden_partial.1 = (f32[4,2,16,1792]{3,2,1,0:T(8,128)S(1)}, bf16[4,2,16,1792]{3,2,1,0:T(8,128)(2,1)S(1)}, bf16[4,2,16,1792]{3,2,1,0:T(8,128)(2,1)S(1)}, bf...) custom-call(s32[4]{0:T(128)S(1)} %pad_add_fusion.refs_0_.core_ref, ...), custom_call_target="tpu_custom_call" | custom-call | flops 1 | bytes 1 | tf_op jit(solution)/shard_map/grad_hidden_partial/pallas_call | solution.py:568
  92.4 0.5 collective-permute-start.14
  92.9 1.0 collective-permute-start.15
  93.9 2.0 %collective-permute-start.16 = (bf16[4,2,16,1792]{3,2,1,0:T(8,128)(2,1)S(1)}, bf16[4,2,16,1792]{3,2,1,0:T(8,128)(2,1)S(1)}, u32[]{:S(2)}, u32[]{:S(2)}) collective-permute-start(bf16[4,2,16,1792]{3,2,1,0:T(8,128)(2,1)S(1)} %get-tuple-element.97), channel_id=1, source_target_pairs={{0,6},{1,7},{2,4},{3,5},{4,2},{5,3},{6,0},{7,1},{8,14},{9,15},{10,... | collective-permute-start | bytes 1376264 | tf_op jit(solution)/shard_map/ppermute | solution.py:134
  96.0 0.7 collective-permute-start.17
  96.7 1.2 collective-permute-start.18
  97.9 7.5 %collective-permute-done.17.refs_5_ = bf16[4,2,16,768]{3,2,1,0:T(8,128)(2,1)S(1)} collective-permute-done((bf16[4,2,16,768]{3,2,1,0:T(8,128)(2,1)S(1)}, bf16[4,2,16,768]{3,2,1,0:T(8,128)(2,1)S(1)}, u32[]{:S(2)}, u32[]{:S(2)}) %collective-permute-start.17) | collective-permute-done | bytes 196640 | tf_op jit(solution)/shard_map/ppermute | solution.py:134
  105.4 1.8 %collective-permute-start.19 = (bf16[4,2,16,768]{3,2,1,0:T(8,128)(2,1)S(1)}, bf16[4,2,16,768]{3,2,1,0:T(8,128)(2,1)S(1)}, u32[]{:S(2)}, u32[]{:S(2)}) collective-permute-start(bf16[4,2,16,768]{3,2,1,0:T(8,128)(2,1)S(1)} %get-tuple-element.100), channel_id=1, source_target_pairs={{0,24},{1,25},{2,26},{3,27},{4,28},{5,29},{6,30},{7,31},{8,16},{9,... | collective-permute-start | bytes 589832 | tf_op jit(solution)/shard_map/ppermute | solution.py:134
  107.2 10.0 %grad_head.1 = bf16[5120,1024]{1,0:T(8,128)(2,1)} custom-call(bf16[64,5120]{1,0:T(8,128)(2,1)S(1)} %constant_dynamic-update-slice_fusion.refs_0_, bf16[64,5120]{1,0:T(8,128)(2,1)S(1)} %collective-permute-done.3.x_ref.refs_1_, bf16[64,5120]{1,0:T(8,128)(2,1)S(1)} %collective-permute-done.4.y_ref.refs_2_, bf16[64,2560]{1,0:T(8,128)(2,1)} %collective-permute-done.5.refs_3_, ...), custom_call_target="tpu_custom_call" | custom-call | flops 1 | bytes 1 | tf_op jit(solution)/shard_map/grad_head/pallas_call | solution.py:592
  117.2 0.3 first_sum.1
  117.5 0.1 collective-permute-start.20
  117.6 2.5 %collective-permute-start.21 = (bf16[2,16,1792]{2,1,0:T(8,128)(2,1)S(1)}, bf16[2,16,1792]{2,1,0:T(8,128)(2,1)S(1)}, u32[]{:S(2)}, u32[]{:S(2)}) collective-permute-start(bf16[2,16,1792]{2,1,0:T(8,128)(2,1)S(1)} %get-tuple-element.113), channel_id=1, source_target_pairs={{0,16},{1,17},{2,18},{3,19},{4,20},{5,21},{6,22},{7,23},{8,24},{9,... | collective-permute-start | bytes 344072 | tf_op jit(solution)/shard_map/ppermute | solution.py:134
  120.1 1.8 %collective-permute-start.22 = (bf16[2,16,1792]{2,1,0:T(8,128)(2,1)S(1)}, bf16[2,16,1792]{2,1,0:T(8,128)(2,1)S(1)}, u32[]{:S(2)}, u32[]{:S(2)}) collective-permute-start(bf16[2,16,1792]{2,1,0:T(8,128)(2,1)S(1)} %get-tuple-element.114), channel_id=1, source_target_pairs={{0,24},{1,25},{2,26},{3,27},{4,28},{5,29},{6,30},{7,31},{8,16},{9,... | collective-permute-start | bytes 344072 | tf_op jit(solution)/shard_map/ppermute | solution.py:134
  122.0 0.5 collective-permute-start.23
  122.4 1.3 collective-permute-start.24
  123.7 2.4 %collective-permute-done.23.refs_5_ = bf16[2,16,768]{2,1,0:T(8,128)(2,1)S(1)} collective-permute-done((bf16[2,16,768]{2,1,0:T(8,128)(2,1)S(1)}, bf16[2,16,768]{2,1,0:T(8,128)(2,1)S(1)}, u32[]{:S(2)}, u32[]{:S(2)}) %collective-permute-start.23) | collective-permute-done | bytes 49184 | tf_op jit(solution)/shard_map/ppermute | solution.py:134
  126.1 1.2 collective-permute-start.25
  127.2 3.8 %collective-permute-done.25.refs_7_ = bf16[2,16,768]{2,1,0:T(8,128)(2,1)S(1)} collective-permute-done((bf16[2,16,768]{2,1,0:T(8,128)(2,1)S(1)}, bf16[2,16,768]{2,1,0:T(8,128)(2,1)S(1)}, u32[]{:S(2)}, u32[]{:S(2)}) %collective-permute-start.25) | collective-permute-done | bytes 49184 | tf_op jit(solution)/shard_map/ppermute | solution.py:134
  131.1 0.1 last_sum.1
  131.2 0.1 collective-permute-start.26
  131.2 0.6 slice_reduce_fusion
  131.9 0.6 collective-permute-done.26
  132.5 0.7 pad_maximum_fusion
  (35 shorter events, 0.1 us)
Async XLA Ops:
  0.6 17.3 %collective-permute-start.1 = (bf16[16,5120]{1,0:T(8,128)(2,1)}, bf16[16,5120]{1,0:T(8,128)(2,1)S(1)}, u32[]{:S(2)}, u32[]{:S(2)}) collective-permute-start(bf16[16,5120]{1,0:T(8,128)(2,1)} %param.7), channel_id=1, source_target_pairs={{0,16},{1,17},{2,18},{3,19},{4,20},{5,21},{6,22},{7,23},{8,24},{9,... | collective-permute-start | bytes 491528 | tf_op jit(solution)/shard_map/ppermute | solution.py:134
  4.7 13.2 %collective-permute-start = (bf16[16,5120]{1,0:T(8,128)(2,1)}, bf16[16,5120]{1,0:T(8,128)(2,1)S(1)}, u32[]{:S(2)}, u32[]{:S(2)}) collective-permute-start(bf16[16,5120]{1,0:T(8,128)(2,1)} %param.7), channel_id=1, source_target_pairs={{0,8},{1,9},{2,10},{3,11},{4,12},{5,13},{6,14},{7,15},{8,0},{9,1},... | collective-permute-start | bytes 491528 | tf_op jit(solution)/shard_map/ppermute | solution.py:134
  6.3 11.7 %collective-permute-start.2 = (bf16[16,5120]{1,0:T(8,128)(2,1)}, bf16[16,5120]{1,0:T(8,128)(2,1)S(1)}, u32[]{:S(2)}, u32[]{:S(2)}) collective-permute-start(bf16[16,5120]{1,0:T(8,128)(2,1)} %param.7), channel_id=1, source_target_pairs={{0,24},{1,25},{2,26},{3,27},{4,28},{5,29},{6,30},{7,31},{8,16},{9,... | collective-permute-start | bytes 491528 | tf_op jit(solution)/shard_map/ppermute | solution.py:134
  7.7 1.0 copy-start.1
  10.8 33.1 %all-to-all-start = ((bf16[32,67,128]{2,1,0:T(8,128)(2,1)}), bf16[32,67,128]{2,1,0:T(8,128)(2,1)}, u32[]{:S(2)}, u32[]{:S(2)}) async-start(bf16[32,67,128]{2,1,0:T(8,128)(2,1)} %slice.8), calls=%async_computation | async-start | bytes 1179648 | tf_op jit(solution)/shard_map/all_to_all | solution.py:499
  18.0 22.4 %collective-permute-start.4 = (bf16[64,5120]{1,0:T(8,128)(2,1)S(1)}, bf16[64,5120]{1,0:T(8,128)(2,1)S(1)}, u32[]{:S(2)}, u32[]{:S(2)}) collective-permute-start(bf16[64,5120]{1,0:T(8,128)(2,1)S(1)} %constant_dynamic-update-slice_fusion.refs_0_), channel_id=1, source_target_pairs={{0,4},{1,5},{2,6},{3,7},{4,0},{5,1},{6,2},{7,3},{8,12},{9,13},{10,... | collective-permute-start | bytes 1966088 | tf_op jit(solution)/shard_map/ppermute | solution.py:134
  19.8 20.7 %collective-permute-start.3 = (bf16[64,5120]{1,0:T(8,128)(2,1)S(1)}, bf16[64,5120]{1,0:T(8,128)(2,1)S(1)}, u32[]{:S(2)}, u32[]{:S(2)}) collective-permute-start(bf16[64,5120]{1,0:T(8,128)(2,1)S(1)} %constant_dynamic-update-slice_fusion.refs_0_), channel_id=1, source_target_pairs={{0,2},{1,3},{2,0},{3,1},{4,6},{5,7},{6,4},{7,5},{8,10},{9,11},{10,... | collective-permute-start | bytes 1966088 | tf_op jit(solution)/shard_map/ppermute | solution.py:134
  21.5 22.4 %copy-start.2 = (s32[4,128]{1,0:T(4,128)S(1)}, s32[4,128]{1,0:T(4,128)}, u32[]{:S(2)}) copy-start(s32[4,128]{1,0:T(4,128)} %param.11) | copy-start | bytes 6148
  21.5 22.4 %copy-start.3 = (f32[512]{0:T(512)S(1)}, f32[512]{0:T(512)}, u32[]{:S(2)}) copy-start(f32[512]{0:T(512)} %param.12) | copy-start | bytes 6148
  26.9 26.2 %collective-permute-start.7 = (bf16[64,5120]{1,0:T(8,128)(2,1)S(1)}, bf16[64,5120]{1,0:T(8,128)(2,1)S(1)}, u32[]{:S(2)}, u32[]{:S(2)}) collective-permute-start(bf16[64,5120]{1,0:T(8,128)(2,1)S(1)} %constant_dynamic-update-slice_fusion.refs_0_), channel_id=1, source_target_pairs={{0,1},{1,0},{2,3},{3,2},{4,5},{5,4},{6,7},{7,6},{8,9},{9,8},{10,11... | collective-permute-start | bytes 1966088 | tf_op jit(solution)/shard_map/ppermute | solution.py:134
  40.5 14.5 %collective-permute-start.8 = (bf16[64,5120]{1,0:T(8,128)(2,1)S(1)}, bf16[64,5120]{1,0:T(8,128)(2,1)S(1)}, u32[]{:S(2)}, u32[]{:S(2)}) collective-permute-start(bf16[64,5120]{1,0:T(8,128)(2,1)S(1)} %collective-permute-done.3.x_ref.refs_1_), channel_id=1, source_target_pairs={{0,1},{1,0},{2,3},{3,2},{4,5},{5,4},{6,7},{7,6},{8,9},{9,8},{10,11... | collective-permute-start | bytes 1966088 | tf_op jit(solution)/shard_map/ppermute | solution.py:134
  41.4 13.6 %collective-permute-start.9 = (bf16[64,5120]{1,0:T(8,128)(2,1)S(1)}, bf16[64,5120]{1,0:T(8,128)(2,1)}, u32[]{:S(2)}, u32[]{:S(2)}) collective-permute-start(bf16[64,5120]{1,0:T(8,128)(2,1)S(1)} %collective-permute-done.4.y_ref.refs_2_), channel_id=1, source_target_pairs={{0,1},{1,0},{2,3},{3,2},{4,5},{5,4},{6,7},{7,6},{8,9},{9,8},{10,11... | collective-permute-start | bytes 1966088 | tf_op jit(solution)/shard_map/ppermute | solution.py:134
  41.9 9.9 %collective-permute-start.5 = (bf16[64,2560]{1,0:T(8,128)(2,1)}, bf16[64,2560]{1,0:T(8,128)(2,1)}, u32[]{:S(2)}, u32[]{:S(2)}) collective-permute-start(bf16[64,2560]{1,0:T(8,128)(2,1)} %get-tuple-element.64), channel_id=1, source_target_pairs={{0,4},{1,5},{2,6},{3,7},{4,0},{5,1},{6,2},{7,3},{8,12},{9,13},{10,... | collective-permute-start | bytes 983048 | tf_op jit(solution)/shard_map/ppermute | solution.py:134
  43.0 9.7 %collective-permute-start.6 = (bf16[64,2560]{1,0:T(8,128)(2,1)}, bf16[64,2560]{1,0:T(8,128)(2,1)}, u32[]{:S(2)}, u32[]{:S(2)}) collective-permute-start(bf16[64,2560]{1,0:T(8,128)(2,1)} %get-tuple-element.65), channel_id=1, source_target_pairs={{0,2},{1,3},{2,0},{3,1},{4,6},{5,7},{6,4},{7,5},{8,10},{9,11},{10,... | collective-permute-start | bytes 983048 | tf_op jit(solution)/shard_map/ppermute | solution.py:134
  52.6 27.1 %copy-start.4 = (f32[512]{0:T(512)S(1)}, f32[512]{0:T(512)}, u32[]{:S(2)}) copy-start(f32[512]{0:T(512)} %param.13) | copy-start | bytes 6148
  52.6 1.8 %collective-permute-start.10 = (bf16[64,2560]{1,0:T(8,128)(2,1)}, bf16[64,2560]{1,0:T(8,128)(2,1)S(1)}, u32[]{:S(2)}, u32[]{:S(2)}) collective-permute-start(bf16[64,2560]{1,0:T(8,128)(2,1)} %collective-permute-done.5.refs_3_), channel_id=1, source_target_pairs={{0,1},{1,0},{2,3},{3,2},{4,5},{5,4},{6,7},{7,6},{8,9},{9,8},{10,11... | collective-permute-start | bytes 983048 | tf_op jit(solution)/shard_map/ppermute | solution.py:134
  52.6 2.3 %collective-permute-start.11 = (bf16[64,2560]{1,0:T(8,128)(2,1)}, bf16[64,2560]{1,0:T(8,128)(2,1)S(1)}, u32[]{:S(2)}, u32[]{:S(2)}) collective-permute-start(bf16[64,2560]{1,0:T(8,128)(2,1)} %collective-permute-done.6.refs_4_), channel_id=1, source_target_pairs={{0,1},{1,0},{2,3},{3,2},{4,5},{5,4},{6,7},{7,6},{8,9},{9,8},{10,11... | collective-permute-start | bytes 983048 | tf_op jit(solution)/shard_map/ppermute | solution.py:134
  54.9 28.8 %collective-permute-start.13 = (bf16[2560,1024]{1,0:T(8,128)(2,1)}, bf16[2560,1024]{1,0:T(8,128)(2,1)S(1)}, u32[]{:S(2)}, u32[]{:S(2)}) collective-permute-start(bf16[2560,1024]{1,0:T(8,128)(2,1)} %constant_dynamic-slice_fusion), channel_id=1, source_target_pairs={{0,1},{1,0},{2,3},{3,2},{4,5},{5,4},{6,7},{7,6},{8,9},{9,8},{10,11... | collective-permute-start | bytes 15728648 | tf_op jit(solution)/shard_map/ppermute | solution.py:134
  81.1 11.4 %copy-start = (bf16[512,1024]{1,0:T(8,128)(2,1)}, bf16[512,1024]{1,0:T(8,128)(2,1)S(1)}, u32[]{:S(2)}) copy-start(bf16[512,1024]{1,0:T(8,128)(2,1)S(1)} %get-tuple-element.101.grad_ref.refs_10_) | copy-start | bytes 3145732
  81.1 2.7 %collective-permute-start.12 = (bf16[512,1024]{1,0:T(8,128)(2,1)S(1)}, bf16[512,1024]{1,0:T(8,128)(2,1)S(1)}, u32[]{:S(2)}, u32[]{:S(2)}) collective-permute-start(bf16[512,1024]{1,0:T(8,128)(2,1)S(1)} %get-tuple-element.101.grad_ref.refs_10_), channel_id=1, source_target_pairs={{0,1},{1,0},{2,3},{3,2},{4,5},{5,4},{6,7},{7,6},{8,9},{9,8},{10,11... | collective-permute-start | bytes 3145736 | tf_op jit(solution)/shard_map/ppermute | solution.py:134
  92.4 24.8 %collective-permute-start.14 = (bf16[4,2,16,1792]{3,2,1,0:T(8,128)(2,1)S(1)}, bf16[4,2,16,1792]{3,2,1,0:T(8,128)(2,1)S(1)}, u32[]{:S(2)}, u32[]{:S(2)}) collective-permute-start(bf16[4,2,16,1792]{3,2,1,0:T(8,128)(2,1)S(1)} %get-tuple-element.95), channel_id=1, source_target_pairs={{0,2},{1,3},{2,0},{3,1},{4,6},{5,7},{6,4},{7,5},{8,10},{9,11},{10,... | collective-permute-start | bytes 1376264 | tf_op jit(solution)/shard_map/ppermute | solution.py:134
  92.9 24.3 %collective-permute-start.15 = (bf16[4,2,16,1792]{3,2,1,0:T(8,128)(2,1)S(1)}, bf16[4,2,16,1792]{3,2,1,0:T(8,128)(2,1)S(1)}, u32[]{:S(2)}, u32[]{:S(2)}) collective-permute-start(bf16[4,2,16,1792]{3,2,1,0:T(8,128)(2,1)S(1)} %get-tuple-element.96), channel_id=1, source_target_pairs={{0,4},{1,5},{2,6},{3,7},{4,0},{5,1},{6,2},{7,3},{8,12},{9,13},{10,... | collective-permute-start | bytes 1376264 | tf_op jit(solution)/shard_map/ppermute | solution.py:134
  93.9 23.3 %collective-permute-start.16 = (bf16[4,2,16,1792]{3,2,1,0:T(8,128)(2,1)S(1)}, bf16[4,2,16,1792]{3,2,1,0:T(8,128)(2,1)S(1)}, u32[]{:S(2)}, u32[]{:S(2)}) collective-permute-start(bf16[4,2,16,1792]{3,2,1,0:T(8,128)(2,1)S(1)} %get-tuple-element.97), channel_id=1, source_target_pairs={{0,6},{1,7},{2,4},{3,5},{4,2},{5,3},{6,0},{7,1},{8,14},{9,15},{10,... | collective-permute-start | bytes 1376264 | tf_op jit(solution)/shard_map/ppermute | solution.py:134
  96.0 9.4 %collective-permute-start.17 = (bf16[4,2,16,768]{3,2,1,0:T(8,128)(2,1)S(1)}, bf16[4,2,16,768]{3,2,1,0:T(8,128)(2,1)S(1)}, u32[]{:S(2)}, u32[]{:S(2)}) collective-permute-start(bf16[4,2,16,768]{3,2,1,0:T(8,128)(2,1)S(1)} %get-tuple-element.98), channel_id=1, source_target_pairs={{0,8},{1,9},{2,10},{3,11},{4,12},{5,13},{6,14},{7,15},{8,0},{9,1},... | collective-permute-start | bytes 589832 | tf_op jit(solution)/shard_map/ppermute | solution.py:134
  96.7 20.5 %collective-permute-start.18 = (bf16[4,2,16,768]{3,2,1,0:T(8,128)(2,1)S(1)}, bf16[4,2,16,768]{3,2,1,0:T(8,128)(2,1)S(1)}, u32[]{:S(2)}, u32[]{:S(2)}) collective-permute-start(bf16[4,2,16,768]{3,2,1,0:T(8,128)(2,1)S(1)} %get-tuple-element.99), channel_id=1, source_target_pairs={{0,16},{1,17},{2,18},{3,19},{4,20},{5,21},{6,22},{7,23},{8,24},{9,... | collective-permute-start | bytes 589832 | tf_op jit(solution)/shard_map/ppermute | solution.py:134
  105.4 11.8 %collective-permute-start.19 = (bf16[4,2,16,768]{3,2,1,0:T(8,128)(2,1)S(1)}, bf16[4,2,16,768]{3,2,1,0:T(8,128)(2,1)S(1)}, u32[]{:S(2)}, u32[]{:S(2)}) collective-permute-start(bf16[4,2,16,768]{3,2,1,0:T(8,128)(2,1)S(1)} %get-tuple-element.100), channel_id=1, source_target_pairs={{0,24},{1,25},{2,26},{3,27},{4,28},{5,29},{6,30},{7,31},{8,16},{9,... | collective-permute-start | bytes 589832 | tf_op jit(solution)/shard_map/ppermute | solution.py:134
  117.5 13.5 %collective-permute-start.20 = (bf16[2,16,1792]{2,1,0:T(8,128)(2,1)S(1)}, bf16[2,16,1792]{2,1,0:T(8,128)(2,1)S(1)}, u32[]{:S(2)}, u32[]{:S(2)}) collective-permute-start(bf16[2,16,1792]{2,1,0:T(8,128)(2,1)S(1)} %get-tuple-element.112), channel_id=1, source_target_pairs={{0,8},{1,9},{2,10},{3,11},{4,12},{5,13},{6,14},{7,15},{8,0},{9,1},... | collective-permute-start | bytes 344072 | tf_op jit(solution)/shard_map/ppermute | solution.py:134
  117.6 13.5 %collective-permute-start.21 = (bf16[2,16,1792]{2,1,0:T(8,128)(2,1)S(1)}, bf16[2,16,1792]{2,1,0:T(8,128)(2,1)S(1)}, u32[]{:S(2)}, u32[]{:S(2)}) collective-permute-start(bf16[2,16,1792]{2,1,0:T(8,128)(2,1)S(1)} %get-tuple-element.113), channel_id=1, source_target_pairs={{0,16},{1,17},{2,18},{3,19},{4,20},{5,21},{6,22},{7,23},{8,24},{9,... | collective-permute-start | bytes 344072 | tf_op jit(solution)/shard_map/ppermute | solution.py:134
  120.1 10.9 %collective-permute-start.22 = (bf16[2,16,1792]{2,1,0:T(8,128)(2,1)S(1)}, bf16[2,16,1792]{2,1,0:T(8,128)(2,1)S(1)}, u32[]{:S(2)}, u32[]{:S(2)}) collective-permute-start(bf16[2,16,1792]{2,1,0:T(8,128)(2,1)S(1)} %get-tuple-element.114), channel_id=1, source_target_pairs={{0,24},{1,25},{2,26},{3,27},{4,28},{5,29},{6,30},{7,31},{8,16},{9,... | collective-permute-start | bytes 344072 | tf_op jit(solution)/shard_map/ppermute | solution.py:134
  122.0 4.1 %collective-permute-start.23 = (bf16[2,16,768]{2,1,0:T(8,128)(2,1)S(1)}, bf16[2,16,768]{2,1,0:T(8,128)(2,1)S(1)}, u32[]{:S(2)}, u32[]{:S(2)}) collective-permute-start(bf16[2,16,768]{2,1,0:T(8,128)(2,1)S(1)} %get-tuple-element.116), channel_id=1, source_target_pairs={{0,2},{1,3},{2,0},{3,1},{4,6},{5,7},{6,4},{7,5},{8,10},{9,11},{10,... | collective-permute-start | bytes 147464 | tf_op jit(solution)/shard_map/ppermute | solution.py:134
  122.4 4.8 %collective-permute-start.24 = (bf16[2,16,768]{2,1,0:T(8,128)(2,1)S(1)}, bf16[2,16,768]{2,1,0:T(8,128)(2,1)S(1)}, u32[]{:S(2)}, u32[]{:S(2)}) collective-permute-start(bf16[2,16,768]{2,1,0:T(8,128)(2,1)S(1)} %get-tuple-element.117), channel_id=1, source_target_pairs={{0,4},{1,5},{2,6},{3,7},{4,0},{5,1},{6,2},{7,3},{8,12},{9,13},{10,... | collective-permute-start | bytes 147464 | tf_op jit(solution)/shard_map/ppermute | solution.py:134
  126.1 5.0 %collective-permute-start.25 = (bf16[2,16,768]{2,1,0:T(8,128)(2,1)S(1)}, bf16[2,16,768]{2,1,0:T(8,128)(2,1)S(1)}, u32[]{:S(2)}, u32[]{:S(2)}) collective-permute-start(bf16[2,16,768]{2,1,0:T(8,128)(2,1)S(1)} %get-tuple-element.118), channel_id=1, source_target_pairs={{0,6},{1,7},{2,4},{3,5},{4,2},{5,3},{6,0},{7,1},{8,14},{9,15},{10,... | collective-permute-start | bytes 147464 | tf_op jit(solution)/shard_map/ppermute | solution.py:134
  131.2 1.3 %collective-permute-start.26 = (bf16[16,2560]{1,0:T(8,128)(2,1)S(1)}, bf16[16,2560]{1,0:T(8,128)(2,1)S(1)}, u32[]{:S(2)}, u32[]{:S(2)}) collective-permute-start(bf16[16,2560]{1,0:T(8,128)(2,1)S(1)} %get-tuple-element.120), channel_id=1, source_target_pairs={{0,1},{1,0},{2,3},{3,2},{4,5},{5,4},{6,7},{7,6},{8,9},{9,8},{10,11... | collective-permute-start | bytes 245768 | tf_op jit(solution)/shard_map/ppermute | solution.py:134

commit v20 on v19

--- a/solution.py
+++ b/solution.py
@@ -524,7 +524,7 @@
     pieces, sent_w = lax.optimization_barrier((pieces, sent_w))
     sib_w = shift(sent_w, 1)
 
-    width = 256 if slab % 256 == 0 else 128
+    width = 512 if slab % 512 == 0 else 128
     tiles = slab // width
     whole = lambda t: (0, 0)
     logits, stat = pl.pallas_call(

time: 134 us -> 133 us (level)
  no operation moved by 1% of the time
where the time goes in v20:
time: 133 us
  Pallas kernels  37.8 us (28%)
  waiting for transfers between devices  35.9 us (27%)
  starting transfers between devices  33.2 us (25%)
  blocking collectives  13.7 us (10%)
  local copies, waits for them, and re-layouts  9.21 us (7%)
  other arithmetic  2 us (2%)
    ppermute x27, waiting for transfers between devices, shift(): return lax.ppermute(x, 'vocab', [(i, i ^ distance) for i in range(n)])  35.9 us
    ppermute x27, starting transfers between devices, shift(): return lax.ppermute(x, 'vocab', [(i, i ^ distance) for i in range(n)])  27 us
    all_to_all x1, blocking collectives, levels_plan(): lax.all_to_all(stat, 'vocab', split_axis=0, concat_axis=0, tiled=True)  13.7 us
    pallas_call x1, Pallas kernels, levels_plan(): pl.pallas_call(functools.partial(logits_kernel, rows), grid=(2 * tiles,),...  10.5 us
    pallas_call x1, Pallas kernels, levels_plan(): pl.pallas_call(functools.partial(head_kernel, rows), grid=(4,), in_specs=...  9.95 us
    pallas_call x1, Pallas kernels, levels_plan(): pl.pallas_call(functools.partial(partial_kernel, rows), grid_spec=pltpu.P...  8.63 us
    all_to_all x1, starting transfers between devices, levels_plan(): lax.all_to_all(payload[:, :3 - STAT_ROWS], 'vocab', split_axis=0, concat_...  6.18 us
    dynamic_slice x1, local copies, waits for them, and re-layouts, levels_plan(): lax.dynamic_slice(head_weight, ((1 - core) * half, 0), (half, slab))  5.43 us
  transfers between devices with their start and end apart: 28, of which 10 were waited for; matrix products, arithmetic and copies ran while one was open for 7% of the time, Pallas kernels for 22%

profile of v20, /device:TPU:0, one launch (start us, length us, event | category | flops | bytes accessed | tf_op | source)
XLA Modules:
  0.0 132.7 jit_solution(2833190792027446177)
XLA Ops:
  0.6 4.1 %collective-permute-start.1 = (bf16[16,5120]{1,0:T(8,128)(2,1)}, bf16[16,5120]{1,0:T(8,128)(2,1)S(1)}, u32[]{:S(2)}, u32[]{:S(2)}) collective-permute-start(bf16[16,5120]{1,0:T(8,128)(2,1)} %param.7), channel_id=1, source_target_pairs={{0,16},{1,17},{2,18},{3,19},{4,20},{5,21},{6,22},{7,23},{8,24},{9,... | collective-permute-start | bytes 491528 | tf_op jit(solution)/shard_map/ppermute | solution.py:134
  4.7 1.6 %collective-permute-start = (bf16[16,5120]{1,0:T(8,128)(2,1)}, bf16[16,5120]{1,0:T(8,128)(2,1)S(1)}, u32[]{:S(2)}, u32[]{:S(2)}) collective-permute-start(bf16[16,5120]{1,0:T(8,128)(2,1)} %param.7), channel_id=1, source_target_pairs={{0,8},{1,9},{2,10},{3,11},{4,12},{5,13},{6,14},{7,15},{8,0},{9,1},... | collective-permute-start | bytes 491528 | tf_op jit(solution)/shard_map/ppermute | solution.py:134
  6.3 0.7 add_select_fusion.1
  7.0 0.1 iota_compare_fusion
  7.1 0.2 convert_reduce_fusion
  7.3 0.1 add.86
  7.4 0.1 add.83
  7.5 0.1 add.89
  7.7 0.0 copy-start.1
  7.7 0.9 copy-done.1
  8.6 1.3 pack_teacher.1
  9.9 0.9 slice.8
  10.8 6.2 %all-to-all-start = ((bf16[32,67,128]{2,1,0:T(8,128)(2,1)}), bf16[32,67,128]{2,1,0:T(8,128)(2,1)}, u32[]{:S(2)}, u32[]{:S(2)}) async-start(bf16[32,67,128]{2,1,0:T(8,128)(2,1)} %slice.8), calls=%async_computation | async-start | bytes 1179648 | tf_op jit(solution)/shard_map/all_to_all | solution.py:499
  17.0 0.9 constant_dynamic-update-slice_fusion.3
  18.0 1.8 %collective-permute-start.4 = (bf16[64,5120]{1,0:T(8,128)(2,1)S(1)}, bf16[64,5120]{1,0:T(8,128)(2,1)S(1)}, u32[]{:S(2)}, u32[]{:S(2)}) collective-permute-start(bf16[64,5120]{1,0:T(8,128)(2,1)S(1)} %constant_dynamic-update-slice_fusion.refs_0_), channel_id=1, source_target_pairs={{0,4},{1,5},{2,6},{3,7},{4,0},{5,1},{6,2},{7,3},{8,12},{9,13},{10,... | collective-permute-start | bytes 1966088 | tf_op jit(solution)/shard_map/ppermute | solution.py:134
  19.8 1.5 %collective-permute-start.3 = (bf16[64,5120]{1,0:T(8,128)(2,1)S(1)}, bf16[64,5120]{1,0:T(8,128)(2,1)S(1)}, u32[]{:S(2)}, u32[]{:S(2)}) collective-permute-start(bf16[64,5120]{1,0:T(8,128)(2,1)S(1)} %constant_dynamic-update-slice_fusion.refs_0_), channel_id=1, source_target_pairs={{0,2},{1,3},{2,0},{3,1},{4,6},{5,7},{6,4},{7,5},{8,10},{9,11},{10,... | collective-permute-start | bytes 1966088 | tf_op jit(solution)/shard_map/ppermute | solution.py:134
  21.3 0.2 select_reduce_fusion
  21.5 0.0 copy-start.2
  21.5 0.0 copy-start.3
  21.5 5.4 %constant_dynamic-slice_fusion = bf16[2560,1024]{1,0:T(8,128)(2,1)} fusion(bf16[5120,1024]{1,0:T(8,128)(2,1)} %w_ref.1, s32[]{:T(128)S(6)} %select_n.54), kind=kLoop, calls=%fused_computation.27 | loop fusion | bytes 10485764 | tf_op jit(solution)/shard_map/dynamic_slice | solution.py:486
  26.9 13.5 %collective-permute-done.4.y_ref.refs_2_ = bf16[64,5120]{1,0:T(8,128)(2,1)S(1)} collective-permute-done((bf16[64,5120]{1,0:T(8,128)(2,1)S(1)}, bf16[64,5120]{1,0:T(8,128)(2,1)S(1)}, u32[]{:S(2)}, u32[]{:S(2)}) %collective-permute-start.4) | collective-permute-done | bytes 655392 | tf_op jit(solution)/shard_map/ppermute | solution.py:134
  40.4 0.0 collective-permute-done.3.x_ref.refs_1_
  40.5 0.0 collective-permute-start.8
  40.5 0.9 cut_halves.1
  41.4 0.5 collective-permute-start.9
  41.9 1.1 collective-permute-start.5
  43.0 0.8 collective-permute-start.6
  43.8 0.1 pad_add_fusion.refs_0_.core_ref
  43.9 4.9 %teacher_prob.1 = (f32[512,1024]{1,0:T(8,128)S(1)}, f32[16,128]{1,0:T(8,128)S(1)}) custom-call(s32[4]{0:T(128)S(1)} %pad_add_fusion.refs_0_.core_ref, s32[4,4]{1,0:T(4,128)S(1)} %broadcast_add_fusion.1.refs_1_, bf16[32,67,128]{2,1,0:T(8,128)(2,1)} %all-to-all-done.refs_2_, s32[4,1,128]{2,1,0:T(1,128)S(1)} %bitcast.9, f32[4,1,128]{2,1,0:T(1,128)S(1)} %bitcast.10), custom_call_target="tpu_custom_call" | custom-call | flops 1 | bytes 1 | tf_op jit(solution)/shard_map/teacher_prob/pallas_call | solution.py:503
  48.8 3.0 %collective-permute-done.5.refs_3_ = bf16[64,2560]{1,0:T(8,128)(2,1)} collective-permute-done((bf16[64,2560]{1,0:T(8,128)(2,1)}, bf16[64,2560]{1,0:T(8,128)(2,1)}, u32[]{:S(2)}, u32[]{:S(2)}) %collective-permute-start.5) | collective-permute-done | bytes 327712 | tf_op jit(solution)/shard_map/ppermute | solution.py:134
  51.8 0.8 collective-permute-done.6.refs_4_
  52.6 0.0 collective-permute-start.10
  52.6 0.5 collective-permute-start.11
  53.1 1.3 collective-permute-done.10.refs_8_
  54.5 0.5 collective-permute-done.11.refs_9_
  54.9 0.1 collective-permute-start.13
  55.1 10.5 %logits.1 = (f32[512,1024]{1,0:T(8,128)S(1)}, f32[32,8,128]{2,1,0:T(8,128)S(1)}) custom-call(bf16[64,5120]{1,0:T(8,128)(2,1)S(1)} %constant_dynamic-update-slice_fusion.refs_0_, bf16[64,5120]{1,0:T(8,128)(2,1)S(1)} %collective-permute-done.3.x_ref.refs_1_, bf16[64,5120]{1,0:T(8,128)(2,1)S(1)} %collective-permute-done.4.y_ref.refs_2_, ...), custom_call_target="tpu_custom_call" | custom-call | flops 1 | bytes 1 | tf_op jit(solution)/shard_map/logits/pallas_call | solution.py:530
  65.6 13.7 %all_to_all.10.refs_1_ = f32[32,8,128]{2,1,0:T(8,128)S(1)} all-to-all(f32[32,8,128]{2,1,0:T(8,128)S(1)} %get-tuple-element.81), channel_id=1, replica_groups=mesh['vocab'=32] {'vocab'}, dimensions={0} | all-to-all | bytes 262144 | tf_op jit(solution)/shard_map/all_to_all | solution.py:550
  79.3 1.3 grad_logits.1
  80.6 0.3 collective-permute-start.12
  80.9 2.4 %collective-permute-done.12.sib_ref = bf16[512,1024]{1,0:T(8,128)(2,1)S(1)} collective-permute-done((bf16[512,1024]{1,0:T(8,128)(2,1)S(1)}, bf16[512,1024]{1,0:T(8,128)(2,1)S(1)}, u32[]{:S(2)}, u32[]{:S(2)}) %collective-permute-start.12) | collective-permute-done | bytes 1048608 | tf_op jit(solution)/shard_map/ppermute | solution.py:134
  83.3 8.6 %grad_hidden_partial.1 = (f32[4,2,16,1792]{3,2,1,0:T(8,128)S(1)}, bf16[4,2,16,1792]{3,2,1,0:T(8,128)(2,1)S(1)}, bf16[4,2,16,1792]{3,2,1,0:T(8,128)(2,1)S(1)}, bf...) custom-call(s32[4]{0:T(128)S(1)} %pad_add_fusion.refs_0_.core_ref, ...), custom_call_target="tpu_custom_call" | custom-call | flops 1 | bytes 1 | tf_op jit(solution)/shard_map/grad_hidden_partial/pallas_call | solution.py:568
  92.0 0.5 collective-permute-start.14
  92.5 1.0 collective-permute-start.15
  93.4 2.1 %collective-permute-start.16 = (bf16[4,2,16,1792]{3,2,1,0:T(8,128)(2,1)S(1)}, bf16[4,2,16,1792]{3,2,1,0:T(8,128)(2,1)S(1)}, u32[]{:S(2)}, u32[]{:S(2)}) collective-permute-start(bf16[4,2,16,1792]{3,2,1,0:T(8,128)(2,1)S(1)} %get-tuple-element.97), channel_id=1, source_target_pairs={{0,6},{1,7},{2,4},{3,5},{4,2},{5,3},{6,0},{7,1},{8,14},{9,15},{10,... | collective-permute-start | bytes 1376264 | tf_op jit(solution)/shard_map/ppermute | solution.py:134
  95.5 0.7 collective-permute-start.17
  96.2 1.2 collective-permute-start.18
  97.4 7.5 %collective-permute-done.17.refs_5_ = bf16[4,2,16,768]{3,2,1,0:T(8,128)(2,1)S(1)} collective-permute-done((bf16[4,2,16,768]{3,2,1,0:T(8,128)(2,1)S(1)}, bf16[4,2,16,768]{3,2,1,0:T(8,128)(2,1)S(1)}, u32[]{:S(2)}, u32[]{:S(2)}) %collective-permute-start.17) | collective-permute-done | bytes 196640 | tf_op jit(solution)/shard_map/ppermute | solution.py:134
  104.9 1.9 %collective-permute-start.19 = (bf16[4,2,16,768]{3,2,1,0:T(8,128)(2,1)S(1)}, bf16[4,2,16,768]{3,2,1,0:T(8,128)(2,1)S(1)}, u32[]{:S(2)}, u32[]{:S(2)}) collective-permute-start(bf16[4,2,16,768]{3,2,1,0:T(8,128)(2,1)S(1)} %get-tuple-element.100), channel_id=1, source_target_pairs={{0,24},{1,25},{2,26},{3,27},{4,28},{5,29},{6,30},{7,31},{8,16},{9,... | collective-permute-start | bytes 589832 | tf_op jit(solution)/shard_map/ppermute | solution.py:134
  106.8 9.9 %grad_head.1 = bf16[5120,1024]{1,0:T(8,128)(2,1)} custom-call(bf16[64,5120]{1,0:T(8,128)(2,1)S(1)} %constant_dynamic-update-slice_fusion.refs_0_, bf16[64,5120]{1,0:T(8,128)(2,1)S(1)} %collective-permute-done.3.x_ref.refs_1_, bf16[64,5120]{1,0:T(8,128)(2,1)S(1)} %collective-permute-done.4.y_ref.refs_2_, bf16[64,2560]{1,0:T(8,128)(2,1)} %collective-permute-done.5.refs_3_, ...), custom_call_target="tpu_custom_call" | custom-call | flops 1 | bytes 1 | tf_op jit(solution)/shard_map/grad_head/pallas_call | solution.py:592
  116.7 0.3 first_sum.1
  117.0 0.1 collective-permute-start.20
  117.1 2.5 %collective-permute-start.21 = (bf16[2,16,1792]{2,1,0:T(8,128)(2,1)S(1)}, bf16[2,16,1792]{2,1,0:T(8,128)(2,1)S(1)}, u32[]{:S(2)}, u32[]{:S(2)}) collective-permute-start(bf16[2,16,1792]{2,1,0:T(8,128)(2,1)S(1)} %get-tuple-element.113), channel_id=1, source_target_pairs={{0,16},{1,17},{2,18},{3,19},{4,20},{5,21},{6,22},{7,23},{8,24},{9,... | collective-permute-start | bytes 344072 | tf_op jit(solution)/shard_map/ppermute | solution.py:134
  119.6 1.8 %collective-permute-start.22 = (bf16[2,16,1792]{2,1,0:T(8,128)(2,1)S(1)}, bf16[2,16,1792]{2,1,0:T(8,128)(2,1)S(1)}, u32[]{:S(2)}, u32[]{:S(2)}) collective-permute-start(bf16[2,16,1792]{2,1,0:T(8,128)(2,1)S(1)} %get-tuple-element.114), channel_id=1, source_target_pairs={{0,24},{1,25},{2,26},{3,27},{4,28},{5,29},{6,30},{7,31},{8,16},{9,... | collective-permute-start | bytes 344072 | tf_op jit(solution)/shard_map/ppermute | solution.py:134
  121.5 0.5 collective-permute-start.23
  122.0 1.3 collective-permute-start.24
  123.2 2.4 %collective-permute-done.23.refs_5_ = bf16[2,16,768]{2,1,0:T(8,128)(2,1)S(1)} collective-permute-done((bf16[2,16,768]{2,1,0:T(8,128)(2,1)S(1)}, bf16[2,16,768]{2,1,0:T(8,128)(2,1)S(1)}, u32[]{:S(2)}, u32[]{:S(2)}) %collective-permute-start.23) | collective-permute-done | bytes 49184 | tf_op jit(solution)/shard_map/ppermute | solution.py:134
  125.6 1.2 collective-permute-start.25
  126.7 3.8 %collective-permute-done.25.refs_7_ = bf16[2,16,768]{2,1,0:T(8,128)(2,1)S(1)} collective-permute-done((bf16[2,16,768]{2,1,0:T(8,128)(2,1)S(1)}, bf16[2,16,768]{2,1,0:T(8,128)(2,1)S(1)}, u32[]{:S(2)}, u32[]{:S(2)}) %collective-permute-start.25) | collective-permute-done | bytes 49184 | tf_op jit(solution)/shard_map/ppermute | solution.py:134
  130.6 0.1 last_sum.1
  130.7 0.1 collective-permute-start.26
  130.7 0.6 slice_reduce_fusion
  131.4 0.6 collective-permute-done.26
  132.0 0.7 pad_maximum_fusion
  (35 shorter events, 0.1 us)
Async XLA Ops:
  0.6 17.3 %collective-permute-start.1 = (bf16[16,5120]{1,0:T(8,128)(2,1)}, bf16[16,5120]{1,0:T(8,128)(2,1)S(1)}, u32[]{:S(2)}, u32[]{:S(2)}) collective-permute-start(bf16[16,5120]{1,0:T(8,128)(2,1)} %param.7), channel_id=1, source_target_pairs={{0,16},{1,17},{2,18},{3,19},{4,20},{5,21},{6,22},{7,23},{8,24},{9,... | collective-permute-start | bytes 491528 | tf_op jit(solution)/shard_map/ppermute | solution.py:134
  4.7 13.2 %collective-permute-start = (bf16[16,5120]{1,0:T(8,128)(2,1)}, bf16[16,5120]{1,0:T(8,128)(2,1)S(1)}, u32[]{:S(2)}, u32[]{:S(2)}) collective-permute-start(bf16[16,5120]{1,0:T(8,128)(2,1)} %param.7), channel_id=1, source_target_pairs={{0,8},{1,9},{2,10},{3,11},{4,12},{5,13},{6,14},{7,15},{8,0},{9,1},... | collective-permute-start | bytes 491528 | tf_op jit(solution)/shard_map/ppermute | solution.py:134
  6.3 11.7 %collective-permute-start.2 = (bf16[16,5120]{1,0:T(8,128)(2,1)}, bf16[16,5120]{1,0:T(8,128)(2,1)S(1)}, u32[]{:S(2)}, u32[]{:S(2)}) collective-permute-start(bf16[16,5120]{1,0:T(8,128)(2,1)} %param.7), channel_id=1, source_target_pairs={{0,24},{1,25},{2,26},{3,27},{4,28},{5,29},{6,30},{7,31},{8,16},{9,... | collective-permute-start | bytes 491528 | tf_op jit(solution)/shard_map/ppermute | solution.py:134
  7.7 1.0 copy-start.1
  10.8 33.1 %all-to-all-start = ((bf16[32,67,128]{2,1,0:T(8,128)(2,1)}), bf16[32,67,128]{2,1,0:T(8,128)(2,1)}, u32[]{:S(2)}, u32[]{:S(2)}) async-start(bf16[32,67,128]{2,1,0:T(8,128)(2,1)} %slice.8), calls=%async_computation | async-start | bytes 1179648 | tf_op jit(solution)/shard_map/all_to_all | solution.py:499
  18.0 22.4 %collective-permute-start.4 = (bf16[64,5120]{1,0:T(8,128)(2,1)S(1)}, bf16[64,5120]{1,0:T(8,128)(2,1)S(1)}, u32[]{:S(2)}, u32[]{:S(2)}) collective-permute-start(bf16[64,5120]{1,0:T(8,128)(2,1)S(1)} %constant_dynamic-update-slice_fusion.refs_0_), channel_id=1, source_target_pairs={{0,4},{1,5},{2,6},{3,7},{4,0},{5,1},{6,2},{7,3},{8,12},{9,13},{10,... | collective-permute-start | bytes 1966088 | tf_op jit(solution)/shard_map/ppermute | solution.py:134
  19.8 20.7 %collective-permute-start.3 = (bf16[64,5120]{1,0:T(8,128)(2,1)S(1)}, bf16[64,5120]{1,0:T(8,128)(2,1)S(1)}, u32[]{:S(2)}, u32[]{:S(2)}) collective-permute-start(bf16[64,5120]{1,0:T(8,128)(2,1)S(1)} %constant_dynamic-update-slice_fusion.refs_0_), channel_id=1, source_target_pairs={{0,2},{1,3},{2,0},{3,1},{4,6},{5,7},{6,4},{7,5},{8,10},{9,11},{10,... | collective-permute-start | bytes 1966088 | tf_op jit(solution)/shard_map/ppermute | solution.py:134
  21.5 22.4 %copy-start.2 = (s32[4,128]{1,0:T(4,128)S(1)}, s32[4,128]{1,0:T(4,128)}, u32[]{:S(2)}) copy-start(s32[4,128]{1,0:T(4,128)} %param.11) | copy-start | bytes 6148
  21.5 22.4 %copy-start.3 = (f32[512]{0:T(512)S(1)}, f32[512]{0:T(512)}, u32[]{:S(2)}) copy-start(f32[512]{0:T(512)} %param.12) | copy-start | bytes 6148
  26.9 26.2 %collective-permute-start.7 = (bf16[64,5120]{1,0:T(8,128)(2,1)S(1)}, bf16[64,5120]{1,0:T(8,128)(2,1)S(1)}, u32[]{:S(2)}, u32[]{:S(2)}) collective-permute-start(bf16[64,5120]{1,0:T(8,128)(2,1)S(1)} %constant_dynamic-update-slice_fusion.refs_0_), channel_id=1, source_target_pairs={{0,1},{1,0},{2,3},{3,2},{4,5},{5,4},{6,7},{7,6},{8,9},{9,8},{10,11... | collective-permute-start | bytes 1966088 | tf_op jit(solution)/shard_map/ppermute | solution.py:134
  40.5 14.5 %collective-permute-start.8 = (bf16[64,5120]{1,0:T(8,128)(2,1)S(1)}, bf16[64,5120]{1,0:T(8,128)(2,1)S(1)}, u32[]{:S(2)}, u32[]{:S(2)}) collective-permute-start(bf16[64,5120]{1,0:T(8,128)(2,1)S(1)} %collective-permute-done.3.x_ref.refs_1_), channel_id=1, source_target_pairs={{0,1},{1,0},{2,3},{3,2},{4,5},{5,4},{6,7},{7,6},{8,9},{9,8},{10,11... | collective-permute-start | bytes 1966088 | tf_op jit(solution)/shard_map/ppermute | solution.py:134
  41.4 13.6 %collective-permute-start.9 = (bf16[64,5120]{1,0:T(8,128)(2,1)S(1)}, bf16[64,5120]{1,0:T(8,128)(2,1)}, u32[]{:S(2)}, u32[]{:S(2)}) collective-permute-start(bf16[64,5120]{1,0:T(8,128)(2,1)S(1)} %collective-permute-done.4.y_ref.refs_2_), channel_id=1, source_target_pairs={{0,1},{1,0},{2,3},{3,2},{4,5},{5,4},{6,7},{7,6},{8,9},{9,8},{10,11... | collective-permute-start | bytes 1966088 | tf_op jit(solution)/shard_map/ppermute | solution.py:134
  41.9 9.9 %collective-permute-start.5 = (bf16[64,2560]{1,0:T(8,128)(2,1)}, bf16[64,2560]{1,0:T(8,128)(2,1)}, u32[]{:S(2)}, u32[]{:S(2)}) collective-permute-start(bf16[64,2560]{1,0:T(8,128)(2,1)} %get-tuple-element.64), channel_id=1, source_target_pairs={{0,4},{1,5},{2,6},{3,7},{4,0},{5,1},{6,2},{7,3},{8,12},{9,13},{10,... | collective-permute-start | bytes 983048 | tf_op jit(solution)/shard_map/ppermute | solution.py:134
  43.0 9.7 %collective-permute-start.6 = (bf16[64,2560]{1,0:T(8,128)(2,1)}, bf16[64,2560]{1,0:T(8,128)(2,1)}, u32[]{:S(2)}, u32[]{:S(2)}) collective-permute-start(bf16[64,2560]{1,0:T(8,128)(2,1)} %get-tuple-element.65), channel_id=1, source_target_pairs={{0,2},{1,3},{2,0},{3,1},{4,6},{5,7},{6,4},{7,5},{8,10},{9,11},{10,... | collective-permute-start | bytes 983048 | tf_op jit(solution)/shard_map/ppermute | solution.py:134
  52.6 26.6 %copy-start.4 = (f32[512]{0:T(512)S(1)}, f32[512]{0:T(512)}, u32[]{:S(2)}) copy-start(f32[512]{0:T(512)} %param.13) | copy-start | bytes 6148
  52.6 1.8 %collective-permute-start.10 = (bf16[64,2560]{1,0:T(8,128)(2,1)}, bf16[64,2560]{1,0:T(8,128)(2,1)S(1)}, u32[]{:S(2)}, u32[]{:S(2)}) collective-permute-start(bf16[64,2560]{1,0:T(8,128)(2,1)} %collective-permute-done.5.refs_3_), channel_id=1, source_target_pairs={{0,1},{1,0},{2,3},{3,2},{4,5},{5,4},{6,7},{7,6},{8,9},{9,8},{10,11... | collective-permute-start | bytes 983048 | tf_op jit(solution)/shard_map/ppermute | solution.py:134
  52.6 2.3 %collective-permute-start.11 = (bf16[64,2560]{1,0:T(8,128)(2,1)}, bf16[64,2560]{1,0:T(8,128)(2,1)S(1)}, u32[]{:S(2)}, u32[]{:S(2)}) collective-permute-start(bf16[64,2560]{1,0:T(8,128)(2,1)} %collective-permute-done.6.refs_4_), channel_id=1, source_target_pairs={{0,1},{1,0},{2,3},{3,2},{4,5},{5,4},{6,7},{7,6},{8,9},{9,8},{10,11... | collective-permute-start | bytes 983048 | tf_op jit(solution)/shard_map/ppermute | solution.py:134
  54.9 28.4 %collective-permute-start.13 = (bf16[2560,1024]{1,0:T(8,128)(2,1)}, bf16[2560,1024]{1,0:T(8,128)(2,1)S(1)}, u32[]{:S(2)}, u32[]{:S(2)}) collective-permute-start(bf16[2560,1024]{1,0:T(8,128)(2,1)} %constant_dynamic-slice_fusion), channel_id=1, source_target_pairs={{0,1},{1,0},{2,3},{3,2},{4,5},{5,4},{6,7},{7,6},{8,9},{9,8},{10,11... | collective-permute-start | bytes 15728648 | tf_op jit(solution)/shard_map/ppermute | solution.py:134
  80.6 11.4 %copy-start = (bf16[512,1024]{1,0:T(8,128)(2,1)}, bf16[512,1024]{1,0:T(8,128)(2,1)S(1)}, u32[]{:S(2)}) copy-start(bf16[512,1024]{1,0:T(8,128)(2,1)S(1)} %get-tuple-element.101.grad_ref.refs_10_) | copy-start | bytes 3145732
  80.6 2.7 %collective-permute-start.12 = (bf16[512,1024]{1,0:T(8,128)(2,1)S(1)}, bf16[512,1024]{1,0:T(8,128)(2,1)S(1)}, u32[]{:S(2)}, u32[]{:S(2)}) collective-permute-start(bf16[512,1024]{1,0:T(8,128)(2,1)S(1)} %get-tuple-element.101.grad_ref.refs_10_), channel_id=1, source_target_pairs={{0,1},{1,0},{2,3},{3,2},{4,5},{5,4},{6,7},{7,6},{8,9},{9,8},{10,11... | collective-permute-start | bytes 3145736 | tf_op jit(solution)/shard_map/ppermute | solution.py:134
  92.0 24.8 %collective-permute-start.14 = (bf16[4,2,16,1792]{3,2,1,0:T(8,128)(2,1)S(1)}, bf16[4,2,16,1792]{3,2,1,0:T(8,128)(2,1)S(1)}, u32[]{:S(2)}, u32[]{:S(2)}) collective-permute-start(bf16[4,2,16,1792]{3,2,1,0:T(8,128)(2,1)S(1)} %get-tuple-element.95), channel_id=1, source_target_pairs={{0,2},{1,3},{2,0},{3,1},{4,6},{5,7},{6,4},{7,5},{8,10},{9,11},{10,... | collective-permute-start | bytes 1376264 | tf_op jit(solution)/shard_map/ppermute | solution.py:134
  92.5 24.3 %collective-permute-start.15 = (bf16[4,2,16,1792]{3,2,1,0:T(8,128)(2,1)S(1)}, bf16[4,2,16,1792]{3,2,1,0:T(8,128)(2,1)S(1)}, u32[]{:S(2)}, u32[]{:S(2)}) collective-permute-start(bf16[4,2,16,1792]{3,2,1,0:T(8,128)(2,1)S(1)} %get-tuple-element.96), channel_id=1, source_target_pairs={{0,4},{1,5},{2,6},{3,7},{4,0},{5,1},{6,2},{7,3},{8,12},{9,13},{10,... | collective-permute-start | bytes 1376264 | tf_op jit(solution)/shard_map/ppermute | solution.py:134
  93.4 23.3 %collective-permute-start.16 = (bf16[4,2,16,1792]{3,2,1,0:T(8,128)(2,1)S(1)}, bf16[4,2,16,1792]{3,2,1,0:T(8,128)(2,1)S(1)}, u32[]{:S(2)}, u32[]{:S(2)}) collective-permute-start(bf16[4,2,16,1792]{3,2,1,0:T(8,128)(2,1)S(1)} %get-tuple-element.97), channel_id=1, source_target_pairs={{0,6},{1,7},{2,4},{3,5},{4,2},{5,3},{6,0},{7,1},{8,14},{9,15},{10,... | collective-permute-start | bytes 1376264 | tf_op jit(solution)/shard_map/ppermute | solution.py:134
  95.5 9.4 %collective-permute-start.17 = (bf16[4,2,16,768]{3,2,1,0:T(8,128)(2,1)S(1)}, bf16[4,2,16,768]{3,2,1,0:T(8,128)(2,1)S(1)}, u32[]{:S(2)}, u32[]{:S(2)}) collective-permute-start(bf16[4,2,16,768]{3,2,1,0:T(8,128)(2,1)S(1)} %get-tuple-element.98), channel_id=1, source_target_pairs={{0,8},{1,9},{2,10},{3,11},{4,12},{5,13},{6,14},{7,15},{8,0},{9,1},... | collective-permute-start | bytes 589832 | tf_op jit(solution)/shard_map/ppermute | solution.py:134
  96.2 20.6 %collective-permute-start.18 = (bf16[4,2,16,768]{3,2,1,0:T(8,128)(2,1)S(1)}, bf16[4,2,16,768]{3,2,1,0:T(8,128)(2,1)S(1)}, u32[]{:S(2)}, u32[]{:S(2)}) collective-permute-start(bf16[4,2,16,768]{3,2,1,0:T(8,128)(2,1)S(1)} %get-tuple-element.99), channel_id=1, source_target_pairs={{0,16},{1,17},{2,18},{3,19},{4,20},{5,21},{6,22},{7,23},{8,24},{9,... | collective-permute-start | bytes 589832 | tf_op jit(solution)/shard_map/ppermute | solution.py:134
  104.9 11.8 %collective-permute-start.19 = (bf16[4,2,16,768]{3,2,1,0:T(8,128)(2,1)S(1)}, bf16[4,2,16,768]{3,2,1,0:T(8,128)(2,1)S(1)}, u32[]{:S(2)}, u32[]{:S(2)}) collective-permute-start(bf16[4,2,16,768]{3,2,1,0:T(8,128)(2,1)S(1)} %get-tuple-element.100), channel_id=1, source_target_pairs={{0,24},{1,25},{2,26},{3,27},{4,28},{5,29},{6,30},{7,31},{8,16},{9,... | collective-permute-start | bytes 589832 | tf_op jit(solution)/shard_map/ppermute | solution.py:134
  117.0 13.5 %collective-permute-start.20 = (bf16[2,16,1792]{2,1,0:T(8,128)(2,1)S(1)}, bf16[2,16,1792]{2,1,0:T(8,128)(2,1)S(1)}, u32[]{:S(2)}, u32[]{:S(2)}) collective-permute-start(bf16[2,16,1792]{2,1,0:T(8,128)(2,1)S(1)} %get-tuple-element.112), channel_id=1, source_target_pairs={{0,8},{1,9},{2,10},{3,11},{4,12},{5,13},{6,14},{7,15},{8,0},{9,1},... | collective-permute-start | bytes 344072 | tf_op jit(solution)/shard_map/ppermute | solution.py:134
  117.1 13.5 %collective-permute-start.21 = (bf16[2,16,1792]{2,1,0:T(8,128)(2,1)S(1)}, bf16[2,16,1792]{2,1,0:T(8,128)(2,1)S(1)}, u32[]{:S(2)}, u32[]{:S(2)}) collective-permute-start(bf16[2,16,1792]{2,1,0:T(8,128)(2,1)S(1)} %get-tuple-element.113), channel_id=1, source_target_pairs={{0,16},{1,17},{2,18},{3,19},{4,20},{5,21},{6,22},{7,23},{8,24},{9,... | collective-permute-start | bytes 344072 | tf_op jit(solution)/shard_map/ppermute | solution.py:134
  119.6 10.9 %collective-permute-start.22 = (bf16[2,16,1792]{2,1,0:T(8,128)(2,1)S(1)}, bf16[2,16,1792]{2,1,0:T(8,128)(2,1)S(1)}, u32[]{:S(2)}, u32[]{:S(2)}) collective-permute-start(bf16[2,16,1792]{2,1,0:T(8,128)(2,1)S(1)} %get-tuple-element.114), channel_id=1, source_target_pairs={{0,24},{1,25},{2,26},{3,27},{4,28},{5,29},{6,30},{7,31},{8,16},{9,... | collective-permute-start | bytes 344072 | tf_op jit(solution)/shard_map/ppermute | solution.py:134
  121.5 4.1 %collective-permute-start.23 = (bf16[2,16,768]{2,1,0:T(8,128)(2,1)S(1)}, bf16[2,16,768]{2,1,0:T(8,128)(2,1)S(1)}, u32[]{:S(2)}, u32[]{:S(2)}) collective-permute-start(bf16[2,16,768]{2,1,0:T(8,128)(2,1)S(1)} %get-tuple-element.116), channel_id=1, source_target_pairs={{0,2},{1,3},{2,0},{3,1},{4,6},{5,7},{6,4},{7,5},{8,10},{9,11},{10,... | collective-permute-start | bytes 147464 | tf_op jit(solution)/shard_map/ppermute | solution.py:134
  122.0 4.8 %collective-permute-start.24 = (bf16[2,16,768]{2,1,0:T(8,128)(2,1)S(1)}, bf16[2,16,768]{2,1,0:T(8,128)(2,1)S(1)}, u32[]{:S(2)}, u32[]{:S(2)}) collective-permute-start(bf16[2,16,768]{2,1,0:T(8,128)(2,1)S(1)} %get-tuple-element.117), channel_id=1, source_target_pairs={{0,4},{1,5},{2,6},{3,7},{4,0},{5,1},{6,2},{7,3},{8,12},{9,13},{10,... | collective-permute-start | bytes 147464 | tf_op jit(solution)/shard_map/ppermute | solution.py:134
  125.6 5.0 %collective-permute-start.25 = (bf16[2,16,768]{2,1,0:T(8,128)(2,1)S(1)}, bf16[2,16,768]{2,1,0:T(8,128)(2,1)S(1)}, u32[]{:S(2)}, u32[]{:S(2)}) collective-permute-start(bf16[2,16,768]{2,1,0:T(8,128)(2,1)S(1)} %get-tuple-element.118), channel_id=1, source_target_pairs={{0,6},{1,7},{2,4},{3,5},{4,2},{5,3},{6,0},{7,1},{8,14},{9,15},{10,... | collective-permute-start | bytes 147464 | tf_op jit(solution)/shard_map/ppermute | solution.py:134
  130.7 1.3 %collective-permute-start.26 = (bf16[16,2560]{1,0:T(8,128)(2,1)S(1)}, bf16[16,2560]{1,0:T(8,128)(2,1)S(1)}, u32[]{:S(2)}, u32[]{:S(2)}) collective-permute-start(bf16[16,2560]{1,0:T(8,128)(2,1)S(1)} %get-tuple-element.120), channel_id=1, source_target_pairs={{0,1},{1,0},{2,3},{3,2},{4,5},{5,4},{6,7},{7,6},{8,9},{9,8},{10,11... | collective-permute-start | bytes 245768 | tf_op jit(solution)/shard_map/ppermute | solution.py:134

commit v21 on v20

--- a/solution.py
+++ b/solution.py
@@ -483,8 +483,6 @@
     column = jnp.concatenate(column, axis=0)
     X, Y = CORES, 2 * CORES
     plane = [column, shift(column, X), shift(column, Y)]
-    sent_w = lax.dynamic_slice(head_weight, ((1 - core) * half, 0), (half, slab))
-    plane[1], plane[2], sent_w = lax.optimization_barrier((plane[1], plane[2], sent_w))
     low, high = pl.pallas_call(
         cut_kernel,
         in_specs=[vmem_spec()] * 2,
@@ -496,8 +494,10 @@
     )(plane[1], plane[2])
     plane += [shift(low, Y), shift(high, X)]
     payload, place = pack_teacher(teacher_logits, block_lists, slab // side)
+    sent_w = lax.dynamic_slice(head_weight, ((1 - core) * half, 0), (half, slab))
+    payload, sent_w = lax.optimization_barrier((payload[:, : 3 - STAT_ROWS], sent_w))
     arrived = lax.all_to_all(
-        payload[:, : 3 - STAT_ROWS], "vocab", split_axis=0, concat_axis=0, tiled=True
+        payload, "vocab", split_axis=0, concat_axis=0, tiled=True
     )
 
     prob, entropy = pl.pallas_call(

time: 133 us -> 137 us (1.030)
  waiting for transfers between devices: 35.9 us -> 41.3 us
    ppermute x27, waiting for transfers between devices: 35.9 us -> 41.3 us  [shift(): return lax.ppermute(x, 'vocab', [(i, i ^ distance) for i in range(n)])]
  transfers between devices with their start and end apart: 28 -> 28, of which waited for: 10 -> 10; matrix products, arithmetic and copies ran while one was open for 7% -> 6% of each run, Pallas kernels for 22% -> 21%
where the time goes in v21:
time: 137 us
  waiting for transfers between devices  41.3 us (30%)
  Pallas kernels  37.8 us (28%)
  starting transfers between devices  33.3 us (24%)
  blocking collectives  13 us (9%)
  local copies, waits for them, and re-layouts  8.31 us (6%)
  other arithmetic  2 us (1%)
    ppermute x27, waiting for transfers between devices, shift(): return lax.ppermute(x, 'vocab', [(i, i ^ distance) for i in range(n)])  41.3 us
    ppermute x27, starting transfers between devices, shift(): return lax.ppermute(x, 'vocab', [(i, i ^ distance) for i in range(n)])  27.1 us
    all_to_all x1, blocking collectives, levels_plan(): lax.all_to_all(stat, 'vocab', split_axis=0, concat_axis=0, tiled=True)  13 us
    pallas_call x1, Pallas kernels, levels_plan(): pl.pallas_call(functools.partial(logits_kernel, rows), grid=(2 * tiles,),...  10.5 us
    pallas_call x1, Pallas kernels, levels_plan(): pl.pallas_call(functools.partial(head_kernel, rows), grid=(4,), in_specs=...  9.96 us
    pallas_call x1, Pallas kernels, levels_plan(): pl.pallas_call(functools.partial(partial_kernel, rows), grid_spec=pltpu.P...  8.62 us
    all_to_all x1, starting transfers between devices, levels_plan(): lax.all_to_all(payload, 'vocab', split_axis=0, concat_axis=0, tiled=True)  6.18 us
    dynamic_slice x1, local copies, waits for them, and re-layouts, levels_plan(): lax.dynamic_slice(head_weight, ((1 - core) * half, 0), (half, slab))  5.45 us
  transfers between devices with their start and end apart: 28, of which 10 were waited for; matrix products, arithmetic and copies ran while one was open for 6% of the time, Pallas kernels for 21%

profile of v21, /device:TPU:0, one launch (start us, length us, event | category | flops | bytes accessed | tf_op | source)
XLA Modules:
  0.0 136.6 jit_solution(15280321337869220726)
XLA Ops:
  0.6 4.1 %collective-permute-start.1 = (bf16[16,5120]{1,0:T(8,128)(2,1)}, bf16[16,5120]{1,0:T(8,128)(2,1)S(1)}, u32[]{:S(2)}, u32[]{:S(2)}) collective-permute-start(bf16[16,5120]{1,0:T(8,128)(2,1)} %param.7), channel_id=1, source_target_pairs={{0,16},{1,17},{2,18},{3,19},{4,20},{5,21},{6,22},{7,23},{8,24},{9,... | collective-permute-start | bytes 491528 | tf_op jit(solution)/shard_map/ppermute | solution.py:134
  4.7 1.6 %collective-permute-start = (bf16[16,5120]{1,0:T(8,128)(2,1)}, bf16[16,5120]{1,0:T(8,128)(2,1)S(1)}, u32[]{:S(2)}, u32[]{:S(2)}) collective-permute-start(bf16[16,5120]{1,0:T(8,128)(2,1)} %param.7), channel_id=1, source_target_pairs={{0,8},{1,9},{2,10},{3,11},{4,12},{5,13},{6,14},{7,15},{8,0},{9,1},... | collective-permute-start | bytes 491528 | tf_op jit(solution)/shard_map/ppermute | solution.py:134
  6.3 0.0 collective-permute-start.2
  6.3 0.7 add_select_fusion.1
  7.0 0.1 iota_compare_fusion
  7.1 0.2 convert_reduce_fusion
  7.3 0.1 add.85
  7.4 0.1 add.82
  7.5 0.1 add.89
  7.7 0.0 copy-start.1
  7.7 0.9 copy-done.1
  8.6 1.3 pack_teacher.1
  9.9 0.9 slice.8
  10.8 5.5 %constant_dynamic-slice_fusion = bf16[2560,1024]{1,0:T(8,128)(2,1)} fusion(bf16[5120,1024]{1,0:T(8,128)(2,1)} %w_ref.1, s32[]{:T(128)S(6)} %select_n.57), kind=kLoop, calls=%fused_computation.27 | loop fusion | bytes 10485764 | tf_op jit(solution)/shard_map/dynamic_slice | solution.py:497
  16.3 6.2 %all-to-all-start = ((bf16[32,67,128]{2,1,0:T(8,128)(2,1)}), bf16[32,67,128]{2,1,0:T(8,128)(2,1)}, u32[]{:S(2)}, u32[]{:S(2)}) async-start(bf16[32,67,128]{2,1,0:T(8,128)(2,1)} %slice.8), calls=%async_computation | async-start | bytes 1179648 | tf_op jit(solution)/shard_map/all_to_all | solution.py:499
  22.6 1.8 %collective-permute-start.4 = (bf16[64,5120]{1,0:T(8,128)(2,1)S(1)}, bf16[64,5120]{1,0:T(8,128)(2,1)S(1)}, u32[]{:S(2)}, u32[]{:S(2)}) collective-permute-start(bf16[64,5120]{1,0:T(8,128)(2,1)S(1)} %constant_dynamic-update-slice_fusion.refs_0_), channel_id=1, source_target_pairs={{0,4},{1,5},{2,6},{3,7},{4,0},{5,1},{6,2},{7,3},{8,12},{9,13},{10,... | collective-permute-start | bytes 1966088 | tf_op jit(solution)/shard_map/ppermute | solution.py:134
  24.3 1.5 %collective-permute-start.3 = (bf16[64,5120]{1,0:T(8,128)(2,1)S(1)}, bf16[64,5120]{1,0:T(8,128)(2,1)S(1)}, u32[]{:S(2)}, u32[]{:S(2)}) collective-permute-start(bf16[64,5120]{1,0:T(8,128)(2,1)S(1)} %constant_dynamic-update-slice_fusion.refs_0_), channel_id=1, source_target_pairs={{0,2},{1,3},{2,0},{3,1},{4,6},{5,7},{6,4},{7,5},{8,10},{9,11},{10,... | collective-permute-start | bytes 1966088 | tf_op jit(solution)/shard_map/ppermute | solution.py:134
  25.8 0.2 select_reduce_fusion
  26.0 0.1 collective-permute-start.7
  26.1 19.5 %collective-permute-done.4.y_ref.refs_2_ = bf16[64,5120]{1,0:T(8,128)(2,1)S(1)} collective-permute-done((bf16[64,5120]{1,0:T(8,128)(2,1)S(1)}, bf16[64,5120]{1,0:T(8,128)(2,1)S(1)}, u32[]{:S(2)}, u32[]{:S(2)}) %collective-permute-start.4) | collective-permute-done | bytes 655392 | tf_op jit(solution)/shard_map/ppermute | solution.py:134
  45.6 0.9 cut_halves.1
  46.5 1.5 %collective-permute-start.5 = (bf16[64,2560]{1,0:T(8,128)(2,1)}, bf16[64,2560]{1,0:T(8,128)(2,1)}, u32[]{:S(2)}, u32[]{:S(2)}) collective-permute-start(bf16[64,2560]{1,0:T(8,128)(2,1)} %get-tuple-element.61), channel_id=1, source_target_pairs={{0,4},{1,5},{2,6},{3,7},{4,0},{5,1},{6,2},{7,3},{8,12},{9,13},{10,... | collective-permute-start | bytes 983048 | tf_op jit(solution)/shard_map/ppermute | solution.py:134
  47.9 0.6 collective-permute-start.6
  48.5 0.0 collective-permute-start.9
  48.5 0.5 collective-permute-start.8
  49.0 0.1 pad_add_fusion.refs_0_.core_ref
  49.1 4.9 %teacher_prob.1 = (f32[512,1024]{1,0:T(8,128)S(1)}, f32[16,128]{1,0:T(8,128)S(1)}) custom-call(s32[4]{0:T(128)S(1)} %pad_add_fusion.refs_0_.core_ref, s32[4,4]{1,0:T(4,128)S(1)} %broadcast_add_fusion.1.refs_1_, bf16[32,67,128]{2,1,0:T(8,128)(2,1)} %all-to-all-done.refs_2_, s32[4,1,128]{2,1,0:T(1,128)S(1)} %bitcast.9, f32[4,1,128]{2,1,0:T(1,128)S(1)} %bitcast.10), custom_call_target="tpu_custom_call" | custom-call | flops 1 | bytes 1 | tf_op jit(solution)/shard_map/teacher_prob/pallas_call | solution.py:503
  54.0 2.0 %collective-permute-done.5.refs_3_ = bf16[64,2560]{1,0:T(8,128)(2,1)} collective-permute-done((bf16[64,2560]{1,0:T(8,128)(2,1)}, bf16[64,2560]{1,0:T(8,128)(2,1)}, u32[]{:S(2)}, u32[]{:S(2)}) %collective-permute-start.5) | collective-permute-done | bytes 327712 | tf_op jit(solution)/shard_map/ppermute | solution.py:134
  56.0 1.2 collective-permute-done.6.refs_4_
  57.2 0.5 collective-permute-start.11
  57.7 0.0 collective-permute-done.7.refs_5_
  57.7 1.3 collective-permute-done.10.refs_8_
  59.0 0.5 collective-permute-done.11.refs_9_
  59.5 0.1 collective-permute-start.13
  59.7 10.5 %logits.1 = (f32[512,1024]{1,0:T(8,128)S(1)}, f32[32,8,128]{2,1,0:T(8,128)S(1)}) custom-call(bf16[64,5120]{1,0:T(8,128)(2,1)S(1)} %constant_dynamic-update-slice_fusion.refs_0_, bf16[64,5120]{1,0:T(8,128)(2,1)S(1)} %collective-permute-done.3.x_ref.refs_1_, bf16[64,5120]{1,0:T(8,128)(2,1)S(1)} %collective-permute-done.4.y_ref.refs_2_, ...), custom_call_target="tpu_custom_call" | custom-call | flops 1 | bytes 1 | tf_op jit(solution)/shard_map/logits/pallas_call | solution.py:530
  70.2 13.0 %all_to_all.10.refs_1_ = f32[32,8,128]{2,1,0:T(8,128)S(1)} all-to-all(f32[32,8,128]{2,1,0:T(8,128)S(1)} %get-tuple-element.79), channel_id=1, replica_groups=mesh['vocab'=32] {'vocab'}, dimensions={0} | all-to-all | bytes 262144 | tf_op jit(solution)/shard_map/all_to_all | solution.py:550
  83.2 1.3 grad_logits.1
  84.5 0.3 collective-permute-start.12
  84.7 2.4 %collective-permute-done.12.sib_ref = bf16[512,1024]{1,0:T(8,128)(2,1)S(1)} collective-permute-done((bf16[512,1024]{1,0:T(8,128)(2,1)S(1)}, bf16[512,1024]{1,0:T(8,128)(2,1)S(1)}, u32[]{:S(2)}, u32[]{:S(2)}) %collective-permute-start.12) | collective-permute-done | bytes 1048608 | tf_op jit(solution)/shard_map/ppermute | solution.py:134
  87.2 8.6 %grad_hidden_partial.1 = (f32[4,2,16,1792]{3,2,1,0:T(8,128)S(1)}, bf16[4,2,16,1792]{3,2,1,0:T(8,128)(2,1)S(1)}, bf16[4,2,16,1792]{3,2,1,0:T(8,128)(2,1)S(1)}, bf...) custom-call(s32[4]{0:T(128)S(1)} %pad_add_fusion.refs_0_.core_ref, ...), custom_call_target="tpu_custom_call" | custom-call | flops 1 | bytes 1 | tf_op jit(solution)/shard_map/grad_hidden_partial/pallas_call | solution.py:568
  95.8 0.5 collective-permute-start.14
  96.3 1.0 collective-permute-start.15
  97.3 2.0 %collective-permute-start.16 = (bf16[4,2,16,1792]{3,2,1,0:T(8,128)(2,1)S(1)}, bf16[4,2,16,1792]{3,2,1,0:T(8,128)(2,1)S(1)}, u32[]{:S(2)}, u32[]{:S(2)}) collective-permute-start(bf16[4,2,16,1792]{3,2,1,0:T(8,128)(2,1)S(1)} %get-tuple-element.95), channel_id=1, source_target_pairs={{0,6},{1,7},{2,4},{3,5},{4,2},{5,3},{6,0},{7,1},{8,14},{9,15},{10,... | collective-permute-start | bytes 1376264 | tf_op jit(solution)/shard_map/ppermute | solution.py:134
  99.4 0.7 collective-permute-start.17
  100.0 1.2 collective-permute-start.18
  101.3 7.5 %collective-permute-done.17.refs_5_ = bf16[4,2,16,768]{3,2,1,0:T(8,128)(2,1)S(1)} collective-permute-done((bf16[4,2,16,768]{3,2,1,0:T(8,128)(2,1)S(1)}, bf16[4,2,16,768]{3,2,1,0:T(8,128)(2,1)S(1)}, u32[]{:S(2)}, u32[]{:S(2)}) %collective-permute-start.17) | collective-permute-done | bytes 196640 | tf_op jit(solution)/shard_map/ppermute | solution.py:134
  108.8 1.8 %collective-permute-start.19 = (bf16[4,2,16,768]{3,2,1,0:T(8,128)(2,1)S(1)}, bf16[4,2,16,768]{3,2,1,0:T(8,128)(2,1)S(1)}, u32[]{:S(2)}, u32[]{:S(2)}) collective-permute-start(bf16[4,2,16,768]{3,2,1,0:T(8,128)(2,1)S(1)} %get-tuple-element.98), channel_id=1, source_target_pairs={{0,24},{1,25},{2,26},{3,27},{4,28},{5,29},{6,30},{7,31},{8,16},{9,... | collective-permute-start | bytes 589832 | tf_op jit(solution)/shard_map/ppermute | solution.py:134
  110.6 10.0 %grad_head.1 = bf16[5120,1024]{1,0:T(8,128)(2,1)} custom-call(bf16[64,5120]{1,0:T(8,128)(2,1)S(1)} %constant_dynamic-update-slice_fusion.refs_0_, bf16[64,5120]{1,0:T(8,128)(2,1)S(1)} %collective-permute-done.3.x_ref.refs_1_, bf16[64,5120]{1,0:T(8,128)(2,1)S(1)} %collective-permute-done.4.y_ref.refs_2_, bf16[64,2560]{1,0:T(8,128)(2,1)} %collective-permute-done.5.refs_3_, ...), custom_call_target="tpu_custom_call" | custom-call | flops 1 | bytes 1 | tf_op jit(solution)/shard_map/grad_head/pallas_call | solution.py:592
  120.6 0.0 collective-permute-done.14.refs_1_
  120.6 0.3 first_sum.1
  120.9 0.1 collective-permute-start.20
  121.0 2.5 %collective-permute-start.21 = (bf16[2,16,1792]{2,1,0:T(8,128)(2,1)S(1)}, bf16[2,16,1792]{2,1,0:T(8,128)(2,1)S(1)}, u32[]{:S(2)}, u32[]{:S(2)}) collective-permute-start(bf16[2,16,1792]{2,1,0:T(8,128)(2,1)S(1)} %get-tuple-element.111), channel_id=1, source_target_pairs={{0,16},{1,17},{2,18},{3,19},{4,20},{5,21},{6,22},{7,23},{8,24},{9,... | collective-permute-start | bytes 344072 | tf_op jit(solution)/shard_map/ppermute | solution.py:134
  123.5 1.9 %collective-permute-start.22 = (bf16[2,16,1792]{2,1,0:T(8,128)(2,1)S(1)}, bf16[2,16,1792]{2,1,0:T(8,128)(2,1)S(1)}, u32[]{:S(2)}, u32[]{:S(2)}) collective-permute-start(bf16[2,16,1792]{2,1,0:T(8,128)(2,1)S(1)} %get-tuple-element.112), channel_id=1, source_target_pairs={{0,24},{1,25},{2,26},{3,27},{4,28},{5,29},{6,30},{7,31},{8,16},{9,... | collective-permute-start | bytes 344072 | tf_op jit(solution)/shard_map/ppermute | solution.py:134
  125.4 0.5 collective-permute-start.23
  125.8 1.3 collective-permute-start.24
  127.1 2.4 %collective-permute-done.23.refs_5_ = bf16[2,16,768]{2,1,0:T(8,128)(2,1)S(1)} collective-permute-done((bf16[2,16,768]{2,1,0:T(8,128)(2,1)S(1)}, bf16[2,16,768]{2,1,0:T(8,128)(2,1)S(1)}, u32[]{:S(2)}, u32[]{:S(2)}) %collective-permute-start.23) | collective-permute-done | bytes 49184 | tf_op jit(solution)/shard_map/ppermute | solution.py:134
  129.5 1.1 collective-permute-start.25
  130.6 0.0 collective-permute-done.24.refs_6_
  130.6 3.8 %collective-permute-done.25.refs_7_ = bf16[2,16,768]{2,1,0:T(8,128)(2,1)S(1)} collective-permute-done((bf16[2,16,768]{2,1,0:T(8,128)(2,1)S(1)}, bf16[2,16,768]{2,1,0:T(8,128)(2,1)S(1)}, u32[]{:S(2)}, u32[]{:S(2)}) %collective-permute-start.25) | collective-permute-done | bytes 49184 | tf_op jit(solution)/shard_map/ppermute | solution.py:134
  134.5 0.1 last_sum.1
  134.6 0.1 collective-permute-start.26
  134.6 0.6 slice_reduce_fusion
  135.3 0.6 collective-permute-done.26
  135.9 0.7 pad_maximum_fusion
  (37 shorter events, 0.2 us)
Async XLA Ops:
  0.6 21.9 %collective-permute-start.1 = (bf16[16,5120]{1,0:T(8,128)(2,1)}, bf16[16,5120]{1,0:T(8,128)(2,1)S(1)}, u32[]{:S(2)}, u32[]{:S(2)}) collective-permute-start(bf16[16,5120]{1,0:T(8,128)(2,1)} %param.7), channel_id=1, source_target_pairs={{0,16},{1,17},{2,18},{3,19},{4,20},{5,21},{6,22},{7,23},{8,24},{9,... | collective-permute-start | bytes 491528 | tf_op jit(solution)/shard_map/ppermute | solution.py:134
  4.7 17.8 %collective-permute-start = (bf16[16,5120]{1,0:T(8,128)(2,1)}, bf16[16,5120]{1,0:T(8,128)(2,1)S(1)}, u32[]{:S(2)}, u32[]{:S(2)}) collective-permute-start(bf16[16,5120]{1,0:T(8,128)(2,1)} %param.7), channel_id=1, source_target_pairs={{0,8},{1,9},{2,10},{3,11},{4,12},{5,13},{6,14},{7,15},{8,0},{9,1},... | collective-permute-start | bytes 491528 | tf_op jit(solution)/shard_map/ppermute | solution.py:134
  6.3 16.2 %collective-permute-start.2 = (bf16[16,5120]{1,0:T(8,128)(2,1)}, bf16[16,5120]{1,0:T(8,128)(2,1)S(1)}, u32[]{:S(2)}, u32[]{:S(2)}) collective-permute-start(bf16[16,5120]{1,0:T(8,128)(2,1)} %param.7), channel_id=1, source_target_pairs={{0,24},{1,25},{2,26},{3,27},{4,28},{5,29},{6,30},{7,31},{8,16},{9,... | collective-permute-start | bytes 491528 | tf_op jit(solution)/shard_map/ppermute | solution.py:134
  7.7 1.0 copy-start.1
  10.8 11.7 %copy-start.5 = (bf16[16,5120]{1,0:T(8,128)(2,1)S(1)}, bf16[16,5120]{1,0:T(8,128)(2,1)}, u32[]{:S(2)}) copy-start(bf16[16,5120]{1,0:T(8,128)(2,1)} %param.7) | copy-start | bytes 491524
  10.8 38.3 %copy-start.2 = (s32[4,128]{1,0:T(4,128)S(1)}, s32[4,128]{1,0:T(4,128)}, u32[]{:S(2)}) copy-start(s32[4,128]{1,0:T(4,128)} %param.11) | copy-start | bytes 6148
  10.8 38.3 %copy-start.3 = (f32[512]{0:T(512)S(1)}, f32[512]{0:T(512)}, u32[]{:S(2)}) copy-start(f32[512]{0:T(512)} %param.12) | copy-start | bytes 6148
  16.3 32.8 %all-to-all-start = ((bf16[32,67,128]{2,1,0:T(8,128)(2,1)}), bf16[32,67,128]{2,1,0:T(8,128)(2,1)}, u32[]{:S(2)}, u32[]{:S(2)}) async-start(bf16[32,67,128]{2,1,0:T(8,128)(2,1)} %slice.8), calls=%async_computation | async-start | bytes 1179648 | tf_op jit(solution)/shard_map/all_to_all | solution.py:499
  22.6 23.0 %collective-permute-start.4 = (bf16[64,5120]{1,0:T(8,128)(2,1)S(1)}, bf16[64,5120]{1,0:T(8,128)(2,1)S(1)}, u32[]{:S(2)}, u32[]{:S(2)}) collective-permute-start(bf16[64,5120]{1,0:T(8,128)(2,1)S(1)} %constant_dynamic-update-slice_fusion.refs_0_), channel_id=1, source_target_pairs={{0,4},{1,5},{2,6},{3,7},{4,0},{5,1},{6,2},{7,3},{8,12},{9,13},{10,... | collective-permute-start | bytes 1966088 | tf_op jit(solution)/shard_map/ppermute | solution.py:134
  24.3 21.2 %collective-permute-start.3 = (bf16[64,5120]{1,0:T(8,128)(2,1)S(1)}, bf16[64,5120]{1,0:T(8,128)(2,1)S(1)}, u32[]{:S(2)}, u32[]{:S(2)}) collective-permute-start(bf16[64,5120]{1,0:T(8,128)(2,1)S(1)} %constant_dynamic-update-slice_fusion.refs_0_), channel_id=1, source_target_pairs={{0,2},{1,3},{2,0},{3,1},{4,6},{5,7},{6,4},{7,5},{8,10},{9,11},{10,... | collective-permute-start | bytes 1966088 | tf_op jit(solution)/shard_map/ppermute | solution.py:134
  26.0 31.7 %collective-permute-start.7 = (bf16[64,5120]{1,0:T(8,128)(2,1)S(1)}, bf16[64,5120]{1,0:T(8,128)(2,1)S(1)}, u32[]{:S(2)}, u32[]{:S(2)}) collective-permute-start(bf16[64,5120]{1,0:T(8,128)(2,1)S(1)} %constant_dynamic-update-slice_fusion.refs_0_), channel_id=1, source_target_pairs={{0,1},{1,0},{2,3},{3,2},{4,5},{5,4},{6,7},{7,6},{8,9},{9,8},{10,11... | collective-permute-start | bytes 1966088 | tf_op jit(solution)/shard_map/ppermute | solution.py:134
  46.5 9.6 %collective-permute-start.5 = (bf16[64,2560]{1,0:T(8,128)(2,1)}, bf16[64,2560]{1,0:T(8,128)(2,1)}, u32[]{:S(2)}, u32[]{:S(2)}) collective-permute-start(bf16[64,2560]{1,0:T(8,128)(2,1)} %get-tuple-element.61), channel_id=1, source_target_pairs={{0,4},{1,5},{2,6},{3,7},{4,0},{5,1},{6,2},{7,3},{8,12},{9,13},{10,... | collective-permute-start | bytes 983048 | tf_op jit(solution)/shard_map/ppermute | solution.py:134
  47.9 9.3 %collective-permute-start.6 = (bf16[64,2560]{1,0:T(8,128)(2,1)}, bf16[64,2560]{1,0:T(8,128)(2,1)}, u32[]{:S(2)}, u32[]{:S(2)}) collective-permute-start(bf16[64,2560]{1,0:T(8,128)(2,1)} %get-tuple-element.62), channel_id=1, source_target_pairs={{0,2},{1,3},{2,0},{3,1},{4,6},{5,7},{6,4},{7,5},{8,10},{9,11},{10,... | collective-permute-start | bytes 983048 | tf_op jit(solution)/shard_map/ppermute | solution.py:134
  48.5 11.0 %collective-permute-start.9 = (bf16[64,5120]{1,0:T(8,128)(2,1)S(1)}, bf16[64,5120]{1,0:T(8,128)(2,1)S(1)}, u32[]{:S(2)}, u32[]{:S(2)}) collective-permute-start(bf16[64,5120]{1,0:T(8,128)(2,1)S(1)} %collective-permute-done.4.y_ref.refs_2_), channel_id=1, source_target_pairs={{0,1},{1,0},{2,3},{3,2},{4,5},{5,4},{6,7},{7,6},{8,9},{9,8},{10,11... | collective-permute-start | bytes 1966088 | tf_op jit(solution)/shard_map/ppermute | solution.py:134
  48.5 11.0 %collective-permute-start.8 = (bf16[64,5120]{1,0:T(8,128)(2,1)S(1)}, bf16[64,5120]{1,0:T(8,128)(2,1)}, u32[]{:S(2)}, u32[]{:S(2)}) collective-permute-start(bf16[64,5120]{1,0:T(8,128)(2,1)S(1)} %collective-permute-done.3.x_ref.refs_1_), channel_id=1, source_target_pairs={{0,1},{1,0},{2,3},{3,2},{4,5},{5,4},{6,7},{7,6},{8,9},{9,8},{10,11... | collective-permute-start | bytes 1966088 | tf_op jit(solution)/shard_map/ppermute | solution.py:134
  57.2 26.0 %copy-start.4 = (f32[512]{0:T(512)S(1)}, f32[512]{0:T(512)}, u32[]{:S(2)}) copy-start(f32[512]{0:T(512)} %param.13) | copy-start | bytes 6148
  57.2 1.8 %collective-permute-start.10 = (bf16[64,2560]{1,0:T(8,128)(2,1)}, bf16[64,2560]{1,0:T(8,128)(2,1)S(1)}, u32[]{:S(2)}, u32[]{:S(2)}) collective-permute-start(bf16[64,2560]{1,0:T(8,128)(2,1)} %collective-permute-done.5.refs_3_), channel_id=1, source_target_pairs={{0,1},{1,0},{2,3},{3,2},{4,5},{5,4},{6,7},{7,6},{8,9},{9,8},{10,11... | collective-permute-start | bytes 983048 | tf_op jit(solution)/shard_map/ppermute | solution.py:134
  57.2 2.3 %collective-permute-start.11 = (bf16[64,2560]{1,0:T(8,128)(2,1)}, bf16[64,2560]{1,0:T(8,128)(2,1)S(1)}, u32[]{:S(2)}, u32[]{:S(2)}) collective-permute-start(bf16[64,2560]{1,0:T(8,128)(2,1)} %collective-permute-done.6.refs_4_), channel_id=1, source_target_pairs={{0,1},{1,0},{2,3},{3,2},{4,5},{5,4},{6,7},{7,6},{8,9},{9,8},{10,11... | collective-permute-start | bytes 983048 | tf_op jit(solution)/shard_map/ppermute | solution.py:134
  59.5 27.7 %collective-permute-start.13 = (bf16[2560,1024]{1,0:T(8,128)(2,1)}, bf16[2560,1024]{1,0:T(8,128)(2,1)S(1)}, u32[]{:S(2)}, u32[]{:S(2)}) collective-permute-start(bf16[2560,1024]{1,0:T(8,128)(2,1)} %constant_dynamic-slice_fusion), channel_id=1, source_target_pairs={{0,1},{1,0},{2,3},{3,2},{4,5},{5,4},{6,7},{7,6},{8,9},{9,8},{10,11... | collective-permute-start | bytes 15728648 | tf_op jit(solution)/shard_map/ppermute | solution.py:134
  84.4 11.4 %copy-start = (bf16[512,1024]{1,0:T(8,128)(2,1)}, bf16[512,1024]{1,0:T(8,128)(2,1)S(1)}, u32[]{:S(2)}) copy-start(bf16[512,1024]{1,0:T(8,128)(2,1)S(1)} %get-tuple-element.99.grad_ref.refs_10_) | copy-start | bytes 3145732
  84.5 2.7 %collective-permute-start.12 = (bf16[512,1024]{1,0:T(8,128)(2,1)S(1)}, bf16[512,1024]{1,0:T(8,128)(2,1)S(1)}, u32[]{:S(2)}, u32[]{:S(2)}) collective-permute-start(bf16[512,1024]{1,0:T(8,128)(2,1)S(1)} %get-tuple-element.99.grad_ref.refs_10_), channel_id=1, source_target_pairs={{0,1},{1,0},{2,3},{3,2},{4,5},{5,4},{6,7},{7,6},{8,9},{9,8},{10,11... | collective-permute-start | bytes 3145736 | tf_op jit(solution)/shard_map/ppermute | solution.py:134
  95.8 24.8 %collective-permute-start.14 = (bf16[4,2,16,1792]{3,2,1,0:T(8,128)(2,1)S(1)}, bf16[4,2,16,1792]{3,2,1,0:T(8,128)(2,1)S(1)}, u32[]{:S(2)}, u32[]{:S(2)}) collective-permute-start(bf16[4,2,16,1792]{3,2,1,0:T(8,128)(2,1)S(1)} %get-tuple-element.93), channel_id=1, source_target_pairs={{0,2},{1,3},{2,0},{3,1},{4,6},{5,7},{6,4},{7,5},{8,10},{9,11},{10,... | collective-permute-start | bytes 1376264 | tf_op jit(solution)/shard_map/ppermute | solution.py:134
  96.3 24.3 %collective-permute-start.15 = (bf16[4,2,16,1792]{3,2,1,0:T(8,128)(2,1)S(1)}, bf16[4,2,16,1792]{3,2,1,0:T(8,128)(2,1)S(1)}, u32[]{:S(2)}, u32[]{:S(2)}) collective-permute-start(bf16[4,2,16,1792]{3,2,1,0:T(8,128)(2,1)S(1)} %get-tuple-element.94), channel_id=1, source_target_pairs={{0,4},{1,5},{2,6},{3,7},{4,0},{5,1},{6,2},{7,3},{8,12},{9,13},{10,... | collective-permute-start | bytes 1376264 | tf_op jit(solution)/shard_map/ppermute | solution.py:134
  97.3 23.3 %collective-permute-start.16 = (bf16[4,2,16,1792]{3,2,1,0:T(8,128)(2,1)S(1)}, bf16[4,2,16,1792]{3,2,1,0:T(8,128)(2,1)S(1)}, u32[]{:S(2)}, u32[]{:S(2)}) collective-permute-start(bf16[4,2,16,1792]{3,2,1,0:T(8,128)(2,1)S(1)} %get-tuple-element.95), channel_id=1, source_target_pairs={{0,6},{1,7},{2,4},{3,5},{4,2},{5,3},{6,0},{7,1},{8,14},{9,15},{10,... | collective-permute-start | bytes 1376264 | tf_op jit(solution)/shard_map/ppermute | solution.py:134
  99.4 9.4 %collective-permute-start.17 = (bf16[4,2,16,768]{3,2,1,0:T(8,128)(2,1)S(1)}, bf16[4,2,16,768]{3,2,1,0:T(8,128)(2,1)S(1)}, u32[]{:S(2)}, u32[]{:S(2)}) collective-permute-start(bf16[4,2,16,768]{3,2,1,0:T(8,128)(2,1)S(1)} %get-tuple-element.96), channel_id=1, source_target_pairs={{0,8},{1,9},{2,10},{3,11},{4,12},{5,13},{6,14},{7,15},{8,0},{9,1},... | collective-permute-start | bytes 589832 | tf_op jit(solution)/shard_map/ppermute | solution.py:134
  100.0 20.6 %collective-permute-start.18 = (bf16[4,2,16,768]{3,2,1,0:T(8,128)(2,1)S(1)}, bf16[4,2,16,768]{3,2,1,0:T(8,128)(2,1)S(1)}, u32[]{:S(2)}, u32[]{:S(2)}) collective-permute-start(bf16[4,2,16,768]{3,2,1,0:T(8,128)(2,1)S(1)} %get-tuple-element.97), channel_id=1, source_target_pairs={{0,16},{1,17},{2,18},{3,19},{4,20},{5,21},{6,22},{7,23},{8,24},{9,... | collective-permute-start | bytes 589832 | tf_op jit(solution)/shard_map/ppermute | solution.py:134
  108.8 11.8 %collective-permute-start.19 = (bf16[4,2,16,768]{3,2,1,0:T(8,128)(2,1)S(1)}, bf16[4,2,16,768]{3,2,1,0:T(8,128)(2,1)S(1)}, u32[]{:S(2)}, u32[]{:S(2)}) collective-permute-start(bf16[4,2,16,768]{3,2,1,0:T(8,128)(2,1)S(1)} %get-tuple-element.98), channel_id=1, source_target_pairs={{0,24},{1,25},{2,26},{3,27},{4,28},{5,29},{6,30},{7,31},{8,16},{9,... | collective-permute-start | bytes 589832 | tf_op jit(solution)/shard_map/ppermute | solution.py:134
  120.9 13.5 %collective-permute-start.20 = (bf16[2,16,1792]{2,1,0:T(8,128)(2,1)S(1)}, bf16[2,16,1792]{2,1,0:T(8,128)(2,1)S(1)}, u32[]{:S(2)}, u32[]{:S(2)}) collective-permute-start(bf16[2,16,1792]{2,1,0:T(8,128)(2,1)S(1)} %get-tuple-element.110), channel_id=1, source_target_pairs={{0,8},{1,9},{2,10},{3,11},{4,12},{5,13},{6,14},{7,15},{8,0},{9,1},... | collective-permute-start | bytes 344072 | tf_op jit(solution)/shard_map/ppermute | solution.py:134
  121.0 13.5 %collective-permute-start.21 = (bf16[2,16,1792]{2,1,0:T(8,128)(2,1)S(1)}, bf16[2,16,1792]{2,1,0:T(8,128)(2,1)S(1)}, u32[]{:S(2)}, u32[]{:S(2)}) collective-permute-start(bf16[2,16,1792]{2,1,0:T(8,128)(2,1)S(1)} %get-tuple-element.111), channel_id=1, source_target_pairs={{0,16},{1,17},{2,18},{3,19},{4,20},{5,21},{6,22},{7,23},{8,24},{9,... | collective-permute-start | bytes 344072 | tf_op jit(solution)/shard_map/ppermute | solution.py:134
  123.5 10.9 %collective-permute-start.22 = (bf16[2,16,1792]{2,1,0:T(8,128)(2,1)S(1)}, bf16[2,16,1792]{2,1,0:T(8,128)(2,1)S(1)}, u32[]{:S(2)}, u32[]{:S(2)}) collective-permute-start(bf16[2,16,1792]{2,1,0:T(8,128)(2,1)S(1)} %get-tuple-element.112), channel_id=1, source_target_pairs={{0,24},{1,25},{2,26},{3,27},{4,28},{5,29},{6,30},{7,31},{8,16},{9,... | collective-permute-start | bytes 344072 | tf_op jit(solution)/shard_map/ppermute | solution.py:134
  125.4 4.1 %collective-permute-start.23 = (bf16[2,16,768]{2,1,0:T(8,128)(2,1)S(1)}, bf16[2,16,768]{2,1,0:T(8,128)(2,1)S(1)}, u32[]{:S(2)}, u32[]{:S(2)}) collective-permute-start(bf16[2,16,768]{2,1,0:T(8,128)(2,1)S(1)} %get-tuple-element.114), channel_id=1, source_target_pairs={{0,2},{1,3},{2,0},{3,1},{4,6},{5,7},{6,4},{7,5},{8,10},{9,11},{10,... | collective-permute-start | bytes 147464 | tf_op jit(solution)/shard_map/ppermute | solution.py:134
  125.8 4.8 %collective-permute-start.24 = (bf16[2,16,768]{2,1,0:T(8,128)(2,1)S(1)}, bf16[2,16,768]{2,1,0:T(8,128)(2,1)S(1)}, u32[]{:S(2)}, u32[]{:S(2)}) collective-permute-start(bf16[2,16,768]{2,1,0:T(8,128)(2,1)S(1)} %get-tuple-element.115), channel_id=1, source_target_pairs={{0,4},{1,5},{2,6},{3,7},{4,0},{5,1},{6,2},{7,3},{8,12},{9,13},{10,... | collective-permute-start | bytes 147464 | tf_op jit(solution)/shard_map/ppermute | solution.py:134
  129.5 5.0 %collective-permute-start.25 = (bf16[2,16,768]{2,1,0:T(8,128)(2,1)S(1)}, bf16[2,16,768]{2,1,0:T(8,128)(2,1)S(1)}, u32[]{:S(2)}, u32[]{:S(2)}) collective-permute-start(bf16[2,16,768]{2,1,0:T(8,128)(2,1)S(1)} %get-tuple-element.116), channel_id=1, source_target_pairs={{0,6},{1,7},{2,4},{3,5},{4,2},{5,3},{6,0},{7,1},{8,14},{9,15},{10,... | collective-permute-start | bytes 147464 | tf_op jit(solution)/shard_map/ppermute | solution.py:134
  134.6 1.3 collective-permute-start.26

commit v22 on v20

--- a/solution.py
+++ b/solution.py
@@ -524,7 +524,7 @@
     pieces, sent_w = lax.optimization_barrier((pieces, sent_w))
     sib_w = shift(sent_w, 1)
 
-    width = 512 if slab % 512 == 0 else 128
+    width = slab
     tiles = slab // width
     whole = lambda t: (0, 0)
     logits, stat = pl.pallas_call(

time: 133 us -> 133 us (level)
  transfers between devices with their start and end apart: 28 -> 28, of which waited for: 10 -> 10; matrix products, arithmetic and copies ran while one was open for 7% -> 7% of each run, Pallas kernels for 22% -> 21%
where the time goes in v22:
time: 133 us; the launch traced here: 132 us
  Pallas kernels  37.4 us (28%)
  waiting for transfers between devices  35.9 us (27%)
  starting transfers between devices  33.2 us (25%)
  blocking collectives  13.7 us (10%)
  local copies, waits for them, and re-layouts  9.21 us (7%)
  other arithmetic  2 us (2%)
    ppermute x27, waiting for transfers between devices, shift(): return lax.ppermute(x, 'vocab', [(i, i ^ distance) for i in range(n)])  35.9 us
    ppermute x27, starting transfers between devices, shift(): return lax.ppermute(x, 'vocab', [(i, i ^ distance) for i in range(n)])  27 us
    all_to_all x1, blocking collectives, levels_plan(): lax.all_to_all(stat, 'vocab', split_axis=0, concat_axis=0, tiled=True)  13.7 us
    pallas_call x1, Pallas kernels, levels_plan(): pl.pallas_call(functools.partial(logits_kernel, rows), grid=(2 * tiles,),...  10.2 us
    pallas_call x1, Pallas kernels, levels_plan(): pl.pallas_call(functools.partial(head_kernel, rows), grid=(4,), in_specs=...  9.96 us
    pallas_call x1, Pallas kernels, levels_plan(): pl.pallas_call(functools.partial(partial_kernel, rows), grid_spec=pltpu.P...  8.63 us
    all_to_all x1, starting transfers between devices, levels_plan(): lax.all_to_all(payload[:, :3 - STAT_ROWS], 'vocab', split_axis=0, concat_...  6.18 us
    dynamic_slice x1, local copies, waits for them, and re-layouts, levels_plan(): lax.dynamic_slice(head_weight, ((1 - core) * half, 0), (half, slab))  5.43 us
  transfers between devices with their start and end apart: 28, of which 10 were waited for; matrix products, arithmetic and copies ran while one was open for 7% of the time, Pallas kernels for 21%

profile of v22, /device:TPU:0, one launch (start us, length us, event | category | flops | bytes accessed | tf_op | source)
XLA Modules:
  0.0 132.4 jit_solution(1016393078946742657)
XLA Ops:
  0.6 4.1 %collective-permute-start.1 = (bf16[16,5120]{1,0:T(8,128)(2,1)}, bf16[16,5120]{1,0:T(8,128)(2,1)S(1)}, u32[]{:S(2)}, u32[]{:S(2)}) collective-permute-start(bf16[16,5120]{1,0:T(8,128)(2,1)} %param.7), channel_id=1, source_target_pairs={{0,16},{1,17},{2,18},{3,19},{4,20},{5,21},{6,22},{7,23},{8,24},{9,... | collective-permute-start | bytes 491528 | tf_op jit(solution)/shard_map/ppermute | solution.py:134
  4.7 1.6 %collective-permute-start = (bf16[16,5120]{1,0:T(8,128)(2,1)}, bf16[16,5120]{1,0:T(8,128)(2,1)S(1)}, u32[]{:S(2)}, u32[]{:S(2)}) collective-permute-start(bf16[16,5120]{1,0:T(8,128)(2,1)} %param.7), channel_id=1, source_target_pairs={{0,8},{1,9},{2,10},{3,11},{4,12},{5,13},{6,14},{7,15},{8,0},{9,1},... | collective-permute-start | bytes 491528 | tf_op jit(solution)/shard_map/ppermute | solution.py:134
  6.3 0.7 add_select_fusion.1
  7.0 0.1 iota_compare_fusion
  7.1 0.2 convert_reduce_fusion
  7.3 0.1 add.86
  7.4 0.1 add.83
  7.5 0.1 add.89
  7.7 0.0 copy-start.1
  7.7 0.9 copy-done.1
  8.6 1.3 pack_teacher.1
  9.9 0.9 slice.8
  10.8 6.2 %all-to-all-start = ((bf16[32,67,128]{2,1,0:T(8,128)(2,1)}), bf16[32,67,128]{2,1,0:T(8,128)(2,1)}, u32[]{:S(2)}, u32[]{:S(2)}) async-start(bf16[32,67,128]{2,1,0:T(8,128)(2,1)} %slice.8), calls=%async_computation | async-start | bytes 1179648 | tf_op jit(solution)/shard_map/all_to_all | solution.py:499
  17.0 0.9 constant_dynamic-update-slice_fusion.3
  17.9 0.0 collective-permute-done
  18.0 1.8 %collective-permute-start.4 = (bf16[64,5120]{1,0:T(8,128)(2,1)S(1)}, bf16[64,5120]{1,0:T(8,128)(2,1)S(1)}, u32[]{:S(2)}, u32[]{:S(2)}) collective-permute-start(bf16[64,5120]{1,0:T(8,128)(2,1)S(1)} %constant_dynamic-update-slice_fusion.refs_0_), channel_id=1, source_target_pairs={{0,4},{1,5},{2,6},{3,7},{4,0},{5,1},{6,2},{7,3},{8,12},{9,13},{10,... | collective-permute-start | bytes 1966088 | tf_op jit(solution)/shard_map/ppermute | solution.py:134
  19.8 1.5 %collective-permute-start.3 = (bf16[64,5120]{1,0:T(8,128)(2,1)S(1)}, bf16[64,5120]{1,0:T(8,128)(2,1)S(1)}, u32[]{:S(2)}, u32[]{:S(2)}) collective-permute-start(bf16[64,5120]{1,0:T(8,128)(2,1)S(1)} %constant_dynamic-update-slice_fusion.refs_0_), channel_id=1, source_target_pairs={{0,2},{1,3},{2,0},{3,1},{4,6},{5,7},{6,4},{7,5},{8,10},{9,11},{10,... | collective-permute-start | bytes 1966088 | tf_op jit(solution)/shard_map/ppermute | solution.py:134
  21.3 0.2 select_reduce_fusion
  21.5 0.0 copy-start.2
  21.5 0.0 copy-start.3
  21.5 5.4 %constant_dynamic-slice_fusion = bf16[2560,1024]{1,0:T(8,128)(2,1)} fusion(bf16[5120,1024]{1,0:T(8,128)(2,1)} %w_ref.1, s32[]{:T(128)S(6)} %select_n.54), kind=kLoop, calls=%fused_computation.27 | loop fusion | bytes 10485764 | tf_op jit(solution)/shard_map/dynamic_slice | solution.py:486
  26.9 13.5 %collective-permute-done.4.y_ref.refs_2_ = bf16[64,5120]{1,0:T(8,128)(2,1)S(1)} collective-permute-done((bf16[64,5120]{1,0:T(8,128)(2,1)S(1)}, bf16[64,5120]{1,0:T(8,128)(2,1)S(1)}, u32[]{:S(2)}, u32[]{:S(2)}) %collective-permute-start.4) | collective-permute-done | bytes 655392 | tf_op jit(solution)/shard_map/ppermute | solution.py:134
  40.4 0.0 collective-permute-done.3.x_ref.refs_1_
  40.5 0.0 collective-permute-start.8
  40.5 0.9 cut_halves.1
  41.4 0.5 collective-permute-start.9
  41.9 1.1 collective-permute-start.5
  43.0 0.8 collective-permute-start.6
  43.8 0.1 pad_add_fusion.refs_0_.core_ref
  43.9 4.9 %teacher_prob.1 = (f32[512,1024]{1,0:T(8,128)S(1)}, f32[16,128]{1,0:T(8,128)S(1)}) custom-call(s32[4]{0:T(128)S(1)} %pad_add_fusion.refs_0_.core_ref, s32[4,4]{1,0:T(4,128)S(1)} %broadcast_add_fusion.1.refs_1_, bf16[32,67,128]{2,1,0:T(8,128)(2,1)} %all-to-all-done.refs_2_, s32[4,1,128]{2,1,0:T(1,128)S(1)} %bitcast.9, f32[4,1,128]{2,1,0:T(1,128)S(1)} %bitcast.10), custom_call_target="tpu_custom_call" | custom-call | flops 1 | bytes 1 | tf_op jit(solution)/shard_map/teacher_prob/pallas_call | solution.py:503
  48.8 3.0 %collective-permute-done.5.refs_3_ = bf16[64,2560]{1,0:T(8,128)(2,1)} collective-permute-done((bf16[64,2560]{1,0:T(8,128)(2,1)}, bf16[64,2560]{1,0:T(8,128)(2,1)}, u32[]{:S(2)}, u32[]{:S(2)}) %collective-permute-start.5) | collective-permute-done | bytes 327712 | tf_op jit(solution)/shard_map/ppermute | solution.py:134
  51.8 0.8 collective-permute-done.6.refs_4_
  52.6 0.5 collective-permute-start.11
  53.1 1.3 %collective-permute-done.10.refs_8_ = bf16[64,2560]{1,0:T(8,128)(2,1)S(1)} collective-permute-done((bf16[64,2560]{1,0:T(8,128)(2,1)}, bf16[64,2560]{1,0:T(8,128)(2,1)S(1)}, u32[]{:S(2)}, u32[]{:S(2)}) %collective-permute-start.10) | collective-permute-done | bytes 327712 | tf_op jit(solution)/shard_map/ppermute | solution.py:134
  54.5 0.5 collective-permute-done.11.refs_9_
  54.9 0.1 collective-permute-start.13
  55.1 10.2 %logits.1 = (f32[512,1024]{1,0:T(8,128)S(1)}, f32[32,8,128]{2,1,0:T(8,128)S(1)}) custom-call(bf16[64,5120]{1,0:T(8,128)(2,1)S(1)} %constant_dynamic-update-slice_fusion.refs_0_, bf16[64,5120]{1,0:T(8,128)(2,1)S(1)} %collective-permute-done.3.x_ref.refs_1_, bf16[64,5120]{1,0:T(8,128)(2,1)S(1)} %collective-permute-done.4.y_ref.refs_2_, ...), custom_call_target="tpu_custom_call" | custom-call | flops 1 | bytes 1 | tf_op jit(solution)/shard_map/logits/pallas_call | solution.py:530
  65.3 13.7 %all_to_all.10.refs_1_ = f32[32,8,128]{2,1,0:T(8,128)S(1)} all-to-all(f32[32,8,128]{2,1,0:T(8,128)S(1)} %get-tuple-element.81), channel_id=1, replica_groups=mesh['vocab'=32] {'vocab'}, dimensions={0} | all-to-all | bytes 262144 | tf_op jit(solution)/shard_map/all_to_all | solution.py:550
  78.9 1.3 grad_logits.1
  80.2 0.3 collective-permute-start.12
  80.5 2.4 %collective-permute-done.12.sib_ref = bf16[512,1024]{1,0:T(8,128)(2,1)S(1)} collective-permute-done((bf16[512,1024]{1,0:T(8,128)(2,1)S(1)}, bf16[512,1024]{1,0:T(8,128)(2,1)S(1)}, u32[]{:S(2)}, u32[]{:S(2)}) %collective-permute-start.12) | collective-permute-done | bytes 1048608 | tf_op jit(solution)/shard_map/ppermute | solution.py:134
  83.0 8.6 %grad_hidden_partial.1 = (f32[4,2,16,1792]{3,2,1,0:T(8,128)S(1)}, bf16[4,2,16,1792]{3,2,1,0:T(8,128)(2,1)S(1)}, bf16[4,2,16,1792]{3,2,1,0:T(8,128)(2,1)S(1)}, bf...) custom-call(s32[4]{0:T(128)S(1)} %pad_add_fusion.refs_0_.core_ref, ...), custom_call_target="tpu_custom_call" | custom-call | flops 1 | bytes 1 | tf_op jit(solution)/shard_map/grad_hidden_partial/pallas_call | solution.py:568
  91.6 0.5 collective-permute-start.14
  92.1 1.0 collective-permute-start.15
  93.1 2.0 %collective-permute-start.16 = (bf16[4,2,16,1792]{3,2,1,0:T(8,128)(2,1)S(1)}, bf16[4,2,16,1792]{3,2,1,0:T(8,128)(2,1)S(1)}, u32[]{:S(2)}, u32[]{:S(2)}) collective-permute-start(bf16[4,2,16,1792]{3,2,1,0:T(8,128)(2,1)S(1)} %get-tuple-element.97), channel_id=1, source_target_pairs={{0,6},{1,7},{2,4},{3,5},{4,2},{5,3},{6,0},{7,1},{8,14},{9,15},{10,... | collective-permute-start | bytes 1376264 | tf_op jit(solution)/shard_map/ppermute | solution.py:134
  95.2 0.7 collective-permute-start.17
  95.8 1.3 collective-permute-start.18
  97.1 7.5 %collective-permute-done.17.refs_5_ = bf16[4,2,16,768]{3,2,1,0:T(8,128)(2,1)S(1)} collective-permute-done((bf16[4,2,16,768]{3,2,1,0:T(8,128)(2,1)S(1)}, bf16[4,2,16,768]{3,2,1,0:T(8,128)(2,1)S(1)}, u32[]{:S(2)}, u32[]{:S(2)}) %collective-permute-start.17) | collective-permute-done | bytes 196640 | tf_op jit(solution)/shard_map/ppermute | solution.py:134
  104.6 1.9 %collective-permute-start.19 = (bf16[4,2,16,768]{3,2,1,0:T(8,128)(2,1)S(1)}, bf16[4,2,16,768]{3,2,1,0:T(8,128)(2,1)S(1)}, u32[]{:S(2)}, u32[]{:S(2)}) collective-permute-start(bf16[4,2,16,768]{3,2,1,0:T(8,128)(2,1)S(1)} %get-tuple-element.100), channel_id=1, source_target_pairs={{0,24},{1,25},{2,26},{3,27},{4,28},{5,29},{6,30},{7,31},{8,16},{9,... | collective-permute-start | bytes 589832 | tf_op jit(solution)/shard_map/ppermute | solution.py:134
  106.4 10.0 %grad_head.1 = bf16[5120,1024]{1,0:T(8,128)(2,1)} custom-call(bf16[64,5120]{1,0:T(8,128)(2,1)S(1)} %constant_dynamic-update-slice_fusion.refs_0_, bf16[64,5120]{1,0:T(8,128)(2,1)S(1)} %collective-permute-done.3.x_ref.refs_1_, bf16[64,5120]{1,0:T(8,128)(2,1)S(1)} %collective-permute-done.4.y_ref.refs_2_, bf16[64,2560]{1,0:T(8,128)(2,1)} %collective-permute-done.5.refs_3_, ...), custom_call_target="tpu_custom_call" | custom-call | flops 1 | bytes 1 | tf_op jit(solution)/shard_map/grad_head/pallas_call | solution.py:592
  116.4 0.3 first_sum.1
  116.7 0.1 collective-permute-start.20
  116.8 2.5 %collective-permute-start.21 = (bf16[2,16,1792]{2,1,0:T(8,128)(2,1)S(1)}, bf16[2,16,1792]{2,1,0:T(8,128)(2,1)S(1)}, u32[]{:S(2)}, u32[]{:S(2)}) collective-permute-start(bf16[2,16,1792]{2,1,0:T(8,128)(2,1)S(1)} %get-tuple-element.113), channel_id=1, source_target_pairs={{0,16},{1,17},{2,18},{3,19},{4,20},{5,21},{6,22},{7,23},{8,24},{9,... | collective-permute-start | bytes 344072 | tf_op jit(solution)/shard_map/ppermute | solution.py:134
  119.3 1.9 %collective-permute-start.22 = (bf16[2,16,1792]{2,1,0:T(8,128)(2,1)S(1)}, bf16[2,16,1792]{2,1,0:T(8,128)(2,1)S(1)}, u32[]{:S(2)}, u32[]{:S(2)}) collective-permute-start(bf16[2,16,1792]{2,1,0:T(8,128)(2,1)S(1)} %get-tuple-element.114), channel_id=1, source_target_pairs={{0,24},{1,25},{2,26},{3,27},{4,28},{5,29},{6,30},{7,31},{8,16},{9,... | collective-permute-start | bytes 344072 | tf_op jit(solution)/shard_map/ppermute | solution.py:134
  121.2 0.5 collective-permute-start.23
  121.6 1.3 collective-permute-start.24
  122.9 2.4 %collective-permute-done.23.refs_5_ = bf16[2,16,768]{2,1,0:T(8,128)(2,1)S(1)} collective-permute-done((bf16[2,16,768]{2,1,0:T(8,128)(2,1)S(1)}, bf16[2,16,768]{2,1,0:T(8,128)(2,1)S(1)}, u32[]{:S(2)}, u32[]{:S(2)}) %collective-permute-start.23) | collective-permute-done | bytes 49184 | tf_op jit(solution)/shard_map/ppermute | solution.py:134
  125.2 1.2 collective-permute-start.25
  126.4 3.8 %collective-permute-done.25.refs_7_ = bf16[2,16,768]{2,1,0:T(8,128)(2,1)S(1)} collective-permute-done((bf16[2,16,768]{2,1,0:T(8,128)(2,1)S(1)}, bf16[2,16,768]{2,1,0:T(8,128)(2,1)S(1)}, u32[]{:S(2)}, u32[]{:S(2)}) %collective-permute-start.25) | collective-permute-done | bytes 49184 | tf_op jit(solution)/shard_map/ppermute | solution.py:134
  130.2 0.1 last_sum.1
  130.3 0.1 collective-permute-start.26
  130.4 0.6 slice_reduce_fusion
  131.0 0.6 collective-permute-done.26
  131.7 0.7 pad_maximum_fusion
  (35 shorter events, 0.1 us)
Async XLA Ops:
  0.6 17.3 %collective-permute-start.1 = (bf16[16,5120]{1,0:T(8,128)(2,1)}, bf16[16,5120]{1,0:T(8,128)(2,1)S(1)}, u32[]{:S(2)}, u32[]{:S(2)}) collective-permute-start(bf16[16,5120]{1,0:T(8,128)(2,1)} %param.7), channel_id=1, source_target_pairs={{0,16},{1,17},{2,18},{3,19},{4,20},{5,21},{6,22},{7,23},{8,24},{9,... | collective-permute-start | bytes 491528 | tf_op jit(solution)/shard_map/ppermute | solution.py:134
  4.7 13.2 %collective-permute-start = (bf16[16,5120]{1,0:T(8,128)(2,1)}, bf16[16,5120]{1,0:T(8,128)(2,1)S(1)}, u32[]{:S(2)}, u32[]{:S(2)}) collective-permute-start(bf16[16,5120]{1,0:T(8,128)(2,1)} %param.7), channel_id=1, source_target_pairs={{0,8},{1,9},{2,10},{3,11},{4,12},{5,13},{6,14},{7,15},{8,0},{9,1},... | collective-permute-start | bytes 491528 | tf_op jit(solution)/shard_map/ppermute | solution.py:134
  6.3 11.7 %collective-permute-start.2 = (bf16[16,5120]{1,0:T(8,128)(2,1)}, bf16[16,5120]{1,0:T(8,128)(2,1)S(1)}, u32[]{:S(2)}, u32[]{:S(2)}) collective-permute-start(bf16[16,5120]{1,0:T(8,128)(2,1)} %param.7), channel_id=1, source_target_pairs={{0,24},{1,25},{2,26},{3,27},{4,28},{5,29},{6,30},{7,31},{8,16},{9,... | collective-permute-start | bytes 491528 | tf_op jit(solution)/shard_map/ppermute | solution.py:134
  7.7 1.0 copy-start.1
  10.8 33.1 %all-to-all-start = ((bf16[32,67,128]{2,1,0:T(8,128)(2,1)}), bf16[32,67,128]{2,1,0:T(8,128)(2,1)}, u32[]{:S(2)}, u32[]{:S(2)}) async-start(bf16[32,67,128]{2,1,0:T(8,128)(2,1)} %slice.8), calls=%async_computation | async-start | bytes 1179648 | tf_op jit(solution)/shard_map/all_to_all | solution.py:499
  18.0 22.4 %collective-permute-start.4 = (bf16[64,5120]{1,0:T(8,128)(2,1)S(1)}, bf16[64,5120]{1,0:T(8,128)(2,1)S(1)}, u32[]{:S(2)}, u32[]{:S(2)}) collective-permute-start(bf16[64,5120]{1,0:T(8,128)(2,1)S(1)} %constant_dynamic-update-slice_fusion.refs_0_), channel_id=1, source_target_pairs={{0,4},{1,5},{2,6},{3,7},{4,0},{5,1},{6,2},{7,3},{8,12},{9,13},{10,... | collective-permute-start | bytes 1966088 | tf_op jit(solution)/shard_map/ppermute | solution.py:134
  19.8 20.7 %collective-permute-start.3 = (bf16[64,5120]{1,0:T(8,128)(2,1)S(1)}, bf16[64,5120]{1,0:T(8,128)(2,1)S(1)}, u32[]{:S(2)}, u32[]{:S(2)}) collective-permute-start(bf16[64,5120]{1,0:T(8,128)(2,1)S(1)} %constant_dynamic-update-slice_fusion.refs_0_), channel_id=1, source_target_pairs={{0,2},{1,3},{2,0},{3,1},{4,6},{5,7},{6,4},{7,5},{8,10},{9,11},{10,... | collective-permute-start | bytes 1966088 | tf_op jit(solution)/shard_map/ppermute | solution.py:134
  21.5 22.4 %copy-start.2 = (s32[4,128]{1,0:T(4,128)S(1)}, s32[4,128]{1,0:T(4,128)}, u32[]{:S(2)}) copy-start(s32[4,128]{1,0:T(4,128)} %param.11) | copy-start | bytes 6148
  21.5 22.4 %copy-start.3 = (f32[512]{0:T(512)S(1)}, f32[512]{0:T(512)}, u32[]{:S(2)}) copy-start(f32[512]{0:T(512)} %param.12) | copy-start | bytes 6148
  26.9 26.2 %collective-permute-start.7 = (bf16[64,5120]{1,0:T(8,128)(2,1)S(1)}, bf16[64,5120]{1,0:T(8,128)(2,1)S(1)}, u32[]{:S(2)}, u32[]{:S(2)}) collective-permute-start(bf16[64,5120]{1,0:T(8,128)(2,1)S(1)} %constant_dynamic-update-slice_fusion.refs_0_), channel_id=1, source_target_pairs={{0,1},{1,0},{2,3},{3,2},{4,5},{5,4},{6,7},{7,6},{8,9},{9,8},{10,11... | collective-permute-start | bytes 1966088 | tf_op jit(solution)/shard_map/ppermute | solution.py:134
  40.5 14.5 %collective-permute-start.8 = (bf16[64,5120]{1,0:T(8,128)(2,1)S(1)}, bf16[64,5120]{1,0:T(8,128)(2,1)S(1)}, u32[]{:S(2)}, u32[]{:S(2)}) collective-permute-start(bf16[64,5120]{1,0:T(8,128)(2,1)S(1)} %collective-permute-done.3.x_ref.refs_1_), channel_id=1, source_target_pairs={{0,1},{1,0},{2,3},{3,2},{4,5},{5,4},{6,7},{7,6},{8,9},{9,8},{10,11... | collective-permute-start | bytes 1966088 | tf_op jit(solution)/shard_map/ppermute | solution.py:134
  41.4 13.6 %collective-permute-start.9 = (bf16[64,5120]{1,0:T(8,128)(2,1)S(1)}, bf16[64,5120]{1,0:T(8,128)(2,1)}, u32[]{:S(2)}, u32[]{:S(2)}) collective-permute-start(bf16[64,5120]{1,0:T(8,128)(2,1)S(1)} %collective-permute-done.4.y_ref.refs_2_), channel_id=1, source_target_pairs={{0,1},{1,0},{2,3},{3,2},{4,5},{5,4},{6,7},{7,6},{8,9},{9,8},{10,11... | collective-permute-start | bytes 1966088 | tf_op jit(solution)/shard_map/ppermute | solution.py:134
  41.9 9.9 %collective-permute-start.5 = (bf16[64,2560]{1,0:T(8,128)(2,1)}, bf16[64,2560]{1,0:T(8,128)(2,1)}, u32[]{:S(2)}, u32[]{:S(2)}) collective-permute-start(bf16[64,2560]{1,0:T(8,128)(2,1)} %get-tuple-element.64), channel_id=1, source_target_pairs={{0,4},{1,5},{2,6},{3,7},{4,0},{5,1},{6,2},{7,3},{8,12},{9,13},{10,... | collective-permute-start | bytes 983048 | tf_op jit(solution)/shard_map/ppermute | solution.py:134
  43.0 9.7 %collective-permute-start.6 = (bf16[64,2560]{1,0:T(8,128)(2,1)}, bf16[64,2560]{1,0:T(8,128)(2,1)}, u32[]{:S(2)}, u32[]{:S(2)}) collective-permute-start(bf16[64,2560]{1,0:T(8,128)(2,1)} %get-tuple-element.65), channel_id=1, source_target_pairs={{0,2},{1,3},{2,0},{3,1},{4,6},{5,7},{6,4},{7,5},{8,10},{9,11},{10,... | collective-permute-start | bytes 983048 | tf_op jit(solution)/shard_map/ppermute | solution.py:134
  52.6 26.3 %copy-start.4 = (f32[512]{0:T(512)S(1)}, f32[512]{0:T(512)}, u32[]{:S(2)}) copy-start(f32[512]{0:T(512)} %param.13) | copy-start | bytes 6148
  52.6 1.8 %collective-permute-start.10 = (bf16[64,2560]{1,0:T(8,128)(2,1)}, bf16[64,2560]{1,0:T(8,128)(2,1)S(1)}, u32[]{:S(2)}, u32[]{:S(2)}) collective-permute-start(bf16[64,2560]{1,0:T(8,128)(2,1)} %collective-permute-done.5.refs_3_), channel_id=1, source_target_pairs={{0,1},{1,0},{2,3},{3,2},{4,5},{5,4},{6,7},{7,6},{8,9},{9,8},{10,11... | collective-permute-start | bytes 983048 | tf_op jit(solution)/shard_map/ppermute | solution.py:134
  52.6 2.3 %collective-permute-start.11 = (bf16[64,2560]{1,0:T(8,128)(2,1)}, bf16[64,2560]{1,0:T(8,128)(2,1)S(1)}, u32[]{:S(2)}, u32[]{:S(2)}) collective-permute-start(bf16[64,2560]{1,0:T(8,128)(2,1)} %collective-permute-done.6.refs_4_), channel_id=1, source_target_pairs={{0,1},{1,0},{2,3},{3,2},{4,5},{5,4},{6,7},{7,6},{8,9},{9,8},{10,11... | collective-permute-start | bytes 983048 | tf_op jit(solution)/shard_map/ppermute | solution.py:134
  54.9 28.0 %collective-permute-start.13 = (bf16[2560,1024]{1,0:T(8,128)(2,1)}, bf16[2560,1024]{1,0:T(8,128)(2,1)S(1)}, u32[]{:S(2)}, u32[]{:S(2)}) collective-permute-start(bf16[2560,1024]{1,0:T(8,128)(2,1)} %constant_dynamic-slice_fusion), channel_id=1, source_target_pairs={{0,1},{1,0},{2,3},{3,2},{4,5},{5,4},{6,7},{7,6},{8,9},{9,8},{10,11... | collective-permute-start | bytes 15728648 | tf_op jit(solution)/shard_map/ppermute | solution.py:134
  80.2 11.4 %copy-start = (bf16[512,1024]{1,0:T(8,128)(2,1)}, bf16[512,1024]{1,0:T(8,128)(2,1)S(1)}, u32[]{:S(2)}) copy-start(bf16[512,1024]{1,0:T(8,128)(2,1)S(1)} %get-tuple-element.101.grad_ref.refs_10_) | copy-start | bytes 3145732
  80.2 2.7 %collective-permute-start.12 = (bf16[512,1024]{1,0:T(8,128)(2,1)S(1)}, bf16[512,1024]{1,0:T(8,128)(2,1)S(1)}, u32[]{:S(2)}, u32[]{:S(2)}) collective-permute-start(bf16[512,1024]{1,0:T(8,128)(2,1)S(1)} %get-tuple-element.101.grad_ref.refs_10_), channel_id=1, source_target_pairs={{0,1},{1,0},{2,3},{3,2},{4,5},{5,4},{6,7},{7,6},{8,9},{9,8},{10,11... | collective-permute-start | bytes 3145736 | tf_op jit(solution)/shard_map/ppermute | solution.py:134
  91.6 24.8 %collective-permute-start.14 = (bf16[4,2,16,1792]{3,2,1,0:T(8,128)(2,1)S(1)}, bf16[4,2,16,1792]{3,2,1,0:T(8,128)(2,1)S(1)}, u32[]{:S(2)}, u32[]{:S(2)}) collective-permute-start(bf16[4,2,16,1792]{3,2,1,0:T(8,128)(2,1)S(1)} %get-tuple-element.95), channel_id=1, source_target_pairs={{0,2},{1,3},{2,0},{3,1},{4,6},{5,7},{6,4},{7,5},{8,10},{9,11},{10,... | collective-permute-start | bytes 1376264 | tf_op jit(solution)/shard_map/ppermute | solution.py:134
  92.1 24.3 %collective-permute-start.15 = (bf16[4,2,16,1792]{3,2,1,0:T(8,128)(2,1)S(1)}, bf16[4,2,16,1792]{3,2,1,0:T(8,128)(2,1)S(1)}, u32[]{:S(2)}, u32[]{:S(2)}) collective-permute-start(bf16[4,2,16,1792]{3,2,1,0:T(8,128)(2,1)S(1)} %get-tuple-element.96), channel_id=1, source_target_pairs={{0,4},{1,5},{2,6},{3,7},{4,0},{5,1},{6,2},{7,3},{8,12},{9,13},{10,... | collective-permute-start | bytes 1376264 | tf_op jit(solution)/shard_map/ppermute | solution.py:134
  93.1 23.3 %collective-permute-start.16 = (bf16[4,2,16,1792]{3,2,1,0:T(8,128)(2,1)S(1)}, bf16[4,2,16,1792]{3,2,1,0:T(8,128)(2,1)S(1)}, u32[]{:S(2)}, u32[]{:S(2)}) collective-permute-start(bf16[4,2,16,1792]{3,2,1,0:T(8,128)(2,1)S(1)} %get-tuple-element.97), channel_id=1, source_target_pairs={{0,6},{1,7},{2,4},{3,5},{4,2},{5,3},{6,0},{7,1},{8,14},{9,15},{10,... | collective-permute-start | bytes 1376264 | tf_op jit(solution)/shard_map/ppermute | solution.py:134
  95.2 9.4 %collective-permute-start.17 = (bf16[4,2,16,768]{3,2,1,0:T(8,128)(2,1)S(1)}, bf16[4,2,16,768]{3,2,1,0:T(8,128)(2,1)S(1)}, u32[]{:S(2)}, u32[]{:S(2)}) collective-permute-start(bf16[4,2,16,768]{3,2,1,0:T(8,128)(2,1)S(1)} %get-tuple-element.98), channel_id=1, source_target_pairs={{0,8},{1,9},{2,10},{3,11},{4,12},{5,13},{6,14},{7,15},{8,0},{9,1},... | collective-permute-start | bytes 589832 | tf_op jit(solution)/shard_map/ppermute | solution.py:134
  95.8 20.6 %collective-permute-start.18 = (bf16[4,2,16,768]{3,2,1,0:T(8,128)(2,1)S(1)}, bf16[4,2,16,768]{3,2,1,0:T(8,128)(2,1)S(1)}, u32[]{:S(2)}, u32[]{:S(2)}) collective-permute-start(bf16[4,2,16,768]{3,2,1,0:T(8,128)(2,1)S(1)} %get-tuple-element.99), channel_id=1, source_target_pairs={{0,16},{1,17},{2,18},{3,19},{4,20},{5,21},{6,22},{7,23},{8,24},{9,... | collective-permute-start | bytes 589832 | tf_op jit(solution)/shard_map/ppermute | solution.py:134
  104.6 11.8 %collective-permute-start.19 = (bf16[4,2,16,768]{3,2,1,0:T(8,128)(2,1)S(1)}, bf16[4,2,16,768]{3,2,1,0:T(8,128)(2,1)S(1)}, u32[]{:S(2)}, u32[]{:S(2)}) collective-permute-start(bf16[4,2,16,768]{3,2,1,0:T(8,128)(2,1)S(1)} %get-tuple-element.100), channel_id=1, source_target_pairs={{0,24},{1,25},{2,26},{3,27},{4,28},{5,29},{6,30},{7,31},{8,16},{9,... | collective-permute-start | bytes 589832 | tf_op jit(solution)/shard_map/ppermute | solution.py:134
  116.7 13.5 %collective-permute-start.20 = (bf16[2,16,1792]{2,1,0:T(8,128)(2,1)S(1)}, bf16[2,16,1792]{2,1,0:T(8,128)(2,1)S(1)}, u32[]{:S(2)}, u32[]{:S(2)}) collective-permute-start(bf16[2,16,1792]{2,1,0:T(8,128)(2,1)S(1)} %get-tuple-element.112), channel_id=1, source_target_pairs={{0,8},{1,9},{2,10},{3,11},{4,12},{5,13},{6,14},{7,15},{8,0},{9,1},... | collective-permute-start | bytes 344072 | tf_op jit(solution)/shard_map/ppermute | solution.py:134
  116.8 13.5 %collective-permute-start.21 = (bf16[2,16,1792]{2,1,0:T(8,128)(2,1)S(1)}, bf16[2,16,1792]{2,1,0:T(8,128)(2,1)S(1)}, u32[]{:S(2)}, u32[]{:S(2)}) collective-permute-start(bf16[2,16,1792]{2,1,0:T(8,128)(2,1)S(1)} %get-tuple-element.113), channel_id=1, source_target_pairs={{0,16},{1,17},{2,18},{3,19},{4,20},{5,21},{6,22},{7,23},{8,24},{9,... | collective-permute-start | bytes 344072 | tf_op jit(solution)/shard_map/ppermute | solution.py:134
  119.3 10.9 %collective-permute-start.22 = (bf16[2,16,1792]{2,1,0:T(8,128)(2,1)S(1)}, bf16[2,16,1792]{2,1,0:T(8,128)(2,1)S(1)}, u32[]{:S(2)}, u32[]{:S(2)}) collective-permute-start(bf16[2,16,1792]{2,1,0:T(8,128)(2,1)S(1)} %get-tuple-element.114), channel_id=1, source_target_pairs={{0,24},{1,25},{2,26},{3,27},{4,28},{5,29},{6,30},{7,31},{8,16},{9,... | collective-permute-start | bytes 344072 | tf_op jit(solution)/shard_map/ppermute | solution.py:134
  121.2 4.1 %collective-permute-start.23 = (bf16[2,16,768]{2,1,0:T(8,128)(2,1)S(1)}, bf16[2,16,768]{2,1,0:T(8,128)(2,1)S(1)}, u32[]{:S(2)}, u32[]{:S(2)}) collective-permute-start(bf16[2,16,768]{2,1,0:T(8,128)(2,1)S(1)} %get-tuple-element.116), channel_id=1, source_target_pairs={{0,2},{1,3},{2,0},{3,1},{4,6},{5,7},{6,4},{7,5},{8,10},{9,11},{10,... | collective-permute-start | bytes 147464 | tf_op jit(solution)/shard_map/ppermute | solution.py:134
  121.6 4.8 %collective-permute-start.24 = (bf16[2,16,768]{2,1,0:T(8,128)(2,1)S(1)}, bf16[2,16,768]{2,1,0:T(8,128)(2,1)S(1)}, u32[]{:S(2)}, u32[]{:S(2)}) collective-permute-start(bf16[2,16,768]{2,1,0:T(8,128)(2,1)S(1)} %get-tuple-element.117), channel_id=1, source_target_pairs={{0,4},{1,5},{2,6},{3,7},{4,0},{5,1},{6,2},{7,3},{8,12},{9,13},{10,... | collective-permute-start | bytes 147464 | tf_op jit(solution)/shard_map/ppermute | solution.py:134
  125.2 5.0 %collective-permute-start.25 = (bf16[2,16,768]{2,1,0:T(8,128)(2,1)S(1)}, bf16[2,16,768]{2,1,0:T(8,128)(2,1)S(1)}, u32[]{:S(2)}, u32[]{:S(2)}) collective-permute-start(bf16[2,16,768]{2,1,0:T(8,128)(2,1)S(1)} %get-tuple-element.118), channel_id=1, source_target_pairs={{0,6},{1,7},{2,4},{3,5},{4,2},{5,3},{6,0},{7,1},{8,14},{9,15},{10,... | collective-permute-start | bytes 147464 | tf_op jit(solution)/shard_map/ppermute | solution.py:134
  130.3 1.3 %collective-permute-start.26 = (bf16[16,2560]{1,0:T(8,128)(2,1)S(1)}, bf16[16,2560]{1,0:T(8,128)(2,1)S(1)}, u32[]{:S(2)}, u32[]{:S(2)}) collective-permute-start(bf16[16,2560]{1,0:T(8,128)(2,1)S(1)} %get-tuple-element.120), channel_id=1, source_target_pairs={{0,1},{1,0},{2,3},{3,2},{4,5},{5,4},{6,7},{7,6},{8,9},{9,8},{10,11... | collective-permute-start | bytes 245768 | tf_op jit(solution)/shard_map/ppermute | solution.py:134
